TPU v7x, 32 devices: a whole 2x2x4 slice. The times are simulated.
32 devices in a mesh: groups: 2 (over x), samp: 16 (over z, y, core).
Axes of the slice: x: 2, y: 2, z: 4, core: 2. Of those that a mesh axis runs over, the one named last changes fastest.
Arguments:
- queries: bfloat16 [16384, 4096], P(('groups', 'samp')), parts along dimension 0, may hold values from -40 to 40
- gen_panel: bfloat16 [512, 4096], P(('groups', 'samp')), parts along dimension 0, may hold values from -40 to 40
- ref_panel: bfloat16 [512, 4096], P(('groups', 'samp')), parts along dimension 0, may hold values from -40 to 40
Outputs:
- proof: float32 [16384], P(('groups', 'samp')), parts along dimension 0
There are 2 independent parts, one for each index of `groups`. A program takes and returns all parts, laid end to end along the dimension named above; each array names one. Nothing has to cross between parts.
All inputs are finite; a program needn't handle non-finite values.
Results may differ from a plain program's by a relative error of at most 0.0003.
The roundings to bfloat16 on the way count: a program that leaves them out, or rounds other values in their place, can miss the bound.
Values may be sent and summed in bfloat16 or wider, within the bound.
No kernel may reach another device: no remote copies, remote signals or barrier semaphores. Data moves between devices by JAX's collectives and lax.ppermute only.
A program may use at most 64 MiB of HBM per device.

v0:
```python
import jax
import jax.numpy as jnp
from jax import lax
from jax.sharding import PartitionSpec as P

TEMP = 64


def center_rows(rows, profile):
    return (rows.astype(jnp.float32) - profile).astype(jnp.bfloat16)


def half_norms(centered):
    return 0.5 * jnp.sum(jnp.square(centered.astype(jnp.float32)), axis=1)


def panel_scores(probes, panel):
    products = lax.dot_general(
        probes, panel, (((1,), (1,)), ((), ())), preferred_element_type=jnp.float32
    )
    return (products - half_norms(panel)) / TEMP


def body(queries, gen_panel, ref_panel):
    row_total = ref_panel.shape[0] * lax.axis_size("samp")
    feature_sum = lax.psum(jnp.sum(ref_panel.astype(jnp.float32), axis=0), "samp")
    profile = feature_sum / row_total
    probes = center_rows(queries, profile)
    gen_c = center_rows(gen_panel, profile)
    ref_c = center_rows(ref_panel, profile)
    gen_all, ref_all = (
        lax.all_gather(gen_c, "samp", axis=0, tiled=True),
        lax.all_gather(ref_c, "samp", axis=0, tiled=True),
    )
    gen_log = jax.nn.logsumexp(panel_scores(probes, gen_all), axis=1)
    ref_log = jax.nn.logsumexp(panel_scores(probes, ref_all), axis=1)
    return gen_log - ref_log


def solution(mesh):
    return jax.shard_map(
        body,
        mesh=mesh,
        in_specs=(
            P(("groups", "samp"), None),
            P(("groups", "samp"), None),
            P(("groups", "samp"), None),
        ),
        out_specs=P(("groups", "samp")),
        check_vma=False,
    )
```

profile of v0, /device:TPU:1, one launch (start us, length us, event | category | flops | bytes accessed | tf_op | source)
XLA Modules:
  0.0 167.1 jit_solution(7804543017972643347)
XLA Ops:
  6.5 0.0 all-gather.3.cloned.1.call-start
  6.5 0.9 convert_reduce_fusion
  7.5 58.0 %psum.7 = f32[4096]{0:T(1024)S(1)} all-reduce(f32[4096]{0:T(1024)S(1)} %convert_reduce_fusion), channel_id=1, replica_groups=mesh['groups'=2,'samp'=16] {'samp'}, use_global_device_ids=true, to_apply=%region_1.0 | all-reduce | flops 4096 | bytes 32768 | tf_op jit(solution)/shard_map/psum | solution.py:26
  65.5 1.7 %subtract_convert_fusion.11 = (bf16[16,4096]{1,0:T(8,128)(2,1)}, bf16[16,4096]{1,0:T(8,128)(2,1)}) fusion(bf16[16,4096]{1,0:T(8,128)(2,1)} %param.4, f32[4096]{0:T(1024)S(1)} %broadcast_multiply_fusion, bf16[16,4096]{1,0:T(8,128)(2,1)} %param.5), kind=kLoop, calls=%fused_computation.14 | loop fusion | flops 393216 | bytes 540672 | tf_op jit(solution)/shard_map/convert_element_type | solution.py:10
  67.2 0.0 all-gather.3.cloned.1.call-update
  67.2 0.0 all-gather.5.cloned.1.call-start
  67.3 0.7 all-gather.5.cloned.1.call-update
  68.0 42.8 %all-gather.3.cloned.1.call-done = bf16[256,4096]{1,0:T(8,128)(2,1)} async-done(((bf16[16,4096]{1,0:T(8,128)(2,1)}), bf16[256,4096]{1,0:T(8,128)(2,1)}) %all-gather.3.cloned.1.call-update) | async-done | bytes 2097168 | tf_op jit(solution)/shard_map/all_gather | solution.py:32
  110.8 2.1 %multiply_reduce_fusion.1 = f32[256]{0:T(256)S(1)} fusion(bf16[256,4096]{1,0:T(8,128)(2,1)} %all-gather.3.cloned.1.call-done), kind=kLoop, calls=%fused_computation.2 | loop fusion | flops 3145472 | bytes 2098176 | tf_op jit(solution)/shard_map/reduce_sum | solution.py:14
  112.9 4.2 %fusion.8 = (f32[512]{0:T(512)S(1)}, f32[512,256]{0,1:T(8,128)S(1)}) fusion(f32[256]{0:T(256)S(1)} %broadcast_multiply_fusion.2, bf16[256,4096]{1,0:T(8,128)(2,1)} %all-gather.3.cloned.1.call-done, bf16[512,4096]{1,0:T(8,128)(2,1)} %param.3, f32[4096]{0:T(1024)S(1)} %broadcast_multiply_fusion), kind=kOutput, calls=%fused_computation.22 | convolution fusion | flops 1080425984 | bytes 6835200 | tf_op jit(solution)/shard_map/dot_general | solution.py:18
  117.1 36.1 %all-gather.5.cloned.1.call-done = bf16[256,4096]{1,0:T(8,128)(2,1)} async-done(((bf16[16,4096]{1,0:T(8,128)(2,1)}), bf16[256,4096]{1,0:T(8,128)(2,1)}) %all-gather.5.cloned.1.call-update) | async-done | bytes 2097168 | tf_op jit(solution)/shard_map/all_gather | solution.py:33
  153.2 2.1 %multiply_reduce_fusion = f32[256]{0:T(256)S(1)} fusion(bf16[256,4096]{1,0:T(8,128)(2,1)} %all-gather.5.cloned.1.call-done), kind=kLoop, calls=%fused_computation.1 | loop fusion | flops 3145472 | bytes 2098176 | tf_op jit(solution)/shard_map/reduce_sum | solution.py:14
  155.2 4.2 %fusion.7 = (f32[512]{0:T(512)S(1)}, f32[512,256]{0,1:T(8,128)S(1)}) fusion(f32[256]{0:T(256)S(1)} %broadcast_multiply_fusion.1, bf16[256,4096]{1,0:T(8,128)(2,1)} %all-gather.5.cloned.1.call-done, bf16[512,4096]{1,0:T(8,128)(2,1)} %param.3, f32[4096]{0:T(1024)S(1)} %broadcast_multiply_fusion), kind=kOutput, calls=%fused_computation.21 | convolution fusion | flops 1080425984 | bytes 6835200 | tf_op jit(solution)/shard_map/dot_general | solution.py:18
  159.4 0.1 exponential_reduce_fusion.1
  159.5 0.1 exponential_reduce_fusion
  159.7 0.6 add_subtract_fusion
  (5 shorter events, 0.0 us)
Async XLA Ops:
  6.5 104.3 %all-gather.3.cloned.1.call-start = ((), (), s32[]{:S(2)}) async-start(), calls=%async_computation | async-start | bytes 2228224 | tf_op jit(solution)/shard_map/all_gather | solution.py:32
  67.2 86.0 %all-gather.5.cloned.1.call-start = ((), (), s32[]{:S(2)}) async-start(), calls=%async_computation.1 | async-start | bytes 2228224 | tf_op jit(solution)/shard_map/all_gather | solution.py:33
Sparse Core Ops, SparseCore 0:
  67.3 43.4 all-gather.2
  113.0 40.1 all-gather.4
where the time goes:
time: 168 us; the launch traced here: 167 us
  waiting for transfers between devices  79.6 us (47%)
  blocking collectives  58 us (35%)
  between operations  13.4 us (8%)
  matrix products  8.35 us (5%)
  other arithmetic  7.65 us (5%)
    psum x1, blocking collectives, body(): lax.psum(jnp.sum(ref_panel.astype(jnp.float32), axis=0), 'samp')  58 us
    all_gather x1, waiting for transfers between devices, body(): lax.all_gather(gen_c, 'samp', axis=0, tiled=True)  42.8 us
    all_gather x1, waiting for transfers between devices, body(): lax.all_gather(ref_c, 'samp', axis=0, tiled=True)  36.1 us
    dot_general x2, matrix products, panel_scores(): lax.dot_general(probes, panel, (((1,), (1,)), ((), ())), preferred_elemen...  8.35 us
    reduce_sum x2, other arithmetic, half_norms(): return 0.5 * jnp.sum(jnp.square(centered.astype(jnp.float32)), axis=1)  4.17 us
  transfers between devices with their start and end apart: 2, of which 2 were waited for; matrix products, arithmetic and copies ran while one was open for 4% of the time, Pallas kernels for 0%

commit v1 on v0

v1 whole, which is shorter than its diff:
```python
import jax
import jax.numpy as jnp
from jax import lax
from jax.sharding import PartitionSpec as P

TEMP = 64


def center_rows(rows, profile):
    centered = rows.astype(jnp.float32) - profile
    return lax.reduce_precision(centered, 8, 7).astype(jnp.bfloat16)


def half_norms(centered):
    return 0.5 * jnp.sum(jnp.square(centered.astype(jnp.float32)), axis=1)


def panel_scores(probes, panel):
    products = lax.dot_general(
        probes, panel, (((1,), (1,)), ((), ())), preferred_element_type=jnp.float32
    )
    return (products - half_norms(panel)) / TEMP


def body(queries, gen_panel, ref_panel):
    both = jnp.stack([ref_panel, gen_panel])
    every = lax.all_gather(both, "samp", axis=1, tiled=True)
    ref_all, gen_all = every[0], every[1]
    profile = jnp.sum(ref_all.astype(jnp.float32), axis=0) / ref_all.shape[0]
    probes = center_rows(queries, profile)
    gen_c = center_rows(gen_all, profile)
    ref_c = center_rows(ref_all, profile)
    gen_log = jax.nn.logsumexp(panel_scores(probes, gen_c), axis=1)
    ref_log = jax.nn.logsumexp(panel_scores(probes, ref_c), axis=1)
    return gen_log - ref_log


def solution(mesh):
    return jax.shard_map(
        body,
        mesh=mesh,
        in_specs=(
            P(("groups", "samp"), None),
            P(("groups", "samp"), None),
            P(("groups", "samp"), None),
        ),
        out_specs=P(("groups", "samp")),
        check_vma=False,
    )
```

time: 168 us -> 81.5 us (0.49)
  blocking collectives: 58 us -> 0 us
  waiting for transfers between devices: 79.6 us -> 54.4 us
  matrix products: 8.35 us -> 4.96 us
    psum x1 -> x0, blocking collectives: 58 us -> none  [body(): lax.psum(jnp.sum(ref_panel.astype(jnp.float32), axis=0), 'samp')]
    all_gather x2 -> x1, waiting for transfers between devices: 78.9 us -> 54.4 us  [body(): every = lax.all_gather(both, 'samp', axis=1, tiled=True)]
    dot_general x2, matrix products: 8.35 us -> 4.96 us  [panel_scores(): lax.dot_general(probes, panel, (((1,), (1,)), ((), ())), preferred_elemen...]
    convert_element_type x1 -> x0, other arithmetic: 1.7 us -> none  [center_rows(): return (rows.astype(jnp.float32) - profile).astype(jnp.bfloat16)]
    reduce_sum x2 -> x1, other arithmetic: 4.17 us -> 3.68 us  [half_norms(): return 0.5 * jnp.sum(jnp.square(centered.astype(jnp.float32)), axis=1)]
  transfers between devices with their start and end apart: 2 -> 1, of which waited for: 2 -> 1; matrix products, arithmetic and copies ran while one was open for 4% -> 0% of each run, Pallas kernels for 0% -> 0%
where the time goes in v1:
time: 81.5 us; the launch traced here: 81.1 us
  waiting for transfers between devices  54.4 us (67%)
  between operations  13.5 us (17%)
  other arithmetic  8.28 us (10%)
  matrix products  4.96 us (6%)
    all_gather x1, waiting for transfers between devices, body(): every = lax.all_gather(both, 'samp', axis=1, tiled=True)  54.4 us
    dot_general x2, matrix products, panel_scores(): lax.dot_general(probes, panel, (((1,), (1,)), ((), ())), preferred_elemen...  4.96 us
    reduce_sum x1, other arithmetic, half_norms(): return 0.5 * jnp.sum(jnp.square(centered.astype(jnp.float32)), axis=1)  3.68 us
    reduce_sum x1, other arithmetic, body(): profile = jnp.sum(ref_all.astype(jnp.float32), axis=0) / ref_all.shape[0]  2.08 us
    another operation x1, other arithmetic, body(): both = jnp.stack([ref_panel, gen_panel])  1.68 us
  transfers between devices with their start and end apart: 1, of which 1 were waited for; matrix products, arithmetic and copies ran while one was open for 0% of the time, Pallas kernels for 0%

profile of v1, /device:TPU:1, one launch (start us, length us, event | category | flops | bytes accessed | tf_op | source)
XLA Modules:
  0.0 81.1 jit_solution(17482133792225984695)
XLA Ops:
  6.5 0.0 all-gather.2.cloned.1.call-start
  6.5 1.7 %pad_maximum_fusion = bf16[2,16,4096]{2,1,0:T(8,128)(2,1)} fusion(bf16[1,16,4096]{2,1,0:T(8,128)(2,1)} %bitcast.33, bf16[1,16,4096]{2,1,0:T(8,128)(2,1)} %bitcast.34), kind=kLoop, calls=%fused_computation.20 | loop fusion | flops 131072 | bytes 524288 | tf_op jit(solution)/shard_map/stack | solution.py:26
  8.2 0.0 all-gather.2.cloned.1.call-update
  8.2 54.4 %all-gather.2.cloned.1.call-done = bf16[2,256,4096]{2,1,0:T(8,128)(2,1)} async-done(((bf16[2,16,4096]{2,1,0:T(8,128)(2,1)}), bf16[2,256,4096]{2,1,0:T(8,128)(2,1)}) %all-gather.2.cloned.1.call-update) | async-done | bytes 4194320 | tf_op jit(solution)/shard_map/all_gather | solution.py:27
  62.7 0.0 copy-start
  62.7 2.1 %convert_reduce_fusion = f32[4096]{0:T(1024)S(1)} fusion(bf16[2,256,4096]{2,1,0:T(8,128)(2,1)} %all-gather.2.cloned.1.call-done), kind=kLoop, calls=%fused_computation.2 | loop fusion | flops 2093056 | bytes 2113536 | tf_op jit(solution)/shard_map/reduce_sum | solution.py:29
  64.8 3.7 %multiply_reduce_fusion.1 = (f32[256]{0:T(256)S(1)}, f32[256]{0:T(256)S(1)}) fusion(f32[4096]{0:T(1024)S(1)} %broadcast_multiply_fusion, bf16[2,256,4096]{2,1,0:T(8,128)(2,1)} %all-gather.2.cloned.1.call-done), kind=kLoop, calls=%fused_computation.10 | loop fusion | flops 14679552 | bytes 4212736 | tf_op jit(solution)/shard_map/reduce_sum | solution.py:15
  68.5 0.0 copy-done
  68.5 0.0 copy-start.1
  68.5 3.7 %fusion.22 = (f32[512]{0:T(512)S(1)}, f32[512,256]{0,1:T(8,128)S(1)}) fusion(f32[256]{0:T(256)S(1)} %get-tuple-element.12, bf16[2,256,4096]{2,1,0:T(8,128)(2,1)S(1)} %copy-done, f32[4096]{0:T(1024)S(1)} %broadcast_multiply_fusion, bf16[512,4096]{1,0:T(8,128)(2,1)} %param.3), kind=kOutput, calls=%fused_computation.28 | convolution fusion | flops 1086717440 | bytes 6851584 | tf_op jit(solution)/shard_map/dot_general | solution.py:19
  72.2 0.0 copy-done.1
  72.2 1.3 %fusion.21 = (f32[512]{0:T(512)S(1)}, f32[512,256]{0,1:T(8,128)S(1)}) fusion(f32[256]{0:T(256)S(1)} %get-tuple-element.11, f32[4096]{0:T(1024)S(1)} %broadcast_multiply_fusion, bf16[2,256,4096]{2,1,0:T(8,128)(2,1)S(1)} %copy-done, bf16[512,4096]{1,0:T(8,128)(2,1)S(1)} %copy-done.1), kind=kOutput, calls=%fused_computation.27 | convolution fusion | flops 1086717440 | bytes 6851584 | tf_op jit(solution)/shard_map/dot_general | solution.py:19
  73.5 0.1 exponential_reduce_fusion.1
  73.6 0.1 exponential_reduce_fusion
  73.7 0.6 add_subtract_fusion
  (4 shorter events, 0.0 us)
Async XLA Ops:
  6.5 56.1 %all-gather.2.cloned.1.call-start = ((), (), s32[]{:S(2)}) async-start(), calls=%async_computation | async-start | bytes 4456448 | tf_op jit(solution)/shard_map/all_gather | solution.py:27
  62.7 5.8 %copy-start = (bf16[2,256,4096]{2,1,0:T(8,128)(2,1)S(1)}, bf16[2,256,4096]{2,1,0:T(8,128)(2,1)}, u32[]{:S(2)}) copy-start(bf16[2,256,4096]{2,1,0:T(8,128)(2,1)} %all-gather.2.cloned.1.call-done) | copy-start | bytes 12582916
  68.5 3.7 %copy-start.1 = (bf16[512,4096]{1,0:T(8,128)(2,1)S(1)}, bf16[512,4096]{1,0:T(8,128)(2,1)}, u32[]{:S(2)}) copy-start(bf16[512,4096]{1,0:T(8,128)(2,1)} %param.3) | copy-start | bytes 12582916
Sparse Core Ops, SparseCore 0:
  9.6 53.0 all-gather.1

commit v2 on v1

--- a/solution.py
+++ b/solution.py
@@ -4,6 +4,43 @@
 from jax.sharding import PartitionSpec as P
 
 TEMP = 64
+
+
+def ring_of_chips(chips):
+    return list(range(0, chips, 2)) + list(range(chips - 1 - chips % 2, 0, -2))
+
+
+def ring_pairs(size):
+    order = ring_of_chips(size // 2)
+    pairs = []
+    for place, chip in enumerate(order):
+        after = order[(place + 1) % len(order)]
+        before = order[place - 1]
+        pairs.append((2 * chip, 2 * after))
+        pairs.append((2 * chip + 1, 2 * before + 1))
+    return pairs
+
+
+def core_pairs(size):
+    return [(i, i ^ 1) for i in range(size)]
+
+
+def gather_pieces(own, size):
+    twins, ring = core_pairs(size), ring_pairs(size)
+    chips = size // 2
+    core = lax.axis_index("samp") % 2
+    other = lax.ppermute(own, "samp", twins)
+    block = jnp.concatenate([own, other], axis=1)
+    pieces = [block]
+    steps = (chips - 1) // 2
+    for _ in range(steps):
+        block = lax.ppermute(block, "samp", ring)
+        pieces += [block, lax.ppermute(block, "samp", twins)]
+    if chips % 2 == 0:
+        half = block.shape[1] // 2
+        last = lax.ppermute(block[:, :half], "samp", ring)
+        pieces += [last, lax.ppermute(last, "samp", twins)]
+    return pieces
 
 
 def center_rows(rows, profile):
@@ -23,8 +60,9 @@
 
 
 def body(queries, gen_panel, ref_panel):
-    both = jnp.stack([ref_panel, gen_panel])
-    every = lax.all_gather(both, "samp", axis=1, tiled=True)
+    size = lax.axis_size("samp")
+    pieces = gather_pieces(jnp.stack([ref_panel, gen_panel]), size)
+    every = jnp.concatenate(pieces, axis=1)
     ref_all, gen_all = every[0], every[1]
     profile = jnp.sum(ref_all.astype(jnp.float32), axis=0) / ref_all.shape[0]
     probes = center_rows(queries, profile)

time: 81.5 us -> 45.6 us (0.56)
  waiting for transfers between devices: 54.4 us -> 26 us
  between operations: 13.5 us -> 0.13 us
  starting transfers between devices: 0.01 us -> 11.5 us
  other arithmetic: 8.28 us -> 4.61 us
  matrix products: 4.96 us -> 2.61 us
    all_gather x1 -> x0, waiting for transfers between devices: 54.4 us -> none  [body(): every = lax.all_gather(both, 'samp', axis=1, tiled=True)]
    ppermute x0 -> x9, waiting for transfers between devices: none -> 26 us  [the longest x3 20.6 us: gather_pieces(): block = lax.ppermute(block, 'samp', ring)]
    ppermute x0 -> x9, starting transfers between devices: none -> 11.5 us  [the longest x3 5.9 us: gather_pieces(): block = lax.ppermute(block, 'samp', ring)]
    dot_general x2, matrix products: 4.96 us -> 2.61 us  [panel_scores(): lax.dot_general(probes, panel, (((1,), (1,)), ((), ())), preferred_elemen...]
    reduce_sum x1, other arithmetic: 3.68 us -> 1.43 us  [half_norms(): return 0.5 * jnp.sum(jnp.square(centered.astype(jnp.float32)), axis=1)]
    reduce_sum x1, other arithmetic: 2.08 us -> 0.34 us  [body(): profile = jnp.sum(ref_all.astype(jnp.float32), axis=0) / ref_all.shape[0]]
    concatenate x0 -> x1, other arithmetic: none -> 1 us  [gather_pieces(): block = jnp.concatenate([own, other], axis=1)]
  transfers between devices with their start and end apart: 1 -> 9, of which waited for: 1 -> 6; matrix products, arithmetic and copies ran while one was open for 0% -> 1% of each run, Pallas kernels for 0% -> 0%
where the time goes in v2:
time: 45.6 us; the launch traced here: 45.1 us
  waiting for transfers between devices  26 us (57%)
  starting transfers between devices  11.5 us (25%)
  other arithmetic  4.61 us (10%)
  matrix products  2.61 us (6%)
    ppermute x3, waiting for transfers between devices, gather_pieces(): block = lax.ppermute(block, 'samp', ring)  20.6 us
    ppermute x3, starting transfers between devices, gather_pieces(): block = lax.ppermute(block, 'samp', ring)  5.9 us
    ppermute x1, waiting for transfers between devices, gather_pieces(): last = lax.ppermute(block[:, :half], 'samp', ring)  2.82 us
    dot_general x2, matrix products, panel_scores(): lax.dot_general(probes, panel, (((1,), (1,)), ((), ())), preferred_elemen...  2.61 us
    ppermute x3, starting transfers between devices, gather_pieces(): pieces += [block, lax.ppermute(block, 'samp', twins)]  2.61 us
    ppermute x1, waiting for transfers between devices, gather_pieces(): other = lax.ppermute(own, 'samp', twins)  1.48 us
    ppermute x1, starting transfers between devices, gather_pieces(): last = lax.ppermute(block[:, :half], 'samp', ring)  1.46 us
    reduce_sum x1, other arithmetic, half_norms(): return 0.5 * jnp.sum(jnp.square(centered.astype(jnp.float32)), axis=1)  1.43 us
  transfers between devices with their start and end apart: 9, of which 6 were waited for; matrix products, arithmetic and copies ran while one was open for 1% of the time, Pallas kernels for 0%

profile of v2, /device:TPU:1, one launch (start us, length us, event | category | flops | bytes accessed | tf_op | source)
XLA Modules:
  0.0 45.1 jit_solution(16996358682179685948)
XLA Ops:
  0.0 1.0 %pad_maximum_fusion.1 = (bf16[2,16,4096]{2,1,0:T(8,128)(2,1)S(1)}, bf16[2,256,4096]{2,1,0:T(8,128)(2,1)S(1)}) fusion(bf16[1,16,4096]{2,1,0:T(8,128)(2,1)} %bitcast.33, bf16[1,16,4096]{2,1,0:T(8,128)(2,1)} %bitcast.35), kind=kLoop, calls=%fused_computation.21 | loop fusion | flops 524287 | bytes 786432 | tf_op jit(solution)/shard_map/stack | solution.py:64
  1.0 0.1 collective-permute-start
  1.1 1.5 %collective-permute-done = bf16[2,16,4096]{2,1,0:T(8,128)(2,1)S(1)} collective-permute-done((bf16[2,16,4096]{2,1,0:T(8,128)(2,1)S(1)}, bf16[2,16,4096]{2,1,0:T(8,128)(2,1)S(1)}, u32[]{:S(2)}, u32[]{:S(2)}) %collective-permute-start) | collective-permute-done | bytes 262176 | tf_op jit(solution)/shard_map/ppermute | solution.py:32
  2.6 1.0 %pad_maximum_fusion = bf16[2,32,4096]{2,1,0:T(8,128)(2,1)S(1)} fusion(bf16[2,16,4096]{2,1,0:T(8,128)(2,1)S(1)} %collective-permute-done, bf16[1,16,4096]{2,1,0:T(8,128)(2,1)} %bitcast.34, bf16[1,16,4096]{2,1,0:T(8,128)(2,1)} %bitcast.36), kind=kLoop, calls=%fused_computation.18 | loop fusion | flops 1572864 | bytes 1048576 | tf_op jit(solution)/shard_map/concatenate | solution.py:33
  3.6 2.4 %collective-permute-start.1 = (bf16[2,32,4096]{2,1,0:T(8,128)(2,1)S(1)}, bf16[2,32,4096]{2,1,0:T(8,128)(2,1)S(1)}, u32[]{:S(2)}, u32[]{:S(2)}) collective-permute-start(bf16[2,32,4096]{2,1,0:T(8,128)(2,1)S(1)} %pad_maximum_fusion), channel_id=1, source_target_pairs={{0,4},{1,3},{4,8},{5,1},{8,12},{9,5},{12,14},{13,9},{14,10},{15,13... | collective-permute-start | bytes 1572872 | tf_op jit(solution)/shard_map/ppermute | solution.py:37
  6.0 6.9 %collective-permute-done.1 = bf16[2,32,4096]{2,1,0:T(8,128)(2,1)S(1)} collective-permute-done((bf16[2,32,4096]{2,1,0:T(8,128)(2,1)S(1)}, bf16[2,32,4096]{2,1,0:T(8,128)(2,1)S(1)}, u32[]{:S(2)}, u32[]{:S(2)}) %collective-permute-start.1) | collective-permute-done | bytes 524320 | tf_op jit(solution)/shard_map/ppermute | solution.py:37
  13.0 0.9 %collective-permute-start.2 = (bf16[2,32,4096]{2,1,0:T(8,128)(2,1)S(1)}, bf16[2,32,4096]{2,1,0:T(8,128)(2,1)S(1)}, u32[]{:S(2)}, u32[]{:S(2)}) collective-permute-start(bf16[2,32,4096]{2,1,0:T(8,128)(2,1)S(1)} %collective-permute-done.1), channel_id=1, source_target_pairs={{0,1},{1,0},{2,3},{3,2},{4,5},{5,4},{6,7},{7,6},{8,9},{9,8},{10,11... | collective-permute-start | bytes 1572872 | tf_op jit(solution)/shard_map/ppermute | solution.py:38
  13.9 1.7 %collective-permute-start.3 = (bf16[2,32,4096]{2,1,0:T(8,128)(2,1)S(1)}, bf16[2,32,4096]{2,1,0:T(8,128)(2,1)S(1)}, u32[]{:S(2)}, u32[]{:S(2)}) collective-permute-start(bf16[2,32,4096]{2,1,0:T(8,128)(2,1)S(1)} %collective-permute-done.1), channel_id=1, source_target_pairs={{0,4},{1,3},{4,8},{5,1},{8,12},{9,5},{12,14},{13,9},{14,10},{15,13... | collective-permute-start | bytes 1572872 | tf_op jit(solution)/shard_map/ppermute | solution.py:37
  15.7 6.9 %collective-permute-done.3 = bf16[2,32,4096]{2,1,0:T(8,128)(2,1)S(1)} collective-permute-done((bf16[2,32,4096]{2,1,0:T(8,128)(2,1)S(1)}, bf16[2,32,4096]{2,1,0:T(8,128)(2,1)S(1)}, u32[]{:S(2)}, u32[]{:S(2)}) %collective-permute-start.3) | collective-permute-done | bytes 524320 | tf_op jit(solution)/shard_map/ppermute | solution.py:37
  22.5 0.5 %collective-permute-start.4 = (bf16[2,32,4096]{2,1,0:T(8,128)(2,1)S(1)}, bf16[2,32,4096]{2,1,0:T(8,128)(2,1)S(1)}, u32[]{:S(2)}, u32[]{:S(2)}) collective-permute-start(bf16[2,32,4096]{2,1,0:T(8,128)(2,1)S(1)} %collective-permute-done.3), channel_id=1, source_target_pairs={{0,1},{1,0},{2,3},{3,2},{4,5},{5,4},{6,7},{7,6},{8,9},{9,8},{10,11... | collective-permute-start | bytes 1572872 | tf_op jit(solution)/shard_map/ppermute | solution.py:38
  23.0 1.7 %collective-permute-start.5 = (bf16[2,32,4096]{2,1,0:T(8,128)(2,1)S(1)}, bf16[2,32,4096]{2,1,0:T(8,128)(2,1)S(1)}, u32[]{:S(2)}, u32[]{:S(2)}) collective-permute-start(bf16[2,32,4096]{2,1,0:T(8,128)(2,1)S(1)} %collective-permute-done.3), channel_id=1, source_target_pairs={{0,4},{1,3},{4,8},{5,1},{8,12},{9,5},{12,14},{13,9},{14,10},{15,13... | collective-permute-start | bytes 1572872 | tf_op jit(solution)/shard_map/ppermute | solution.py:37
  24.8 0.0 collective-permute-done.2
  24.9 6.8 %collective-permute-done.5 = bf16[2,32,4096]{2,1,0:T(8,128)(2,1)S(1)} collective-permute-done((bf16[2,32,4096]{2,1,0:T(8,128)(2,1)S(1)}, bf16[2,32,4096]{2,1,0:T(8,128)(2,1)S(1)}, u32[]{:S(2)}, u32[]{:S(2)}) %collective-permute-start.5) | collective-permute-done | bytes 524320 | tf_op jit(solution)/shard_map/ppermute | solution.py:37
  31.7 1.5 %collective-permute-start.7 = (bf16[2,16,4096]{2,1,0:T(8,128)(2,1)S(1)}, bf16[2,16,4096]{2,1,0:T(8,128)(2,1)S(1)}, u32[]{:S(2)}, u32[]{:S(2)}) collective-permute-start(bf16[2,16,4096]{2,1,0:T(8,128)(2,1)S(1)} %slice.12), channel_id=1, source_target_pairs={{0,4},{1,3},{4,8},{5,1},{8,12},{9,5},{12,14},{13,9},{14,10},{15,13... | collective-permute-start | bytes 786440 | tf_op jit(solution)/shard_map/ppermute | solution.py:41
  33.2 1.2 %collective-permute-start.6 = (bf16[2,32,4096]{2,1,0:T(8,128)(2,1)S(1)}, bf16[2,32,4096]{2,1,0:T(8,128)(2,1)S(1)}, u32[]{:S(2)}, u32[]{:S(2)}) collective-permute-start(bf16[2,32,4096]{2,1,0:T(8,128)(2,1)S(1)} %collective-permute-done.5), channel_id=1, source_target_pairs={{0,1},{1,0},{2,3},{3,2},{4,5},{5,4},{6,7},{7,6},{8,9},{9,8},{10,11... | collective-permute-start | bytes 1572872 | tf_op jit(solution)/shard_map/ppermute | solution.py:38
  34.4 0.0 collective-permute-done.4
  34.5 0.0 copy-start
  34.5 2.8 %collective-permute-done.7 = bf16[2,16,4096]{2,1,0:T(8,128)(2,1)S(1)} collective-permute-done((bf16[2,16,4096]{2,1,0:T(8,128)(2,1)S(1)}, bf16[2,16,4096]{2,1,0:T(8,128)(2,1)S(1)}, u32[]{:S(2)}, u32[]{:S(2)}) %collective-permute-start.7) | collective-permute-done | bytes 262176 | tf_op jit(solution)/shard_map/ppermute | solution.py:41
  37.3 1.4 %collective-permute-start.8 = (bf16[2,16,4096]{2,1,0:T(8,128)(2,1)S(1)}, bf16[2,16,4096]{2,1,0:T(8,128)(2,1)S(1)}, u32[]{:S(2)}, u32[]{:S(2)}) collective-permute-start(bf16[2,16,4096]{2,1,0:T(8,128)(2,1)S(1)} %collective-permute-done.7), channel_id=1, source_target_pairs={{0,1},{1,0},{2,3},{3,2},{4,5},{5,4},{6,7},{7,6},{8,9},{9,8},{10,11... | collective-permute-start | bytes 786440 | tf_op jit(solution)/shard_map/ppermute | solution.py:42
  38.7 0.0 collective-permute-done.6
  38.7 1.1 %collective-permute-done.8 = bf16[2,16,4096]{2,1,0:T(8,128)(2,1)S(1)} collective-permute-done((bf16[2,16,4096]{2,1,0:T(8,128)(2,1)S(1)}, bf16[2,16,4096]{2,1,0:T(8,128)(2,1)S(1)}, u32[]{:S(2)}, u32[]{:S(2)}) %collective-permute-start.8) | collective-permute-done | bytes 262176 | tf_op jit(solution)/shard_map/ppermute | solution.py:42
  39.9 0.3 convert_reduce_fusion
  40.2 1.4 %multiply_reduce_fusion.1 = (f32[256]{0:T(256)S(1)}, f32[256]{0:T(256)S(1)}) fusion(f32[4096]{0:T(1024)S(1)} %broadcast_multiply_fusion, bf16[2,256,4096]{2,1,0:T(8,128)(2,1)S(1)} %constant_dynamic-update-slice_fusion), kind=kLoop, calls=%fused_computation.10 | loop fusion | flops 14679552 | bytes 4212736 | tf_op jit(solution)/shard_map/reduce_sum | solution.py:52
  41.7 0.0 copy-done
  41.7 1.3 %fusion.22 = (f32[512]{0:T(512)S(1)}, f32[512,256]{0,1:T(8,128)S(1)}) fusion(f32[256]{0:T(256)S(1)} %get-tuple-element.14, bf16[2,256,4096]{2,1,0:T(8,128)(2,1)S(1)} %constant_dynamic-update-slice_fusion, f32[4096]{0:T(1024)S(1)} %broadcast_multiply_fusion, bf16[512,4096]{1,0:T(8,128)(2,1)S(1)} %copy-done), kind=kOutput, calls=%fused_computation.39 | convolution fusion | flops 1086717440 | bytes 6851584 | tf_op jit(solution)/shard_map/dot_general | solution.py:56
  43.0 1.3 %fusion.21 = (f32[512]{0:T(512)S(1)}, f32[512,256]{0,1:T(8,128)S(1)}) fusion(f32[256]{0:T(256)S(1)} %get-tuple-element.13, f32[4096]{0:T(1024)S(1)} %broadcast_multiply_fusion, bf16[2,256,4096]{2,1,0:T(8,128)(2,1)S(1)} %constant_dynamic-update-slice_fusion, bf16[512,4096]{1,0:T(8,128)(2,1)S(1)} %copy-done), kind=kOutput, calls=%fused_computation.38 | convolution fusion | flops 1086717440 | bytes 6851584 | tf_op jit(solution)/shard_map/dot_general | solution.py:56
  44.3 0.1 exponential_reduce_fusion.1
  44.4 0.1 exponential_reduce_fusion
  44.5 0.6 %add_subtract_fusion = f32[512]{0:T(512)} fusion(f32[512]{0:T(512)S(1)} %exponential_reduce_fusion, f32[512]{0:T(512)S(1)} %exponential_reduce_fusion.1, f32[512]{0:T(512)S(1)} %get-tuple-element.11, f32[512]{0:T(512)S(1)} %get-tuple-element.9), kind=kLoop, calls=%fused_computation.35 | loop fusion | flops 4608 | bytes 10240 | tf_op jit(solution)/shard_map/sub | solution.py:73
  (14 shorter events, 0.3 us)
Async XLA Ops:
  1.0 1.6 %collective-permute-start = (bf16[2,16,4096]{2,1,0:T(8,128)(2,1)S(1)}, bf16[2,16,4096]{2,1,0:T(8,128)(2,1)S(1)}, u32[]{:S(2)}, u32[]{:S(2)}) collective-permute-start(bf16[2,16,4096]{2,1,0:T(8,128)(2,1)S(1)} %get-tuple-element.7), channel_id=1, source_target_pairs={{0,1},{1,0},{2,3},{3,2},{4,5},{5,4},{6,7},{7,6},{8,9},{9,8},{10,11... | collective-permute-start | bytes 786440 | tf_op jit(solution)/shard_map/ppermute | solution.py:32
  3.6 9.3 %collective-permute-start.1 = (bf16[2,32,4096]{2,1,0:T(8,128)(2,1)S(1)}, bf16[2,32,4096]{2,1,0:T(8,128)(2,1)S(1)}, u32[]{:S(2)}, u32[]{:S(2)}) collective-permute-start(bf16[2,32,4096]{2,1,0:T(8,128)(2,1)S(1)} %pad_maximum_fusion), channel_id=1, source_target_pairs={{0,4},{1,3},{4,8},{5,1},{8,12},{9,5},{12,14},{13,9},{14,10},{15,13... | collective-permute-start | bytes 1572872 | tf_op jit(solution)/shard_map/ppermute | solution.py:37
  13.0 11.8 %collective-permute-start.2 = (bf16[2,32,4096]{2,1,0:T(8,128)(2,1)S(1)}, bf16[2,32,4096]{2,1,0:T(8,128)(2,1)S(1)}, u32[]{:S(2)}, u32[]{:S(2)}) collective-permute-start(bf16[2,32,4096]{2,1,0:T(8,128)(2,1)S(1)} %collective-permute-done.1), channel_id=1, source_target_pairs={{0,1},{1,0},{2,3},{3,2},{4,5},{5,4},{6,7},{7,6},{8,9},{9,8},{10,11... | collective-permute-start | bytes 1572872 | tf_op jit(solution)/shard_map/ppermute | solution.py:38
  13.9 8.7 %collective-permute-start.3 = (bf16[2,32,4096]{2,1,0:T(8,128)(2,1)S(1)}, bf16[2,32,4096]{2,1,0:T(8,128)(2,1)S(1)}, u32[]{:S(2)}, u32[]{:S(2)}) collective-permute-start(bf16[2,32,4096]{2,1,0:T(8,128)(2,1)S(1)} %collective-permute-done.1), channel_id=1, source_target_pairs={{0,4},{1,3},{4,8},{5,1},{8,12},{9,5},{12,14},{13,9},{14,10},{15,13... | collective-permute-start | bytes 1572872 | tf_op jit(solution)/shard_map/ppermute | solution.py:37
  22.5 11.9 %collective-permute-start.4 = (bf16[2,32,4096]{2,1,0:T(8,128)(2,1)S(1)}, bf16[2,32,4096]{2,1,0:T(8,128)(2,1)S(1)}, u32[]{:S(2)}, u32[]{:S(2)}) collective-permute-start(bf16[2,32,4096]{2,1,0:T(8,128)(2,1)S(1)} %collective-permute-done.3), channel_id=1, source_target_pairs={{0,1},{1,0},{2,3},{3,2},{4,5},{5,4},{6,7},{7,6},{8,9},{9,8},{10,11... | collective-permute-start | bytes 1572872 | tf_op jit(solution)/shard_map/ppermute | solution.py:38
  23.0 8.7 %collective-permute-start.5 = (bf16[2,32,4096]{2,1,0:T(8,128)(2,1)S(1)}, bf16[2,32,4096]{2,1,0:T(8,128)(2,1)S(1)}, u32[]{:S(2)}, u32[]{:S(2)}) collective-permute-start(bf16[2,32,4096]{2,1,0:T(8,128)(2,1)S(1)} %collective-permute-done.3), channel_id=1, source_target_pairs={{0,4},{1,3},{4,8},{5,1},{8,12},{9,5},{12,14},{13,9},{14,10},{15,13... | collective-permute-start | bytes 1572872 | tf_op jit(solution)/shard_map/ppermute | solution.py:37
  31.7 5.6 %collective-permute-start.7 = (bf16[2,16,4096]{2,1,0:T(8,128)(2,1)S(1)}, bf16[2,16,4096]{2,1,0:T(8,128)(2,1)S(1)}, u32[]{:S(2)}, u32[]{:S(2)}) collective-permute-start(bf16[2,16,4096]{2,1,0:T(8,128)(2,1)S(1)} %slice.12), channel_id=1, source_target_pairs={{0,4},{1,3},{4,8},{5,1},{8,12},{9,5},{12,14},{13,9},{14,10},{15,13... | collective-permute-start | bytes 786440 | tf_op jit(solution)/shard_map/ppermute | solution.py:41
  33.2 5.5 %collective-permute-start.6 = (bf16[2,32,4096]{2,1,0:T(8,128)(2,1)S(1)}, bf16[2,32,4096]{2,1,0:T(8,128)(2,1)S(1)}, u32[]{:S(2)}, u32[]{:S(2)}) collective-permute-start(bf16[2,32,4096]{2,1,0:T(8,128)(2,1)S(1)} %collective-permute-done.5), channel_id=1, source_target_pairs={{0,1},{1,0},{2,3},{3,2},{4,5},{5,4},{6,7},{7,6},{8,9},{9,8},{10,11... | collective-permute-start | bytes 1572872 | tf_op jit(solution)/shard_map/ppermute | solution.py:38
  34.5 7.2 %copy-start = (bf16[512,4096]{1,0:T(8,128)(2,1)S(1)}, bf16[512,4096]{1,0:T(8,128)(2,1)}, u32[]{:S(2)}) copy-start(bf16[512,4096]{1,0:T(8,128)(2,1)} %param.3) | copy-start | bytes 12582916
  37.3 2.5 %collective-permute-start.8 = (bf16[2,16,4096]{2,1,0:T(8,128)(2,1)S(1)}, bf16[2,16,4096]{2,1,0:T(8,128)(2,1)S(1)}, u32[]{:S(2)}, u32[]{:S(2)}) collective-permute-start(bf16[2,16,4096]{2,1,0:T(8,128)(2,1)S(1)} %collective-permute-done.7), channel_id=1, source_target_pairs={{0,1},{1,0},{2,3},{3,2},{4,5},{5,4},{6,7},{7,6},{8,9},{9,8},{10,11... | collective-permute-start | bytes 786440 | tf_op jit(solution)/shard_map/ppermute | solution.py:42

commit v3 on v2

--- a/solution.py
+++ b/solution.py
@@ -28,18 +28,24 @@
 def gather_pieces(own, size):
     twins, ring = core_pairs(size), ring_pairs(size)
     chips = size // 2
-    core = lax.axis_index("samp") % 2
-    other = lax.ppermute(own, "samp", twins)
-    block = jnp.concatenate([own, other], axis=1)
-    pieces = [block]
+
+    def hop(block):
+        return lax.ppermute(block, "samp", ring)
+
+    def hand_over(block):
+        return lax.ppermute(block, "samp", twins)
+
     steps = (chips - 1) // 2
+    mine = own
+    pieces = [own]
+    other = hand_over(own)
+    pieces.append(other)
     for _ in range(steps):
-        block = lax.ppermute(block, "samp", ring)
-        pieces += [block, lax.ppermute(block, "samp", twins)]
+        mine, other = hop(mine), hop(other)
+        pieces += [mine, other, hand_over(mine), hand_over(other)]
     if chips % 2 == 0:
-        half = block.shape[1] // 2
-        last = lax.ppermute(block[:, :half], "samp", ring)
-        pieces += [last, lax.ppermute(last, "samp", twins)]
+        mine = hop(mine)
+        pieces += [mine, hand_over(mine)]
     return pieces
 
 

time: 45.6 us -> 40.1 us (0.88)
  waiting for transfers between devices: 26 us -> 16.4 us
  starting transfers between devices: 11.5 us -> 16.5 us
  other arithmetic: 4.61 us -> 3.61 us
    ppermute x9 -> x15, waiting for transfers between devices: 26 us -> 16.4 us  [the longest x7 15.4 us: hop(): return lax.ppermute(block, 'samp', ring)]
    ppermute x9 -> x15, starting transfers between devices: 11.5 us -> 16.5 us  [the longest x7 11.3 us: hop(): return lax.ppermute(block, 'samp', ring)]
    concatenate x1 -> x0, other arithmetic: 1 us -> none  [gather_pieces(): block = jnp.concatenate([own, other], axis=1)]
  transfers between devices with their start and end apart: 9 -> 15, of which waited for: 6 -> 7; matrix products, arithmetic and copies ran while one was open for 1% -> 1% of each run, Pallas kernels for 0% -> 0%
where the time goes in v3:
time: 40.1 us; the launch traced here: 39.6 us
  starting transfers between devices  16.5 us (41%)
  waiting for transfers between devices  16.4 us (41%)
  other arithmetic  3.61 us (9%)
  matrix products  2.61 us (7%)
    ppermute x7, waiting for transfers between devices, hop(): return lax.ppermute(block, 'samp', ring)  15.4 us
    ppermute x7, starting transfers between devices, hop(): return lax.ppermute(block, 'samp', ring)  11.3 us
    ppermute x8, starting transfers between devices, hand_over(): return lax.ppermute(block, 'samp', twins)  5.17 us
    dot_general x2, matrix products, panel_scores(): lax.dot_general(probes, panel, (((1,), (1,)), ((), ())), preferred_elemen...  2.61 us
    reduce_sum x1, other arithmetic, half_norms(): return 0.5 * jnp.sum(jnp.square(centered.astype(jnp.float32)), axis=1)  1.43 us
    ppermute x8, waiting for transfers between devices, hand_over(): return lax.ppermute(block, 'samp', twins)  1.04 us
    another operation x1, other arithmetic, body(): pieces = gather_pieces(jnp.stack([ref_panel, gen_panel]), size)  1 us
  transfers between devices with their start and end apart: 15, of which 7 were waited for; matrix products, arithmetic and copies ran while one was open for 1% of the time, Pallas kernels for 0%

profile of v3, /device:TPU:1, one launch (start us, length us, event | category | flops | bytes accessed | tf_op | source)
XLA Modules:
  0.0 39.6 jit_solution(12260806348284129485)
XLA Ops:
  0.0 1.0 %pad_maximum_fusion = (bf16[2,16,4096]{2,1,0:T(8,128)(2,1)S(1)}, bf16[2,256,4096]{2,1,0:T(8,128)(2,1)S(1)}) fusion(bf16[1,16,4096]{2,1,0:T(8,128)(2,1)} %bitcast.33, bf16[1,16,4096]{2,1,0:T(8,128)(2,1)} %bitcast.34), kind=kLoop, calls=%fused_computation.20 | loop fusion | flops 524287 | bytes 786432 | tf_op jit(solution)/shard_map/stack | solution.py:70
  1.0 2.1 %collective-permute-start.1 = (bf16[2,16,4096]{2,1,0:T(8,128)(2,1)S(1)}, bf16[2,16,4096]{2,1,0:T(8,128)(2,1)S(1)}, u32[]{:S(2)}, u32[]{:S(2)}) collective-permute-start(bf16[2,16,4096]{2,1,0:T(8,128)(2,1)S(1)} %get-tuple-element.7), channel_id=1, source_target_pairs={{0,4},{1,3},{4,8},{5,1},{8,12},{9,5},{12,14},{13,9},{14,10},{15,13... | collective-permute-start | bytes 786440 | tf_op jit(solution)/shard_map/ppermute | solution.py:33
  3.1 1.0 %collective-permute-start = (bf16[2,16,4096]{2,1,0:T(8,128)(2,1)S(1)}, bf16[2,16,4096]{2,1,0:T(8,128)(2,1)S(1)}, u32[]{:S(2)}, u32[]{:S(2)}) collective-permute-start(bf16[2,16,4096]{2,1,0:T(8,128)(2,1)S(1)} %get-tuple-element.7), channel_id=1, source_target_pairs={{0,1},{1,0},{2,3},{3,2},{4,5},{5,4},{6,7},{7,6},{8,9},{9,8},{10,11... | collective-permute-start | bytes 786440 | tf_op jit(solution)/shard_map/ppermute | solution.py:36
  4.1 3.1 %collective-permute-done.1 = bf16[2,16,4096]{2,1,0:T(8,128)(2,1)S(1)} collective-permute-done((bf16[2,16,4096]{2,1,0:T(8,128)(2,1)S(1)}, bf16[2,16,4096]{2,1,0:T(8,128)(2,1)S(1)}, u32[]{:S(2)}, u32[]{:S(2)}) %collective-permute-start.1) | collective-permute-done | bytes 262176 | tf_op jit(solution)/shard_map/ppermute | solution.py:33
  7.2 1.2 %collective-permute-start.3 = (bf16[2,16,4096]{2,1,0:T(8,128)(2,1)S(1)}, bf16[2,16,4096]{2,1,0:T(8,128)(2,1)S(1)}, u32[]{:S(2)}, u32[]{:S(2)}) collective-permute-start(bf16[2,16,4096]{2,1,0:T(8,128)(2,1)S(1)} %collective-permute-done.1), channel_id=1, source_target_pairs={{0,1},{1,0},{2,3},{3,2},{4,5},{5,4},{6,7},{7,6},{8,9},{9,8},{10,11... | collective-permute-start | bytes 786440 | tf_op jit(solution)/shard_map/ppermute | solution.py:36
  8.4 1.7 %collective-permute-start.5 = (bf16[2,16,4096]{2,1,0:T(8,128)(2,1)S(1)}, bf16[2,16,4096]{2,1,0:T(8,128)(2,1)S(1)}, u32[]{:S(2)}, u32[]{:S(2)}) collective-permute-start(bf16[2,16,4096]{2,1,0:T(8,128)(2,1)S(1)} %collective-permute-done.1), channel_id=1, source_target_pairs={{0,4},{1,3},{4,8},{5,1},{8,12},{9,5},{12,14},{13,9},{14,10},{15,13... | collective-permute-start | bytes 786440 | tf_op jit(solution)/shard_map/ppermute | solution.py:33
  10.2 0.0 collective-permute-done
  10.2 1.3 %collective-permute-start.2 = (bf16[2,16,4096]{2,1,0:T(8,128)(2,1)S(1)}, bf16[2,16,4096]{2,1,0:T(8,128)(2,1)S(1)}, u32[]{:S(2)}, u32[]{:S(2)}) collective-permute-start(bf16[2,16,4096]{2,1,0:T(8,128)(2,1)S(1)} %collective-permute-done), channel_id=1, source_target_pairs={{0,4},{1,3},{4,8},{5,1},{8,12},{9,5},{12,14},{13,9},{14,10},{15,13... | collective-permute-start | bytes 786440 | tf_op jit(solution)/shard_map/ppermute | solution.py:33
  11.5 5.6 %collective-permute-done.2 = bf16[2,16,4096]{2,1,0:T(8,128)(2,1)S(1)} collective-permute-done((bf16[2,16,4096]{2,1,0:T(8,128)(2,1)S(1)}, bf16[2,16,4096]{2,1,0:T(8,128)(2,1)S(1)}, u32[]{:S(2)}, u32[]{:S(2)}) %collective-permute-start.2) | collective-permute-done | bytes 262176 | tf_op jit(solution)/shard_map/ppermute | solution.py:33
  17.1 0.5 %collective-permute-start.4 = (bf16[2,16,4096]{2,1,0:T(8,128)(2,1)S(1)}, bf16[2,16,4096]{2,1,0:T(8,128)(2,1)S(1)}, u32[]{:S(2)}, u32[]{:S(2)}) collective-permute-start(bf16[2,16,4096]{2,1,0:T(8,128)(2,1)S(1)} %collective-permute-done.2), channel_id=1, source_target_pairs={{0,1},{1,0},{2,3},{3,2},{4,5},{5,4},{6,7},{7,6},{8,9},{9,8},{10,11... | collective-permute-start | bytes 786440 | tf_op jit(solution)/shard_map/ppermute | solution.py:36
  17.6 1.7 %collective-permute-start.6 = (bf16[2,16,4096]{2,1,0:T(8,128)(2,1)S(1)}, bf16[2,16,4096]{2,1,0:T(8,128)(2,1)S(1)}, u32[]{:S(2)}, u32[]{:S(2)}) collective-permute-start(bf16[2,16,4096]{2,1,0:T(8,128)(2,1)S(1)} %collective-permute-done.2), channel_id=1, source_target_pairs={{0,4},{1,3},{4,8},{5,1},{8,12},{9,5},{12,14},{13,9},{14,10},{15,13... | collective-permute-start | bytes 786440 | tf_op jit(solution)/shard_map/ppermute | solution.py:33
  19.4 0.0 collective-permute-done.5
  19.4 0.3 collective-permute-start.7
  19.7 1.0 %collective-permute-start.9 = (bf16[2,16,4096]{2,1,0:T(8,128)(2,1)S(1)}, bf16[2,16,4096]{2,1,0:T(8,128)(2,1)S(1)}, u32[]{:S(2)}, u32[]{:S(2)}) collective-permute-start(bf16[2,16,4096]{2,1,0:T(8,128)(2,1)S(1)} %collective-permute-done.5), channel_id=1, source_target_pairs={{0,4},{1,3},{4,8},{5,1},{8,12},{9,5},{12,14},{13,9},{14,10},{15,13... | collective-permute-start | bytes 786440 | tf_op jit(solution)/shard_map/ppermute | solution.py:33
  20.7 0.0 collective-permute-done.3
  20.7 2.7 %collective-permute-done.6 = bf16[2,16,4096]{2,1,0:T(8,128)(2,1)S(1)} collective-permute-done((bf16[2,16,4096]{2,1,0:T(8,128)(2,1)S(1)}, bf16[2,16,4096]{2,1,0:T(8,128)(2,1)S(1)}, u32[]{:S(2)}, u32[]{:S(2)}) %collective-permute-start.6) | collective-permute-done | bytes 262176 | tf_op jit(solution)/shard_map/ppermute | solution.py:33
  23.5 0.5 %collective-permute-start.8 = (bf16[2,16,4096]{2,1,0:T(8,128)(2,1)S(1)}, bf16[2,16,4096]{2,1,0:T(8,128)(2,1)S(1)}, u32[]{:S(2)}, u32[]{:S(2)}) collective-permute-start(bf16[2,16,4096]{2,1,0:T(8,128)(2,1)S(1)} %collective-permute-done.6), channel_id=1, source_target_pairs={{0,1},{1,0},{2,3},{3,2},{4,5},{5,4},{6,7},{7,6},{8,9},{9,8},{10,11... | collective-permute-start | bytes 786440 | tf_op jit(solution)/shard_map/ppermute | solution.py:36
  24.0 1.7 %collective-permute-start.10 = (bf16[2,16,4096]{2,1,0:T(8,128)(2,1)S(1)}, bf16[2,16,4096]{2,1,0:T(8,128)(2,1)S(1)}, u32[]{:S(2)}, u32[]{:S(2)}) collective-permute-start(bf16[2,16,4096]{2,1,0:T(8,128)(2,1)S(1)} %collective-permute-done.6), channel_id=1, source_target_pairs={{0,4},{1,3},{4,8},{5,1},{8,12},{9,5},{12,14},{13,9},{14,10},{15,13... | collective-permute-start | bytes 786440 | tf_op jit(solution)/shard_map/ppermute | solution.py:33
  25.7 0.5 %collective-permute-done.9 = bf16[2,16,4096]{2,1,0:T(8,128)(2,1)S(1)} collective-permute-done((bf16[2,16,4096]{2,1,0:T(8,128)(2,1)S(1)}, bf16[2,16,4096]{2,1,0:T(8,128)(2,1)S(1)}, u32[]{:S(2)}, u32[]{:S(2)}) %collective-permute-start.9) | collective-permute-done | bytes 262176 | tf_op jit(solution)/shard_map/ppermute | solution.py:33
  26.3 0.5 %collective-permute-start.11 = (bf16[2,16,4096]{2,1,0:T(8,128)(2,1)S(1)}, bf16[2,16,4096]{2,1,0:T(8,128)(2,1)S(1)}, u32[]{:S(2)}, u32[]{:S(2)}) collective-permute-start(bf16[2,16,4096]{2,1,0:T(8,128)(2,1)S(1)} %collective-permute-done.9), channel_id=1, source_target_pairs={{0,1},{1,0},{2,3},{3,2},{4,5},{5,4},{6,7},{7,6},{8,9},{9,8},{10,11... | collective-permute-start | bytes 786440 | tf_op jit(solution)/shard_map/ppermute | solution.py:36
  26.8 0.0 collective-permute-done.4
  26.8 1.7 %collective-permute-start.13 = (bf16[2,16,4096]{2,1,0:T(8,128)(2,1)S(1)}, bf16[2,16,4096]{2,1,0:T(8,128)(2,1)S(1)}, u32[]{:S(2)}, u32[]{:S(2)}) collective-permute-start(bf16[2,16,4096]{2,1,0:T(8,128)(2,1)S(1)} %collective-permute-done.9), channel_id=1, source_target_pairs={{0,4},{1,3},{4,8},{5,1},{8,12},{9,5},{12,14},{13,9},{14,10},{15,13... | collective-permute-start | bytes 786440 | tf_op jit(solution)/shard_map/ppermute | solution.py:33
  28.6 0.0 collective-permute-done.7
  28.7 1.2 %collective-permute-done.10 = bf16[2,16,4096]{2,1,0:T(8,128)(2,1)S(1)} collective-permute-done((bf16[2,16,4096]{2,1,0:T(8,128)(2,1)S(1)}, bf16[2,16,4096]{2,1,0:T(8,128)(2,1)S(1)}, u32[]{:S(2)}, u32[]{:S(2)}) %collective-permute-start.10) | collective-permute-done | bytes 262176 | tf_op jit(solution)/shard_map/ppermute | solution.py:33
  29.8 0.5 %collective-permute-start.12 = (bf16[2,16,4096]{2,1,0:T(8,128)(2,1)S(1)}, bf16[2,16,4096]{2,1,0:T(8,128)(2,1)S(1)}, u32[]{:S(2)}, u32[]{:S(2)}) collective-permute-start(bf16[2,16,4096]{2,1,0:T(8,128)(2,1)S(1)} %collective-permute-done.10), channel_id=1, source_target_pairs={{0,1},{1,0},{2,3},{3,2},{4,5},{5,4},{6,7},{7,6},{8,9},{9,8},{10,11... | collective-permute-start | bytes 786440 | tf_op jit(solution)/shard_map/ppermute | solution.py:36
  30.4 0.0 collective-permute-done.8
  30.4 2.2 %collective-permute-done.13 = bf16[2,16,4096]{2,1,0:T(8,128)(2,1)S(1)} collective-permute-done((bf16[2,16,4096]{2,1,0:T(8,128)(2,1)S(1)}, bf16[2,16,4096]{2,1,0:T(8,128)(2,1)S(1)}, u32[]{:S(2)}, u32[]{:S(2)}) %collective-permute-start.13) | collective-permute-done | bytes 262176 | tf_op jit(solution)/shard_map/ppermute | solution.py:33
  32.7 0.5 %collective-permute-start.14 = (bf16[2,16,4096]{2,1,0:T(8,128)(2,1)S(1)}, bf16[2,16,4096]{2,1,0:T(8,128)(2,1)S(1)}, u32[]{:S(2)}, u32[]{:S(2)}) collective-permute-start(bf16[2,16,4096]{2,1,0:T(8,128)(2,1)S(1)} %collective-permute-done.13), channel_id=1, source_target_pairs={{0,1},{1,0},{2,3},{3,2},{4,5},{5,4},{6,7},{7,6},{8,9},{9,8},{10,11... | collective-permute-start | bytes 786440 | tf_op jit(solution)/shard_map/ppermute | solution.py:36
  33.2 0.0 copy-start
  33.2 0.0 collective-permute-done.11
  33.3 0.0 collective-permute-done.12
  33.3 1.0 %collective-permute-done.14 = bf16[2,16,4096]{2,1,0:T(8,128)(2,1)S(1)} collective-permute-done((bf16[2,16,4096]{2,1,0:T(8,128)(2,1)S(1)}, bf16[2,16,4096]{2,1,0:T(8,128)(2,1)S(1)}, u32[]{:S(2)}, u32[]{:S(2)}) %collective-permute-start.14) | collective-permute-done | bytes 262176 | tf_op jit(solution)/shard_map/ppermute | solution.py:36
  34.4 0.3 convert_reduce_fusion
  34.7 1.4 %multiply_reduce_fusion.1 = (f32[256]{0:T(256)S(1)}, f32[256]{0:T(256)S(1)}) fusion(f32[4096]{0:T(1024)S(1)} %broadcast_multiply_fusion, bf16[2,256,4096]{2,1,0:T(8,128)(2,1)S(1)} %constant_dynamic-update-slice_fusion), kind=kLoop, calls=%fused_computation.10 | loop fusion | flops 14679552 | bytes 4212736 | tf_op jit(solution)/shard_map/reduce_sum | solution.py:58
  36.2 0.0 copy-done
  36.2 1.3 %fusion.22 = (f32[512]{0:T(512)S(1)}, f32[512,256]{0,1:T(8,128)S(1)}) fusion(f32[256]{0:T(256)S(1)} %get-tuple-element.14, bf16[2,256,4096]{2,1,0:T(8,128)(2,1)S(1)} %constant_dynamic-update-slice_fusion, f32[4096]{0:T(1024)S(1)} %broadcast_multiply_fusion, bf16[512,4096]{1,0:T(8,128)(2,1)S(1)} %copy-done), kind=kOutput, calls=%fused_computation.44 | convolution fusion | flops 1086717440 | bytes 6851584 | tf_op jit(solution)/shard_map/dot_general | solution.py:62
  37.5 1.3 %fusion.21 = (f32[512]{0:T(512)S(1)}, f32[512,256]{0,1:T(8,128)S(1)}) fusion(f32[256]{0:T(256)S(1)} %get-tuple-element.13, f32[4096]{0:T(1024)S(1)} %broadcast_multiply_fusion, bf16[2,256,4096]{2,1,0:T(8,128)(2,1)S(1)} %constant_dynamic-update-slice_fusion, bf16[512,4096]{1,0:T(8,128)(2,1)S(1)} %copy-done), kind=kOutput, calls=%fused_computation.43 | convolution fusion | flops 1086717440 | bytes 6851584 | tf_op jit(solution)/shard_map/dot_general | solution.py:62
  38.8 0.1 exponential_reduce_fusion.1
  38.9 0.1 exponential_reduce_fusion
  39.0 0.6 %add_subtract_fusion = f32[512]{0:T(512)} fusion(f32[512]{0:T(512)S(1)} %exponential_reduce_fusion, f32[512]{0:T(512)S(1)} %exponential_reduce_fusion.1, f32[512]{0:T(512)S(1)} %get-tuple-element.11, f32[512]{0:T(512)S(1)} %get-tuple-element.9), kind=kLoop, calls=%fused_computation.40 | loop fusion | flops 4608 | bytes 10240 | tf_op jit(solution)/shard_map/sub | solution.py:79
  (19 shorter events, 0.3 us)
Async XLA Ops:
  1.0 6.2 %collective-permute-start.1 = (bf16[2,16,4096]{2,1,0:T(8,128)(2,1)S(1)}, bf16[2,16,4096]{2,1,0:T(8,128)(2,1)S(1)}, u32[]{:S(2)}, u32[]{:S(2)}) collective-permute-start(bf16[2,16,4096]{2,1,0:T(8,128)(2,1)S(1)} %get-tuple-element.7), channel_id=1, source_target_pairs={{0,4},{1,3},{4,8},{5,1},{8,12},{9,5},{12,14},{13,9},{14,10},{15,13... | collective-permute-start | bytes 786440 | tf_op jit(solution)/shard_map/ppermute | solution.py:33
  3.1 7.1 %collective-permute-start = (bf16[2,16,4096]{2,1,0:T(8,128)(2,1)S(1)}, bf16[2,16,4096]{2,1,0:T(8,128)(2,1)S(1)}, u32[]{:S(2)}, u32[]{:S(2)}) collective-permute-start(bf16[2,16,4096]{2,1,0:T(8,128)(2,1)S(1)} %get-tuple-element.7), channel_id=1, source_target_pairs={{0,1},{1,0},{2,3},{3,2},{4,5},{5,4},{6,7},{7,6},{8,9},{9,8},{10,11... | collective-permute-start | bytes 786440 | tf_op jit(solution)/shard_map/ppermute | solution.py:36
  7.2 13.4 %collective-permute-start.3 = (bf16[2,16,4096]{2,1,0:T(8,128)(2,1)S(1)}, bf16[2,16,4096]{2,1,0:T(8,128)(2,1)S(1)}, u32[]{:S(2)}, u32[]{:S(2)}) collective-permute-start(bf16[2,16,4096]{2,1,0:T(8,128)(2,1)S(1)} %collective-permute-done.1), channel_id=1, source_target_pairs={{0,1},{1,0},{2,3},{3,2},{4,5},{5,4},{6,7},{7,6},{8,9},{9,8},{10,11... | collective-permute-start | bytes 786440 | tf_op jit(solution)/shard_map/ppermute | solution.py:36
  8.4 10.9 %collective-permute-start.5 = (bf16[2,16,4096]{2,1,0:T(8,128)(2,1)S(1)}, bf16[2,16,4096]{2,1,0:T(8,128)(2,1)S(1)}, u32[]{:S(2)}, u32[]{:S(2)}) collective-permute-start(bf16[2,16,4096]{2,1,0:T(8,128)(2,1)S(1)} %collective-permute-done.1), channel_id=1, source_target_pairs={{0,4},{1,3},{4,8},{5,1},{8,12},{9,5},{12,14},{13,9},{14,10},{15,13... | collective-permute-start | bytes 786440 | tf_op jit(solution)/shard_map/ppermute | solution.py:33
  10.2 6.9 %collective-permute-start.2 = (bf16[2,16,4096]{2,1,0:T(8,128)(2,1)S(1)}, bf16[2,16,4096]{2,1,0:T(8,128)(2,1)S(1)}, u32[]{:S(2)}, u32[]{:S(2)}) collective-permute-start(bf16[2,16,4096]{2,1,0:T(8,128)(2,1)S(1)} %collective-permute-done), channel_id=1, source_target_pairs={{0,4},{1,3},{4,8},{5,1},{8,12},{9,5},{12,14},{13,9},{14,10},{15,13... | collective-permute-start | bytes 786440 | tf_op jit(solution)/shard_map/ppermute | solution.py:33
  17.1 9.7 %collective-permute-start.4 = (bf16[2,16,4096]{2,1,0:T(8,128)(2,1)S(1)}, bf16[2,16,4096]{2,1,0:T(8,128)(2,1)S(1)}, u32[]{:S(2)}, u32[]{:S(2)}) collective-permute-start(bf16[2,16,4096]{2,1,0:T(8,128)(2,1)S(1)} %collective-permute-done.2), channel_id=1, source_target_pairs={{0,1},{1,0},{2,3},{3,2},{4,5},{5,4},{6,7},{7,6},{8,9},{9,8},{10,11... | collective-permute-start | bytes 786440 | tf_op jit(solution)/shard_map/ppermute | solution.py:36
  17.6 5.9 %collective-permute-start.6 = (bf16[2,16,4096]{2,1,0:T(8,128)(2,1)S(1)}, bf16[2,16,4096]{2,1,0:T(8,128)(2,1)S(1)}, u32[]{:S(2)}, u32[]{:S(2)}) collective-permute-start(bf16[2,16,4096]{2,1,0:T(8,128)(2,1)S(1)} %collective-permute-done.2), channel_id=1, source_target_pairs={{0,4},{1,3},{4,8},{5,1},{8,12},{9,5},{12,14},{13,9},{14,10},{15,13... | collective-permute-start | bytes 786440 | tf_op jit(solution)/shard_map/ppermute | solution.py:33
  19.4 9.3 %collective-permute-start.7 = (bf16[2,16,4096]{2,1,0:T(8,128)(2,1)S(1)}, bf16[2,16,4096]{2,1,0:T(8,128)(2,1)S(1)}, u32[]{:S(2)}, u32[]{:S(2)}) collective-permute-start(bf16[2,16,4096]{2,1,0:T(8,128)(2,1)S(1)} %collective-permute-done.5), channel_id=1, source_target_pairs={{0,1},{1,0},{2,3},{3,2},{4,5},{5,4},{6,7},{7,6},{8,9},{9,8},{10,11... | collective-permute-start | bytes 786440 | tf_op jit(solution)/shard_map/ppermute | solution.py:36
  19.7 6.6 %collective-permute-start.9 = (bf16[2,16,4096]{2,1,0:T(8,128)(2,1)S(1)}, bf16[2,16,4096]{2,1,0:T(8,128)(2,1)S(1)}, u32[]{:S(2)}, u32[]{:S(2)}) collective-permute-start(bf16[2,16,4096]{2,1,0:T(8,128)(2,1)S(1)} %collective-permute-done.5), channel_id=1, source_target_pairs={{0,4},{1,3},{4,8},{5,1},{8,12},{9,5},{12,14},{13,9},{14,10},{15,13... | collective-permute-start | bytes 786440 | tf_op jit(solution)/shard_map/ppermute | solution.py:33
  23.5 6.9 %collective-permute-start.8 = (bf16[2,16,4096]{2,1,0:T(8,128)(2,1)S(1)}, bf16[2,16,4096]{2,1,0:T(8,128)(2,1)S(1)}, u32[]{:S(2)}, u32[]{:S(2)}) collective-permute-start(bf16[2,16,4096]{2,1,0:T(8,128)(2,1)S(1)} %collective-permute-done.6), channel_id=1, source_target_pairs={{0,1},{1,0},{2,3},{3,2},{4,5},{5,4},{6,7},{7,6},{8,9},{9,8},{10,11... | collective-permute-start | bytes 786440 | tf_op jit(solution)/shard_map/ppermute | solution.py:36
  24.0 5.9 %collective-permute-start.10 = (bf16[2,16,4096]{2,1,0:T(8,128)(2,1)S(1)}, bf16[2,16,4096]{2,1,0:T(8,128)(2,1)S(1)}, u32[]{:S(2)}, u32[]{:S(2)}) collective-permute-start(bf16[2,16,4096]{2,1,0:T(8,128)(2,1)S(1)} %collective-permute-done.6), channel_id=1, source_target_pairs={{0,4},{1,3},{4,8},{5,1},{8,12},{9,5},{12,14},{13,9},{14,10},{15,13... | collective-permute-start | bytes 786440 | tf_op jit(solution)/shard_map/ppermute | solution.py:33
  26.3 6.9 %collective-permute-start.11 = (bf16[2,16,4096]{2,1,0:T(8,128)(2,1)S(1)}, bf16[2,16,4096]{2,1,0:T(8,128)(2,1)S(1)}, u32[]{:S(2)}, u32[]{:S(2)}) collective-permute-start(bf16[2,16,4096]{2,1,0:T(8,128)(2,1)S(1)} %collective-permute-done.9), channel_id=1, source_target_pairs={{0,1},{1,0},{2,3},{3,2},{4,5},{5,4},{6,7},{7,6},{8,9},{9,8},{10,11... | collective-permute-start | bytes 786440 | tf_op jit(solution)/shard_map/ppermute | solution.py:36
  26.8 5.9 %collective-permute-start.13 = (bf16[2,16,4096]{2,1,0:T(8,128)(2,1)S(1)}, bf16[2,16,4096]{2,1,0:T(8,128)(2,1)S(1)}, u32[]{:S(2)}, u32[]{:S(2)}) collective-permute-start(bf16[2,16,4096]{2,1,0:T(8,128)(2,1)S(1)} %collective-permute-done.9), channel_id=1, source_target_pairs={{0,4},{1,3},{4,8},{5,1},{8,12},{9,5},{12,14},{13,9},{14,10},{15,13... | collective-permute-start | bytes 786440 | tf_op jit(solution)/shard_map/ppermute | solution.py:33
  29.8 3.4 %collective-permute-start.12 = (bf16[2,16,4096]{2,1,0:T(8,128)(2,1)S(1)}, bf16[2,16,4096]{2,1,0:T(8,128)(2,1)S(1)}, u32[]{:S(2)}, u32[]{:S(2)}) collective-permute-start(bf16[2,16,4096]{2,1,0:T(8,128)(2,1)S(1)} %collective-permute-done.10), channel_id=1, source_target_pairs={{0,1},{1,0},{2,3},{3,2},{4,5},{5,4},{6,7},{7,6},{8,9},{9,8},{10,11... | collective-permute-start | bytes 786440 | tf_op jit(solution)/shard_map/ppermute | solution.py:36
  32.7 1.7 %collective-permute-start.14 = (bf16[2,16,4096]{2,1,0:T(8,128)(2,1)S(1)}, bf16[2,16,4096]{2,1,0:T(8,128)(2,1)S(1)}, u32[]{:S(2)}, u32[]{:S(2)}) collective-permute-start(bf16[2,16,4096]{2,1,0:T(8,128)(2,1)S(1)} %collective-permute-done.13), channel_id=1, source_target_pairs={{0,1},{1,0},{2,3},{3,2},{4,5},{5,4},{6,7},{7,6},{8,9},{9,8},{10,11... | collective-permute-start | bytes 786440 | tf_op jit(solution)/shard_map/ppermute | solution.py:36
  33.2 3.0 %copy-start = (bf16[512,4096]{1,0:T(8,128)(2,1)S(1)}, bf16[512,4096]{1,0:T(8,128)(2,1)}, u32[]{:S(2)}) copy-start(bf16[512,4096]{1,0:T(8,128)(2,1)} %param.3) | copy-start | bytes 12582916

commit v4 on v2

--- a/solution.py
+++ b/solution.py
@@ -25,21 +25,16 @@
     return [(i, i ^ 1) for i in range(size)]
 
 
-def gather_pieces(own, size):
+def gather_pieces(block, size):
     twins, ring = core_pairs(size), ring_pairs(size)
     chips = size // 2
-    core = lax.axis_index("samp") % 2
-    other = lax.ppermute(own, "samp", twins)
-    block = jnp.concatenate([own, other], axis=1)
     pieces = [block]
-    steps = (chips - 1) // 2
-    for _ in range(steps):
+    for _ in range((chips - 1) // 2):
         block = lax.ppermute(block, "samp", ring)
         pieces += [block, lax.ppermute(block, "samp", twins)]
     if chips % 2 == 0:
-        half = block.shape[1] // 2
-        last = lax.ppermute(block[:, :half], "samp", ring)
-        pieces += [last, lax.ppermute(last, "samp", twins)]
+        block = lax.ppermute(block[: block.shape[0] // 2], "samp", ring)
+        pieces += [block, lax.ppermute(block, "samp", twins)]
     return pieces
 
 
@@ -61,9 +56,11 @@
 
 def body(queries, gen_panel, ref_panel):
     size = lax.axis_size("samp")
-    pieces = gather_pieces(jnp.stack([ref_panel, gen_panel]), size)
-    every = jnp.concatenate(pieces, axis=1)
-    ref_all, gen_all = every[0], every[1]
+    own = lax.optimization_barrier(jnp.stack([ref_panel, gen_panel]))
+    other = lax.ppermute(own, "samp", core_pairs(size))
+    chip = jnp.concatenate([own, other], axis=1)
+    ref_all = jnp.concatenate(gather_pieces(chip[0], size), axis=0)
+    gen_all = jnp.concatenate(gather_pieces(chip[1], size), axis=0)
     profile = jnp.sum(ref_all.astype(jnp.float32), axis=0) / ref_all.shape[0]
     probes = center_rows(queries, profile)
     gen_c = center_rows(gen_all, profile)

time: 45.6 us -> 38.4 us (0.84)
  waiting for transfers between devices: 26 us -> 10.6 us
  starting transfers between devices: 11.5 us -> 19.7 us
  other arithmetic: 4.61 us -> 3.67 us
  local copies, waits for them, and re-layouts: 0.29 us -> 1.03 us
    ppermute x3 -> x6, waiting for transfers between devices: 20.6 us -> 7.31 us  [gather_pieces(): block = lax.ppermute(block, 'samp', ring)]
    ppermute x3 -> x6, starting transfers between devices: 5.9 us -> 10.7 us  [gather_pieces(): block = lax.ppermute(block, 'samp', ring)]
    ppermute x3 -> x8, starting transfers between devices: 2.61 us -> 5.98 us  [gather_pieces(): pieces += [block, lax.ppermute(block, 'samp', twins)]]
    ppermute x3, waiting for transfers between devices: 5.39 us -> 2.29 us  [the longest x1 1.48 us: body(): other = lax.ppermute(own, 'samp', core_pairs(size))]
    concatenate x1 -> x0, other arithmetic: 1 us -> none  [gather_pieces(): block = jnp.concatenate([own, other], axis=1)]
    ppermute x3 -> x8, waiting for transfers between devices: 0.01 us -> 0.96 us  [gather_pieces(): pieces += [block, lax.ppermute(block, 'samp', twins)]]
    unnamed x10 -> x16, local copies, waits for them, and re-layouts: 0.26 us -> 0.99 us
  transfers between devices with their start and end apart: 9 -> 17, of which waited for: 6 -> 9; matrix products, arithmetic and copies ran while one was open for 1% -> 2% of each run, Pallas kernels for 0% -> 0%
where the time goes in v4:
time: 38.4 us; the launch traced here: 37.9 us
  starting transfers between devices  19.7 us (51%)
  waiting for transfers between devices  10.6 us (28%)
  other arithmetic  3.67 us (10%)
  matrix products  2.75 us (7%)
  local copies, waits for them, and re-layouts  1.03 us (3%)
    ppermute x6, starting transfers between devices, gather_pieces(): block = lax.ppermute(block, 'samp', ring)  10.7 us
    ppermute x6, waiting for transfers between devices, gather_pieces(): block = lax.ppermute(block, 'samp', ring)  7.31 us
    ppermute x8, starting transfers between devices, gather_pieces(): pieces += [block, lax.ppermute(block, 'samp', twins)]  5.98 us
    ppermute x2, starting transfers between devices, gather_pieces(): block = lax.ppermute(block[:block.shape[0] // 2], 'samp', ring)  2.92 us
    dot_general x2, matrix products, panel_scores(): lax.dot_general(probes, panel, (((1,), (1,)), ((), ())), preferred_elemen...  2.75 us
    ppermute x1, waiting for transfers between devices, body(): other = lax.ppermute(own, 'samp', core_pairs(size))  1.48 us
    reduce_sum x1, other arithmetic, half_norms(): return 0.5 * jnp.sum(jnp.square(centered.astype(jnp.float32)), axis=1)  1.43 us
    another operation x1, other arithmetic, body(): own = lax.optimization_barrier(jnp.stack([ref_panel, gen_panel]))  0.99 us
  transfers between devices with their start and end apart: 17, of which 9 were waited for; matrix products, arithmetic and copies ran while one was open for 2% of the time, Pallas kernels for 0%

profile of v4, /device:TPU:1, one launch (start us, length us, event | category | flops | bytes accessed | tf_op | source)
XLA Modules:
  0.0 37.9 jit_solution(5602178987562425928)
XLA Ops:
  0.0 1.0 %pad_maximum_fusion.1 = bf16[2,16,4096]{2,1,0:T(8,128)(2,1)S(1)} fusion(bf16[1,16,4096]{2,1,0:T(8,128)(2,1)} %bitcast.8, bf16[1,16,4096]{2,1,0:T(8,128)(2,1)} %bitcast.9), kind=kLoop, calls=%fused_computation.22 | loop fusion | flops 131072 | bytes 524288 | tf_op jit(solution)/shard_map/stack | solution.py:59
  1.0 0.1 collective-permute-start
  1.1 1.5 %collective-permute-done = bf16[2,16,4096]{2,1,0:T(8,128)(2,1)S(1)} collective-permute-done((bf16[2,16,4096]{2,1,0:T(8,128)(2,1)S(1)}, bf16[2,16,4096]{2,1,0:T(8,128)(2,1)S(1)}, u32[]{:S(2)}, u32[]{:S(2)}) %collective-permute-start) | collective-permute-done | bytes 262176 | tf_op jit(solution)/shard_map/ppermute | solution.py:60
  2.6 0.1 constant_dynamic-update-slice_fusion.17
  2.7 2.4 %collective-permute-start.9 = (bf16[32,4096]{1,0:T(8,128)(2,1)S(1)}, bf16[32,4096]{1,0:T(8,128)(2,1)S(1)}, u32[]{:S(2)}, u32[]{:S(2)}) collective-permute-start(bf16[32,4096]{1,0:T(8,128)(2,1)S(1)} %get-tuple-element.8), channel_id=1, source_target_pairs={{0,4},{1,3},{4,8},{5,1},{8,12},{9,5},{12,14},{13,9},{14,10},{15,13... | collective-permute-start | bytes 786440 | tf_op jit(solution)/shard_map/ppermute | solution.py:33
  5.1 1.3 %collective-permute-start.1 = (bf16[32,4096]{1,0:T(8,128)(2,1)S(1)}, bf16[32,4096]{1,0:T(8,128)(2,1)S(1)}, u32[]{:S(2)}, u32[]{:S(2)}) collective-permute-start(bf16[32,4096]{1,0:T(8,128)(2,1)S(1)} %get-tuple-element.12), channel_id=1, source_target_pairs={{0,4},{1,3},{4,8},{5,1},{8,12},{9,5},{12,14},{13,9},{14,10},{15,13... | collective-permute-start | bytes 786440 | tf_op jit(solution)/shard_map/ppermute | solution.py:33
  6.4 2.8 %collective-permute-done.9 = bf16[32,4096]{1,0:T(8,128)(2,1)S(1)} collective-permute-done((bf16[32,4096]{1,0:T(8,128)(2,1)S(1)}, bf16[32,4096]{1,0:T(8,128)(2,1)S(1)}, u32[]{:S(2)}, u32[]{:S(2)}) %collective-permute-start.9) | collective-permute-done | bytes 262176 | tf_op jit(solution)/shard_map/ppermute | solution.py:33
  9.2 0.9 %collective-permute-start.10 = (bf16[32,4096]{1,0:T(8,128)(2,1)S(1)}, bf16[32,4096]{1,0:T(8,128)(2,1)S(1)}, u32[]{:S(2)}, u32[]{:S(2)}) collective-permute-start(bf16[32,4096]{1,0:T(8,128)(2,1)S(1)} %collective-permute-done.9), channel_id=1, source_target_pairs={{0,1},{1,0},{2,3},{3,2},{4,5},{5,4},{6,7},{7,6},{8,9},{9,8},{10,11... | collective-permute-start | bytes 786440 | tf_op jit(solution)/shard_map/ppermute | solution.py:34
  10.1 1.7 %collective-permute-start.11 = (bf16[32,4096]{1,0:T(8,128)(2,1)S(1)}, bf16[32,4096]{1,0:T(8,128)(2,1)S(1)}, u32[]{:S(2)}, u32[]{:S(2)}) collective-permute-start(bf16[32,4096]{1,0:T(8,128)(2,1)S(1)} %collective-permute-done.9), channel_id=1, source_target_pairs={{0,4},{1,3},{4,8},{5,1},{8,12},{9,5},{12,14},{13,9},{14,10},{15,13... | collective-permute-start | bytes 786440 | tf_op jit(solution)/shard_map/ppermute | solution.py:33
  11.8 0.2 collective-permute-done.1
  12.0 0.9 %collective-permute-start.2 = (bf16[32,4096]{1,0:T(8,128)(2,1)S(1)}, bf16[32,4096]{1,0:T(8,128)(2,1)S(1)}, u32[]{:S(2)}, u32[]{:S(2)}) collective-permute-start(bf16[32,4096]{1,0:T(8,128)(2,1)S(1)} %collective-permute-done.1), channel_id=1, source_target_pairs={{0,1},{1,0},{2,3},{3,2},{4,5},{5,4},{6,7},{7,6},{8,9},{9,8},{10,11... | collective-permute-start | bytes 786440 | tf_op jit(solution)/shard_map/ppermute | solution.py:34
  12.9 1.7 %collective-permute-start.3 = (bf16[32,4096]{1,0:T(8,128)(2,1)S(1)}, bf16[32,4096]{1,0:T(8,128)(2,1)S(1)}, u32[]{:S(2)}, u32[]{:S(2)}) collective-permute-start(bf16[32,4096]{1,0:T(8,128)(2,1)S(1)} %collective-permute-done.1), channel_id=1, source_target_pairs={{0,4},{1,3},{4,8},{5,1},{8,12},{9,5},{12,14},{13,9},{14,10},{15,13... | collective-permute-start | bytes 786440 | tf_op jit(solution)/shard_map/ppermute | solution.py:33
  14.7 1.3 %collective-permute-done.11 = bf16[32,4096]{1,0:T(8,128)(2,1)S(1)} collective-permute-done((bf16[32,4096]{1,0:T(8,128)(2,1)S(1)}, bf16[32,4096]{1,0:T(8,128)(2,1)S(1)}, u32[]{:S(2)}, u32[]{:S(2)}) %collective-permute-start.11) | collective-permute-done | bytes 262176 | tf_op jit(solution)/shard_map/ppermute | solution.py:33
  16.0 0.5 %collective-permute-start.12 = (bf16[32,4096]{1,0:T(8,128)(2,1)S(1)}, bf16[32,4096]{1,0:T(8,128)(2,1)S(1)}, u32[]{:S(2)}, u32[]{:S(2)}) collective-permute-start(bf16[32,4096]{1,0:T(8,128)(2,1)S(1)} %collective-permute-done.11), channel_id=1, source_target_pairs={{0,1},{1,0},{2,3},{3,2},{4,5},{5,4},{6,7},{7,6},{8,9},{9,8},{10,11... | collective-permute-start | bytes 786440 | tf_op jit(solution)/shard_map/ppermute | solution.py:34
  16.5 1.7 %collective-permute-start.13 = (bf16[32,4096]{1,0:T(8,128)(2,1)S(1)}, bf16[32,4096]{1,0:T(8,128)(2,1)S(1)}, u32[]{:S(2)}, u32[]{:S(2)}) collective-permute-start(bf16[32,4096]{1,0:T(8,128)(2,1)S(1)} %collective-permute-done.11), channel_id=1, source_target_pairs={{0,4},{1,3},{4,8},{5,1},{8,12},{9,5},{12,14},{13,9},{14,10},{15,13... | collective-permute-start | bytes 786440 | tf_op jit(solution)/shard_map/ppermute | solution.py:33
  18.2 0.5 %collective-permute-done.3 = bf16[32,4096]{1,0:T(8,128)(2,1)S(1)} collective-permute-done((bf16[32,4096]{1,0:T(8,128)(2,1)S(1)}, bf16[32,4096]{1,0:T(8,128)(2,1)S(1)}, u32[]{:S(2)}, u32[]{:S(2)}) %collective-permute-start.3) | collective-permute-done | bytes 262176 | tf_op jit(solution)/shard_map/ppermute | solution.py:33
  18.8 0.5 %collective-permute-start.4 = (bf16[32,4096]{1,0:T(8,128)(2,1)S(1)}, bf16[32,4096]{1,0:T(8,128)(2,1)S(1)}, u32[]{:S(2)}, u32[]{:S(2)}) collective-permute-start(bf16[32,4096]{1,0:T(8,128)(2,1)S(1)} %collective-permute-done.3), channel_id=1, source_target_pairs={{0,1},{1,0},{2,3},{3,2},{4,5},{5,4},{6,7},{7,6},{8,9},{9,8},{10,11... | collective-permute-start | bytes 786440 | tf_op jit(solution)/shard_map/ppermute | solution.py:34
  19.3 0.0 collective-permute-done.10
  19.3 1.7 %collective-permute-start.5 = (bf16[32,4096]{1,0:T(8,128)(2,1)S(1)}, bf16[32,4096]{1,0:T(8,128)(2,1)S(1)}, u32[]{:S(2)}, u32[]{:S(2)}) collective-permute-start(bf16[32,4096]{1,0:T(8,128)(2,1)S(1)} %collective-permute-done.3), channel_id=1, source_target_pairs={{0,4},{1,3},{4,8},{5,1},{8,12},{9,5},{12,14},{13,9},{14,10},{15,13... | collective-permute-start | bytes 786440 | tf_op jit(solution)/shard_map/ppermute | solution.py:33
  21.1 0.0 collective-permute-done.2
  21.1 1.2 %collective-permute-done.13 = bf16[32,4096]{1,0:T(8,128)(2,1)S(1)} collective-permute-done((bf16[32,4096]{1,0:T(8,128)(2,1)S(1)}, bf16[32,4096]{1,0:T(8,128)(2,1)S(1)}, u32[]{:S(2)}, u32[]{:S(2)}) %collective-permute-start.13) | collective-permute-done | bytes 262176 | tf_op jit(solution)/shard_map/ppermute | solution.py:33
  22.3 1.5 %collective-permute-start.15 = (bf16[16,4096]{1,0:T(8,128)(2,1)S(1)}, bf16[16,4096]{1,0:T(8,128)(2,1)S(1)}, u32[]{:S(2)}, u32[]{:S(2)}) collective-permute-start(bf16[16,4096]{1,0:T(8,128)(2,1)S(1)} %slice.19), channel_id=1, source_target_pairs={{0,4},{1,3},{4,8},{5,1},{8,12},{9,5},{12,14},{13,9},{14,10},{15,13... | collective-permute-start | bytes 393224 | tf_op jit(solution)/shard_map/ppermute | solution.py:36
  23.8 1.3 %collective-permute-done.5 = bf16[32,4096]{1,0:T(8,128)(2,1)S(1)} collective-permute-done((bf16[32,4096]{1,0:T(8,128)(2,1)S(1)}, bf16[32,4096]{1,0:T(8,128)(2,1)S(1)}, u32[]{:S(2)}, u32[]{:S(2)}) %collective-permute-start.5) | collective-permute-done | bytes 262176 | tf_op jit(solution)/shard_map/ppermute | solution.py:33
  25.2 1.5 %collective-permute-start.7 = (bf16[16,4096]{1,0:T(8,128)(2,1)S(1)}, bf16[16,4096]{1,0:T(8,128)(2,1)S(1)}, u32[]{:S(2)}, u32[]{:S(2)}) collective-permute-start(bf16[16,4096]{1,0:T(8,128)(2,1)S(1)} %slice.18), channel_id=1, source_target_pairs={{0,4},{1,3},{4,8},{5,1},{8,12},{9,5},{12,14},{13,9},{14,10},{15,13... | collective-permute-start | bytes 393224 | tf_op jit(solution)/shard_map/ppermute | solution.py:36
  26.6 1.2 %collective-permute-start.14 = (bf16[32,4096]{1,0:T(8,128)(2,1)S(1)}, bf16[32,4096]{1,0:T(8,128)(2,1)S(1)}, u32[]{:S(2)}, u32[]{:S(2)}) collective-permute-start(bf16[32,4096]{1,0:T(8,128)(2,1)S(1)} %collective-permute-done.13), channel_id=1, source_target_pairs={{0,1},{1,0},{2,3},{3,2},{4,5},{5,4},{6,7},{7,6},{8,9},{9,8},{10,11... | collective-permute-start | bytes 786440 | tf_op jit(solution)/shard_map/ppermute | solution.py:34
  27.8 0.0 collective-permute-done.12
  27.8 0.0 collective-permute-start.6
  27.9 0.0 collective-permute-done.4
  27.9 0.0 collective-permute-done.15
  27.9 0.6 %collective-permute-start.16 = (bf16[16,4096]{1,0:T(8,128)(2,1)S(1)}, bf16[16,4096]{1,0:T(8,128)(2,1)S(1)}, u32[]{:S(2)}, u32[]{:S(2)}) collective-permute-start(bf16[16,4096]{1,0:T(8,128)(2,1)S(1)} %collective-permute-done.15), channel_id=1, source_target_pairs={{0,1},{1,0},{2,3},{3,2},{4,5},{5,4},{6,7},{7,6},{8,9},{9,8},{10,11... | collective-permute-start | bytes 393224 | tf_op jit(solution)/shard_map/ppermute | solution.py:37
  28.5 0.8 %collective-permute-done.7 = bf16[16,4096]{1,0:T(8,128)(2,1)S(1)} collective-permute-done((bf16[16,4096]{1,0:T(8,128)(2,1)S(1)}, bf16[16,4096]{1,0:T(8,128)(2,1)S(1)}, u32[]{:S(2)}, u32[]{:S(2)}) %collective-permute-start.7) | collective-permute-done | bytes 131104 | tf_op jit(solution)/shard_map/ppermute | solution.py:36
  29.3 1.4 %collective-permute-start.8 = (bf16[16,4096]{1,0:T(8,128)(2,1)S(1)}, bf16[16,4096]{1,0:T(8,128)(2,1)S(1)}, u32[]{:S(2)}, u32[]{:S(2)}) collective-permute-start(bf16[16,4096]{1,0:T(8,128)(2,1)S(1)} %collective-permute-done.7), channel_id=1, source_target_pairs={{0,1},{1,0},{2,3},{3,2},{4,5},{5,4},{6,7},{7,6},{8,9},{9,8},{10,11... | collective-permute-start | bytes 393224 | tf_op jit(solution)/shard_map/ppermute | solution.py:37
  30.7 0.0 collective-permute-done.6
  30.7 0.9 %collective-permute-done.8 = bf16[16,4096]{1,0:T(8,128)(2,1)S(1)} collective-permute-done((bf16[16,4096]{1,0:T(8,128)(2,1)S(1)}, bf16[16,4096]{1,0:T(8,128)(2,1)S(1)}, u32[]{:S(2)}, u32[]{:S(2)}) %collective-permute-start.8) | collective-permute-done | bytes 131104 | tf_op jit(solution)/shard_map/ppermute | solution.py:37
  31.7 0.3 convert_reduce_fusion
  32.0 0.0 collective-permute-done.14
  32.1 0.0 collective-permute-done.16
  32.1 0.0 copy-start
  32.2 1.4 %multiply_reduce_fusion.1 = (f32[256]{0:T(256)S(1)}, f32[256]{0:T(256)S(1)}) fusion(f32[4096]{0:T(1024)S(1)} %broadcast_multiply_fusion, bf16[256,4096]{1,0:T(8,128)(2,1)S(1)} %constant_dynamic-update-slice_fusion.9, bf16[256,4096]{1,0:T(8,128)(2,1)S(1)} %constant_dynamic-update-slice_fusion), kind=kLoop, calls=%fused_computation.6 | loop fusion | flops 14679552 | bytes 4212736 | tf_op jit(solution)/shard_map/reduce_sum | solution.py:47
  33.6 0.7 %copy-done = bf16[512,4096]{1,0:T(8,128)(2,1)S(1)} copy-done((bf16[512,4096]{1,0:T(8,128)(2,1)S(1)}, bf16[512,4096]{1,0:T(8,128)(2,1)}, u32[]{:S(2)}) %copy-start) | copy-done | bytes 4194328
  34.3 1.4 %fusion.19 = (f32[512]{0:T(512)S(1)}, f32[512,256]{0,1:T(8,128)S(1)}) fusion(f32[256]{0:T(256)S(1)} %get-tuple-element.18, bf16[256,4096]{1,0:T(8,128)(2,1)S(1)} %constant_dynamic-update-slice_fusion.9, f32[4096]{0:T(1024)S(1)} %broadcast_multiply_fusion, bf16[512,4096]{1,0:T(8,128)(2,1)S(1)} %copy-done), kind=kOutput, calls=%fused_computation.48 | convolution fusion | flops 1086717440 | bytes 6835200 | tf_op jit(solution)/shard_map/dot_general | solution.py:51
  35.7 1.4 %fusion.18 = (f32[512]{0:T(512)S(1)}, f32[512,256]{0,1:T(8,128)S(1)}) fusion(f32[256]{0:T(256)S(1)} %get-tuple-element.17, bf16[256,4096]{1,0:T(8,128)(2,1)S(1)} %constant_dynamic-update-slice_fusion, f32[4096]{0:T(1024)S(1)} %broadcast_multiply_fusion, bf16[512,4096]{1,0:T(8,128)(2,1)S(1)} %copy-done), kind=kOutput, calls=%fused_computation.47 | convolution fusion | flops 1086717440 | bytes 6835200 | tf_op jit(solution)/shard_map/dot_general | solution.py:51
  37.1 0.1 exponential_reduce_fusion.1
  37.2 0.1 exponential_reduce_fusion
  37.3 0.6 %add_subtract_fusion = f32[512]{0:T(512)} fusion(f32[512]{0:T(512)S(1)} %exponential_reduce_fusion, f32[512]{0:T(512)S(1)} %exponential_reduce_fusion.1, f32[512]{0:T(512)S(1)} %get-tuple-element.15, f32[512]{0:T(512)S(1)} %get-tuple-element.13), kind=kLoop, calls=%fused_computation.44 | loop fusion | flops 4608 | bytes 10240 | tf_op jit(solution)/shard_map/sub | solution.py:70
  (22 shorter events, 0.3 us)
Async XLA Ops:
  1.0 1.6 %collective-permute-start = (bf16[2,16,4096]{2,1,0:T(8,128)(2,1)S(1)}, bf16[2,16,4096]{2,1,0:T(8,128)(2,1)S(1)}, u32[]{:S(2)}, u32[]{:S(2)}) collective-permute-start(bf16[2,16,4096]{2,1,0:T(8,128)(2,1)S(1)} %pad_maximum_fusion.1), channel_id=1, source_target_pairs={{0,1},{1,0},{2,3},{3,2},{4,5},{5,4},{6,7},{7,6},{8,9},{9,8},{10,11... | collective-permute-start | bytes 786440 | tf_op jit(solution)/shard_map/ppermute | solution.py:60
  2.7 6.5 %collective-permute-start.9 = (bf16[32,4096]{1,0:T(8,128)(2,1)S(1)}, bf16[32,4096]{1,0:T(8,128)(2,1)S(1)}, u32[]{:S(2)}, u32[]{:S(2)}) collective-permute-start(bf16[32,4096]{1,0:T(8,128)(2,1)S(1)} %get-tuple-element.8), channel_id=1, source_target_pairs={{0,4},{1,3},{4,8},{5,1},{8,12},{9,5},{12,14},{13,9},{14,10},{15,13... | collective-permute-start | bytes 786440 | tf_op jit(solution)/shard_map/ppermute | solution.py:33
  5.1 6.9 %collective-permute-start.1 = (bf16[32,4096]{1,0:T(8,128)(2,1)S(1)}, bf16[32,4096]{1,0:T(8,128)(2,1)S(1)}, u32[]{:S(2)}, u32[]{:S(2)}) collective-permute-start(bf16[32,4096]{1,0:T(8,128)(2,1)S(1)} %get-tuple-element.12), channel_id=1, source_target_pairs={{0,4},{1,3},{4,8},{5,1},{8,12},{9,5},{12,14},{13,9},{14,10},{15,13... | collective-permute-start | bytes 786440 | tf_op jit(solution)/shard_map/ppermute | solution.py:33
  9.2 10.1 %collective-permute-start.10 = (bf16[32,4096]{1,0:T(8,128)(2,1)S(1)}, bf16[32,4096]{1,0:T(8,128)(2,1)S(1)}, u32[]{:S(2)}, u32[]{:S(2)}) collective-permute-start(bf16[32,4096]{1,0:T(8,128)(2,1)S(1)} %collective-permute-done.9), channel_id=1, source_target_pairs={{0,1},{1,0},{2,3},{3,2},{4,5},{5,4},{6,7},{7,6},{8,9},{9,8},{10,11... | collective-permute-start | bytes 786440 | tf_op jit(solution)/shard_map/ppermute | solution.py:34
  10.1 5.9 %collective-permute-start.11 = (bf16[32,4096]{1,0:T(8,128)(2,1)S(1)}, bf16[32,4096]{1,0:T(8,128)(2,1)S(1)}, u32[]{:S(2)}, u32[]{:S(2)}) collective-permute-start(bf16[32,4096]{1,0:T(8,128)(2,1)S(1)} %collective-permute-done.9), channel_id=1, source_target_pairs={{0,4},{1,3},{4,8},{5,1},{8,12},{9,5},{12,14},{13,9},{14,10},{15,13... | collective-permute-start | bytes 786440 | tf_op jit(solution)/shard_map/ppermute | solution.py:33
  12.0 9.1 %collective-permute-start.2 = (bf16[32,4096]{1,0:T(8,128)(2,1)S(1)}, bf16[32,4096]{1,0:T(8,128)(2,1)S(1)}, u32[]{:S(2)}, u32[]{:S(2)}) collective-permute-start(bf16[32,4096]{1,0:T(8,128)(2,1)S(1)} %collective-permute-done.1), channel_id=1, source_target_pairs={{0,1},{1,0},{2,3},{3,2},{4,5},{5,4},{6,7},{7,6},{8,9},{9,8},{10,11... | collective-permute-start | bytes 786440 | tf_op jit(solution)/shard_map/ppermute | solution.py:34
  12.9 5.9 %collective-permute-start.3 = (bf16[32,4096]{1,0:T(8,128)(2,1)S(1)}, bf16[32,4096]{1,0:T(8,128)(2,1)S(1)}, u32[]{:S(2)}, u32[]{:S(2)}) collective-permute-start(bf16[32,4096]{1,0:T(8,128)(2,1)S(1)} %collective-permute-done.1), channel_id=1, source_target_pairs={{0,4},{1,3},{4,8},{5,1},{8,12},{9,5},{12,14},{13,9},{14,10},{15,13... | collective-permute-start | bytes 786440 | tf_op jit(solution)/shard_map/ppermute | solution.py:33
  16.0 11.9 %collective-permute-start.12 = (bf16[32,4096]{1,0:T(8,128)(2,1)S(1)}, bf16[32,4096]{1,0:T(8,128)(2,1)S(1)}, u32[]{:S(2)}, u32[]{:S(2)}) collective-permute-start(bf16[32,4096]{1,0:T(8,128)(2,1)S(1)} %collective-permute-done.11), channel_id=1, source_target_pairs={{0,1},{1,0},{2,3},{3,2},{4,5},{5,4},{6,7},{7,6},{8,9},{9,8},{10,11... | collective-permute-start | bytes 786440 | tf_op jit(solution)/shard_map/ppermute | solution.py:34
  16.5 5.9 %collective-permute-start.13 = (bf16[32,4096]{1,0:T(8,128)(2,1)S(1)}, bf16[32,4096]{1,0:T(8,128)(2,1)S(1)}, u32[]{:S(2)}, u32[]{:S(2)}) collective-permute-start(bf16[32,4096]{1,0:T(8,128)(2,1)S(1)} %collective-permute-done.11), channel_id=1, source_target_pairs={{0,4},{1,3},{4,8},{5,1},{8,12},{9,5},{12,14},{13,9},{14,10},{15,13... | collective-permute-start | bytes 786440 | tf_op jit(solution)/shard_map/ppermute | solution.py:33
  18.8 9.1 %collective-permute-start.4 = (bf16[32,4096]{1,0:T(8,128)(2,1)S(1)}, bf16[32,4096]{1,0:T(8,128)(2,1)S(1)}, u32[]{:S(2)}, u32[]{:S(2)}) collective-permute-start(bf16[32,4096]{1,0:T(8,128)(2,1)S(1)} %collective-permute-done.3), channel_id=1, source_target_pairs={{0,1},{1,0},{2,3},{3,2},{4,5},{5,4},{6,7},{7,6},{8,9},{9,8},{10,11... | collective-permute-start | bytes 786440 | tf_op jit(solution)/shard_map/ppermute | solution.py:34
  19.3 5.9 %collective-permute-start.5 = (bf16[32,4096]{1,0:T(8,128)(2,1)S(1)}, bf16[32,4096]{1,0:T(8,128)(2,1)S(1)}, u32[]{:S(2)}, u32[]{:S(2)}) collective-permute-start(bf16[32,4096]{1,0:T(8,128)(2,1)S(1)} %collective-permute-done.3), channel_id=1, source_target_pairs={{0,4},{1,3},{4,8},{5,1},{8,12},{9,5},{12,14},{13,9},{14,10},{15,13... | collective-permute-start | bytes 786440 | tf_op jit(solution)/shard_map/ppermute | solution.py:33
  22.3 5.6 %collective-permute-start.15 = (bf16[16,4096]{1,0:T(8,128)(2,1)S(1)}, bf16[16,4096]{1,0:T(8,128)(2,1)S(1)}, u32[]{:S(2)}, u32[]{:S(2)}) collective-permute-start(bf16[16,4096]{1,0:T(8,128)(2,1)S(1)} %slice.19), channel_id=1, source_target_pairs={{0,4},{1,3},{4,8},{5,1},{8,12},{9,5},{12,14},{13,9},{14,10},{15,13... | collective-permute-start | bytes 393224 | tf_op jit(solution)/shard_map/ppermute | solution.py:36
  25.2 4.2 %collective-permute-start.7 = (bf16[16,4096]{1,0:T(8,128)(2,1)S(1)}, bf16[16,4096]{1,0:T(8,128)(2,1)S(1)}, u32[]{:S(2)}, u32[]{:S(2)}) collective-permute-start(bf16[16,4096]{1,0:T(8,128)(2,1)S(1)} %slice.18), channel_id=1, source_target_pairs={{0,4},{1,3},{4,8},{5,1},{8,12},{9,5},{12,14},{13,9},{14,10},{15,13... | collective-permute-start | bytes 393224 | tf_op jit(solution)/shard_map/ppermute | solution.py:36
  26.6 5.4 %collective-permute-start.14 = (bf16[32,4096]{1,0:T(8,128)(2,1)S(1)}, bf16[32,4096]{1,0:T(8,128)(2,1)S(1)}, u32[]{:S(2)}, u32[]{:S(2)}) collective-permute-start(bf16[32,4096]{1,0:T(8,128)(2,1)S(1)} %collective-permute-done.13), channel_id=1, source_target_pairs={{0,1},{1,0},{2,3},{3,2},{4,5},{5,4},{6,7},{7,6},{8,9},{9,8},{10,11... | collective-permute-start | bytes 786440 | tf_op jit(solution)/shard_map/ppermute | solution.py:34
  27.8 2.9 %collective-permute-start.6 = (bf16[32,4096]{1,0:T(8,128)(2,1)S(1)}, bf16[32,4096]{1,0:T(8,128)(2,1)S(1)}, u32[]{:S(2)}, u32[]{:S(2)}) collective-permute-start(bf16[32,4096]{1,0:T(8,128)(2,1)S(1)} %collective-permute-done.5), channel_id=1, source_target_pairs={{0,1},{1,0},{2,3},{3,2},{4,5},{5,4},{6,7},{7,6},{8,9},{9,8},{10,11... | collective-permute-start | bytes 786440 | tf_op jit(solution)/shard_map/ppermute | solution.py:34
  27.9 4.2 %collective-permute-start.16 = (bf16[16,4096]{1,0:T(8,128)(2,1)S(1)}, bf16[16,4096]{1,0:T(8,128)(2,1)S(1)}, u32[]{:S(2)}, u32[]{:S(2)}) collective-permute-start(bf16[16,4096]{1,0:T(8,128)(2,1)S(1)} %collective-permute-done.15), channel_id=1, source_target_pairs={{0,1},{1,0},{2,3},{3,2},{4,5},{5,4},{6,7},{7,6},{8,9},{9,8},{10,11... | collective-permute-start | bytes 393224 | tf_op jit(solution)/shard_map/ppermute | solution.py:37
  29.3 2.4 %collective-permute-start.8 = (bf16[16,4096]{1,0:T(8,128)(2,1)S(1)}, bf16[16,4096]{1,0:T(8,128)(2,1)S(1)}, u32[]{:S(2)}, u32[]{:S(2)}) collective-permute-start(bf16[16,4096]{1,0:T(8,128)(2,1)S(1)} %collective-permute-done.7), channel_id=1, source_target_pairs={{0,1},{1,0},{2,3},{3,2},{4,5},{5,4},{6,7},{7,6},{8,9},{9,8},{10,11... | collective-permute-start | bytes 393224 | tf_op jit(solution)/shard_map/ppermute | solution.py:37
  32.1 2.2 %copy-start = (bf16[512,4096]{1,0:T(8,128)(2,1)S(1)}, bf16[512,4096]{1,0:T(8,128)(2,1)}, u32[]{:S(2)}) copy-start(bf16[512,4096]{1,0:T(8,128)(2,1)} %param.3) | copy-start | bytes 12582916

commit v5 on v4

--- a/solution.py
+++ b/solution.py
@@ -1,9 +1,15 @@
 import jax
 import jax.numpy as jnp
 from jax import lax
+from jax.experimental import pallas as pl
+from jax.experimental.pallas import tpu as pltpu
 from jax.sharding import PartitionSpec as P
 
 TEMP = 64
+LANES = 128
+CHUNK = 1024
+GROUP = 32
+LIMIT = 40 * 2**20
 
 
 def ring_of_chips(chips):
@@ -38,20 +44,109 @@
     return pieces
 
 
-def center_rows(rows, profile):
-    centered = rows.astype(jnp.float32) - profile
-    return lax.reduce_precision(centered, 8, 7).astype(jnp.bfloat16)
+def row_groups(rows, step):
+    return [slice(r, min(r + step, rows)) for r in range(0, rows, step)]
 
 
-def half_norms(centered):
-    return 0.5 * jnp.sum(jnp.square(centered.astype(jnp.float32)), axis=1)
+def center(rows, mean):
+    return (rows.astype(jnp.float32) - mean).astype(jnp.bfloat16)
 
 
-def panel_scores(probes, panel):
+def add_panel_chunk(cols, mean, panel, probes, centered, squares, scores, first):
+    for rows in row_groups(panel.shape[0], GROUP):
+        part = center(panel[rows, cols], mean)
+        centered[rows, cols] = part
+        wide = jnp.square(part.astype(jnp.float32))
+        total = wide[:, :LANES]
+        for lane in range(LANES, wide.shape[1], LANES):
+            total += wide[:, lane : lane + LANES]
+        squares[rows, :] = total if first else squares[rows, :] + total
     products = lax.dot_general(
-        probes, panel, (((1,), (1,)), ((), ())), preferred_element_type=jnp.float32
+        centered[:, cols], probes[:, cols], (((1,), (1,)), ((), ())),
+        preferred_element_type=jnp.float32,
     )
-    return (products - half_norms(panel)) / TEMP
+    scores[...] = products if first else scores[...] + products
+
+
+def log_sum(squares, scores):
+    half = 0.5 * jnp.sum(squares[...], axis=1, keepdims=True)
+    x = (scores[...] - half) / TEMP
+    top = jnp.max(x, axis=0, keepdims=True)
+    return jnp.log(jnp.sum(jnp.exp(x - top), axis=0, keepdims=True)) + top
+
+
+def ref_kernel(queries, panel, probes, mean, ref_log, centered, squares, scores):
+    count, features = panel.shape
+    for start in range(0, features, CHUNK):
+        cols = slice(start, start + CHUNK)
+        total = None
+        for rows in row_groups(count, GROUP):
+            part = jnp.sum(panel[rows, cols].astype(jnp.float32), axis=0, keepdims=True)
+            total = part if total is None else total + part
+        here = total / count
+        mean[:, cols] = here
+        for rows in row_groups(queries.shape[0], GROUP):
+            probes[rows, cols] = center(queries[rows, cols], here)
+        add_panel_chunk(cols, here, panel, probes, centered, squares, scores, start == 0)
+    ref_log[...] = log_sum(squares, scores)
+
+
+def gen_kernel(probes, mean, panel, ref_log, proof, centered, squares, scores):
+    for start in range(0, panel.shape[1], CHUNK):
+        cols = slice(start, start + CHUNK)
+        add_panel_chunk(cols, mean[:, cols], panel, probes, centered, squares, scores, start == 0)
+    proof[...] = log_sum(squares, scores) - ref_log[...]
+
+
+def scratch(panel, queries):
+    count, features = panel.shape
+    return [
+        pltpu.VMEM((count, features), jnp.bfloat16),
+        pltpu.VMEM((count, LANES), jnp.float32),
+        pltpu.VMEM((count, queries.shape[0]), jnp.float32),
+    ]
+
+
+def in_vmem(n):
+    return [pl.BlockSpec(memory_space=pltpu.VMEM)] * n
+
+
+def cost(queries, panel):
+    work = queries.shape[0] * panel.shape[0]
+    return pl.CostEstimate(
+        flops=2 * work * panel.shape[1],
+        bytes_accessed=2 * (queries.size + panel.size),
+        transcendentals=work,
+    )
+
+
+def score_ref(queries, panel):
+    count, features = queries.shape
+    return pl.pallas_call(
+        ref_kernel,
+        out_shape=(
+            jax.ShapeDtypeStruct((count, features), jnp.bfloat16),
+            jax.ShapeDtypeStruct((1, features), jnp.float32),
+            jax.ShapeDtypeStruct((1, count), jnp.float32),
+        ),
+        in_specs=in_vmem(2),
+        out_specs=tuple(in_vmem(3)),
+        scratch_shapes=scratch(panel, queries),
+        compiler_params=pltpu.CompilerParams(vmem_limit_bytes=LIMIT),
+        cost_estimate=cost(queries, panel),
+    )(queries, panel)
+
+
+def score_gen(probes, mean, panel, ref_log):
+    return pl.pallas_call(
+        gen_kernel,
+        out_shape=jax.ShapeDtypeStruct((1, probes.shape[0]), jnp.float32),
+        in_specs=in_vmem(4),
+        out_specs=in_vmem(1)[0],
+        scratch_shapes=scratch(panel, probes),
+        compiler_params=pltpu.CompilerParams(vmem_limit_bytes=LIMIT),
+        cost_estimate=cost(probes, panel),
+    )(probes, mean, panel, ref_log)
 
 
 def body(queries, gen_panel, ref_panel):
@@ -61,13 +156,8 @@
     chip = jnp.concatenate([own, other], axis=1)
     ref_all = jnp.concatenate(gather_pieces(chip[0], size), axis=0)
     gen_all = jnp.concatenate(gather_pieces(chip[1], size), axis=0)
-    profile = jnp.sum(ref_all.astype(jnp.float32), axis=0) / ref_all.shape[0]
-    probes = center_rows(queries, profile)
-    gen_c = center_rows(gen_all, profile)
-    ref_c = center_rows(ref_all, profile)
-    gen_log = jax.nn.logsumexp(panel_scores(probes, gen_c), axis=1)
-    ref_log = jax.nn.logsumexp(panel_scores(probes, ref_c), axis=1)
-    return gen_log - ref_log
+    probes, mean, ref_log = score_ref(queries, ref_all)
+    return score_gen(probes, mean, gen_all, ref_log).reshape(-1)
 
 
 def solution(mesh):

time: 38.4 us -> 37 us (0.964)
  Pallas kernels: 0 us -> 4.75 us
  waiting for transfers between devices: 10.6 us -> 7.37 us
  starting transfers between devices: 19.7 us -> 22.8 us
  matrix products: 2.75 us -> 0 us
  other arithmetic: 3.67 us -> 1.09 us
  local copies, waits for them, and re-layouts: 1.03 us -> 0.3 us
    ppermute x8, starting transfers between devices: 5.98 us -> 13.6 us  [gather_pieces(): pieces += [block, lax.ppermute(block, 'samp', twins)]]
    pallas_call x0 -> x2, Pallas kernels: none -> 4.75 us  [the longest x1 2.71 us: score_ref(): pl.pallas_call(ref_kernel, out_shape=(jax.ShapeDtypeStruct((count, featur...]
    dot_general x2 -> x0, matrix products: 2.75 us -> none  [panel_scores(): lax.dot_general(probes, panel, (((1,), (1,)), ((), ())), preferred_elemen...]
    ppermute x6, starting transfers between devices: 10.7 us -> 8.03 us  [gather_pieces(): block = lax.ppermute(block, 'samp', ring)]
    ppermute x6, waiting for transfers between devices: 7.31 us -> 4.98 us  [gather_pieces(): block = lax.ppermute(block, 'samp', ring)]
    reduce_sum x4 -> x0, other arithmetic: 2 us -> none  [the longest x1 1.43 us: half_norms(): return 0.5 * jnp.sum(jnp.square(centered.astype(jnp.float32)), axis=1)]
    ppermute x2, starting transfers between devices: 2.92 us -> 1.03 us  [gather_pieces(): block = lax.ppermute(block[:block.shape[0] // 2], 'samp', ring)]
    ppermute x2, waiting for transfers between devices: 0.81 us -> 0.01 us  [gather_pieces(): block = lax.ppermute(block[:block.shape[0] // 2], 'samp', ring)]
  transfers between devices with their start and end apart: 17 -> 17, of which waited for: 9 -> 4; matrix products, arithmetic and copies ran while one was open for 2% -> 1% of each run, Pallas kernels for 0% -> 7%
where the time goes in v5:
time: 37 us; the launch traced here: 36.5 us
  starting transfers between devices  22.8 us (62%)
  waiting for transfers between devices  7.37 us (20%)
  Pallas kernels  4.75 us (13%)
  other arithmetic  1.09 us (3%)
    ppermute x8, starting transfers between devices, gather_pieces(): pieces += [block, lax.ppermute(block, 'samp', twins)]  13.6 us
    ppermute x6, starting transfers between devices, gather_pieces(): block = lax.ppermute(block, 'samp', ring)  8.03 us
    ppermute x6, waiting for transfers between devices, gather_pieces(): block = lax.ppermute(block, 'samp', ring)  4.98 us
    pallas_call x1, Pallas kernels, score_ref(): pl.pallas_call(ref_kernel, out_shape=(jax.ShapeDtypeStruct((count, featur...  2.71 us
    pallas_call x1, Pallas kernels, score_gen(): pl.pallas_call(gen_kernel, out_shape=jax.ShapeDtypeStruct((1, probes.shap...  2.04 us
    ppermute x1, waiting for transfers between devices, body(): other = lax.ppermute(own, 'samp', core_pairs(size))  1.48 us
    ppermute x2, starting transfers between devices, gather_pieces(): block = lax.ppermute(block[:block.shape[0] // 2], 'samp', ring)  1.03 us
    another operation x1, other arithmetic, body(): own = lax.optimization_barrier(jnp.stack([ref_panel, gen_panel]))  0.99 us
  transfers between devices with their start and end apart: 17, of which 4 were waited for; matrix products, arithmetic and copies ran while one was open for 1% of the time, Pallas kernels for 7%

profile of v5, /device:TPU:1, one launch (start us, length us, event | category | flops | bytes accessed | tf_op | source)
XLA Modules:
  0.0 36.5 jit_solution(10614283545649754002)
XLA Ops:
  0.0 1.0 %pad_maximum_fusion.1 = bf16[2,16,4096]{2,1,0:T(8,128)(2,1)S(1)} fusion(bf16[1,16,4096]{2,1,0:T(8,128)(2,1)} %bitcast.9, bf16[1,16,4096]{2,1,0:T(8,128)(2,1)} %bitcast.10), kind=kLoop, calls=%fused_computation.6 | loop fusion | flops 131072 | bytes 524288 | tf_op jit(solution)/shard_map/stack | solution.py:154
  1.0 0.1 collective-permute-start
  1.1 1.5 %collective-permute-done = bf16[2,16,4096]{2,1,0:T(8,128)(2,1)S(1)} collective-permute-done((bf16[2,16,4096]{2,1,0:T(8,128)(2,1)S(1)}, bf16[2,16,4096]{2,1,0:T(8,128)(2,1)S(1)}, u32[]{:S(2)}, u32[]{:S(2)}) %collective-permute-start) | collective-permute-done | bytes 262176 | tf_op jit(solution)/shard_map/ppermute | solution.py:155
  2.6 0.1 constant_dynamic-update-slice_fusion.17
  2.7 2.4 %collective-permute-start.9 = (bf16[32,4096]{1,0:T(8,128)(2,1)S(1)}, bf16[32,4096]{1,0:T(8,128)(2,1)S(1)}, u32[]{:S(2)}, u32[]{:S(2)}) collective-permute-start(bf16[32,4096]{1,0:T(8,128)(2,1)S(1)} %get-tuple-element.12), channel_id=1, source_target_pairs={{0,4},{1,3},{4,8},{5,1},{8,12},{9,5},{12,14},{13,9},{14,10},{15,13... | collective-permute-start | bytes 786440 | tf_op jit(solution)/shard_map/ppermute | solution.py:39
  5.1 1.3 %collective-permute-start.1 = (bf16[32,4096]{1,0:T(8,128)(2,1)S(1)}, bf16[32,4096]{1,0:T(8,128)(2,1)S(1)}, u32[]{:S(2)}, u32[]{:S(2)}) collective-permute-start(bf16[32,4096]{1,0:T(8,128)(2,1)S(1)} %get-tuple-element.16), channel_id=1, source_target_pairs={{0,4},{1,3},{4,8},{5,1},{8,12},{9,5},{12,14},{13,9},{14,10},{15,13... | collective-permute-start | bytes 786440 | tf_op jit(solution)/shard_map/ppermute | solution.py:39
  6.4 2.8 %collective-permute-done.9 = bf16[32,4096]{1,0:T(8,128)(2,1)S(1)} collective-permute-done((bf16[32,4096]{1,0:T(8,128)(2,1)S(1)}, bf16[32,4096]{1,0:T(8,128)(2,1)S(1)}, u32[]{:S(2)}, u32[]{:S(2)}) %collective-permute-start.9) | collective-permute-done | bytes 262176 | tf_op jit(solution)/shard_map/ppermute | solution.py:39
  9.2 1.4 %collective-permute-start.11 = (bf16[32,4096]{1,0:T(8,128)(2,1)S(1)}, bf16[32,4096]{1,0:T(8,128)(2,1)S(1)}, u32[]{:S(2)}, u32[]{:S(2)}) collective-permute-start(bf16[32,4096]{1,0:T(8,128)(2,1)S(1)} %collective-permute-done.9), channel_id=1, source_target_pairs={{0,4},{1,3},{4,8},{5,1},{8,12},{9,5},{12,14},{13,9},{14,10},{15,13... | collective-permute-start | bytes 786440 | tf_op jit(solution)/shard_map/ppermute | solution.py:39
  10.6 1.6 %collective-permute-start.10 = (bf16[32,4096]{1,0:T(8,128)(2,1)S(1)}, bf16[32,4096]{1,0:T(8,128)(2,1)S(1)}, u32[]{:S(2)}, u32[]{:S(2)}) collective-permute-start(bf16[32,4096]{1,0:T(8,128)(2,1)S(1)} %collective-permute-done.9), channel_id=1, source_target_pairs={{0,1},{1,0},{2,3},{3,2},{4,5},{5,4},{6,7},{7,6},{8,9},{9,8},{10,11... | collective-permute-start | bytes 786440 | tf_op jit(solution)/shard_map/ppermute | solution.py:40
  12.2 0.0 collective-permute-done.1
  12.2 1.2 %collective-permute-start.3 = (bf16[32,4096]{1,0:T(8,128)(2,1)S(1)}, bf16[32,4096]{1,0:T(8,128)(2,1)S(1)}, u32[]{:S(2)}, u32[]{:S(2)}) collective-permute-start(bf16[32,4096]{1,0:T(8,128)(2,1)S(1)} %collective-permute-done.1), channel_id=1, source_target_pairs={{0,4},{1,3},{4,8},{5,1},{8,12},{9,5},{12,14},{13,9},{14,10},{15,13... | collective-permute-start | bytes 786440 | tf_op jit(solution)/shard_map/ppermute | solution.py:39
  13.5 1.6 %collective-permute-start.2 = (bf16[32,4096]{1,0:T(8,128)(2,1)S(1)}, bf16[32,4096]{1,0:T(8,128)(2,1)S(1)}, u32[]{:S(2)}, u32[]{:S(2)}) collective-permute-start(bf16[32,4096]{1,0:T(8,128)(2,1)S(1)} %collective-permute-done.1), channel_id=1, source_target_pairs={{0,1},{1,0},{2,3},{3,2},{4,5},{5,4},{6,7},{7,6},{8,9},{9,8},{10,11... | collective-permute-start | bytes 786440 | tf_op jit(solution)/shard_map/ppermute | solution.py:40
  15.1 0.0 collective-permute-done.11
  15.1 1.2 %collective-permute-start.13 = (bf16[32,4096]{1,0:T(8,128)(2,1)S(1)}, bf16[32,4096]{1,0:T(8,128)(2,1)S(1)}, u32[]{:S(2)}, u32[]{:S(2)}) collective-permute-start(bf16[32,4096]{1,0:T(8,128)(2,1)S(1)} %collective-permute-done.11), channel_id=1, source_target_pairs={{0,4},{1,3},{4,8},{5,1},{8,12},{9,5},{12,14},{13,9},{14,10},{15,13... | collective-permute-start | bytes 786440 | tf_op jit(solution)/shard_map/ppermute | solution.py:39
  16.3 2.3 %collective-permute-start.12 = (bf16[32,4096]{1,0:T(8,128)(2,1)S(1)}, bf16[32,4096]{1,0:T(8,128)(2,1)S(1)}, u32[]{:S(2)}, u32[]{:S(2)}) collective-permute-start(bf16[32,4096]{1,0:T(8,128)(2,1)S(1)} %collective-permute-done.11), channel_id=1, source_target_pairs={{0,1},{1,0},{2,3},{3,2},{4,5},{5,4},{6,7},{7,6},{8,9},{9,8},{10,11... | collective-permute-start | bytes 786440 | tf_op jit(solution)/shard_map/ppermute | solution.py:40
  18.6 0.0 collective-permute-done.3
  18.6 0.5 %collective-permute-start.5 = (bf16[32,4096]{1,0:T(8,128)(2,1)S(1)}, bf16[32,4096]{1,0:T(8,128)(2,1)S(1)}, u32[]{:S(2)}, u32[]{:S(2)}) collective-permute-start(bf16[32,4096]{1,0:T(8,128)(2,1)S(1)} %collective-permute-done.3), channel_id=1, source_target_pairs={{0,4},{1,3},{4,8},{5,1},{8,12},{9,5},{12,14},{13,9},{14,10},{15,13... | collective-permute-start | bytes 786440 | tf_op jit(solution)/shard_map/ppermute | solution.py:39
  19.1 0.0 collective-permute-done.10
  19.1 2.3 %collective-permute-start.4 = (bf16[32,4096]{1,0:T(8,128)(2,1)S(1)}, bf16[32,4096]{1,0:T(8,128)(2,1)S(1)}, u32[]{:S(2)}, u32[]{:S(2)}) collective-permute-start(bf16[32,4096]{1,0:T(8,128)(2,1)S(1)} %collective-permute-done.3), channel_id=1, source_target_pairs={{0,1},{1,0},{2,3},{3,2},{4,5},{5,4},{6,7},{7,6},{8,9},{9,8},{10,11... | collective-permute-start | bytes 786440 | tf_op jit(solution)/shard_map/ppermute | solution.py:40
  21.4 0.0 collective-permute-done.2
  21.5 0.0 collective-permute-done.13
  21.5 0.0 copy-start
  21.6 0.4 %collective-permute-start.15 = (bf16[16,4096]{1,0:T(8,128)(2,1)S(1)}, bf16[16,4096]{1,0:T(8,128)(2,1)S(1)}, u32[]{:S(2)}, u32[]{:S(2)}) collective-permute-start(bf16[16,4096]{1,0:T(8,128)(2,1)S(1)} %slice.19), channel_id=1, source_target_pairs={{0,4},{1,3},{4,8},{5,1},{8,12},{9,5},{12,14},{13,9},{14,10},{15,13... | collective-permute-start | bytes 393224 | tf_op jit(solution)/shard_map/ppermute | solution.py:42
  21.9 2.2 %collective-permute-done.5 = bf16[32,4096]{1,0:T(8,128)(2,1)S(1)} collective-permute-done((bf16[32,4096]{1,0:T(8,128)(2,1)S(1)}, bf16[32,4096]{1,0:T(8,128)(2,1)S(1)}, u32[]{:S(2)}, u32[]{:S(2)}) %collective-permute-start.5) | collective-permute-done | bytes 262176 | tf_op jit(solution)/shard_map/ppermute | solution.py:39
  24.1 0.6 %collective-permute-start.7 = (bf16[16,4096]{1,0:T(8,128)(2,1)S(1)}, bf16[16,4096]{1,0:T(8,128)(2,1)S(1)}, u32[]{:S(2)}, u32[]{:S(2)}) collective-permute-start(bf16[16,4096]{1,0:T(8,128)(2,1)S(1)} %slice.18), channel_id=1, source_target_pairs={{0,4},{1,3},{4,8},{5,1},{8,12},{9,5},{12,14},{13,9},{14,10},{15,13... | collective-permute-start | bytes 393224 | tf_op jit(solution)/shard_map/ppermute | solution.py:42
  24.8 3.1 %collective-permute-start.14 = (bf16[32,4096]{1,0:T(8,128)(2,1)S(1)}, bf16[32,4096]{1,0:T(8,128)(2,1)S(1)}, u32[]{:S(2)}, u32[]{:S(2)}) collective-permute-start(bf16[32,4096]{1,0:T(8,128)(2,1)S(1)} %collective-permute-done.13), channel_id=1, source_target_pairs={{0,1},{1,0},{2,3},{3,2},{4,5},{5,4},{6,7},{7,6},{8,9},{9,8},{10,11... | collective-permute-start | bytes 786440 | tf_op jit(solution)/shard_map/ppermute | solution.py:40
  27.8 0.0 collective-permute-done.12
  27.8 0.0 collective-permute-start.6
  27.9 0.0 collective-permute-done.4
  28.0 0.0 collective-permute-done.15
  28.0 0.6 %collective-permute-start.16 = (bf16[16,4096]{1,0:T(8,128)(2,1)S(1)}, bf16[16,4096]{1,0:T(8,128)(2,1)S(1)}, u32[]{:S(2)}, u32[]{:S(2)}) collective-permute-start(bf16[16,4096]{1,0:T(8,128)(2,1)S(1)} %collective-permute-done.15), channel_id=1, source_target_pairs={{0,1},{1,0},{2,3},{3,2},{4,5},{5,4},{6,7},{7,6},{8,9},{9,8},{10,11... | collective-permute-start | bytes 393224 | tf_op jit(solution)/shard_map/ppermute | solution.py:43
  28.5 0.0 collective-permute-done.7
  28.5 2.2 %collective-permute-start.8 = (bf16[16,4096]{1,0:T(8,128)(2,1)S(1)}, bf16[16,4096]{1,0:T(8,128)(2,1)S(1)}, u32[]{:S(2)}, u32[]{:S(2)}) collective-permute-start(bf16[16,4096]{1,0:T(8,128)(2,1)S(1)} %collective-permute-done.7), channel_id=1, source_target_pairs={{0,1},{1,0},{2,3},{3,2},{4,5},{5,4},{6,7},{7,6},{8,9},{9,8},{10,11... | collective-permute-start | bytes 393224 | tf_op jit(solution)/shard_map/ppermute | solution.py:43
  30.7 0.0 collective-permute-done.14
  30.8 0.0 collective-permute-done.6
  30.8 0.9 %collective-permute-done.8 = bf16[16,4096]{1,0:T(8,128)(2,1)S(1)} collective-permute-done((bf16[16,4096]{1,0:T(8,128)(2,1)S(1)}, bf16[16,4096]{1,0:T(8,128)(2,1)S(1)}, u32[]{:S(2)}, u32[]{:S(2)}) %collective-permute-start.8) | collective-permute-done | bytes 131104 | tf_op jit(solution)/shard_map/ppermute | solution.py:43
  31.7 0.0 copy-done
  31.7 2.7 %shard_map.37 = (bf16[512,4096]{1,0:T(8,128)(2,1)S(1)}, f32[1,4096]{1,0:T(1,128)S(1)}, f32[1,512]{1,0:T(1,128)S(1)}) custom-call(bf16[512,4096]{1,0:T(8,128)(2,1)S(1)} %copy-done, bf16[256,4096]{1,0:T(8,128)(2,1)S(1)} %constant_dynamic-update-slice_fusion.panel), custom_call_target="tpu_custom_call" | custom-call | flops 1073741824 | bytes 6291456 | tf_op jit(solution)/shard_map/pallas_call | solution.py:125
  34.4 0.0 collective-permute-done.16
  34.5 2.0 %shard_map.38 = f32[1,512]{1,0:T(1,128)} custom-call(bf16[512,4096]{1,0:T(8,128)(2,1)S(1)} %get-tuple-element.8.probes, f32[1,4096]{1,0:T(1,128)S(1)} %get-tuple-element.9.mean, bf16[256,4096]{1,0:T(8,128)(2,1)S(1)} %constant_dynamic-update-slice_fusion.9.panel, f32[1,512]{1,0:T(1,128)S(1)} %get-tuple-element.10.ref_log), custom_call_target="tpu_custom_call" | custom-call | flops 1073741824 | bytes 6291456 | tf_op jit(solution)/shard_map/pallas_call | solution.py:141
  (18 shorter events, 0.3 us)
Async XLA Ops:
  1.0 1.6 %collective-permute-start = (bf16[2,16,4096]{2,1,0:T(8,128)(2,1)S(1)}, bf16[2,16,4096]{2,1,0:T(8,128)(2,1)S(1)}, u32[]{:S(2)}, u32[]{:S(2)}) collective-permute-start(bf16[2,16,4096]{2,1,0:T(8,128)(2,1)S(1)} %pad_maximum_fusion.1), channel_id=1, source_target_pairs={{0,1},{1,0},{2,3},{3,2},{4,5},{5,4},{6,7},{7,6},{8,9},{9,8},{10,11... | collective-permute-start | bytes 786440 | tf_op jit(solution)/shard_map/ppermute | solution.py:155
  2.7 6.5 %collective-permute-start.9 = (bf16[32,4096]{1,0:T(8,128)(2,1)S(1)}, bf16[32,4096]{1,0:T(8,128)(2,1)S(1)}, u32[]{:S(2)}, u32[]{:S(2)}) collective-permute-start(bf16[32,4096]{1,0:T(8,128)(2,1)S(1)} %get-tuple-element.12), channel_id=1, source_target_pairs={{0,4},{1,3},{4,8},{5,1},{8,12},{9,5},{12,14},{13,9},{14,10},{15,13... | collective-permute-start | bytes 786440 | tf_op jit(solution)/shard_map/ppermute | solution.py:39
  5.1 7.1 %collective-permute-start.1 = (bf16[32,4096]{1,0:T(8,128)(2,1)S(1)}, bf16[32,4096]{1,0:T(8,128)(2,1)S(1)}, u32[]{:S(2)}, u32[]{:S(2)}) collective-permute-start(bf16[32,4096]{1,0:T(8,128)(2,1)S(1)} %get-tuple-element.16), channel_id=1, source_target_pairs={{0,4},{1,3},{4,8},{5,1},{8,12},{9,5},{12,14},{13,9},{14,10},{15,13... | collective-permute-start | bytes 786440 | tf_op jit(solution)/shard_map/ppermute | solution.py:39
  9.2 5.8 %collective-permute-start.11 = (bf16[32,4096]{1,0:T(8,128)(2,1)S(1)}, bf16[32,4096]{1,0:T(8,128)(2,1)S(1)}, u32[]{:S(2)}, u32[]{:S(2)}) collective-permute-start(bf16[32,4096]{1,0:T(8,128)(2,1)S(1)} %collective-permute-done.9), channel_id=1, source_target_pairs={{0,4},{1,3},{4,8},{5,1},{8,12},{9,5},{12,14},{13,9},{14,10},{15,13... | collective-permute-start | bytes 786440 | tf_op jit(solution)/shard_map/ppermute | solution.py:39
  10.6 8.4 %collective-permute-start.10 = (bf16[32,4096]{1,0:T(8,128)(2,1)S(1)}, bf16[32,4096]{1,0:T(8,128)(2,1)S(1)}, u32[]{:S(2)}, u32[]{:S(2)}) collective-permute-start(bf16[32,4096]{1,0:T(8,128)(2,1)S(1)} %collective-permute-done.9), channel_id=1, source_target_pairs={{0,1},{1,0},{2,3},{3,2},{4,5},{5,4},{6,7},{7,6},{8,9},{9,8},{10,11... | collective-permute-start | bytes 786440 | tf_op jit(solution)/shard_map/ppermute | solution.py:40
  12.2 6.4 %collective-permute-start.3 = (bf16[32,4096]{1,0:T(8,128)(2,1)S(1)}, bf16[32,4096]{1,0:T(8,128)(2,1)S(1)}, u32[]{:S(2)}, u32[]{:S(2)}) collective-permute-start(bf16[32,4096]{1,0:T(8,128)(2,1)S(1)} %collective-permute-done.1), channel_id=1, source_target_pairs={{0,4},{1,3},{4,8},{5,1},{8,12},{9,5},{12,14},{13,9},{14,10},{15,13... | collective-permute-start | bytes 786440 | tf_op jit(solution)/shard_map/ppermute | solution.py:39
  13.5 8.0 %collective-permute-start.2 = (bf16[32,4096]{1,0:T(8,128)(2,1)S(1)}, bf16[32,4096]{1,0:T(8,128)(2,1)S(1)}, u32[]{:S(2)}, u32[]{:S(2)}) collective-permute-start(bf16[32,4096]{1,0:T(8,128)(2,1)S(1)} %collective-permute-done.1), channel_id=1, source_target_pairs={{0,1},{1,0},{2,3},{3,2},{4,5},{5,4},{6,7},{7,6},{8,9},{9,8},{10,11... | collective-permute-start | bytes 786440 | tf_op jit(solution)/shard_map/ppermute | solution.py:40
  15.1 6.4 %collective-permute-start.13 = (bf16[32,4096]{1,0:T(8,128)(2,1)S(1)}, bf16[32,4096]{1,0:T(8,128)(2,1)S(1)}, u32[]{:S(2)}, u32[]{:S(2)}) collective-permute-start(bf16[32,4096]{1,0:T(8,128)(2,1)S(1)} %collective-permute-done.11), channel_id=1, source_target_pairs={{0,4},{1,3},{4,8},{5,1},{8,12},{9,5},{12,14},{13,9},{14,10},{15,13... | collective-permute-start | bytes 786440 | tf_op jit(solution)/shard_map/ppermute | solution.py:39
  16.3 11.6 %collective-permute-start.12 = (bf16[32,4096]{1,0:T(8,128)(2,1)S(1)}, bf16[32,4096]{1,0:T(8,128)(2,1)S(1)}, u32[]{:S(2)}, u32[]{:S(2)}) collective-permute-start(bf16[32,4096]{1,0:T(8,128)(2,1)S(1)} %collective-permute-done.11), channel_id=1, source_target_pairs={{0,1},{1,0},{2,3},{3,2},{4,5},{5,4},{6,7},{7,6},{8,9},{9,8},{10,11... | collective-permute-start | bytes 786440 | tf_op jit(solution)/shard_map/ppermute | solution.py:40
  18.6 5.5 %collective-permute-start.5 = (bf16[32,4096]{1,0:T(8,128)(2,1)S(1)}, bf16[32,4096]{1,0:T(8,128)(2,1)S(1)}, u32[]{:S(2)}, u32[]{:S(2)}) collective-permute-start(bf16[32,4096]{1,0:T(8,128)(2,1)S(1)} %collective-permute-done.3), channel_id=1, source_target_pairs={{0,4},{1,3},{4,8},{5,1},{8,12},{9,5},{12,14},{13,9},{14,10},{15,13... | collective-permute-start | bytes 786440 | tf_op jit(solution)/shard_map/ppermute | solution.py:39
  19.1 8.8 %collective-permute-start.4 = (bf16[32,4096]{1,0:T(8,128)(2,1)S(1)}, bf16[32,4096]{1,0:T(8,128)(2,1)S(1)}, u32[]{:S(2)}, u32[]{:S(2)}) collective-permute-start(bf16[32,4096]{1,0:T(8,128)(2,1)S(1)} %collective-permute-done.3), channel_id=1, source_target_pairs={{0,1},{1,0},{2,3},{3,2},{4,5},{5,4},{6,7},{7,6},{8,9},{9,8},{10,11... | collective-permute-start | bytes 786440 | tf_op jit(solution)/shard_map/ppermute | solution.py:40
  21.5 10.2 %copy-start = (bf16[512,4096]{1,0:T(8,128)(2,1)S(1)}, bf16[512,4096]{1,0:T(8,128)(2,1)}, u32[]{:S(2)}) copy-start(bf16[512,4096]{1,0:T(8,128)(2,1)} %queries.1) | copy-start | bytes 12582916
  21.6 6.4 %collective-permute-start.15 = (bf16[16,4096]{1,0:T(8,128)(2,1)S(1)}, bf16[16,4096]{1,0:T(8,128)(2,1)S(1)}, u32[]{:S(2)}, u32[]{:S(2)}) collective-permute-start(bf16[16,4096]{1,0:T(8,128)(2,1)S(1)} %slice.19), channel_id=1, source_target_pairs={{0,4},{1,3},{4,8},{5,1},{8,12},{9,5},{12,14},{13,9},{14,10},{15,13... | collective-permute-start | bytes 393224 | tf_op jit(solution)/shard_map/ppermute | solution.py:42
  24.1 4.4 %collective-permute-start.7 = (bf16[16,4096]{1,0:T(8,128)(2,1)S(1)}, bf16[16,4096]{1,0:T(8,128)(2,1)S(1)}, u32[]{:S(2)}, u32[]{:S(2)}) collective-permute-start(bf16[16,4096]{1,0:T(8,128)(2,1)S(1)} %slice.18), channel_id=1, source_target_pairs={{0,4},{1,3},{4,8},{5,1},{8,12},{9,5},{12,14},{13,9},{14,10},{15,13... | collective-permute-start | bytes 393224 | tf_op jit(solution)/shard_map/ppermute | solution.py:42
  24.8 6.0 %collective-permute-start.14 = (bf16[32,4096]{1,0:T(8,128)(2,1)S(1)}, bf16[32,4096]{1,0:T(8,128)(2,1)S(1)}, u32[]{:S(2)}, u32[]{:S(2)}) collective-permute-start(bf16[32,4096]{1,0:T(8,128)(2,1)S(1)} %collective-permute-done.13), channel_id=1, source_target_pairs={{0,1},{1,0},{2,3},{3,2},{4,5},{5,4},{6,7},{7,6},{8,9},{9,8},{10,11... | collective-permute-start | bytes 786440 | tf_op jit(solution)/shard_map/ppermute | solution.py:40
  27.8 2.9 %collective-permute-start.6 = (bf16[32,4096]{1,0:T(8,128)(2,1)S(1)}, bf16[32,4096]{1,0:T(8,128)(2,1)S(1)}, u32[]{:S(2)}, u32[]{:S(2)}) collective-permute-start(bf16[32,4096]{1,0:T(8,128)(2,1)S(1)} %collective-permute-done.5), channel_id=1, source_target_pairs={{0,1},{1,0},{2,3},{3,2},{4,5},{5,4},{6,7},{7,6},{8,9},{9,8},{10,11... | collective-permute-start | bytes 786440 | tf_op jit(solution)/shard_map/ppermute | solution.py:40
  28.0 6.5 %collective-permute-start.16 = (bf16[16,4096]{1,0:T(8,128)(2,1)S(1)}, bf16[16,4096]{1,0:T(8,128)(2,1)S(1)}, u32[]{:S(2)}, u32[]{:S(2)}) collective-permute-start(bf16[16,4096]{1,0:T(8,128)(2,1)S(1)} %collective-permute-done.15), channel_id=1, source_target_pairs={{0,1},{1,0},{2,3},{3,2},{4,5},{5,4},{6,7},{7,6},{8,9},{9,8},{10,11... | collective-permute-start | bytes 393224 | tf_op jit(solution)/shard_map/ppermute | solution.py:43
  28.5 3.2 %collective-permute-start.8 = (bf16[16,4096]{1,0:T(8,128)(2,1)S(1)}, bf16[16,4096]{1,0:T(8,128)(2,1)S(1)}, u32[]{:S(2)}, u32[]{:S(2)}) collective-permute-start(bf16[16,4096]{1,0:T(8,128)(2,1)S(1)} %collective-permute-done.7), channel_id=1, source_target_pairs={{0,1},{1,0},{2,3},{3,2},{4,5},{5,4},{6,7},{7,6},{8,9},{9,8},{10,11... | collective-permute-start | bytes 393224 | tf_op jit(solution)/shard_map/ppermute | solution.py:43

commit v6 on v5

--- a/solution.py
+++ b/solution.py
@@ -31,17 +31,29 @@
     return [(i, i ^ 1) for i in range(size)]
 
 
-def gather_pieces(block, size):
+def gather_panels(panels, size):
     twins, ring = core_pairs(size), ring_pairs(size)
     chips = size // 2
-    pieces = [block]
+
+    def hop(block):
+        return lax.ppermute(block, "samp", ring)
+
+    def hand_over(block):
+        return lax.ppermute(block, "samp", twins)
+
+    mine = list(panels)
+    other = [hand_over(p) for p in mine]
+    pieces = [[m, o] for m, o in zip(mine, other)]
     for _ in range((chips - 1) // 2):
-        block = lax.ppermute(block, "samp", ring)
-        pieces += [block, lax.ppermute(block, "samp", twins)]
+        for i in range(len(panels)):
+            mine[i], other[i] = hop(mine[i]), hop(other[i])
+            both = jnp.concatenate([mine[i], other[i]], axis=0)
+            pieces[i] += [both, hand_over(both)]
     if chips % 2 == 0:
-        block = lax.ppermute(block[: block.shape[0] // 2], "samp", ring)
-        pieces += [block, lax.ppermute(block, "samp", twins)]
-    return pieces
+        for i in range(len(panels)):
+            mine[i] = hop(mine[i])
+            pieces[i] += [mine[i], hand_over(mine[i])]
+    return [jnp.concatenate(p, axis=0) for p in pieces]
 
 
 def row_groups(rows, step):
@@ -151,11 +163,7 @@
 
 def body(queries, gen_panel, ref_panel):
     size = lax.axis_size("samp")
-    own = lax.optimization_barrier(jnp.stack([ref_panel, gen_panel]))
-    other = lax.ppermute(own, "samp", core_pairs(size))
-    chip = jnp.concatenate([own, other], axis=1)
-    ref_all = jnp.concatenate(gather_pieces(chip[0], size), axis=0)
-    gen_all = jnp.concatenate(gather_pieces(chip[1], size), axis=0)
+    gen_all, ref_all = gather_panels([gen_panel, ref_panel], size)
     probes, mean, ref_log = score_ref(queries, ref_all)
     return score_gen(probes, mean, gen_all, ref_log).reshape(-1)
 

time: 37 us -> 44.1 us (1.19)
  starting transfers between devices: 22.8 us -> 28.6 us
  local copies, waits for them, and re-layouts: 0.3 us -> 2.14 us
  other arithmetic: 1.09 us -> 0.11 us
  waiting for transfers between devices: 7.37 us -> 7.86 us
    ppermute x17 -> x24, starting transfers between devices: 22.8 us -> 28.6 us  [the longest x10 16 us: hand_over(): return lax.ppermute(block, 'samp', twins)]
    unnamed x16 -> x26, local copies, waits for them, and re-layouts: 0.26 us -> 2.12 us
    another operation x1 -> x0, other arithmetic: 0.99 us -> none  [body(): own = lax.optimization_barrier(jnp.stack([ref_panel, gen_panel]))]
    ppermute x17 -> x24, waiting for transfers between devices: 7.37 us -> 7.86 us  [the longest x14 6.74 us: hop(): return lax.ppermute(block, 'samp', ring)]
  transfers between devices with their start and end apart: 17 -> 24, of which waited for: 4 -> 7; matrix products, arithmetic and copies ran while one was open for 1% -> 5% of each run, Pallas kernels for 7% -> 6%
where the time goes in v6:
time: 44.1 us; the launch traced here: 43.8 us
  starting transfers between devices  28.6 us (65%)
  waiting for transfers between devices  7.86 us (18%)
  Pallas kernels  4.76 us (11%)
  local copies, waits for them, and re-layouts  2.14 us (5%)
    ppermute x10, starting transfers between devices, hand_over(): return lax.ppermute(block, 'samp', twins)  16 us
    ppermute x14, starting transfers between devices, hop(): return lax.ppermute(block, 'samp', ring)  12.7 us
    ppermute x14, waiting for transfers between devices, hop(): return lax.ppermute(block, 'samp', ring)  6.74 us
    pallas_call x1, Pallas kernels, score_ref(): pl.pallas_call(ref_kernel, out_shape=(jax.ShapeDtypeStruct((count, featur...  2.72 us
    unnamed x26, local copies, waits for them, and re-layouts  2.12 us
    pallas_call x1, Pallas kernels, score_gen(): pl.pallas_call(gen_kernel, out_shape=jax.ShapeDtypeStruct((1, probes.shap...  2.04 us
    ppermute x10, waiting for transfers between devices, hand_over(): return lax.ppermute(block, 'samp', twins)  1.12 us
  transfers between devices with their start and end apart: 24, of which 7 were waited for; matrix products, arithmetic and copies ran while one was open for 5% of the time, Pallas kernels for 6%

profile of v6, /device:TPU:1, one launch (start us, length us, event | category | flops | bytes accessed | tf_op | source)
XLA Modules:
  0.0 43.8 jit_solution(4930326602493961679)
XLA Ops:
  0.0 0.1 collective-permute-start.12
  0.1 2.7 %collective-permute-start.13 = (bf16[16,4096]{1,0:T(8,128)(2,1)}, bf16[16,4096]{1,0:T(8,128)(2,1)S(1)}, u32[]{:S(2)}, u32[]{:S(2)}) collective-permute-start(bf16[16,4096]{1,0:T(8,128)(2,1)} %param.4), channel_id=1, source_target_pairs={{0,4},{1,3},{4,8},{5,1},{8,12},{9,5},{12,14},{13,9},{14,10},{15,13... | collective-permute-start | bytes 393224 | tf_op jit(solution)/shard_map/ppermute | solution.py:39
  2.7 0.3 collective-permute-start
  3.1 1.0 %collective-permute-start.1 = (bf16[16,4096]{1,0:T(8,128)(2,1)}, bf16[16,4096]{1,0:T(8,128)(2,1)S(1)}, u32[]{:S(2)}, u32[]{:S(2)}) collective-permute-start(bf16[16,4096]{1,0:T(8,128)(2,1)} %param.5), channel_id=1, source_target_pairs={{0,4},{1,3},{4,8},{5,1},{8,12},{9,5},{12,14},{13,9},{14,10},{15,13... | collective-permute-start | bytes 393224 | tf_op jit(solution)/shard_map/ppermute | solution.py:39
  4.0 0.9 %constant_dynamic-update-slice_fusion.25 = bf16[256,4096]{1,0:T(8,128)(2,1)S(1)} fusion(bf16[16,4096]{1,0:T(8,128)(2,1)} %param.4), kind=kLoop, calls=%fused_computation.31 | loop fusion | bytes 262144
  5.0 0.9 %constant_dynamic-update-slice_fusion.12 = bf16[256,4096]{1,0:T(8,128)(2,1)S(1)} fusion(bf16[16,4096]{1,0:T(8,128)(2,1)} %param.5), kind=kLoop, calls=%fused_computation.18 | loop fusion | bytes 262144
  5.9 0.0 collective-permute-done.12
  5.9 1.3 %collective-permute-start.14 = (bf16[16,4096]{1,0:T(8,128)(2,1)S(1)}, bf16[16,4096]{1,0:T(8,128)(2,1)S(1)}, u32[]{:S(2)}, u32[]{:S(2)}) collective-permute-start(bf16[16,4096]{1,0:T(8,128)(2,1)S(1)} %collective-permute-done.12), channel_id=1, source_target_pairs={{0,4},{1,3},{4,8},{5,1},{8,12},{9,5},{12,14},{13,9},{14,10},{15,13... | collective-permute-start | bytes 393224 | tf_op jit(solution)/shard_map/ppermute | solution.py:39
  7.2 0.0 collective-permute-done.13
  7.2 1.3 %collective-permute-start.16 = (bf16[16,4096]{1,0:T(8,128)(2,1)S(1)}, bf16[16,4096]{1,0:T(8,128)(2,1)S(1)}, u32[]{:S(2)}, u32[]{:S(2)}) collective-permute-start(bf16[16,4096]{1,0:T(8,128)(2,1)S(1)} %collective-permute-done.13), channel_id=1, source_target_pairs={{0,4},{1,3},{4,8},{5,1},{8,12},{9,5},{12,14},{13,9},{14,10},{15,13... | collective-permute-start | bytes 393224 | tf_op jit(solution)/shard_map/ppermute | solution.py:39
  8.5 0.0 collective-permute-done
  8.5 0.5 %collective-permute-start.2 = (bf16[16,4096]{1,0:T(8,128)(2,1)S(1)}, bf16[16,4096]{1,0:T(8,128)(2,1)S(1)}, u32[]{:S(2)}, u32[]{:S(2)}) collective-permute-start(bf16[16,4096]{1,0:T(8,128)(2,1)S(1)} %collective-permute-done), channel_id=1, source_target_pairs={{0,4},{1,3},{4,8},{5,1},{8,12},{9,5},{12,14},{13,9},{14,10},{15,13... | collective-permute-start | bytes 393224 | tf_op jit(solution)/shard_map/ppermute | solution.py:39
  9.0 0.0 collective-permute-done.1
  9.0 1.3 %collective-permute-start.4 = (bf16[16,4096]{1,0:T(8,128)(2,1)S(1)}, bf16[16,4096]{1,0:T(8,128)(2,1)S(1)}, u32[]{:S(2)}, u32[]{:S(2)}) collective-permute-start(bf16[16,4096]{1,0:T(8,128)(2,1)S(1)} %collective-permute-done.1), channel_id=1, source_target_pairs={{0,4},{1,3},{4,8},{5,1},{8,12},{9,5},{12,14},{13,9},{14,10},{15,13... | collective-permute-start | bytes 393224 | tf_op jit(solution)/shard_map/ppermute | solution.py:39
  10.4 0.0 collective-permute-done.14
  10.4 1.7 %collective-permute-start.15 = (bf16[32,4096]{1,0:T(8,128)(2,1)S(1)}, bf16[32,4096]{1,0:T(8,128)(2,1)S(1)}, u32[]{:S(2)}, u32[]{:S(2)}) collective-permute-start(bf16[32,4096]{1,0:T(8,128)(2,1)S(1)} %pad_maximum_fusion.3), channel_id=1, source_target_pairs={{0,1},{1,0},{2,3},{3,2},{4,5},{5,4},{6,7},{7,6},{8,9},{9,8},{10,11... | collective-permute-start | bytes 786440 | tf_op jit(solution)/shard_map/ppermute | solution.py:42
  12.1 0.8 %collective-permute-done.2 = bf16[16,4096]{1,0:T(8,128)(2,1)S(1)} collective-permute-done((bf16[16,4096]{1,0:T(8,128)(2,1)S(1)}, bf16[16,4096]{1,0:T(8,128)(2,1)S(1)}, u32[]{:S(2)}, u32[]{:S(2)}) %collective-permute-start.2) | collective-permute-done | bytes 131104 | tf_op jit(solution)/shard_map/ppermute | solution.py:39
  12.9 1.8 %collective-permute-start.3 = (bf16[32,4096]{1,0:T(8,128)(2,1)S(1)}, bf16[32,4096]{1,0:T(8,128)(2,1)S(1)}, u32[]{:S(2)}, u32[]{:S(2)}) collective-permute-start(bf16[32,4096]{1,0:T(8,128)(2,1)S(1)} %pad_maximum_fusion), channel_id=1, source_target_pairs={{0,1},{1,0},{2,3},{3,2},{4,5},{5,4},{6,7},{7,6},{8,9},{9,8},{10,11... | collective-permute-start | bytes 786440 | tf_op jit(solution)/shard_map/ppermute | solution.py:42
  14.7 0.2 collective-permute-start.17
  15.0 0.0 collective-permute-done.16
  15.0 1.2 %collective-permute-start.5 = (bf16[16,4096]{1,0:T(8,128)(2,1)S(1)}, bf16[16,4096]{1,0:T(8,128)(2,1)S(1)}, u32[]{:S(2)}, u32[]{:S(2)}) collective-permute-start(bf16[16,4096]{1,0:T(8,128)(2,1)S(1)} %collective-permute-done.2), channel_id=1, source_target_pairs={{0,4},{1,3},{4,8},{5,1},{8,12},{9,5},{12,14},{13,9},{14,10},{15,13... | collective-permute-start | bytes 393224 | tf_op jit(solution)/shard_map/ppermute | solution.py:39
  16.2 0.0 collective-permute-done.4
  16.2 1.3 %collective-permute-start.19 = (bf16[16,4096]{1,0:T(8,128)(2,1)S(1)}, bf16[16,4096]{1,0:T(8,128)(2,1)S(1)}, u32[]{:S(2)}, u32[]{:S(2)}) collective-permute-start(bf16[16,4096]{1,0:T(8,128)(2,1)S(1)} %collective-permute-done.16), channel_id=1, source_target_pairs={{0,4},{1,3},{4,8},{5,1},{8,12},{9,5},{12,14},{13,9},{14,10},{15,13... | collective-permute-start | bytes 393224 | tf_op jit(solution)/shard_map/ppermute | solution.py:39
  17.5 1.4 %collective-permute-done.17 = bf16[16,4096]{1,0:T(8,128)(2,1)S(1)} collective-permute-done((bf16[16,4096]{1,0:T(8,128)(2,1)S(1)}, bf16[16,4096]{1,0:T(8,128)(2,1)S(1)}, u32[]{:S(2)}, u32[]{:S(2)}) %collective-permute-start.17) | collective-permute-done | bytes 131104 | tf_op jit(solution)/shard_map/ppermute | solution.py:39
  18.8 0.2 collective-permute-start.7
  19.1 1.2 %collective-permute-done.5 = bf16[16,4096]{1,0:T(8,128)(2,1)S(1)} collective-permute-done((bf16[16,4096]{1,0:T(8,128)(2,1)S(1)}, bf16[16,4096]{1,0:T(8,128)(2,1)S(1)}, u32[]{:S(2)}, u32[]{:S(2)}) %collective-permute-start.5) | collective-permute-done | bytes 131104 | tf_op jit(solution)/shard_map/ppermute | solution.py:39
  20.2 0.2 collective-permute-start.20
  20.5 1.2 %collective-permute-done.19 = bf16[16,4096]{1,0:T(8,128)(2,1)S(1)} collective-permute-done((bf16[16,4096]{1,0:T(8,128)(2,1)S(1)}, bf16[16,4096]{1,0:T(8,128)(2,1)S(1)}, u32[]{:S(2)}, u32[]{:S(2)}) %collective-permute-start.19) | collective-permute-done | bytes 131104 | tf_op jit(solution)/shard_map/ppermute | solution.py:39
  21.6 1.1 %collective-permute-start.18 = (bf16[32,4096]{1,0:T(8,128)(2,1)S(1)}, bf16[32,4096]{1,0:T(8,128)(2,1)S(1)}, u32[]{:S(2)}, u32[]{:S(2)}) collective-permute-start(bf16[32,4096]{1,0:T(8,128)(2,1)S(1)} %pad_maximum_fusion.4), channel_id=1, source_target_pairs={{0,1},{1,0},{2,3},{3,2},{4,5},{5,4},{6,7},{7,6},{8,9},{9,8},{10,11... | collective-permute-start | bytes 786440 | tf_op jit(solution)/shard_map/ppermute | solution.py:42
  22.8 1.7 %collective-permute-done.20 = bf16[16,4096]{1,0:T(8,128)(2,1)S(1)} collective-permute-done((bf16[16,4096]{1,0:T(8,128)(2,1)S(1)}, bf16[16,4096]{1,0:T(8,128)(2,1)S(1)}, u32[]{:S(2)}, u32[]{:S(2)}) %collective-permute-start.20) | collective-permute-done | bytes 131104 | tf_op jit(solution)/shard_map/ppermute | solution.py:39
  24.5 0.1 collective-permute-start.8
  24.6 0.0 collective-permute-done.7
  24.6 3.1 %collective-permute-start.6 = (bf16[32,4096]{1,0:T(8,128)(2,1)S(1)}, bf16[32,4096]{1,0:T(8,128)(2,1)S(1)}, u32[]{:S(2)}, u32[]{:S(2)}) collective-permute-start(bf16[32,4096]{1,0:T(8,128)(2,1)S(1)} %pad_maximum_fusion.1), channel_id=1, source_target_pairs={{0,1},{1,0},{2,3},{3,2},{4,5},{5,4},{6,7},{7,6},{8,9},{9,8},{10,11... | collective-permute-start | bytes 786440 | tf_op jit(solution)/shard_map/ppermute | solution.py:42
  27.7 0.6 %collective-permute-done.8 = bf16[16,4096]{1,0:T(8,128)(2,1)S(1)} collective-permute-done((bf16[16,4096]{1,0:T(8,128)(2,1)S(1)}, bf16[16,4096]{1,0:T(8,128)(2,1)S(1)}, u32[]{:S(2)}, u32[]{:S(2)}) %collective-permute-start.8) | collective-permute-done | bytes 131104 | tf_op jit(solution)/shard_map/ppermute | solution.py:39
  28.3 0.1 collective-permute-start.22
  28.4 0.0 collective-permute-done.15
  28.4 1.3 %collective-permute-start.10 = (bf16[16,4096]{1,0:T(8,128)(2,1)S(1)}, bf16[16,4096]{1,0:T(8,128)(2,1)S(1)}, u32[]{:S(2)}, u32[]{:S(2)}) collective-permute-start(bf16[16,4096]{1,0:T(8,128)(2,1)S(1)} %collective-permute-done.7), channel_id=1, source_target_pairs={{0,4},{1,3},{4,8},{5,1},{8,12},{9,5},{12,14},{13,9},{14,10},{15,13... | collective-permute-start | bytes 393224 | tf_op jit(solution)/shard_map/ppermute | solution.py:39
  29.8 0.0 collective-permute-done.3
  29.8 4.4 %collective-permute-start.21 = (bf16[32,4096]{1,0:T(8,128)(2,1)S(1)}, bf16[32,4096]{1,0:T(8,128)(2,1)S(1)}, u32[]{:S(2)}, u32[]{:S(2)}) collective-permute-start(bf16[32,4096]{1,0:T(8,128)(2,1)S(1)} %pad_maximum_fusion.5), channel_id=1, source_target_pairs={{0,1},{1,0},{2,3},{3,2},{4,5},{5,4},{6,7},{7,6},{8,9},{9,8},{10,11... | collective-permute-start | bytes 786440 | tf_op jit(solution)/shard_map/ppermute | solution.py:42
  34.1 0.0 copy-start
  34.2 0.0 collective-permute-done.22
  34.2 2.0 %collective-permute-start.9 = (bf16[32,4096]{1,0:T(8,128)(2,1)S(1)}, bf16[32,4096]{1,0:T(8,128)(2,1)S(1)}, u32[]{:S(2)}, u32[]{:S(2)}) collective-permute-start(bf16[32,4096]{1,0:T(8,128)(2,1)S(1)} %pad_maximum_fusion.2), channel_id=1, source_target_pairs={{0,1},{1,0},{2,3},{3,2},{4,5},{5,4},{6,7},{7,6},{8,9},{9,8},{10,11... | collective-permute-start | bytes 786440 | tf_op jit(solution)/shard_map/ppermute | solution.py:42
  36.2 0.0 collective-permute-done.10
  36.2 1.5 %collective-permute-start.23 = (bf16[16,4096]{1,0:T(8,128)(2,1)S(1)}, bf16[16,4096]{1,0:T(8,128)(2,1)S(1)}, u32[]{:S(2)}, u32[]{:S(2)}) collective-permute-start(bf16[16,4096]{1,0:T(8,128)(2,1)S(1)} %collective-permute-done.22), channel_id=1, source_target_pairs={{0,1},{1,0},{2,3},{3,2},{4,5},{5,4},{6,7},{7,6},{8,9},{9,8},{10,11... | collective-permute-start | bytes 393224 | tf_op jit(solution)/shard_map/ppermute | solution.py:42
  37.6 0.0 collective-permute-done.18
  37.6 0.0 collective-permute-start.11
  37.7 0.0 collective-permute-done.6
  37.8 0.0 collective-permute-done.21
  37.8 0.0 collective-permute-done.9
  37.9 1.1 %collective-permute-done.11 = bf16[16,4096]{1,0:T(8,128)(2,1)S(1)} collective-permute-done((bf16[16,4096]{1,0:T(8,128)(2,1)S(1)}, bf16[16,4096]{1,0:T(8,128)(2,1)S(1)}, u32[]{:S(2)}, u32[]{:S(2)}) %collective-permute-start.11) | collective-permute-done | bytes 131104 | tf_op jit(solution)/shard_map/ppermute | solution.py:42
  39.0 0.0 copy-done
  39.0 2.7 %shard_map.37 = (bf16[512,4096]{1,0:T(8,128)(2,1)S(1)}, f32[1,4096]{1,0:T(1,128)S(1)}, f32[1,512]{1,0:T(1,128)S(1)}) custom-call(bf16[512,4096]{1,0:T(8,128)(2,1)S(1)} %copy-done, bf16[256,4096]{1,0:T(8,128)(2,1)S(1)} %constant_dynamic-update-slice_fusion.panel), custom_call_target="tpu_custom_call" | custom-call | flops 1073741824 | bytes 6291456 | tf_op jit(solution)/shard_map/pallas_call | solution.py:137
  41.7 0.0 collective-permute-done.23
  41.8 2.0 %shard_map.38 = f32[1,512]{1,0:T(1,128)} custom-call(bf16[512,4096]{1,0:T(8,128)(2,1)S(1)} %get-tuple-element.8.probes, f32[1,4096]{1,0:T(1,128)S(1)} %get-tuple-element.9.mean, bf16[256,4096]{1,0:T(8,128)(2,1)S(1)} %constant_dynamic-update-slice_fusion.13.panel, f32[1,512]{1,0:T(1,128)S(1)} %get-tuple-element.10.ref_log), custom_call_target="tpu_custom_call" | custom-call | flops 1073741824 | bytes 6291456 | tf_op jit(solution)/shard_map/pallas_call | solution.py:153
  (30 shorter events, 0.4 us)
Async XLA Ops:
  0.0 5.9 %collective-permute-start.12 = (bf16[16,4096]{1,0:T(8,128)(2,1)}, bf16[16,4096]{1,0:T(8,128)(2,1)S(1)}, u32[]{:S(2)}, u32[]{:S(2)}) collective-permute-start(bf16[16,4096]{1,0:T(8,128)(2,1)} %param.4), channel_id=1, source_target_pairs={{0,1},{1,0},{2,3},{3,2},{4,5},{5,4},{6,7},{7,6},{8,9},{9,8},{10,11... | collective-permute-start | bytes 393224 | tf_op jit(solution)/shard_map/ppermute | solution.py:42
  0.1 7.2 %collective-permute-start.13 = (bf16[16,4096]{1,0:T(8,128)(2,1)}, bf16[16,4096]{1,0:T(8,128)(2,1)S(1)}, u32[]{:S(2)}, u32[]{:S(2)}) collective-permute-start(bf16[16,4096]{1,0:T(8,128)(2,1)} %param.4), channel_id=1, source_target_pairs={{0,4},{1,3},{4,8},{5,1},{8,12},{9,5},{12,14},{13,9},{14,10},{15,13... | collective-permute-start | bytes 393224 | tf_op jit(solution)/shard_map/ppermute | solution.py:39
  2.7 5.8 %collective-permute-start = (bf16[16,4096]{1,0:T(8,128)(2,1)}, bf16[16,4096]{1,0:T(8,128)(2,1)S(1)}, u32[]{:S(2)}, u32[]{:S(2)}) collective-permute-start(bf16[16,4096]{1,0:T(8,128)(2,1)} %param.5), channel_id=1, source_target_pairs={{0,1},{1,0},{2,3},{3,2},{4,5},{5,4},{6,7},{7,6},{8,9},{9,8},{10,11... | collective-permute-start | bytes 393224 | tf_op jit(solution)/shard_map/ppermute | solution.py:42
  3.1 5.9 %collective-permute-start.1 = (bf16[16,4096]{1,0:T(8,128)(2,1)}, bf16[16,4096]{1,0:T(8,128)(2,1)S(1)}, u32[]{:S(2)}, u32[]{:S(2)}) collective-permute-start(bf16[16,4096]{1,0:T(8,128)(2,1)} %param.5), channel_id=1, source_target_pairs={{0,4},{1,3},{4,8},{5,1},{8,12},{9,5},{12,14},{13,9},{14,10},{15,13... | collective-permute-start | bytes 393224 | tf_op jit(solution)/shard_map/ppermute | solution.py:39
  5.9 4.5 %collective-permute-start.14 = (bf16[16,4096]{1,0:T(8,128)(2,1)S(1)}, bf16[16,4096]{1,0:T(8,128)(2,1)S(1)}, u32[]{:S(2)}, u32[]{:S(2)}) collective-permute-start(bf16[16,4096]{1,0:T(8,128)(2,1)S(1)} %collective-permute-done.12), channel_id=1, source_target_pairs={{0,4},{1,3},{4,8},{5,1},{8,12},{9,5},{12,14},{13,9},{14,10},{15,13... | collective-permute-start | bytes 393224 | tf_op jit(solution)/shard_map/ppermute | solution.py:39
  7.2 7.7 %collective-permute-start.16 = (bf16[16,4096]{1,0:T(8,128)(2,1)S(1)}, bf16[16,4096]{1,0:T(8,128)(2,1)S(1)}, u32[]{:S(2)}, u32[]{:S(2)}) collective-permute-start(bf16[16,4096]{1,0:T(8,128)(2,1)S(1)} %collective-permute-done.13), channel_id=1, source_target_pairs={{0,4},{1,3},{4,8},{5,1},{8,12},{9,5},{12,14},{13,9},{14,10},{15,13... | collective-permute-start | bytes 393224 | tf_op jit(solution)/shard_map/ppermute | solution.py:39
  8.5 4.3 %collective-permute-start.2 = (bf16[16,4096]{1,0:T(8,128)(2,1)S(1)}, bf16[16,4096]{1,0:T(8,128)(2,1)S(1)}, u32[]{:S(2)}, u32[]{:S(2)}) collective-permute-start(bf16[16,4096]{1,0:T(8,128)(2,1)S(1)} %collective-permute-done), channel_id=1, source_target_pairs={{0,4},{1,3},{4,8},{5,1},{8,12},{9,5},{12,14},{13,9},{14,10},{15,13... | collective-permute-start | bytes 393224 | tf_op jit(solution)/shard_map/ppermute | solution.py:39
  9.0 7.2 %collective-permute-start.4 = (bf16[16,4096]{1,0:T(8,128)(2,1)S(1)}, bf16[16,4096]{1,0:T(8,128)(2,1)S(1)}, u32[]{:S(2)}, u32[]{:S(2)}) collective-permute-start(bf16[16,4096]{1,0:T(8,128)(2,1)S(1)} %collective-permute-done.1), channel_id=1, source_target_pairs={{0,4},{1,3},{4,8},{5,1},{8,12},{9,5},{12,14},{13,9},{14,10},{15,13... | collective-permute-start | bytes 393224 | tf_op jit(solution)/shard_map/ppermute | solution.py:39
  10.4 18.0 %collective-permute-start.15 = (bf16[32,4096]{1,0:T(8,128)(2,1)S(1)}, bf16[32,4096]{1,0:T(8,128)(2,1)S(1)}, u32[]{:S(2)}, u32[]{:S(2)}) collective-permute-start(bf16[32,4096]{1,0:T(8,128)(2,1)S(1)} %pad_maximum_fusion.3), channel_id=1, source_target_pairs={{0,1},{1,0},{2,3},{3,2},{4,5},{5,4},{6,7},{7,6},{8,9},{9,8},{10,11... | collective-permute-start | bytes 786440 | tf_op jit(solution)/shard_map/ppermute | solution.py:42
  12.9 16.9 %collective-permute-start.3 = (bf16[32,4096]{1,0:T(8,128)(2,1)S(1)}, bf16[32,4096]{1,0:T(8,128)(2,1)S(1)}, u32[]{:S(2)}, u32[]{:S(2)}) collective-permute-start(bf16[32,4096]{1,0:T(8,128)(2,1)S(1)} %pad_maximum_fusion), channel_id=1, source_target_pairs={{0,1},{1,0},{2,3},{3,2},{4,5},{5,4},{6,7},{7,6},{8,9},{9,8},{10,11... | collective-permute-start | bytes 786440 | tf_op jit(solution)/shard_map/ppermute | solution.py:42
  14.7 4.1 %collective-permute-start.17 = (bf16[16,4096]{1,0:T(8,128)(2,1)S(1)}, bf16[16,4096]{1,0:T(8,128)(2,1)S(1)}, u32[]{:S(2)}, u32[]{:S(2)}) collective-permute-start(bf16[16,4096]{1,0:T(8,128)(2,1)S(1)} %collective-permute-done.14), channel_id=1, source_target_pairs={{0,4},{1,3},{4,8},{5,1},{8,12},{9,5},{12,14},{13,9},{14,10},{15,13... | collective-permute-start | bytes 393224 | tf_op jit(solution)/shard_map/ppermute | solution.py:39
  15.0 5.2 %collective-permute-start.5 = (bf16[16,4096]{1,0:T(8,128)(2,1)S(1)}, bf16[16,4096]{1,0:T(8,128)(2,1)S(1)}, u32[]{:S(2)}, u32[]{:S(2)}) collective-permute-start(bf16[16,4096]{1,0:T(8,128)(2,1)S(1)} %collective-permute-done.2), channel_id=1, source_target_pairs={{0,4},{1,3},{4,8},{5,1},{8,12},{9,5},{12,14},{13,9},{14,10},{15,13... | collective-permute-start | bytes 393224 | tf_op jit(solution)/shard_map/ppermute | solution.py:39
  16.2 5.5 %collective-permute-start.19 = (bf16[16,4096]{1,0:T(8,128)(2,1)S(1)}, bf16[16,4096]{1,0:T(8,128)(2,1)S(1)}, u32[]{:S(2)}, u32[]{:S(2)}) collective-permute-start(bf16[16,4096]{1,0:T(8,128)(2,1)S(1)} %collective-permute-done.16), channel_id=1, source_target_pairs={{0,4},{1,3},{4,8},{5,1},{8,12},{9,5},{12,14},{13,9},{14,10},{15,13... | collective-permute-start | bytes 393224 | tf_op jit(solution)/shard_map/ppermute | solution.py:39
  18.8 5.7 %collective-permute-start.7 = (bf16[16,4096]{1,0:T(8,128)(2,1)S(1)}, bf16[16,4096]{1,0:T(8,128)(2,1)S(1)}, u32[]{:S(2)}, u32[]{:S(2)}) collective-permute-start(bf16[16,4096]{1,0:T(8,128)(2,1)S(1)} %collective-permute-done.4), channel_id=1, source_target_pairs={{0,4},{1,3},{4,8},{5,1},{8,12},{9,5},{12,14},{13,9},{14,10},{15,13... | collective-permute-start | bytes 393224 | tf_op jit(solution)/shard_map/ppermute | solution.py:39
  20.2 4.2 %collective-permute-start.20 = (bf16[16,4096]{1,0:T(8,128)(2,1)S(1)}, bf16[16,4096]{1,0:T(8,128)(2,1)S(1)}, u32[]{:S(2)}, u32[]{:S(2)}) collective-permute-start(bf16[16,4096]{1,0:T(8,128)(2,1)S(1)} %collective-permute-done.17), channel_id=1, source_target_pairs={{0,4},{1,3},{4,8},{5,1},{8,12},{9,5},{12,14},{13,9},{14,10},{15,13... | collective-permute-start | bytes 393224 | tf_op jit(solution)/shard_map/ppermute | solution.py:39
  21.6 16.0 %collective-permute-start.18 = (bf16[32,4096]{1,0:T(8,128)(2,1)S(1)}, bf16[32,4096]{1,0:T(8,128)(2,1)S(1)}, u32[]{:S(2)}, u32[]{:S(2)}) collective-permute-start(bf16[32,4096]{1,0:T(8,128)(2,1)S(1)} %pad_maximum_fusion.4), channel_id=1, source_target_pairs={{0,1},{1,0},{2,3},{3,2},{4,5},{5,4},{6,7},{7,6},{8,9},{9,8},{10,11... | collective-permute-start | bytes 786440 | tf_op jit(solution)/shard_map/ppermute | solution.py:42
  24.5 3.8 %collective-permute-start.8 = (bf16[16,4096]{1,0:T(8,128)(2,1)S(1)}, bf16[16,4096]{1,0:T(8,128)(2,1)S(1)}, u32[]{:S(2)}, u32[]{:S(2)}) collective-permute-start(bf16[16,4096]{1,0:T(8,128)(2,1)S(1)} %collective-permute-done.5), channel_id=1, source_target_pairs={{0,4},{1,3},{4,8},{5,1},{8,12},{9,5},{12,14},{13,9},{14,10},{15,13... | collective-permute-start | bytes 393224 | tf_op jit(solution)/shard_map/ppermute | solution.py:39
  24.6 13.1 %collective-permute-start.6 = (bf16[32,4096]{1,0:T(8,128)(2,1)S(1)}, bf16[32,4096]{1,0:T(8,128)(2,1)S(1)}, u32[]{:S(2)}, u32[]{:S(2)}) collective-permute-start(bf16[32,4096]{1,0:T(8,128)(2,1)S(1)} %pad_maximum_fusion.1), channel_id=1, source_target_pairs={{0,1},{1,0},{2,3},{3,2},{4,5},{5,4},{6,7},{7,6},{8,9},{9,8},{10,11... | collective-permute-start | bytes 786440 | tf_op jit(solution)/shard_map/ppermute | solution.py:42
  28.3 5.9 %collective-permute-start.22 = (bf16[16,4096]{1,0:T(8,128)(2,1)S(1)}, bf16[16,4096]{1,0:T(8,128)(2,1)S(1)}, u32[]{:S(2)}, u32[]{:S(2)}) collective-permute-start(bf16[16,4096]{1,0:T(8,128)(2,1)S(1)} %collective-permute-done.19), channel_id=1, source_target_pairs={{0,4},{1,3},{4,8},{5,1},{8,12},{9,5},{12,14},{13,9},{14,10},{15,13... | collective-permute-start | bytes 393224 | tf_op jit(solution)/shard_map/ppermute | solution.py:39
  28.4 7.8 %collective-permute-start.10 = (bf16[16,4096]{1,0:T(8,128)(2,1)S(1)}, bf16[16,4096]{1,0:T(8,128)(2,1)S(1)}, u32[]{:S(2)}, u32[]{:S(2)}) collective-permute-start(bf16[16,4096]{1,0:T(8,128)(2,1)S(1)} %collective-permute-done.7), channel_id=1, source_target_pairs={{0,4},{1,3},{4,8},{5,1},{8,12},{9,5},{12,14},{13,9},{14,10},{15,13... | collective-permute-start | bytes 393224 | tf_op jit(solution)/shard_map/ppermute | solution.py:39
  29.8 8.0 %collective-permute-start.21 = (bf16[32,4096]{1,0:T(8,128)(2,1)S(1)}, bf16[32,4096]{1,0:T(8,128)(2,1)S(1)}, u32[]{:S(2)}, u32[]{:S(2)}) collective-permute-start(bf16[32,4096]{1,0:T(8,128)(2,1)S(1)} %pad_maximum_fusion.5), channel_id=1, source_target_pairs={{0,1},{1,0},{2,3},{3,2},{4,5},{5,4},{6,7},{7,6},{8,9},{9,8},{10,11... | collective-permute-start | bytes 786440 | tf_op jit(solution)/shard_map/ppermute | solution.py:42
  34.1 4.9 %copy-start = (bf16[512,4096]{1,0:T(8,128)(2,1)S(1)}, bf16[512,4096]{1,0:T(8,128)(2,1)}, u32[]{:S(2)}) copy-start(bf16[512,4096]{1,0:T(8,128)(2,1)} %queries.1) | copy-start | bytes 12582916
  34.2 3.6 %collective-permute-start.9 = (bf16[32,4096]{1,0:T(8,128)(2,1)S(1)}, bf16[32,4096]{1,0:T(8,128)(2,1)S(1)}, u32[]{:S(2)}, u32[]{:S(2)}) collective-permute-start(bf16[32,4096]{1,0:T(8,128)(2,1)S(1)} %pad_maximum_fusion.2), channel_id=1, source_target_pairs={{0,1},{1,0},{2,3},{3,2},{4,5},{5,4},{6,7},{7,6},{8,9},{9,8},{10,11... | collective-permute-start | bytes 786440 | tf_op jit(solution)/shard_map/ppermute | solution.py:42
  36.2 5.6 %collective-permute-start.23 = (bf16[16,4096]{1,0:T(8,128)(2,1)S(1)}, bf16[16,4096]{1,0:T(8,128)(2,1)S(1)}, u32[]{:S(2)}, u32[]{:S(2)}) collective-permute-start(bf16[16,4096]{1,0:T(8,128)(2,1)S(1)} %collective-permute-done.22), channel_id=1, source_target_pairs={{0,1},{1,0},{2,3},{3,2},{4,5},{5,4},{6,7},{7,6},{8,9},{9,8},{10,11... | collective-permute-start | bytes 393224 | tf_op jit(solution)/shard_map/ppermute | solution.py:42
  37.6 1.3 %collective-permute-start.11 = (bf16[16,4096]{1,0:T(8,128)(2,1)S(1)}, bf16[16,4096]{1,0:T(8,128)(2,1)S(1)}, u32[]{:S(2)}, u32[]{:S(2)}) collective-permute-start(bf16[16,4096]{1,0:T(8,128)(2,1)S(1)} %collective-permute-done.10), channel_id=1, source_target_pairs={{0,1},{1,0},{2,3},{3,2},{4,5},{5,4},{6,7},{7,6},{8,9},{9,8},{10,11... | collective-permute-start | bytes 393224 | tf_op jit(solution)/shard_map/ppermute | solution.py:42

commit v7 on v6

v7 whole, which is shorter than its diff:
```python
import jax
import jax.numpy as jnp
from jax import lax
from jax.experimental import pallas as pl
from jax.experimental.pallas import tpu as pltpu
from jax.sharding import PartitionSpec as P

TEMP = 64
LANES = 128
CHUNK = 1024
GROUP = 32
LIMIT = 40 * 2**20


def ring_of_chips(chips):
    return list(range(0, chips, 2)) + list(range(chips - 1 - chips % 2, 0, -2))


def ring_pairs(size, way):
    order = ring_of_chips(size // 2)
    pairs = []
    for place, chip in enumerate(order):
        to = order[(place + way) % len(order)]
        pairs += [(2 * chip + core, 2 * to + core) for core in range(2)]
    return pairs


def gather_panels(panels, size):
    chips, rows = size // 2, panels[0].shape[0]
    to_twin = [(i, i ^ 1) for i in range(size)]
    ways = [ring_pairs(size, 1), ring_pairs(size, -1)]

    def hop(block, way):
        return lax.ppermute(block, "samp", ways[way])

    def hand_over(block):
        return lax.ppermute(block, "samp", to_twin)

    chains = [list(panels), list(panels)]
    pieces = [[] for _ in panels]
    steps = (chips - 1) // 2
    if steps == 0:
        pieces = [[hand_over(p)] for p in panels]
    for step in range(steps):
        for i in range(len(panels)):
            for way in range(2):
                chains[way][i] = hop(chains[way][i], way)
        arrived = [[chains[way][i] for way in range(2)] for i in range(len(panels))]
        if step == 0:
            give = [[p] + a for p, a in zip(panels, arrived)]
        else:
            give = arrived
        given = hand_over(jnp.concatenate(give[0] + give[1], axis=0))
        count = rows * len(give[0])
        for i in range(len(panels)):
            pieces[i] += arrived[i] + [given[count * i : count * (i + 1)]]
    if chips % 2 == 0:
        for i in range(len(panels)):
            last = hop(chains[1 - i][i], 1 - i)
            pieces[i] += [last, hand_over(last)]
    return [jnp.concatenate(p, axis=0) for p in pieces]


def row_groups(rows, step):
    return [slice(r, min(r + step, rows)) for r in range(0, rows, step)]


def center(rows, mean):
    return (rows.astype(jnp.float32) - mean).astype(jnp.bfloat16)


def add_panel_chunk(cols, mean, panels, probes, centered, squares, scores, first):
    at = 0
    for panel in panels:
        for rows in row_groups(panel.shape[0], GROUP):
            here = slice(at, at + rows.stop - rows.start)
            at = here.stop
            part = center(panel[rows, cols], mean)
            centered[here, cols] = part
            wide = jnp.square(part.astype(jnp.float32))
            total = wide[:, :LANES]
            for lane in range(LANES, wide.shape[1], LANES):
                total += wide[:, lane : lane + LANES]
            squares[here, :] = total if first else squares[here, :] + total
    products = lax.dot_general(
        centered[:, cols], probes[:, cols], (((1,), (1,)), ((), ())),
        preferred_element_type=jnp.float32,
    )
    scores[...] = products if first else scores[...] + products


def log_sum(squares, scores):
    half = 0.5 * jnp.sum(squares[...], axis=1, keepdims=True)
    x = (scores[...] - half) / TEMP
    top = jnp.max(x, axis=0, keepdims=True)
    return jnp.log(jnp.sum(jnp.exp(x - top), axis=0, keepdims=True)) + top


def ref_kernel(queries, own, others, probes, mean, ref_log, centered, squares, scores):
    panels = (own, others)
    count, features = centered.shape
    for start in range(0, features, CHUNK):
        cols = slice(start, start + CHUNK)
        total = None
        for panel in panels:
            for rows in row_groups(panel.shape[0], GROUP):
                part = jnp.sum(panel[rows, cols].astype(jnp.float32), axis=0, keepdims=True)
                total = part if total is None else total + part
        here = total / count
        mean[:, cols] = here
        for rows in row_groups(queries.shape[0], GROUP):
            probes[rows, cols] = center(queries[rows, cols], here)
        add_panel_chunk(cols, here, panels, probes, centered, squares, scores, start == 0)
    ref_log[...] = log_sum(squares, scores)


def gen_kernel(probes, mean, own, others, ref_log, proof, centered, squares, scores):
    panels = (own, others)
    for start in range(0, centered.shape[1], CHUNK):
        cols = slice(start, start + CHUNK)
        add_panel_chunk(cols, mean[:, cols], panels, probes, centered, squares, scores, start == 0)
    proof[...] = log_sum(squares, scores) - ref_log[...]


def in_vmem(n):
    return [pl.BlockSpec(memory_space=pltpu.VMEM)] * n


def call_options(queries, own, others):
    rows, (count, features) = own.shape[0] + others.shape[0], queries.shape
    return dict(
        scratch_shapes=[
            pltpu.VMEM((rows, features), jnp.bfloat16),
            pltpu.VMEM((rows, LANES), jnp.float32),
            pltpu.VMEM((rows, count), jnp.float32),
        ],
        compiler_params=pltpu.CompilerParams(vmem_limit_bytes=LIMIT),
        cost_estimate=pl.CostEstimate(
            flops=2 * rows * count * features,
            bytes_accessed=2 * (rows + count) * features,
            transcendentals=rows * count,
        ),
    )


def score_ref(queries, own, others):
    count, features = queries.shape
    return pl.pallas_call(
        ref_kernel,
        out_shape=(
            jax.ShapeDtypeStruct((count, features), jnp.bfloat16),
            jax.ShapeDtypeStruct((1, features), jnp.float32),
            jax.ShapeDtypeStruct((1, count), jnp.float32),
        ),
        in_specs=in_vmem(3),
        out_specs=tuple(in_vmem(3)),
        **call_options(queries, own, others),
    )(queries, own, others)


def score_gen(probes, mean, own, others, ref_log):
    return pl.pallas_call(
        gen_kernel,
        out_shape=jax.ShapeDtypeStruct((1, probes.shape[0]), jnp.float32),
        in_specs=in_vmem(5),
        out_specs=in_vmem(1)[0],
        **call_options(probes, own, others),
    )(probes, mean, own, others, ref_log)


def body(queries, gen_panel, ref_panel):
    size = lax.axis_size("samp")
    ref_others, gen_others = gather_panels([ref_panel, gen_panel], size)
    probes, mean, ref_log = score_ref(queries, ref_panel, ref_others)
    return score_gen(probes, mean, gen_panel, gen_others, ref_log).reshape(-1)


def solution(mesh):
    return jax.shard_map(
        body,
        mesh=mesh,
        in_specs=(
            P(("groups", "samp"), None),
            P(("groups", "samp"), None),
            P(("groups", "samp"), None),
        ),
        out_specs=P(("groups", "samp")),
        check_vma=False,
    )
```

time: 44.1 us -> 36 us (0.82)
  starting transfers between devices: 28.6 us -> 23.5 us
  waiting for transfers between devices: 7.86 us -> 3.54 us
  local copies, waits for them, and re-layouts: 2.14 us -> 3.99 us
    ppermute x24 -> x19, starting transfers between devices: 28.6 us -> 23.5 us  [the longest x5 12.5 us: hand_over(): return lax.ppermute(block, 'samp', to_twin)]
    ppermute x24 -> x19, waiting for transfers between devices: 7.86 us -> 3.54 us  [the longest x14 3.38 us: hop(): return lax.ppermute(block, 'samp', ways[way])]
    unnamed x26 -> x25, local copies, waits for them, and re-layouts: 2.12 us -> 3.97 us
  transfers between devices with their start and end apart: 24 -> 19, of which waited for: 7 -> 5; matrix products, arithmetic and copies ran while one was open for 5% -> 6% of each run, Pallas kernels for 6% -> 7%
where the time goes in v7:
time: 36 us; the launch traced here: 35.8 us
  starting transfers between devices  23.5 us (65%)
  Pallas kernels  4.47 us (12%)
  local copies, waits for them, and re-layouts  3.99 us (11%)
  waiting for transfers between devices  3.54 us (10%)
    ppermute x5, starting transfers between devices, hand_over(): return lax.ppermute(block, 'samp', to_twin)  12.5 us
    ppermute x14, starting transfers between devices, hop(): return lax.ppermute(block, 'samp', ways[way])  11 us
    unnamed x25, local copies, waits for them, and re-layouts  3.97 us
    ppermute x14, waiting for transfers between devices, hop(): return lax.ppermute(block, 'samp', ways[way])  3.38 us
    pallas_call x1, Pallas kernels, score_ref(): pl.pallas_call(ref_kernel, out_shape=(jax.ShapeDtypeStruct((count, featur...  2.43 us
    pallas_call x1, Pallas kernels, score_gen(): pl.pallas_call(gen_kernel, out_shape=jax.ShapeDtypeStruct((1, probes.shap...  2.04 us
  transfers between devices with their start and end apart: 19, of which 5 were waited for; matrix products, arithmetic and copies ran while one was open for 6% of the time, Pallas kernels for 7%

profile of v7, /device:TPU:1, one launch (start us, length us, event | category | flops | bytes accessed | tf_op | source)
XLA Modules:
  0.0 35.8 jit_solution(14322651903875495117)
XLA Ops:
  0.0 2.1 %collective-permute-start = (bf16[16,4096]{1,0:T(8,128)(2,1)}, bf16[16,4096]{1,0:T(8,128)(2,1)S(1)}, u32[]{:S(2)}, u32[]{:S(2)}) collective-permute-start(bf16[16,4096]{1,0:T(8,128)(2,1)} %own.2), channel_id=1, source_target_pairs={{0,4},{1,5},{4,8},{5,9},{8,12},{9,13},{12,14},{13,15},{14,10},{15,... | collective-permute-start | bytes 393224 | tf_op jit(solution)/shard_map/ppermute | solution.py:34
  2.1 0.0 collective-permute-start.1
  2.1 1.5 %collective-permute-start.2 = (bf16[16,4096]{1,0:T(8,128)(2,1)}, bf16[16,4096]{1,0:T(8,128)(2,1)S(1)}, u32[]{:S(2)}, u32[]{:S(2)}) collective-permute-start(bf16[16,4096]{1,0:T(8,128)(2,1)} %own.3), channel_id=1, source_target_pairs={{0,4},{1,5},{4,8},{5,9},{8,12},{9,13},{12,14},{13,15},{14,10},{15,... | collective-permute-start | bytes 393224 | tf_op jit(solution)/shard_map/ppermute | solution.py:34
  3.6 0.0 collective-permute-start.3
  3.6 0.9 %constant_dynamic-update-slice_fusion.5 = bf16[96,4096]{1,0:T(8,128)(2,1)S(1)} fusion(bf16[16,4096]{1,0:T(8,128)(2,1)} %own.2), kind=kLoop, calls=%fused_computation.13 | loop fusion | bytes 262144
  4.5 1.0 %collective-permute-done = bf16[16,4096]{1,0:T(8,128)(2,1)S(1)} collective-permute-done((bf16[16,4096]{1,0:T(8,128)(2,1)}, bf16[16,4096]{1,0:T(8,128)(2,1)S(1)}, u32[]{:S(2)}, u32[]{:S(2)}) %collective-permute-start) | collective-permute-done | bytes 131104 | tf_op jit(solution)/shard_map/ppermute | solution.py:34
  5.5 0.9 %collective-permute-done.1 = bf16[16,4096]{1,0:T(8,128)(2,1)S(1)} collective-permute-done((bf16[16,4096]{1,0:T(8,128)(2,1)}, bf16[16,4096]{1,0:T(8,128)(2,1)S(1)}, u32[]{:S(2)}, u32[]{:S(2)}) %collective-permute-start.1) | collective-permute-done | bytes 131104 | tf_op jit(solution)/shard_map/ppermute | solution.py:34
  6.5 0.9 %constant_dynamic-update-slice_fusion.2 = bf16[96,4096]{1,0:T(8,128)(2,1)S(1)} fusion(bf16[96,4096]{1,0:T(8,128)(2,1)S(1)} %get-tuple-element.21, bf16[16,4096]{1,0:T(8,128)(2,1)} %own.3), kind=kLoop, calls=%fused_computation.10 | loop fusion | bytes 262144
  7.4 1.3 %collective-permute-start.5 = (bf16[16,4096]{1,0:T(8,128)(2,1)S(1)}, bf16[16,4096]{1,0:T(8,128)(2,1)S(1)}, u32[]{:S(2)}, u32[]{:S(2)}) collective-permute-start(bf16[16,4096]{1,0:T(8,128)(2,1)S(1)} %collective-permute-done), channel_id=1, source_target_pairs={{0,4},{1,5},{4,8},{5,9},{8,12},{9,13},{12,14},{13,15},{14,10},{15,... | collective-permute-start | bytes 393224 | tf_op jit(solution)/shard_map/ppermute | solution.py:34
  8.7 0.2 collective-permute-start.6
  8.9 0.0 collective-permute-done.2
  8.9 1.3 %collective-permute-start.7 = (bf16[16,4096]{1,0:T(8,128)(2,1)S(1)}, bf16[16,4096]{1,0:T(8,128)(2,1)S(1)}, u32[]{:S(2)}, u32[]{:S(2)}) collective-permute-start(bf16[16,4096]{1,0:T(8,128)(2,1)S(1)} %collective-permute-done.2), channel_id=1, source_target_pairs={{0,4},{1,5},{4,8},{5,9},{8,12},{9,13},{12,14},{13,15},{14,10},{15,... | collective-permute-start | bytes 393224 | tf_op jit(solution)/shard_map/ppermute | solution.py:34
  10.2 0.0 collective-permute-done.3
  10.2 0.2 collective-permute-start.8
  10.5 4.3 %collective-permute-start.4 = (bf16[96,4096]{1,0:T(8,128)(2,1)S(1)}, bf16[96,4096]{1,0:T(8,128)(2,1)S(1)}, u32[]{:S(2)}, u32[]{:S(2)}) collective-permute-start(bf16[96,4096]{1,0:T(8,128)(2,1)S(1)} %get-tuple-element.18), channel_id=1, source_target_pairs={{0,1},{1,0},{2,3},{3,2},{4,5},{5,4},{6,7},{7,6},{8,9},{9,8},{10,11... | collective-permute-start | bytes 2359304 | tf_op jit(solution)/shard_map/ppermute | solution.py:37
  14.8 0.0 collective-permute-done.5
  14.8 1.3 %collective-permute-start.10 = (bf16[16,4096]{1,0:T(8,128)(2,1)S(1)}, bf16[16,4096]{1,0:T(8,128)(2,1)S(1)}, u32[]{:S(2)}, u32[]{:S(2)}) collective-permute-start(bf16[16,4096]{1,0:T(8,128)(2,1)S(1)} %collective-permute-done.5), channel_id=1, source_target_pairs={{0,4},{1,5},{4,8},{5,9},{8,12},{9,13},{12,14},{13,15},{14,10},{15,... | collective-permute-start | bytes 393224 | tf_op jit(solution)/shard_map/ppermute | solution.py:34
  16.1 0.0 collective-permute-done.6
  16.1 0.2 collective-permute-start.11
  16.3 0.0 collective-permute-done.7
  16.3 1.3 %collective-permute-start.12 = (bf16[16,4096]{1,0:T(8,128)(2,1)S(1)}, bf16[16,4096]{1,0:T(8,128)(2,1)S(1)}, u32[]{:S(2)}, u32[]{:S(2)}) collective-permute-start(bf16[16,4096]{1,0:T(8,128)(2,1)S(1)} %collective-permute-done.7), channel_id=1, source_target_pairs={{0,4},{1,5},{4,8},{5,9},{8,12},{9,13},{12,14},{13,15},{14,10},{15,... | collective-permute-start | bytes 393224 | tf_op jit(solution)/shard_map/ppermute | solution.py:34
  17.6 0.0 collective-permute-done.8
  17.6 0.2 collective-permute-start.13
  17.8 1.3 %collective-permute-done.10 = bf16[16,4096]{1,0:T(8,128)(2,1)S(1)} collective-permute-done((bf16[16,4096]{1,0:T(8,128)(2,1)S(1)}, bf16[16,4096]{1,0:T(8,128)(2,1)S(1)}, u32[]{:S(2)}, u32[]{:S(2)}) %collective-permute-start.10) | collective-permute-done | bytes 131104 | tf_op jit(solution)/shard_map/ppermute | solution.py:34
  19.1 2.8 %collective-permute-start.9 = (bf16[64,4096]{1,0:T(8,128)(2,1)S(1)}, bf16[64,4096]{1,0:T(8,128)(2,1)S(1)}, u32[]{:S(2)}, u32[]{:S(2)}) collective-permute-start(bf16[64,4096]{1,0:T(8,128)(2,1)S(1)} %pad_maximum_fusion), channel_id=1, source_target_pairs={{0,1},{1,0},{2,3},{3,2},{4,5},{5,4},{6,7},{7,6},{8,9},{9,8},{10,11... | collective-permute-start | bytes 1572872 | tf_op jit(solution)/shard_map/ppermute | solution.py:37
  22.0 0.0 collective-permute-done.11
  22.0 0.0 collective-permute-start.15
  22.0 0.0 collective-permute-done.12
  22.0 1.5 %collective-permute-start.17 = (bf16[16,4096]{1,0:T(8,128)(2,1)S(1)}, bf16[16,4096]{1,0:T(8,128)(2,1)S(1)}, u32[]{:S(2)}, u32[]{:S(2)}) collective-permute-start(bf16[16,4096]{1,0:T(8,128)(2,1)S(1)} %collective-permute-done.12), channel_id=1, source_target_pairs={{0,4},{1,5},{4,8},{5,9},{8,12},{9,13},{12,14},{13,15},{14,10},{15,... | collective-permute-start | bytes 393224 | tf_op jit(solution)/shard_map/ppermute | solution.py:34
  23.4 0.0 collective-permute-done.13
  23.5 2.2 %collective-permute-start.14 = (bf16[64,4096]{1,0:T(8,128)(2,1)S(1)}, bf16[64,4096]{1,0:T(8,128)(2,1)S(1)}, u32[]{:S(2)}, u32[]{:S(2)}) collective-permute-start(bf16[64,4096]{1,0:T(8,128)(2,1)S(1)} %pad_maximum_fusion.1), channel_id=1, source_target_pairs={{0,1},{1,0},{2,3},{3,2},{4,5},{5,4},{6,7},{7,6},{8,9},{9,8},{10,11... | collective-permute-start | bytes 1572872 | tf_op jit(solution)/shard_map/ppermute | solution.py:37
  25.7 0.1 collective-permute-done.15
  25.8 2.7 %collective-permute-start.16 = (bf16[16,4096]{1,0:T(8,128)(2,1)S(1)}, bf16[16,4096]{1,0:T(8,128)(2,1)S(1)}, u32[]{:S(2)}, u32[]{:S(2)}) collective-permute-start(bf16[16,4096]{1,0:T(8,128)(2,1)S(1)} %collective-permute-done.15), channel_id=1, source_target_pairs={{0,1},{1,0},{2,3},{3,2},{4,5},{5,4},{6,7},{7,6},{8,9},{9,8},{10,11... | collective-permute-start | bytes 393224 | tf_op jit(solution)/shard_map/ppermute | solution.py:37
  28.5 0.0 collective-permute-done.17
  28.5 0.5 %collective-permute-start.18 = (bf16[16,4096]{1,0:T(8,128)(2,1)S(1)}, bf16[16,4096]{1,0:T(8,128)(2,1)S(1)}, u32[]{:S(2)}, u32[]{:S(2)}) collective-permute-start(bf16[16,4096]{1,0:T(8,128)(2,1)S(1)} %collective-permute-done.17), channel_id=1, source_target_pairs={{0,1},{1,0},{2,3},{3,2},{4,5},{5,4},{6,7},{7,6},{8,9},{9,8},{10,11... | collective-permute-start | bytes 393224 | tf_op jit(solution)/shard_map/ppermute | solution.py:37
  28.9 0.0 collective-permute-done.4
  28.9 0.1 slice_dynamic-update-slice_fusion
  29.0 0.0 copy-start.1
  29.1 0.0 copy-start
  29.1 0.0 collective-permute-done.9
  29.2 0.0 collective-permute-done.14
  29.3 0.1 collective-permute-done.16
  29.5 0.5 %copy-done.1 = bf16[16,4096]{1,0:T(8,128)(2,1)S(1)} copy-done((bf16[16,4096]{1,0:T(8,128)(2,1)S(1)}, bf16[16,4096]{1,0:T(8,128)(2,1)}, u32[]{:S(2)}) %copy-start.1) | copy-done | bytes 131096
  30.0 1.4 %copy-done = bf16[512,4096]{1,0:T(8,128)(2,1)S(1)} copy-done((bf16[512,4096]{1,0:T(8,128)(2,1)S(1)}, bf16[512,4096]{1,0:T(8,128)(2,1)}, u32[]{:S(2)}) %copy-start) | copy-done | bytes 4194328
  31.3 0.0 copy-start.2
  31.3 2.4 %shard_map.37 = (bf16[512,4096]{1,0:T(8,128)(2,1)S(1)}, f32[1,4096]{1,0:T(1,128)S(1)}, f32[1,512]{1,0:T(1,128)S(1)}) custom-call(bf16[512,4096]{1,0:T(8,128)(2,1)S(1)} %copy-done, bf16[16,4096]{1,0:T(8,128)(2,1)S(1)} %copy-done.1, bf16[240,4096]{1,0:T(8,128)(2,1)S(1)} %constant_dynamic-update-slice_fusion.6.others), custom_call_target="tpu_custom_call" | custom-call | flops 1073741824 | bytes 6291456 | tf_op jit(solution)/shard_map/pallas_call | solution.py:148
  33.7 0.0 collective-permute-done.18
  33.8 0.0 copy-done.2
  33.8 2.0 %shard_map.38 = f32[1,512]{1,0:T(1,128)} custom-call(bf16[512,4096]{1,0:T(8,128)(2,1)S(1)} %get-tuple-element.8.probes, f32[1,4096]{1,0:T(1,128)S(1)} %get-tuple-element.9.mean, bf16[16,4096]{1,0:T(8,128)(2,1)S(1)} %copy-done.2, bf16[240,4096]{1,0:T(8,128)(2,1)S(1)} %constant_dynamic-update-slice_fusion.14.others, f32[1,512]{1,0:T(1,128)S(1)} %get-tuple-element.10.ref_log), custom_call_target="tpu_custom_call" | custom-call | flops 1073741824 | bytes 6291456 | tf_op jit(solution)/shard_map/pallas_call | solution.py:162
  (20 shorter events, 0.3 us)
Async XLA Ops:
  0.0 5.5 %collective-permute-start = (bf16[16,4096]{1,0:T(8,128)(2,1)}, bf16[16,4096]{1,0:T(8,128)(2,1)S(1)}, u32[]{:S(2)}, u32[]{:S(2)}) collective-permute-start(bf16[16,4096]{1,0:T(8,128)(2,1)} %own.2), channel_id=1, source_target_pairs={{0,4},{1,5},{4,8},{5,9},{8,12},{9,13},{12,14},{13,15},{14,10},{15,... | collective-permute-start | bytes 393224 | tf_op jit(solution)/shard_map/ppermute | solution.py:34
  2.1 4.3 %collective-permute-start.1 = (bf16[16,4096]{1,0:T(8,128)(2,1)}, bf16[16,4096]{1,0:T(8,128)(2,1)S(1)}, u32[]{:S(2)}, u32[]{:S(2)}) collective-permute-start(bf16[16,4096]{1,0:T(8,128)(2,1)} %own.2), channel_id=1, source_target_pairs={{0,2},{1,3},{4,0},{5,1},{8,4},{9,5},{12,8},{13,9},{14,12},{15,13},... | collective-permute-start | bytes 393224 | tf_op jit(solution)/shard_map/ppermute | solution.py:34
  2.1 6.8 %collective-permute-start.2 = (bf16[16,4096]{1,0:T(8,128)(2,1)}, bf16[16,4096]{1,0:T(8,128)(2,1)S(1)}, u32[]{:S(2)}, u32[]{:S(2)}) collective-permute-start(bf16[16,4096]{1,0:T(8,128)(2,1)} %own.3), channel_id=1, source_target_pairs={{0,4},{1,5},{4,8},{5,9},{8,12},{9,13},{12,14},{13,15},{14,10},{15,... | collective-permute-start | bytes 393224 | tf_op jit(solution)/shard_map/ppermute | solution.py:34
  3.6 6.6 %collective-permute-start.3 = (bf16[16,4096]{1,0:T(8,128)(2,1)}, bf16[16,4096]{1,0:T(8,128)(2,1)S(1)}, u32[]{:S(2)}, u32[]{:S(2)}) collective-permute-start(bf16[16,4096]{1,0:T(8,128)(2,1)} %own.3), channel_id=1, source_target_pairs={{0,2},{1,3},{4,0},{5,1},{8,4},{9,5},{12,8},{13,9},{14,12},{15,13},... | collective-permute-start | bytes 393224 | tf_op jit(solution)/shard_map/ppermute | solution.py:34
  7.4 7.4 %collective-permute-start.5 = (bf16[16,4096]{1,0:T(8,128)(2,1)S(1)}, bf16[16,4096]{1,0:T(8,128)(2,1)S(1)}, u32[]{:S(2)}, u32[]{:S(2)}) collective-permute-start(bf16[16,4096]{1,0:T(8,128)(2,1)S(1)} %collective-permute-done), channel_id=1, source_target_pairs={{0,4},{1,5},{4,8},{5,9},{8,12},{9,13},{12,14},{13,15},{14,10},{15,... | collective-permute-start | bytes 393224 | tf_op jit(solution)/shard_map/ppermute | solution.py:34
  8.7 7.4 %collective-permute-start.6 = (bf16[16,4096]{1,0:T(8,128)(2,1)S(1)}, bf16[16,4096]{1,0:T(8,128)(2,1)S(1)}, u32[]{:S(2)}, u32[]{:S(2)}) collective-permute-start(bf16[16,4096]{1,0:T(8,128)(2,1)S(1)} %collective-permute-done.1), channel_id=1, source_target_pairs={{0,2},{1,3},{4,0},{5,1},{8,4},{9,5},{12,8},{13,9},{14,12},{15,13},... | collective-permute-start | bytes 393224 | tf_op jit(solution)/shard_map/ppermute | solution.py:34
  8.9 7.4 %collective-permute-start.7 = (bf16[16,4096]{1,0:T(8,128)(2,1)S(1)}, bf16[16,4096]{1,0:T(8,128)(2,1)S(1)}, u32[]{:S(2)}, u32[]{:S(2)}) collective-permute-start(bf16[16,4096]{1,0:T(8,128)(2,1)S(1)} %collective-permute-done.2), channel_id=1, source_target_pairs={{0,4},{1,5},{4,8},{5,9},{8,12},{9,13},{12,14},{13,15},{14,10},{15,... | collective-permute-start | bytes 393224 | tf_op jit(solution)/shard_map/ppermute | solution.py:34
  10.2 7.4 %collective-permute-start.8 = (bf16[16,4096]{1,0:T(8,128)(2,1)S(1)}, bf16[16,4096]{1,0:T(8,128)(2,1)S(1)}, u32[]{:S(2)}, u32[]{:S(2)}) collective-permute-start(bf16[16,4096]{1,0:T(8,128)(2,1)S(1)} %collective-permute-done.3), channel_id=1, source_target_pairs={{0,2},{1,3},{4,0},{5,1},{8,4},{9,5},{12,8},{13,9},{14,12},{15,13},... | collective-permute-start | bytes 393224 | tf_op jit(solution)/shard_map/ppermute | solution.py:34
  10.5 18.5 %collective-permute-start.4 = (bf16[96,4096]{1,0:T(8,128)(2,1)S(1)}, bf16[96,4096]{1,0:T(8,128)(2,1)S(1)}, u32[]{:S(2)}, u32[]{:S(2)}) collective-permute-start(bf16[96,4096]{1,0:T(8,128)(2,1)S(1)} %get-tuple-element.18), channel_id=1, source_target_pairs={{0,1},{1,0},{2,3},{3,2},{4,5},{5,4},{6,7},{7,6},{8,9},{9,8},{10,11... | collective-permute-start | bytes 2359304 | tf_op jit(solution)/shard_map/ppermute | solution.py:37
  14.8 4.3 %collective-permute-start.10 = (bf16[16,4096]{1,0:T(8,128)(2,1)S(1)}, bf16[16,4096]{1,0:T(8,128)(2,1)S(1)}, u32[]{:S(2)}, u32[]{:S(2)}) collective-permute-start(bf16[16,4096]{1,0:T(8,128)(2,1)S(1)} %collective-permute-done.5), channel_id=1, source_target_pairs={{0,4},{1,5},{4,8},{5,9},{8,12},{9,13},{12,14},{13,15},{14,10},{15,... | collective-permute-start | bytes 393224 | tf_op jit(solution)/shard_map/ppermute | solution.py:34
  16.1 5.8 %collective-permute-start.11 = (bf16[16,4096]{1,0:T(8,128)(2,1)S(1)}, bf16[16,4096]{1,0:T(8,128)(2,1)S(1)}, u32[]{:S(2)}, u32[]{:S(2)}) collective-permute-start(bf16[16,4096]{1,0:T(8,128)(2,1)S(1)} %collective-permute-done.6), channel_id=1, source_target_pairs={{0,2},{1,3},{4,0},{5,1},{8,4},{9,5},{12,8},{13,9},{14,12},{15,13},... | collective-permute-start | bytes 393224 | tf_op jit(solution)/shard_map/ppermute | solution.py:34
  16.3 5.7 %collective-permute-start.12 = (bf16[16,4096]{1,0:T(8,128)(2,1)S(1)}, bf16[16,4096]{1,0:T(8,128)(2,1)S(1)}, u32[]{:S(2)}, u32[]{:S(2)}) collective-permute-start(bf16[16,4096]{1,0:T(8,128)(2,1)S(1)} %collective-permute-done.7), channel_id=1, source_target_pairs={{0,4},{1,5},{4,8},{5,9},{8,12},{9,13},{12,14},{13,15},{14,10},{15,... | collective-permute-start | bytes 393224 | tf_op jit(solution)/shard_map/ppermute | solution.py:34
  17.6 5.8 %collective-permute-start.13 = (bf16[16,4096]{1,0:T(8,128)(2,1)S(1)}, bf16[16,4096]{1,0:T(8,128)(2,1)S(1)}, u32[]{:S(2)}, u32[]{:S(2)}) collective-permute-start(bf16[16,4096]{1,0:T(8,128)(2,1)S(1)} %collective-permute-done.8), channel_id=1, source_target_pairs={{0,2},{1,3},{4,0},{5,1},{8,4},{9,5},{12,8},{13,9},{14,12},{15,13},... | collective-permute-start | bytes 393224 | tf_op jit(solution)/shard_map/ppermute | solution.py:34
  19.1 10.0 %collective-permute-start.9 = (bf16[64,4096]{1,0:T(8,128)(2,1)S(1)}, bf16[64,4096]{1,0:T(8,128)(2,1)S(1)}, u32[]{:S(2)}, u32[]{:S(2)}) collective-permute-start(bf16[64,4096]{1,0:T(8,128)(2,1)S(1)} %pad_maximum_fusion), channel_id=1, source_target_pairs={{0,1},{1,0},{2,3},{3,2},{4,5},{5,4},{6,7},{7,6},{8,9},{9,8},{10,11... | collective-permute-start | bytes 1572872 | tf_op jit(solution)/shard_map/ppermute | solution.py:37
  22.0 3.8 %collective-permute-start.15 = (bf16[16,4096]{1,0:T(8,128)(2,1)S(1)}, bf16[16,4096]{1,0:T(8,128)(2,1)S(1)}, u32[]{:S(2)}, u32[]{:S(2)}) collective-permute-start(bf16[16,4096]{1,0:T(8,128)(2,1)S(1)} %collective-permute-done.11), channel_id=1, source_target_pairs={{0,2},{1,3},{4,0},{5,1},{8,4},{9,5},{12,8},{13,9},{14,12},{15,13},... | collective-permute-start | bytes 393224 | tf_op jit(solution)/shard_map/ppermute | solution.py:34
  22.0 6.5 %collective-permute-start.17 = (bf16[16,4096]{1,0:T(8,128)(2,1)S(1)}, bf16[16,4096]{1,0:T(8,128)(2,1)S(1)}, u32[]{:S(2)}, u32[]{:S(2)}) collective-permute-start(bf16[16,4096]{1,0:T(8,128)(2,1)S(1)} %collective-permute-done.12), channel_id=1, source_target_pairs={{0,4},{1,5},{4,8},{5,9},{8,12},{9,13},{12,14},{13,15},{14,10},{15,... | collective-permute-start | bytes 393224 | tf_op jit(solution)/shard_map/ppermute | solution.py:34
  23.5 5.8 %collective-permute-start.14 = (bf16[64,4096]{1,0:T(8,128)(2,1)S(1)}, bf16[64,4096]{1,0:T(8,128)(2,1)S(1)}, u32[]{:S(2)}, u32[]{:S(2)}) collective-permute-start(bf16[64,4096]{1,0:T(8,128)(2,1)S(1)} %pad_maximum_fusion.1), channel_id=1, source_target_pairs={{0,1},{1,0},{2,3},{3,2},{4,5},{5,4},{6,7},{7,6},{8,9},{9,8},{10,11... | collective-permute-start | bytes 1572872 | tf_op jit(solution)/shard_map/ppermute | solution.py:37
  25.8 3.7 %collective-permute-start.16 = (bf16[16,4096]{1,0:T(8,128)(2,1)S(1)}, bf16[16,4096]{1,0:T(8,128)(2,1)S(1)}, u32[]{:S(2)}, u32[]{:S(2)}) collective-permute-start(bf16[16,4096]{1,0:T(8,128)(2,1)S(1)} %collective-permute-done.15), channel_id=1, source_target_pairs={{0,1},{1,0},{2,3},{3,2},{4,5},{5,4},{6,7},{7,6},{8,9},{9,8},{10,11... | collective-permute-start | bytes 393224 | tf_op jit(solution)/shard_map/ppermute | solution.py:37
  28.5 5.3 %collective-permute-start.18 = (bf16[16,4096]{1,0:T(8,128)(2,1)S(1)}, bf16[16,4096]{1,0:T(8,128)(2,1)S(1)}, u32[]{:S(2)}, u32[]{:S(2)}) collective-permute-start(bf16[16,4096]{1,0:T(8,128)(2,1)S(1)} %collective-permute-done.17), channel_id=1, source_target_pairs={{0,1},{1,0},{2,3},{3,2},{4,5},{5,4},{6,7},{7,6},{8,9},{9,8},{10,11... | collective-permute-start | bytes 393224 | tf_op jit(solution)/shard_map/ppermute | solution.py:37
  29.0 0.9 %copy-start.1 = (bf16[16,4096]{1,0:T(8,128)(2,1)S(1)}, bf16[16,4096]{1,0:T(8,128)(2,1)}, u32[]{:S(2)}) copy-start(bf16[16,4096]{1,0:T(8,128)(2,1)} %own.2) | copy-start | bytes 393220
  29.1 2.2 %copy-start = (bf16[512,4096]{1,0:T(8,128)(2,1)S(1)}, bf16[512,4096]{1,0:T(8,128)(2,1)}, u32[]{:S(2)}) copy-start(bf16[512,4096]{1,0:T(8,128)(2,1)} %queries.1) | copy-start | bytes 12582916
  31.3 2.5 %copy-start.2 = (bf16[16,4096]{1,0:T(8,128)(2,1)S(1)}, bf16[16,4096]{1,0:T(8,128)(2,1)}, u32[]{:S(2)}) copy-start(bf16[16,4096]{1,0:T(8,128)(2,1)} %own.3) | copy-start | bytes 393220

commit v8 on v3

v8 whole, which is shorter than its diff:
```python
import functools

import jax
import jax.numpy as jnp
from jax import lax
from jax.experimental import pallas as pl
from jax.experimental.pallas import tpu as pltpu
from jax.sharding import PartitionSpec as P

TEMP = 64
LANES = 128
CHUNK = 1024
GROUP = 32
LIMIT = 40 * 2**20


def ring_of_chips(chips):
    return list(range(0, chips, 2)) + list(range(chips - 1 - chips % 2, 0, -2))


def ring_pairs(size):
    order = ring_of_chips(size // 2)
    pairs = []
    for place, chip in enumerate(order):
        after = order[(place + 1) % len(order)]
        before = order[place - 1]
        pairs.append((2 * chip, 2 * after))
        pairs.append((2 * chip + 1, 2 * before + 1))
    return pairs


def core_pairs(size):
    return [(i, i ^ 1) for i in range(size)]


def gather_panels(panels, early, size):
    twins, ring = core_pairs(size), ring_pairs(size)
    chips, rows = size // 2, panels[0].shape[0]

    def hop(block):
        return lax.ppermute(block, "samp", ring)

    def hand_over(block):
        return lax.ppermute(block, "samp", twins)

    steps = (chips - 1) // 2
    mine, other = list(panels), None
    pieces = [[(p, 0, rows)] for p in panels]
    fresh = [[] for _ in panels]
    for period in range(steps + 1):
        last = period == steps
        if period == 1:
            mine[0], early = lax.optimization_barrier((mine[0], early))
        other = [hop(o) for o in other] if period else [hand_over(p) for p in panels]
        arrived = [[] for _ in panels]
        if not last or chips % 2 == 0:
            mine = [hop(m) for m in mine]
            arrived = [[m] for m in mine]
        for i, o in enumerate(other):
            pieces[i] += [(a, 0, rows) for a in arrived[i] + [o]]
            fresh[i] += arrived[i] + ([o] if period else [])
        if last:
            for i in range(len(panels)):
                if fresh[i]:
                    block = hand_over(jnp.concatenate(fresh[i], axis=0))
                    pieces[i].append((block, 0, block.shape[0]))
        elif period:
            block, at = hand_over(jnp.concatenate([f for g in fresh for f in g], axis=0)), 0
            for i in range(len(panels)):
                upto = at + rows * len(fresh[i])
                pieces[i].append((block, at, upto))
                fresh[i], at = [], upto
    return pieces, early


def row_groups(rows, step):
    return [slice(r, min(r + step, rows)) for r in range(0, rows, step)]


def panel_groups(refs, spans):
    groups, at = [], 0
    for ref, (low, high) in zip(refs, spans):
        for rows in row_groups(high - low, GROUP):
            size = rows.stop - rows.start
            groups.append((ref, slice(low + rows.start, low + rows.stop), slice(at, at + size)))
            at += size
    return groups


def center(rows, mean):
    return (rows.astype(jnp.float32) - mean).astype(jnp.bfloat16)


def center_panel_chunk(cols, mean, groups, centered, squares, first):
    for ref, rows, here in groups:
        part = center(ref[rows, cols], mean)
        centered[here, cols] = part
        wide = jnp.square(part.astype(jnp.float32))
        total = wide[:, :LANES]
        for lane in range(LANES, wide.shape[1], LANES):
            total += wide[:, lane : lane + LANES]
        squares[here, :] = total if first else squares[here, :] + total


def add_products(cols, probes, centered, scores, first):
    products = lax.dot_general(
        centered[:, cols], probes[:, cols], (((1,), (1,)), ((), ())),
        preferred_element_type=jnp.float32,
    )
    scores[...] = products if first else scores[...] + products


def log_sum(squares, scores):
    half = 0.5 * jnp.sum(squares[...], axis=1, keepdims=True)
    x = (scores[...] - half) / TEMP
    top = jnp.max(x, axis=0, keepdims=True)
    return jnp.log(jnp.sum(jnp.exp(x - top), axis=0, keepdims=True)) + top


def stage_kernel(queries, own, total):
    total[...] = jnp.sum(own[...].astype(jnp.float32), axis=0, keepdims=True)


def stage(queries, own):
    in_vmem = pl.BlockSpec(memory_space=pltpu.VMEM)
    return pl.pallas_call(
        stage_kernel,
        out_shape=jax.ShapeDtypeStruct((1, own.shape[1]), jnp.float32),
        in_specs=[in_vmem] * 2,
        out_specs=in_vmem,
        compiler_params=pltpu.CompilerParams(vmem_limit_bytes=LIMIT),
        cost_estimate=pl.CostEstimate(
            flops=own.size, bytes_accessed=2 * (queries.size + own.size), transcendentals=0
        ),
    )(queries, own)


def ref_kernel(spans, queries, own_total, *refs):
    panel, (probes, mean, ref_log, centered, squares, scores) = refs[: len(spans)], refs[len(spans) :]
    groups = panel_groups(panel, spans)
    others = [group for group in groups if group[0] is not panel[0]]
    count, features = centered.shape
    for start in range(0, features, CHUNK):
        cols = slice(start, start + CHUNK)
        total = own_total[:, cols]
        for ref, rows, _ in others:
            total += jnp.sum(ref[rows, cols].astype(jnp.float32), axis=0, keepdims=True)
        here = total / count
        mean[:, cols] = here
        center_panel_chunk(cols, here, groups, centered, squares, start == 0)
        for rows in row_groups(probes.shape[0], GROUP):
            probes[rows, cols] = center(queries[rows, cols], here)
        add_products(cols, probes, centered, scores, start == 0)
    ref_log[...] = log_sum(squares, scores)


def gen_kernel(spans, ref_log, probes, mean, *refs):
    panel, (proof, centered, squares, scores) = refs[: len(spans)], refs[len(spans) :]
    groups = panel_groups(panel, spans)
    for start in range(0, centered.shape[1], CHUNK):
        cols = slice(start, start + CHUNK)
        center_panel_chunk(cols, mean[:, cols], groups, centered, squares, start == 0)
        add_products(cols, probes, centered, scores, start == 0)
    proof[...] = log_sum(squares, scores) - ref_log[...]


def call(kernel, before, pieces, count, out_shape):
    spans = [(low, high) for _, low, high in pieces]
    operands = [*before, *(array for array, _, _ in pieces)]
    rows, features = sum(high - low for low, high in spans), operands[-1].shape[1]
    in_vmem = pl.BlockSpec(memory_space=pltpu.VMEM)
    return pl.pallas_call(
        functools.partial(kernel, spans),
        out_shape=out_shape,
        in_specs=[in_vmem] * len(operands),
        out_specs=jax.tree.map(lambda _: in_vmem, out_shape),
        scratch_shapes=[
            pltpu.VMEM((rows, features), jnp.bfloat16),
            pltpu.VMEM((rows, LANES), jnp.float32),
            pltpu.VMEM((rows, count), jnp.float32),
        ],
        compiler_params=pltpu.CompilerParams(vmem_limit_bytes=LIMIT),
        cost_estimate=pl.CostEstimate(
            flops=2 * rows * count * features,
            bytes_accessed=2 * (rows + count) * features,
            transcendentals=rows * count,
        ),
    )(*operands)


def body(queries, gen_panel, ref_panel):
    panels = [ref_panel, gen_panel]
    own_total = stage(queries, ref_panel)
    (ref_pieces, gen_pieces), own_total = gather_panels(panels, own_total, lax.axis_size("samp"))
    count, features = queries.shape
    logs = jax.ShapeDtypeStruct((1, count), jnp.float32)
    probes, mean, ref_log = call(
        ref_kernel,
        [queries, own_total],
        ref_pieces,
        count,
        (
            jax.ShapeDtypeStruct((count, features), jnp.bfloat16),
            jax.ShapeDtypeStruct((1, features), jnp.float32),
            logs,
        ),
    )
    return call(gen_kernel, [ref_log, probes, mean], gen_pieces, count, logs).reshape(-1)


def solution(mesh):
    return jax.shard_map(
        body,
        mesh=mesh,
        in_specs=(
            P(("groups", "samp"), None),
            P(("groups", "samp"), None),
            P(("groups", "samp"), None),
        ),
        out_specs=P(("groups", "samp")),
        check_vma=False,
    )
```

time: 40.1 us -> 34.7 us (0.87)
  waiting for transfers between devices: 16.4 us -> 7.48 us
  Pallas kernels: 0 us -> 4.42 us
  other arithmetic: 3.61 us -> 0.08 us
  local copies, waits for them, and re-layouts: 0.29 us -> 3.16 us
  starting transfers between devices: 16.5 us -> 19.3 us
  matrix products: 2.61 us -> 0 us
    ppermute x7 -> x14, waiting for transfers between devices: 15.4 us -> 7.46 us  [hop(): return lax.ppermute(block, 'samp', ring)]
    pallas_call x0 -> x3, Pallas kernels: none -> 4.42 us  [the longest x2 4.37 us: call(): pl.pallas_call(functools.partial(kernel, spans), out_shape=out_shape, in_...]
    ppermute x8 -> x6, starting transfers between devices: 5.17 us -> 9.08 us  [hand_over(): return lax.ppermute(block, 'samp', twins)]
    unnamed x16 -> x11, local copies, waits for them, and re-layouts: 0.27 us -> 3.15 us
    dot_general x2 -> x0, matrix products: 2.61 us -> none  [panel_scores(): lax.dot_general(probes, panel, (((1,), (1,)), ((), ())), preferred_elemen...]
    reduce_sum x4 -> x0, other arithmetic: 2 us -> none  [the longest x1 1.43 us: half_norms(): return 0.5 * jnp.sum(jnp.square(centered.astype(jnp.float32)), axis=1)]
    ppermute x7 -> x14, starting transfers between devices: 11.3 us -> 10.2 us  [hop(): return lax.ppermute(block, 'samp', ring)]
    ppermute x8 -> x6, waiting for transfers between devices: 1.04 us -> 0.02 us  [hand_over(): return lax.ppermute(block, 'samp', twins)]
  transfers between devices with their start and end apart: 15 -> 20, of which waited for: 7 -> 8; matrix products, arithmetic and copies ran while one was open for 1% -> 0% of each run, Pallas kernels for 0% -> 7%
where the time goes in v8:
time: 34.7 us; the launch traced here: 34.5 us
  starting transfers between devices  19.3 us (56%)
  waiting for transfers between devices  7.48 us (22%)
  Pallas kernels  4.42 us (13%)
  local copies, waits for them, and re-layouts  3.16 us (9%)
    ppermute x14, starting transfers between devices, hop(): return lax.ppermute(block, 'samp', ring)  10.2 us
    ppermute x6, starting transfers between devices, hand_over(): return lax.ppermute(block, 'samp', twins)  9.08 us
    ppermute x14, waiting for transfers between devices, hop(): return lax.ppermute(block, 'samp', ring)  7.46 us
    pallas_call x2, Pallas kernels, call(): pl.pallas_call(functools.partial(kernel, spans), out_shape=out_shape, in_...  4.37 us
    unnamed x11, local copies, waits for them, and re-layouts  3.15 us
  transfers between devices with their start and end apart: 20, of which 8 were waited for; matrix products, arithmetic and copies ran while one was open for 0% of the time, Pallas kernels for 7%

profile of v8, /device:TPU:1, one launch (start us, length us, event | category | flops | bytes accessed | tf_op | source)
XLA Modules:
  0.0 34.5 jit_solution(5353366189501676288)
XLA Ops:
  0.0 2.1 %collective-permute-start = (bf16[16,4096]{1,0:T(8,128)(2,1)}, bf16[16,4096]{1,0:T(8,128)(2,1)S(1)}, u32[]{:S(2)}, u32[]{:S(2)}) collective-permute-start(bf16[16,4096]{1,0:T(8,128)(2,1)} %refs_0_.2), channel_id=1, source_target_pairs={{0,4},{1,3},{4,8},{5,1},{8,12},{9,5},{12,14},{13,9},{14,10},{15,13... | collective-permute-start | bytes 393224 | tf_op jit(solution)/shard_map/ppermute | solution.py:41
  2.1 1.3 %collective-permute-start.4 = (bf16[16,4096]{1,0:T(8,128)(2,1)}, bf16[16,4096]{1,0:T(8,128)(2,1)S(1)}, u32[]{:S(2)}, u32[]{:S(2)}) collective-permute-start(bf16[16,4096]{1,0:T(8,128)(2,1)} %refs_0_.3), channel_id=1, source_target_pairs={{0,4},{1,3},{4,8},{5,1},{8,12},{9,5},{12,14},{13,9},{14,10},{15,13... | collective-permute-start | bytes 393224 | tf_op jit(solution)/shard_map/ppermute | solution.py:41
  3.4 1.3 %collective-permute-start.1 = (bf16[16,4096]{1,0:T(8,128)(2,1)}, bf16[16,4096]{1,0:T(8,128)(2,1)S(1)}, u32[]{:S(2)}, u32[]{:S(2)}) collective-permute-start(bf16[16,4096]{1,0:T(8,128)(2,1)} %refs_0_.2), channel_id=1, source_target_pairs={{0,1},{1,0},{2,3},{3,2},{4,5},{5,4},{6,7},{7,6},{8,9},{9,8},{10,11... | collective-permute-start | bytes 393224 | tf_op jit(solution)/shard_map/ppermute | solution.py:44
  4.7 0.0 collective-permute-start.6
  4.7 0.0 copy-start
  4.7 2.2 %copy-done = bf16[512,4096]{1,0:T(8,128)(2,1)S(1)} copy-done((bf16[512,4096]{1,0:T(8,128)(2,1)S(1)}, bf16[512,4096]{1,0:T(8,128)(2,1)}, u32[]{:S(2)}) %copy-start) | copy-done | bytes 4194328
  6.9 0.0 copy-start.1
  6.9 0.9 %copy-done.1 = bf16[16,4096]{1,0:T(8,128)(2,1)S(1)} copy-done((bf16[16,4096]{1,0:T(8,128)(2,1)S(1)}, bf16[16,4096]{1,0:T(8,128)(2,1)}, u32[]{:S(2)}) %copy-start.1) | copy-done | bytes 131096
  7.8 0.1 shard_map.37.own_total
  7.8 0.0 collective-permute-done.refs_1_
  7.8 0.6 %collective-permute-start.2 = (bf16[16,4096]{1,0:T(8,128)(2,1)S(1)}, bf16[16,4096]{1,0:T(8,128)(2,1)S(1)}, u32[]{:S(2)}, u32[]{:S(2)}) collective-permute-start(bf16[16,4096]{1,0:T(8,128)(2,1)S(1)} %collective-permute-done.refs_1_), channel_id=1, source_target_pairs={{0,4},{1,3},{4,8},{5,1},{8,12},{9,5},{12,14},{13,9},{14,10},{15,13... | collective-permute-start | bytes 393224 | tf_op jit(solution)/shard_map/ppermute | solution.py:41
  8.4 0.0 collective-permute-done.4.refs_1_
  8.4 1.3 %collective-permute-start.5 = (bf16[16,4096]{1,0:T(8,128)(2,1)S(1)}, bf16[16,4096]{1,0:T(8,128)(2,1)S(1)}, u32[]{:S(2)}, u32[]{:S(2)}) collective-permute-start(bf16[16,4096]{1,0:T(8,128)(2,1)S(1)} %collective-permute-done.4.refs_1_), channel_id=1, source_target_pairs={{0,4},{1,3},{4,8},{5,1},{8,12},{9,5},{12,14},{13,9},{14,10},{15,13... | collective-permute-start | bytes 393224 | tf_op jit(solution)/shard_map/ppermute | solution.py:41
  9.7 0.0 collective-permute-done.1.refs_2_
  9.7 0.2 collective-permute-start.3
  9.9 0.0 collective-permute-done.6.refs_2_
  9.9 0.8 %collective-permute-start.7 = (bf16[16,4096]{1,0:T(8,128)(2,1)S(1)}, bf16[16,4096]{1,0:T(8,128)(2,1)S(1)}, u32[]{:S(2)}, u32[]{:S(2)}) collective-permute-start(bf16[16,4096]{1,0:T(8,128)(2,1)S(1)} %collective-permute-done.6.refs_2_), channel_id=1, source_target_pairs={{0,4},{1,3},{4,8},{5,1},{8,12},{9,5},{12,14},{13,9},{14,10},{15,13... | collective-permute-start | bytes 393224 | tf_op jit(solution)/shard_map/ppermute | solution.py:41
  10.8 1.2 %collective-permute-done.2.refs_3_ = bf16[16,4096]{1,0:T(8,128)(2,1)S(1)} collective-permute-done((bf16[16,4096]{1,0:T(8,128)(2,1)S(1)}, bf16[16,4096]{1,0:T(8,128)(2,1)S(1)}, u32[]{:S(2)}, u32[]{:S(2)}) %collective-permute-start.2) | collective-permute-done | bytes 131104 | tf_op jit(solution)/shard_map/ppermute | solution.py:41
  12.0 0.5 %collective-permute-start.9 = (bf16[16,4096]{1,0:T(8,128)(2,1)S(1)}, bf16[16,4096]{1,0:T(8,128)(2,1)S(1)}, u32[]{:S(2)}, u32[]{:S(2)}) collective-permute-start(bf16[16,4096]{1,0:T(8,128)(2,1)S(1)} %collective-permute-done.2.refs_3_), channel_id=1, source_target_pairs={{0,4},{1,3},{4,8},{5,1},{8,12},{9,5},{12,14},{13,9},{14,10},{15,13... | collective-permute-start | bytes 393224 | tf_op jit(solution)/shard_map/ppermute | solution.py:41
  12.5 0.9 %collective-permute-done.5.refs_3_ = bf16[16,4096]{1,0:T(8,128)(2,1)S(1)} collective-permute-done((bf16[16,4096]{1,0:T(8,128)(2,1)S(1)}, bf16[16,4096]{1,0:T(8,128)(2,1)S(1)}, u32[]{:S(2)}, u32[]{:S(2)}) %collective-permute-start.5) | collective-permute-done | bytes 131104 | tf_op jit(solution)/shard_map/ppermute | solution.py:41
  13.4 0.5 %collective-permute-start.11 = (bf16[16,4096]{1,0:T(8,128)(2,1)S(1)}, bf16[16,4096]{1,0:T(8,128)(2,1)S(1)}, u32[]{:S(2)}, u32[]{:S(2)}) collective-permute-start(bf16[16,4096]{1,0:T(8,128)(2,1)S(1)} %collective-permute-done.5.refs_3_), channel_id=1, source_target_pairs={{0,4},{1,3},{4,8},{5,1},{8,12},{9,5},{12,14},{13,9},{14,10},{15,13... | collective-permute-start | bytes 393224 | tf_op jit(solution)/shard_map/ppermute | solution.py:41
  13.9 0.9 %collective-permute-done.3.refs_4_ = bf16[16,4096]{1,0:T(8,128)(2,1)S(1)} collective-permute-done((bf16[16,4096]{1,0:T(8,128)(2,1)S(1)}, bf16[16,4096]{1,0:T(8,128)(2,1)S(1)}, u32[]{:S(2)}, u32[]{:S(2)}) %collective-permute-start.3) | collective-permute-done | bytes 131104 | tf_op jit(solution)/shard_map/ppermute | solution.py:41
  14.8 0.5 %collective-permute-start.10 = (bf16[16,4096]{1,0:T(8,128)(2,1)S(1)}, bf16[16,4096]{1,0:T(8,128)(2,1)S(1)}, u32[]{:S(2)}, u32[]{:S(2)}) collective-permute-start(bf16[16,4096]{1,0:T(8,128)(2,1)S(1)} %collective-permute-done.3.refs_4_), channel_id=1, source_target_pairs={{0,4},{1,3},{4,8},{5,1},{8,12},{9,5},{12,14},{13,9},{14,10},{15,13... | collective-permute-start | bytes 393224 | tf_op jit(solution)/shard_map/ppermute | solution.py:41
  15.3 0.9 %collective-permute-done.7.refs_4_ = bf16[16,4096]{1,0:T(8,128)(2,1)S(1)} collective-permute-done((bf16[16,4096]{1,0:T(8,128)(2,1)S(1)}, bf16[16,4096]{1,0:T(8,128)(2,1)S(1)}, u32[]{:S(2)}, u32[]{:S(2)}) %collective-permute-start.7) | collective-permute-done | bytes 131104 | tf_op jit(solution)/shard_map/ppermute | solution.py:41
  16.2 0.5 %collective-permute-start.12 = (bf16[16,4096]{1,0:T(8,128)(2,1)S(1)}, bf16[16,4096]{1,0:T(8,128)(2,1)S(1)}, u32[]{:S(2)}, u32[]{:S(2)}) collective-permute-start(bf16[16,4096]{1,0:T(8,128)(2,1)S(1)} %collective-permute-done.7.refs_4_), channel_id=1, source_target_pairs={{0,4},{1,3},{4,8},{5,1},{8,12},{9,5},{12,14},{13,9},{14,10},{15,13... | collective-permute-start | bytes 393224 | tf_op jit(solution)/shard_map/ppermute | solution.py:41
  16.8 2.6 %collective-permute-start.8 = (bf16[96,4096]{1,0:T(8,128)(2,1)S(1)}, bf16[96,4096]{1,0:T(8,128)(2,1)S(1)}, u32[]{:S(2)}, u32[]{:S(2)}) collective-permute-start(bf16[96,4096]{1,0:T(8,128)(2,1)S(1)} %constant_dynamic-update-slice_fusion), channel_id=1, source_target_pairs={{0,1},{1,0},{2,3},{3,2},{4,5},{5,4},{6,7},{7,6},{8,9},{9,8},{10,11... | collective-permute-start | bytes 2359304 | tf_op jit(solution)/shard_map/ppermute | solution.py:44
  19.4 0.0 collective-permute-done.9.refs_6_
  19.4 0.3 %collective-permute-start.14 = (bf16[16,4096]{1,0:T(8,128)(2,1)S(1)}, bf16[16,4096]{1,0:T(8,128)(2,1)S(1)}, u32[]{:S(2)}, u32[]{:S(2)}) collective-permute-start(bf16[16,4096]{1,0:T(8,128)(2,1)S(1)} %collective-permute-done.9.refs_6_), channel_id=1, source_target_pairs={{0,4},{1,3},{4,8},{5,1},{8,12},{9,5},{12,14},{13,9},{14,10},{15,13... | collective-permute-start | bytes 393224 | tf_op jit(solution)/shard_map/ppermute | solution.py:41
  19.8 0.7 %collective-permute-done.10.refs_7_ = bf16[16,4096]{1,0:T(8,128)(2,1)S(1)} collective-permute-done((bf16[16,4096]{1,0:T(8,128)(2,1)S(1)}, bf16[16,4096]{1,0:T(8,128)(2,1)S(1)}, u32[]{:S(2)}, u32[]{:S(2)}) %collective-permute-start.10) | collective-permute-done | bytes 131104 | tf_op jit(solution)/shard_map/ppermute | solution.py:41
  20.4 0.5 %collective-permute-start.15 = (bf16[16,4096]{1,0:T(8,128)(2,1)S(1)}, bf16[16,4096]{1,0:T(8,128)(2,1)S(1)}, u32[]{:S(2)}, u32[]{:S(2)}) collective-permute-start(bf16[16,4096]{1,0:T(8,128)(2,1)S(1)} %collective-permute-done.10.refs_7_), channel_id=1, source_target_pairs={{0,4},{1,3},{4,8},{5,1},{8,12},{9,5},{12,14},{13,9},{14,10},{15,13... | collective-permute-start | bytes 393224 | tf_op jit(solution)/shard_map/ppermute | solution.py:41
  20.9 0.0 collective-permute-done.11.refs_6_
  20.9 0.9 %collective-permute-done.12.refs_7_ = bf16[16,4096]{1,0:T(8,128)(2,1)S(1)} collective-permute-done((bf16[16,4096]{1,0:T(8,128)(2,1)S(1)}, bf16[16,4096]{1,0:T(8,128)(2,1)S(1)}, u32[]{:S(2)}, u32[]{:S(2)}) %collective-permute-start.12) | collective-permute-done | bytes 131104 | tf_op jit(solution)/shard_map/ppermute | solution.py:41
  21.9 0.0 copy-start.2
  21.9 1.7 %collective-permute-start.13 = (bf16[64,4096]{1,0:T(8,128)(2,1)S(1)}, bf16[64,4096]{1,0:T(8,128)(2,1)S(1)}, u32[]{:S(2)}, u32[]{:S(2)}) collective-permute-start(bf16[64,4096]{1,0:T(8,128)(2,1)S(1)} %pad_maximum_fusion), channel_id=1, source_target_pairs={{0,1},{1,0},{2,3},{3,2},{4,5},{5,4},{6,7},{7,6},{8,9},{9,8},{10,11... | collective-permute-start | bytes 1572872 | tf_op jit(solution)/shard_map/ppermute | solution.py:44
  23.6 0.3 %collective-permute-start.17 = (bf16[16,4096]{1,0:T(8,128)(2,1)S(1)}, bf16[16,4096]{1,0:T(8,128)(2,1)S(1)}, u32[]{:S(2)}, u32[]{:S(2)}) collective-permute-start(bf16[16,4096]{1,0:T(8,128)(2,1)S(1)} %collective-permute-done.11.refs_6_), channel_id=1, source_target_pairs={{0,4},{1,3},{4,8},{5,1},{8,12},{9,5},{12,14},{13,9},{14,10},{15,13... | collective-permute-start | bytes 393224 | tf_op jit(solution)/shard_map/ppermute | solution.py:41
  23.9 0.0 collective-permute-done.14.refs_9_
  24.0 0.7 %collective-permute-start.18 = (bf16[16,4096]{1,0:T(8,128)(2,1)S(1)}, bf16[16,4096]{1,0:T(8,128)(2,1)S(1)}, u32[]{:S(2)}, u32[]{:S(2)}) collective-permute-start(bf16[16,4096]{1,0:T(8,128)(2,1)S(1)} %collective-permute-done.12.refs_7_), channel_id=1, source_target_pairs={{0,4},{1,3},{4,8},{5,1},{8,12},{9,5},{12,14},{13,9},{14,10},{15,13... | collective-permute-start | bytes 393224 | tf_op jit(solution)/shard_map/ppermute | solution.py:41
  24.6 0.0 collective-permute-done.15.refs_10_
  24.7 2.5 %collective-permute-start.16 = (bf16[32,4096]{1,0:T(8,128)(2,1)S(1)}, bf16[32,4096]{1,0:T(8,128)(2,1)S(1)}, u32[]{:S(2)}, u32[]{:S(2)}) collective-permute-start(bf16[32,4096]{1,0:T(8,128)(2,1)S(1)} %pad_maximum_fusion.1), channel_id=1, source_target_pairs={{0,1},{1,0},{2,3},{3,2},{4,5},{5,4},{6,7},{7,6},{8,9},{9,8},{10,11... | collective-permute-start | bytes 786440 | tf_op jit(solution)/shard_map/ppermute | solution.py:44
  27.1 0.6 %collective-permute-done.17.refs_9_ = bf16[16,4096]{1,0:T(8,128)(2,1)S(1)} collective-permute-done((bf16[16,4096]{1,0:T(8,128)(2,1)S(1)}, bf16[16,4096]{1,0:T(8,128)(2,1)S(1)}, u32[]{:S(2)}, u32[]{:S(2)}) %collective-permute-start.17) | collective-permute-done | bytes 131104 | tf_op jit(solution)/shard_map/ppermute | solution.py:41
  27.7 1.4 %collective-permute-done.18.refs_10_ = bf16[16,4096]{1,0:T(8,128)(2,1)S(1)} collective-permute-done((bf16[16,4096]{1,0:T(8,128)(2,1)S(1)}, bf16[16,4096]{1,0:T(8,128)(2,1)S(1)}, u32[]{:S(2)}, u32[]{:S(2)}) %collective-permute-start.18) | collective-permute-done | bytes 131104 | tf_op jit(solution)/shard_map/ppermute | solution.py:41
  29.1 1.0 %collective-permute-start.19 = (bf16[32,4096]{1,0:T(8,128)(2,1)S(1)}, bf16[32,4096]{1,0:T(8,128)(2,1)S(1)}, u32[]{:S(2)}, u32[]{:S(2)}) collective-permute-start(bf16[32,4096]{1,0:T(8,128)(2,1)S(1)} %pad_maximum_fusion.2), channel_id=1, source_target_pairs={{0,1},{1,0},{2,3},{3,2},{4,5},{5,4},{6,7},{7,6},{8,9},{9,8},{10,11... | collective-permute-start | bytes 786440 | tf_op jit(solution)/shard_map/ppermute | solution.py:44
  30.1 0.0 collective-permute-done.16.refs_11_
  30.1 0.0 collective-permute-done.13.refs_8_
  30.1 0.0 collective-permute-done.8.refs_5_
  30.1 2.3 %shard_map.38 = (bf16[512,4096]{1,0:T(8,128)(2,1)S(1)}, f32[1,4096]{1,0:T(1,128)S(1)}, f32[1,512]{1,0:T(1,128)S(1)}) custom-call(bf16[512,4096]{1,0:T(8,128)(2,1)S(1)} %copy-done, f32[1,4096]{1,0:T(1,128)S(1)} %shard_map.37.own_total, bf16[16,4096]{1,0:T(8,128)(2,1)S(1)} %copy-done.1, bf16[16,4096]{1,0:T(8,128)(2,1)S(1)} %collective-permute-done.refs_1_, ...), custom_call_target="tpu_custom_call" | custom-call | flops 1073741824 | bytes 6291456 | tf_op jit(solution)/shard_map/pallas_call | solution.py:172
  32.5 0.0 collective-permute-done.19.refs_11_
  32.5 0.0 copy-done.2
  32.5 2.0 %shard_map.39 = f32[1,512]{1,0:T(1,128)} custom-call(f32[1,512]{1,0:T(1,128)S(1)} %get-tuple-element.12.ref_log, bf16[512,4096]{1,0:T(8,128)(2,1)S(1)} %get-tuple-element.13.probes, f32[1,4096]{1,0:T(1,128)S(1)} %get-tuple-element.14.mean, bf16[16,4096]{1,0:T(8,128)(2,1)S(1)} %copy-done.2, bf16[16,4096]{1,0:T(8,128)(2,1)S(1)} %collective-permute-done.4.refs_1_, ...), custom_call_target="tpu_custom_call" | custom-call | flops 1073741824 | bytes 6291456 | tf_op jit(solution)/shard_map/pallas_call | solution.py:172
  (9 shorter events, 0.1 us)
Async XLA Ops:
  0.0 7.8 %collective-permute-start = (bf16[16,4096]{1,0:T(8,128)(2,1)}, bf16[16,4096]{1,0:T(8,128)(2,1)S(1)}, u32[]{:S(2)}, u32[]{:S(2)}) collective-permute-start(bf16[16,4096]{1,0:T(8,128)(2,1)} %refs_0_.2), channel_id=1, source_target_pairs={{0,4},{1,3},{4,8},{5,1},{8,12},{9,5},{12,14},{13,9},{14,10},{15,13... | collective-permute-start | bytes 393224 | tf_op jit(solution)/shard_map/ppermute | solution.py:41
  2.1 6.3 %collective-permute-start.4 = (bf16[16,4096]{1,0:T(8,128)(2,1)}, bf16[16,4096]{1,0:T(8,128)(2,1)S(1)}, u32[]{:S(2)}, u32[]{:S(2)}) collective-permute-start(bf16[16,4096]{1,0:T(8,128)(2,1)} %refs_0_.3), channel_id=1, source_target_pairs={{0,4},{1,3},{4,8},{5,1},{8,12},{9,5},{12,14},{13,9},{14,10},{15,13... | collective-permute-start | bytes 393224 | tf_op jit(solution)/shard_map/ppermute | solution.py:41
  3.4 6.3 %collective-permute-start.1 = (bf16[16,4096]{1,0:T(8,128)(2,1)}, bf16[16,4096]{1,0:T(8,128)(2,1)S(1)}, u32[]{:S(2)}, u32[]{:S(2)}) collective-permute-start(bf16[16,4096]{1,0:T(8,128)(2,1)} %refs_0_.2), channel_id=1, source_target_pairs={{0,1},{1,0},{2,3},{3,2},{4,5},{5,4},{6,7},{7,6},{8,9},{9,8},{10,11... | collective-permute-start | bytes 393224 | tf_op jit(solution)/shard_map/ppermute | solution.py:44
  4.7 5.3 %collective-permute-start.6 = (bf16[16,4096]{1,0:T(8,128)(2,1)}, bf16[16,4096]{1,0:T(8,128)(2,1)S(1)}, u32[]{:S(2)}, u32[]{:S(2)}) collective-permute-start(bf16[16,4096]{1,0:T(8,128)(2,1)} %refs_0_.3), channel_id=1, source_target_pairs={{0,1},{1,0},{2,3},{3,2},{4,5},{5,4},{6,7},{7,6},{8,9},{9,8},{10,11... | collective-permute-start | bytes 393224 | tf_op jit(solution)/shard_map/ppermute | solution.py:44
  4.7 2.2 %copy-start = (bf16[512,4096]{1,0:T(8,128)(2,1)S(1)}, bf16[512,4096]{1,0:T(8,128)(2,1)}, u32[]{:S(2)}) copy-start(bf16[512,4096]{1,0:T(8,128)(2,1)} %queries.3) | copy-start | bytes 12582916
  6.9 0.9 %copy-start.1 = (bf16[16,4096]{1,0:T(8,128)(2,1)S(1)}, bf16[16,4096]{1,0:T(8,128)(2,1)}, u32[]{:S(2)}) copy-start(bf16[16,4096]{1,0:T(8,128)(2,1)} %refs_0_.2) | copy-start | bytes 393220
  7.8 4.2 %collective-permute-start.2 = (bf16[16,4096]{1,0:T(8,128)(2,1)S(1)}, bf16[16,4096]{1,0:T(8,128)(2,1)S(1)}, u32[]{:S(2)}, u32[]{:S(2)}) collective-permute-start(bf16[16,4096]{1,0:T(8,128)(2,1)S(1)} %collective-permute-done.refs_1_), channel_id=1, source_target_pairs={{0,4},{1,3},{4,8},{5,1},{8,12},{9,5},{12,14},{13,9},{14,10},{15,13... | collective-permute-start | bytes 393224 | tf_op jit(solution)/shard_map/ppermute | solution.py:41
  8.4 5.0 %collective-permute-start.5 = (bf16[16,4096]{1,0:T(8,128)(2,1)S(1)}, bf16[16,4096]{1,0:T(8,128)(2,1)S(1)}, u32[]{:S(2)}, u32[]{:S(2)}) collective-permute-start(bf16[16,4096]{1,0:T(8,128)(2,1)S(1)} %collective-permute-done.4.refs_1_), channel_id=1, source_target_pairs={{0,4},{1,3},{4,8},{5,1},{8,12},{9,5},{12,14},{13,9},{14,10},{15,13... | collective-permute-start | bytes 393224 | tf_op jit(solution)/shard_map/ppermute | solution.py:41
  9.7 5.1 %collective-permute-start.3 = (bf16[16,4096]{1,0:T(8,128)(2,1)S(1)}, bf16[16,4096]{1,0:T(8,128)(2,1)S(1)}, u32[]{:S(2)}, u32[]{:S(2)}) collective-permute-start(bf16[16,4096]{1,0:T(8,128)(2,1)S(1)} %collective-permute-done.1.refs_2_), channel_id=1, source_target_pairs={{0,4},{1,3},{4,8},{5,1},{8,12},{9,5},{12,14},{13,9},{14,10},{15,13... | collective-permute-start | bytes 393224 | tf_op jit(solution)/shard_map/ppermute | solution.py:41
  9.9 6.3 %collective-permute-start.7 = (bf16[16,4096]{1,0:T(8,128)(2,1)S(1)}, bf16[16,4096]{1,0:T(8,128)(2,1)S(1)}, u32[]{:S(2)}, u32[]{:S(2)}) collective-permute-start(bf16[16,4096]{1,0:T(8,128)(2,1)S(1)} %collective-permute-done.6.refs_2_), channel_id=1, source_target_pairs={{0,4},{1,3},{4,8},{5,1},{8,12},{9,5},{12,14},{13,9},{14,10},{15,13... | collective-permute-start | bytes 393224 | tf_op jit(solution)/shard_map/ppermute | solution.py:41
  12.0 7.4 %collective-permute-start.9 = (bf16[16,4096]{1,0:T(8,128)(2,1)S(1)}, bf16[16,4096]{1,0:T(8,128)(2,1)S(1)}, u32[]{:S(2)}, u32[]{:S(2)}) collective-permute-start(bf16[16,4096]{1,0:T(8,128)(2,1)S(1)} %collective-permute-done.2.refs_3_), channel_id=1, source_target_pairs={{0,4},{1,3},{4,8},{5,1},{8,12},{9,5},{12,14},{13,9},{14,10},{15,13... | collective-permute-start | bytes 393224 | tf_op jit(solution)/shard_map/ppermute | solution.py:41
  13.4 7.5 %collective-permute-start.11 = (bf16[16,4096]{1,0:T(8,128)(2,1)S(1)}, bf16[16,4096]{1,0:T(8,128)(2,1)S(1)}, u32[]{:S(2)}, u32[]{:S(2)}) collective-permute-start(bf16[16,4096]{1,0:T(8,128)(2,1)S(1)} %collective-permute-done.5.refs_3_), channel_id=1, source_target_pairs={{0,4},{1,3},{4,8},{5,1},{8,12},{9,5},{12,14},{13,9},{14,10},{15,13... | collective-permute-start | bytes 393224 | tf_op jit(solution)/shard_map/ppermute | solution.py:41
  14.8 5.6 %collective-permute-start.10 = (bf16[16,4096]{1,0:T(8,128)(2,1)S(1)}, bf16[16,4096]{1,0:T(8,128)(2,1)S(1)}, u32[]{:S(2)}, u32[]{:S(2)}) collective-permute-start(bf16[16,4096]{1,0:T(8,128)(2,1)S(1)} %collective-permute-done.3.refs_4_), channel_id=1, source_target_pairs={{0,4},{1,3},{4,8},{5,1},{8,12},{9,5},{12,14},{13,9},{14,10},{15,13... | collective-permute-start | bytes 393224 | tf_op jit(solution)/shard_map/ppermute | solution.py:41
  16.2 5.6 %collective-permute-start.12 = (bf16[16,4096]{1,0:T(8,128)(2,1)S(1)}, bf16[16,4096]{1,0:T(8,128)(2,1)S(1)}, u32[]{:S(2)}, u32[]{:S(2)}) collective-permute-start(bf16[16,4096]{1,0:T(8,128)(2,1)S(1)} %collective-permute-done.7.refs_4_), channel_id=1, source_target_pairs={{0,4},{1,3},{4,8},{5,1},{8,12},{9,5},{12,14},{13,9},{14,10},{15,13... | collective-permute-start | bytes 393224 | tf_op jit(solution)/shard_map/ppermute | solution.py:41
  16.8 13.3 %collective-permute-start.8 = (bf16[96,4096]{1,0:T(8,128)(2,1)S(1)}, bf16[96,4096]{1,0:T(8,128)(2,1)S(1)}, u32[]{:S(2)}, u32[]{:S(2)}) collective-permute-start(bf16[96,4096]{1,0:T(8,128)(2,1)S(1)} %constant_dynamic-update-slice_fusion), channel_id=1, source_target_pairs={{0,1},{1,0},{2,3},{3,2},{4,5},{5,4},{6,7},{7,6},{8,9},{9,8},{10,11... | collective-permute-start | bytes 2359304 | tf_op jit(solution)/shard_map/ppermute | solution.py:44
  19.4 4.5 %collective-permute-start.14 = (bf16[16,4096]{1,0:T(8,128)(2,1)S(1)}, bf16[16,4096]{1,0:T(8,128)(2,1)S(1)}, u32[]{:S(2)}, u32[]{:S(2)}) collective-permute-start(bf16[16,4096]{1,0:T(8,128)(2,1)S(1)} %collective-permute-done.9.refs_6_), channel_id=1, source_target_pairs={{0,4},{1,3},{4,8},{5,1},{8,12},{9,5},{12,14},{13,9},{14,10},{15,13... | collective-permute-start | bytes 393224 | tf_op jit(solution)/shard_map/ppermute | solution.py:41
  20.4 4.2 %collective-permute-start.15 = (bf16[16,4096]{1,0:T(8,128)(2,1)S(1)}, bf16[16,4096]{1,0:T(8,128)(2,1)S(1)}, u32[]{:S(2)}, u32[]{:S(2)}) collective-permute-start(bf16[16,4096]{1,0:T(8,128)(2,1)S(1)} %collective-permute-done.10.refs_7_), channel_id=1, source_target_pairs={{0,4},{1,3},{4,8},{5,1},{8,12},{9,5},{12,14},{13,9},{14,10},{15,13... | collective-permute-start | bytes 393224 | tf_op jit(solution)/shard_map/ppermute | solution.py:41
  21.9 10.6 %copy-start.2 = (bf16[16,4096]{1,0:T(8,128)(2,1)S(1)}, bf16[16,4096]{1,0:T(8,128)(2,1)}, u32[]{:S(2)}) copy-start(bf16[16,4096]{1,0:T(8,128)(2,1)} %refs_0_.3) | copy-start | bytes 393220
  21.9 8.3 %collective-permute-start.13 = (bf16[64,4096]{1,0:T(8,128)(2,1)S(1)}, bf16[64,4096]{1,0:T(8,128)(2,1)S(1)}, u32[]{:S(2)}, u32[]{:S(2)}) collective-permute-start(bf16[64,4096]{1,0:T(8,128)(2,1)S(1)} %pad_maximum_fusion), channel_id=1, source_target_pairs={{0,1},{1,0},{2,3},{3,2},{4,5},{5,4},{6,7},{7,6},{8,9},{9,8},{10,11... | collective-permute-start | bytes 1572872 | tf_op jit(solution)/shard_map/ppermute | solution.py:44
  23.6 4.1 %collective-permute-start.17 = (bf16[16,4096]{1,0:T(8,128)(2,1)S(1)}, bf16[16,4096]{1,0:T(8,128)(2,1)S(1)}, u32[]{:S(2)}, u32[]{:S(2)}) collective-permute-start(bf16[16,4096]{1,0:T(8,128)(2,1)S(1)} %collective-permute-done.11.refs_6_), channel_id=1, source_target_pairs={{0,4},{1,3},{4,8},{5,1},{8,12},{9,5},{12,14},{13,9},{14,10},{15,13... | collective-permute-start | bytes 393224 | tf_op jit(solution)/shard_map/ppermute | solution.py:41
  24.0 5.2 %collective-permute-start.18 = (bf16[16,4096]{1,0:T(8,128)(2,1)S(1)}, bf16[16,4096]{1,0:T(8,128)(2,1)S(1)}, u32[]{:S(2)}, u32[]{:S(2)}) collective-permute-start(bf16[16,4096]{1,0:T(8,128)(2,1)S(1)} %collective-permute-done.12.refs_7_), channel_id=1, source_target_pairs={{0,4},{1,3},{4,8},{5,1},{8,12},{9,5},{12,14},{13,9},{14,10},{15,13... | collective-permute-start | bytes 393224 | tf_op jit(solution)/shard_map/ppermute | solution.py:41
  24.7 5.5 %collective-permute-start.16 = (bf16[32,4096]{1,0:T(8,128)(2,1)S(1)}, bf16[32,4096]{1,0:T(8,128)(2,1)S(1)}, u32[]{:S(2)}, u32[]{:S(2)}) collective-permute-start(bf16[32,4096]{1,0:T(8,128)(2,1)S(1)} %pad_maximum_fusion.1), channel_id=1, source_target_pairs={{0,1},{1,0},{2,3},{3,2},{4,5},{5,4},{6,7},{7,6},{8,9},{9,8},{10,11... | collective-permute-start | bytes 786440 | tf_op jit(solution)/shard_map/ppermute | solution.py:44
  29.1 3.3 %collective-permute-start.19 = (bf16[32,4096]{1,0:T(8,128)(2,1)S(1)}, bf16[32,4096]{1,0:T(8,128)(2,1)S(1)}, u32[]{:S(2)}, u32[]{:S(2)}) collective-permute-start(bf16[32,4096]{1,0:T(8,128)(2,1)S(1)} %pad_maximum_fusion.2), channel_id=1, source_target_pairs={{0,1},{1,0},{2,3},{3,2},{4,5},{5,4},{6,7},{7,6},{8,9},{9,8},{10,11... | collective-permute-start | bytes 786440 | tf_op jit(solution)/shard_map/ppermute | solution.py:44

commit v9 on v8

--- a/solution.py
+++ b/solution.py
@@ -33,7 +33,7 @@
     return [(i, i ^ 1) for i in range(size)]
 
 
-def gather_panels(panels, early, size):
+def gather_panels(panels, size, on_first):
     twins, ring = core_pairs(size), ring_pairs(size)
     chips, rows = size // 2, panels[0].shape[0]
 
@@ -45,20 +45,22 @@
 
     steps = (chips - 1) // 2
     mine, other = list(panels), None
-    pieces = [[(p, 0, rows)] for p in panels]
+    pieces = [[] for _ in panels]
     fresh = [[] for _ in panels]
     for period in range(steps + 1):
         last = period == steps
-        if period == 1:
-            mine[0], early = lax.optimization_barrier((mine[0], early))
+        if last and period:
+            mine[-1], extra = lax.optimization_barrier((mine[-1], extra))
         other = [hop(o) for o in other] if period else [hand_over(p) for p in panels]
+        if not period:
+            extra = on_first(other[0])
         arrived = [[] for _ in panels]
         if not last or chips % 2 == 0:
             mine = [hop(m) for m in mine]
             arrived = [[m] for m in mine]
         for i, o in enumerate(other):
-            pieces[i] += [(a, 0, rows) for a in arrived[i] + [o]]
-            fresh[i] += arrived[i] + ([o] if period else [])
+            pieces[i] += [(a, 0, rows) for a in [o] + arrived[i]]
+            fresh[i] += [o] + arrived[i]
         if last:
             for i in range(len(panels)):
                 if fresh[i]:
@@ -70,7 +72,7 @@
                 upto = at + rows * len(fresh[i])
                 pieces[i].append((block, at, upto))
                 fresh[i], at = [], upto
-    return pieces, early
+    return pieces, extra
 
 
 def row_groups(rows, step):
@@ -117,34 +119,34 @@
     return jnp.log(jnp.sum(jnp.exp(x - top), axis=0, keepdims=True)) + top
 
 
-def stage_kernel(queries, own, total):
-    total[...] = jnp.sum(own[...].astype(jnp.float32), axis=0, keepdims=True)
-
-
-def stage(queries, own):
+def total_kernel(rows, total):
+    total[...] = jnp.sum(rows[...].astype(jnp.float32), axis=0, keepdims=True)
+
+
+def feature_total(rows, beside):
     in_vmem = pl.BlockSpec(memory_space=pltpu.VMEM)
     return pl.pallas_call(
-        stage_kernel,
-        out_shape=jax.ShapeDtypeStruct((1, own.shape[1]), jnp.float32),
-        in_specs=[in_vmem] * 2,
+        total_kernel,
+        out_shape=jax.ShapeDtypeStruct((1, rows.shape[1]), jnp.float32),
+        in_specs=[in_vmem],
         out_specs=in_vmem,
         compiler_params=pltpu.CompilerParams(vmem_limit_bytes=LIMIT),
         cost_estimate=pl.CostEstimate(
-            flops=own.size, bytes_accessed=2 * (queries.size + own.size), transcendentals=0
-        ),
-    )(queries, own)
-
-
-def ref_kernel(spans, queries, own_total, *refs):
+            flops=rows.size, bytes_accessed=4 * beside.size, transcendentals=0
+        ),
+    )(rows)
+
+
+def ref_kernel(spans, queries, first_total, *refs):
     panel, (probes, mean, ref_log, centered, squares, scores) = refs[: len(spans)], refs[len(spans) :]
     groups = panel_groups(panel, spans)
-    others = [group for group in groups if group[0] is not panel[0]]
     count, features = centered.shape
     for start in range(0, features, CHUNK):
         cols = slice(start, start + CHUNK)
-        total = own_total[:, cols]
-        for ref, rows, _ in others:
-            total += jnp.sum(ref[rows, cols].astype(jnp.float32), axis=0, keepdims=True)
+        total = first_total[:, cols]
+        for ref, rows, _ in groups:
+            if ref is not panel[0]:
+                total += jnp.sum(ref[rows, cols].astype(jnp.float32), axis=0, keepdims=True)
         here = total / count
         mean[:, cols] = here
         center_panel_chunk(cols, here, groups, centered, squares, start == 0)
@@ -190,13 +192,14 @@
 
 def body(queries, gen_panel, ref_panel):
     panels = [ref_panel, gen_panel]
-    own_total = stage(queries, ref_panel)
-    (ref_pieces, gen_pieces), own_total = gather_panels(panels, own_total, lax.axis_size("samp"))
+    (ref_pieces, gen_pieces), first_total = gather_panels(
+        panels, lax.axis_size("samp"), functools.partial(feature_total, beside=queries)
+    )
     count, features = queries.shape
     logs = jax.ShapeDtypeStruct((1, count), jnp.float32)
     probes, mean, ref_log = call(
         ref_kernel,
-        [queries, own_total],
+        [queries, first_total],
         ref_pieces,
         count,
         (

time: 34.7 us -> 32.1 us (0.925)
  starting transfers between devices: 19.3 us -> 22.8 us
  local copies, waits for them, and re-layouts: 3.16 us -> 0.08 us
  waiting for transfers between devices: 7.48 us -> 4.55 us
    ppermute x14, starting transfers between devices: 10.2 us -> 15.2 us  [hop(): return lax.ppermute(block, 'samp', ring)]
    unnamed x11 -> x9, local copies, waits for them, and re-layouts: 3.15 us -> 0.07 us
    ppermute x14, waiting for transfers between devices: 7.46 us -> 4.53 us  [hop(): return lax.ppermute(block, 'samp', ring)]
    ppermute x6, starting transfers between devices: 9.08 us -> 7.58 us  [hand_over(): return lax.ppermute(block, 'samp', twins)]
  transfers between devices with their start and end apart: 20 -> 20, of which waited for: 8 -> 6; matrix products, arithmetic and copies ran while one was open for 0% -> 0% of each run, Pallas kernels for 7% -> 7%
where the time goes in v9:
time: 32.1 us; the launch traced here: 32 us
  starting transfers between devices  22.8 us (71%)
  waiting for transfers between devices  4.55 us (14%)
  Pallas kernels  4.41 us (14%)
    ppermute x14, starting transfers between devices, hop(): return lax.ppermute(block, 'samp', ring)  15.2 us
    ppermute x6, starting transfers between devices, hand_over(): return lax.ppermute(block, 'samp', twins)  7.58 us
    ppermute x14, waiting for transfers between devices, hop(): return lax.ppermute(block, 'samp', ring)  4.53 us
    pallas_call x2, Pallas kernels, call(): pl.pallas_call(functools.partial(kernel, spans), out_shape=out_shape, in_...  4.35 us
  transfers between devices with their start and end apart: 20, of which 6 were waited for; matrix products, arithmetic and copies ran while one was open for 0% of the time, Pallas kernels for 7%

profile of v9, /device:TPU:1, one launch (start us, length us, event | category | flops | bytes accessed | tf_op | source)
XLA Modules:
  0.0 32.0 jit_solution(17910471915659567490)
XLA Ops:
  0.0 0.0 copy-start
  0.0 0.1 collective-permute-start.3
  0.1 2.7 %collective-permute-start.4 = (bf16[16,4096]{1,0:T(8,128)(2,1)}, bf16[16,4096]{1,0:T(8,128)(2,1)S(1)}, u32[]{:S(2)}, u32[]{:S(2)}) collective-permute-start(bf16[16,4096]{1,0:T(8,128)(2,1)} %param.5), channel_id=1, source_target_pairs={{0,4},{1,3},{4,8},{5,1},{8,12},{9,5},{12,14},{13,9},{14,10},{15,13... | collective-permute-start | bytes 393224 | tf_op jit(solution)/shard_map/ppermute | solution.py:41
  2.7 0.4 %collective-permute-start.7 = (bf16[16,4096]{1,0:T(8,128)(2,1)}, bf16[16,4096]{1,0:T(8,128)(2,1)S(1)}, u32[]{:S(2)}, u32[]{:S(2)}) collective-permute-start(bf16[16,4096]{1,0:T(8,128)(2,1)} %param.4), channel_id=1, source_target_pairs={{0,1},{1,0},{2,3},{3,2},{4,5},{5,4},{6,7},{7,6},{8,9},{9,8},{10,11... | collective-permute-start | bytes 393224 | tf_op jit(solution)/shard_map/ppermute | solution.py:44
  3.1 0.9 %collective-permute-start = (bf16[16,4096]{1,0:T(8,128)(2,1)}, bf16[16,4096]{1,0:T(8,128)(2,1)S(1)}, u32[]{:S(2)}, u32[]{:S(2)}) collective-permute-start(bf16[16,4096]{1,0:T(8,128)(2,1)} %param.4), channel_id=1, source_target_pairs={{0,4},{1,3},{4,8},{5,1},{8,12},{9,5},{12,14},{13,9},{14,10},{15,13... | collective-permute-start | bytes 393224 | tf_op jit(solution)/shard_map/ppermute | solution.py:41
  4.0 0.0 collective-permute-done.3.rows.refs_0_
  4.1 1.3 %collective-permute-start.5 = (bf16[16,4096]{1,0:T(8,128)(2,1)S(1)}, bf16[16,4096]{1,0:T(8,128)(2,1)S(1)}, u32[]{:S(2)}, u32[]{:S(2)}) collective-permute-start(bf16[16,4096]{1,0:T(8,128)(2,1)S(1)} %collective-permute-done.3.rows.refs_0_), channel_id=1, source_target_pairs={{0,4},{1,3},{4,8},{5,1},{8,12},{9,5},{12,14},{13,9},{14,10},{15,13... | collective-permute-start | bytes 393224 | tf_op jit(solution)/shard_map/ppermute | solution.py:41
  5.4 0.3 collective-permute-done.4.refs_1_
  5.7 1.4 %collective-permute-start.6 = (bf16[16,4096]{1,0:T(8,128)(2,1)S(1)}, bf16[16,4096]{1,0:T(8,128)(2,1)S(1)}, u32[]{:S(2)}, u32[]{:S(2)}) collective-permute-start(bf16[16,4096]{1,0:T(8,128)(2,1)S(1)} %collective-permute-done.4.refs_1_), channel_id=1, source_target_pairs={{0,4},{1,3},{4,8},{5,1},{8,12},{9,5},{12,14},{13,9},{14,10},{15,13... | collective-permute-start | bytes 393224 | tf_op jit(solution)/shard_map/ppermute | solution.py:41
  7.1 0.1 shard_map.37.first_total
  7.1 0.0 collective-permute-done.7.refs_0_
  7.2 1.3 %collective-permute-start.8 = (bf16[16,4096]{1,0:T(8,128)(2,1)S(1)}, bf16[16,4096]{1,0:T(8,128)(2,1)S(1)}, u32[]{:S(2)}, u32[]{:S(2)}) collective-permute-start(bf16[16,4096]{1,0:T(8,128)(2,1)S(1)} %collective-permute-done.7.refs_0_), channel_id=1, source_target_pairs={{0,4},{1,3},{4,8},{5,1},{8,12},{9,5},{12,14},{13,9},{14,10},{15,13... | collective-permute-start | bytes 393224 | tf_op jit(solution)/shard_map/ppermute | solution.py:41
  8.5 0.0 collective-permute-done.refs_1_
  8.5 1.3 %collective-permute-start.1 = (bf16[16,4096]{1,0:T(8,128)(2,1)S(1)}, bf16[16,4096]{1,0:T(8,128)(2,1)S(1)}, u32[]{:S(2)}, u32[]{:S(2)}) collective-permute-start(bf16[16,4096]{1,0:T(8,128)(2,1)S(1)} %collective-permute-done.refs_1_), channel_id=1, source_target_pairs={{0,4},{1,3},{4,8},{5,1},{8,12},{9,5},{12,14},{13,9},{14,10},{15,13... | collective-permute-start | bytes 393224 | tf_op jit(solution)/shard_map/ppermute | solution.py:41
  9.8 0.0 collective-permute-done.5.refs_2_
  9.8 1.3 %collective-permute-start.10 = (bf16[16,4096]{1,0:T(8,128)(2,1)S(1)}, bf16[16,4096]{1,0:T(8,128)(2,1)S(1)}, u32[]{:S(2)}, u32[]{:S(2)}) collective-permute-start(bf16[16,4096]{1,0:T(8,128)(2,1)S(1)} %collective-permute-done.5.refs_2_), channel_id=1, source_target_pairs={{0,4},{1,3},{4,8},{5,1},{8,12},{9,5},{12,14},{13,9},{14,10},{15,13... | collective-permute-start | bytes 393224 | tf_op jit(solution)/shard_map/ppermute | solution.py:41
  11.1 0.0 collective-permute-done.6.refs_3_
  11.1 0.3 collective-permute-start.11
  11.5 0.2 collective-permute-done.8.refs_2_
  11.7 1.0 %collective-permute-start.12 = (bf16[16,4096]{1,0:T(8,128)(2,1)S(1)}, bf16[16,4096]{1,0:T(8,128)(2,1)S(1)}, u32[]{:S(2)}, u32[]{:S(2)}) collective-permute-start(bf16[16,4096]{1,0:T(8,128)(2,1)S(1)} %collective-permute-done.8.refs_2_), channel_id=1, source_target_pairs={{0,4},{1,3},{4,8},{5,1},{8,12},{9,5},{12,14},{13,9},{14,10},{15,13... | collective-permute-start | bytes 393224 | tf_op jit(solution)/shard_map/ppermute | solution.py:41
  12.7 0.3 collective-permute-done.1.refs_3_
  13.0 1.1 %collective-permute-start.2 = (bf16[16,4096]{1,0:T(8,128)(2,1)S(1)}, bf16[16,4096]{1,0:T(8,128)(2,1)S(1)}, u32[]{:S(2)}, u32[]{:S(2)}) collective-permute-start(bf16[16,4096]{1,0:T(8,128)(2,1)S(1)} %collective-permute-done.1.refs_3_), channel_id=1, source_target_pairs={{0,4},{1,3},{4,8},{5,1},{8,12},{9,5},{12,14},{13,9},{14,10},{15,13... | collective-permute-start | bytes 393224 | tf_op jit(solution)/shard_map/ppermute | solution.py:41
  14.1 2.6 %collective-permute-start.9 = (bf16[128,4096]{1,0:T(8,128)(2,1)S(1)}, bf16[128,4096]{1,0:T(8,128)(2,1)S(1)}, u32[]{:S(2)}, u32[]{:S(2)}) collective-permute-start(bf16[128,4096]{1,0:T(8,128)(2,1)S(1)} %constant_dynamic-update-slice_fusion), channel_id=1, source_target_pairs={{0,1},{1,0},{2,3},{3,2},{4,5},{5,4},{6,7},{7,6},{8,9},{9,8},{10,11... | collective-permute-start | bytes 3145736 | tf_op jit(solution)/shard_map/ppermute | solution.py:44
  16.7 0.0 collective-permute-done.10.refs_5_
  16.7 0.2 collective-permute-start.14
  16.9 0.0 collective-permute-done.11.refs_6_
  16.9 0.7 %collective-permute-start.15 = (bf16[16,4096]{1,0:T(8,128)(2,1)S(1)}, bf16[16,4096]{1,0:T(8,128)(2,1)S(1)}, u32[]{:S(2)}, u32[]{:S(2)}) collective-permute-start(bf16[16,4096]{1,0:T(8,128)(2,1)S(1)} %collective-permute-done.11.refs_6_), channel_id=1, source_target_pairs={{0,4},{1,3},{4,8},{5,1},{8,12},{9,5},{12,14},{13,9},{14,10},{15,13... | collective-permute-start | bytes 393224 | tf_op jit(solution)/shard_map/ppermute | solution.py:41
  17.6 0.0 collective-permute-done.12.refs_5_
  17.6 1.1 %collective-permute-done.2.refs_6_ = bf16[16,4096]{1,0:T(8,128)(2,1)S(1)} collective-permute-done((bf16[16,4096]{1,0:T(8,128)(2,1)S(1)}, bf16[16,4096]{1,0:T(8,128)(2,1)S(1)}, u32[]{:S(2)}, u32[]{:S(2)}) %collective-permute-start.2) | collective-permute-done | bytes 131104 | tf_op jit(solution)/shard_map/ppermute | solution.py:41
  18.7 2.4 %collective-permute-start.13 = (bf16[64,4096]{1,0:T(8,128)(2,1)S(1)}, bf16[64,4096]{1,0:T(8,128)(2,1)S(1)}, u32[]{:S(2)}, u32[]{:S(2)}) collective-permute-start(bf16[64,4096]{1,0:T(8,128)(2,1)S(1)} %pad_maximum_fusion), channel_id=1, source_target_pairs={{0,1},{1,0},{2,3},{3,2},{4,5},{5,4},{6,7},{7,6},{8,9},{9,8},{10,11... | collective-permute-start | bytes 1572872 | tf_op jit(solution)/shard_map/ppermute | solution.py:44
  21.1 0.5 %collective-permute-start.18 = (bf16[16,4096]{1,0:T(8,128)(2,1)S(1)}, bf16[16,4096]{1,0:T(8,128)(2,1)S(1)}, u32[]{:S(2)}, u32[]{:S(2)}) collective-permute-start(bf16[16,4096]{1,0:T(8,128)(2,1)S(1)} %collective-permute-done.2.refs_6_), channel_id=1, source_target_pairs={{0,4},{1,3},{4,8},{5,1},{8,12},{9,5},{12,14},{13,9},{14,10},{15,13... | collective-permute-start | bytes 393224 | tf_op jit(solution)/shard_map/ppermute | solution.py:41
  21.5 0.0 collective-permute-done.14.refs_8_
  21.6 1.2 %collective-permute-start.17 = (bf16[16,4096]{1,0:T(8,128)(2,1)S(1)}, bf16[16,4096]{1,0:T(8,128)(2,1)S(1)}, u32[]{:S(2)}, u32[]{:S(2)}) collective-permute-start(bf16[16,4096]{1,0:T(8,128)(2,1)S(1)} %collective-permute-done.12.refs_5_), channel_id=1, source_target_pairs={{0,4},{1,3},{4,8},{5,1},{8,12},{9,5},{12,14},{13,9},{14,10},{15,13... | collective-permute-start | bytes 393224 | tf_op jit(solution)/shard_map/ppermute | solution.py:41
  22.8 0.0 collective-permute-done.15.refs_9_
  22.8 1.2 %collective-permute-start.16 = (bf16[32,4096]{1,0:T(8,128)(2,1)S(1)}, bf16[32,4096]{1,0:T(8,128)(2,1)S(1)}, u32[]{:S(2)}, u32[]{:S(2)}) collective-permute-start(bf16[32,4096]{1,0:T(8,128)(2,1)S(1)} %pad_maximum_fusion.1), channel_id=1, source_target_pairs={{0,1},{1,0},{2,3},{3,2},{4,5},{5,4},{6,7},{7,6},{8,9},{9,8},{10,11... | collective-permute-start | bytes 786440 | tf_op jit(solution)/shard_map/ppermute | solution.py:44
  24.0 1.2 %collective-permute-done.18.refs_9_ = bf16[16,4096]{1,0:T(8,128)(2,1)S(1)} collective-permute-done((bf16[16,4096]{1,0:T(8,128)(2,1)S(1)}, bf16[16,4096]{1,0:T(8,128)(2,1)S(1)}, u32[]{:S(2)}, u32[]{:S(2)}) %collective-permute-start.18) | collective-permute-done | bytes 131104 | tf_op jit(solution)/shard_map/ppermute | solution.py:41
  25.2 1.4 %collective-permute-done.17.refs_8_ = bf16[16,4096]{1,0:T(8,128)(2,1)S(1)} collective-permute-done((bf16[16,4096]{1,0:T(8,128)(2,1)S(1)}, bf16[16,4096]{1,0:T(8,128)(2,1)S(1)}, u32[]{:S(2)}, u32[]{:S(2)}) %collective-permute-start.17) | collective-permute-done | bytes 131104 | tf_op jit(solution)/shard_map/ppermute | solution.py:41
  26.6 1.0 %collective-permute-start.19 = (bf16[32,4096]{1,0:T(8,128)(2,1)S(1)}, bf16[32,4096]{1,0:T(8,128)(2,1)S(1)}, u32[]{:S(2)}, u32[]{:S(2)}) collective-permute-start(bf16[32,4096]{1,0:T(8,128)(2,1)S(1)} %pad_maximum_fusion.2), channel_id=1, source_target_pairs={{0,1},{1,0},{2,3},{3,2},{4,5},{5,4},{6,7},{7,6},{8,9},{9,8},{10,11... | collective-permute-start | bytes 786440 | tf_op jit(solution)/shard_map/ppermute | solution.py:44
  27.6 0.0 collective-permute-done.16.refs_10_
  27.6 0.0 collective-permute-done.13.refs_7_
  27.6 0.0 collective-permute-done.9.refs_4_
  27.6 0.0 copy-done
  27.6 2.3 %shard_map.38 = (bf16[512,4096]{1,0:T(8,128)(2,1)S(1)}, f32[1,4096]{1,0:T(1,128)S(1)}, f32[1,512]{1,0:T(1,128)S(1)}) custom-call(bf16[512,4096]{1,0:T(8,128)(2,1)S(1)} %copy-done, f32[1,4096]{1,0:T(1,128)S(1)} %shard_map.37.first_total, bf16[16,4096]{1,0:T(8,128)(2,1)S(1)} %collective-permute-done.3.rows.refs_0_, ...), custom_call_target="tpu_custom_call" | custom-call | flops 1073741824 | bytes 6291456 | tf_op jit(solution)/shard_map/pallas_call | solution.py:174
  29.9 0.0 collective-permute-done.19.refs_10_
  30.0 2.0 %shard_map.39 = f32[1,512]{1,0:T(1,128)} custom-call(f32[1,512]{1,0:T(1,128)S(1)} %get-tuple-element.11.ref_log, bf16[512,4096]{1,0:T(8,128)(2,1)S(1)} %get-tuple-element.12.probes, f32[1,4096]{1,0:T(1,128)S(1)} %get-tuple-element.13.mean, bf16[16,4096]{1,0:T(8,128)(2,1)S(1)} %collective-permute-done.7.refs_0_, ...), custom_call_target="tpu_custom_call" | custom-call | flops 1073741824 | bytes 6291456 | tf_op jit(solution)/shard_map/pallas_call | solution.py:174
  (11 shorter events, 0.2 us)
Async XLA Ops:
  0.0 27.6 %copy-start = (bf16[512,4096]{1,0:T(8,128)(2,1)S(1)}, bf16[512,4096]{1,0:T(8,128)(2,1)}, u32[]{:S(2)}) copy-start(bf16[512,4096]{1,0:T(8,128)(2,1)} %queries.1) | copy-start | bytes 12582916
  0.0 4.0 %collective-permute-start.3 = (bf16[16,4096]{1,0:T(8,128)(2,1)}, bf16[16,4096]{1,0:T(8,128)(2,1)S(1)}, u32[]{:S(2)}, u32[]{:S(2)}) collective-permute-start(bf16[16,4096]{1,0:T(8,128)(2,1)} %param.5), channel_id=1, source_target_pairs={{0,1},{1,0},{2,3},{3,2},{4,5},{5,4},{6,7},{7,6},{8,9},{9,8},{10,11... | collective-permute-start | bytes 393224 | tf_op jit(solution)/shard_map/ppermute | solution.py:44
  0.1 5.6 %collective-permute-start.4 = (bf16[16,4096]{1,0:T(8,128)(2,1)}, bf16[16,4096]{1,0:T(8,128)(2,1)S(1)}, u32[]{:S(2)}, u32[]{:S(2)}) collective-permute-start(bf16[16,4096]{1,0:T(8,128)(2,1)} %param.5), channel_id=1, source_target_pairs={{0,4},{1,3},{4,8},{5,1},{8,12},{9,5},{12,14},{13,9},{14,10},{15,13... | collective-permute-start | bytes 393224 | tf_op jit(solution)/shard_map/ppermute | solution.py:41
  2.7 4.4 %collective-permute-start.7 = (bf16[16,4096]{1,0:T(8,128)(2,1)}, bf16[16,4096]{1,0:T(8,128)(2,1)S(1)}, u32[]{:S(2)}, u32[]{:S(2)}) collective-permute-start(bf16[16,4096]{1,0:T(8,128)(2,1)} %param.4), channel_id=1, source_target_pairs={{0,1},{1,0},{2,3},{3,2},{4,5},{5,4},{6,7},{7,6},{8,9},{9,8},{10,11... | collective-permute-start | bytes 393224 | tf_op jit(solution)/shard_map/ppermute | solution.py:44
  3.1 5.4 %collective-permute-start = (bf16[16,4096]{1,0:T(8,128)(2,1)}, bf16[16,4096]{1,0:T(8,128)(2,1)S(1)}, u32[]{:S(2)}, u32[]{:S(2)}) collective-permute-start(bf16[16,4096]{1,0:T(8,128)(2,1)} %param.4), channel_id=1, source_target_pairs={{0,4},{1,3},{4,8},{5,1},{8,12},{9,5},{12,14},{13,9},{14,10},{15,13... | collective-permute-start | bytes 393224 | tf_op jit(solution)/shard_map/ppermute | solution.py:41
  4.1 5.7 %collective-permute-start.5 = (bf16[16,4096]{1,0:T(8,128)(2,1)S(1)}, bf16[16,4096]{1,0:T(8,128)(2,1)S(1)}, u32[]{:S(2)}, u32[]{:S(2)}) collective-permute-start(bf16[16,4096]{1,0:T(8,128)(2,1)S(1)} %collective-permute-done.3.rows.refs_0_), channel_id=1, source_target_pairs={{0,4},{1,3},{4,8},{5,1},{8,12},{9,5},{12,14},{13,9},{14,10},{15,13... | collective-permute-start | bytes 393224 | tf_op jit(solution)/shard_map/ppermute | solution.py:41
  5.7 5.5 %collective-permute-start.6 = (bf16[16,4096]{1,0:T(8,128)(2,1)S(1)}, bf16[16,4096]{1,0:T(8,128)(2,1)S(1)}, u32[]{:S(2)}, u32[]{:S(2)}) collective-permute-start(bf16[16,4096]{1,0:T(8,128)(2,1)S(1)} %collective-permute-done.4.refs_1_), channel_id=1, source_target_pairs={{0,4},{1,3},{4,8},{5,1},{8,12},{9,5},{12,14},{13,9},{14,10},{15,13... | collective-permute-start | bytes 393224 | tf_op jit(solution)/shard_map/ppermute | solution.py:41
  7.2 4.5 %collective-permute-start.8 = (bf16[16,4096]{1,0:T(8,128)(2,1)S(1)}, bf16[16,4096]{1,0:T(8,128)(2,1)S(1)}, u32[]{:S(2)}, u32[]{:S(2)}) collective-permute-start(bf16[16,4096]{1,0:T(8,128)(2,1)S(1)} %collective-permute-done.7.refs_0_), channel_id=1, source_target_pairs={{0,4},{1,3},{4,8},{5,1},{8,12},{9,5},{12,14},{13,9},{14,10},{15,13... | collective-permute-start | bytes 393224 | tf_op jit(solution)/shard_map/ppermute | solution.py:41
  8.5 4.5 %collective-permute-start.1 = (bf16[16,4096]{1,0:T(8,128)(2,1)S(1)}, bf16[16,4096]{1,0:T(8,128)(2,1)S(1)}, u32[]{:S(2)}, u32[]{:S(2)}) collective-permute-start(bf16[16,4096]{1,0:T(8,128)(2,1)S(1)} %collective-permute-done.refs_1_), channel_id=1, source_target_pairs={{0,4},{1,3},{4,8},{5,1},{8,12},{9,5},{12,14},{13,9},{14,10},{15,13... | collective-permute-start | bytes 393224 | tf_op jit(solution)/shard_map/ppermute | solution.py:41
  9.8 6.9 %collective-permute-start.10 = (bf16[16,4096]{1,0:T(8,128)(2,1)S(1)}, bf16[16,4096]{1,0:T(8,128)(2,1)S(1)}, u32[]{:S(2)}, u32[]{:S(2)}) collective-permute-start(bf16[16,4096]{1,0:T(8,128)(2,1)S(1)} %collective-permute-done.5.refs_2_), channel_id=1, source_target_pairs={{0,4},{1,3},{4,8},{5,1},{8,12},{9,5},{12,14},{13,9},{14,10},{15,13... | collective-permute-start | bytes 393224 | tf_op jit(solution)/shard_map/ppermute | solution.py:41
  11.1 5.8 %collective-permute-start.11 = (bf16[16,4096]{1,0:T(8,128)(2,1)S(1)}, bf16[16,4096]{1,0:T(8,128)(2,1)S(1)}, u32[]{:S(2)}, u32[]{:S(2)}) collective-permute-start(bf16[16,4096]{1,0:T(8,128)(2,1)S(1)} %collective-permute-done.6.refs_3_), channel_id=1, source_target_pairs={{0,4},{1,3},{4,8},{5,1},{8,12},{9,5},{12,14},{13,9},{14,10},{15,13... | collective-permute-start | bytes 393224 | tf_op jit(solution)/shard_map/ppermute | solution.py:41
  11.7 5.9 %collective-permute-start.12 = (bf16[16,4096]{1,0:T(8,128)(2,1)S(1)}, bf16[16,4096]{1,0:T(8,128)(2,1)S(1)}, u32[]{:S(2)}, u32[]{:S(2)}) collective-permute-start(bf16[16,4096]{1,0:T(8,128)(2,1)S(1)} %collective-permute-done.8.refs_2_), channel_id=1, source_target_pairs={{0,4},{1,3},{4,8},{5,1},{8,12},{9,5},{12,14},{13,9},{14,10},{15,13... | collective-permute-start | bytes 393224 | tf_op jit(solution)/shard_map/ppermute | solution.py:41
  13.0 5.7 %collective-permute-start.2 = (bf16[16,4096]{1,0:T(8,128)(2,1)S(1)}, bf16[16,4096]{1,0:T(8,128)(2,1)S(1)}, u32[]{:S(2)}, u32[]{:S(2)}) collective-permute-start(bf16[16,4096]{1,0:T(8,128)(2,1)S(1)} %collective-permute-done.1.refs_3_), channel_id=1, source_target_pairs={{0,4},{1,3},{4,8},{5,1},{8,12},{9,5},{12,14},{13,9},{14,10},{15,13... | collective-permute-start | bytes 393224 | tf_op jit(solution)/shard_map/ppermute | solution.py:41
  14.1 13.5 %collective-permute-start.9 = (bf16[128,4096]{1,0:T(8,128)(2,1)S(1)}, bf16[128,4096]{1,0:T(8,128)(2,1)S(1)}, u32[]{:S(2)}, u32[]{:S(2)}) collective-permute-start(bf16[128,4096]{1,0:T(8,128)(2,1)S(1)} %constant_dynamic-update-slice_fusion), channel_id=1, source_target_pairs={{0,1},{1,0},{2,3},{3,2},{4,5},{5,4},{6,7},{7,6},{8,9},{9,8},{10,11... | collective-permute-start | bytes 3145736 | tf_op jit(solution)/shard_map/ppermute | solution.py:44
  16.7 4.8 %collective-permute-start.14 = (bf16[16,4096]{1,0:T(8,128)(2,1)S(1)}, bf16[16,4096]{1,0:T(8,128)(2,1)S(1)}, u32[]{:S(2)}, u32[]{:S(2)}) collective-permute-start(bf16[16,4096]{1,0:T(8,128)(2,1)S(1)} %collective-permute-done.10.refs_5_), channel_id=1, source_target_pairs={{0,4},{1,3},{4,8},{5,1},{8,12},{9,5},{12,14},{13,9},{14,10},{15,13... | collective-permute-start | bytes 393224 | tf_op jit(solution)/shard_map/ppermute | solution.py:41
  16.9 5.9 %collective-permute-start.15 = (bf16[16,4096]{1,0:T(8,128)(2,1)S(1)}, bf16[16,4096]{1,0:T(8,128)(2,1)S(1)}, u32[]{:S(2)}, u32[]{:S(2)}) collective-permute-start(bf16[16,4096]{1,0:T(8,128)(2,1)S(1)} %collective-permute-done.11.refs_6_), channel_id=1, source_target_pairs={{0,4},{1,3},{4,8},{5,1},{8,12},{9,5},{12,14},{13,9},{14,10},{15,13... | collective-permute-start | bytes 393224 | tf_op jit(solution)/shard_map/ppermute | solution.py:41
  18.7 8.9 %collective-permute-start.13 = (bf16[64,4096]{1,0:T(8,128)(2,1)S(1)}, bf16[64,4096]{1,0:T(8,128)(2,1)S(1)}, u32[]{:S(2)}, u32[]{:S(2)}) collective-permute-start(bf16[64,4096]{1,0:T(8,128)(2,1)S(1)} %pad_maximum_fusion), channel_id=1, source_target_pairs={{0,1},{1,0},{2,3},{3,2},{4,5},{5,4},{6,7},{7,6},{8,9},{9,8},{10,11... | collective-permute-start | bytes 1572872 | tf_op jit(solution)/shard_map/ppermute | solution.py:44
  21.1 4.1 %collective-permute-start.18 = (bf16[16,4096]{1,0:T(8,128)(2,1)S(1)}, bf16[16,4096]{1,0:T(8,128)(2,1)S(1)}, u32[]{:S(2)}, u32[]{:S(2)}) collective-permute-start(bf16[16,4096]{1,0:T(8,128)(2,1)S(1)} %collective-permute-done.2.refs_6_), channel_id=1, source_target_pairs={{0,4},{1,3},{4,8},{5,1},{8,12},{9,5},{12,14},{13,9},{14,10},{15,13... | collective-permute-start | bytes 393224 | tf_op jit(solution)/shard_map/ppermute | solution.py:41
  21.6 5.1 %collective-permute-start.17 = (bf16[16,4096]{1,0:T(8,128)(2,1)S(1)}, bf16[16,4096]{1,0:T(8,128)(2,1)S(1)}, u32[]{:S(2)}, u32[]{:S(2)}) collective-permute-start(bf16[16,4096]{1,0:T(8,128)(2,1)S(1)} %collective-permute-done.12.refs_5_), channel_id=1, source_target_pairs={{0,4},{1,3},{4,8},{5,1},{8,12},{9,5},{12,14},{13,9},{14,10},{15,13... | collective-permute-start | bytes 393224 | tf_op jit(solution)/shard_map/ppermute | solution.py:41
  22.8 4.8 %collective-permute-start.16 = (bf16[32,4096]{1,0:T(8,128)(2,1)S(1)}, bf16[32,4096]{1,0:T(8,128)(2,1)S(1)}, u32[]{:S(2)}, u32[]{:S(2)}) collective-permute-start(bf16[32,4096]{1,0:T(8,128)(2,1)S(1)} %pad_maximum_fusion.1), channel_id=1, source_target_pairs={{0,1},{1,0},{2,3},{3,2},{4,5},{5,4},{6,7},{7,6},{8,9},{9,8},{10,11... | collective-permute-start | bytes 786440 | tf_op jit(solution)/shard_map/ppermute | solution.py:44
  26.6 3.3 %collective-permute-start.19 = (bf16[32,4096]{1,0:T(8,128)(2,1)S(1)}, bf16[32,4096]{1,0:T(8,128)(2,1)S(1)}, u32[]{:S(2)}, u32[]{:S(2)}) collective-permute-start(bf16[32,4096]{1,0:T(8,128)(2,1)S(1)} %pad_maximum_fusion.2), channel_id=1, source_target_pairs={{0,1},{1,0},{2,3},{3,2},{4,5},{5,4},{6,7},{7,6},{8,9},{9,8},{10,11... | collective-permute-start | bytes 786440 | tf_op jit(solution)/shard_map/ppermute | solution.py:44

commit v10 on v9

--- a/solution.py
+++ b/solution.py
@@ -9,6 +9,7 @@
 
 TEMP = 64
 LANES = 128
+EIGHT = 8
 CHUNK = 1024
 GROUP = 32
 LIMIT = 40 * 2**20
@@ -119,15 +120,23 @@
     return jnp.log(jnp.sum(jnp.exp(x - top), axis=0, keepdims=True)) + top
 
 
+def fold_rows(rows):
+    wide = rows.astype(jnp.float32)
+    total = wide[:EIGHT]
+    for row in range(EIGHT, wide.shape[0], EIGHT):
+        total += wide[row : row + EIGHT]
+    return total
+
+
 def total_kernel(rows, total):
-    total[...] = jnp.sum(rows[...].astype(jnp.float32), axis=0, keepdims=True)
+    total[...] = fold_rows(rows[...])
 
 
 def feature_total(rows, beside):
     in_vmem = pl.BlockSpec(memory_space=pltpu.VMEM)
     return pl.pallas_call(
         total_kernel,
-        out_shape=jax.ShapeDtypeStruct((1, rows.shape[1]), jnp.float32),
+        out_shape=jax.ShapeDtypeStruct((EIGHT, rows.shape[1]), jnp.float32),
         in_specs=[in_vmem],
         out_specs=in_vmem,
         compiler_params=pltpu.CompilerParams(vmem_limit_bytes=LIMIT),
@@ -146,8 +155,8 @@
         total = first_total[:, cols]
         for ref, rows, _ in groups:
             if ref is not panel[0]:
-                total += jnp.sum(ref[rows, cols].astype(jnp.float32), axis=0, keepdims=True)
-        here = total / count
+                total += fold_rows(ref[rows, cols])
+        here = jnp.sum(total, axis=0, keepdims=True) / count
         mean[:, cols] = here
         center_panel_chunk(cols, here, groups, centered, squares, start == 0)
         for rows in row_groups(probes.shape[0], GROUP):

time: 32.1 us -> 32.3 us (level)
  transfers between devices with their start and end apart: 20 -> 20, of which waited for: 6 -> 6; matrix products, arithmetic and copies ran while one was open for 0% -> 0% of each run, Pallas kernels for 7% -> 8%
where the time goes in v10:
time: 32.3 us; the launch traced here: 32.2 us
  starting transfers between devices  22.8 us (71%)
  waiting for transfers between devices  4.55 us (14%)
  Pallas kernels  4.55 us (14%)
    ppermute x14, starting transfers between devices, hop(): return lax.ppermute(block, 'samp', ring)  15.3 us
    ppermute x6, starting transfers between devices, hand_over(): return lax.ppermute(block, 'samp', twins)  7.49 us
    pallas_call x2, Pallas kernels, call(): pl.pallas_call(functools.partial(kernel, spans), out_shape=out_shape, in_...  4.54 us
    ppermute x14, waiting for transfers between devices, hop(): return lax.ppermute(block, 'samp', ring)  4.53 us
  transfers between devices with their start and end apart: 20, of which 6 were waited for; matrix products, arithmetic and copies ran while one was open for 0% of the time, Pallas kernels for 8%

profile of v10, /device:TPU:1, one launch (start us, length us, event | category | flops | bytes accessed | tf_op | source)
XLA Modules:
  0.0 32.2 jit_solution(6556885232873488131)
XLA Ops:
  0.0 0.0 copy-start
  0.0 0.1 collective-permute-start.3
  0.1 2.7 %collective-permute-start.4 = (bf16[16,4096]{1,0:T(8,128)(2,1)}, bf16[16,4096]{1,0:T(8,128)(2,1)S(1)}, u32[]{:S(2)}, u32[]{:S(2)}) collective-permute-start(bf16[16,4096]{1,0:T(8,128)(2,1)} %param.5), channel_id=1, source_target_pairs={{0,4},{1,3},{4,8},{5,1},{8,12},{9,5},{12,14},{13,9},{14,10},{15,13... | collective-permute-start | bytes 393224 | tf_op jit(solution)/shard_map/ppermute | solution.py:42
  2.7 0.4 %collective-permute-start.7 = (bf16[16,4096]{1,0:T(8,128)(2,1)}, bf16[16,4096]{1,0:T(8,128)(2,1)S(1)}, u32[]{:S(2)}, u32[]{:S(2)}) collective-permute-start(bf16[16,4096]{1,0:T(8,128)(2,1)} %param.4), channel_id=1, source_target_pairs={{0,1},{1,0},{2,3},{3,2},{4,5},{5,4},{6,7},{7,6},{8,9},{9,8},{10,11... | collective-permute-start | bytes 393224 | tf_op jit(solution)/shard_map/ppermute | solution.py:45
  3.1 0.9 %collective-permute-start = (bf16[16,4096]{1,0:T(8,128)(2,1)}, bf16[16,4096]{1,0:T(8,128)(2,1)S(1)}, u32[]{:S(2)}, u32[]{:S(2)}) collective-permute-start(bf16[16,4096]{1,0:T(8,128)(2,1)} %param.4), channel_id=1, source_target_pairs={{0,4},{1,3},{4,8},{5,1},{8,12},{9,5},{12,14},{13,9},{14,10},{15,13... | collective-permute-start | bytes 393224 | tf_op jit(solution)/shard_map/ppermute | solution.py:42
  4.0 0.0 collective-permute-done.3.rows.refs_0_
  4.1 1.3 %collective-permute-start.5 = (bf16[16,4096]{1,0:T(8,128)(2,1)S(1)}, bf16[16,4096]{1,0:T(8,128)(2,1)S(1)}, u32[]{:S(2)}, u32[]{:S(2)}) collective-permute-start(bf16[16,4096]{1,0:T(8,128)(2,1)S(1)} %collective-permute-done.3.rows.refs_0_), channel_id=1, source_target_pairs={{0,4},{1,3},{4,8},{5,1},{8,12},{9,5},{12,14},{13,9},{14,10},{15,13... | collective-permute-start | bytes 393224 | tf_op jit(solution)/shard_map/ppermute | solution.py:42
  5.4 0.3 collective-permute-done.4.refs_1_
  5.7 1.4 %collective-permute-start.6 = (bf16[16,4096]{1,0:T(8,128)(2,1)S(1)}, bf16[16,4096]{1,0:T(8,128)(2,1)S(1)}, u32[]{:S(2)}, u32[]{:S(2)}) collective-permute-start(bf16[16,4096]{1,0:T(8,128)(2,1)S(1)} %collective-permute-done.4.refs_1_), channel_id=1, source_target_pairs={{0,4},{1,3},{4,8},{5,1},{8,12},{9,5},{12,14},{13,9},{14,10},{15,13... | collective-permute-start | bytes 393224 | tf_op jit(solution)/shard_map/ppermute | solution.py:42
  7.1 0.0 collective-permute-done.7.refs_0_
  7.1 1.3 %collective-permute-start.8 = (bf16[16,4096]{1,0:T(8,128)(2,1)S(1)}, bf16[16,4096]{1,0:T(8,128)(2,1)S(1)}, u32[]{:S(2)}, u32[]{:S(2)}) collective-permute-start(bf16[16,4096]{1,0:T(8,128)(2,1)S(1)} %collective-permute-done.7.refs_0_), channel_id=1, source_target_pairs={{0,4},{1,3},{4,8},{5,1},{8,12},{9,5},{12,14},{13,9},{14,10},{15,13... | collective-permute-start | bytes 393224 | tf_op jit(solution)/shard_map/ppermute | solution.py:42
  8.5 0.0 collective-permute-done.refs_1_
  8.5 1.3 %collective-permute-start.1 = (bf16[16,4096]{1,0:T(8,128)(2,1)S(1)}, bf16[16,4096]{1,0:T(8,128)(2,1)S(1)}, u32[]{:S(2)}, u32[]{:S(2)}) collective-permute-start(bf16[16,4096]{1,0:T(8,128)(2,1)S(1)} %collective-permute-done.refs_1_), channel_id=1, source_target_pairs={{0,4},{1,3},{4,8},{5,1},{8,12},{9,5},{12,14},{13,9},{14,10},{15,13... | collective-permute-start | bytes 393224 | tf_op jit(solution)/shard_map/ppermute | solution.py:42
  9.8 0.0 collective-permute-done.5.refs_2_
  9.8 1.3 %collective-permute-start.10 = (bf16[16,4096]{1,0:T(8,128)(2,1)S(1)}, bf16[16,4096]{1,0:T(8,128)(2,1)S(1)}, u32[]{:S(2)}, u32[]{:S(2)}) collective-permute-start(bf16[16,4096]{1,0:T(8,128)(2,1)S(1)} %collective-permute-done.5.refs_2_), channel_id=1, source_target_pairs={{0,4},{1,3},{4,8},{5,1},{8,12},{9,5},{12,14},{13,9},{14,10},{15,13... | collective-permute-start | bytes 393224 | tf_op jit(solution)/shard_map/ppermute | solution.py:42
  11.1 0.0 collective-permute-done.6.refs_3_
  11.1 0.3 collective-permute-start.11
  11.4 0.2 collective-permute-done.8.refs_2_
  11.7 1.0 %collective-permute-start.12 = (bf16[16,4096]{1,0:T(8,128)(2,1)S(1)}, bf16[16,4096]{1,0:T(8,128)(2,1)S(1)}, u32[]{:S(2)}, u32[]{:S(2)}) collective-permute-start(bf16[16,4096]{1,0:T(8,128)(2,1)S(1)} %collective-permute-done.8.refs_2_), channel_id=1, source_target_pairs={{0,4},{1,3},{4,8},{5,1},{8,12},{9,5},{12,14},{13,9},{14,10},{15,13... | collective-permute-start | bytes 393224 | tf_op jit(solution)/shard_map/ppermute | solution.py:42
  12.7 0.3 collective-permute-done.1.refs_3_
  13.0 1.1 %collective-permute-start.2 = (bf16[16,4096]{1,0:T(8,128)(2,1)S(1)}, bf16[16,4096]{1,0:T(8,128)(2,1)S(1)}, u32[]{:S(2)}, u32[]{:S(2)}) collective-permute-start(bf16[16,4096]{1,0:T(8,128)(2,1)S(1)} %collective-permute-done.1.refs_3_), channel_id=1, source_target_pairs={{0,4},{1,3},{4,8},{5,1},{8,12},{9,5},{12,14},{13,9},{14,10},{15,13... | collective-permute-start | bytes 393224 | tf_op jit(solution)/shard_map/ppermute | solution.py:42
  14.1 2.6 %collective-permute-start.9 = (bf16[128,4096]{1,0:T(8,128)(2,1)S(1)}, bf16[128,4096]{1,0:T(8,128)(2,1)S(1)}, u32[]{:S(2)}, u32[]{:S(2)}) collective-permute-start(bf16[128,4096]{1,0:T(8,128)(2,1)S(1)} %constant_dynamic-update-slice_fusion), channel_id=1, source_target_pairs={{0,1},{1,0},{2,3},{3,2},{4,5},{5,4},{6,7},{7,6},{8,9},{9,8},{10,11... | collective-permute-start | bytes 3145736 | tf_op jit(solution)/shard_map/ppermute | solution.py:45
  16.7 0.0 collective-permute-done.10.refs_5_
  16.7 0.2 collective-permute-start.14
  16.9 0.0 collective-permute-done.11.refs_6_
  16.9 0.7 %collective-permute-start.15 = (bf16[16,4096]{1,0:T(8,128)(2,1)S(1)}, bf16[16,4096]{1,0:T(8,128)(2,1)S(1)}, u32[]{:S(2)}, u32[]{:S(2)}) collective-permute-start(bf16[16,4096]{1,0:T(8,128)(2,1)S(1)} %collective-permute-done.11.refs_6_), channel_id=1, source_target_pairs={{0,4},{1,3},{4,8},{5,1},{8,12},{9,5},{12,14},{13,9},{14,10},{15,13... | collective-permute-start | bytes 393224 | tf_op jit(solution)/shard_map/ppermute | solution.py:42
  17.6 0.0 collective-permute-done.12.refs_5_
  17.6 1.1 %collective-permute-done.2.refs_6_ = bf16[16,4096]{1,0:T(8,128)(2,1)S(1)} collective-permute-done((bf16[16,4096]{1,0:T(8,128)(2,1)S(1)}, bf16[16,4096]{1,0:T(8,128)(2,1)S(1)}, u32[]{:S(2)}, u32[]{:S(2)}) %collective-permute-start.2) | collective-permute-done | bytes 131104 | tf_op jit(solution)/shard_map/ppermute | solution.py:42
  18.7 2.3 %collective-permute-start.13 = (bf16[64,4096]{1,0:T(8,128)(2,1)S(1)}, bf16[64,4096]{1,0:T(8,128)(2,1)S(1)}, u32[]{:S(2)}, u32[]{:S(2)}) collective-permute-start(bf16[64,4096]{1,0:T(8,128)(2,1)S(1)} %pad_maximum_fusion), channel_id=1, source_target_pairs={{0,1},{1,0},{2,3},{3,2},{4,5},{5,4},{6,7},{7,6},{8,9},{9,8},{10,11... | collective-permute-start | bytes 1572872 | tf_op jit(solution)/shard_map/ppermute | solution.py:45
  21.1 0.5 %collective-permute-start.18 = (bf16[16,4096]{1,0:T(8,128)(2,1)S(1)}, bf16[16,4096]{1,0:T(8,128)(2,1)S(1)}, u32[]{:S(2)}, u32[]{:S(2)}) collective-permute-start(bf16[16,4096]{1,0:T(8,128)(2,1)S(1)} %collective-permute-done.2.refs_6_), channel_id=1, source_target_pairs={{0,4},{1,3},{4,8},{5,1},{8,12},{9,5},{12,14},{13,9},{14,10},{15,13... | collective-permute-start | bytes 393224 | tf_op jit(solution)/shard_map/ppermute | solution.py:42
  21.5 0.0 collective-permute-done.14.refs_8_
  21.5 1.3 %collective-permute-start.17 = (bf16[16,4096]{1,0:T(8,128)(2,1)S(1)}, bf16[16,4096]{1,0:T(8,128)(2,1)S(1)}, u32[]{:S(2)}, u32[]{:S(2)}) collective-permute-start(bf16[16,4096]{1,0:T(8,128)(2,1)S(1)} %collective-permute-done.12.refs_5_), channel_id=1, source_target_pairs={{0,4},{1,3},{4,8},{5,1},{8,12},{9,5},{12,14},{13,9},{14,10},{15,13... | collective-permute-start | bytes 393224 | tf_op jit(solution)/shard_map/ppermute | solution.py:42
  22.8 0.0 collective-permute-done.15.refs_9_
  22.8 1.1 %collective-permute-start.16 = (bf16[32,4096]{1,0:T(8,128)(2,1)S(1)}, bf16[32,4096]{1,0:T(8,128)(2,1)S(1)}, u32[]{:S(2)}, u32[]{:S(2)}) collective-permute-start(bf16[32,4096]{1,0:T(8,128)(2,1)S(1)} %pad_maximum_fusion.1), channel_id=1, source_target_pairs={{0,1},{1,0},{2,3},{3,2},{4,5},{5,4},{6,7},{7,6},{8,9},{9,8},{10,11... | collective-permute-start | bytes 786440 | tf_op jit(solution)/shard_map/ppermute | solution.py:45
  23.9 1.2 %collective-permute-done.18.refs_9_ = bf16[16,4096]{1,0:T(8,128)(2,1)S(1)} collective-permute-done((bf16[16,4096]{1,0:T(8,128)(2,1)S(1)}, bf16[16,4096]{1,0:T(8,128)(2,1)S(1)}, u32[]{:S(2)}, u32[]{:S(2)}) %collective-permute-start.18) | collective-permute-done | bytes 131104 | tf_op jit(solution)/shard_map/ppermute | solution.py:42
  25.2 1.4 %collective-permute-done.17.refs_8_ = bf16[16,4096]{1,0:T(8,128)(2,1)S(1)} collective-permute-done((bf16[16,4096]{1,0:T(8,128)(2,1)S(1)}, bf16[16,4096]{1,0:T(8,128)(2,1)S(1)}, u32[]{:S(2)}, u32[]{:S(2)}) %collective-permute-start.17) | collective-permute-done | bytes 131104 | tf_op jit(solution)/shard_map/ppermute | solution.py:42
  26.6 1.0 %collective-permute-start.19 = (bf16[32,4096]{1,0:T(8,128)(2,1)S(1)}, bf16[32,4096]{1,0:T(8,128)(2,1)S(1)}, u32[]{:S(2)}, u32[]{:S(2)}) collective-permute-start(bf16[32,4096]{1,0:T(8,128)(2,1)S(1)} %pad_maximum_fusion.2), channel_id=1, source_target_pairs={{0,1},{1,0},{2,3},{3,2},{4,5},{5,4},{6,7},{7,6},{8,9},{9,8},{10,11... | collective-permute-start | bytes 786440 | tf_op jit(solution)/shard_map/ppermute | solution.py:45
  27.6 0.0 collective-permute-done.16.refs_10_
  27.6 0.0 collective-permute-done.13.refs_7_
  27.6 0.0 collective-permute-done.9.refs_4_
  27.6 0.0 copy-done
  27.6 2.5 %shard_map.38 = (bf16[512,4096]{1,0:T(8,128)(2,1)S(1)}, f32[1,4096]{1,0:T(1,128)S(1)}, f32[1,512]{1,0:T(1,128)S(1)}) custom-call(bf16[512,4096]{1,0:T(8,128)(2,1)S(1)} %copy-done, f32[8,4096]{1,0:T(8,128)S(1)} %shard_map.37.first_total, bf16[16,4096]{1,0:T(8,128)(2,1)S(1)} %collective-permute-done.3.rows.refs_0_, ...), custom_call_target="tpu_custom_call" | custom-call | flops 1073741824 | bytes 6291456 | tf_op jit(solution)/shard_map/pallas_call | solution.py:183
  30.1 0.0 collective-permute-done.19.refs_10_
  30.1 2.1 %shard_map.39 = f32[1,512]{1,0:T(1,128)} custom-call(f32[1,512]{1,0:T(1,128)S(1)} %get-tuple-element.11.ref_log, bf16[512,4096]{1,0:T(8,128)(2,1)S(1)} %get-tuple-element.12.probes, f32[1,4096]{1,0:T(1,128)S(1)} %get-tuple-element.13.mean, bf16[16,4096]{1,0:T(8,128)(2,1)S(1)} %collective-permute-done.7.refs_0_, ...), custom_call_target="tpu_custom_call" | custom-call | flops 1073741824 | bytes 6291456 | tf_op jit(solution)/shard_map/pallas_call | solution.py:183
  (12 shorter events, 0.2 us)
Async XLA Ops:
  0.0 27.6 %copy-start = (bf16[512,4096]{1,0:T(8,128)(2,1)S(1)}, bf16[512,4096]{1,0:T(8,128)(2,1)}, u32[]{:S(2)}) copy-start(bf16[512,4096]{1,0:T(8,128)(2,1)} %queries.1) | copy-start | bytes 12582916
  0.0 4.0 %collective-permute-start.3 = (bf16[16,4096]{1,0:T(8,128)(2,1)}, bf16[16,4096]{1,0:T(8,128)(2,1)S(1)}, u32[]{:S(2)}, u32[]{:S(2)}) collective-permute-start(bf16[16,4096]{1,0:T(8,128)(2,1)} %param.5), channel_id=1, source_target_pairs={{0,1},{1,0},{2,3},{3,2},{4,5},{5,4},{6,7},{7,6},{8,9},{9,8},{10,11... | collective-permute-start | bytes 393224 | tf_op jit(solution)/shard_map/ppermute | solution.py:45
  0.1 5.6 %collective-permute-start.4 = (bf16[16,4096]{1,0:T(8,128)(2,1)}, bf16[16,4096]{1,0:T(8,128)(2,1)S(1)}, u32[]{:S(2)}, u32[]{:S(2)}) collective-permute-start(bf16[16,4096]{1,0:T(8,128)(2,1)} %param.5), channel_id=1, source_target_pairs={{0,4},{1,3},{4,8},{5,1},{8,12},{9,5},{12,14},{13,9},{14,10},{15,13... | collective-permute-start | bytes 393224 | tf_op jit(solution)/shard_map/ppermute | solution.py:42
  2.7 4.4 %collective-permute-start.7 = (bf16[16,4096]{1,0:T(8,128)(2,1)}, bf16[16,4096]{1,0:T(8,128)(2,1)S(1)}, u32[]{:S(2)}, u32[]{:S(2)}) collective-permute-start(bf16[16,4096]{1,0:T(8,128)(2,1)} %param.4), channel_id=1, source_target_pairs={{0,1},{1,0},{2,3},{3,2},{4,5},{5,4},{6,7},{7,6},{8,9},{9,8},{10,11... | collective-permute-start | bytes 393224 | tf_op jit(solution)/shard_map/ppermute | solution.py:45
  3.1 5.3 %collective-permute-start = (bf16[16,4096]{1,0:T(8,128)(2,1)}, bf16[16,4096]{1,0:T(8,128)(2,1)S(1)}, u32[]{:S(2)}, u32[]{:S(2)}) collective-permute-start(bf16[16,4096]{1,0:T(8,128)(2,1)} %param.4), channel_id=1, source_target_pairs={{0,4},{1,3},{4,8},{5,1},{8,12},{9,5},{12,14},{13,9},{14,10},{15,13... | collective-permute-start | bytes 393224 | tf_op jit(solution)/shard_map/ppermute | solution.py:42
  4.1 5.7 %collective-permute-start.5 = (bf16[16,4096]{1,0:T(8,128)(2,1)S(1)}, bf16[16,4096]{1,0:T(8,128)(2,1)S(1)}, u32[]{:S(2)}, u32[]{:S(2)}) collective-permute-start(bf16[16,4096]{1,0:T(8,128)(2,1)S(1)} %collective-permute-done.3.rows.refs_0_), channel_id=1, source_target_pairs={{0,4},{1,3},{4,8},{5,1},{8,12},{9,5},{12,14},{13,9},{14,10},{15,13... | collective-permute-start | bytes 393224 | tf_op jit(solution)/shard_map/ppermute | solution.py:42
  5.7 5.4 %collective-permute-start.6 = (bf16[16,4096]{1,0:T(8,128)(2,1)S(1)}, bf16[16,4096]{1,0:T(8,128)(2,1)S(1)}, u32[]{:S(2)}, u32[]{:S(2)}) collective-permute-start(bf16[16,4096]{1,0:T(8,128)(2,1)S(1)} %collective-permute-done.4.refs_1_), channel_id=1, source_target_pairs={{0,4},{1,3},{4,8},{5,1},{8,12},{9,5},{12,14},{13,9},{14,10},{15,13... | collective-permute-start | bytes 393224 | tf_op jit(solution)/shard_map/ppermute | solution.py:42
  7.1 4.6 %collective-permute-start.8 = (bf16[16,4096]{1,0:T(8,128)(2,1)S(1)}, bf16[16,4096]{1,0:T(8,128)(2,1)S(1)}, u32[]{:S(2)}, u32[]{:S(2)}) collective-permute-start(bf16[16,4096]{1,0:T(8,128)(2,1)S(1)} %collective-permute-done.7.refs_0_), channel_id=1, source_target_pairs={{0,4},{1,3},{4,8},{5,1},{8,12},{9,5},{12,14},{13,9},{14,10},{15,13... | collective-permute-start | bytes 393224 | tf_op jit(solution)/shard_map/ppermute | solution.py:42
  8.5 4.5 %collective-permute-start.1 = (bf16[16,4096]{1,0:T(8,128)(2,1)S(1)}, bf16[16,4096]{1,0:T(8,128)(2,1)S(1)}, u32[]{:S(2)}, u32[]{:S(2)}) collective-permute-start(bf16[16,4096]{1,0:T(8,128)(2,1)S(1)} %collective-permute-done.refs_1_), channel_id=1, source_target_pairs={{0,4},{1,3},{4,8},{5,1},{8,12},{9,5},{12,14},{13,9},{14,10},{15,13... | collective-permute-start | bytes 393224 | tf_op jit(solution)/shard_map/ppermute | solution.py:42
  9.8 6.9 %collective-permute-start.10 = (bf16[16,4096]{1,0:T(8,128)(2,1)S(1)}, bf16[16,4096]{1,0:T(8,128)(2,1)S(1)}, u32[]{:S(2)}, u32[]{:S(2)}) collective-permute-start(bf16[16,4096]{1,0:T(8,128)(2,1)S(1)} %collective-permute-done.5.refs_2_), channel_id=1, source_target_pairs={{0,4},{1,3},{4,8},{5,1},{8,12},{9,5},{12,14},{13,9},{14,10},{15,13... | collective-permute-start | bytes 393224 | tf_op jit(solution)/shard_map/ppermute | solution.py:42
  11.1 5.8 %collective-permute-start.11 = (bf16[16,4096]{1,0:T(8,128)(2,1)S(1)}, bf16[16,4096]{1,0:T(8,128)(2,1)S(1)}, u32[]{:S(2)}, u32[]{:S(2)}) collective-permute-start(bf16[16,4096]{1,0:T(8,128)(2,1)S(1)} %collective-permute-done.6.refs_3_), channel_id=1, source_target_pairs={{0,4},{1,3},{4,8},{5,1},{8,12},{9,5},{12,14},{13,9},{14,10},{15,13... | collective-permute-start | bytes 393224 | tf_op jit(solution)/shard_map/ppermute | solution.py:42
  11.7 5.9 %collective-permute-start.12 = (bf16[16,4096]{1,0:T(8,128)(2,1)S(1)}, bf16[16,4096]{1,0:T(8,128)(2,1)S(1)}, u32[]{:S(2)}, u32[]{:S(2)}) collective-permute-start(bf16[16,4096]{1,0:T(8,128)(2,1)S(1)} %collective-permute-done.8.refs_2_), channel_id=1, source_target_pairs={{0,4},{1,3},{4,8},{5,1},{8,12},{9,5},{12,14},{13,9},{14,10},{15,13... | collective-permute-start | bytes 393224 | tf_op jit(solution)/shard_map/ppermute | solution.py:42
  13.0 5.7 %collective-permute-start.2 = (bf16[16,4096]{1,0:T(8,128)(2,1)S(1)}, bf16[16,4096]{1,0:T(8,128)(2,1)S(1)}, u32[]{:S(2)}, u32[]{:S(2)}) collective-permute-start(bf16[16,4096]{1,0:T(8,128)(2,1)S(1)} %collective-permute-done.1.refs_3_), channel_id=1, source_target_pairs={{0,4},{1,3},{4,8},{5,1},{8,12},{9,5},{12,14},{13,9},{14,10},{15,13... | collective-permute-start | bytes 393224 | tf_op jit(solution)/shard_map/ppermute | solution.py:42
  14.1 13.5 %collective-permute-start.9 = (bf16[128,4096]{1,0:T(8,128)(2,1)S(1)}, bf16[128,4096]{1,0:T(8,128)(2,1)S(1)}, u32[]{:S(2)}, u32[]{:S(2)}) collective-permute-start(bf16[128,4096]{1,0:T(8,128)(2,1)S(1)} %constant_dynamic-update-slice_fusion), channel_id=1, source_target_pairs={{0,1},{1,0},{2,3},{3,2},{4,5},{5,4},{6,7},{7,6},{8,9},{9,8},{10,11... | collective-permute-start | bytes 3145736 | tf_op jit(solution)/shard_map/ppermute | solution.py:45
  16.7 4.8 %collective-permute-start.14 = (bf16[16,4096]{1,0:T(8,128)(2,1)S(1)}, bf16[16,4096]{1,0:T(8,128)(2,1)S(1)}, u32[]{:S(2)}, u32[]{:S(2)}) collective-permute-start(bf16[16,4096]{1,0:T(8,128)(2,1)S(1)} %collective-permute-done.10.refs_5_), channel_id=1, source_target_pairs={{0,4},{1,3},{4,8},{5,1},{8,12},{9,5},{12,14},{13,9},{14,10},{15,13... | collective-permute-start | bytes 393224 | tf_op jit(solution)/shard_map/ppermute | solution.py:42
  16.9 5.9 %collective-permute-start.15 = (bf16[16,4096]{1,0:T(8,128)(2,1)S(1)}, bf16[16,4096]{1,0:T(8,128)(2,1)S(1)}, u32[]{:S(2)}, u32[]{:S(2)}) collective-permute-start(bf16[16,4096]{1,0:T(8,128)(2,1)S(1)} %collective-permute-done.11.refs_6_), channel_id=1, source_target_pairs={{0,4},{1,3},{4,8},{5,1},{8,12},{9,5},{12,14},{13,9},{14,10},{15,13... | collective-permute-start | bytes 393224 | tf_op jit(solution)/shard_map/ppermute | solution.py:42
  18.7 8.9 %collective-permute-start.13 = (bf16[64,4096]{1,0:T(8,128)(2,1)S(1)}, bf16[64,4096]{1,0:T(8,128)(2,1)S(1)}, u32[]{:S(2)}, u32[]{:S(2)}) collective-permute-start(bf16[64,4096]{1,0:T(8,128)(2,1)S(1)} %pad_maximum_fusion), channel_id=1, source_target_pairs={{0,1},{1,0},{2,3},{3,2},{4,5},{5,4},{6,7},{7,6},{8,9},{9,8},{10,11... | collective-permute-start | bytes 1572872 | tf_op jit(solution)/shard_map/ppermute | solution.py:45
  21.1 4.1 %collective-permute-start.18 = (bf16[16,4096]{1,0:T(8,128)(2,1)S(1)}, bf16[16,4096]{1,0:T(8,128)(2,1)S(1)}, u32[]{:S(2)}, u32[]{:S(2)}) collective-permute-start(bf16[16,4096]{1,0:T(8,128)(2,1)S(1)} %collective-permute-done.2.refs_6_), channel_id=1, source_target_pairs={{0,4},{1,3},{4,8},{5,1},{8,12},{9,5},{12,14},{13,9},{14,10},{15,13... | collective-permute-start | bytes 393224 | tf_op jit(solution)/shard_map/ppermute | solution.py:42
  21.5 5.1 %collective-permute-start.17 = (bf16[16,4096]{1,0:T(8,128)(2,1)S(1)}, bf16[16,4096]{1,0:T(8,128)(2,1)S(1)}, u32[]{:S(2)}, u32[]{:S(2)}) collective-permute-start(bf16[16,4096]{1,0:T(8,128)(2,1)S(1)} %collective-permute-done.12.refs_5_), channel_id=1, source_target_pairs={{0,4},{1,3},{4,8},{5,1},{8,12},{9,5},{12,14},{13,9},{14,10},{15,13... | collective-permute-start | bytes 393224 | tf_op jit(solution)/shard_map/ppermute | solution.py:42
  22.8 4.8 %collective-permute-start.16 = (bf16[32,4096]{1,0:T(8,128)(2,1)S(1)}, bf16[32,4096]{1,0:T(8,128)(2,1)S(1)}, u32[]{:S(2)}, u32[]{:S(2)}) collective-permute-start(bf16[32,4096]{1,0:T(8,128)(2,1)S(1)} %pad_maximum_fusion.1), channel_id=1, source_target_pairs={{0,1},{1,0},{2,3},{3,2},{4,5},{5,4},{6,7},{7,6},{8,9},{9,8},{10,11... | collective-permute-start | bytes 786440 | tf_op jit(solution)/shard_map/ppermute | solution.py:45
  26.6 3.5 %collective-permute-start.19 = (bf16[32,4096]{1,0:T(8,128)(2,1)S(1)}, bf16[32,4096]{1,0:T(8,128)(2,1)S(1)}, u32[]{:S(2)}, u32[]{:S(2)}) collective-permute-start(bf16[32,4096]{1,0:T(8,128)(2,1)S(1)} %pad_maximum_fusion.2), channel_id=1, source_target_pairs={{0,1},{1,0},{2,3},{3,2},{4,5},{5,4},{6,7},{7,6},{8,9},{9,8},{10,11... | collective-permute-start | bytes 786440 | tf_op jit(solution)/shard_map/ppermute | solution.py:45

commit v11 on v9

--- a/solution.py
+++ b/solution.py
@@ -106,17 +106,17 @@
 
 def add_products(cols, probes, centered, scores, first):
     products = lax.dot_general(
-        centered[:, cols], probes[:, cols], (((1,), (1,)), ((), ())),
+        probes[:, cols], centered[:, cols], (((1,), (1,)), ((), ())),
         preferred_element_type=jnp.float32,
     )
     scores[...] = products if first else scores[...] + products
 
 
 def log_sum(squares, scores):
-    half = 0.5 * jnp.sum(squares[...], axis=1, keepdims=True)
+    half = 0.5 * jnp.sum(squares[...].T, axis=0, keepdims=True)
     x = (scores[...] - half) / TEMP
-    top = jnp.max(x, axis=0, keepdims=True)
-    return jnp.log(jnp.sum(jnp.exp(x - top), axis=0, keepdims=True)) + top
+    top = jnp.max(x, axis=1, keepdims=True)
+    return jnp.log(jnp.sum(jnp.exp(x - top), axis=1, keepdims=True)) + top
 
 
 def total_kernel(rows, total):
@@ -163,7 +163,8 @@
         cols = slice(start, start + CHUNK)
         center_panel_chunk(cols, mean[:, cols], groups, centered, squares, start == 0)
         add_products(cols, probes, centered, scores, start == 0)
-    proof[...] = log_sum(squares, scores) - ref_log[...]
+    column = log_sum(squares, scores) - ref_log[...]
+    proof[...] = jnp.broadcast_to(column, (column.shape[0], LANES)).T[:1]
 
 
 def call(kernel, before, pieces, count, out_shape):
@@ -179,7 +180,7 @@
         scratch_shapes=[
             pltpu.VMEM((rows, features), jnp.bfloat16),
             pltpu.VMEM((rows, LANES), jnp.float32),
-            pltpu.VMEM((rows, count), jnp.float32),
+            pltpu.VMEM((count, rows), jnp.float32),
         ],
         compiler_params=pltpu.CompilerParams(vmem_limit_bytes=LIMIT),
         cost_estimate=pl.CostEstimate(
@@ -196,7 +197,7 @@
         panels, lax.axis_size("samp"), functools.partial(feature_total, beside=queries)
     )
     count, features = queries.shape
-    logs = jax.ShapeDtypeStruct((1, count), jnp.float32)
+    column, row = (jax.ShapeDtypeStruct(s, jnp.float32) for s in ((count, 1), (1, count)))
     probes, mean, ref_log = call(
         ref_kernel,
         [queries, first_total],
@@ -205,10 +206,10 @@
         (
             jax.ShapeDtypeStruct((count, features), jnp.bfloat16),
             jax.ShapeDtypeStruct((1, features), jnp.float32),
-            logs,
-        ),
-    )
-    return call(gen_kernel, [ref_log, probes, mean], gen_pieces, count, logs).reshape(-1)
+            column,
+        ),
+    )
+    return call(gen_kernel, [ref_log, probes, mean], gen_pieces, count, row).reshape(-1)
 
 
 def solution(mesh):

time: 32.1 us -> 32.6 us (1.016)
  Pallas kernels: 4.41 us -> 4.83 us
    pallas_call x2, Pallas kernels: 4.35 us -> 4.78 us  [call(): pl.pallas_call(functools.partial(kernel, spans), out_shape=out_shape, in_...]
where the time goes in v11:
time: 32.6 us; the launch traced here: 32.4 us
  starting transfers between devices  22.8 us (70%)
  Pallas kernels  4.83 us (15%)
  waiting for transfers between devices  4.55 us (14%)
    ppermute x14, starting transfers between devices, hop(): return lax.ppermute(block, 'samp', ring)  15.2 us
    ppermute x6, starting transfers between devices, hand_over(): return lax.ppermute(block, 'samp', twins)  7.58 us
    pallas_call x2, Pallas kernels, call(): pl.pallas_call(functools.partial(kernel, spans), out_shape=out_shape, in_...  4.78 us
    ppermute x14, waiting for transfers between devices, hop(): return lax.ppermute(block, 'samp', ring)  4.53 us
  transfers between devices with their start and end apart: 20, of which 6 were waited for; matrix products, arithmetic and copies ran while one was open for 0% of the time, Pallas kernels for 7%

profile of v11, /device:TPU:1, one launch (start us, length us, event | category | flops | bytes accessed | tf_op | source)
XLA Modules:
  0.0 32.4 jit_solution(5978008784304769364)
XLA Ops:
  0.0 0.0 copy-start
  0.0 0.1 collective-permute-start.3
  0.1 2.7 %collective-permute-start.4 = (bf16[16,4096]{1,0:T(8,128)(2,1)}, bf16[16,4096]{1,0:T(8,128)(2,1)S(1)}, u32[]{:S(2)}, u32[]{:S(2)}) collective-permute-start(bf16[16,4096]{1,0:T(8,128)(2,1)} %param.5), channel_id=1, source_target_pairs={{0,4},{1,3},{4,8},{5,1},{8,12},{9,5},{12,14},{13,9},{14,10},{15,13... | collective-permute-start | bytes 393224 | tf_op jit(solution)/shard_map/ppermute | solution.py:41
  2.7 0.4 %collective-permute-start.7 = (bf16[16,4096]{1,0:T(8,128)(2,1)}, bf16[16,4096]{1,0:T(8,128)(2,1)S(1)}, u32[]{:S(2)}, u32[]{:S(2)}) collective-permute-start(bf16[16,4096]{1,0:T(8,128)(2,1)} %param.4), channel_id=1, source_target_pairs={{0,1},{1,0},{2,3},{3,2},{4,5},{5,4},{6,7},{7,6},{8,9},{9,8},{10,11... | collective-permute-start | bytes 393224 | tf_op jit(solution)/shard_map/ppermute | solution.py:44
  3.1 0.9 %collective-permute-start = (bf16[16,4096]{1,0:T(8,128)(2,1)}, bf16[16,4096]{1,0:T(8,128)(2,1)S(1)}, u32[]{:S(2)}, u32[]{:S(2)}) collective-permute-start(bf16[16,4096]{1,0:T(8,128)(2,1)} %param.4), channel_id=1, source_target_pairs={{0,4},{1,3},{4,8},{5,1},{8,12},{9,5},{12,14},{13,9},{14,10},{15,13... | collective-permute-start | bytes 393224 | tf_op jit(solution)/shard_map/ppermute | solution.py:41
  4.0 0.0 collective-permute-done.3.rows.refs_0_
  4.1 1.3 %collective-permute-start.5 = (bf16[16,4096]{1,0:T(8,128)(2,1)S(1)}, bf16[16,4096]{1,0:T(8,128)(2,1)S(1)}, u32[]{:S(2)}, u32[]{:S(2)}) collective-permute-start(bf16[16,4096]{1,0:T(8,128)(2,1)S(1)} %collective-permute-done.3.rows.refs_0_), channel_id=1, source_target_pairs={{0,4},{1,3},{4,8},{5,1},{8,12},{9,5},{12,14},{13,9},{14,10},{15,13... | collective-permute-start | bytes 393224 | tf_op jit(solution)/shard_map/ppermute | solution.py:41
  5.4 0.3 collective-permute-done.4.refs_1_
  5.7 1.4 %collective-permute-start.6 = (bf16[16,4096]{1,0:T(8,128)(2,1)S(1)}, bf16[16,4096]{1,0:T(8,128)(2,1)S(1)}, u32[]{:S(2)}, u32[]{:S(2)}) collective-permute-start(bf16[16,4096]{1,0:T(8,128)(2,1)S(1)} %collective-permute-done.4.refs_1_), channel_id=1, source_target_pairs={{0,4},{1,3},{4,8},{5,1},{8,12},{9,5},{12,14},{13,9},{14,10},{15,13... | collective-permute-start | bytes 393224 | tf_op jit(solution)/shard_map/ppermute | solution.py:41
  7.1 0.1 shard_map.37.first_total
  7.1 0.0 collective-permute-done.7.refs_0_
  7.2 1.3 %collective-permute-start.8 = (bf16[16,4096]{1,0:T(8,128)(2,1)S(1)}, bf16[16,4096]{1,0:T(8,128)(2,1)S(1)}, u32[]{:S(2)}, u32[]{:S(2)}) collective-permute-start(bf16[16,4096]{1,0:T(8,128)(2,1)S(1)} %collective-permute-done.7.refs_0_), channel_id=1, source_target_pairs={{0,4},{1,3},{4,8},{5,1},{8,12},{9,5},{12,14},{13,9},{14,10},{15,13... | collective-permute-start | bytes 393224 | tf_op jit(solution)/shard_map/ppermute | solution.py:41
  8.5 0.0 collective-permute-done.refs_1_
  8.5 1.3 %collective-permute-start.1 = (bf16[16,4096]{1,0:T(8,128)(2,1)S(1)}, bf16[16,4096]{1,0:T(8,128)(2,1)S(1)}, u32[]{:S(2)}, u32[]{:S(2)}) collective-permute-start(bf16[16,4096]{1,0:T(8,128)(2,1)S(1)} %collective-permute-done.refs_1_), channel_id=1, source_target_pairs={{0,4},{1,3},{4,8},{5,1},{8,12},{9,5},{12,14},{13,9},{14,10},{15,13... | collective-permute-start | bytes 393224 | tf_op jit(solution)/shard_map/ppermute | solution.py:41
  9.8 0.0 collective-permute-done.5.refs_2_
  9.8 1.3 %collective-permute-start.10 = (bf16[16,4096]{1,0:T(8,128)(2,1)S(1)}, bf16[16,4096]{1,0:T(8,128)(2,1)S(1)}, u32[]{:S(2)}, u32[]{:S(2)}) collective-permute-start(bf16[16,4096]{1,0:T(8,128)(2,1)S(1)} %collective-permute-done.5.refs_2_), channel_id=1, source_target_pairs={{0,4},{1,3},{4,8},{5,1},{8,12},{9,5},{12,14},{13,9},{14,10},{15,13... | collective-permute-start | bytes 393224 | tf_op jit(solution)/shard_map/ppermute | solution.py:41
  11.1 0.0 collective-permute-done.6.refs_3_
  11.1 0.3 collective-permute-start.11
  11.5 0.2 collective-permute-done.8.refs_2_
  11.7 1.0 %collective-permute-start.12 = (bf16[16,4096]{1,0:T(8,128)(2,1)S(1)}, bf16[16,4096]{1,0:T(8,128)(2,1)S(1)}, u32[]{:S(2)}, u32[]{:S(2)}) collective-permute-start(bf16[16,4096]{1,0:T(8,128)(2,1)S(1)} %collective-permute-done.8.refs_2_), channel_id=1, source_target_pairs={{0,4},{1,3},{4,8},{5,1},{8,12},{9,5},{12,14},{13,9},{14,10},{15,13... | collective-permute-start | bytes 393224 | tf_op jit(solution)/shard_map/ppermute | solution.py:41
  12.7 0.3 collective-permute-done.1.refs_3_
  13.0 1.1 %collective-permute-start.2 = (bf16[16,4096]{1,0:T(8,128)(2,1)S(1)}, bf16[16,4096]{1,0:T(8,128)(2,1)S(1)}, u32[]{:S(2)}, u32[]{:S(2)}) collective-permute-start(bf16[16,4096]{1,0:T(8,128)(2,1)S(1)} %collective-permute-done.1.refs_3_), channel_id=1, source_target_pairs={{0,4},{1,3},{4,8},{5,1},{8,12},{9,5},{12,14},{13,9},{14,10},{15,13... | collective-permute-start | bytes 393224 | tf_op jit(solution)/shard_map/ppermute | solution.py:41
  14.1 2.6 %collective-permute-start.9 = (bf16[128,4096]{1,0:T(8,128)(2,1)S(1)}, bf16[128,4096]{1,0:T(8,128)(2,1)S(1)}, u32[]{:S(2)}, u32[]{:S(2)}) collective-permute-start(bf16[128,4096]{1,0:T(8,128)(2,1)S(1)} %constant_dynamic-update-slice_fusion), channel_id=1, source_target_pairs={{0,1},{1,0},{2,3},{3,2},{4,5},{5,4},{6,7},{7,6},{8,9},{9,8},{10,11... | collective-permute-start | bytes 3145736 | tf_op jit(solution)/shard_map/ppermute | solution.py:44
  16.7 0.0 collective-permute-done.10.refs_5_
  16.7 0.2 collective-permute-start.14
  16.9 0.0 collective-permute-done.11.refs_6_
  16.9 0.7 %collective-permute-start.15 = (bf16[16,4096]{1,0:T(8,128)(2,1)S(1)}, bf16[16,4096]{1,0:T(8,128)(2,1)S(1)}, u32[]{:S(2)}, u32[]{:S(2)}) collective-permute-start(bf16[16,4096]{1,0:T(8,128)(2,1)S(1)} %collective-permute-done.11.refs_6_), channel_id=1, source_target_pairs={{0,4},{1,3},{4,8},{5,1},{8,12},{9,5},{12,14},{13,9},{14,10},{15,13... | collective-permute-start | bytes 393224 | tf_op jit(solution)/shard_map/ppermute | solution.py:41
  17.6 0.0 collective-permute-done.12.refs_5_
  17.6 1.1 %collective-permute-done.2.refs_6_ = bf16[16,4096]{1,0:T(8,128)(2,1)S(1)} collective-permute-done((bf16[16,4096]{1,0:T(8,128)(2,1)S(1)}, bf16[16,4096]{1,0:T(8,128)(2,1)S(1)}, u32[]{:S(2)}, u32[]{:S(2)}) %collective-permute-start.2) | collective-permute-done | bytes 131104 | tf_op jit(solution)/shard_map/ppermute | solution.py:41
  18.7 2.4 %collective-permute-start.13 = (bf16[64,4096]{1,0:T(8,128)(2,1)S(1)}, bf16[64,4096]{1,0:T(8,128)(2,1)S(1)}, u32[]{:S(2)}, u32[]{:S(2)}) collective-permute-start(bf16[64,4096]{1,0:T(8,128)(2,1)S(1)} %pad_maximum_fusion), channel_id=1, source_target_pairs={{0,1},{1,0},{2,3},{3,2},{4,5},{5,4},{6,7},{7,6},{8,9},{9,8},{10,11... | collective-permute-start | bytes 1572872 | tf_op jit(solution)/shard_map/ppermute | solution.py:44
  21.1 0.5 %collective-permute-start.18 = (bf16[16,4096]{1,0:T(8,128)(2,1)S(1)}, bf16[16,4096]{1,0:T(8,128)(2,1)S(1)}, u32[]{:S(2)}, u32[]{:S(2)}) collective-permute-start(bf16[16,4096]{1,0:T(8,128)(2,1)S(1)} %collective-permute-done.2.refs_6_), channel_id=1, source_target_pairs={{0,4},{1,3},{4,8},{5,1},{8,12},{9,5},{12,14},{13,9},{14,10},{15,13... | collective-permute-start | bytes 393224 | tf_op jit(solution)/shard_map/ppermute | solution.py:41
  21.5 0.0 collective-permute-done.14.refs_8_
  21.5 1.2 %collective-permute-start.17 = (bf16[16,4096]{1,0:T(8,128)(2,1)S(1)}, bf16[16,4096]{1,0:T(8,128)(2,1)S(1)}, u32[]{:S(2)}, u32[]{:S(2)}) collective-permute-start(bf16[16,4096]{1,0:T(8,128)(2,1)S(1)} %collective-permute-done.12.refs_5_), channel_id=1, source_target_pairs={{0,4},{1,3},{4,8},{5,1},{8,12},{9,5},{12,14},{13,9},{14,10},{15,13... | collective-permute-start | bytes 393224 | tf_op jit(solution)/shard_map/ppermute | solution.py:41
  22.8 0.0 collective-permute-done.15.refs_9_
  22.8 1.2 %collective-permute-start.16 = (bf16[32,4096]{1,0:T(8,128)(2,1)S(1)}, bf16[32,4096]{1,0:T(8,128)(2,1)S(1)}, u32[]{:S(2)}, u32[]{:S(2)}) collective-permute-start(bf16[32,4096]{1,0:T(8,128)(2,1)S(1)} %pad_maximum_fusion.1), channel_id=1, source_target_pairs={{0,1},{1,0},{2,3},{3,2},{4,5},{5,4},{6,7},{7,6},{8,9},{9,8},{10,11... | collective-permute-start | bytes 786440 | tf_op jit(solution)/shard_map/ppermute | solution.py:44
  24.0 1.2 %collective-permute-done.18.refs_9_ = bf16[16,4096]{1,0:T(8,128)(2,1)S(1)} collective-permute-done((bf16[16,4096]{1,0:T(8,128)(2,1)S(1)}, bf16[16,4096]{1,0:T(8,128)(2,1)S(1)}, u32[]{:S(2)}, u32[]{:S(2)}) %collective-permute-start.18) | collective-permute-done | bytes 131104 | tf_op jit(solution)/shard_map/ppermute | solution.py:41
  25.2 1.4 %collective-permute-done.17.refs_8_ = bf16[16,4096]{1,0:T(8,128)(2,1)S(1)} collective-permute-done((bf16[16,4096]{1,0:T(8,128)(2,1)S(1)}, bf16[16,4096]{1,0:T(8,128)(2,1)S(1)}, u32[]{:S(2)}, u32[]{:S(2)}) %collective-permute-start.17) | collective-permute-done | bytes 131104 | tf_op jit(solution)/shard_map/ppermute | solution.py:41
  26.6 1.0 %collective-permute-start.19 = (bf16[32,4096]{1,0:T(8,128)(2,1)S(1)}, bf16[32,4096]{1,0:T(8,128)(2,1)S(1)}, u32[]{:S(2)}, u32[]{:S(2)}) collective-permute-start(bf16[32,4096]{1,0:T(8,128)(2,1)S(1)} %pad_maximum_fusion.2), channel_id=1, source_target_pairs={{0,1},{1,0},{2,3},{3,2},{4,5},{5,4},{6,7},{7,6},{8,9},{9,8},{10,11... | collective-permute-start | bytes 786440 | tf_op jit(solution)/shard_map/ppermute | solution.py:44
  27.6 0.0 collective-permute-done.16.refs_10_
  27.6 0.0 collective-permute-done.13.refs_7_
  27.6 0.0 collective-permute-done.9.refs_4_
  27.6 0.0 copy-done
  27.6 2.2 %shard_map.38 = (bf16[512,4096]{1,0:T(8,128)(2,1)S(1)}, f32[1,4096]{1,0:T(1,128)S(1)}, f32[512,1]{1,0:T(8,128)S(1)}) custom-call(bf16[512,4096]{1,0:T(8,128)(2,1)S(1)} %copy-done, f32[1,4096]{1,0:T(1,128)S(1)} %shard_map.37.first_total, bf16[16,4096]{1,0:T(8,128)(2,1)S(1)} %collective-permute-done.3.rows.refs_0_, ...), custom_call_target="tpu_custom_call" | custom-call | flops 1073741824 | bytes 6291456 | tf_op jit(solution)/shard_map/pallas_call | solution.py:175
  29.9 0.0 collective-permute-done.19.refs_10_
  29.9 2.6 %shard_map.39 = f32[1,512]{1,0:T(1,128)} custom-call(f32[512,1]{1,0:T(8,128)S(1)} %get-tuple-element.11.ref_log, bf16[512,4096]{1,0:T(8,128)(2,1)S(1)} %get-tuple-element.12.probes, f32[1,4096]{1,0:T(1,128)S(1)} %get-tuple-element.13.mean, bf16[16,4096]{1,0:T(8,128)(2,1)S(1)} %collective-permute-done.7.refs_0_, ...), custom_call_target="tpu_custom_call" | custom-call | flops 1073741824 | bytes 6291456 | tf_op jit(solution)/shard_map/pallas_call | solution.py:175
  (11 shorter events, 0.1 us)
Async XLA Ops:
  0.0 27.6 %copy-start = (bf16[512,4096]{1,0:T(8,128)(2,1)S(1)}, bf16[512,4096]{1,0:T(8,128)(2,1)}, u32[]{:S(2)}) copy-start(bf16[512,4096]{1,0:T(8,128)(2,1)} %queries.1) | copy-start | bytes 12582916
  0.0 4.0 %collective-permute-start.3 = (bf16[16,4096]{1,0:T(8,128)(2,1)}, bf16[16,4096]{1,0:T(8,128)(2,1)S(1)}, u32[]{:S(2)}, u32[]{:S(2)}) collective-permute-start(bf16[16,4096]{1,0:T(8,128)(2,1)} %param.5), channel_id=1, source_target_pairs={{0,1},{1,0},{2,3},{3,2},{4,5},{5,4},{6,7},{7,6},{8,9},{9,8},{10,11... | collective-permute-start | bytes 393224 | tf_op jit(solution)/shard_map/ppermute | solution.py:44
  0.1 5.6 %collective-permute-start.4 = (bf16[16,4096]{1,0:T(8,128)(2,1)}, bf16[16,4096]{1,0:T(8,128)(2,1)S(1)}, u32[]{:S(2)}, u32[]{:S(2)}) collective-permute-start(bf16[16,4096]{1,0:T(8,128)(2,1)} %param.5), channel_id=1, source_target_pairs={{0,4},{1,3},{4,8},{5,1},{8,12},{9,5},{12,14},{13,9},{14,10},{15,13... | collective-permute-start | bytes 393224 | tf_op jit(solution)/shard_map/ppermute | solution.py:41
  2.7 4.4 %collective-permute-start.7 = (bf16[16,4096]{1,0:T(8,128)(2,1)}, bf16[16,4096]{1,0:T(8,128)(2,1)S(1)}, u32[]{:S(2)}, u32[]{:S(2)}) collective-permute-start(bf16[16,4096]{1,0:T(8,128)(2,1)} %param.4), channel_id=1, source_target_pairs={{0,1},{1,0},{2,3},{3,2},{4,5},{5,4},{6,7},{7,6},{8,9},{9,8},{10,11... | collective-permute-start | bytes 393224 | tf_op jit(solution)/shard_map/ppermute | solution.py:44
  3.1 5.4 %collective-permute-start = (bf16[16,4096]{1,0:T(8,128)(2,1)}, bf16[16,4096]{1,0:T(8,128)(2,1)S(1)}, u32[]{:S(2)}, u32[]{:S(2)}) collective-permute-start(bf16[16,4096]{1,0:T(8,128)(2,1)} %param.4), channel_id=1, source_target_pairs={{0,4},{1,3},{4,8},{5,1},{8,12},{9,5},{12,14},{13,9},{14,10},{15,13... | collective-permute-start | bytes 393224 | tf_op jit(solution)/shard_map/ppermute | solution.py:41
  4.1 5.7 %collective-permute-start.5 = (bf16[16,4096]{1,0:T(8,128)(2,1)S(1)}, bf16[16,4096]{1,0:T(8,128)(2,1)S(1)}, u32[]{:S(2)}, u32[]{:S(2)}) collective-permute-start(bf16[16,4096]{1,0:T(8,128)(2,1)S(1)} %collective-permute-done.3.rows.refs_0_), channel_id=1, source_target_pairs={{0,4},{1,3},{4,8},{5,1},{8,12},{9,5},{12,14},{13,9},{14,10},{15,13... | collective-permute-start | bytes 393224 | tf_op jit(solution)/shard_map/ppermute | solution.py:41
  5.7 5.5 %collective-permute-start.6 = (bf16[16,4096]{1,0:T(8,128)(2,1)S(1)}, bf16[16,4096]{1,0:T(8,128)(2,1)S(1)}, u32[]{:S(2)}, u32[]{:S(2)}) collective-permute-start(bf16[16,4096]{1,0:T(8,128)(2,1)S(1)} %collective-permute-done.4.refs_1_), channel_id=1, source_target_pairs={{0,4},{1,3},{4,8},{5,1},{8,12},{9,5},{12,14},{13,9},{14,10},{15,13... | collective-permute-start | bytes 393224 | tf_op jit(solution)/shard_map/ppermute | solution.py:41
  7.2 4.5 %collective-permute-start.8 = (bf16[16,4096]{1,0:T(8,128)(2,1)S(1)}, bf16[16,4096]{1,0:T(8,128)(2,1)S(1)}, u32[]{:S(2)}, u32[]{:S(2)}) collective-permute-start(bf16[16,4096]{1,0:T(8,128)(2,1)S(1)} %collective-permute-done.7.refs_0_), channel_id=1, source_target_pairs={{0,4},{1,3},{4,8},{5,1},{8,12},{9,5},{12,14},{13,9},{14,10},{15,13... | collective-permute-start | bytes 393224 | tf_op jit(solution)/shard_map/ppermute | solution.py:41
  8.5 4.5 %collective-permute-start.1 = (bf16[16,4096]{1,0:T(8,128)(2,1)S(1)}, bf16[16,4096]{1,0:T(8,128)(2,1)S(1)}, u32[]{:S(2)}, u32[]{:S(2)}) collective-permute-start(bf16[16,4096]{1,0:T(8,128)(2,1)S(1)} %collective-permute-done.refs_1_), channel_id=1, source_target_pairs={{0,4},{1,3},{4,8},{5,1},{8,12},{9,5},{12,14},{13,9},{14,10},{15,13... | collective-permute-start | bytes 393224 | tf_op jit(solution)/shard_map/ppermute | solution.py:41
  9.8 6.9 %collective-permute-start.10 = (bf16[16,4096]{1,0:T(8,128)(2,1)S(1)}, bf16[16,4096]{1,0:T(8,128)(2,1)S(1)}, u32[]{:S(2)}, u32[]{:S(2)}) collective-permute-start(bf16[16,4096]{1,0:T(8,128)(2,1)S(1)} %collective-permute-done.5.refs_2_), channel_id=1, source_target_pairs={{0,4},{1,3},{4,8},{5,1},{8,12},{9,5},{12,14},{13,9},{14,10},{15,13... | collective-permute-start | bytes 393224 | tf_op jit(solution)/shard_map/ppermute | solution.py:41
  11.1 5.8 %collective-permute-start.11 = (bf16[16,4096]{1,0:T(8,128)(2,1)S(1)}, bf16[16,4096]{1,0:T(8,128)(2,1)S(1)}, u32[]{:S(2)}, u32[]{:S(2)}) collective-permute-start(bf16[16,4096]{1,0:T(8,128)(2,1)S(1)} %collective-permute-done.6.refs_3_), channel_id=1, source_target_pairs={{0,4},{1,3},{4,8},{5,1},{8,12},{9,5},{12,14},{13,9},{14,10},{15,13... | collective-permute-start | bytes 393224 | tf_op jit(solution)/shard_map/ppermute | solution.py:41
  11.7 5.9 %collective-permute-start.12 = (bf16[16,4096]{1,0:T(8,128)(2,1)S(1)}, bf16[16,4096]{1,0:T(8,128)(2,1)S(1)}, u32[]{:S(2)}, u32[]{:S(2)}) collective-permute-start(bf16[16,4096]{1,0:T(8,128)(2,1)S(1)} %collective-permute-done.8.refs_2_), channel_id=1, source_target_pairs={{0,4},{1,3},{4,8},{5,1},{8,12},{9,5},{12,14},{13,9},{14,10},{15,13... | collective-permute-start | bytes 393224 | tf_op jit(solution)/shard_map/ppermute | solution.py:41
  13.0 5.7 %collective-permute-start.2 = (bf16[16,4096]{1,0:T(8,128)(2,1)S(1)}, bf16[16,4096]{1,0:T(8,128)(2,1)S(1)}, u32[]{:S(2)}, u32[]{:S(2)}) collective-permute-start(bf16[16,4096]{1,0:T(8,128)(2,1)S(1)} %collective-permute-done.1.refs_3_), channel_id=1, source_target_pairs={{0,4},{1,3},{4,8},{5,1},{8,12},{9,5},{12,14},{13,9},{14,10},{15,13... | collective-permute-start | bytes 393224 | tf_op jit(solution)/shard_map/ppermute | solution.py:41
  14.1 13.5 %collective-permute-start.9 = (bf16[128,4096]{1,0:T(8,128)(2,1)S(1)}, bf16[128,4096]{1,0:T(8,128)(2,1)S(1)}, u32[]{:S(2)}, u32[]{:S(2)}) collective-permute-start(bf16[128,4096]{1,0:T(8,128)(2,1)S(1)} %constant_dynamic-update-slice_fusion), channel_id=1, source_target_pairs={{0,1},{1,0},{2,3},{3,2},{4,5},{5,4},{6,7},{7,6},{8,9},{9,8},{10,11... | collective-permute-start | bytes 3145736 | tf_op jit(solution)/shard_map/ppermute | solution.py:44
  16.7 4.8 %collective-permute-start.14 = (bf16[16,4096]{1,0:T(8,128)(2,1)S(1)}, bf16[16,4096]{1,0:T(8,128)(2,1)S(1)}, u32[]{:S(2)}, u32[]{:S(2)}) collective-permute-start(bf16[16,4096]{1,0:T(8,128)(2,1)S(1)} %collective-permute-done.10.refs_5_), channel_id=1, source_target_pairs={{0,4},{1,3},{4,8},{5,1},{8,12},{9,5},{12,14},{13,9},{14,10},{15,13... | collective-permute-start | bytes 393224 | tf_op jit(solution)/shard_map/ppermute | solution.py:41
  16.9 5.9 %collective-permute-start.15 = (bf16[16,4096]{1,0:T(8,128)(2,1)S(1)}, bf16[16,4096]{1,0:T(8,128)(2,1)S(1)}, u32[]{:S(2)}, u32[]{:S(2)}) collective-permute-start(bf16[16,4096]{1,0:T(8,128)(2,1)S(1)} %collective-permute-done.11.refs_6_), channel_id=1, source_target_pairs={{0,4},{1,3},{4,8},{5,1},{8,12},{9,5},{12,14},{13,9},{14,10},{15,13... | collective-permute-start | bytes 393224 | tf_op jit(solution)/shard_map/ppermute | solution.py:41
  18.7 8.9 %collective-permute-start.13 = (bf16[64,4096]{1,0:T(8,128)(2,1)S(1)}, bf16[64,4096]{1,0:T(8,128)(2,1)S(1)}, u32[]{:S(2)}, u32[]{:S(2)}) collective-permute-start(bf16[64,4096]{1,0:T(8,128)(2,1)S(1)} %pad_maximum_fusion), channel_id=1, source_target_pairs={{0,1},{1,0},{2,3},{3,2},{4,5},{5,4},{6,7},{7,6},{8,9},{9,8},{10,11... | collective-permute-start | bytes 1572872 | tf_op jit(solution)/shard_map/ppermute | solution.py:44
  21.1 4.1 %collective-permute-start.18 = (bf16[16,4096]{1,0:T(8,128)(2,1)S(1)}, bf16[16,4096]{1,0:T(8,128)(2,1)S(1)}, u32[]{:S(2)}, u32[]{:S(2)}) collective-permute-start(bf16[16,4096]{1,0:T(8,128)(2,1)S(1)} %collective-permute-done.2.refs_6_), channel_id=1, source_target_pairs={{0,4},{1,3},{4,8},{5,1},{8,12},{9,5},{12,14},{13,9},{14,10},{15,13... | collective-permute-start | bytes 393224 | tf_op jit(solution)/shard_map/ppermute | solution.py:41
  21.5 5.1 %collective-permute-start.17 = (bf16[16,4096]{1,0:T(8,128)(2,1)S(1)}, bf16[16,4096]{1,0:T(8,128)(2,1)S(1)}, u32[]{:S(2)}, u32[]{:S(2)}) collective-permute-start(bf16[16,4096]{1,0:T(8,128)(2,1)S(1)} %collective-permute-done.12.refs_5_), channel_id=1, source_target_pairs={{0,4},{1,3},{4,8},{5,1},{8,12},{9,5},{12,14},{13,9},{14,10},{15,13... | collective-permute-start | bytes 393224 | tf_op jit(solution)/shard_map/ppermute | solution.py:41
  22.8 4.8 %collective-permute-start.16 = (bf16[32,4096]{1,0:T(8,128)(2,1)S(1)}, bf16[32,4096]{1,0:T(8,128)(2,1)S(1)}, u32[]{:S(2)}, u32[]{:S(2)}) collective-permute-start(bf16[32,4096]{1,0:T(8,128)(2,1)S(1)} %pad_maximum_fusion.1), channel_id=1, source_target_pairs={{0,1},{1,0},{2,3},{3,2},{4,5},{5,4},{6,7},{7,6},{8,9},{9,8},{10,11... | collective-permute-start | bytes 786440 | tf_op jit(solution)/shard_map/ppermute | solution.py:44
  26.6 3.2 %collective-permute-start.19 = (bf16[32,4096]{1,0:T(8,128)(2,1)S(1)}, bf16[32,4096]{1,0:T(8,128)(2,1)S(1)}, u32[]{:S(2)}, u32[]{:S(2)}) collective-permute-start(bf16[32,4096]{1,0:T(8,128)(2,1)S(1)} %pad_maximum_fusion.2), channel_id=1, source_target_pairs={{0,1},{1,0},{2,3},{3,2},{4,5},{5,4},{6,7},{7,6},{8,9},{9,8},{10,11... | collective-permute-start | bytes 786440 | tf_op jit(solution)/shard_map/ppermute | solution.py:44

commit v12 on v9

--- a/solution.py
+++ b/solution.py
@@ -11,6 +11,7 @@
 LANES = 128
 CHUNK = 1024
 GROUP = 32
+BLOCK = 256
 LIMIT = 40 * 2**20
 
 
@@ -93,28 +94,47 @@
     return (rows.astype(jnp.float32) - mean).astype(jnp.bfloat16)
 
 
-def center_panel_chunk(cols, mean, groups, centered, squares, first):
-    for ref, rows, here in groups:
-        part = center(ref[rows, cols], mean)
-        centered[here, cols] = part
-        wide = jnp.square(part.astype(jnp.float32))
-        total = wide[:, :LANES]
-        for lane in range(LANES, wide.shape[1], LANES):
-            total += wide[:, lane : lane + LANES]
-        squares[here, :] = total if first else squares[here, :] + total
-
-
-def add_products(cols, probes, centered, scores, first):
+def center_group(group, cols, mean, centered, squares, first):
+    ref, rows, here = group
+    part = center(ref[rows, cols], mean[:, cols])
+    centered[here, cols] = part
+    wide = jnp.square(part.astype(jnp.float32))
+    total = wide[:, :LANES]
+    for lane in range(LANES, wide.shape[1], LANES):
+        total += wide[:, lane : lane + LANES]
+    squares[here, :] = total if first else squares[here, :] + total
+
+
+def add_products(cols, queries, probes, centered, scores, first):
     products = lax.dot_general(
-        centered[:, cols], probes[:, cols], (((1,), (1,)), ((), ())),
+        centered[:, cols], probes[queries, cols], (((1,), (1,)), ((), ())),
         preferred_element_type=jnp.float32,
     )
-    scores[...] = products if first else scores[...] + products
-
-
-def log_sum(squares, scores):
+    scores[:, queries] = products if first else scores[:, queries] + products
+
+
+def interleave(features, prepare, probes, centered, scores):
+    waiting = []
+    for start in range(0, features, CHUNK):
+        cols, first = slice(start, start + CHUNK), start == 0
+        work = prepare(cols, first)
+        share = -(-len(work) // max(len(waiting), 1))
+        for i in range(0, len(work), share):
+            if waiting:
+                waiting.pop(0)()
+            for step in work[i : i + share]:
+                step()
+        waiting += [
+            functools.partial(add_products, cols, queries, probes, centered, scores, first)
+            for queries in row_groups(probes.shape[0], BLOCK)
+        ]
+    for step in waiting:
+        step()
+
+
+def log_sum(squares, scores, queries):
     half = 0.5 * jnp.sum(squares[...], axis=1, keepdims=True)
-    x = (scores[...] - half) / TEMP
+    x = (scores[:, queries] - half) / TEMP
     top = jnp.max(x, axis=0, keepdims=True)
     return jnp.log(jnp.sum(jnp.exp(x - top), axis=0, keepdims=True)) + top
 
@@ -141,29 +161,43 @@
     panel, (probes, mean, ref_log, centered, squares, scores) = refs[: len(spans)], refs[len(spans) :]
     groups = panel_groups(panel, spans)
     count, features = centered.shape
-    for start in range(0, features, CHUNK):
-        cols = slice(start, start + CHUNK)
+
+    def take_mean(cols):
         total = first_total[:, cols]
         for ref, rows, _ in groups:
             if ref is not panel[0]:
                 total += jnp.sum(ref[rows, cols].astype(jnp.float32), axis=0, keepdims=True)
-        here = total / count
-        mean[:, cols] = here
-        center_panel_chunk(cols, here, groups, centered, squares, start == 0)
+        mean[:, cols] = total / count
+
+    def center_queries(rows, cols):
+        probes[rows, cols] = center(queries[rows, cols], mean[:, cols])
+
+    def prepare(cols, first):
+        work = [functools.partial(take_mean, cols)]
+        for group in groups:
+            work.append(functools.partial(center_group, group, cols, mean, centered, squares, first))
         for rows in row_groups(probes.shape[0], GROUP):
-            probes[rows, cols] = center(queries[rows, cols], here)
-        add_products(cols, probes, centered, scores, start == 0)
-    ref_log[...] = log_sum(squares, scores)
+            work.append(functools.partial(center_queries, rows, cols))
+        return work
+
+    interleave(features, prepare, probes, centered, scores)
+    for block in row_groups(probes.shape[0], BLOCK):
+        ref_log[:, block] = log_sum(squares, scores, block)
 
 
 def gen_kernel(spans, ref_log, probes, mean, *refs):
     panel, (proof, centered, squares, scores) = refs[: len(spans)], refs[len(spans) :]
     groups = panel_groups(panel, spans)
-    for start in range(0, centered.shape[1], CHUNK):
-        cols = slice(start, start + CHUNK)
-        center_panel_chunk(cols, mean[:, cols], groups, centered, squares, start == 0)
-        add_products(cols, probes, centered, scores, start == 0)
-    proof[...] = log_sum(squares, scores) - ref_log[...]
+
+    def prepare(cols, first):
+        return [
+            functools.partial(center_group, group, cols, mean, centered, squares, first)
+            for group in groups
+        ]
+
+    interleave(centered.shape[1], prepare, probes, centered, scores)
+    for block in row_groups(probes.shape[0], BLOCK):
+        proof[:, block] = log_sum(squares, scores, block) - ref_log[:, block]
 
 
 def call(kernel, before, pieces, count, out_shape):

time: 32.1 us -> 32.2 us (level)
  no operation moved by 1% of the time
where the time goes in v12:
time: 32.2 us; the launch traced here: 32 us
  starting transfers between devices  22.8 us (71%)
  waiting for transfers between devices  4.55 us (14%)
  Pallas kernels  4.43 us (14%)
    ppermute x14, starting transfers between devices, hop(): return lax.ppermute(block, 'samp', ring)  15.2 us
    ppermute x6, starting transfers between devices, hand_over(): return lax.ppermute(block, 'samp', twins)  7.58 us
    ppermute x14, waiting for transfers between devices, hop(): return lax.ppermute(block, 'samp', ring)  4.53 us
    pallas_call x2, Pallas kernels, call(): pl.pallas_call(functools.partial(kernel, spans), out_shape=out_shape, in_...  4.37 us
  transfers between devices with their start and end apart: 20, of which 6 were waited for; matrix products, arithmetic and copies ran while one was open for 0% of the time, Pallas kernels for 7%

profile of v12, /device:TPU:1, one launch (start us, length us, event | category | flops | bytes accessed | tf_op | source)
XLA Modules:
  0.0 32.0 jit_solution(11109352607158404153)
XLA Ops:
  0.0 0.0 copy-start
  0.0 0.1 collective-permute-start.3
  0.1 2.7 %collective-permute-start.4 = (bf16[16,4096]{1,0:T(8,128)(2,1)}, bf16[16,4096]{1,0:T(8,128)(2,1)S(1)}, u32[]{:S(2)}, u32[]{:S(2)}) collective-permute-start(bf16[16,4096]{1,0:T(8,128)(2,1)} %param.5), channel_id=1, source_target_pairs={{0,4},{1,3},{4,8},{5,1},{8,12},{9,5},{12,14},{13,9},{14,10},{15,13... | collective-permute-start | bytes 393224 | tf_op jit(solution)/shard_map/ppermute | solution.py:42
  2.7 0.4 %collective-permute-start.7 = (bf16[16,4096]{1,0:T(8,128)(2,1)}, bf16[16,4096]{1,0:T(8,128)(2,1)S(1)}, u32[]{:S(2)}, u32[]{:S(2)}) collective-permute-start(bf16[16,4096]{1,0:T(8,128)(2,1)} %param.4), channel_id=1, source_target_pairs={{0,1},{1,0},{2,3},{3,2},{4,5},{5,4},{6,7},{7,6},{8,9},{9,8},{10,11... | collective-permute-start | bytes 393224 | tf_op jit(solution)/shard_map/ppermute | solution.py:45
  3.1 0.9 %collective-permute-start = (bf16[16,4096]{1,0:T(8,128)(2,1)}, bf16[16,4096]{1,0:T(8,128)(2,1)S(1)}, u32[]{:S(2)}, u32[]{:S(2)}) collective-permute-start(bf16[16,4096]{1,0:T(8,128)(2,1)} %param.4), channel_id=1, source_target_pairs={{0,4},{1,3},{4,8},{5,1},{8,12},{9,5},{12,14},{13,9},{14,10},{15,13... | collective-permute-start | bytes 393224 | tf_op jit(solution)/shard_map/ppermute | solution.py:42
  4.0 0.0 collective-permute-done.3.rows.refs_0_
  4.1 1.3 %collective-permute-start.5 = (bf16[16,4096]{1,0:T(8,128)(2,1)S(1)}, bf16[16,4096]{1,0:T(8,128)(2,1)S(1)}, u32[]{:S(2)}, u32[]{:S(2)}) collective-permute-start(bf16[16,4096]{1,0:T(8,128)(2,1)S(1)} %collective-permute-done.3.rows.refs_0_), channel_id=1, source_target_pairs={{0,4},{1,3},{4,8},{5,1},{8,12},{9,5},{12,14},{13,9},{14,10},{15,13... | collective-permute-start | bytes 393224 | tf_op jit(solution)/shard_map/ppermute | solution.py:42
  5.4 0.3 collective-permute-done.4.refs_1_
  5.7 1.4 %collective-permute-start.6 = (bf16[16,4096]{1,0:T(8,128)(2,1)S(1)}, bf16[16,4096]{1,0:T(8,128)(2,1)S(1)}, u32[]{:S(2)}, u32[]{:S(2)}) collective-permute-start(bf16[16,4096]{1,0:T(8,128)(2,1)S(1)} %collective-permute-done.4.refs_1_), channel_id=1, source_target_pairs={{0,4},{1,3},{4,8},{5,1},{8,12},{9,5},{12,14},{13,9},{14,10},{15,13... | collective-permute-start | bytes 393224 | tf_op jit(solution)/shard_map/ppermute | solution.py:42
  7.1 0.1 shard_map.37.first_total
  7.1 0.0 collective-permute-done.7.refs_0_
  7.2 1.3 %collective-permute-start.8 = (bf16[16,4096]{1,0:T(8,128)(2,1)S(1)}, bf16[16,4096]{1,0:T(8,128)(2,1)S(1)}, u32[]{:S(2)}, u32[]{:S(2)}) collective-permute-start(bf16[16,4096]{1,0:T(8,128)(2,1)S(1)} %collective-permute-done.7.refs_0_), channel_id=1, source_target_pairs={{0,4},{1,3},{4,8},{5,1},{8,12},{9,5},{12,14},{13,9},{14,10},{15,13... | collective-permute-start | bytes 393224 | tf_op jit(solution)/shard_map/ppermute | solution.py:42
  8.5 0.0 collective-permute-done.refs_1_
  8.5 1.3 %collective-permute-start.1 = (bf16[16,4096]{1,0:T(8,128)(2,1)S(1)}, bf16[16,4096]{1,0:T(8,128)(2,1)S(1)}, u32[]{:S(2)}, u32[]{:S(2)}) collective-permute-start(bf16[16,4096]{1,0:T(8,128)(2,1)S(1)} %collective-permute-done.refs_1_), channel_id=1, source_target_pairs={{0,4},{1,3},{4,8},{5,1},{8,12},{9,5},{12,14},{13,9},{14,10},{15,13... | collective-permute-start | bytes 393224 | tf_op jit(solution)/shard_map/ppermute | solution.py:42
  9.8 0.0 collective-permute-done.5.refs_2_
  9.8 1.3 %collective-permute-start.10 = (bf16[16,4096]{1,0:T(8,128)(2,1)S(1)}, bf16[16,4096]{1,0:T(8,128)(2,1)S(1)}, u32[]{:S(2)}, u32[]{:S(2)}) collective-permute-start(bf16[16,4096]{1,0:T(8,128)(2,1)S(1)} %collective-permute-done.5.refs_2_), channel_id=1, source_target_pairs={{0,4},{1,3},{4,8},{5,1},{8,12},{9,5},{12,14},{13,9},{14,10},{15,13... | collective-permute-start | bytes 393224 | tf_op jit(solution)/shard_map/ppermute | solution.py:42
  11.1 0.0 collective-permute-done.6.refs_3_
  11.1 0.3 collective-permute-start.11
  11.5 0.2 collective-permute-done.8.refs_2_
  11.7 1.0 %collective-permute-start.12 = (bf16[16,4096]{1,0:T(8,128)(2,1)S(1)}, bf16[16,4096]{1,0:T(8,128)(2,1)S(1)}, u32[]{:S(2)}, u32[]{:S(2)}) collective-permute-start(bf16[16,4096]{1,0:T(8,128)(2,1)S(1)} %collective-permute-done.8.refs_2_), channel_id=1, source_target_pairs={{0,4},{1,3},{4,8},{5,1},{8,12},{9,5},{12,14},{13,9},{14,10},{15,13... | collective-permute-start | bytes 393224 | tf_op jit(solution)/shard_map/ppermute | solution.py:42
  12.7 0.3 collective-permute-done.1.refs_3_
  13.0 1.1 %collective-permute-start.2 = (bf16[16,4096]{1,0:T(8,128)(2,1)S(1)}, bf16[16,4096]{1,0:T(8,128)(2,1)S(1)}, u32[]{:S(2)}, u32[]{:S(2)}) collective-permute-start(bf16[16,4096]{1,0:T(8,128)(2,1)S(1)} %collective-permute-done.1.refs_3_), channel_id=1, source_target_pairs={{0,4},{1,3},{4,8},{5,1},{8,12},{9,5},{12,14},{13,9},{14,10},{15,13... | collective-permute-start | bytes 393224 | tf_op jit(solution)/shard_map/ppermute | solution.py:42
  14.1 2.6 %collective-permute-start.9 = (bf16[128,4096]{1,0:T(8,128)(2,1)S(1)}, bf16[128,4096]{1,0:T(8,128)(2,1)S(1)}, u32[]{:S(2)}, u32[]{:S(2)}) collective-permute-start(bf16[128,4096]{1,0:T(8,128)(2,1)S(1)} %constant_dynamic-update-slice_fusion), channel_id=1, source_target_pairs={{0,1},{1,0},{2,3},{3,2},{4,5},{5,4},{6,7},{7,6},{8,9},{9,8},{10,11... | collective-permute-start | bytes 3145736 | tf_op jit(solution)/shard_map/ppermute | solution.py:45
  16.7 0.0 collective-permute-done.10.refs_5_
  16.7 0.2 collective-permute-start.14
  16.9 0.0 collective-permute-done.11.refs_6_
  16.9 0.7 %collective-permute-start.15 = (bf16[16,4096]{1,0:T(8,128)(2,1)S(1)}, bf16[16,4096]{1,0:T(8,128)(2,1)S(1)}, u32[]{:S(2)}, u32[]{:S(2)}) collective-permute-start(bf16[16,4096]{1,0:T(8,128)(2,1)S(1)} %collective-permute-done.11.refs_6_), channel_id=1, source_target_pairs={{0,4},{1,3},{4,8},{5,1},{8,12},{9,5},{12,14},{13,9},{14,10},{15,13... | collective-permute-start | bytes 393224 | tf_op jit(solution)/shard_map/ppermute | solution.py:42
  17.6 0.0 collective-permute-done.12.refs_5_
  17.6 1.1 %collective-permute-done.2.refs_6_ = bf16[16,4096]{1,0:T(8,128)(2,1)S(1)} collective-permute-done((bf16[16,4096]{1,0:T(8,128)(2,1)S(1)}, bf16[16,4096]{1,0:T(8,128)(2,1)S(1)}, u32[]{:S(2)}, u32[]{:S(2)}) %collective-permute-start.2) | collective-permute-done | bytes 131104 | tf_op jit(solution)/shard_map/ppermute | solution.py:42
  18.7 2.4 %collective-permute-start.13 = (bf16[64,4096]{1,0:T(8,128)(2,1)S(1)}, bf16[64,4096]{1,0:T(8,128)(2,1)S(1)}, u32[]{:S(2)}, u32[]{:S(2)}) collective-permute-start(bf16[64,4096]{1,0:T(8,128)(2,1)S(1)} %pad_maximum_fusion), channel_id=1, source_target_pairs={{0,1},{1,0},{2,3},{3,2},{4,5},{5,4},{6,7},{7,6},{8,9},{9,8},{10,11... | collective-permute-start | bytes 1572872 | tf_op jit(solution)/shard_map/ppermute | solution.py:45
  21.1 0.5 %collective-permute-start.18 = (bf16[16,4096]{1,0:T(8,128)(2,1)S(1)}, bf16[16,4096]{1,0:T(8,128)(2,1)S(1)}, u32[]{:S(2)}, u32[]{:S(2)}) collective-permute-start(bf16[16,4096]{1,0:T(8,128)(2,1)S(1)} %collective-permute-done.2.refs_6_), channel_id=1, source_target_pairs={{0,4},{1,3},{4,8},{5,1},{8,12},{9,5},{12,14},{13,9},{14,10},{15,13... | collective-permute-start | bytes 393224 | tf_op jit(solution)/shard_map/ppermute | solution.py:42
  21.5 0.0 collective-permute-done.14.refs_8_
  21.6 1.2 %collective-permute-start.17 = (bf16[16,4096]{1,0:T(8,128)(2,1)S(1)}, bf16[16,4096]{1,0:T(8,128)(2,1)S(1)}, u32[]{:S(2)}, u32[]{:S(2)}) collective-permute-start(bf16[16,4096]{1,0:T(8,128)(2,1)S(1)} %collective-permute-done.12.refs_5_), channel_id=1, source_target_pairs={{0,4},{1,3},{4,8},{5,1},{8,12},{9,5},{12,14},{13,9},{14,10},{15,13... | collective-permute-start | bytes 393224 | tf_op jit(solution)/shard_map/ppermute | solution.py:42
  22.8 0.0 collective-permute-done.15.refs_9_
  22.8 1.2 %collective-permute-start.16 = (bf16[32,4096]{1,0:T(8,128)(2,1)S(1)}, bf16[32,4096]{1,0:T(8,128)(2,1)S(1)}, u32[]{:S(2)}, u32[]{:S(2)}) collective-permute-start(bf16[32,4096]{1,0:T(8,128)(2,1)S(1)} %pad_maximum_fusion.1), channel_id=1, source_target_pairs={{0,1},{1,0},{2,3},{3,2},{4,5},{5,4},{6,7},{7,6},{8,9},{9,8},{10,11... | collective-permute-start | bytes 786440 | tf_op jit(solution)/shard_map/ppermute | solution.py:45
  24.0 1.2 %collective-permute-done.18.refs_9_ = bf16[16,4096]{1,0:T(8,128)(2,1)S(1)} collective-permute-done((bf16[16,4096]{1,0:T(8,128)(2,1)S(1)}, bf16[16,4096]{1,0:T(8,128)(2,1)S(1)}, u32[]{:S(2)}, u32[]{:S(2)}) %collective-permute-start.18) | collective-permute-done | bytes 131104 | tf_op jit(solution)/shard_map/ppermute | solution.py:42
  25.2 1.4 %collective-permute-done.17.refs_8_ = bf16[16,4096]{1,0:T(8,128)(2,1)S(1)} collective-permute-done((bf16[16,4096]{1,0:T(8,128)(2,1)S(1)}, bf16[16,4096]{1,0:T(8,128)(2,1)S(1)}, u32[]{:S(2)}, u32[]{:S(2)}) %collective-permute-start.17) | collective-permute-done | bytes 131104 | tf_op jit(solution)/shard_map/ppermute | solution.py:42
  26.6 1.0 %collective-permute-start.19 = (bf16[32,4096]{1,0:T(8,128)(2,1)S(1)}, bf16[32,4096]{1,0:T(8,128)(2,1)S(1)}, u32[]{:S(2)}, u32[]{:S(2)}) collective-permute-start(bf16[32,4096]{1,0:T(8,128)(2,1)S(1)} %pad_maximum_fusion.2), channel_id=1, source_target_pairs={{0,1},{1,0},{2,3},{3,2},{4,5},{5,4},{6,7},{7,6},{8,9},{9,8},{10,11... | collective-permute-start | bytes 786440 | tf_op jit(solution)/shard_map/ppermute | solution.py:45
  27.6 0.0 collective-permute-done.16.refs_10_
  27.6 0.0 collective-permute-done.13.refs_7_
  27.6 0.0 collective-permute-done.9.refs_4_
  27.6 0.0 copy-done
  27.6 2.3 %shard_map.38 = (bf16[512,4096]{1,0:T(8,128)(2,1)S(1)}, f32[1,4096]{1,0:T(1,128)S(1)}, f32[1,512]{1,0:T(1,128)S(1)}) custom-call(bf16[512,4096]{1,0:T(8,128)(2,1)S(1)} %copy-done, f32[1,4096]{1,0:T(1,128)S(1)} %shard_map.37.first_total, bf16[16,4096]{1,0:T(8,128)(2,1)S(1)} %collective-permute-done.3.rows.refs_0_, ...), custom_call_target="tpu_custom_call" | custom-call | flops 1073741824 | bytes 6291456 | tf_op jit(solution)/shard_map/pallas_call | solution.py:208
  30.0 0.0 collective-permute-done.19.refs_10_
  30.0 2.1 %shard_map.39 = f32[1,512]{1,0:T(1,128)} custom-call(f32[1,512]{1,0:T(1,128)S(1)} %get-tuple-element.11.ref_log, bf16[512,4096]{1,0:T(8,128)(2,1)S(1)} %get-tuple-element.12.probes, f32[1,4096]{1,0:T(1,128)S(1)} %get-tuple-element.13.mean, bf16[16,4096]{1,0:T(8,128)(2,1)S(1)} %collective-permute-done.7.refs_0_, ...), custom_call_target="tpu_custom_call" | custom-call | flops 1073741824 | bytes 6291456 | tf_op jit(solution)/shard_map/pallas_call | solution.py:208
  (11 shorter events, 0.2 us)
Async XLA Ops:
  0.0 27.6 %copy-start = (bf16[512,4096]{1,0:T(8,128)(2,1)S(1)}, bf16[512,4096]{1,0:T(8,128)(2,1)}, u32[]{:S(2)}) copy-start(bf16[512,4096]{1,0:T(8,128)(2,1)} %queries.1) | copy-start | bytes 12582916
  0.0 4.0 %collective-permute-start.3 = (bf16[16,4096]{1,0:T(8,128)(2,1)}, bf16[16,4096]{1,0:T(8,128)(2,1)S(1)}, u32[]{:S(2)}, u32[]{:S(2)}) collective-permute-start(bf16[16,4096]{1,0:T(8,128)(2,1)} %param.5), channel_id=1, source_target_pairs={{0,1},{1,0},{2,3},{3,2},{4,5},{5,4},{6,7},{7,6},{8,9},{9,8},{10,11... | collective-permute-start | bytes 393224 | tf_op jit(solution)/shard_map/ppermute | solution.py:45
  0.1 5.6 %collective-permute-start.4 = (bf16[16,4096]{1,0:T(8,128)(2,1)}, bf16[16,4096]{1,0:T(8,128)(2,1)S(1)}, u32[]{:S(2)}, u32[]{:S(2)}) collective-permute-start(bf16[16,4096]{1,0:T(8,128)(2,1)} %param.5), channel_id=1, source_target_pairs={{0,4},{1,3},{4,8},{5,1},{8,12},{9,5},{12,14},{13,9},{14,10},{15,13... | collective-permute-start | bytes 393224 | tf_op jit(solution)/shard_map/ppermute | solution.py:42
  2.7 4.4 %collective-permute-start.7 = (bf16[16,4096]{1,0:T(8,128)(2,1)}, bf16[16,4096]{1,0:T(8,128)(2,1)S(1)}, u32[]{:S(2)}, u32[]{:S(2)}) collective-permute-start(bf16[16,4096]{1,0:T(8,128)(2,1)} %param.4), channel_id=1, source_target_pairs={{0,1},{1,0},{2,3},{3,2},{4,5},{5,4},{6,7},{7,6},{8,9},{9,8},{10,11... | collective-permute-start | bytes 393224 | tf_op jit(solution)/shard_map/ppermute | solution.py:45
  3.1 5.4 %collective-permute-start = (bf16[16,4096]{1,0:T(8,128)(2,1)}, bf16[16,4096]{1,0:T(8,128)(2,1)S(1)}, u32[]{:S(2)}, u32[]{:S(2)}) collective-permute-start(bf16[16,4096]{1,0:T(8,128)(2,1)} %param.4), channel_id=1, source_target_pairs={{0,4},{1,3},{4,8},{5,1},{8,12},{9,5},{12,14},{13,9},{14,10},{15,13... | collective-permute-start | bytes 393224 | tf_op jit(solution)/shard_map/ppermute | solution.py:42
  4.1 5.7 %collective-permute-start.5 = (bf16[16,4096]{1,0:T(8,128)(2,1)S(1)}, bf16[16,4096]{1,0:T(8,128)(2,1)S(1)}, u32[]{:S(2)}, u32[]{:S(2)}) collective-permute-start(bf16[16,4096]{1,0:T(8,128)(2,1)S(1)} %collective-permute-done.3.rows.refs_0_), channel_id=1, source_target_pairs={{0,4},{1,3},{4,8},{5,1},{8,12},{9,5},{12,14},{13,9},{14,10},{15,13... | collective-permute-start | bytes 393224 | tf_op jit(solution)/shard_map/ppermute | solution.py:42
  5.7 5.5 %collective-permute-start.6 = (bf16[16,4096]{1,0:T(8,128)(2,1)S(1)}, bf16[16,4096]{1,0:T(8,128)(2,1)S(1)}, u32[]{:S(2)}, u32[]{:S(2)}) collective-permute-start(bf16[16,4096]{1,0:T(8,128)(2,1)S(1)} %collective-permute-done.4.refs_1_), channel_id=1, source_target_pairs={{0,4},{1,3},{4,8},{5,1},{8,12},{9,5},{12,14},{13,9},{14,10},{15,13... | collective-permute-start | bytes 393224 | tf_op jit(solution)/shard_map/ppermute | solution.py:42
  7.2 4.5 %collective-permute-start.8 = (bf16[16,4096]{1,0:T(8,128)(2,1)S(1)}, bf16[16,4096]{1,0:T(8,128)(2,1)S(1)}, u32[]{:S(2)}, u32[]{:S(2)}) collective-permute-start(bf16[16,4096]{1,0:T(8,128)(2,1)S(1)} %collective-permute-done.7.refs_0_), channel_id=1, source_target_pairs={{0,4},{1,3},{4,8},{5,1},{8,12},{9,5},{12,14},{13,9},{14,10},{15,13... | collective-permute-start | bytes 393224 | tf_op jit(solution)/shard_map/ppermute | solution.py:42
  8.5 4.5 %collective-permute-start.1 = (bf16[16,4096]{1,0:T(8,128)(2,1)S(1)}, bf16[16,4096]{1,0:T(8,128)(2,1)S(1)}, u32[]{:S(2)}, u32[]{:S(2)}) collective-permute-start(bf16[16,4096]{1,0:T(8,128)(2,1)S(1)} %collective-permute-done.refs_1_), channel_id=1, source_target_pairs={{0,4},{1,3},{4,8},{5,1},{8,12},{9,5},{12,14},{13,9},{14,10},{15,13... | collective-permute-start | bytes 393224 | tf_op jit(solution)/shard_map/ppermute | solution.py:42
  9.8 6.9 %collective-permute-start.10 = (bf16[16,4096]{1,0:T(8,128)(2,1)S(1)}, bf16[16,4096]{1,0:T(8,128)(2,1)S(1)}, u32[]{:S(2)}, u32[]{:S(2)}) collective-permute-start(bf16[16,4096]{1,0:T(8,128)(2,1)S(1)} %collective-permute-done.5.refs_2_), channel_id=1, source_target_pairs={{0,4},{1,3},{4,8},{5,1},{8,12},{9,5},{12,14},{13,9},{14,10},{15,13... | collective-permute-start | bytes 393224 | tf_op jit(solution)/shard_map/ppermute | solution.py:42
  11.1 5.8 %collective-permute-start.11 = (bf16[16,4096]{1,0:T(8,128)(2,1)S(1)}, bf16[16,4096]{1,0:T(8,128)(2,1)S(1)}, u32[]{:S(2)}, u32[]{:S(2)}) collective-permute-start(bf16[16,4096]{1,0:T(8,128)(2,1)S(1)} %collective-permute-done.6.refs_3_), channel_id=1, source_target_pairs={{0,4},{1,3},{4,8},{5,1},{8,12},{9,5},{12,14},{13,9},{14,10},{15,13... | collective-permute-start | bytes 393224 | tf_op jit(solution)/shard_map/ppermute | solution.py:42
  11.7 5.9 %collective-permute-start.12 = (bf16[16,4096]{1,0:T(8,128)(2,1)S(1)}, bf16[16,4096]{1,0:T(8,128)(2,1)S(1)}, u32[]{:S(2)}, u32[]{:S(2)}) collective-permute-start(bf16[16,4096]{1,0:T(8,128)(2,1)S(1)} %collective-permute-done.8.refs_2_), channel_id=1, source_target_pairs={{0,4},{1,3},{4,8},{5,1},{8,12},{9,5},{12,14},{13,9},{14,10},{15,13... | collective-permute-start | bytes 393224 | tf_op jit(solution)/shard_map/ppermute | solution.py:42
  13.0 5.7 %collective-permute-start.2 = (bf16[16,4096]{1,0:T(8,128)(2,1)S(1)}, bf16[16,4096]{1,0:T(8,128)(2,1)S(1)}, u32[]{:S(2)}, u32[]{:S(2)}) collective-permute-start(bf16[16,4096]{1,0:T(8,128)(2,1)S(1)} %collective-permute-done.1.refs_3_), channel_id=1, source_target_pairs={{0,4},{1,3},{4,8},{5,1},{8,12},{9,5},{12,14},{13,9},{14,10},{15,13... | collective-permute-start | bytes 393224 | tf_op jit(solution)/shard_map/ppermute | solution.py:42
  14.1 13.5 %collective-permute-start.9 = (bf16[128,4096]{1,0:T(8,128)(2,1)S(1)}, bf16[128,4096]{1,0:T(8,128)(2,1)S(1)}, u32[]{:S(2)}, u32[]{:S(2)}) collective-permute-start(bf16[128,4096]{1,0:T(8,128)(2,1)S(1)} %constant_dynamic-update-slice_fusion), channel_id=1, source_target_pairs={{0,1},{1,0},{2,3},{3,2},{4,5},{5,4},{6,7},{7,6},{8,9},{9,8},{10,11... | collective-permute-start | bytes 3145736 | tf_op jit(solution)/shard_map/ppermute | solution.py:45
  16.7 4.8 %collective-permute-start.14 = (bf16[16,4096]{1,0:T(8,128)(2,1)S(1)}, bf16[16,4096]{1,0:T(8,128)(2,1)S(1)}, u32[]{:S(2)}, u32[]{:S(2)}) collective-permute-start(bf16[16,4096]{1,0:T(8,128)(2,1)S(1)} %collective-permute-done.10.refs_5_), channel_id=1, source_target_pairs={{0,4},{1,3},{4,8},{5,1},{8,12},{9,5},{12,14},{13,9},{14,10},{15,13... | collective-permute-start | bytes 393224 | tf_op jit(solution)/shard_map/ppermute | solution.py:42
  16.9 5.9 %collective-permute-start.15 = (bf16[16,4096]{1,0:T(8,128)(2,1)S(1)}, bf16[16,4096]{1,0:T(8,128)(2,1)S(1)}, u32[]{:S(2)}, u32[]{:S(2)}) collective-permute-start(bf16[16,4096]{1,0:T(8,128)(2,1)S(1)} %collective-permute-done.11.refs_6_), channel_id=1, source_target_pairs={{0,4},{1,3},{4,8},{5,1},{8,12},{9,5},{12,14},{13,9},{14,10},{15,13... | collective-permute-start | bytes 393224 | tf_op jit(solution)/shard_map/ppermute | solution.py:42
  18.7 8.9 %collective-permute-start.13 = (bf16[64,4096]{1,0:T(8,128)(2,1)S(1)}, bf16[64,4096]{1,0:T(8,128)(2,1)S(1)}, u32[]{:S(2)}, u32[]{:S(2)}) collective-permute-start(bf16[64,4096]{1,0:T(8,128)(2,1)S(1)} %pad_maximum_fusion), channel_id=1, source_target_pairs={{0,1},{1,0},{2,3},{3,2},{4,5},{5,4},{6,7},{7,6},{8,9},{9,8},{10,11... | collective-permute-start | bytes 1572872 | tf_op jit(solution)/shard_map/ppermute | solution.py:45
  21.1 4.1 %collective-permute-start.18 = (bf16[16,4096]{1,0:T(8,128)(2,1)S(1)}, bf16[16,4096]{1,0:T(8,128)(2,1)S(1)}, u32[]{:S(2)}, u32[]{:S(2)}) collective-permute-start(bf16[16,4096]{1,0:T(8,128)(2,1)S(1)} %collective-permute-done.2.refs_6_), channel_id=1, source_target_pairs={{0,4},{1,3},{4,8},{5,1},{8,12},{9,5},{12,14},{13,9},{14,10},{15,13... | collective-permute-start | bytes 393224 | tf_op jit(solution)/shard_map/ppermute | solution.py:42
  21.6 5.1 %collective-permute-start.17 = (bf16[16,4096]{1,0:T(8,128)(2,1)S(1)}, bf16[16,4096]{1,0:T(8,128)(2,1)S(1)}, u32[]{:S(2)}, u32[]{:S(2)}) collective-permute-start(bf16[16,4096]{1,0:T(8,128)(2,1)S(1)} %collective-permute-done.12.refs_5_), channel_id=1, source_target_pairs={{0,4},{1,3},{4,8},{5,1},{8,12},{9,5},{12,14},{13,9},{14,10},{15,13... | collective-permute-start | bytes 393224 | tf_op jit(solution)/shard_map/ppermute | solution.py:42
  22.8 4.8 %collective-permute-start.16 = (bf16[32,4096]{1,0:T(8,128)(2,1)S(1)}, bf16[32,4096]{1,0:T(8,128)(2,1)S(1)}, u32[]{:S(2)}, u32[]{:S(2)}) collective-permute-start(bf16[32,4096]{1,0:T(8,128)(2,1)S(1)} %pad_maximum_fusion.1), channel_id=1, source_target_pairs={{0,1},{1,0},{2,3},{3,2},{4,5},{5,4},{6,7},{7,6},{8,9},{9,8},{10,11... | collective-permute-start | bytes 786440 | tf_op jit(solution)/shard_map/ppermute | solution.py:45
  26.6 3.3 %collective-permute-start.19 = (bf16[32,4096]{1,0:T(8,128)(2,1)S(1)}, bf16[32,4096]{1,0:T(8,128)(2,1)S(1)}, u32[]{:S(2)}, u32[]{:S(2)}) collective-permute-start(bf16[32,4096]{1,0:T(8,128)(2,1)S(1)} %pad_maximum_fusion.2), channel_id=1, source_target_pairs={{0,1},{1,0},{2,3},{3,2},{4,5},{5,4},{6,7},{7,6},{8,9},{9,8},{10,11... | collective-permute-start | bytes 786440 | tf_op jit(solution)/shard_map/ppermute | solution.py:45

commit v13 on v12

--- a/solution.py
+++ b/solution.py
@@ -105,31 +105,14 @@
     squares[here, :] = total if first else squares[here, :] + total
 
 
-def add_products(cols, queries, probes, centered, scores, first):
-    products = lax.dot_general(
-        centered[:, cols], probes[queries, cols], (((1,), (1,)), ((), ())),
-        preferred_element_type=jnp.float32,
-    )
-    scores[:, queries] = products if first else scores[:, queries] + products
-
-
-def interleave(features, prepare, probes, centered, scores):
-    waiting = []
-    for start in range(0, features, CHUNK):
-        cols, first = slice(start, start + CHUNK), start == 0
-        work = prepare(cols, first)
-        share = -(-len(work) // max(len(waiting), 1))
-        for i in range(0, len(work), share):
-            if waiting:
-                waiting.pop(0)()
-            for step in work[i : i + share]:
-                step()
-        waiting += [
-            functools.partial(add_products, cols, queries, probes, centered, scores, first)
-            for queries in row_groups(probes.shape[0], BLOCK)
-        ]
-    for step in waiting:
-        step()
+def add_log_sums(probes, centered, squares, scores, store):
+    for queries in row_groups(probes.shape[0], BLOCK):
+        scores[:, queries] = lax.dot_general(
+            centered[...], probes[queries, :], (((1,), (1,)), ((), ())),
+            preferred_element_type=jnp.float32,
+        )
+    for queries in row_groups(probes.shape[0], BLOCK):
+        store(queries, log_sum(squares, scores, queries))
 
 
 def log_sum(squares, scores, queries):
@@ -172,32 +155,32 @@
     def center_queries(rows, cols):
         probes[rows, cols] = center(queries[rows, cols], mean[:, cols])
 
-    def prepare(cols, first):
-        work = [functools.partial(take_mean, cols)]
+    for start in range(0, features, CHUNK):
+        cols = slice(start, start + CHUNK)
+        take_mean(cols)
         for group in groups:
-            work.append(functools.partial(center_group, group, cols, mean, centered, squares, first))
+            center_group(group, cols, mean, centered, squares, start == 0)
         for rows in row_groups(probes.shape[0], GROUP):
-            work.append(functools.partial(center_queries, rows, cols))
-        return work
-
-    interleave(features, prepare, probes, centered, scores)
-    for block in row_groups(probes.shape[0], BLOCK):
-        ref_log[:, block] = log_sum(squares, scores, block)
+            center_queries(rows, cols)
+
+    def store(block, value):
+        ref_log[:, block] = value
+
+    add_log_sums(probes, centered, squares, scores, store)
 
 
 def gen_kernel(spans, ref_log, probes, mean, *refs):
     panel, (proof, centered, squares, scores) = refs[: len(spans)], refs[len(spans) :]
     groups = panel_groups(panel, spans)
 
-    def prepare(cols, first):
-        return [
-            functools.partial(center_group, group, cols, mean, centered, squares, first)
-            for group in groups
-        ]
-
-    interleave(centered.shape[1], prepare, probes, centered, scores)
-    for block in row_groups(probes.shape[0], BLOCK):
-        proof[:, block] = log_sum(squares, scores, block) - ref_log[:, block]
+    for start in range(0, centered.shape[1], CHUNK):
+        for group in groups:
+            center_group(group, slice(start, start + CHUNK), mean, centered, squares, start == 0)
+
+    def store(block, value):
+        proof[:, block] = value - ref_log[:, block]
+
+    add_log_sums(probes, centered, squares, scores, store)
 
 
 def call(kernel, before, pieces, count, out_shape):

time: 32.2 us -> 32.2 us (level)
  no operation moved by 1% of the time
where the time goes in v13:
time: 32.2 us; the launch traced here: 32 us
  starting transfers between devices  22.8 us (71%)
  waiting for transfers between devices  4.55 us (14%)
  Pallas kernels  4.43 us (14%)
    ppermute x14, starting transfers between devices, hop(): return lax.ppermute(block, 'samp', ring)  15.2 us
    ppermute x6, starting transfers between devices, hand_over(): return lax.ppermute(block, 'samp', twins)  7.58 us
    ppermute x14, waiting for transfers between devices, hop(): return lax.ppermute(block, 'samp', ring)  4.53 us
    pallas_call x2, Pallas kernels, call(): pl.pallas_call(functools.partial(kernel, spans), out_shape=out_shape, in_...  4.37 us
  transfers between devices with their start and end apart: 20, of which 6 were waited for; matrix products, arithmetic and copies ran while one was open for 0% of the time, Pallas kernels for 7%

profile of v13, /device:TPU:1, one launch (start us, length us, event | category | flops | bytes accessed | tf_op | source)
XLA Modules:
  0.0 32.0 jit_solution(2164177292702358949)
XLA Ops:
  0.0 0.0 copy-start
  0.0 0.1 collective-permute-start.3
  0.1 2.7 %collective-permute-start.4 = (bf16[16,4096]{1,0:T(8,128)(2,1)}, bf16[16,4096]{1,0:T(8,128)(2,1)S(1)}, u32[]{:S(2)}, u32[]{:S(2)}) collective-permute-start(bf16[16,4096]{1,0:T(8,128)(2,1)} %param.5), channel_id=1, source_target_pairs={{0,4},{1,3},{4,8},{5,1},{8,12},{9,5},{12,14},{13,9},{14,10},{15,13... | collective-permute-start | bytes 393224 | tf_op jit(solution)/shard_map/ppermute | solution.py:42
  2.7 0.4 %collective-permute-start.7 = (bf16[16,4096]{1,0:T(8,128)(2,1)}, bf16[16,4096]{1,0:T(8,128)(2,1)S(1)}, u32[]{:S(2)}, u32[]{:S(2)}) collective-permute-start(bf16[16,4096]{1,0:T(8,128)(2,1)} %param.4), channel_id=1, source_target_pairs={{0,1},{1,0},{2,3},{3,2},{4,5},{5,4},{6,7},{7,6},{8,9},{9,8},{10,11... | collective-permute-start | bytes 393224 | tf_op jit(solution)/shard_map/ppermute | solution.py:45
  3.1 0.9 %collective-permute-start = (bf16[16,4096]{1,0:T(8,128)(2,1)}, bf16[16,4096]{1,0:T(8,128)(2,1)S(1)}, u32[]{:S(2)}, u32[]{:S(2)}) collective-permute-start(bf16[16,4096]{1,0:T(8,128)(2,1)} %param.4), channel_id=1, source_target_pairs={{0,4},{1,3},{4,8},{5,1},{8,12},{9,5},{12,14},{13,9},{14,10},{15,13... | collective-permute-start | bytes 393224 | tf_op jit(solution)/shard_map/ppermute | solution.py:42
  4.0 0.0 collective-permute-done.3.rows.refs_0_
  4.1 1.3 %collective-permute-start.5 = (bf16[16,4096]{1,0:T(8,128)(2,1)S(1)}, bf16[16,4096]{1,0:T(8,128)(2,1)S(1)}, u32[]{:S(2)}, u32[]{:S(2)}) collective-permute-start(bf16[16,4096]{1,0:T(8,128)(2,1)S(1)} %collective-permute-done.3.rows.refs_0_), channel_id=1, source_target_pairs={{0,4},{1,3},{4,8},{5,1},{8,12},{9,5},{12,14},{13,9},{14,10},{15,13... | collective-permute-start | bytes 393224 | tf_op jit(solution)/shard_map/ppermute | solution.py:42
  5.4 0.3 collective-permute-done.4.refs_1_
  5.7 1.4 %collective-permute-start.6 = (bf16[16,4096]{1,0:T(8,128)(2,1)S(1)}, bf16[16,4096]{1,0:T(8,128)(2,1)S(1)}, u32[]{:S(2)}, u32[]{:S(2)}) collective-permute-start(bf16[16,4096]{1,0:T(8,128)(2,1)S(1)} %collective-permute-done.4.refs_1_), channel_id=1, source_target_pairs={{0,4},{1,3},{4,8},{5,1},{8,12},{9,5},{12,14},{13,9},{14,10},{15,13... | collective-permute-start | bytes 393224 | tf_op jit(solution)/shard_map/ppermute | solution.py:42
  7.1 0.1 shard_map.37.first_total
  7.1 0.0 collective-permute-done.7.refs_0_
  7.2 1.3 %collective-permute-start.8 = (bf16[16,4096]{1,0:T(8,128)(2,1)S(1)}, bf16[16,4096]{1,0:T(8,128)(2,1)S(1)}, u32[]{:S(2)}, u32[]{:S(2)}) collective-permute-start(bf16[16,4096]{1,0:T(8,128)(2,1)S(1)} %collective-permute-done.7.refs_0_), channel_id=1, source_target_pairs={{0,4},{1,3},{4,8},{5,1},{8,12},{9,5},{12,14},{13,9},{14,10},{15,13... | collective-permute-start | bytes 393224 | tf_op jit(solution)/shard_map/ppermute | solution.py:42
  8.5 0.0 collective-permute-done.refs_1_
  8.5 1.3 %collective-permute-start.1 = (bf16[16,4096]{1,0:T(8,128)(2,1)S(1)}, bf16[16,4096]{1,0:T(8,128)(2,1)S(1)}, u32[]{:S(2)}, u32[]{:S(2)}) collective-permute-start(bf16[16,4096]{1,0:T(8,128)(2,1)S(1)} %collective-permute-done.refs_1_), channel_id=1, source_target_pairs={{0,4},{1,3},{4,8},{5,1},{8,12},{9,5},{12,14},{13,9},{14,10},{15,13... | collective-permute-start | bytes 393224 | tf_op jit(solution)/shard_map/ppermute | solution.py:42
  9.8 0.0 collective-permute-done.5.refs_2_
  9.8 1.3 %collective-permute-start.10 = (bf16[16,4096]{1,0:T(8,128)(2,1)S(1)}, bf16[16,4096]{1,0:T(8,128)(2,1)S(1)}, u32[]{:S(2)}, u32[]{:S(2)}) collective-permute-start(bf16[16,4096]{1,0:T(8,128)(2,1)S(1)} %collective-permute-done.5.refs_2_), channel_id=1, source_target_pairs={{0,4},{1,3},{4,8},{5,1},{8,12},{9,5},{12,14},{13,9},{14,10},{15,13... | collective-permute-start | bytes 393224 | tf_op jit(solution)/shard_map/ppermute | solution.py:42
  11.1 0.0 collective-permute-done.6.refs_3_
  11.1 0.3 collective-permute-start.11
  11.5 0.2 collective-permute-done.8.refs_2_
  11.7 1.0 %collective-permute-start.12 = (bf16[16,4096]{1,0:T(8,128)(2,1)S(1)}, bf16[16,4096]{1,0:T(8,128)(2,1)S(1)}, u32[]{:S(2)}, u32[]{:S(2)}) collective-permute-start(bf16[16,4096]{1,0:T(8,128)(2,1)S(1)} %collective-permute-done.8.refs_2_), channel_id=1, source_target_pairs={{0,4},{1,3},{4,8},{5,1},{8,12},{9,5},{12,14},{13,9},{14,10},{15,13... | collective-permute-start | bytes 393224 | tf_op jit(solution)/shard_map/ppermute | solution.py:42
  12.7 0.3 collective-permute-done.1.refs_3_
  13.0 1.1 %collective-permute-start.2 = (bf16[16,4096]{1,0:T(8,128)(2,1)S(1)}, bf16[16,4096]{1,0:T(8,128)(2,1)S(1)}, u32[]{:S(2)}, u32[]{:S(2)}) collective-permute-start(bf16[16,4096]{1,0:T(8,128)(2,1)S(1)} %collective-permute-done.1.refs_3_), channel_id=1, source_target_pairs={{0,4},{1,3},{4,8},{5,1},{8,12},{9,5},{12,14},{13,9},{14,10},{15,13... | collective-permute-start | bytes 393224 | tf_op jit(solution)/shard_map/ppermute | solution.py:42
  14.1 2.6 %collective-permute-start.9 = (bf16[128,4096]{1,0:T(8,128)(2,1)S(1)}, bf16[128,4096]{1,0:T(8,128)(2,1)S(1)}, u32[]{:S(2)}, u32[]{:S(2)}) collective-permute-start(bf16[128,4096]{1,0:T(8,128)(2,1)S(1)} %constant_dynamic-update-slice_fusion), channel_id=1, source_target_pairs={{0,1},{1,0},{2,3},{3,2},{4,5},{5,4},{6,7},{7,6},{8,9},{9,8},{10,11... | collective-permute-start | bytes 3145736 | tf_op jit(solution)/shard_map/ppermute | solution.py:45
  16.7 0.0 collective-permute-done.10.refs_5_
  16.7 0.2 collective-permute-start.14
  16.9 0.0 collective-permute-done.11.refs_6_
  16.9 0.7 %collective-permute-start.15 = (bf16[16,4096]{1,0:T(8,128)(2,1)S(1)}, bf16[16,4096]{1,0:T(8,128)(2,1)S(1)}, u32[]{:S(2)}, u32[]{:S(2)}) collective-permute-start(bf16[16,4096]{1,0:T(8,128)(2,1)S(1)} %collective-permute-done.11.refs_6_), channel_id=1, source_target_pairs={{0,4},{1,3},{4,8},{5,1},{8,12},{9,5},{12,14},{13,9},{14,10},{15,13... | collective-permute-start | bytes 393224 | tf_op jit(solution)/shard_map/ppermute | solution.py:42
  17.6 0.0 collective-permute-done.12.refs_5_
  17.6 1.1 %collective-permute-done.2.refs_6_ = bf16[16,4096]{1,0:T(8,128)(2,1)S(1)} collective-permute-done((bf16[16,4096]{1,0:T(8,128)(2,1)S(1)}, bf16[16,4096]{1,0:T(8,128)(2,1)S(1)}, u32[]{:S(2)}, u32[]{:S(2)}) %collective-permute-start.2) | collective-permute-done | bytes 131104 | tf_op jit(solution)/shard_map/ppermute | solution.py:42
  18.7 2.4 %collective-permute-start.13 = (bf16[64,4096]{1,0:T(8,128)(2,1)S(1)}, bf16[64,4096]{1,0:T(8,128)(2,1)S(1)}, u32[]{:S(2)}, u32[]{:S(2)}) collective-permute-start(bf16[64,4096]{1,0:T(8,128)(2,1)S(1)} %pad_maximum_fusion), channel_id=1, source_target_pairs={{0,1},{1,0},{2,3},{3,2},{4,5},{5,4},{6,7},{7,6},{8,9},{9,8},{10,11... | collective-permute-start | bytes 1572872 | tf_op jit(solution)/shard_map/ppermute | solution.py:45
  21.1 0.5 %collective-permute-start.18 = (bf16[16,4096]{1,0:T(8,128)(2,1)S(1)}, bf16[16,4096]{1,0:T(8,128)(2,1)S(1)}, u32[]{:S(2)}, u32[]{:S(2)}) collective-permute-start(bf16[16,4096]{1,0:T(8,128)(2,1)S(1)} %collective-permute-done.2.refs_6_), channel_id=1, source_target_pairs={{0,4},{1,3},{4,8},{5,1},{8,12},{9,5},{12,14},{13,9},{14,10},{15,13... | collective-permute-start | bytes 393224 | tf_op jit(solution)/shard_map/ppermute | solution.py:42
  21.5 0.0 collective-permute-done.14.refs_8_
  21.6 1.2 %collective-permute-start.17 = (bf16[16,4096]{1,0:T(8,128)(2,1)S(1)}, bf16[16,4096]{1,0:T(8,128)(2,1)S(1)}, u32[]{:S(2)}, u32[]{:S(2)}) collective-permute-start(bf16[16,4096]{1,0:T(8,128)(2,1)S(1)} %collective-permute-done.12.refs_5_), channel_id=1, source_target_pairs={{0,4},{1,3},{4,8},{5,1},{8,12},{9,5},{12,14},{13,9},{14,10},{15,13... | collective-permute-start | bytes 393224 | tf_op jit(solution)/shard_map/ppermute | solution.py:42
  22.8 0.0 collective-permute-done.15.refs_9_
  22.8 1.2 %collective-permute-start.16 = (bf16[32,4096]{1,0:T(8,128)(2,1)S(1)}, bf16[32,4096]{1,0:T(8,128)(2,1)S(1)}, u32[]{:S(2)}, u32[]{:S(2)}) collective-permute-start(bf16[32,4096]{1,0:T(8,128)(2,1)S(1)} %pad_maximum_fusion.1), channel_id=1, source_target_pairs={{0,1},{1,0},{2,3},{3,2},{4,5},{5,4},{6,7},{7,6},{8,9},{9,8},{10,11... | collective-permute-start | bytes 786440 | tf_op jit(solution)/shard_map/ppermute | solution.py:45
  24.0 1.2 %collective-permute-done.18.refs_9_ = bf16[16,4096]{1,0:T(8,128)(2,1)S(1)} collective-permute-done((bf16[16,4096]{1,0:T(8,128)(2,1)S(1)}, bf16[16,4096]{1,0:T(8,128)(2,1)S(1)}, u32[]{:S(2)}, u32[]{:S(2)}) %collective-permute-start.18) | collective-permute-done | bytes 131104 | tf_op jit(solution)/shard_map/ppermute | solution.py:42
  25.2 1.4 %collective-permute-done.17.refs_8_ = bf16[16,4096]{1,0:T(8,128)(2,1)S(1)} collective-permute-done((bf16[16,4096]{1,0:T(8,128)(2,1)S(1)}, bf16[16,4096]{1,0:T(8,128)(2,1)S(1)}, u32[]{:S(2)}, u32[]{:S(2)}) %collective-permute-start.17) | collective-permute-done | bytes 131104 | tf_op jit(solution)/shard_map/ppermute | solution.py:42
  26.6 1.0 %collective-permute-start.19 = (bf16[32,4096]{1,0:T(8,128)(2,1)S(1)}, bf16[32,4096]{1,0:T(8,128)(2,1)S(1)}, u32[]{:S(2)}, u32[]{:S(2)}) collective-permute-start(bf16[32,4096]{1,0:T(8,128)(2,1)S(1)} %pad_maximum_fusion.2), channel_id=1, source_target_pairs={{0,1},{1,0},{2,3},{3,2},{4,5},{5,4},{6,7},{7,6},{8,9},{9,8},{10,11... | collective-permute-start | bytes 786440 | tf_op jit(solution)/shard_map/ppermute | solution.py:45
  27.6 0.0 collective-permute-done.16.refs_10_
  27.6 0.0 collective-permute-done.13.refs_7_
  27.6 0.0 collective-permute-done.9.refs_4_
  27.6 0.0 copy-done
  27.6 2.3 %shard_map.38 = (bf16[512,4096]{1,0:T(8,128)(2,1)S(1)}, f32[1,4096]{1,0:T(1,128)S(1)}, f32[1,512]{1,0:T(1,128)S(1)}) custom-call(bf16[512,4096]{1,0:T(8,128)(2,1)S(1)} %copy-done, f32[1,4096]{1,0:T(1,128)S(1)} %shard_map.37.first_total, bf16[16,4096]{1,0:T(8,128)(2,1)S(1)} %collective-permute-done.3.rows.refs_0_, ...), custom_call_target="tpu_custom_call" | custom-call | flops 1073741824 | bytes 6291456 | tf_op jit(solution)/shard_map/pallas_call | solution.py:191
  30.0 0.0 collective-permute-done.19.refs_10_
  30.0 2.1 %shard_map.39 = f32[1,512]{1,0:T(1,128)} custom-call(f32[1,512]{1,0:T(1,128)S(1)} %get-tuple-element.11.ref_log, bf16[512,4096]{1,0:T(8,128)(2,1)S(1)} %get-tuple-element.12.probes, f32[1,4096]{1,0:T(1,128)S(1)} %get-tuple-element.13.mean, bf16[16,4096]{1,0:T(8,128)(2,1)S(1)} %collective-permute-done.7.refs_0_, ...), custom_call_target="tpu_custom_call" | custom-call | flops 1073741824 | bytes 6291456 | tf_op jit(solution)/shard_map/pallas_call | solution.py:191
  (11 shorter events, 0.2 us)
Async XLA Ops:
  0.0 27.6 %copy-start = (bf16[512,4096]{1,0:T(8,128)(2,1)S(1)}, bf16[512,4096]{1,0:T(8,128)(2,1)}, u32[]{:S(2)}) copy-start(bf16[512,4096]{1,0:T(8,128)(2,1)} %queries.1) | copy-start | bytes 12582916
  0.0 4.0 %collective-permute-start.3 = (bf16[16,4096]{1,0:T(8,128)(2,1)}, bf16[16,4096]{1,0:T(8,128)(2,1)S(1)}, u32[]{:S(2)}, u32[]{:S(2)}) collective-permute-start(bf16[16,4096]{1,0:T(8,128)(2,1)} %param.5), channel_id=1, source_target_pairs={{0,1},{1,0},{2,3},{3,2},{4,5},{5,4},{6,7},{7,6},{8,9},{9,8},{10,11... | collective-permute-start | bytes 393224 | tf_op jit(solution)/shard_map/ppermute | solution.py:45
  0.1 5.6 %collective-permute-start.4 = (bf16[16,4096]{1,0:T(8,128)(2,1)}, bf16[16,4096]{1,0:T(8,128)(2,1)S(1)}, u32[]{:S(2)}, u32[]{:S(2)}) collective-permute-start(bf16[16,4096]{1,0:T(8,128)(2,1)} %param.5), channel_id=1, source_target_pairs={{0,4},{1,3},{4,8},{5,1},{8,12},{9,5},{12,14},{13,9},{14,10},{15,13... | collective-permute-start | bytes 393224 | tf_op jit(solution)/shard_map/ppermute | solution.py:42
  2.7 4.4 %collective-permute-start.7 = (bf16[16,4096]{1,0:T(8,128)(2,1)}, bf16[16,4096]{1,0:T(8,128)(2,1)S(1)}, u32[]{:S(2)}, u32[]{:S(2)}) collective-permute-start(bf16[16,4096]{1,0:T(8,128)(2,1)} %param.4), channel_id=1, source_target_pairs={{0,1},{1,0},{2,3},{3,2},{4,5},{5,4},{6,7},{7,6},{8,9},{9,8},{10,11... | collective-permute-start | bytes 393224 | tf_op jit(solution)/shard_map/ppermute | solution.py:45
  3.1 5.4 %collective-permute-start = (bf16[16,4096]{1,0:T(8,128)(2,1)}, bf16[16,4096]{1,0:T(8,128)(2,1)S(1)}, u32[]{:S(2)}, u32[]{:S(2)}) collective-permute-start(bf16[16,4096]{1,0:T(8,128)(2,1)} %param.4), channel_id=1, source_target_pairs={{0,4},{1,3},{4,8},{5,1},{8,12},{9,5},{12,14},{13,9},{14,10},{15,13... | collective-permute-start | bytes 393224 | tf_op jit(solution)/shard_map/ppermute | solution.py:42
  4.1 5.7 %collective-permute-start.5 = (bf16[16,4096]{1,0:T(8,128)(2,1)S(1)}, bf16[16,4096]{1,0:T(8,128)(2,1)S(1)}, u32[]{:S(2)}, u32[]{:S(2)}) collective-permute-start(bf16[16,4096]{1,0:T(8,128)(2,1)S(1)} %collective-permute-done.3.rows.refs_0_), channel_id=1, source_target_pairs={{0,4},{1,3},{4,8},{5,1},{8,12},{9,5},{12,14},{13,9},{14,10},{15,13... | collective-permute-start | bytes 393224 | tf_op jit(solution)/shard_map/ppermute | solution.py:42
  5.7 5.5 %collective-permute-start.6 = (bf16[16,4096]{1,0:T(8,128)(2,1)S(1)}, bf16[16,4096]{1,0:T(8,128)(2,1)S(1)}, u32[]{:S(2)}, u32[]{:S(2)}) collective-permute-start(bf16[16,4096]{1,0:T(8,128)(2,1)S(1)} %collective-permute-done.4.refs_1_), channel_id=1, source_target_pairs={{0,4},{1,3},{4,8},{5,1},{8,12},{9,5},{12,14},{13,9},{14,10},{15,13... | collective-permute-start | bytes 393224 | tf_op jit(solution)/shard_map/ppermute | solution.py:42
  7.2 4.5 %collective-permute-start.8 = (bf16[16,4096]{1,0:T(8,128)(2,1)S(1)}, bf16[16,4096]{1,0:T(8,128)(2,1)S(1)}, u32[]{:S(2)}, u32[]{:S(2)}) collective-permute-start(bf16[16,4096]{1,0:T(8,128)(2,1)S(1)} %collective-permute-done.7.refs_0_), channel_id=1, source_target_pairs={{0,4},{1,3},{4,8},{5,1},{8,12},{9,5},{12,14},{13,9},{14,10},{15,13... | collective-permute-start | bytes 393224 | tf_op jit(solution)/shard_map/ppermute | solution.py:42
  8.5 4.5 %collective-permute-start.1 = (bf16[16,4096]{1,0:T(8,128)(2,1)S(1)}, bf16[16,4096]{1,0:T(8,128)(2,1)S(1)}, u32[]{:S(2)}, u32[]{:S(2)}) collective-permute-start(bf16[16,4096]{1,0:T(8,128)(2,1)S(1)} %collective-permute-done.refs_1_), channel_id=1, source_target_pairs={{0,4},{1,3},{4,8},{5,1},{8,12},{9,5},{12,14},{13,9},{14,10},{15,13... | collective-permute-start | bytes 393224 | tf_op jit(solution)/shard_map/ppermute | solution.py:42
  9.8 6.9 %collective-permute-start.10 = (bf16[16,4096]{1,0:T(8,128)(2,1)S(1)}, bf16[16,4096]{1,0:T(8,128)(2,1)S(1)}, u32[]{:S(2)}, u32[]{:S(2)}) collective-permute-start(bf16[16,4096]{1,0:T(8,128)(2,1)S(1)} %collective-permute-done.5.refs_2_), channel_id=1, source_target_pairs={{0,4},{1,3},{4,8},{5,1},{8,12},{9,5},{12,14},{13,9},{14,10},{15,13... | collective-permute-start | bytes 393224 | tf_op jit(solution)/shard_map/ppermute | solution.py:42
  11.1 5.8 %collective-permute-start.11 = (bf16[16,4096]{1,0:T(8,128)(2,1)S(1)}, bf16[16,4096]{1,0:T(8,128)(2,1)S(1)}, u32[]{:S(2)}, u32[]{:S(2)}) collective-permute-start(bf16[16,4096]{1,0:T(8,128)(2,1)S(1)} %collective-permute-done.6.refs_3_), channel_id=1, source_target_pairs={{0,4},{1,3},{4,8},{5,1},{8,12},{9,5},{12,14},{13,9},{14,10},{15,13... | collective-permute-start | bytes 393224 | tf_op jit(solution)/shard_map/ppermute | solution.py:42
  11.7 5.9 %collective-permute-start.12 = (bf16[16,4096]{1,0:T(8,128)(2,1)S(1)}, bf16[16,4096]{1,0:T(8,128)(2,1)S(1)}, u32[]{:S(2)}, u32[]{:S(2)}) collective-permute-start(bf16[16,4096]{1,0:T(8,128)(2,1)S(1)} %collective-permute-done.8.refs_2_), channel_id=1, source_target_pairs={{0,4},{1,3},{4,8},{5,1},{8,12},{9,5},{12,14},{13,9},{14,10},{15,13... | collective-permute-start | bytes 393224 | tf_op jit(solution)/shard_map/ppermute | solution.py:42
  13.0 5.7 %collective-permute-start.2 = (bf16[16,4096]{1,0:T(8,128)(2,1)S(1)}, bf16[16,4096]{1,0:T(8,128)(2,1)S(1)}, u32[]{:S(2)}, u32[]{:S(2)}) collective-permute-start(bf16[16,4096]{1,0:T(8,128)(2,1)S(1)} %collective-permute-done.1.refs_3_), channel_id=1, source_target_pairs={{0,4},{1,3},{4,8},{5,1},{8,12},{9,5},{12,14},{13,9},{14,10},{15,13... | collective-permute-start | bytes 393224 | tf_op jit(solution)/shard_map/ppermute | solution.py:42
  14.1 13.5 %collective-permute-start.9 = (bf16[128,4096]{1,0:T(8,128)(2,1)S(1)}, bf16[128,4096]{1,0:T(8,128)(2,1)S(1)}, u32[]{:S(2)}, u32[]{:S(2)}) collective-permute-start(bf16[128,4096]{1,0:T(8,128)(2,1)S(1)} %constant_dynamic-update-slice_fusion), channel_id=1, source_target_pairs={{0,1},{1,0},{2,3},{3,2},{4,5},{5,4},{6,7},{7,6},{8,9},{9,8},{10,11... | collective-permute-start | bytes 3145736 | tf_op jit(solution)/shard_map/ppermute | solution.py:45
  16.7 4.8 %collective-permute-start.14 = (bf16[16,4096]{1,0:T(8,128)(2,1)S(1)}, bf16[16,4096]{1,0:T(8,128)(2,1)S(1)}, u32[]{:S(2)}, u32[]{:S(2)}) collective-permute-start(bf16[16,4096]{1,0:T(8,128)(2,1)S(1)} %collective-permute-done.10.refs_5_), channel_id=1, source_target_pairs={{0,4},{1,3},{4,8},{5,1},{8,12},{9,5},{12,14},{13,9},{14,10},{15,13... | collective-permute-start | bytes 393224 | tf_op jit(solution)/shard_map/ppermute | solution.py:42
  16.9 5.9 %collective-permute-start.15 = (bf16[16,4096]{1,0:T(8,128)(2,1)S(1)}, bf16[16,4096]{1,0:T(8,128)(2,1)S(1)}, u32[]{:S(2)}, u32[]{:S(2)}) collective-permute-start(bf16[16,4096]{1,0:T(8,128)(2,1)S(1)} %collective-permute-done.11.refs_6_), channel_id=1, source_target_pairs={{0,4},{1,3},{4,8},{5,1},{8,12},{9,5},{12,14},{13,9},{14,10},{15,13... | collective-permute-start | bytes 393224 | tf_op jit(solution)/shard_map/ppermute | solution.py:42
  18.7 8.9 %collective-permute-start.13 = (bf16[64,4096]{1,0:T(8,128)(2,1)S(1)}, bf16[64,4096]{1,0:T(8,128)(2,1)S(1)}, u32[]{:S(2)}, u32[]{:S(2)}) collective-permute-start(bf16[64,4096]{1,0:T(8,128)(2,1)S(1)} %pad_maximum_fusion), channel_id=1, source_target_pairs={{0,1},{1,0},{2,3},{3,2},{4,5},{5,4},{6,7},{7,6},{8,9},{9,8},{10,11... | collective-permute-start | bytes 1572872 | tf_op jit(solution)/shard_map/ppermute | solution.py:45
  21.1 4.1 %collective-permute-start.18 = (bf16[16,4096]{1,0:T(8,128)(2,1)S(1)}, bf16[16,4096]{1,0:T(8,128)(2,1)S(1)}, u32[]{:S(2)}, u32[]{:S(2)}) collective-permute-start(bf16[16,4096]{1,0:T(8,128)(2,1)S(1)} %collective-permute-done.2.refs_6_), channel_id=1, source_target_pairs={{0,4},{1,3},{4,8},{5,1},{8,12},{9,5},{12,14},{13,9},{14,10},{15,13... | collective-permute-start | bytes 393224 | tf_op jit(solution)/shard_map/ppermute | solution.py:42
  21.6 5.1 %collective-permute-start.17 = (bf16[16,4096]{1,0:T(8,128)(2,1)S(1)}, bf16[16,4096]{1,0:T(8,128)(2,1)S(1)}, u32[]{:S(2)}, u32[]{:S(2)}) collective-permute-start(bf16[16,4096]{1,0:T(8,128)(2,1)S(1)} %collective-permute-done.12.refs_5_), channel_id=1, source_target_pairs={{0,4},{1,3},{4,8},{5,1},{8,12},{9,5},{12,14},{13,9},{14,10},{15,13... | collective-permute-start | bytes 393224 | tf_op jit(solution)/shard_map/ppermute | solution.py:42
  22.8 4.8 %collective-permute-start.16 = (bf16[32,4096]{1,0:T(8,128)(2,1)S(1)}, bf16[32,4096]{1,0:T(8,128)(2,1)S(1)}, u32[]{:S(2)}, u32[]{:S(2)}) collective-permute-start(bf16[32,4096]{1,0:T(8,128)(2,1)S(1)} %pad_maximum_fusion.1), channel_id=1, source_target_pairs={{0,1},{1,0},{2,3},{3,2},{4,5},{5,4},{6,7},{7,6},{8,9},{9,8},{10,11... | collective-permute-start | bytes 786440 | tf_op jit(solution)/shard_map/ppermute | solution.py:45
  26.6 3.3 %collective-permute-start.19 = (bf16[32,4096]{1,0:T(8,128)(2,1)S(1)}, bf16[32,4096]{1,0:T(8,128)(2,1)S(1)}, u32[]{:S(2)}, u32[]{:S(2)}) collective-permute-start(bf16[32,4096]{1,0:T(8,128)(2,1)S(1)} %pad_maximum_fusion.2), channel_id=1, source_target_pairs={{0,1},{1,0},{2,3},{3,2},{4,5},{5,4},{6,7},{7,6},{8,9},{9,8},{10,11... | collective-permute-start | bytes 786440 | tf_op jit(solution)/shard_map/ppermute | solution.py:45

commit v14 on v12

--- a/solution.py
+++ b/solution.py
@@ -51,7 +51,7 @@
     for period in range(steps + 1):
         last = period == steps
         if last and period:
-            mine[-1], extra = lax.optimization_barrier((mine[-1], extra))
+            other[0], extra = lax.optimization_barrier((other[0], extra))
         other = [hop(o) for o in other] if period else [hand_over(p) for p in panels]
         if not period:
             extra = on_first(other[0])
@@ -67,7 +67,7 @@
                 if fresh[i]:
                     block = hand_over(jnp.concatenate(fresh[i], axis=0))
                     pieces[i].append((block, 0, block.shape[0]))
-        elif period:
+        elif period and period < steps - 1:
             block, at = hand_over(jnp.concatenate([f for g in fresh for f in g], axis=0)), 0
             for i in range(len(panels)):
                 upto = at + rows * len(fresh[i])

time: 32.2 us -> 31.2 us (0.969)
  waiting for transfers between devices: 4.55 us -> 4.04 us
  starting transfers between devices: 22.8 us -> 22.3 us
    ppermute x6 -> x5, starting transfers between devices: 7.58 us -> 6.88 us  [hand_over(): return lax.ppermute(block, 'samp', twins)]
    ppermute x14, waiting for transfers between devices: 4.53 us -> 4.03 us  [hop(): return lax.ppermute(block, 'samp', ring)]
  transfers between devices with their start and end apart: 20 -> 19, of which waited for: 6 -> 7; matrix products, arithmetic and copies ran while one was open for 0% -> 1% of each run, Pallas kernels for 7% -> 8%
where the time goes in v14:
time: 31.2 us; the launch traced here: 31 us
  starting transfers between devices  22.3 us (71%)
  Pallas kernels  4.44 us (14%)
  waiting for transfers between devices  4.04 us (13%)
    ppermute x14, starting transfers between devices, hop(): return lax.ppermute(block, 'samp', ring)  15.4 us
    ppermute x5, starting transfers between devices, hand_over(): return lax.ppermute(block, 'samp', twins)  6.88 us
    pallas_call x2, Pallas kernels, call(): pl.pallas_call(functools.partial(kernel, spans), out_shape=out_shape, in_...  4.39 us
    ppermute x14, waiting for transfers between devices, hop(): return lax.ppermute(block, 'samp', ring)  4.03 us
  transfers between devices with their start and end apart: 19, of which 7 were waited for; matrix products, arithmetic and copies ran while one was open for 1% of the time, Pallas kernels for 8%

profile of v14, /device:TPU:1, one launch (start us, length us, event | category | flops | bytes accessed | tf_op | source)
XLA Modules:
  0.0 31.0 jit_solution(17173732175020736335)
XLA Ops:
  0.0 0.0 copy-start
  0.0 0.1 collective-permute-start
  0.1 2.7 %collective-permute-start.3 = (bf16[16,4096]{1,0:T(8,128)(2,1)}, bf16[16,4096]{1,0:T(8,128)(2,1)S(1)}, u32[]{:S(2)}, u32[]{:S(2)}) collective-permute-start(bf16[16,4096]{1,0:T(8,128)(2,1)} %param.5), channel_id=1, source_target_pairs={{0,4},{1,3},{4,8},{5,1},{8,12},{9,5},{12,14},{13,9},{14,10},{15,13... | collective-permute-start | bytes 393224 | tf_op jit(solution)/shard_map/ppermute | solution.py:42
  2.7 0.4 %collective-permute-start.5 = (bf16[16,4096]{1,0:T(8,128)(2,1)}, bf16[16,4096]{1,0:T(8,128)(2,1)S(1)}, u32[]{:S(2)}, u32[]{:S(2)}) collective-permute-start(bf16[16,4096]{1,0:T(8,128)(2,1)} %param.4), channel_id=1, source_target_pairs={{0,1},{1,0},{2,3},{3,2},{4,5},{5,4},{6,7},{7,6},{8,9},{9,8},{10,11... | collective-permute-start | bytes 393224 | tf_op jit(solution)/shard_map/ppermute | solution.py:45
  3.1 0.9 %collective-permute-start.6 = (bf16[16,4096]{1,0:T(8,128)(2,1)}, bf16[16,4096]{1,0:T(8,128)(2,1)S(1)}, u32[]{:S(2)}, u32[]{:S(2)}) collective-permute-start(bf16[16,4096]{1,0:T(8,128)(2,1)} %param.4), channel_id=1, source_target_pairs={{0,4},{1,3},{4,8},{5,1},{8,12},{9,5},{12,14},{13,9},{14,10},{15,13... | collective-permute-start | bytes 393224 | tf_op jit(solution)/shard_map/ppermute | solution.py:42
  4.0 0.0 collective-permute-done.rows.refs_0_
  4.1 1.3 %collective-permute-start.1 = (bf16[16,4096]{1,0:T(8,128)(2,1)S(1)}, bf16[16,4096]{1,0:T(8,128)(2,1)S(1)}, u32[]{:S(2)}, u32[]{:S(2)}) collective-permute-start(bf16[16,4096]{1,0:T(8,128)(2,1)S(1)} %collective-permute-done.rows.refs_0_), channel_id=1, source_target_pairs={{0,4},{1,3},{4,8},{5,1},{8,12},{9,5},{12,14},{13,9},{14,10},{15,13... | collective-permute-start | bytes 393224 | tf_op jit(solution)/shard_map/ppermute | solution.py:42
  5.4 0.3 collective-permute-done.3.refs_1_
  5.7 1.4 %collective-permute-start.4 = (bf16[16,4096]{1,0:T(8,128)(2,1)S(1)}, bf16[16,4096]{1,0:T(8,128)(2,1)S(1)}, u32[]{:S(2)}, u32[]{:S(2)}) collective-permute-start(bf16[16,4096]{1,0:T(8,128)(2,1)S(1)} %collective-permute-done.3.refs_1_), channel_id=1, source_target_pairs={{0,4},{1,3},{4,8},{5,1},{8,12},{9,5},{12,14},{13,9},{14,10},{15,13... | collective-permute-start | bytes 393224 | tf_op jit(solution)/shard_map/ppermute | solution.py:42
  7.1 0.1 shard_map.37.first_total
  7.1 0.0 collective-permute-done.5.refs_0_
  7.2 1.3 %collective-permute-start.7 = (bf16[16,4096]{1,0:T(8,128)(2,1)S(1)}, bf16[16,4096]{1,0:T(8,128)(2,1)S(1)}, u32[]{:S(2)}, u32[]{:S(2)}) collective-permute-start(bf16[16,4096]{1,0:T(8,128)(2,1)S(1)} %collective-permute-done.5.refs_0_), channel_id=1, source_target_pairs={{0,4},{1,3},{4,8},{5,1},{8,12},{9,5},{12,14},{13,9},{14,10},{15,13... | collective-permute-start | bytes 393224 | tf_op jit(solution)/shard_map/ppermute | solution.py:42
  8.5 0.0 collective-permute-done.6.refs_1_
  8.5 1.3 %collective-permute-start.8 = (bf16[16,4096]{1,0:T(8,128)(2,1)S(1)}, bf16[16,4096]{1,0:T(8,128)(2,1)S(1)}, u32[]{:S(2)}, u32[]{:S(2)}) collective-permute-start(bf16[16,4096]{1,0:T(8,128)(2,1)S(1)} %collective-permute-done.6.refs_1_), channel_id=1, source_target_pairs={{0,4},{1,3},{4,8},{5,1},{8,12},{9,5},{12,14},{13,9},{14,10},{15,13... | collective-permute-start | bytes 393224 | tf_op jit(solution)/shard_map/ppermute | solution.py:42
  9.8 0.0 collective-permute-done.1.refs_2_
  9.8 1.3 %collective-permute-start.2 = (bf16[16,4096]{1,0:T(8,128)(2,1)S(1)}, bf16[16,4096]{1,0:T(8,128)(2,1)S(1)}, u32[]{:S(2)}, u32[]{:S(2)}) collective-permute-start(bf16[16,4096]{1,0:T(8,128)(2,1)S(1)} %collective-permute-done.1.refs_2_), channel_id=1, source_target_pairs={{0,4},{1,3},{4,8},{5,1},{8,12},{9,5},{12,14},{13,9},{14,10},{15,13... | collective-permute-start | bytes 393224 | tf_op jit(solution)/shard_map/ppermute | solution.py:42
  11.1 0.0 collective-permute-done.4.refs_3_
  11.1 0.2 collective-permute-start.10
  11.4 0.3 collective-permute-done.7.refs_2_
  11.7 1.0 %collective-permute-start.14 = (bf16[16,4096]{1,0:T(8,128)(2,1)S(1)}, bf16[16,4096]{1,0:T(8,128)(2,1)S(1)}, u32[]{:S(2)}, u32[]{:S(2)}) collective-permute-start(bf16[16,4096]{1,0:T(8,128)(2,1)S(1)} %collective-permute-done.7.refs_2_), channel_id=1, source_target_pairs={{0,4},{1,3},{4,8},{5,1},{8,12},{9,5},{12,14},{13,9},{14,10},{15,13... | collective-permute-start | bytes 393224 | tf_op jit(solution)/shard_map/ppermute | solution.py:42
  12.7 0.3 collective-permute-done.8.refs_3_
  13.0 1.1 %collective-permute-start.15 = (bf16[16,4096]{1,0:T(8,128)(2,1)S(1)}, bf16[16,4096]{1,0:T(8,128)(2,1)S(1)}, u32[]{:S(2)}, u32[]{:S(2)}) collective-permute-start(bf16[16,4096]{1,0:T(8,128)(2,1)S(1)} %collective-permute-done.8.refs_3_), channel_id=1, source_target_pairs={{0,4},{1,3},{4,8},{5,1},{8,12},{9,5},{12,14},{13,9},{14,10},{15,13... | collective-permute-start | bytes 393224 | tf_op jit(solution)/shard_map/ppermute | solution.py:42
  14.1 0.4 %collective-permute-done.2.refs_5_ = bf16[16,4096]{1,0:T(8,128)(2,1)S(1)} collective-permute-done((bf16[16,4096]{1,0:T(8,128)(2,1)S(1)}, bf16[16,4096]{1,0:T(8,128)(2,1)S(1)}, u32[]{:S(2)}, u32[]{:S(2)}) %collective-permute-start.2) | collective-permute-done | bytes 131104 | tf_op jit(solution)/shard_map/ppermute | solution.py:42
  14.5 1.0 %collective-permute-start.11 = (bf16[16,4096]{1,0:T(8,128)(2,1)S(1)}, bf16[16,4096]{1,0:T(8,128)(2,1)S(1)}, u32[]{:S(2)}, u32[]{:S(2)}) collective-permute-start(bf16[16,4096]{1,0:T(8,128)(2,1)S(1)} %collective-permute-done.2.refs_5_), channel_id=1, source_target_pairs={{0,4},{1,3},{4,8},{5,1},{8,12},{9,5},{12,14},{13,9},{14,10},{15,13... | collective-permute-start | bytes 393224 | tf_op jit(solution)/shard_map/ppermute | solution.py:42
  15.5 0.4 %collective-permute-done.10.refs_6_ = bf16[16,4096]{1,0:T(8,128)(2,1)S(1)} collective-permute-done((bf16[16,4096]{1,0:T(8,128)(2,1)S(1)}, bf16[16,4096]{1,0:T(8,128)(2,1)S(1)}, u32[]{:S(2)}, u32[]{:S(2)}) %collective-permute-start.10) | collective-permute-done | bytes 131104 | tf_op jit(solution)/shard_map/ppermute | solution.py:42
  15.9 1.0 %collective-permute-start.12 = (bf16[16,4096]{1,0:T(8,128)(2,1)S(1)}, bf16[16,4096]{1,0:T(8,128)(2,1)S(1)}, u32[]{:S(2)}, u32[]{:S(2)}) collective-permute-start(bf16[16,4096]{1,0:T(8,128)(2,1)S(1)} %collective-permute-done.10.refs_6_), channel_id=1, source_target_pairs={{0,4},{1,3},{4,8},{5,1},{8,12},{9,5},{12,14},{13,9},{14,10},{15,13... | collective-permute-start | bytes 393224 | tf_op jit(solution)/shard_map/ppermute | solution.py:42
  16.9 2.7 %collective-permute-start.9 = (bf16[128,4096]{1,0:T(8,128)(2,1)S(1)}, bf16[128,4096]{1,0:T(8,128)(2,1)S(1)}, u32[]{:S(2)}, u32[]{:S(2)}) collective-permute-start(bf16[128,4096]{1,0:T(8,128)(2,1)S(1)} %constant_dynamic-update-slice_fusion), channel_id=1, source_target_pairs={{0,1},{1,0},{2,3},{3,2},{4,5},{5,4},{6,7},{7,6},{8,9},{9,8},{10,11... | collective-permute-start | bytes 3145736 | tf_op jit(solution)/shard_map/ppermute | solution.py:45
  19.6 0.0 collective-permute-done.14.refs_5_
  19.6 0.4 %collective-permute-start.16 = (bf16[16,4096]{1,0:T(8,128)(2,1)S(1)}, bf16[16,4096]{1,0:T(8,128)(2,1)S(1)}, u32[]{:S(2)}, u32[]{:S(2)}) collective-permute-start(bf16[16,4096]{1,0:T(8,128)(2,1)S(1)} %collective-permute-done.14.refs_5_), channel_id=1, source_target_pairs={{0,4},{1,3},{4,8},{5,1},{8,12},{9,5},{12,14},{13,9},{14,10},{15,13... | collective-permute-start | bytes 393224 | tf_op jit(solution)/shard_map/ppermute | solution.py:42
  20.0 0.0 collective-permute-done.15.refs_6_
  20.0 0.4 %collective-permute-start.17 = (bf16[16,4096]{1,0:T(8,128)(2,1)S(1)}, bf16[16,4096]{1,0:T(8,128)(2,1)S(1)}, u32[]{:S(2)}, u32[]{:S(2)}) collective-permute-start(bf16[16,4096]{1,0:T(8,128)(2,1)S(1)} %collective-permute-done.15.refs_6_), channel_id=1, source_target_pairs={{0,4},{1,3},{4,8},{5,1},{8,12},{9,5},{12,14},{13,9},{14,10},{15,13... | collective-permute-start | bytes 393224 | tf_op jit(solution)/shard_map/ppermute | solution.py:42
  20.4 0.0 collective-permute-done.11.refs_7_
  20.4 1.1 %collective-permute-done.12.refs_8_ = bf16[16,4096]{1,0:T(8,128)(2,1)S(1)} collective-permute-done((bf16[16,4096]{1,0:T(8,128)(2,1)S(1)}, bf16[16,4096]{1,0:T(8,128)(2,1)S(1)}, u32[]{:S(2)}, u32[]{:S(2)}) %collective-permute-start.12) | collective-permute-done | bytes 131104 | tf_op jit(solution)/shard_map/ppermute | solution.py:42
  21.5 2.3 %collective-permute-start.13 = (bf16[64,4096]{1,0:T(8,128)(2,1)S(1)}, bf16[64,4096]{1,0:T(8,128)(2,1)S(1)}, u32[]{:S(2)}, u32[]{:S(2)}) collective-permute-start(bf16[64,4096]{1,0:T(8,128)(2,1)S(1)} %pad_maximum_fusion), channel_id=1, source_target_pairs={{0,1},{1,0},{2,3},{3,2},{4,5},{5,4},{6,7},{7,6},{8,9},{9,8},{10,11... | collective-permute-start | bytes 1572872 | tf_op jit(solution)/shard_map/ppermute | solution.py:45
  23.8 0.0 collective-permute-done.16.refs_7_
  23.8 1.3 %collective-permute-done.17.refs_8_ = bf16[16,4096]{1,0:T(8,128)(2,1)S(1)} collective-permute-done((bf16[16,4096]{1,0:T(8,128)(2,1)S(1)}, bf16[16,4096]{1,0:T(8,128)(2,1)S(1)}, u32[]{:S(2)}, u32[]{:S(2)}) %collective-permute-start.17) | collective-permute-done | bytes 131104 | tf_op jit(solution)/shard_map/ppermute | solution.py:42
  25.1 1.5 %collective-permute-start.18 = (bf16[64,4096]{1,0:T(8,128)(2,1)S(1)}, bf16[64,4096]{1,0:T(8,128)(2,1)S(1)}, u32[]{:S(2)}, u32[]{:S(2)}) collective-permute-start(bf16[64,4096]{1,0:T(8,128)(2,1)S(1)} %pad_maximum_fusion.1), channel_id=1, source_target_pairs={{0,1},{1,0},{2,3},{3,2},{4,5},{5,4},{6,7},{7,6},{8,9},{9,8},{10,11... | collective-permute-start | bytes 1572872 | tf_op jit(solution)/shard_map/ppermute | solution.py:45
  26.6 0.0 collective-permute-done.13.refs_9_
  26.6 0.0 collective-permute-done.9.refs_4_
  26.6 0.0 copy-done
  26.7 2.3 %shard_map.38 = (bf16[512,4096]{1,0:T(8,128)(2,1)S(1)}, f32[1,4096]{1,0:T(1,128)S(1)}, f32[1,512]{1,0:T(1,128)S(1)}) custom-call(bf16[512,4096]{1,0:T(8,128)(2,1)S(1)} %copy-done, f32[1,4096]{1,0:T(1,128)S(1)} %shard_map.37.first_total, bf16[16,4096]{1,0:T(8,128)(2,1)S(1)} %collective-permute-done.rows.refs_0_, ...), custom_call_target="tpu_custom_call" | custom-call | flops 1073741824 | bytes 6291456 | tf_op jit(solution)/shard_map/pallas_call | solution.py:208
  29.0 0.0 collective-permute-done.18.refs_9_
  29.0 2.0 %shard_map.39 = f32[1,512]{1,0:T(1,128)} custom-call(f32[1,512]{1,0:T(1,128)S(1)} %get-tuple-element.12.ref_log, bf16[512,4096]{1,0:T(8,128)(2,1)S(1)} %get-tuple-element.13.probes, f32[1,4096]{1,0:T(1,128)S(1)} %get-tuple-element.14.mean, bf16[16,4096]{1,0:T(8,128)(2,1)S(1)} %collective-permute-done.5.refs_0_, ...), custom_call_target="tpu_custom_call" | custom-call | flops 1073741824 | bytes 6291456 | tf_op jit(solution)/shard_map/pallas_call | solution.py:208
  (10 shorter events, 0.2 us)
Async XLA Ops:
  0.0 26.6 %copy-start = (bf16[512,4096]{1,0:T(8,128)(2,1)S(1)}, bf16[512,4096]{1,0:T(8,128)(2,1)}, u32[]{:S(2)}) copy-start(bf16[512,4096]{1,0:T(8,128)(2,1)} %queries.1) | copy-start | bytes 12582916
  0.0 4.0 %collective-permute-start = (bf16[16,4096]{1,0:T(8,128)(2,1)}, bf16[16,4096]{1,0:T(8,128)(2,1)S(1)}, u32[]{:S(2)}, u32[]{:S(2)}) collective-permute-start(bf16[16,4096]{1,0:T(8,128)(2,1)} %param.5), channel_id=1, source_target_pairs={{0,1},{1,0},{2,3},{3,2},{4,5},{5,4},{6,7},{7,6},{8,9},{9,8},{10,11... | collective-permute-start | bytes 393224 | tf_op jit(solution)/shard_map/ppermute | solution.py:45
  0.1 5.6 %collective-permute-start.3 = (bf16[16,4096]{1,0:T(8,128)(2,1)}, bf16[16,4096]{1,0:T(8,128)(2,1)S(1)}, u32[]{:S(2)}, u32[]{:S(2)}) collective-permute-start(bf16[16,4096]{1,0:T(8,128)(2,1)} %param.5), channel_id=1, source_target_pairs={{0,4},{1,3},{4,8},{5,1},{8,12},{9,5},{12,14},{13,9},{14,10},{15,13... | collective-permute-start | bytes 393224 | tf_op jit(solution)/shard_map/ppermute | solution.py:42
  2.7 4.4 %collective-permute-start.5 = (bf16[16,4096]{1,0:T(8,128)(2,1)}, bf16[16,4096]{1,0:T(8,128)(2,1)S(1)}, u32[]{:S(2)}, u32[]{:S(2)}) collective-permute-start(bf16[16,4096]{1,0:T(8,128)(2,1)} %param.4), channel_id=1, source_target_pairs={{0,1},{1,0},{2,3},{3,2},{4,5},{5,4},{6,7},{7,6},{8,9},{9,8},{10,11... | collective-permute-start | bytes 393224 | tf_op jit(solution)/shard_map/ppermute | solution.py:45
  3.1 5.4 %collective-permute-start.6 = (bf16[16,4096]{1,0:T(8,128)(2,1)}, bf16[16,4096]{1,0:T(8,128)(2,1)S(1)}, u32[]{:S(2)}, u32[]{:S(2)}) collective-permute-start(bf16[16,4096]{1,0:T(8,128)(2,1)} %param.4), channel_id=1, source_target_pairs={{0,4},{1,3},{4,8},{5,1},{8,12},{9,5},{12,14},{13,9},{14,10},{15,13... | collective-permute-start | bytes 393224 | tf_op jit(solution)/shard_map/ppermute | solution.py:42
  4.1 5.8 %collective-permute-start.1 = (bf16[16,4096]{1,0:T(8,128)(2,1)S(1)}, bf16[16,4096]{1,0:T(8,128)(2,1)S(1)}, u32[]{:S(2)}, u32[]{:S(2)}) collective-permute-start(bf16[16,4096]{1,0:T(8,128)(2,1)S(1)} %collective-permute-done.rows.refs_0_), channel_id=1, source_target_pairs={{0,4},{1,3},{4,8},{5,1},{8,12},{9,5},{12,14},{13,9},{14,10},{15,13... | collective-permute-start | bytes 393224 | tf_op jit(solution)/shard_map/ppermute | solution.py:42
  5.7 5.4 %collective-permute-start.4 = (bf16[16,4096]{1,0:T(8,128)(2,1)S(1)}, bf16[16,4096]{1,0:T(8,128)(2,1)S(1)}, u32[]{:S(2)}, u32[]{:S(2)}) collective-permute-start(bf16[16,4096]{1,0:T(8,128)(2,1)S(1)} %collective-permute-done.3.refs_1_), channel_id=1, source_target_pairs={{0,4},{1,3},{4,8},{5,1},{8,12},{9,5},{12,14},{13,9},{14,10},{15,13... | collective-permute-start | bytes 393224 | tf_op jit(solution)/shard_map/ppermute | solution.py:42
  7.2 4.5 %collective-permute-start.7 = (bf16[16,4096]{1,0:T(8,128)(2,1)S(1)}, bf16[16,4096]{1,0:T(8,128)(2,1)S(1)}, u32[]{:S(2)}, u32[]{:S(2)}) collective-permute-start(bf16[16,4096]{1,0:T(8,128)(2,1)S(1)} %collective-permute-done.5.refs_0_), channel_id=1, source_target_pairs={{0,4},{1,3},{4,8},{5,1},{8,12},{9,5},{12,14},{13,9},{14,10},{15,13... | collective-permute-start | bytes 393224 | tf_op jit(solution)/shard_map/ppermute | solution.py:42
  8.5 4.5 %collective-permute-start.8 = (bf16[16,4096]{1,0:T(8,128)(2,1)S(1)}, bf16[16,4096]{1,0:T(8,128)(2,1)S(1)}, u32[]{:S(2)}, u32[]{:S(2)}) collective-permute-start(bf16[16,4096]{1,0:T(8,128)(2,1)S(1)} %collective-permute-done.6.refs_1_), channel_id=1, source_target_pairs={{0,4},{1,3},{4,8},{5,1},{8,12},{9,5},{12,14},{13,9},{14,10},{15,13... | collective-permute-start | bytes 393224 | tf_op jit(solution)/shard_map/ppermute | solution.py:42
  9.8 4.7 %collective-permute-start.2 = (bf16[16,4096]{1,0:T(8,128)(2,1)S(1)}, bf16[16,4096]{1,0:T(8,128)(2,1)S(1)}, u32[]{:S(2)}, u32[]{:S(2)}) collective-permute-start(bf16[16,4096]{1,0:T(8,128)(2,1)S(1)} %collective-permute-done.1.refs_2_), channel_id=1, source_target_pairs={{0,4},{1,3},{4,8},{5,1},{8,12},{9,5},{12,14},{13,9},{14,10},{15,13... | collective-permute-start | bytes 393224 | tf_op jit(solution)/shard_map/ppermute | solution.py:42
  11.1 4.8 %collective-permute-start.10 = (bf16[16,4096]{1,0:T(8,128)(2,1)S(1)}, bf16[16,4096]{1,0:T(8,128)(2,1)S(1)}, u32[]{:S(2)}, u32[]{:S(2)}) collective-permute-start(bf16[16,4096]{1,0:T(8,128)(2,1)S(1)} %collective-permute-done.4.refs_3_), channel_id=1, source_target_pairs={{0,4},{1,3},{4,8},{5,1},{8,12},{9,5},{12,14},{13,9},{14,10},{15,13... | collective-permute-start | bytes 393224 | tf_op jit(solution)/shard_map/ppermute | solution.py:42
  11.7 7.9 %collective-permute-start.14 = (bf16[16,4096]{1,0:T(8,128)(2,1)S(1)}, bf16[16,4096]{1,0:T(8,128)(2,1)S(1)}, u32[]{:S(2)}, u32[]{:S(2)}) collective-permute-start(bf16[16,4096]{1,0:T(8,128)(2,1)S(1)} %collective-permute-done.7.refs_2_), channel_id=1, source_target_pairs={{0,4},{1,3},{4,8},{5,1},{8,12},{9,5},{12,14},{13,9},{14,10},{15,13... | collective-permute-start | bytes 393224 | tf_op jit(solution)/shard_map/ppermute | solution.py:42
  13.0 7.0 %collective-permute-start.15 = (bf16[16,4096]{1,0:T(8,128)(2,1)S(1)}, bf16[16,4096]{1,0:T(8,128)(2,1)S(1)}, u32[]{:S(2)}, u32[]{:S(2)}) collective-permute-start(bf16[16,4096]{1,0:T(8,128)(2,1)S(1)} %collective-permute-done.8.refs_3_), channel_id=1, source_target_pairs={{0,4},{1,3},{4,8},{5,1},{8,12},{9,5},{12,14},{13,9},{14,10},{15,13... | collective-permute-start | bytes 393224 | tf_op jit(solution)/shard_map/ppermute | solution.py:42
  14.5 5.9 %collective-permute-start.11 = (bf16[16,4096]{1,0:T(8,128)(2,1)S(1)}, bf16[16,4096]{1,0:T(8,128)(2,1)S(1)}, u32[]{:S(2)}, u32[]{:S(2)}) collective-permute-start(bf16[16,4096]{1,0:T(8,128)(2,1)S(1)} %collective-permute-done.2.refs_5_), channel_id=1, source_target_pairs={{0,4},{1,3},{4,8},{5,1},{8,12},{9,5},{12,14},{13,9},{14,10},{15,13... | collective-permute-start | bytes 393224 | tf_op jit(solution)/shard_map/ppermute | solution.py:42
  15.9 5.6 %collective-permute-start.12 = (bf16[16,4096]{1,0:T(8,128)(2,1)S(1)}, bf16[16,4096]{1,0:T(8,128)(2,1)S(1)}, u32[]{:S(2)}, u32[]{:S(2)}) collective-permute-start(bf16[16,4096]{1,0:T(8,128)(2,1)S(1)} %collective-permute-done.10.refs_6_), channel_id=1, source_target_pairs={{0,4},{1,3},{4,8},{5,1},{8,12},{9,5},{12,14},{13,9},{14,10},{15,13... | collective-permute-start | bytes 393224 | tf_op jit(solution)/shard_map/ppermute | solution.py:42
  16.9 9.7 %collective-permute-start.9 = (bf16[128,4096]{1,0:T(8,128)(2,1)S(1)}, bf16[128,4096]{1,0:T(8,128)(2,1)S(1)}, u32[]{:S(2)}, u32[]{:S(2)}) collective-permute-start(bf16[128,4096]{1,0:T(8,128)(2,1)S(1)} %constant_dynamic-update-slice_fusion), channel_id=1, source_target_pairs={{0,1},{1,0},{2,3},{3,2},{4,5},{5,4},{6,7},{7,6},{8,9},{9,8},{10,11... | collective-permute-start | bytes 3145736 | tf_op jit(solution)/shard_map/ppermute | solution.py:45
  19.6 4.2 %collective-permute-start.16 = (bf16[16,4096]{1,0:T(8,128)(2,1)S(1)}, bf16[16,4096]{1,0:T(8,128)(2,1)S(1)}, u32[]{:S(2)}, u32[]{:S(2)}) collective-permute-start(bf16[16,4096]{1,0:T(8,128)(2,1)S(1)} %collective-permute-done.14.refs_5_), channel_id=1, source_target_pairs={{0,4},{1,3},{4,8},{5,1},{8,12},{9,5},{12,14},{13,9},{14,10},{15,13... | collective-permute-start | bytes 393224 | tf_op jit(solution)/shard_map/ppermute | solution.py:42
  20.0 5.1 %collective-permute-start.17 = (bf16[16,4096]{1,0:T(8,128)(2,1)S(1)}, bf16[16,4096]{1,0:T(8,128)(2,1)S(1)}, u32[]{:S(2)}, u32[]{:S(2)}) collective-permute-start(bf16[16,4096]{1,0:T(8,128)(2,1)S(1)} %collective-permute-done.15.refs_6_), channel_id=1, source_target_pairs={{0,4},{1,3},{4,8},{5,1},{8,12},{9,5},{12,14},{13,9},{14,10},{15,13... | collective-permute-start | bytes 393224 | tf_op jit(solution)/shard_map/ppermute | solution.py:42
  21.5 5.1 %collective-permute-start.13 = (bf16[64,4096]{1,0:T(8,128)(2,1)S(1)}, bf16[64,4096]{1,0:T(8,128)(2,1)S(1)}, u32[]{:S(2)}, u32[]{:S(2)}) collective-permute-start(bf16[64,4096]{1,0:T(8,128)(2,1)S(1)} %pad_maximum_fusion), channel_id=1, source_target_pairs={{0,1},{1,0},{2,3},{3,2},{4,5},{5,4},{6,7},{7,6},{8,9},{9,8},{10,11... | collective-permute-start | bytes 1572872 | tf_op jit(solution)/shard_map/ppermute | solution.py:45
  25.1 3.8 %collective-permute-start.18 = (bf16[64,4096]{1,0:T(8,128)(2,1)S(1)}, bf16[64,4096]{1,0:T(8,128)(2,1)S(1)}, u32[]{:S(2)}, u32[]{:S(2)}) collective-permute-start(bf16[64,4096]{1,0:T(8,128)(2,1)S(1)} %pad_maximum_fusion.1), channel_id=1, source_target_pairs={{0,1},{1,0},{2,3},{3,2},{4,5},{5,4},{6,7},{7,6},{8,9},{9,8},{10,11... | collective-permute-start | bytes 1572872 | tf_op jit(solution)/shard_map/ppermute | solution.py:45

commit v15 on v14

--- a/solution.py
+++ b/solution.py
@@ -9,8 +9,8 @@
 
 TEMP = 64
 LANES = 128
-CHUNK = 1024
-GROUP = 32
+CHUNK = 512
+GROUP = 16
 BLOCK = 256
 LIMIT = 40 * 2**20
 
@@ -134,7 +134,7 @@
 
 def log_sum(squares, scores, queries):
     half = 0.5 * jnp.sum(squares[...], axis=1, keepdims=True)
-    x = (scores[:, queries] - half) / TEMP
+    x = (scores[:, queries] - half) * (1 / TEMP)
     top = jnp.max(x, axis=0, keepdims=True)
     return jnp.log(jnp.sum(jnp.exp(x - top), axis=0, keepdims=True)) + top
 
@@ -167,7 +167,7 @@
         for ref, rows, _ in groups:
             if ref is not panel[0]:
                 total += jnp.sum(ref[rows, cols].astype(jnp.float32), axis=0, keepdims=True)
-        mean[:, cols] = total / count
+        mean[:, cols] = total * (1 / count) if count & (count - 1) == 0 else total / count
 
     def center_queries(rows, cols):
         probes[rows, cols] = center(queries[rows, cols], mean[:, cols])

time: 31.2 us -> 31.5 us (level)
  Pallas kernels: 4.44 us -> 4.78 us
    pallas_call x2, Pallas kernels: 4.39 us -> 4.73 us  [call(): pl.pallas_call(functools.partial(kernel, spans), out_shape=out_shape, in_...]
  transfers between devices with their start and end apart: 19 -> 19, of which waited for: 7 -> 7; matrix products, arithmetic and copies ran while one was open for 1% -> 1% of each run, Pallas kernels for 8% -> 9%
where the time goes in v15:
time: 31.5 us; the launch traced here: 31.4 us
  starting transfers between devices  22.3 us (71%)
  Pallas kernels  4.78 us (15%)
  waiting for transfers between devices  4.04 us (13%)
    ppermute x14, starting transfers between devices, hop(): return lax.ppermute(block, 'samp', ring)  15.4 us
    ppermute x5, starting transfers between devices, hand_over(): return lax.ppermute(block, 'samp', twins)  6.88 us
    pallas_call x2, Pallas kernels, call(): pl.pallas_call(functools.partial(kernel, spans), out_shape=out_shape, in_...  4.73 us
    ppermute x14, waiting for transfers between devices, hop(): return lax.ppermute(block, 'samp', ring)  4.03 us
  transfers between devices with their start and end apart: 19, of which 7 were waited for; matrix products, arithmetic and copies ran while one was open for 1% of the time, Pallas kernels for 9%

profile of v15, /device:TPU:1, one launch (start us, length us, event | category | flops | bytes accessed | tf_op | source)
XLA Modules:
  0.0 31.4 jit_solution(7376193707952271264)
XLA Ops:
  0.0 0.0 copy-start
  0.0 0.1 collective-permute-start
  0.1 2.7 %collective-permute-start.3 = (bf16[16,4096]{1,0:T(8,128)(2,1)}, bf16[16,4096]{1,0:T(8,128)(2,1)S(1)}, u32[]{:S(2)}, u32[]{:S(2)}) collective-permute-start(bf16[16,4096]{1,0:T(8,128)(2,1)} %param.5), channel_id=1, source_target_pairs={{0,4},{1,3},{4,8},{5,1},{8,12},{9,5},{12,14},{13,9},{14,10},{15,13... | collective-permute-start | bytes 393224 | tf_op jit(solution)/shard_map/ppermute | solution.py:42
  2.7 0.4 %collective-permute-start.5 = (bf16[16,4096]{1,0:T(8,128)(2,1)}, bf16[16,4096]{1,0:T(8,128)(2,1)S(1)}, u32[]{:S(2)}, u32[]{:S(2)}) collective-permute-start(bf16[16,4096]{1,0:T(8,128)(2,1)} %param.4), channel_id=1, source_target_pairs={{0,1},{1,0},{2,3},{3,2},{4,5},{5,4},{6,7},{7,6},{8,9},{9,8},{10,11... | collective-permute-start | bytes 393224 | tf_op jit(solution)/shard_map/ppermute | solution.py:45
  3.1 0.9 %collective-permute-start.6 = (bf16[16,4096]{1,0:T(8,128)(2,1)}, bf16[16,4096]{1,0:T(8,128)(2,1)S(1)}, u32[]{:S(2)}, u32[]{:S(2)}) collective-permute-start(bf16[16,4096]{1,0:T(8,128)(2,1)} %param.4), channel_id=1, source_target_pairs={{0,4},{1,3},{4,8},{5,1},{8,12},{9,5},{12,14},{13,9},{14,10},{15,13... | collective-permute-start | bytes 393224 | tf_op jit(solution)/shard_map/ppermute | solution.py:42
  4.0 0.0 collective-permute-done.rows.refs_0_
  4.1 1.3 %collective-permute-start.1 = (bf16[16,4096]{1,0:T(8,128)(2,1)S(1)}, bf16[16,4096]{1,0:T(8,128)(2,1)S(1)}, u32[]{:S(2)}, u32[]{:S(2)}) collective-permute-start(bf16[16,4096]{1,0:T(8,128)(2,1)S(1)} %collective-permute-done.rows.refs_0_), channel_id=1, source_target_pairs={{0,4},{1,3},{4,8},{5,1},{8,12},{9,5},{12,14},{13,9},{14,10},{15,13... | collective-permute-start | bytes 393224 | tf_op jit(solution)/shard_map/ppermute | solution.py:42
  5.4 0.3 collective-permute-done.3.refs_1_
  5.7 1.4 %collective-permute-start.4 = (bf16[16,4096]{1,0:T(8,128)(2,1)S(1)}, bf16[16,4096]{1,0:T(8,128)(2,1)S(1)}, u32[]{:S(2)}, u32[]{:S(2)}) collective-permute-start(bf16[16,4096]{1,0:T(8,128)(2,1)S(1)} %collective-permute-done.3.refs_1_), channel_id=1, source_target_pairs={{0,4},{1,3},{4,8},{5,1},{8,12},{9,5},{12,14},{13,9},{14,10},{15,13... | collective-permute-start | bytes 393224 | tf_op jit(solution)/shard_map/ppermute | solution.py:42
  7.1 0.1 shard_map.37.first_total
  7.1 0.0 collective-permute-done.5.refs_0_
  7.2 1.3 %collective-permute-start.7 = (bf16[16,4096]{1,0:T(8,128)(2,1)S(1)}, bf16[16,4096]{1,0:T(8,128)(2,1)S(1)}, u32[]{:S(2)}, u32[]{:S(2)}) collective-permute-start(bf16[16,4096]{1,0:T(8,128)(2,1)S(1)} %collective-permute-done.5.refs_0_), channel_id=1, source_target_pairs={{0,4},{1,3},{4,8},{5,1},{8,12},{9,5},{12,14},{13,9},{14,10},{15,13... | collective-permute-start | bytes 393224 | tf_op jit(solution)/shard_map/ppermute | solution.py:42
  8.5 0.0 collective-permute-done.6.refs_1_
  8.5 1.3 %collective-permute-start.8 = (bf16[16,4096]{1,0:T(8,128)(2,1)S(1)}, bf16[16,4096]{1,0:T(8,128)(2,1)S(1)}, u32[]{:S(2)}, u32[]{:S(2)}) collective-permute-start(bf16[16,4096]{1,0:T(8,128)(2,1)S(1)} %collective-permute-done.6.refs_1_), channel_id=1, source_target_pairs={{0,4},{1,3},{4,8},{5,1},{8,12},{9,5},{12,14},{13,9},{14,10},{15,13... | collective-permute-start | bytes 393224 | tf_op jit(solution)/shard_map/ppermute | solution.py:42
  9.8 0.0 collective-permute-done.1.refs_2_
  9.8 1.3 %collective-permute-start.2 = (bf16[16,4096]{1,0:T(8,128)(2,1)S(1)}, bf16[16,4096]{1,0:T(8,128)(2,1)S(1)}, u32[]{:S(2)}, u32[]{:S(2)}) collective-permute-start(bf16[16,4096]{1,0:T(8,128)(2,1)S(1)} %collective-permute-done.1.refs_2_), channel_id=1, source_target_pairs={{0,4},{1,3},{4,8},{5,1},{8,12},{9,5},{12,14},{13,9},{14,10},{15,13... | collective-permute-start | bytes 393224 | tf_op jit(solution)/shard_map/ppermute | solution.py:42
  11.1 0.0 collective-permute-done.4.refs_3_
  11.1 0.2 collective-permute-start.10
  11.4 0.3 collective-permute-done.7.refs_2_
  11.7 1.0 %collective-permute-start.14 = (bf16[16,4096]{1,0:T(8,128)(2,1)S(1)}, bf16[16,4096]{1,0:T(8,128)(2,1)S(1)}, u32[]{:S(2)}, u32[]{:S(2)}) collective-permute-start(bf16[16,4096]{1,0:T(8,128)(2,1)S(1)} %collective-permute-done.7.refs_2_), channel_id=1, source_target_pairs={{0,4},{1,3},{4,8},{5,1},{8,12},{9,5},{12,14},{13,9},{14,10},{15,13... | collective-permute-start | bytes 393224 | tf_op jit(solution)/shard_map/ppermute | solution.py:42
  12.7 0.3 collective-permute-done.8.refs_3_
  13.0 1.1 %collective-permute-start.15 = (bf16[16,4096]{1,0:T(8,128)(2,1)S(1)}, bf16[16,4096]{1,0:T(8,128)(2,1)S(1)}, u32[]{:S(2)}, u32[]{:S(2)}) collective-permute-start(bf16[16,4096]{1,0:T(8,128)(2,1)S(1)} %collective-permute-done.8.refs_3_), channel_id=1, source_target_pairs={{0,4},{1,3},{4,8},{5,1},{8,12},{9,5},{12,14},{13,9},{14,10},{15,13... | collective-permute-start | bytes 393224 | tf_op jit(solution)/shard_map/ppermute | solution.py:42
  14.1 0.4 %collective-permute-done.2.refs_5_ = bf16[16,4096]{1,0:T(8,128)(2,1)S(1)} collective-permute-done((bf16[16,4096]{1,0:T(8,128)(2,1)S(1)}, bf16[16,4096]{1,0:T(8,128)(2,1)S(1)}, u32[]{:S(2)}, u32[]{:S(2)}) %collective-permute-start.2) | collective-permute-done | bytes 131104 | tf_op jit(solution)/shard_map/ppermute | solution.py:42
  14.5 1.0 %collective-permute-start.11 = (bf16[16,4096]{1,0:T(8,128)(2,1)S(1)}, bf16[16,4096]{1,0:T(8,128)(2,1)S(1)}, u32[]{:S(2)}, u32[]{:S(2)}) collective-permute-start(bf16[16,4096]{1,0:T(8,128)(2,1)S(1)} %collective-permute-done.2.refs_5_), channel_id=1, source_target_pairs={{0,4},{1,3},{4,8},{5,1},{8,12},{9,5},{12,14},{13,9},{14,10},{15,13... | collective-permute-start | bytes 393224 | tf_op jit(solution)/shard_map/ppermute | solution.py:42
  15.5 0.4 %collective-permute-done.10.refs_6_ = bf16[16,4096]{1,0:T(8,128)(2,1)S(1)} collective-permute-done((bf16[16,4096]{1,0:T(8,128)(2,1)S(1)}, bf16[16,4096]{1,0:T(8,128)(2,1)S(1)}, u32[]{:S(2)}, u32[]{:S(2)}) %collective-permute-start.10) | collective-permute-done | bytes 131104 | tf_op jit(solution)/shard_map/ppermute | solution.py:42
  15.9 1.0 %collective-permute-start.12 = (bf16[16,4096]{1,0:T(8,128)(2,1)S(1)}, bf16[16,4096]{1,0:T(8,128)(2,1)S(1)}, u32[]{:S(2)}, u32[]{:S(2)}) collective-permute-start(bf16[16,4096]{1,0:T(8,128)(2,1)S(1)} %collective-permute-done.10.refs_6_), channel_id=1, source_target_pairs={{0,4},{1,3},{4,8},{5,1},{8,12},{9,5},{12,14},{13,9},{14,10},{15,13... | collective-permute-start | bytes 393224 | tf_op jit(solution)/shard_map/ppermute | solution.py:42
  16.9 2.7 %collective-permute-start.9 = (bf16[128,4096]{1,0:T(8,128)(2,1)S(1)}, bf16[128,4096]{1,0:T(8,128)(2,1)S(1)}, u32[]{:S(2)}, u32[]{:S(2)}) collective-permute-start(bf16[128,4096]{1,0:T(8,128)(2,1)S(1)} %constant_dynamic-update-slice_fusion), channel_id=1, source_target_pairs={{0,1},{1,0},{2,3},{3,2},{4,5},{5,4},{6,7},{7,6},{8,9},{9,8},{10,11... | collective-permute-start | bytes 3145736 | tf_op jit(solution)/shard_map/ppermute | solution.py:45
  19.6 0.0 collective-permute-done.14.refs_5_
  19.6 0.4 %collective-permute-start.16 = (bf16[16,4096]{1,0:T(8,128)(2,1)S(1)}, bf16[16,4096]{1,0:T(8,128)(2,1)S(1)}, u32[]{:S(2)}, u32[]{:S(2)}) collective-permute-start(bf16[16,4096]{1,0:T(8,128)(2,1)S(1)} %collective-permute-done.14.refs_5_), channel_id=1, source_target_pairs={{0,4},{1,3},{4,8},{5,1},{8,12},{9,5},{12,14},{13,9},{14,10},{15,13... | collective-permute-start | bytes 393224 | tf_op jit(solution)/shard_map/ppermute | solution.py:42
  20.0 0.0 collective-permute-done.15.refs_6_
  20.0 0.4 %collective-permute-start.17 = (bf16[16,4096]{1,0:T(8,128)(2,1)S(1)}, bf16[16,4096]{1,0:T(8,128)(2,1)S(1)}, u32[]{:S(2)}, u32[]{:S(2)}) collective-permute-start(bf16[16,4096]{1,0:T(8,128)(2,1)S(1)} %collective-permute-done.15.refs_6_), channel_id=1, source_target_pairs={{0,4},{1,3},{4,8},{5,1},{8,12},{9,5},{12,14},{13,9},{14,10},{15,13... | collective-permute-start | bytes 393224 | tf_op jit(solution)/shard_map/ppermute | solution.py:42
  20.4 0.0 collective-permute-done.11.refs_7_
  20.4 1.1 %collective-permute-done.12.refs_8_ = bf16[16,4096]{1,0:T(8,128)(2,1)S(1)} collective-permute-done((bf16[16,4096]{1,0:T(8,128)(2,1)S(1)}, bf16[16,4096]{1,0:T(8,128)(2,1)S(1)}, u32[]{:S(2)}, u32[]{:S(2)}) %collective-permute-start.12) | collective-permute-done | bytes 131104 | tf_op jit(solution)/shard_map/ppermute | solution.py:42
  21.5 2.3 %collective-permute-start.13 = (bf16[64,4096]{1,0:T(8,128)(2,1)S(1)}, bf16[64,4096]{1,0:T(8,128)(2,1)S(1)}, u32[]{:S(2)}, u32[]{:S(2)}) collective-permute-start(bf16[64,4096]{1,0:T(8,128)(2,1)S(1)} %pad_maximum_fusion), channel_id=1, source_target_pairs={{0,1},{1,0},{2,3},{3,2},{4,5},{5,4},{6,7},{7,6},{8,9},{9,8},{10,11... | collective-permute-start | bytes 1572872 | tf_op jit(solution)/shard_map/ppermute | solution.py:45
  23.8 0.0 collective-permute-done.16.refs_7_
  23.8 1.3 %collective-permute-done.17.refs_8_ = bf16[16,4096]{1,0:T(8,128)(2,1)S(1)} collective-permute-done((bf16[16,4096]{1,0:T(8,128)(2,1)S(1)}, bf16[16,4096]{1,0:T(8,128)(2,1)S(1)}, u32[]{:S(2)}, u32[]{:S(2)}) %collective-permute-start.17) | collective-permute-done | bytes 131104 | tf_op jit(solution)/shard_map/ppermute | solution.py:42
  25.1 1.5 %collective-permute-start.18 = (bf16[64,4096]{1,0:T(8,128)(2,1)S(1)}, bf16[64,4096]{1,0:T(8,128)(2,1)S(1)}, u32[]{:S(2)}, u32[]{:S(2)}) collective-permute-start(bf16[64,4096]{1,0:T(8,128)(2,1)S(1)} %pad_maximum_fusion.1), channel_id=1, source_target_pairs={{0,1},{1,0},{2,3},{3,2},{4,5},{5,4},{6,7},{7,6},{8,9},{9,8},{10,11... | collective-permute-start | bytes 1572872 | tf_op jit(solution)/shard_map/ppermute | solution.py:45
  26.6 0.0 collective-permute-done.13.refs_9_
  26.6 0.0 collective-permute-done.9.refs_4_
  26.6 0.0 copy-done
  26.7 2.7 %shard_map.38 = (bf16[512,4096]{1,0:T(8,128)(2,1)S(1)}, f32[1,4096]{1,0:T(1,128)S(1)}, f32[1,512]{1,0:T(1,128)S(1)}) custom-call(bf16[512,4096]{1,0:T(8,128)(2,1)S(1)} %copy-done, f32[1,4096]{1,0:T(1,128)S(1)} %shard_map.37.first_total, bf16[16,4096]{1,0:T(8,128)(2,1)S(1)} %collective-permute-done.rows.refs_0_, ...), custom_call_target="tpu_custom_call" | custom-call | flops 1073741824 | bytes 6291456 | tf_op jit(solution)/shard_map/pallas_call | solution.py:208
  29.3 0.0 collective-permute-done.18.refs_9_
  29.3 2.1 %shard_map.39 = f32[1,512]{1,0:T(1,128)} custom-call(f32[1,512]{1,0:T(1,128)S(1)} %get-tuple-element.12.ref_log, bf16[512,4096]{1,0:T(8,128)(2,1)S(1)} %get-tuple-element.13.probes, f32[1,4096]{1,0:T(1,128)S(1)} %get-tuple-element.14.mean, bf16[16,4096]{1,0:T(8,128)(2,1)S(1)} %collective-permute-done.5.refs_0_, ...), custom_call_target="tpu_custom_call" | custom-call | flops 1073741824 | bytes 6291456 | tf_op jit(solution)/shard_map/pallas_call | solution.py:208
  (10 shorter events, 0.2 us)
Async XLA Ops:
  0.0 26.6 %copy-start = (bf16[512,4096]{1,0:T(8,128)(2,1)S(1)}, bf16[512,4096]{1,0:T(8,128)(2,1)}, u32[]{:S(2)}) copy-start(bf16[512,4096]{1,0:T(8,128)(2,1)} %queries.1) | copy-start | bytes 12582916
  0.0 4.0 %collective-permute-start = (bf16[16,4096]{1,0:T(8,128)(2,1)}, bf16[16,4096]{1,0:T(8,128)(2,1)S(1)}, u32[]{:S(2)}, u32[]{:S(2)}) collective-permute-start(bf16[16,4096]{1,0:T(8,128)(2,1)} %param.5), channel_id=1, source_target_pairs={{0,1},{1,0},{2,3},{3,2},{4,5},{5,4},{6,7},{7,6},{8,9},{9,8},{10,11... | collective-permute-start | bytes 393224 | tf_op jit(solution)/shard_map/ppermute | solution.py:45
  0.1 5.6 %collective-permute-start.3 = (bf16[16,4096]{1,0:T(8,128)(2,1)}, bf16[16,4096]{1,0:T(8,128)(2,1)S(1)}, u32[]{:S(2)}, u32[]{:S(2)}) collective-permute-start(bf16[16,4096]{1,0:T(8,128)(2,1)} %param.5), channel_id=1, source_target_pairs={{0,4},{1,3},{4,8},{5,1},{8,12},{9,5},{12,14},{13,9},{14,10},{15,13... | collective-permute-start | bytes 393224 | tf_op jit(solution)/shard_map/ppermute | solution.py:42
  2.7 4.4 %collective-permute-start.5 = (bf16[16,4096]{1,0:T(8,128)(2,1)}, bf16[16,4096]{1,0:T(8,128)(2,1)S(1)}, u32[]{:S(2)}, u32[]{:S(2)}) collective-permute-start(bf16[16,4096]{1,0:T(8,128)(2,1)} %param.4), channel_id=1, source_target_pairs={{0,1},{1,0},{2,3},{3,2},{4,5},{5,4},{6,7},{7,6},{8,9},{9,8},{10,11... | collective-permute-start | bytes 393224 | tf_op jit(solution)/shard_map/ppermute | solution.py:45
  3.1 5.4 %collective-permute-start.6 = (bf16[16,4096]{1,0:T(8,128)(2,1)}, bf16[16,4096]{1,0:T(8,128)(2,1)S(1)}, u32[]{:S(2)}, u32[]{:S(2)}) collective-permute-start(bf16[16,4096]{1,0:T(8,128)(2,1)} %param.4), channel_id=1, source_target_pairs={{0,4},{1,3},{4,8},{5,1},{8,12},{9,5},{12,14},{13,9},{14,10},{15,13... | collective-permute-start | bytes 393224 | tf_op jit(solution)/shard_map/ppermute | solution.py:42
  4.1 5.8 %collective-permute-start.1 = (bf16[16,4096]{1,0:T(8,128)(2,1)S(1)}, bf16[16,4096]{1,0:T(8,128)(2,1)S(1)}, u32[]{:S(2)}, u32[]{:S(2)}) collective-permute-start(bf16[16,4096]{1,0:T(8,128)(2,1)S(1)} %collective-permute-done.rows.refs_0_), channel_id=1, source_target_pairs={{0,4},{1,3},{4,8},{5,1},{8,12},{9,5},{12,14},{13,9},{14,10},{15,13... | collective-permute-start | bytes 393224 | tf_op jit(solution)/shard_map/ppermute | solution.py:42
  5.7 5.4 %collective-permute-start.4 = (bf16[16,4096]{1,0:T(8,128)(2,1)S(1)}, bf16[16,4096]{1,0:T(8,128)(2,1)S(1)}, u32[]{:S(2)}, u32[]{:S(2)}) collective-permute-start(bf16[16,4096]{1,0:T(8,128)(2,1)S(1)} %collective-permute-done.3.refs_1_), channel_id=1, source_target_pairs={{0,4},{1,3},{4,8},{5,1},{8,12},{9,5},{12,14},{13,9},{14,10},{15,13... | collective-permute-start | bytes 393224 | tf_op jit(solution)/shard_map/ppermute | solution.py:42
  7.2 4.5 %collective-permute-start.7 = (bf16[16,4096]{1,0:T(8,128)(2,1)S(1)}, bf16[16,4096]{1,0:T(8,128)(2,1)S(1)}, u32[]{:S(2)}, u32[]{:S(2)}) collective-permute-start(bf16[16,4096]{1,0:T(8,128)(2,1)S(1)} %collective-permute-done.5.refs_0_), channel_id=1, source_target_pairs={{0,4},{1,3},{4,8},{5,1},{8,12},{9,5},{12,14},{13,9},{14,10},{15,13... | collective-permute-start | bytes 393224 | tf_op jit(solution)/shard_map/ppermute | solution.py:42
  8.5 4.5 %collective-permute-start.8 = (bf16[16,4096]{1,0:T(8,128)(2,1)S(1)}, bf16[16,4096]{1,0:T(8,128)(2,1)S(1)}, u32[]{:S(2)}, u32[]{:S(2)}) collective-permute-start(bf16[16,4096]{1,0:T(8,128)(2,1)S(1)} %collective-permute-done.6.refs_1_), channel_id=1, source_target_pairs={{0,4},{1,3},{4,8},{5,1},{8,12},{9,5},{12,14},{13,9},{14,10},{15,13... | collective-permute-start | bytes 393224 | tf_op jit(solution)/shard_map/ppermute | solution.py:42
  9.8 4.7 %collective-permute-start.2 = (bf16[16,4096]{1,0:T(8,128)(2,1)S(1)}, bf16[16,4096]{1,0:T(8,128)(2,1)S(1)}, u32[]{:S(2)}, u32[]{:S(2)}) collective-permute-start(bf16[16,4096]{1,0:T(8,128)(2,1)S(1)} %collective-permute-done.1.refs_2_), channel_id=1, source_target_pairs={{0,4},{1,3},{4,8},{5,1},{8,12},{9,5},{12,14},{13,9},{14,10},{15,13... | collective-permute-start | bytes 393224 | tf_op jit(solution)/shard_map/ppermute | solution.py:42
  11.1 4.8 %collective-permute-start.10 = (bf16[16,4096]{1,0:T(8,128)(2,1)S(1)}, bf16[16,4096]{1,0:T(8,128)(2,1)S(1)}, u32[]{:S(2)}, u32[]{:S(2)}) collective-permute-start(bf16[16,4096]{1,0:T(8,128)(2,1)S(1)} %collective-permute-done.4.refs_3_), channel_id=1, source_target_pairs={{0,4},{1,3},{4,8},{5,1},{8,12},{9,5},{12,14},{13,9},{14,10},{15,13... | collective-permute-start | bytes 393224 | tf_op jit(solution)/shard_map/ppermute | solution.py:42
  11.7 7.9 %collective-permute-start.14 = (bf16[16,4096]{1,0:T(8,128)(2,1)S(1)}, bf16[16,4096]{1,0:T(8,128)(2,1)S(1)}, u32[]{:S(2)}, u32[]{:S(2)}) collective-permute-start(bf16[16,4096]{1,0:T(8,128)(2,1)S(1)} %collective-permute-done.7.refs_2_), channel_id=1, source_target_pairs={{0,4},{1,3},{4,8},{5,1},{8,12},{9,5},{12,14},{13,9},{14,10},{15,13... | collective-permute-start | bytes 393224 | tf_op jit(solution)/shard_map/ppermute | solution.py:42
  13.0 7.0 %collective-permute-start.15 = (bf16[16,4096]{1,0:T(8,128)(2,1)S(1)}, bf16[16,4096]{1,0:T(8,128)(2,1)S(1)}, u32[]{:S(2)}, u32[]{:S(2)}) collective-permute-start(bf16[16,4096]{1,0:T(8,128)(2,1)S(1)} %collective-permute-done.8.refs_3_), channel_id=1, source_target_pairs={{0,4},{1,3},{4,8},{5,1},{8,12},{9,5},{12,14},{13,9},{14,10},{15,13... | collective-permute-start | bytes 393224 | tf_op jit(solution)/shard_map/ppermute | solution.py:42
  14.5 5.9 %collective-permute-start.11 = (bf16[16,4096]{1,0:T(8,128)(2,1)S(1)}, bf16[16,4096]{1,0:T(8,128)(2,1)S(1)}, u32[]{:S(2)}, u32[]{:S(2)}) collective-permute-start(bf16[16,4096]{1,0:T(8,128)(2,1)S(1)} %collective-permute-done.2.refs_5_), channel_id=1, source_target_pairs={{0,4},{1,3},{4,8},{5,1},{8,12},{9,5},{12,14},{13,9},{14,10},{15,13... | collective-permute-start | bytes 393224 | tf_op jit(solution)/shard_map/ppermute | solution.py:42
  15.9 5.6 %collective-permute-start.12 = (bf16[16,4096]{1,0:T(8,128)(2,1)S(1)}, bf16[16,4096]{1,0:T(8,128)(2,1)S(1)}, u32[]{:S(2)}, u32[]{:S(2)}) collective-permute-start(bf16[16,4096]{1,0:T(8,128)(2,1)S(1)} %collective-permute-done.10.refs_6_), channel_id=1, source_target_pairs={{0,4},{1,3},{4,8},{5,1},{8,12},{9,5},{12,14},{13,9},{14,10},{15,13... | collective-permute-start | bytes 393224 | tf_op jit(solution)/shard_map/ppermute | solution.py:42
  16.9 9.7 %collective-permute-start.9 = (bf16[128,4096]{1,0:T(8,128)(2,1)S(1)}, bf16[128,4096]{1,0:T(8,128)(2,1)S(1)}, u32[]{:S(2)}, u32[]{:S(2)}) collective-permute-start(bf16[128,4096]{1,0:T(8,128)(2,1)S(1)} %constant_dynamic-update-slice_fusion), channel_id=1, source_target_pairs={{0,1},{1,0},{2,3},{3,2},{4,5},{5,4},{6,7},{7,6},{8,9},{9,8},{10,11... | collective-permute-start | bytes 3145736 | tf_op jit(solution)/shard_map/ppermute | solution.py:45
  19.6 4.2 %collective-permute-start.16 = (bf16[16,4096]{1,0:T(8,128)(2,1)S(1)}, bf16[16,4096]{1,0:T(8,128)(2,1)S(1)}, u32[]{:S(2)}, u32[]{:S(2)}) collective-permute-start(bf16[16,4096]{1,0:T(8,128)(2,1)S(1)} %collective-permute-done.14.refs_5_), channel_id=1, source_target_pairs={{0,4},{1,3},{4,8},{5,1},{8,12},{9,5},{12,14},{13,9},{14,10},{15,13... | collective-permute-start | bytes 393224 | tf_op jit(solution)/shard_map/ppermute | solution.py:42
  20.0 5.1 %collective-permute-start.17 = (bf16[16,4096]{1,0:T(8,128)(2,1)S(1)}, bf16[16,4096]{1,0:T(8,128)(2,1)S(1)}, u32[]{:S(2)}, u32[]{:S(2)}) collective-permute-start(bf16[16,4096]{1,0:T(8,128)(2,1)S(1)} %collective-permute-done.15.refs_6_), channel_id=1, source_target_pairs={{0,4},{1,3},{4,8},{5,1},{8,12},{9,5},{12,14},{13,9},{14,10},{15,13... | collective-permute-start | bytes 393224 | tf_op jit(solution)/shard_map/ppermute | solution.py:42
  21.5 5.1 %collective-permute-start.13 = (bf16[64,4096]{1,0:T(8,128)(2,1)S(1)}, bf16[64,4096]{1,0:T(8,128)(2,1)S(1)}, u32[]{:S(2)}, u32[]{:S(2)}) collective-permute-start(bf16[64,4096]{1,0:T(8,128)(2,1)S(1)} %pad_maximum_fusion), channel_id=1, source_target_pairs={{0,1},{1,0},{2,3},{3,2},{4,5},{5,4},{6,7},{7,6},{8,9},{9,8},{10,11... | collective-permute-start | bytes 1572872 | tf_op jit(solution)/shard_map/ppermute | solution.py:45
  25.1 4.2 %collective-permute-start.18 = (bf16[64,4096]{1,0:T(8,128)(2,1)S(1)}, bf16[64,4096]{1,0:T(8,128)(2,1)S(1)}, u32[]{:S(2)}, u32[]{:S(2)}) collective-permute-start(bf16[64,4096]{1,0:T(8,128)(2,1)S(1)} %pad_maximum_fusion.1), channel_id=1, source_target_pairs={{0,1},{1,0},{2,3},{3,2},{4,5},{5,4},{6,7},{7,6},{8,9},{9,8},{10,11... | collective-permute-start | bytes 1572872 | tf_op jit(solution)/shard_map/ppermute | solution.py:45

commit v16 on v9

--- a/solution.py
+++ b/solution.py
@@ -50,7 +50,7 @@
     for period in range(steps + 1):
         last = period == steps
         if last and period:
-            mine[-1], extra = lax.optimization_barrier((mine[-1], extra))
+            other[0], extra = lax.optimization_barrier((other[0], extra))
         other = [hop(o) for o in other] if period else [hand_over(p) for p in panels]
         if not period:
             extra = on_first(other[0])
@@ -66,7 +66,7 @@
                 if fresh[i]:
                     block = hand_over(jnp.concatenate(fresh[i], axis=0))
                     pieces[i].append((block, 0, block.shape[0]))
-        elif period:
+        elif period and period < steps - 1:
             block, at = hand_over(jnp.concatenate([f for g in fresh for f in g], axis=0)), 0
             for i in range(len(panels)):
                 upto = at + rows * len(fresh[i])
@@ -93,15 +93,12 @@
     return (rows.astype(jnp.float32) - mean).astype(jnp.bfloat16)
 
 
-def center_panel_chunk(cols, mean, groups, centered, squares, first):
-    for ref, rows, here in groups:
-        part = center(ref[rows, cols], mean)
-        centered[here, cols] = part
-        wide = jnp.square(part.astype(jnp.float32))
-        total = wide[:, :LANES]
-        for lane in range(LANES, wide.shape[1], LANES):
-            total += wide[:, lane : lane + LANES]
-        squares[here, :] = total if first else squares[here, :] + total
+def add_squares(rows, cols, centered, squares, first):
+    wide = jnp.square(centered[rows, cols].astype(jnp.float32))
+    total = wide[:, :LANES]
+    for lane in range(LANES, wide.shape[1], LANES):
+        total += wide[:, lane : lane + LANES]
+    squares[rows, :] = total if first else squares[rows, :] + total
 
 
 def add_products(cols, probes, centered, scores, first):
@@ -114,7 +111,7 @@
 
 def log_sum(squares, scores):
     half = 0.5 * jnp.sum(squares[...], axis=1, keepdims=True)
-    x = (scores[...] - half) / TEMP
+    x = (scores[...] - half) * (1 / TEMP)
     top = jnp.max(x, axis=0, keepdims=True)
     return jnp.log(jnp.sum(jnp.exp(x - top), axis=0, keepdims=True)) + top
 
@@ -137,36 +134,43 @@
     )(rows)
 
 
+def chunks(features):
+    return [(slice(start, start + CHUNK), start == 0) for start in range(0, features, CHUNK)]
+
+
 def ref_kernel(spans, queries, first_total, *refs):
-    panel, (probes, mean, ref_log, centered, squares, scores) = refs[: len(spans)], refs[len(spans) :]
+    panel, (probes, mean, centered, scores) = refs[: len(spans)], refs[len(spans) :]
     groups = panel_groups(panel, spans)
     count, features = centered.shape
-    for start in range(0, features, CHUNK):
-        cols = slice(start, start + CHUNK)
+    for cols, first in chunks(features):
         total = first_total[:, cols]
         for ref, rows, _ in groups:
             if ref is not panel[0]:
                 total += jnp.sum(ref[rows, cols].astype(jnp.float32), axis=0, keepdims=True)
         here = total / count
         mean[:, cols] = here
-        center_panel_chunk(cols, here, groups, centered, squares, start == 0)
-        for rows in row_groups(probes.shape[0], GROUP):
+        for ref, rows, to in groups:
+            centered[to, cols] = center(ref[rows, cols], here)
+        for rows in row_groups(queries.shape[0], GROUP):
             probes[rows, cols] = center(queries[rows, cols], here)
-        add_products(cols, probes, centered, scores, start == 0)
-    ref_log[...] = log_sum(squares, scores)
-
-
-def gen_kernel(spans, ref_log, probes, mean, *refs):
-    panel, (proof, centered, squares, scores) = refs[: len(spans)], refs[len(spans) :]
+        add_products(cols, probes, centered, scores, first)
+
+
+def gen_kernel(spans, probes, mean, ref_centered, ref_scores, *refs):
+    panel, (proof, centered, squares, scores, ref_squares) = refs[: len(spans)], refs[len(spans) :]
     groups = panel_groups(panel, spans)
-    for start in range(0, centered.shape[1], CHUNK):
-        cols = slice(start, start + CHUNK)
-        center_panel_chunk(cols, mean[:, cols], groups, centered, squares, start == 0)
-        add_products(cols, probes, centered, scores, start == 0)
-    proof[...] = log_sum(squares, scores) - ref_log[...]
-
-
-def call(kernel, before, pieces, count, out_shape):
+    for cols, first in chunks(centered.shape[1]):
+        for ref, rows, to in groups:
+            centered[to, cols] = center(ref[rows, cols], mean[:, cols])
+            add_squares(to, cols, centered, squares, first)
+        add_products(cols, probes, centered, scores, first)
+        for rows in row_groups(ref_centered.shape[0], GROUP):
+            add_squares(rows, cols, ref_centered, ref_squares, first)
+    ref_log = log_sum(ref_squares, ref_scores)
+    proof[...] = log_sum(squares, scores) - ref_log
+
+
+def call(kernel, before, pieces, count, out_shape, scratch):
     spans = [(low, high) for _, low, high in pieces]
     operands = [*before, *(array for array, _, _ in pieces)]
     rows, features = sum(high - low for low, high in spans), operands[-1].shape[1]
@@ -176,11 +180,7 @@
         out_shape=out_shape,
         in_specs=[in_vmem] * len(operands),
         out_specs=jax.tree.map(lambda _: in_vmem, out_shape),
-        scratch_shapes=[
-            pltpu.VMEM((rows, features), jnp.bfloat16),
-            pltpu.VMEM((rows, LANES), jnp.float32),
-            pltpu.VMEM((rows, count), jnp.float32),
-        ],
+        scratch_shapes=[pltpu.VMEM(s.shape, s.dtype) for s in scratch],
         compiler_params=pltpu.CompilerParams(vmem_limit_bytes=LIMIT),
         cost_estimate=pl.CostEstimate(
             flops=2 * rows * count * features,
@@ -191,24 +191,20 @@
 
 
 def body(queries, gen_panel, ref_panel):
-    panels = [ref_panel, gen_panel]
+    panels, size = [ref_panel, gen_panel], lax.axis_size("samp")
     (ref_pieces, gen_pieces), first_total = gather_panels(
-        panels, lax.axis_size("samp"), functools.partial(feature_total, beside=queries)
+        panels, size, functools.partial(feature_total, beside=queries)
     )
     count, features = queries.shape
-    logs = jax.ShapeDtypeStruct((1, count), jnp.float32)
-    probes, mean, ref_log = call(
-        ref_kernel,
-        [queries, first_total],
-        ref_pieces,
-        count,
-        (
-            jax.ShapeDtypeStruct((count, features), jnp.bfloat16),
-            jax.ShapeDtypeStruct((1, features), jnp.float32),
-            logs,
-        ),
-    )
-    return call(gen_kernel, [ref_log, probes, mean], gen_pieces, count, logs).reshape(-1)
+    rows = size * ref_panel.shape[0]
+    float32 = functools.partial(jax.ShapeDtypeStruct, dtype=jnp.float32)
+    centered = jax.ShapeDtypeStruct((rows, features), jnp.bfloat16)
+    squares, scores = float32((rows, LANES)), float32((rows, count))
+    probes = jax.ShapeDtypeStruct((count, features), jnp.bfloat16)
+    outputs = (probes, float32((1, features)), centered, scores)
+    before = call(ref_kernel, [queries, first_total], ref_pieces, count, outputs, [])
+    scratch = [centered, squares, scores, squares]
+    return call(gen_kernel, before, gen_pieces, count, float32((1, count)), scratch).reshape(-1)
 
 
 def solution(mesh):

time: 32.1 us -> 31.5 us (0.981)
  starting transfers between devices: 22.8 us -> 22.3 us
  waiting for transfers between devices: 4.55 us -> 4.05 us
  Pallas kernels: 4.41 us -> 4.79 us
    ppermute x6 -> x5, starting transfers between devices: 7.58 us -> 6.88 us  [hand_over(): return lax.ppermute(block, 'samp', twins)]
    ppermute x14, waiting for transfers between devices: 4.53 us -> 4.04 us  [hop(): return lax.ppermute(block, 'samp', ring)]
    pallas_call x2, Pallas kernels: 4.35 us -> 4.73 us  [call(): pl.pallas_call(functools.partial(kernel, spans), out_shape=out_shape, in_...]
  transfers between devices with their start and end apart: 20 -> 19, of which waited for: 6 -> 7; matrix products, arithmetic and copies ran while one was open for 0% -> 0% of each run, Pallas kernels for 7% -> 7%
where the time goes in v16:
time: 31.5 us; the launch traced here: 31.4 us
  starting transfers between devices  22.3 us (71%)
  Pallas kernels  4.79 us (15%)
  waiting for transfers between devices  4.05 us (13%)
    ppermute x14, starting transfers between devices, hop(): return lax.ppermute(block, 'samp', ring)  15.4 us
    ppermute x5, starting transfers between devices, hand_over(): return lax.ppermute(block, 'samp', twins)  6.88 us
    pallas_call x2, Pallas kernels, call(): pl.pallas_call(functools.partial(kernel, spans), out_shape=out_shape, in_...  4.73 us
    ppermute x14, waiting for transfers between devices, hop(): return lax.ppermute(block, 'samp', ring)  4.04 us
  transfers between devices with their start and end apart: 19, of which 7 were waited for; matrix products, arithmetic and copies ran while one was open for 0% of the time, Pallas kernels for 7%

profile of v16, /device:TPU:1, one launch (start us, length us, event | category | flops | bytes accessed | tf_op | source)
XLA Modules:
  0.0 31.4 jit_solution(16143049748624525090)
XLA Ops:
  0.0 0.0 copy-start
  0.0 0.1 collective-permute-start
  0.1 2.7 %collective-permute-start.3 = (bf16[16,4096]{1,0:T(8,128)(2,1)}, bf16[16,4096]{1,0:T(8,128)(2,1)S(1)}, u32[]{:S(2)}, u32[]{:S(2)}) collective-permute-start(bf16[16,4096]{1,0:T(8,128)(2,1)} %param.5), channel_id=1, source_target_pairs={{0,4},{1,3},{4,8},{5,1},{8,12},{9,5},{12,14},{13,9},{14,10},{15,13... | collective-permute-start | bytes 393224 | tf_op jit(solution)/shard_map/ppermute | solution.py:41
  2.7 0.4 %collective-permute-start.5 = (bf16[16,4096]{1,0:T(8,128)(2,1)}, bf16[16,4096]{1,0:T(8,128)(2,1)S(1)}, u32[]{:S(2)}, u32[]{:S(2)}) collective-permute-start(bf16[16,4096]{1,0:T(8,128)(2,1)} %param.4), channel_id=1, source_target_pairs={{0,1},{1,0},{2,3},{3,2},{4,5},{5,4},{6,7},{7,6},{8,9},{9,8},{10,11... | collective-permute-start | bytes 393224 | tf_op jit(solution)/shard_map/ppermute | solution.py:44
  3.1 0.9 %collective-permute-start.6 = (bf16[16,4096]{1,0:T(8,128)(2,1)}, bf16[16,4096]{1,0:T(8,128)(2,1)S(1)}, u32[]{:S(2)}, u32[]{:S(2)}) collective-permute-start(bf16[16,4096]{1,0:T(8,128)(2,1)} %param.4), channel_id=1, source_target_pairs={{0,4},{1,3},{4,8},{5,1},{8,12},{9,5},{12,14},{13,9},{14,10},{15,13... | collective-permute-start | bytes 393224 | tf_op jit(solution)/shard_map/ppermute | solution.py:41
  4.0 0.0 collective-permute-done.rows.refs_0_
  4.1 1.3 %collective-permute-start.1 = (bf16[16,4096]{1,0:T(8,128)(2,1)S(1)}, bf16[16,4096]{1,0:T(8,128)(2,1)S(1)}, u32[]{:S(2)}, u32[]{:S(2)}) collective-permute-start(bf16[16,4096]{1,0:T(8,128)(2,1)S(1)} %collective-permute-done.rows.refs_0_), channel_id=1, source_target_pairs={{0,4},{1,3},{4,8},{5,1},{8,12},{9,5},{12,14},{13,9},{14,10},{15,13... | collective-permute-start | bytes 393224 | tf_op jit(solution)/shard_map/ppermute | solution.py:41
  5.4 0.3 collective-permute-done.3.refs_1_
  5.7 1.4 %collective-permute-start.4 = (bf16[16,4096]{1,0:T(8,128)(2,1)S(1)}, bf16[16,4096]{1,0:T(8,128)(2,1)S(1)}, u32[]{:S(2)}, u32[]{:S(2)}) collective-permute-start(bf16[16,4096]{1,0:T(8,128)(2,1)S(1)} %collective-permute-done.3.refs_1_), channel_id=1, source_target_pairs={{0,4},{1,3},{4,8},{5,1},{8,12},{9,5},{12,14},{13,9},{14,10},{15,13... | collective-permute-start | bytes 393224 | tf_op jit(solution)/shard_map/ppermute | solution.py:41
  7.1 0.1 shard_map.37.first_total
  7.1 0.0 collective-permute-done.5.refs_0_
  7.2 1.3 %collective-permute-start.7 = (bf16[16,4096]{1,0:T(8,128)(2,1)S(1)}, bf16[16,4096]{1,0:T(8,128)(2,1)S(1)}, u32[]{:S(2)}, u32[]{:S(2)}) collective-permute-start(bf16[16,4096]{1,0:T(8,128)(2,1)S(1)} %collective-permute-done.5.refs_0_), channel_id=1, source_target_pairs={{0,4},{1,3},{4,8},{5,1},{8,12},{9,5},{12,14},{13,9},{14,10},{15,13... | collective-permute-start | bytes 393224 | tf_op jit(solution)/shard_map/ppermute | solution.py:41
  8.5 0.0 collective-permute-done.6.refs_1_
  8.5 1.3 %collective-permute-start.8 = (bf16[16,4096]{1,0:T(8,128)(2,1)S(1)}, bf16[16,4096]{1,0:T(8,128)(2,1)S(1)}, u32[]{:S(2)}, u32[]{:S(2)}) collective-permute-start(bf16[16,4096]{1,0:T(8,128)(2,1)S(1)} %collective-permute-done.6.refs_1_), channel_id=1, source_target_pairs={{0,4},{1,3},{4,8},{5,1},{8,12},{9,5},{12,14},{13,9},{14,10},{15,13... | collective-permute-start | bytes 393224 | tf_op jit(solution)/shard_map/ppermute | solution.py:41
  9.8 0.0 collective-permute-done.1.refs_2_
  9.8 1.3 %collective-permute-start.2 = (bf16[16,4096]{1,0:T(8,128)(2,1)S(1)}, bf16[16,4096]{1,0:T(8,128)(2,1)S(1)}, u32[]{:S(2)}, u32[]{:S(2)}) collective-permute-start(bf16[16,4096]{1,0:T(8,128)(2,1)S(1)} %collective-permute-done.1.refs_2_), channel_id=1, source_target_pairs={{0,4},{1,3},{4,8},{5,1},{8,12},{9,5},{12,14},{13,9},{14,10},{15,13... | collective-permute-start | bytes 393224 | tf_op jit(solution)/shard_map/ppermute | solution.py:41
  11.1 0.0 collective-permute-done.4.refs_3_
  11.1 0.2 collective-permute-start.10
  11.4 0.3 collective-permute-done.7.refs_2_
  11.7 1.0 %collective-permute-start.14 = (bf16[16,4096]{1,0:T(8,128)(2,1)S(1)}, bf16[16,4096]{1,0:T(8,128)(2,1)S(1)}, u32[]{:S(2)}, u32[]{:S(2)}) collective-permute-start(bf16[16,4096]{1,0:T(8,128)(2,1)S(1)} %collective-permute-done.7.refs_2_), channel_id=1, source_target_pairs={{0,4},{1,3},{4,8},{5,1},{8,12},{9,5},{12,14},{13,9},{14,10},{15,13... | collective-permute-start | bytes 393224 | tf_op jit(solution)/shard_map/ppermute | solution.py:41
  12.7 0.3 collective-permute-done.8.refs_3_
  13.0 1.1 %collective-permute-start.15 = (bf16[16,4096]{1,0:T(8,128)(2,1)S(1)}, bf16[16,4096]{1,0:T(8,128)(2,1)S(1)}, u32[]{:S(2)}, u32[]{:S(2)}) collective-permute-start(bf16[16,4096]{1,0:T(8,128)(2,1)S(1)} %collective-permute-done.8.refs_3_), channel_id=1, source_target_pairs={{0,4},{1,3},{4,8},{5,1},{8,12},{9,5},{12,14},{13,9},{14,10},{15,13... | collective-permute-start | bytes 393224 | tf_op jit(solution)/shard_map/ppermute | solution.py:41
  14.1 0.4 %collective-permute-done.2.refs_5_ = bf16[16,4096]{1,0:T(8,128)(2,1)S(1)} collective-permute-done((bf16[16,4096]{1,0:T(8,128)(2,1)S(1)}, bf16[16,4096]{1,0:T(8,128)(2,1)S(1)}, u32[]{:S(2)}, u32[]{:S(2)}) %collective-permute-start.2) | collective-permute-done | bytes 131104 | tf_op jit(solution)/shard_map/ppermute | solution.py:41
  14.5 1.0 %collective-permute-start.11 = (bf16[16,4096]{1,0:T(8,128)(2,1)S(1)}, bf16[16,4096]{1,0:T(8,128)(2,1)S(1)}, u32[]{:S(2)}, u32[]{:S(2)}) collective-permute-start(bf16[16,4096]{1,0:T(8,128)(2,1)S(1)} %collective-permute-done.2.refs_5_), channel_id=1, source_target_pairs={{0,4},{1,3},{4,8},{5,1},{8,12},{9,5},{12,14},{13,9},{14,10},{15,13... | collective-permute-start | bytes 393224 | tf_op jit(solution)/shard_map/ppermute | solution.py:41
  15.5 0.4 %collective-permute-done.10.refs_6_ = bf16[16,4096]{1,0:T(8,128)(2,1)S(1)} collective-permute-done((bf16[16,4096]{1,0:T(8,128)(2,1)S(1)}, bf16[16,4096]{1,0:T(8,128)(2,1)S(1)}, u32[]{:S(2)}, u32[]{:S(2)}) %collective-permute-start.10) | collective-permute-done | bytes 131104 | tf_op jit(solution)/shard_map/ppermute | solution.py:41
  15.9 1.0 %collective-permute-start.12 = (bf16[16,4096]{1,0:T(8,128)(2,1)S(1)}, bf16[16,4096]{1,0:T(8,128)(2,1)S(1)}, u32[]{:S(2)}, u32[]{:S(2)}) collective-permute-start(bf16[16,4096]{1,0:T(8,128)(2,1)S(1)} %collective-permute-done.10.refs_6_), channel_id=1, source_target_pairs={{0,4},{1,3},{4,8},{5,1},{8,12},{9,5},{12,14},{13,9},{14,10},{15,13... | collective-permute-start | bytes 393224 | tf_op jit(solution)/shard_map/ppermute | solution.py:41
  16.9 2.7 %collective-permute-start.9 = (bf16[128,4096]{1,0:T(8,128)(2,1)S(1)}, bf16[128,4096]{1,0:T(8,128)(2,1)S(1)}, u32[]{:S(2)}, u32[]{:S(2)}) collective-permute-start(bf16[128,4096]{1,0:T(8,128)(2,1)S(1)} %constant_dynamic-update-slice_fusion), channel_id=1, source_target_pairs={{0,1},{1,0},{2,3},{3,2},{4,5},{5,4},{6,7},{7,6},{8,9},{9,8},{10,11... | collective-permute-start | bytes 3145736 | tf_op jit(solution)/shard_map/ppermute | solution.py:44
  19.6 0.0 collective-permute-done.14.refs_5_
  19.6 0.4 %collective-permute-start.16 = (bf16[16,4096]{1,0:T(8,128)(2,1)S(1)}, bf16[16,4096]{1,0:T(8,128)(2,1)S(1)}, u32[]{:S(2)}, u32[]{:S(2)}) collective-permute-start(bf16[16,4096]{1,0:T(8,128)(2,1)S(1)} %collective-permute-done.14.refs_5_), channel_id=1, source_target_pairs={{0,4},{1,3},{4,8},{5,1},{8,12},{9,5},{12,14},{13,9},{14,10},{15,13... | collective-permute-start | bytes 393224 | tf_op jit(solution)/shard_map/ppermute | solution.py:41
  20.0 0.0 collective-permute-done.15.refs_6_
  20.0 0.4 %collective-permute-start.17 = (bf16[16,4096]{1,0:T(8,128)(2,1)S(1)}, bf16[16,4096]{1,0:T(8,128)(2,1)S(1)}, u32[]{:S(2)}, u32[]{:S(2)}) collective-permute-start(bf16[16,4096]{1,0:T(8,128)(2,1)S(1)} %collective-permute-done.15.refs_6_), channel_id=1, source_target_pairs={{0,4},{1,3},{4,8},{5,1},{8,12},{9,5},{12,14},{13,9},{14,10},{15,13... | collective-permute-start | bytes 393224 | tf_op jit(solution)/shard_map/ppermute | solution.py:41
  20.4 0.0 collective-permute-done.11.refs_7_
  20.4 1.1 %collective-permute-done.12.refs_8_ = bf16[16,4096]{1,0:T(8,128)(2,1)S(1)} collective-permute-done((bf16[16,4096]{1,0:T(8,128)(2,1)S(1)}, bf16[16,4096]{1,0:T(8,128)(2,1)S(1)}, u32[]{:S(2)}, u32[]{:S(2)}) %collective-permute-start.12) | collective-permute-done | bytes 131104 | tf_op jit(solution)/shard_map/ppermute | solution.py:41
  21.5 2.3 %collective-permute-start.13 = (bf16[64,4096]{1,0:T(8,128)(2,1)S(1)}, bf16[64,4096]{1,0:T(8,128)(2,1)S(1)}, u32[]{:S(2)}, u32[]{:S(2)}) collective-permute-start(bf16[64,4096]{1,0:T(8,128)(2,1)S(1)} %pad_maximum_fusion), channel_id=1, source_target_pairs={{0,1},{1,0},{2,3},{3,2},{4,5},{5,4},{6,7},{7,6},{8,9},{9,8},{10,11... | collective-permute-start | bytes 1572872 | tf_op jit(solution)/shard_map/ppermute | solution.py:44
  23.8 0.0 collective-permute-done.16.refs_7_
  23.8 1.3 %collective-permute-done.17.refs_8_ = bf16[16,4096]{1,0:T(8,128)(2,1)S(1)} collective-permute-done((bf16[16,4096]{1,0:T(8,128)(2,1)S(1)}, bf16[16,4096]{1,0:T(8,128)(2,1)S(1)}, u32[]{:S(2)}, u32[]{:S(2)}) %collective-permute-start.17) | collective-permute-done | bytes 131104 | tf_op jit(solution)/shard_map/ppermute | solution.py:41
  25.1 1.5 %collective-permute-start.18 = (bf16[64,4096]{1,0:T(8,128)(2,1)S(1)}, bf16[64,4096]{1,0:T(8,128)(2,1)S(1)}, u32[]{:S(2)}, u32[]{:S(2)}) collective-permute-start(bf16[64,4096]{1,0:T(8,128)(2,1)S(1)} %pad_maximum_fusion.1), channel_id=1, source_target_pairs={{0,1},{1,0},{2,3},{3,2},{4,5},{5,4},{6,7},{7,6},{8,9},{9,8},{10,11... | collective-permute-start | bytes 1572872 | tf_op jit(solution)/shard_map/ppermute | solution.py:44
  26.6 0.0 collective-permute-done.13.refs_9_
  26.6 0.0 collective-permute-done.9.refs_4_
  26.6 0.0 copy-done
  26.6 2.1 %shard_map.38 = (bf16[512,4096]{1,0:T(8,128)(2,1)S(1)}, f32[1,4096]{1,0:T(1,128)S(1)}, bf16[256,4096]{1,0:T(8,128)(2,1)S(1)}, f32[256,512]{1,0:T(8,128)S(1)}) custom-call(bf16[512,4096]{1,0:T(8,128)(2,1)S(1)} %copy-done, f32[1,4096]{1,0:T(1,128)S(1)} %shard_map.37.first_total, bf16[16,4096]{1,0:T(8,128)(2,1)S(1)} %collective-permute-done.rows.refs_0_, ...), custom_call_target="tpu_custom_call" | custom-call | flops 1073741824 | bytes 6291456 | tf_op jit(solution)/shard_map/pallas_call | solution.py:178
  28.8 0.0 collective-permute-done.18.refs_9_
  28.8 2.6 %shard_map.39 = f32[1,512]{1,0:T(1,128)} custom-call(bf16[512,4096]{1,0:T(8,128)(2,1)S(1)} %get-tuple-element.13.probes, f32[1,4096]{1,0:T(1,128)S(1)} %get-tuple-element.14.mean, bf16[256,4096]{1,0:T(8,128)(2,1)S(1)} %get-tuple-element.15.ref_centered, f32[256,512]{1,0:T(8,128)S(1)} %get-tuple-element.16.ref_scores, ...), custom_call_target="tpu_custom_call" | custom-call | flops 1073741824 | bytes 6291456 | tf_op jit(solution)/shard_map/pallas_call | solution.py:178
  (10 shorter events, 0.1 us)
Async XLA Ops:
  0.0 26.6 %copy-start = (bf16[512,4096]{1,0:T(8,128)(2,1)S(1)}, bf16[512,4096]{1,0:T(8,128)(2,1)}, u32[]{:S(2)}) copy-start(bf16[512,4096]{1,0:T(8,128)(2,1)} %queries.1) | copy-start | bytes 12582916
  0.0 4.0 %collective-permute-start = (bf16[16,4096]{1,0:T(8,128)(2,1)}, bf16[16,4096]{1,0:T(8,128)(2,1)S(1)}, u32[]{:S(2)}, u32[]{:S(2)}) collective-permute-start(bf16[16,4096]{1,0:T(8,128)(2,1)} %param.5), channel_id=1, source_target_pairs={{0,1},{1,0},{2,3},{3,2},{4,5},{5,4},{6,7},{7,6},{8,9},{9,8},{10,11... | collective-permute-start | bytes 393224 | tf_op jit(solution)/shard_map/ppermute | solution.py:44
  0.1 5.6 %collective-permute-start.3 = (bf16[16,4096]{1,0:T(8,128)(2,1)}, bf16[16,4096]{1,0:T(8,128)(2,1)S(1)}, u32[]{:S(2)}, u32[]{:S(2)}) collective-permute-start(bf16[16,4096]{1,0:T(8,128)(2,1)} %param.5), channel_id=1, source_target_pairs={{0,4},{1,3},{4,8},{5,1},{8,12},{9,5},{12,14},{13,9},{14,10},{15,13... | collective-permute-start | bytes 393224 | tf_op jit(solution)/shard_map/ppermute | solution.py:41
  2.7 4.4 %collective-permute-start.5 = (bf16[16,4096]{1,0:T(8,128)(2,1)}, bf16[16,4096]{1,0:T(8,128)(2,1)S(1)}, u32[]{:S(2)}, u32[]{:S(2)}) collective-permute-start(bf16[16,4096]{1,0:T(8,128)(2,1)} %param.4), channel_id=1, source_target_pairs={{0,1},{1,0},{2,3},{3,2},{4,5},{5,4},{6,7},{7,6},{8,9},{9,8},{10,11... | collective-permute-start | bytes 393224 | tf_op jit(solution)/shard_map/ppermute | solution.py:44
  3.1 5.4 %collective-permute-start.6 = (bf16[16,4096]{1,0:T(8,128)(2,1)}, bf16[16,4096]{1,0:T(8,128)(2,1)S(1)}, u32[]{:S(2)}, u32[]{:S(2)}) collective-permute-start(bf16[16,4096]{1,0:T(8,128)(2,1)} %param.4), channel_id=1, source_target_pairs={{0,4},{1,3},{4,8},{5,1},{8,12},{9,5},{12,14},{13,9},{14,10},{15,13... | collective-permute-start | bytes 393224 | tf_op jit(solution)/shard_map/ppermute | solution.py:41
  4.1 5.8 %collective-permute-start.1 = (bf16[16,4096]{1,0:T(8,128)(2,1)S(1)}, bf16[16,4096]{1,0:T(8,128)(2,1)S(1)}, u32[]{:S(2)}, u32[]{:S(2)}) collective-permute-start(bf16[16,4096]{1,0:T(8,128)(2,1)S(1)} %collective-permute-done.rows.refs_0_), channel_id=1, source_target_pairs={{0,4},{1,3},{4,8},{5,1},{8,12},{9,5},{12,14},{13,9},{14,10},{15,13... | collective-permute-start | bytes 393224 | tf_op jit(solution)/shard_map/ppermute | solution.py:41
  5.7 5.4 %collective-permute-start.4 = (bf16[16,4096]{1,0:T(8,128)(2,1)S(1)}, bf16[16,4096]{1,0:T(8,128)(2,1)S(1)}, u32[]{:S(2)}, u32[]{:S(2)}) collective-permute-start(bf16[16,4096]{1,0:T(8,128)(2,1)S(1)} %collective-permute-done.3.refs_1_), channel_id=1, source_target_pairs={{0,4},{1,3},{4,8},{5,1},{8,12},{9,5},{12,14},{13,9},{14,10},{15,13... | collective-permute-start | bytes 393224 | tf_op jit(solution)/shard_map/ppermute | solution.py:41
  7.2 4.5 %collective-permute-start.7 = (bf16[16,4096]{1,0:T(8,128)(2,1)S(1)}, bf16[16,4096]{1,0:T(8,128)(2,1)S(1)}, u32[]{:S(2)}, u32[]{:S(2)}) collective-permute-start(bf16[16,4096]{1,0:T(8,128)(2,1)S(1)} %collective-permute-done.5.refs_0_), channel_id=1, source_target_pairs={{0,4},{1,3},{4,8},{5,1},{8,12},{9,5},{12,14},{13,9},{14,10},{15,13... | collective-permute-start | bytes 393224 | tf_op jit(solution)/shard_map/ppermute | solution.py:41
  8.5 4.5 %collective-permute-start.8 = (bf16[16,4096]{1,0:T(8,128)(2,1)S(1)}, bf16[16,4096]{1,0:T(8,128)(2,1)S(1)}, u32[]{:S(2)}, u32[]{:S(2)}) collective-permute-start(bf16[16,4096]{1,0:T(8,128)(2,1)S(1)} %collective-permute-done.6.refs_1_), channel_id=1, source_target_pairs={{0,4},{1,3},{4,8},{5,1},{8,12},{9,5},{12,14},{13,9},{14,10},{15,13... | collective-permute-start | bytes 393224 | tf_op jit(solution)/shard_map/ppermute | solution.py:41
  9.8 4.7 %collective-permute-start.2 = (bf16[16,4096]{1,0:T(8,128)(2,1)S(1)}, bf16[16,4096]{1,0:T(8,128)(2,1)S(1)}, u32[]{:S(2)}, u32[]{:S(2)}) collective-permute-start(bf16[16,4096]{1,0:T(8,128)(2,1)S(1)} %collective-permute-done.1.refs_2_), channel_id=1, source_target_pairs={{0,4},{1,3},{4,8},{5,1},{8,12},{9,5},{12,14},{13,9},{14,10},{15,13... | collective-permute-start | bytes 393224 | tf_op jit(solution)/shard_map/ppermute | solution.py:41
  11.1 4.8 %collective-permute-start.10 = (bf16[16,4096]{1,0:T(8,128)(2,1)S(1)}, bf16[16,4096]{1,0:T(8,128)(2,1)S(1)}, u32[]{:S(2)}, u32[]{:S(2)}) collective-permute-start(bf16[16,4096]{1,0:T(8,128)(2,1)S(1)} %collective-permute-done.4.refs_3_), channel_id=1, source_target_pairs={{0,4},{1,3},{4,8},{5,1},{8,12},{9,5},{12,14},{13,9},{14,10},{15,13... | collective-permute-start | bytes 393224 | tf_op jit(solution)/shard_map/ppermute | solution.py:41
  11.7 7.9 %collective-permute-start.14 = (bf16[16,4096]{1,0:T(8,128)(2,1)S(1)}, bf16[16,4096]{1,0:T(8,128)(2,1)S(1)}, u32[]{:S(2)}, u32[]{:S(2)}) collective-permute-start(bf16[16,4096]{1,0:T(8,128)(2,1)S(1)} %collective-permute-done.7.refs_2_), channel_id=1, source_target_pairs={{0,4},{1,3},{4,8},{5,1},{8,12},{9,5},{12,14},{13,9},{14,10},{15,13... | collective-permute-start | bytes 393224 | tf_op jit(solution)/shard_map/ppermute | solution.py:41
  13.0 7.0 %collective-permute-start.15 = (bf16[16,4096]{1,0:T(8,128)(2,1)S(1)}, bf16[16,4096]{1,0:T(8,128)(2,1)S(1)}, u32[]{:S(2)}, u32[]{:S(2)}) collective-permute-start(bf16[16,4096]{1,0:T(8,128)(2,1)S(1)} %collective-permute-done.8.refs_3_), channel_id=1, source_target_pairs={{0,4},{1,3},{4,8},{5,1},{8,12},{9,5},{12,14},{13,9},{14,10},{15,13... | collective-permute-start | bytes 393224 | tf_op jit(solution)/shard_map/ppermute | solution.py:41
  14.5 5.9 %collective-permute-start.11 = (bf16[16,4096]{1,0:T(8,128)(2,1)S(1)}, bf16[16,4096]{1,0:T(8,128)(2,1)S(1)}, u32[]{:S(2)}, u32[]{:S(2)}) collective-permute-start(bf16[16,4096]{1,0:T(8,128)(2,1)S(1)} %collective-permute-done.2.refs_5_), channel_id=1, source_target_pairs={{0,4},{1,3},{4,8},{5,1},{8,12},{9,5},{12,14},{13,9},{14,10},{15,13... | collective-permute-start | bytes 393224 | tf_op jit(solution)/shard_map/ppermute | solution.py:41
  15.9 5.6 %collective-permute-start.12 = (bf16[16,4096]{1,0:T(8,128)(2,1)S(1)}, bf16[16,4096]{1,0:T(8,128)(2,1)S(1)}, u32[]{:S(2)}, u32[]{:S(2)}) collective-permute-start(bf16[16,4096]{1,0:T(8,128)(2,1)S(1)} %collective-permute-done.10.refs_6_), channel_id=1, source_target_pairs={{0,4},{1,3},{4,8},{5,1},{8,12},{9,5},{12,14},{13,9},{14,10},{15,13... | collective-permute-start | bytes 393224 | tf_op jit(solution)/shard_map/ppermute | solution.py:41
  16.9 9.7 %collective-permute-start.9 = (bf16[128,4096]{1,0:T(8,128)(2,1)S(1)}, bf16[128,4096]{1,0:T(8,128)(2,1)S(1)}, u32[]{:S(2)}, u32[]{:S(2)}) collective-permute-start(bf16[128,4096]{1,0:T(8,128)(2,1)S(1)} %constant_dynamic-update-slice_fusion), channel_id=1, source_target_pairs={{0,1},{1,0},{2,3},{3,2},{4,5},{5,4},{6,7},{7,6},{8,9},{9,8},{10,11... | collective-permute-start | bytes 3145736 | tf_op jit(solution)/shard_map/ppermute | solution.py:44
  19.6 4.2 %collective-permute-start.16 = (bf16[16,4096]{1,0:T(8,128)(2,1)S(1)}, bf16[16,4096]{1,0:T(8,128)(2,1)S(1)}, u32[]{:S(2)}, u32[]{:S(2)}) collective-permute-start(bf16[16,4096]{1,0:T(8,128)(2,1)S(1)} %collective-permute-done.14.refs_5_), channel_id=1, source_target_pairs={{0,4},{1,3},{4,8},{5,1},{8,12},{9,5},{12,14},{13,9},{14,10},{15,13... | collective-permute-start | bytes 393224 | tf_op jit(solution)/shard_map/ppermute | solution.py:41
  20.0 5.1 %collective-permute-start.17 = (bf16[16,4096]{1,0:T(8,128)(2,1)S(1)}, bf16[16,4096]{1,0:T(8,128)(2,1)S(1)}, u32[]{:S(2)}, u32[]{:S(2)}) collective-permute-start(bf16[16,4096]{1,0:T(8,128)(2,1)S(1)} %collective-permute-done.15.refs_6_), channel_id=1, source_target_pairs={{0,4},{1,3},{4,8},{5,1},{8,12},{9,5},{12,14},{13,9},{14,10},{15,13... | collective-permute-start | bytes 393224 | tf_op jit(solution)/shard_map/ppermute | solution.py:41
  21.5 5.1 %collective-permute-start.13 = (bf16[64,4096]{1,0:T(8,128)(2,1)S(1)}, bf16[64,4096]{1,0:T(8,128)(2,1)S(1)}, u32[]{:S(2)}, u32[]{:S(2)}) collective-permute-start(bf16[64,4096]{1,0:T(8,128)(2,1)S(1)} %pad_maximum_fusion), channel_id=1, source_target_pairs={{0,1},{1,0},{2,3},{3,2},{4,5},{5,4},{6,7},{7,6},{8,9},{9,8},{10,11... | collective-permute-start | bytes 1572872 | tf_op jit(solution)/shard_map/ppermute | solution.py:44
  25.1 3.6 %collective-permute-start.18 = (bf16[64,4096]{1,0:T(8,128)(2,1)S(1)}, bf16[64,4096]{1,0:T(8,128)(2,1)S(1)}, u32[]{:S(2)}, u32[]{:S(2)}) collective-permute-start(bf16[64,4096]{1,0:T(8,128)(2,1)S(1)} %pad_maximum_fusion.1), channel_id=1, source_target_pairs={{0,1},{1,0},{2,3},{3,2},{4,5},{5,4},{6,7},{7,6},{8,9},{9,8},{10,11... | collective-permute-start | bytes 1572872 | tf_op jit(solution)/shard_map/ppermute | solution.py:44

commit v17 on v14

--- a/solution.py
+++ b/solution.py
@@ -94,30 +94,33 @@
     return (rows.astype(jnp.float32) - mean).astype(jnp.bfloat16)
 
 
-def center_group(group, cols, mean, centered, squares, first):
+def center_group(group, at, mean, centered, squares):
     ref, rows, here = group
-    part = center(ref[rows, cols], mean[:, cols])
-    centered[here, cols] = part
+    part = center(ref[rows, chunk(at)], mean[:, chunk(at)])
+    centered[at][here, :] = part
     wide = jnp.square(part.astype(jnp.float32))
     total = wide[:, :LANES]
     for lane in range(LANES, wide.shape[1], LANES):
         total += wide[:, lane : lane + LANES]
-    squares[here, :] = total if first else squares[here, :] + total
-
-
-def add_products(cols, queries, probes, centered, scores, first):
+    squares[here, :] = total if at == 0 else squares[here, :] + total
+
+
+def add_products(at, queries, probes, centered, scores):
     products = lax.dot_general(
-        centered[:, cols], probes[queries, cols], (((1,), (1,)), ((), ())),
+        centered[at][...], probes[at][queries, :], (((1,), (1,)), ((), ())),
         preferred_element_type=jnp.float32,
     )
-    scores[:, queries] = products if first else scores[:, queries] + products
-
-
-def interleave(features, prepare, probes, centered, scores):
+    scores[:, queries] = products if at == 0 else scores[:, queries] + products
+
+
+def chunk(at):
+    return slice(at * CHUNK, (at + 1) * CHUNK)
+
+
+def interleave(prepare, probes, centered, scores):
     waiting = []
-    for start in range(0, features, CHUNK):
-        cols, first = slice(start, start + CHUNK), start == 0
-        work = prepare(cols, first)
+    for at in range(len(centered)):
+        work = prepare(at)
         share = -(-len(work) // max(len(waiting), 1))
         for i in range(0, len(work), share):
             if waiting:
@@ -125,8 +128,8 @@
             for step in work[i : i + share]:
                 step()
         waiting += [
-            functools.partial(add_products, cols, queries, probes, centered, scores, first)
-            for queries in row_groups(probes.shape[0], BLOCK)
+            functools.partial(add_products, at, queries, probes, centered, scores)
+            for queries in row_groups(probes[at].shape[0], BLOCK)
         ]
     for step in waiting:
         step()
@@ -134,7 +137,7 @@
 
 def log_sum(squares, scores, queries):
     half = 0.5 * jnp.sum(squares[...], axis=1, keepdims=True)
-    x = (scores[:, queries] - half) / TEMP
+    x = (scores[:, queries] - half) * (1 / TEMP)
     top = jnp.max(x, axis=0, keepdims=True)
     return jnp.log(jnp.sum(jnp.exp(x - top), axis=0, keepdims=True)) + top
 
@@ -157,46 +160,62 @@
     )(rows)
 
 
-def ref_kernel(spans, queries, first_total, *refs):
-    panel, (probes, mean, ref_log, centered, squares, scores) = refs[: len(spans)], refs[len(spans) :]
+def split(refs, *counts):
+    runs = []
+    for count in counts:
+        runs.append(refs[:count])
+        refs = refs[count:]
+    return *runs, refs
+
+
+def ref_kernel(spans, parts, queries, first_total, *refs):
+    panel, probes, centered, (mean, ref_log, squares, scores) = arrange(refs, spans, parts)
     groups = panel_groups(panel, spans)
-    count, features = centered.shape
-
-    def take_mean(cols):
+    count = scores.shape[0]
+
+    def take_mean(at):
+        cols = chunk(at)
         total = first_total[:, cols]
         for ref, rows, _ in groups:
             if ref is not panel[0]:
                 total += jnp.sum(ref[rows, cols].astype(jnp.float32), axis=0, keepdims=True)
         mean[:, cols] = total / count
 
-    def center_queries(rows, cols):
-        probes[rows, cols] = center(queries[rows, cols], mean[:, cols])
-
-    def prepare(cols, first):
-        work = [functools.partial(take_mean, cols)]
+    def center_queries(rows, at):
+        probes[at][rows, :] = center(queries[rows, chunk(at)], mean[:, chunk(at)])
+
+    def prepare(at):
+        work = [functools.partial(take_mean, at)]
         for group in groups:
-            work.append(functools.partial(center_group, group, cols, mean, centered, squares, first))
-        for rows in row_groups(probes.shape[0], GROUP):
-            work.append(functools.partial(center_queries, rows, cols))
+            work.append(functools.partial(center_group, group, at, mean, centered, squares))
+        for rows in row_groups(queries.shape[0], GROUP):
+            work.append(functools.partial(center_queries, rows, at))
         return work
 
-    interleave(features, prepare, probes, centered, scores)
-    for block in row_groups(probes.shape[0], BLOCK):
+    interleave(prepare, probes, centered, scores)
+    for block in row_groups(queries.shape[0], BLOCK):
         ref_log[:, block] = log_sum(squares, scores, block)
 
 
-def gen_kernel(spans, ref_log, probes, mean, *refs):
-    panel, (proof, centered, squares, scores) = refs[: len(spans)], refs[len(spans) :]
+def arrange(refs, spans, parts):
+    panel, probes, (mean, log), centered, rest = split(refs, len(spans), parts, 2, parts)
+    return panel, probes, centered, (mean, log, *rest)
+
+
+def gen_kernel(spans, parts, *refs):
+    probes, (mean, ref_log), panel, (proof,), centered, (squares, scores) = split(
+        refs, parts, 2, len(spans), 1, parts
+    )
     groups = panel_groups(panel, spans)
 
-    def prepare(cols, first):
+    def prepare(at):
         return [
-            functools.partial(center_group, group, cols, mean, centered, squares, first)
+            functools.partial(center_group, group, at, mean, centered, squares)
             for group in groups
         ]
 
-    interleave(centered.shape[1], prepare, probes, centered, scores)
-    for block in row_groups(probes.shape[0], BLOCK):
+    interleave(prepare, probes, centered, scores)
+    for block in row_groups(probes[0].shape[0], BLOCK):
         proof[:, block] = log_sum(squares, scores, block) - ref_log[:, block]
 
 
@@ -204,17 +223,15 @@
     spans = [(low, high) for _, low, high in pieces]
     operands = [*before, *(array for array, _, _ in pieces)]
     rows, features = sum(high - low for low, high in spans), operands[-1].shape[1]
+    parts = features // CHUNK
     in_vmem = pl.BlockSpec(memory_space=pltpu.VMEM)
     return pl.pallas_call(
-        functools.partial(kernel, spans),
+        functools.partial(kernel, spans, parts),
         out_shape=out_shape,
         in_specs=[in_vmem] * len(operands),
         out_specs=jax.tree.map(lambda _: in_vmem, out_shape),
-        scratch_shapes=[
-            pltpu.VMEM((rows, features), jnp.bfloat16),
-            pltpu.VMEM((rows, LANES), jnp.float32),
-            pltpu.VMEM((rows, count), jnp.float32),
-        ],
+        scratch_shapes=[pltpu.VMEM((rows, CHUNK), jnp.bfloat16)] * parts
+        + [pltpu.VMEM((rows, LANES), jnp.float32), pltpu.VMEM((rows, count), jnp.float32)],
         compiler_params=pltpu.CompilerParams(vmem_limit_bytes=LIMIT),
         cost_estimate=pl.CostEstimate(
             flops=2 * rows * count * features,
@@ -231,18 +248,11 @@
     )
     count, features = queries.shape
     logs = jax.ShapeDtypeStruct((1, count), jnp.float32)
-    probes, mean, ref_log = call(
-        ref_kernel,
-        [queries, first_total],
-        ref_pieces,
-        count,
-        (
-            jax.ShapeDtypeStruct((count, features), jnp.bfloat16),
-            jax.ShapeDtypeStruct((1, features), jnp.float32),
-            logs,
-        ),
-    )
-    return call(gen_kernel, [ref_log, probes, mean], gen_pieces, count, logs).reshape(-1)
+    probes = jax.ShapeDtypeStruct((count, CHUNK), jnp.bfloat16)
+    mean = jax.ShapeDtypeStruct((1, features), jnp.float32)
+    outputs = (*[probes] * (features // CHUNK), mean, logs)
+    before = call(ref_kernel, [queries, first_total], ref_pieces, count, outputs)
+    return call(gen_kernel, before, gen_pieces, count, logs).reshape(-1)
 
 
 def solution(mesh):

time: 31.2 us -> 31.2 us (level)
  no operation moved by 1% of the time
where the time goes in v17:
time: 31.2 us; the launch traced here: 31.1 us
  starting transfers between devices  22.3 us (71%)
  Pallas kernels  4.45 us (14%)
  waiting for transfers between devices  4.04 us (13%)
    ppermute x14, starting transfers between devices, hop(): return lax.ppermute(block, 'samp', ring)  15.4 us
    ppermute x5, starting transfers between devices, hand_over(): return lax.ppermute(block, 'samp', twins)  6.88 us
    pallas_call x2, Pallas kernels, call(): pl.pallas_call(functools.partial(kernel, spans, parts), out_shape=out_sha...  4.4 us
    ppermute x14, waiting for transfers between devices, hop(): return lax.ppermute(block, 'samp', ring)  4.03 us
  transfers between devices with their start and end apart: 19, of which 7 were waited for; matrix products, arithmetic and copies ran while one was open for 1% of the time, Pallas kernels for 8%

profile of v17, /device:TPU:1, one launch (start us, length us, event | category | flops | bytes accessed | tf_op | source)
XLA Modules:
  0.0 31.1 jit_solution(14189720190643831913)
XLA Ops:
  0.0 0.0 copy-start
  0.0 0.1 collective-permute-start
  0.1 2.7 %collective-permute-start.3 = (bf16[16,4096]{1,0:T(8,128)(2,1)}, bf16[16,4096]{1,0:T(8,128)(2,1)S(1)}, u32[]{:S(2)}, u32[]{:S(2)}) collective-permute-start(bf16[16,4096]{1,0:T(8,128)(2,1)} %param.5), channel_id=1, source_target_pairs={{0,4},{1,3},{4,8},{5,1},{8,12},{9,5},{12,14},{13,9},{14,10},{15,13... | collective-permute-start | bytes 393224 | tf_op jit(solution)/shard_map/ppermute | solution.py:42
  2.7 0.4 %collective-permute-start.5 = (bf16[16,4096]{1,0:T(8,128)(2,1)}, bf16[16,4096]{1,0:T(8,128)(2,1)S(1)}, u32[]{:S(2)}, u32[]{:S(2)}) collective-permute-start(bf16[16,4096]{1,0:T(8,128)(2,1)} %param.4), channel_id=1, source_target_pairs={{0,1},{1,0},{2,3},{3,2},{4,5},{5,4},{6,7},{7,6},{8,9},{9,8},{10,11... | collective-permute-start | bytes 393224 | tf_op jit(solution)/shard_map/ppermute | solution.py:45
  3.1 0.9 %collective-permute-start.6 = (bf16[16,4096]{1,0:T(8,128)(2,1)}, bf16[16,4096]{1,0:T(8,128)(2,1)S(1)}, u32[]{:S(2)}, u32[]{:S(2)}) collective-permute-start(bf16[16,4096]{1,0:T(8,128)(2,1)} %param.4), channel_id=1, source_target_pairs={{0,4},{1,3},{4,8},{5,1},{8,12},{9,5},{12,14},{13,9},{14,10},{15,13... | collective-permute-start | bytes 393224 | tf_op jit(solution)/shard_map/ppermute | solution.py:42
  4.0 0.0 collective-permute-done.rows.refs_0_
  4.1 1.3 %collective-permute-start.1 = (bf16[16,4096]{1,0:T(8,128)(2,1)S(1)}, bf16[16,4096]{1,0:T(8,128)(2,1)S(1)}, u32[]{:S(2)}, u32[]{:S(2)}) collective-permute-start(bf16[16,4096]{1,0:T(8,128)(2,1)S(1)} %collective-permute-done.rows.refs_0_), channel_id=1, source_target_pairs={{0,4},{1,3},{4,8},{5,1},{8,12},{9,5},{12,14},{13,9},{14,10},{15,13... | collective-permute-start | bytes 393224 | tf_op jit(solution)/shard_map/ppermute | solution.py:42
  5.4 0.3 collective-permute-done.3.refs_1_
  5.7 1.4 %collective-permute-start.4 = (bf16[16,4096]{1,0:T(8,128)(2,1)S(1)}, bf16[16,4096]{1,0:T(8,128)(2,1)S(1)}, u32[]{:S(2)}, u32[]{:S(2)}) collective-permute-start(bf16[16,4096]{1,0:T(8,128)(2,1)S(1)} %collective-permute-done.3.refs_1_), channel_id=1, source_target_pairs={{0,4},{1,3},{4,8},{5,1},{8,12},{9,5},{12,14},{13,9},{14,10},{15,13... | collective-permute-start | bytes 393224 | tf_op jit(solution)/shard_map/ppermute | solution.py:42
  7.1 0.1 shard_map.37.first_total
  7.1 0.0 collective-permute-done.5.refs_6_
  7.2 1.3 %collective-permute-start.7 = (bf16[16,4096]{1,0:T(8,128)(2,1)S(1)}, bf16[16,4096]{1,0:T(8,128)(2,1)S(1)}, u32[]{:S(2)}, u32[]{:S(2)}) collective-permute-start(bf16[16,4096]{1,0:T(8,128)(2,1)S(1)} %collective-permute-done.5.refs_6_), channel_id=1, source_target_pairs={{0,4},{1,3},{4,8},{5,1},{8,12},{9,5},{12,14},{13,9},{14,10},{15,13... | collective-permute-start | bytes 393224 | tf_op jit(solution)/shard_map/ppermute | solution.py:42
  8.5 0.0 collective-permute-done.6.refs_7_
  8.5 1.3 %collective-permute-start.8 = (bf16[16,4096]{1,0:T(8,128)(2,1)S(1)}, bf16[16,4096]{1,0:T(8,128)(2,1)S(1)}, u32[]{:S(2)}, u32[]{:S(2)}) collective-permute-start(bf16[16,4096]{1,0:T(8,128)(2,1)S(1)} %collective-permute-done.6.refs_7_), channel_id=1, source_target_pairs={{0,4},{1,3},{4,8},{5,1},{8,12},{9,5},{12,14},{13,9},{14,10},{15,13... | collective-permute-start | bytes 393224 | tf_op jit(solution)/shard_map/ppermute | solution.py:42
  9.8 0.0 collective-permute-done.1.refs_2_
  9.8 1.3 %collective-permute-start.2 = (bf16[16,4096]{1,0:T(8,128)(2,1)S(1)}, bf16[16,4096]{1,0:T(8,128)(2,1)S(1)}, u32[]{:S(2)}, u32[]{:S(2)}) collective-permute-start(bf16[16,4096]{1,0:T(8,128)(2,1)S(1)} %collective-permute-done.1.refs_2_), channel_id=1, source_target_pairs={{0,4},{1,3},{4,8},{5,1},{8,12},{9,5},{12,14},{13,9},{14,10},{15,13... | collective-permute-start | bytes 393224 | tf_op jit(solution)/shard_map/ppermute | solution.py:42
  11.1 0.0 collective-permute-done.4.refs_3_
  11.1 0.2 collective-permute-start.10
  11.4 0.3 collective-permute-done.7.refs_8_
  11.7 1.0 %collective-permute-start.14 = (bf16[16,4096]{1,0:T(8,128)(2,1)S(1)}, bf16[16,4096]{1,0:T(8,128)(2,1)S(1)}, u32[]{:S(2)}, u32[]{:S(2)}) collective-permute-start(bf16[16,4096]{1,0:T(8,128)(2,1)S(1)} %collective-permute-done.7.refs_8_), channel_id=1, source_target_pairs={{0,4},{1,3},{4,8},{5,1},{8,12},{9,5},{12,14},{13,9},{14,10},{15,13... | collective-permute-start | bytes 393224 | tf_op jit(solution)/shard_map/ppermute | solution.py:42
  12.7 0.3 collective-permute-done.8.refs_9_
  13.0 1.1 %collective-permute-start.15 = (bf16[16,4096]{1,0:T(8,128)(2,1)S(1)}, bf16[16,4096]{1,0:T(8,128)(2,1)S(1)}, u32[]{:S(2)}, u32[]{:S(2)}) collective-permute-start(bf16[16,4096]{1,0:T(8,128)(2,1)S(1)} %collective-permute-done.8.refs_9_), channel_id=1, source_target_pairs={{0,4},{1,3},{4,8},{5,1},{8,12},{9,5},{12,14},{13,9},{14,10},{15,13... | collective-permute-start | bytes 393224 | tf_op jit(solution)/shard_map/ppermute | solution.py:42
  14.1 0.4 %collective-permute-done.2.refs_5_ = bf16[16,4096]{1,0:T(8,128)(2,1)S(1)} collective-permute-done((bf16[16,4096]{1,0:T(8,128)(2,1)S(1)}, bf16[16,4096]{1,0:T(8,128)(2,1)S(1)}, u32[]{:S(2)}, u32[]{:S(2)}) %collective-permute-start.2) | collective-permute-done | bytes 131104 | tf_op jit(solution)/shard_map/ppermute | solution.py:42
  14.5 1.0 %collective-permute-start.11 = (bf16[16,4096]{1,0:T(8,128)(2,1)S(1)}, bf16[16,4096]{1,0:T(8,128)(2,1)S(1)}, u32[]{:S(2)}, u32[]{:S(2)}) collective-permute-start(bf16[16,4096]{1,0:T(8,128)(2,1)S(1)} %collective-permute-done.2.refs_5_), channel_id=1, source_target_pairs={{0,4},{1,3},{4,8},{5,1},{8,12},{9,5},{12,14},{13,9},{14,10},{15,13... | collective-permute-start | bytes 393224 | tf_op jit(solution)/shard_map/ppermute | solution.py:42
  15.5 0.4 %collective-permute-done.10.refs_6_ = bf16[16,4096]{1,0:T(8,128)(2,1)S(1)} collective-permute-done((bf16[16,4096]{1,0:T(8,128)(2,1)S(1)}, bf16[16,4096]{1,0:T(8,128)(2,1)S(1)}, u32[]{:S(2)}, u32[]{:S(2)}) %collective-permute-start.10) | collective-permute-done | bytes 131104 | tf_op jit(solution)/shard_map/ppermute | solution.py:42
  15.9 1.0 %collective-permute-start.12 = (bf16[16,4096]{1,0:T(8,128)(2,1)S(1)}, bf16[16,4096]{1,0:T(8,128)(2,1)S(1)}, u32[]{:S(2)}, u32[]{:S(2)}) collective-permute-start(bf16[16,4096]{1,0:T(8,128)(2,1)S(1)} %collective-permute-done.10.refs_6_), channel_id=1, source_target_pairs={{0,4},{1,3},{4,8},{5,1},{8,12},{9,5},{12,14},{13,9},{14,10},{15,13... | collective-permute-start | bytes 393224 | tf_op jit(solution)/shard_map/ppermute | solution.py:42
  16.9 2.7 %collective-permute-start.9 = (bf16[128,4096]{1,0:T(8,128)(2,1)S(1)}, bf16[128,4096]{1,0:T(8,128)(2,1)S(1)}, u32[]{:S(2)}, u32[]{:S(2)}) collective-permute-start(bf16[128,4096]{1,0:T(8,128)(2,1)S(1)} %constant_dynamic-update-slice_fusion), channel_id=1, source_target_pairs={{0,1},{1,0},{2,3},{3,2},{4,5},{5,4},{6,7},{7,6},{8,9},{9,8},{10,11... | collective-permute-start | bytes 3145736 | tf_op jit(solution)/shard_map/ppermute | solution.py:45
  19.6 0.0 collective-permute-done.14.refs_11_
  19.6 0.4 %collective-permute-start.16 = (bf16[16,4096]{1,0:T(8,128)(2,1)S(1)}, bf16[16,4096]{1,0:T(8,128)(2,1)S(1)}, u32[]{:S(2)}, u32[]{:S(2)}) collective-permute-start(bf16[16,4096]{1,0:T(8,128)(2,1)S(1)} %collective-permute-done.14.refs_11_), channel_id=1, source_target_pairs={{0,4},{1,3},{4,8},{5,1},{8,12},{9,5},{12,14},{13,9},{14,10},{15,13... | collective-permute-start | bytes 393224 | tf_op jit(solution)/shard_map/ppermute | solution.py:42
  20.0 0.0 collective-permute-done.15.refs_12_
  20.0 0.4 %collective-permute-start.17 = (bf16[16,4096]{1,0:T(8,128)(2,1)S(1)}, bf16[16,4096]{1,0:T(8,128)(2,1)S(1)}, u32[]{:S(2)}, u32[]{:S(2)}) collective-permute-start(bf16[16,4096]{1,0:T(8,128)(2,1)S(1)} %collective-permute-done.15.refs_12_), channel_id=1, source_target_pairs={{0,4},{1,3},{4,8},{5,1},{8,12},{9,5},{12,14},{13,9},{14,10},{15,13... | collective-permute-start | bytes 393224 | tf_op jit(solution)/shard_map/ppermute | solution.py:42
  20.4 0.0 collective-permute-done.11.refs_7_
  20.4 1.1 %collective-permute-done.12.refs_8_ = bf16[16,4096]{1,0:T(8,128)(2,1)S(1)} collective-permute-done((bf16[16,4096]{1,0:T(8,128)(2,1)S(1)}, bf16[16,4096]{1,0:T(8,128)(2,1)S(1)}, u32[]{:S(2)}, u32[]{:S(2)}) %collective-permute-start.12) | collective-permute-done | bytes 131104 | tf_op jit(solution)/shard_map/ppermute | solution.py:42
  21.5 2.3 %collective-permute-start.13 = (bf16[64,4096]{1,0:T(8,128)(2,1)S(1)}, bf16[64,4096]{1,0:T(8,128)(2,1)S(1)}, u32[]{:S(2)}, u32[]{:S(2)}) collective-permute-start(bf16[64,4096]{1,0:T(8,128)(2,1)S(1)} %pad_maximum_fusion), channel_id=1, source_target_pairs={{0,1},{1,0},{2,3},{3,2},{4,5},{5,4},{6,7},{7,6},{8,9},{9,8},{10,11... | collective-permute-start | bytes 1572872 | tf_op jit(solution)/shard_map/ppermute | solution.py:45
  23.8 0.0 collective-permute-done.16.refs_13_
  23.8 1.3 %collective-permute-done.17.refs_14_ = bf16[16,4096]{1,0:T(8,128)(2,1)S(1)} collective-permute-done((bf16[16,4096]{1,0:T(8,128)(2,1)S(1)}, bf16[16,4096]{1,0:T(8,128)(2,1)S(1)}, u32[]{:S(2)}, u32[]{:S(2)}) %collective-permute-start.17) | collective-permute-done | bytes 131104 | tf_op jit(solution)/shard_map/ppermute | solution.py:42
  25.1 1.5 %collective-permute-start.18 = (bf16[64,4096]{1,0:T(8,128)(2,1)S(1)}, bf16[64,4096]{1,0:T(8,128)(2,1)S(1)}, u32[]{:S(2)}, u32[]{:S(2)}) collective-permute-start(bf16[64,4096]{1,0:T(8,128)(2,1)S(1)} %pad_maximum_fusion.1), channel_id=1, source_target_pairs={{0,1},{1,0},{2,3},{3,2},{4,5},{5,4},{6,7},{7,6},{8,9},{9,8},{10,11... | collective-permute-start | bytes 1572872 | tf_op jit(solution)/shard_map/ppermute | solution.py:45
  26.6 0.0 collective-permute-done.13.refs_9_
  26.6 0.0 collective-permute-done.9.refs_4_.refs_10_
  26.6 0.0 copy-done
  26.7 2.3 %shard_map.38 = (bf16[512,1024]{1,0:T(8,128)(2,1)S(1)}, bf16[512,1024]{1,0:T(8,128)(2,1)S(1)}, bf16[512,1024]{1,0:T(8,128)(2,1)S(1)}, bf16[512,1024]{1,0:T(8,128...) custom-call(bf16[512,4096]{1,0:T(8,128)(2,1)S(1)} %copy-done, f32[1,4096]{1,0:T(1,128)S(1)} %shard_map.37.first_total, ...), custom_call_target="tpu_custom_call" | custom-call | flops 1073741824 | bytes 6291456 | tf_op jit(solution)/shard_map/pallas_call | solution.py:228
  29.0 0.0 collective-permute-done.18.refs_15_
  29.0 2.1 %shard_map.39 = f32[1,512]{1,0:T(1,128)} custom-call(bf16[512,1024]{1,0:T(8,128)(2,1)S(1)} %get-tuple-element.15.refs_0_, bf16[512,1024]{1,0:T(8,128)(2,1)S(1)} %get-tuple-element.16.refs_1_, bf16[512,1024]{1,0:T(8,128)(2,1)S(1)} %get-tuple-element.17.refs_2_, bf16[512,1024]{1,0:T(8,128)(2,1)S(1)} %get-tuple-element.18.refs_3_, ...), custom_call_target="tpu_custom_call" | custom-call | flops 1073741824 | bytes 6291456 | tf_op jit(solution)/shard_map/pallas_call | solution.py:228
  (10 shorter events, 0.2 us)
Async XLA Ops:
  0.0 26.6 %copy-start = (bf16[512,4096]{1,0:T(8,128)(2,1)S(1)}, bf16[512,4096]{1,0:T(8,128)(2,1)}, u32[]{:S(2)}) copy-start(bf16[512,4096]{1,0:T(8,128)(2,1)} %queries.1) | copy-start | bytes 12582916
  0.0 4.0 %collective-permute-start = (bf16[16,4096]{1,0:T(8,128)(2,1)}, bf16[16,4096]{1,0:T(8,128)(2,1)S(1)}, u32[]{:S(2)}, u32[]{:S(2)}) collective-permute-start(bf16[16,4096]{1,0:T(8,128)(2,1)} %param.5), channel_id=1, source_target_pairs={{0,1},{1,0},{2,3},{3,2},{4,5},{5,4},{6,7},{7,6},{8,9},{9,8},{10,11... | collective-permute-start | bytes 393224 | tf_op jit(solution)/shard_map/ppermute | solution.py:45
  0.1 5.6 %collective-permute-start.3 = (bf16[16,4096]{1,0:T(8,128)(2,1)}, bf16[16,4096]{1,0:T(8,128)(2,1)S(1)}, u32[]{:S(2)}, u32[]{:S(2)}) collective-permute-start(bf16[16,4096]{1,0:T(8,128)(2,1)} %param.5), channel_id=1, source_target_pairs={{0,4},{1,3},{4,8},{5,1},{8,12},{9,5},{12,14},{13,9},{14,10},{15,13... | collective-permute-start | bytes 393224 | tf_op jit(solution)/shard_map/ppermute | solution.py:42
  2.7 4.4 %collective-permute-start.5 = (bf16[16,4096]{1,0:T(8,128)(2,1)}, bf16[16,4096]{1,0:T(8,128)(2,1)S(1)}, u32[]{:S(2)}, u32[]{:S(2)}) collective-permute-start(bf16[16,4096]{1,0:T(8,128)(2,1)} %param.4), channel_id=1, source_target_pairs={{0,1},{1,0},{2,3},{3,2},{4,5},{5,4},{6,7},{7,6},{8,9},{9,8},{10,11... | collective-permute-start | bytes 393224 | tf_op jit(solution)/shard_map/ppermute | solution.py:45
  3.1 5.4 %collective-permute-start.6 = (bf16[16,4096]{1,0:T(8,128)(2,1)}, bf16[16,4096]{1,0:T(8,128)(2,1)S(1)}, u32[]{:S(2)}, u32[]{:S(2)}) collective-permute-start(bf16[16,4096]{1,0:T(8,128)(2,1)} %param.4), channel_id=1, source_target_pairs={{0,4},{1,3},{4,8},{5,1},{8,12},{9,5},{12,14},{13,9},{14,10},{15,13... | collective-permute-start | bytes 393224 | tf_op jit(solution)/shard_map/ppermute | solution.py:42
  4.1 5.8 %collective-permute-start.1 = (bf16[16,4096]{1,0:T(8,128)(2,1)S(1)}, bf16[16,4096]{1,0:T(8,128)(2,1)S(1)}, u32[]{:S(2)}, u32[]{:S(2)}) collective-permute-start(bf16[16,4096]{1,0:T(8,128)(2,1)S(1)} %collective-permute-done.rows.refs_0_), channel_id=1, source_target_pairs={{0,4},{1,3},{4,8},{5,1},{8,12},{9,5},{12,14},{13,9},{14,10},{15,13... | collective-permute-start | bytes 393224 | tf_op jit(solution)/shard_map/ppermute | solution.py:42
  5.7 5.4 %collective-permute-start.4 = (bf16[16,4096]{1,0:T(8,128)(2,1)S(1)}, bf16[16,4096]{1,0:T(8,128)(2,1)S(1)}, u32[]{:S(2)}, u32[]{:S(2)}) collective-permute-start(bf16[16,4096]{1,0:T(8,128)(2,1)S(1)} %collective-permute-done.3.refs_1_), channel_id=1, source_target_pairs={{0,4},{1,3},{4,8},{5,1},{8,12},{9,5},{12,14},{13,9},{14,10},{15,13... | collective-permute-start | bytes 393224 | tf_op jit(solution)/shard_map/ppermute | solution.py:42
  7.2 4.5 %collective-permute-start.7 = (bf16[16,4096]{1,0:T(8,128)(2,1)S(1)}, bf16[16,4096]{1,0:T(8,128)(2,1)S(1)}, u32[]{:S(2)}, u32[]{:S(2)}) collective-permute-start(bf16[16,4096]{1,0:T(8,128)(2,1)S(1)} %collective-permute-done.5.refs_6_), channel_id=1, source_target_pairs={{0,4},{1,3},{4,8},{5,1},{8,12},{9,5},{12,14},{13,9},{14,10},{15,13... | collective-permute-start | bytes 393224 | tf_op jit(solution)/shard_map/ppermute | solution.py:42
  8.5 4.5 %collective-permute-start.8 = (bf16[16,4096]{1,0:T(8,128)(2,1)S(1)}, bf16[16,4096]{1,0:T(8,128)(2,1)S(1)}, u32[]{:S(2)}, u32[]{:S(2)}) collective-permute-start(bf16[16,4096]{1,0:T(8,128)(2,1)S(1)} %collective-permute-done.6.refs_7_), channel_id=1, source_target_pairs={{0,4},{1,3},{4,8},{5,1},{8,12},{9,5},{12,14},{13,9},{14,10},{15,13... | collective-permute-start | bytes 393224 | tf_op jit(solution)/shard_map/ppermute | solution.py:42
  9.8 4.7 %collective-permute-start.2 = (bf16[16,4096]{1,0:T(8,128)(2,1)S(1)}, bf16[16,4096]{1,0:T(8,128)(2,1)S(1)}, u32[]{:S(2)}, u32[]{:S(2)}) collective-permute-start(bf16[16,4096]{1,0:T(8,128)(2,1)S(1)} %collective-permute-done.1.refs_2_), channel_id=1, source_target_pairs={{0,4},{1,3},{4,8},{5,1},{8,12},{9,5},{12,14},{13,9},{14,10},{15,13... | collective-permute-start | bytes 393224 | tf_op jit(solution)/shard_map/ppermute | solution.py:42
  11.1 4.8 %collective-permute-start.10 = (bf16[16,4096]{1,0:T(8,128)(2,1)S(1)}, bf16[16,4096]{1,0:T(8,128)(2,1)S(1)}, u32[]{:S(2)}, u32[]{:S(2)}) collective-permute-start(bf16[16,4096]{1,0:T(8,128)(2,1)S(1)} %collective-permute-done.4.refs_3_), channel_id=1, source_target_pairs={{0,4},{1,3},{4,8},{5,1},{8,12},{9,5},{12,14},{13,9},{14,10},{15,13... | collective-permute-start | bytes 393224 | tf_op jit(solution)/shard_map/ppermute | solution.py:42
  11.7 7.9 %collective-permute-start.14 = (bf16[16,4096]{1,0:T(8,128)(2,1)S(1)}, bf16[16,4096]{1,0:T(8,128)(2,1)S(1)}, u32[]{:S(2)}, u32[]{:S(2)}) collective-permute-start(bf16[16,4096]{1,0:T(8,128)(2,1)S(1)} %collective-permute-done.7.refs_8_), channel_id=1, source_target_pairs={{0,4},{1,3},{4,8},{5,1},{8,12},{9,5},{12,14},{13,9},{14,10},{15,13... | collective-permute-start | bytes 393224 | tf_op jit(solution)/shard_map/ppermute | solution.py:42
  13.0 7.0 %collective-permute-start.15 = (bf16[16,4096]{1,0:T(8,128)(2,1)S(1)}, bf16[16,4096]{1,0:T(8,128)(2,1)S(1)}, u32[]{:S(2)}, u32[]{:S(2)}) collective-permute-start(bf16[16,4096]{1,0:T(8,128)(2,1)S(1)} %collective-permute-done.8.refs_9_), channel_id=1, source_target_pairs={{0,4},{1,3},{4,8},{5,1},{8,12},{9,5},{12,14},{13,9},{14,10},{15,13... | collective-permute-start | bytes 393224 | tf_op jit(solution)/shard_map/ppermute | solution.py:42
  14.5 5.9 %collective-permute-start.11 = (bf16[16,4096]{1,0:T(8,128)(2,1)S(1)}, bf16[16,4096]{1,0:T(8,128)(2,1)S(1)}, u32[]{:S(2)}, u32[]{:S(2)}) collective-permute-start(bf16[16,4096]{1,0:T(8,128)(2,1)S(1)} %collective-permute-done.2.refs_5_), channel_id=1, source_target_pairs={{0,4},{1,3},{4,8},{5,1},{8,12},{9,5},{12,14},{13,9},{14,10},{15,13... | collective-permute-start | bytes 393224 | tf_op jit(solution)/shard_map/ppermute | solution.py:42
  15.9 5.6 %collective-permute-start.12 = (bf16[16,4096]{1,0:T(8,128)(2,1)S(1)}, bf16[16,4096]{1,0:T(8,128)(2,1)S(1)}, u32[]{:S(2)}, u32[]{:S(2)}) collective-permute-start(bf16[16,4096]{1,0:T(8,128)(2,1)S(1)} %collective-permute-done.10.refs_6_), channel_id=1, source_target_pairs={{0,4},{1,3},{4,8},{5,1},{8,12},{9,5},{12,14},{13,9},{14,10},{15,13... | collective-permute-start | bytes 393224 | tf_op jit(solution)/shard_map/ppermute | solution.py:42
  16.9 9.7 %collective-permute-start.9 = (bf16[128,4096]{1,0:T(8,128)(2,1)S(1)}, bf16[128,4096]{1,0:T(8,128)(2,1)S(1)}, u32[]{:S(2)}, u32[]{:S(2)}) collective-permute-start(bf16[128,4096]{1,0:T(8,128)(2,1)S(1)} %constant_dynamic-update-slice_fusion), channel_id=1, source_target_pairs={{0,1},{1,0},{2,3},{3,2},{4,5},{5,4},{6,7},{7,6},{8,9},{9,8},{10,11... | collective-permute-start | bytes 3145736 | tf_op jit(solution)/shard_map/ppermute | solution.py:45
  19.6 4.2 %collective-permute-start.16 = (bf16[16,4096]{1,0:T(8,128)(2,1)S(1)}, bf16[16,4096]{1,0:T(8,128)(2,1)S(1)}, u32[]{:S(2)}, u32[]{:S(2)}) collective-permute-start(bf16[16,4096]{1,0:T(8,128)(2,1)S(1)} %collective-permute-done.14.refs_11_), channel_id=1, source_target_pairs={{0,4},{1,3},{4,8},{5,1},{8,12},{9,5},{12,14},{13,9},{14,10},{15,13... | collective-permute-start | bytes 393224 | tf_op jit(solution)/shard_map/ppermute | solution.py:42
  20.0 5.1 %collective-permute-start.17 = (bf16[16,4096]{1,0:T(8,128)(2,1)S(1)}, bf16[16,4096]{1,0:T(8,128)(2,1)S(1)}, u32[]{:S(2)}, u32[]{:S(2)}) collective-permute-start(bf16[16,4096]{1,0:T(8,128)(2,1)S(1)} %collective-permute-done.15.refs_12_), channel_id=1, source_target_pairs={{0,4},{1,3},{4,8},{5,1},{8,12},{9,5},{12,14},{13,9},{14,10},{15,13... | collective-permute-start | bytes 393224 | tf_op jit(solution)/shard_map/ppermute | solution.py:42
  21.5 5.1 %collective-permute-start.13 = (bf16[64,4096]{1,0:T(8,128)(2,1)S(1)}, bf16[64,4096]{1,0:T(8,128)(2,1)S(1)}, u32[]{:S(2)}, u32[]{:S(2)}) collective-permute-start(bf16[64,4096]{1,0:T(8,128)(2,1)S(1)} %pad_maximum_fusion), channel_id=1, source_target_pairs={{0,1},{1,0},{2,3},{3,2},{4,5},{5,4},{6,7},{7,6},{8,9},{9,8},{10,11... | collective-permute-start | bytes 1572872 | tf_op jit(solution)/shard_map/ppermute | solution.py:45
  25.1 3.8 %collective-permute-start.18 = (bf16[64,4096]{1,0:T(8,128)(2,1)S(1)}, bf16[64,4096]{1,0:T(8,128)(2,1)S(1)}, u32[]{:S(2)}, u32[]{:S(2)}) collective-permute-start(bf16[64,4096]{1,0:T(8,128)(2,1)S(1)} %pad_maximum_fusion.1), channel_id=1, source_target_pairs={{0,1},{1,0},{2,3},{3,2},{4,5},{5,4},{6,7},{7,6},{8,9},{9,8},{10,11... | collective-permute-start | bytes 1572872 | tf_op jit(solution)/shard_map/ppermute | solution.py:45

commit v18 on v17

--- a/solution.py
+++ b/solution.py
@@ -9,7 +9,7 @@
 
 TEMP = 64
 LANES = 128
-CHUNK = 1024
+CHUNK = 256
 GROUP = 32
 BLOCK = 256
 LIMIT = 40 * 2**20

time: 31.2 us -> 31.8 us (1.019)
  Pallas kernels: 4.45 us -> 5.05 us
    pallas_call x2, Pallas kernels: 4.4 us -> 4.99 us  [call(): pl.pallas_call(functools.partial(kernel, spans, parts), out_shape=out_sha...]
  transfers between devices with their start and end apart: 19 -> 19, of which waited for: 7 -> 7; matrix products, arithmetic and copies ran while one was open for 1% -> 0% of each run, Pallas kernels for 8% -> 9%
where the time goes in v18:
time: 31.8 us; the launch traced here: 31.7 us
  starting transfers between devices  22.3 us (70%)
  Pallas kernels  5.05 us (16%)
  waiting for transfers between devices  4.04 us (13%)
    ppermute x14, starting transfers between devices, hop(): return lax.ppermute(block, 'samp', ring)  15.4 us
    ppermute x5, starting transfers between devices, hand_over(): return lax.ppermute(block, 'samp', twins)  6.88 us
    pallas_call x2, Pallas kernels, call(): pl.pallas_call(functools.partial(kernel, spans, parts), out_shape=out_sha...  4.99 us
    ppermute x14, waiting for transfers between devices, hop(): return lax.ppermute(block, 'samp', ring)  4.03 us
  transfers between devices with their start and end apart: 19, of which 7 were waited for; matrix products, arithmetic and copies ran while one was open for 0% of the time, Pallas kernels for 9%

profile of v18, /device:TPU:1, one launch (start us, length us, event | category | flops | bytes accessed | tf_op | source)
XLA Modules:
  0.0 31.7 jit_solution(7668033644548368691)
XLA Ops:
  0.0 0.0 copy-start
  0.0 0.1 collective-permute-start
  0.1 2.7 %collective-permute-start.3 = (bf16[16,4096]{1,0:T(8,128)(2,1)}, bf16[16,4096]{1,0:T(8,128)(2,1)S(1)}, u32[]{:S(2)}, u32[]{:S(2)}) collective-permute-start(bf16[16,4096]{1,0:T(8,128)(2,1)} %param.5), channel_id=1, source_target_pairs={{0,4},{1,3},{4,8},{5,1},{8,12},{9,5},{12,14},{13,9},{14,10},{15,13... | collective-permute-start | bytes 393224 | tf_op jit(solution)/shard_map/ppermute | solution.py:42
  2.7 0.4 %collective-permute-start.5 = (bf16[16,4096]{1,0:T(8,128)(2,1)}, bf16[16,4096]{1,0:T(8,128)(2,1)S(1)}, u32[]{:S(2)}, u32[]{:S(2)}) collective-permute-start(bf16[16,4096]{1,0:T(8,128)(2,1)} %param.4), channel_id=1, source_target_pairs={{0,1},{1,0},{2,3},{3,2},{4,5},{5,4},{6,7},{7,6},{8,9},{9,8},{10,11... | collective-permute-start | bytes 393224 | tf_op jit(solution)/shard_map/ppermute | solution.py:45
  3.1 0.9 %collective-permute-start.6 = (bf16[16,4096]{1,0:T(8,128)(2,1)}, bf16[16,4096]{1,0:T(8,128)(2,1)S(1)}, u32[]{:S(2)}, u32[]{:S(2)}) collective-permute-start(bf16[16,4096]{1,0:T(8,128)(2,1)} %param.4), channel_id=1, source_target_pairs={{0,4},{1,3},{4,8},{5,1},{8,12},{9,5},{12,14},{13,9},{14,10},{15,13... | collective-permute-start | bytes 393224 | tf_op jit(solution)/shard_map/ppermute | solution.py:42
  4.0 0.0 collective-permute-done.rows.refs_0_
  4.1 1.3 %collective-permute-start.1 = (bf16[16,4096]{1,0:T(8,128)(2,1)S(1)}, bf16[16,4096]{1,0:T(8,128)(2,1)S(1)}, u32[]{:S(2)}, u32[]{:S(2)}) collective-permute-start(bf16[16,4096]{1,0:T(8,128)(2,1)S(1)} %collective-permute-done.rows.refs_0_), channel_id=1, source_target_pairs={{0,4},{1,3},{4,8},{5,1},{8,12},{9,5},{12,14},{13,9},{14,10},{15,13... | collective-permute-start | bytes 393224 | tf_op jit(solution)/shard_map/ppermute | solution.py:42
  5.4 0.3 collective-permute-done.3.refs_1_
  5.7 1.4 %collective-permute-start.4 = (bf16[16,4096]{1,0:T(8,128)(2,1)S(1)}, bf16[16,4096]{1,0:T(8,128)(2,1)S(1)}, u32[]{:S(2)}, u32[]{:S(2)}) collective-permute-start(bf16[16,4096]{1,0:T(8,128)(2,1)S(1)} %collective-permute-done.3.refs_1_), channel_id=1, source_target_pairs={{0,4},{1,3},{4,8},{5,1},{8,12},{9,5},{12,14},{13,9},{14,10},{15,13... | collective-permute-start | bytes 393224 | tf_op jit(solution)/shard_map/ppermute | solution.py:42
  7.1 0.1 shard_map.37.first_total
  7.1 0.0 collective-permute-done.5.refs_18_
  7.2 1.3 %collective-permute-start.7 = (bf16[16,4096]{1,0:T(8,128)(2,1)S(1)}, bf16[16,4096]{1,0:T(8,128)(2,1)S(1)}, u32[]{:S(2)}, u32[]{:S(2)}) collective-permute-start(bf16[16,4096]{1,0:T(8,128)(2,1)S(1)} %collective-permute-done.5.refs_18_), channel_id=1, source_target_pairs={{0,4},{1,3},{4,8},{5,1},{8,12},{9,5},{12,14},{13,9},{14,10},{15,13... | collective-permute-start | bytes 393224 | tf_op jit(solution)/shard_map/ppermute | solution.py:42
  8.5 0.0 collective-permute-done.6.refs_19_
  8.5 1.3 %collective-permute-start.8 = (bf16[16,4096]{1,0:T(8,128)(2,1)S(1)}, bf16[16,4096]{1,0:T(8,128)(2,1)S(1)}, u32[]{:S(2)}, u32[]{:S(2)}) collective-permute-start(bf16[16,4096]{1,0:T(8,128)(2,1)S(1)} %collective-permute-done.6.refs_19_), channel_id=1, source_target_pairs={{0,4},{1,3},{4,8},{5,1},{8,12},{9,5},{12,14},{13,9},{14,10},{15,13... | collective-permute-start | bytes 393224 | tf_op jit(solution)/shard_map/ppermute | solution.py:42
  9.8 0.0 collective-permute-done.1.refs_2_
  9.8 1.3 %collective-permute-start.2 = (bf16[16,4096]{1,0:T(8,128)(2,1)S(1)}, bf16[16,4096]{1,0:T(8,128)(2,1)S(1)}, u32[]{:S(2)}, u32[]{:S(2)}) collective-permute-start(bf16[16,4096]{1,0:T(8,128)(2,1)S(1)} %collective-permute-done.1.refs_2_), channel_id=1, source_target_pairs={{0,4},{1,3},{4,8},{5,1},{8,12},{9,5},{12,14},{13,9},{14,10},{15,13... | collective-permute-start | bytes 393224 | tf_op jit(solution)/shard_map/ppermute | solution.py:42
  11.1 0.0 collective-permute-done.4.refs_3_
  11.1 0.2 collective-permute-start.10
  11.4 0.3 collective-permute-done.7.refs_20_
  11.7 1.0 %collective-permute-start.14 = (bf16[16,4096]{1,0:T(8,128)(2,1)S(1)}, bf16[16,4096]{1,0:T(8,128)(2,1)S(1)}, u32[]{:S(2)}, u32[]{:S(2)}) collective-permute-start(bf16[16,4096]{1,0:T(8,128)(2,1)S(1)} %collective-permute-done.7.refs_20_), channel_id=1, source_target_pairs={{0,4},{1,3},{4,8},{5,1},{8,12},{9,5},{12,14},{13,9},{14,10},{15,13... | collective-permute-start | bytes 393224 | tf_op jit(solution)/shard_map/ppermute | solution.py:42
  12.7 0.3 collective-permute-done.8.refs_21_
  13.0 1.1 %collective-permute-start.15 = (bf16[16,4096]{1,0:T(8,128)(2,1)S(1)}, bf16[16,4096]{1,0:T(8,128)(2,1)S(1)}, u32[]{:S(2)}, u32[]{:S(2)}) collective-permute-start(bf16[16,4096]{1,0:T(8,128)(2,1)S(1)} %collective-permute-done.8.refs_21_), channel_id=1, source_target_pairs={{0,4},{1,3},{4,8},{5,1},{8,12},{9,5},{12,14},{13,9},{14,10},{15,13... | collective-permute-start | bytes 393224 | tf_op jit(solution)/shard_map/ppermute | solution.py:42
  14.1 0.4 %collective-permute-done.2.refs_5_ = bf16[16,4096]{1,0:T(8,128)(2,1)S(1)} collective-permute-done((bf16[16,4096]{1,0:T(8,128)(2,1)S(1)}, bf16[16,4096]{1,0:T(8,128)(2,1)S(1)}, u32[]{:S(2)}, u32[]{:S(2)}) %collective-permute-start.2) | collective-permute-done | bytes 131104 | tf_op jit(solution)/shard_map/ppermute | solution.py:42
  14.5 1.0 %collective-permute-start.11 = (bf16[16,4096]{1,0:T(8,128)(2,1)S(1)}, bf16[16,4096]{1,0:T(8,128)(2,1)S(1)}, u32[]{:S(2)}, u32[]{:S(2)}) collective-permute-start(bf16[16,4096]{1,0:T(8,128)(2,1)S(1)} %collective-permute-done.2.refs_5_), channel_id=1, source_target_pairs={{0,4},{1,3},{4,8},{5,1},{8,12},{9,5},{12,14},{13,9},{14,10},{15,13... | collective-permute-start | bytes 393224 | tf_op jit(solution)/shard_map/ppermute | solution.py:42
  15.5 0.4 %collective-permute-done.10.refs_6_ = bf16[16,4096]{1,0:T(8,128)(2,1)S(1)} collective-permute-done((bf16[16,4096]{1,0:T(8,128)(2,1)S(1)}, bf16[16,4096]{1,0:T(8,128)(2,1)S(1)}, u32[]{:S(2)}, u32[]{:S(2)}) %collective-permute-start.10) | collective-permute-done | bytes 131104 | tf_op jit(solution)/shard_map/ppermute | solution.py:42
  15.9 1.0 %collective-permute-start.12 = (bf16[16,4096]{1,0:T(8,128)(2,1)S(1)}, bf16[16,4096]{1,0:T(8,128)(2,1)S(1)}, u32[]{:S(2)}, u32[]{:S(2)}) collective-permute-start(bf16[16,4096]{1,0:T(8,128)(2,1)S(1)} %collective-permute-done.10.refs_6_), channel_id=1, source_target_pairs={{0,4},{1,3},{4,8},{5,1},{8,12},{9,5},{12,14},{13,9},{14,10},{15,13... | collective-permute-start | bytes 393224 | tf_op jit(solution)/shard_map/ppermute | solution.py:42
  16.9 2.7 %collective-permute-start.9 = (bf16[128,4096]{1,0:T(8,128)(2,1)S(1)}, bf16[128,4096]{1,0:T(8,128)(2,1)S(1)}, u32[]{:S(2)}, u32[]{:S(2)}) collective-permute-start(bf16[128,4096]{1,0:T(8,128)(2,1)S(1)} %constant_dynamic-update-slice_fusion), channel_id=1, source_target_pairs={{0,1},{1,0},{2,3},{3,2},{4,5},{5,4},{6,7},{7,6},{8,9},{9,8},{10,11... | collective-permute-start | bytes 3145736 | tf_op jit(solution)/shard_map/ppermute | solution.py:45
  19.6 0.0 collective-permute-done.14.refs_23_
  19.6 0.4 %collective-permute-start.16 = (bf16[16,4096]{1,0:T(8,128)(2,1)S(1)}, bf16[16,4096]{1,0:T(8,128)(2,1)S(1)}, u32[]{:S(2)}, u32[]{:S(2)}) collective-permute-start(bf16[16,4096]{1,0:T(8,128)(2,1)S(1)} %collective-permute-done.14.refs_23_), channel_id=1, source_target_pairs={{0,4},{1,3},{4,8},{5,1},{8,12},{9,5},{12,14},{13,9},{14,10},{15,13... | collective-permute-start | bytes 393224 | tf_op jit(solution)/shard_map/ppermute | solution.py:42
  20.0 0.0 collective-permute-done.15.refs_24_
  20.0 0.4 %collective-permute-start.17 = (bf16[16,4096]{1,0:T(8,128)(2,1)S(1)}, bf16[16,4096]{1,0:T(8,128)(2,1)S(1)}, u32[]{:S(2)}, u32[]{:S(2)}) collective-permute-start(bf16[16,4096]{1,0:T(8,128)(2,1)S(1)} %collective-permute-done.15.refs_24_), channel_id=1, source_target_pairs={{0,4},{1,3},{4,8},{5,1},{8,12},{9,5},{12,14},{13,9},{14,10},{15,13... | collective-permute-start | bytes 393224 | tf_op jit(solution)/shard_map/ppermute | solution.py:42
  20.4 0.0 collective-permute-done.11.refs_7_
  20.4 1.1 %collective-permute-done.12.refs_8_ = bf16[16,4096]{1,0:T(8,128)(2,1)S(1)} collective-permute-done((bf16[16,4096]{1,0:T(8,128)(2,1)S(1)}, bf16[16,4096]{1,0:T(8,128)(2,1)S(1)}, u32[]{:S(2)}, u32[]{:S(2)}) %collective-permute-start.12) | collective-permute-done | bytes 131104 | tf_op jit(solution)/shard_map/ppermute | solution.py:42
  21.5 2.3 %collective-permute-start.13 = (bf16[64,4096]{1,0:T(8,128)(2,1)S(1)}, bf16[64,4096]{1,0:T(8,128)(2,1)S(1)}, u32[]{:S(2)}, u32[]{:S(2)}) collective-permute-start(bf16[64,4096]{1,0:T(8,128)(2,1)S(1)} %pad_maximum_fusion), channel_id=1, source_target_pairs={{0,1},{1,0},{2,3},{3,2},{4,5},{5,4},{6,7},{7,6},{8,9},{9,8},{10,11... | collective-permute-start | bytes 1572872 | tf_op jit(solution)/shard_map/ppermute | solution.py:45
  23.8 0.0 collective-permute-done.16.refs_25_
  23.8 1.3 %collective-permute-done.17.refs_26_ = bf16[16,4096]{1,0:T(8,128)(2,1)S(1)} collective-permute-done((bf16[16,4096]{1,0:T(8,128)(2,1)S(1)}, bf16[16,4096]{1,0:T(8,128)(2,1)S(1)}, u32[]{:S(2)}, u32[]{:S(2)}) %collective-permute-start.17) | collective-permute-done | bytes 131104 | tf_op jit(solution)/shard_map/ppermute | solution.py:42
  25.1 1.5 %collective-permute-start.18 = (bf16[64,4096]{1,0:T(8,128)(2,1)S(1)}, bf16[64,4096]{1,0:T(8,128)(2,1)S(1)}, u32[]{:S(2)}, u32[]{:S(2)}) collective-permute-start(bf16[64,4096]{1,0:T(8,128)(2,1)S(1)} %pad_maximum_fusion.1), channel_id=1, source_target_pairs={{0,1},{1,0},{2,3},{3,2},{4,5},{5,4},{6,7},{7,6},{8,9},{9,8},{10,11... | collective-permute-start | bytes 1572872 | tf_op jit(solution)/shard_map/ppermute | solution.py:45
  26.6 0.0 collective-permute-done.13.refs_9_
  26.6 0.0 collective-permute-done.9.refs_4_.refs_22_
  26.6 0.0 copy-done
  26.6 2.9 %shard_map.38 = (bf16[512,256]{1,0:T(8,128)(2,1)S(1)}, bf16[512,256]{1,0:T(8,128)(2,1)S(1)}, bf16[512,256]{1,0:T(8,128)(2,1)S(1)}, bf16[512,256]{1,0:T(8,128)(2,...) custom-call(bf16[512,4096]{1,0:T(8,128)(2,1)S(1)} %copy-done, ...), custom_call_target="tpu_custom_call" | custom-call | flops 1073741824 | bytes 6291456 | tf_op jit(solution)/shard_map/pallas_call | solution.py:228
  29.6 0.0 collective-permute-done.18.refs_27_
  29.6 2.1 %shard_map.39 = f32[1,512]{1,0:T(1,128)} custom-call(bf16[512,256]{1,0:T(8,128)(2,1)S(1)} %get-tuple-element.27.refs_0_, bf16[512,256]{1,0:T(8,128)(2,1)S(1)} %get-tuple-element.28.refs_1_, bf16[512,256]{1,0:T(8,128)(2,1)S(1)} %get-tuple-element.29.refs_2_, bf16[512,256]{1,0:T(8,128)(2,1)S(1)} %get-tuple-element.30.refs_3_, ...), custom_call_target="tpu_custom_call" | custom-call | flops 1073741824 | bytes 6291456 | tf_op jit(solution)/shard_map/pallas_call | solution.py:228
  (10 shorter events, 0.2 us)
Async XLA Ops:
  0.0 26.6 %copy-start = (bf16[512,4096]{1,0:T(8,128)(2,1)S(1)}, bf16[512,4096]{1,0:T(8,128)(2,1)}, u32[]{:S(2)}) copy-start(bf16[512,4096]{1,0:T(8,128)(2,1)} %queries.1) | copy-start | bytes 12582916
  0.0 4.0 %collective-permute-start = (bf16[16,4096]{1,0:T(8,128)(2,1)}, bf16[16,4096]{1,0:T(8,128)(2,1)S(1)}, u32[]{:S(2)}, u32[]{:S(2)}) collective-permute-start(bf16[16,4096]{1,0:T(8,128)(2,1)} %param.5), channel_id=1, source_target_pairs={{0,1},{1,0},{2,3},{3,2},{4,5},{5,4},{6,7},{7,6},{8,9},{9,8},{10,11... | collective-permute-start | bytes 393224 | tf_op jit(solution)/shard_map/ppermute | solution.py:45
  0.1 5.6 %collective-permute-start.3 = (bf16[16,4096]{1,0:T(8,128)(2,1)}, bf16[16,4096]{1,0:T(8,128)(2,1)S(1)}, u32[]{:S(2)}, u32[]{:S(2)}) collective-permute-start(bf16[16,4096]{1,0:T(8,128)(2,1)} %param.5), channel_id=1, source_target_pairs={{0,4},{1,3},{4,8},{5,1},{8,12},{9,5},{12,14},{13,9},{14,10},{15,13... | collective-permute-start | bytes 393224 | tf_op jit(solution)/shard_map/ppermute | solution.py:42
  2.7 4.4 %collective-permute-start.5 = (bf16[16,4096]{1,0:T(8,128)(2,1)}, bf16[16,4096]{1,0:T(8,128)(2,1)S(1)}, u32[]{:S(2)}, u32[]{:S(2)}) collective-permute-start(bf16[16,4096]{1,0:T(8,128)(2,1)} %param.4), channel_id=1, source_target_pairs={{0,1},{1,0},{2,3},{3,2},{4,5},{5,4},{6,7},{7,6},{8,9},{9,8},{10,11... | collective-permute-start | bytes 393224 | tf_op jit(solution)/shard_map/ppermute | solution.py:45
  3.1 5.4 %collective-permute-start.6 = (bf16[16,4096]{1,0:T(8,128)(2,1)}, bf16[16,4096]{1,0:T(8,128)(2,1)S(1)}, u32[]{:S(2)}, u32[]{:S(2)}) collective-permute-start(bf16[16,4096]{1,0:T(8,128)(2,1)} %param.4), channel_id=1, source_target_pairs={{0,4},{1,3},{4,8},{5,1},{8,12},{9,5},{12,14},{13,9},{14,10},{15,13... | collective-permute-start | bytes 393224 | tf_op jit(solution)/shard_map/ppermute | solution.py:42
  4.1 5.8 %collective-permute-start.1 = (bf16[16,4096]{1,0:T(8,128)(2,1)S(1)}, bf16[16,4096]{1,0:T(8,128)(2,1)S(1)}, u32[]{:S(2)}, u32[]{:S(2)}) collective-permute-start(bf16[16,4096]{1,0:T(8,128)(2,1)S(1)} %collective-permute-done.rows.refs_0_), channel_id=1, source_target_pairs={{0,4},{1,3},{4,8},{5,1},{8,12},{9,5},{12,14},{13,9},{14,10},{15,13... | collective-permute-start | bytes 393224 | tf_op jit(solution)/shard_map/ppermute | solution.py:42
  5.7 5.4 %collective-permute-start.4 = (bf16[16,4096]{1,0:T(8,128)(2,1)S(1)}, bf16[16,4096]{1,0:T(8,128)(2,1)S(1)}, u32[]{:S(2)}, u32[]{:S(2)}) collective-permute-start(bf16[16,4096]{1,0:T(8,128)(2,1)S(1)} %collective-permute-done.3.refs_1_), channel_id=1, source_target_pairs={{0,4},{1,3},{4,8},{5,1},{8,12},{9,5},{12,14},{13,9},{14,10},{15,13... | collective-permute-start | bytes 393224 | tf_op jit(solution)/shard_map/ppermute | solution.py:42
  7.2 4.5 %collective-permute-start.7 = (bf16[16,4096]{1,0:T(8,128)(2,1)S(1)}, bf16[16,4096]{1,0:T(8,128)(2,1)S(1)}, u32[]{:S(2)}, u32[]{:S(2)}) collective-permute-start(bf16[16,4096]{1,0:T(8,128)(2,1)S(1)} %collective-permute-done.5.refs_18_), channel_id=1, source_target_pairs={{0,4},{1,3},{4,8},{5,1},{8,12},{9,5},{12,14},{13,9},{14,10},{15,13... | collective-permute-start | bytes 393224 | tf_op jit(solution)/shard_map/ppermute | solution.py:42
  8.5 4.5 %collective-permute-start.8 = (bf16[16,4096]{1,0:T(8,128)(2,1)S(1)}, bf16[16,4096]{1,0:T(8,128)(2,1)S(1)}, u32[]{:S(2)}, u32[]{:S(2)}) collective-permute-start(bf16[16,4096]{1,0:T(8,128)(2,1)S(1)} %collective-permute-done.6.refs_19_), channel_id=1, source_target_pairs={{0,4},{1,3},{4,8},{5,1},{8,12},{9,5},{12,14},{13,9},{14,10},{15,13... | collective-permute-start | bytes 393224 | tf_op jit(solution)/shard_map/ppermute | solution.py:42
  9.8 4.7 %collective-permute-start.2 = (bf16[16,4096]{1,0:T(8,128)(2,1)S(1)}, bf16[16,4096]{1,0:T(8,128)(2,1)S(1)}, u32[]{:S(2)}, u32[]{:S(2)}) collective-permute-start(bf16[16,4096]{1,0:T(8,128)(2,1)S(1)} %collective-permute-done.1.refs_2_), channel_id=1, source_target_pairs={{0,4},{1,3},{4,8},{5,1},{8,12},{9,5},{12,14},{13,9},{14,10},{15,13... | collective-permute-start | bytes 393224 | tf_op jit(solution)/shard_map/ppermute | solution.py:42
  11.1 4.8 %collective-permute-start.10 = (bf16[16,4096]{1,0:T(8,128)(2,1)S(1)}, bf16[16,4096]{1,0:T(8,128)(2,1)S(1)}, u32[]{:S(2)}, u32[]{:S(2)}) collective-permute-start(bf16[16,4096]{1,0:T(8,128)(2,1)S(1)} %collective-permute-done.4.refs_3_), channel_id=1, source_target_pairs={{0,4},{1,3},{4,8},{5,1},{8,12},{9,5},{12,14},{13,9},{14,10},{15,13... | collective-permute-start | bytes 393224 | tf_op jit(solution)/shard_map/ppermute | solution.py:42
  11.7 7.9 %collective-permute-start.14 = (bf16[16,4096]{1,0:T(8,128)(2,1)S(1)}, bf16[16,4096]{1,0:T(8,128)(2,1)S(1)}, u32[]{:S(2)}, u32[]{:S(2)}) collective-permute-start(bf16[16,4096]{1,0:T(8,128)(2,1)S(1)} %collective-permute-done.7.refs_20_), channel_id=1, source_target_pairs={{0,4},{1,3},{4,8},{5,1},{8,12},{9,5},{12,14},{13,9},{14,10},{15,13... | collective-permute-start | bytes 393224 | tf_op jit(solution)/shard_map/ppermute | solution.py:42
  13.0 7.0 %collective-permute-start.15 = (bf16[16,4096]{1,0:T(8,128)(2,1)S(1)}, bf16[16,4096]{1,0:T(8,128)(2,1)S(1)}, u32[]{:S(2)}, u32[]{:S(2)}) collective-permute-start(bf16[16,4096]{1,0:T(8,128)(2,1)S(1)} %collective-permute-done.8.refs_21_), channel_id=1, source_target_pairs={{0,4},{1,3},{4,8},{5,1},{8,12},{9,5},{12,14},{13,9},{14,10},{15,13... | collective-permute-start | bytes 393224 | tf_op jit(solution)/shard_map/ppermute | solution.py:42
  14.5 5.9 %collective-permute-start.11 = (bf16[16,4096]{1,0:T(8,128)(2,1)S(1)}, bf16[16,4096]{1,0:T(8,128)(2,1)S(1)}, u32[]{:S(2)}, u32[]{:S(2)}) collective-permute-start(bf16[16,4096]{1,0:T(8,128)(2,1)S(1)} %collective-permute-done.2.refs_5_), channel_id=1, source_target_pairs={{0,4},{1,3},{4,8},{5,1},{8,12},{9,5},{12,14},{13,9},{14,10},{15,13... | collective-permute-start | bytes 393224 | tf_op jit(solution)/shard_map/ppermute | solution.py:42
  15.9 5.6 %collective-permute-start.12 = (bf16[16,4096]{1,0:T(8,128)(2,1)S(1)}, bf16[16,4096]{1,0:T(8,128)(2,1)S(1)}, u32[]{:S(2)}, u32[]{:S(2)}) collective-permute-start(bf16[16,4096]{1,0:T(8,128)(2,1)S(1)} %collective-permute-done.10.refs_6_), channel_id=1, source_target_pairs={{0,4},{1,3},{4,8},{5,1},{8,12},{9,5},{12,14},{13,9},{14,10},{15,13... | collective-permute-start | bytes 393224 | tf_op jit(solution)/shard_map/ppermute | solution.py:42
  16.9 9.7 %collective-permute-start.9 = (bf16[128,4096]{1,0:T(8,128)(2,1)S(1)}, bf16[128,4096]{1,0:T(8,128)(2,1)S(1)}, u32[]{:S(2)}, u32[]{:S(2)}) collective-permute-start(bf16[128,4096]{1,0:T(8,128)(2,1)S(1)} %constant_dynamic-update-slice_fusion), channel_id=1, source_target_pairs={{0,1},{1,0},{2,3},{3,2},{4,5},{5,4},{6,7},{7,6},{8,9},{9,8},{10,11... | collective-permute-start | bytes 3145736 | tf_op jit(solution)/shard_map/ppermute | solution.py:45
  19.6 4.2 %collective-permute-start.16 = (bf16[16,4096]{1,0:T(8,128)(2,1)S(1)}, bf16[16,4096]{1,0:T(8,128)(2,1)S(1)}, u32[]{:S(2)}, u32[]{:S(2)}) collective-permute-start(bf16[16,4096]{1,0:T(8,128)(2,1)S(1)} %collective-permute-done.14.refs_23_), channel_id=1, source_target_pairs={{0,4},{1,3},{4,8},{5,1},{8,12},{9,5},{12,14},{13,9},{14,10},{15,13... | collective-permute-start | bytes 393224 | tf_op jit(solution)/shard_map/ppermute | solution.py:42
  20.0 5.1 %collective-permute-start.17 = (bf16[16,4096]{1,0:T(8,128)(2,1)S(1)}, bf16[16,4096]{1,0:T(8,128)(2,1)S(1)}, u32[]{:S(2)}, u32[]{:S(2)}) collective-permute-start(bf16[16,4096]{1,0:T(8,128)(2,1)S(1)} %collective-permute-done.15.refs_24_), channel_id=1, source_target_pairs={{0,4},{1,3},{4,8},{5,1},{8,12},{9,5},{12,14},{13,9},{14,10},{15,13... | collective-permute-start | bytes 393224 | tf_op jit(solution)/shard_map/ppermute | solution.py:42
  21.5 5.1 %collective-permute-start.13 = (bf16[64,4096]{1,0:T(8,128)(2,1)S(1)}, bf16[64,4096]{1,0:T(8,128)(2,1)S(1)}, u32[]{:S(2)}, u32[]{:S(2)}) collective-permute-start(bf16[64,4096]{1,0:T(8,128)(2,1)S(1)} %pad_maximum_fusion), channel_id=1, source_target_pairs={{0,1},{1,0},{2,3},{3,2},{4,5},{5,4},{6,7},{7,6},{8,9},{9,8},{10,11... | collective-permute-start | bytes 1572872 | tf_op jit(solution)/shard_map/ppermute | solution.py:45
  25.1 4.4 %collective-permute-start.18 = (bf16[64,4096]{1,0:T(8,128)(2,1)S(1)}, bf16[64,4096]{1,0:T(8,128)(2,1)S(1)}, u32[]{:S(2)}, u32[]{:S(2)}) collective-permute-start(bf16[64,4096]{1,0:T(8,128)(2,1)S(1)} %pad_maximum_fusion.1), channel_id=1, source_target_pairs={{0,1},{1,0},{2,3},{3,2},{4,5},{5,4},{6,7},{7,6},{8,9},{9,8},{10,11... | collective-permute-start | bytes 1572872 | tf_op jit(solution)/shard_map/ppermute | solution.py:45

commit v19 on v14

--- a/solution.py
+++ b/solution.py
@@ -34,7 +34,7 @@
     return [(i, i ^ 1) for i in range(size)]
 
 
-def gather_panels(panels, size, on_first):
+def gather_panels(panels, size, on_first, on_next):
     twins, ring = core_pairs(size), ring_pairs(size)
     chips, rows = size // 2, panels[0].shape[0]
 
@@ -65,7 +65,13 @@
         if last:
             for i in range(len(panels)):
                 if fresh[i]:
-                    block = hand_over(jnp.concatenate(fresh[i], axis=0))
+                    block = jnp.concatenate(fresh[i], axis=0)
+                    if i == 0:
+                        now = [k for k, piece in enumerate(pieces[0]) if k and piece[0].shape[0] == rows]
+                        late = [k for k in range(1, len(pieces[0]) + 1) if k not in now]
+                        total = on_next([pieces[0][k] for k in now])
+                        block, total = lax.optimization_barrier((block, total))
+                    block = hand_over(block)
                     pieces[i].append((block, 0, block.shape[0]))
         elif period and period < steps - 1:
             block, at = hand_over(jnp.concatenate([f for g in fresh for f in g], axis=0)), 0
@@ -73,7 +79,7 @@
                 upto = at + rows * len(fresh[i])
                 pieces[i].append((block, at, upto))
                 fresh[i], at = [], upto
-    return pieces, extra
+    return pieces, (extra, total), late
 
 
 def row_groups(rows, step):
@@ -134,46 +140,54 @@
 
 def log_sum(squares, scores, queries):
     half = 0.5 * jnp.sum(squares[...], axis=1, keepdims=True)
-    x = (scores[:, queries] - half) / TEMP
+    x = (scores[:, queries] - half) * (1 / TEMP)
     top = jnp.max(x, axis=0, keepdims=True)
     return jnp.log(jnp.sum(jnp.exp(x - top), axis=0, keepdims=True)) + top
 
 
-def total_kernel(rows, total):
-    total[...] = jnp.sum(rows[...].astype(jnp.float32), axis=0, keepdims=True)
-
-
-def feature_total(rows, beside):
+def total_kernel(spans, *refs):
+    *panel, total = refs
+    for start in range(0, total.shape[1], CHUNK):
+        cols = slice(start, start + CHUNK)
+        sums = [
+            jnp.sum(ref[low:high, cols].astype(jnp.float32), axis=0, keepdims=True)
+            for ref, (low, high) in zip(panel, spans)
+        ]
+        total[:, cols] = functools.reduce(jnp.add, sums)
+
+
+def feature_total(pieces, cost):
     in_vmem = pl.BlockSpec(memory_space=pltpu.VMEM)
+    spans = [(low, high) for _, low, high in pieces]
+    arrays = [array for array, _, _ in pieces]
     return pl.pallas_call(
-        total_kernel,
-        out_shape=jax.ShapeDtypeStruct((1, rows.shape[1]), jnp.float32),
-        in_specs=[in_vmem],
+        functools.partial(total_kernel, spans),
+        out_shape=jax.ShapeDtypeStruct((1, arrays[0].shape[1]), jnp.float32),
+        in_specs=[in_vmem] * len(arrays),
         out_specs=in_vmem,
         compiler_params=pltpu.CompilerParams(vmem_limit_bytes=LIMIT),
-        cost_estimate=pl.CostEstimate(
-            flops=rows.size, bytes_accessed=4 * beside.size, transcendentals=0
-        ),
-    )(rows)
-
-
-def ref_kernel(spans, queries, first_total, *refs):
+        cost_estimate=pl.CostEstimate(flops=0, bytes_accessed=cost, transcendentals=0),
+    )(*arrays)
+
+
+def ref_kernel(late, spans, queries, *refs):
+    totals, refs = refs[:2], refs[2:]
     panel, (probes, mean, ref_log, centered, squares, scores) = refs[: len(spans)], refs[len(spans) :]
     groups = panel_groups(panel, spans)
     count, features = centered.shape
-
-    def take_mean(cols):
-        total = first_total[:, cols]
-        for ref, rows, _ in groups:
-            if ref is not panel[0]:
-                total += jnp.sum(ref[rows, cols].astype(jnp.float32), axis=0, keepdims=True)
+    for start in range(0, features, CHUNK):
+        cols = slice(start, start + CHUNK)
+        total = totals[0][:, cols] + totals[1][:, cols]
+        for k in late:
+            low, high = spans[k]
+            total += jnp.sum(panel[k][low:high, cols].astype(jnp.float32), axis=0, keepdims=True)
         mean[:, cols] = total / count
 
     def center_queries(rows, cols):
         probes[rows, cols] = center(queries[rows, cols], mean[:, cols])
 
     def prepare(cols, first):
-        work = [functools.partial(take_mean, cols)]
+        work = []
         for group in groups:
             work.append(functools.partial(center_group, group, cols, mean, centered, squares, first))
         for rows in row_groups(probes.shape[0], GROUP):
@@ -226,14 +240,17 @@
 
 def body(queries, gen_panel, ref_panel):
     panels = [ref_panel, gen_panel]
-    (ref_pieces, gen_pieces), first_total = gather_panels(
-        panels, lax.axis_size("samp"), functools.partial(feature_total, beside=queries)
+    (ref_pieces, gen_pieces), totals, late = gather_panels(
+        panels,
+        lax.axis_size("samp"),
+        lambda rows: feature_total([(rows, 0, rows.shape[0])], 4 * queries.size),
+        lambda pieces: feature_total(pieces, 0),
     )
     count, features = queries.shape
     logs = jax.ShapeDtypeStruct((1, count), jnp.float32)
     probes, mean, ref_log = call(
-        ref_kernel,
-        [queries, first_total],
+        functools.partial(ref_kernel, late),
+        [queries, *totals],
         ref_pieces,
         count,
         (

time: 31.2 us -> 30.8 us (0.987)
    pallas_call x2, Pallas kernels: 4.39 us -> 3.99 us  [call(): pl.pallas_call(functools.partial(kernel, spans), out_shape=out_shape, in_...]
  transfers between devices with their start and end apart: 19 -> 19, of which waited for: 7 -> 7; matrix products, arithmetic and copies ran while one was open for 1% -> 0% of each run, Pallas kernels for 8% -> 7%
where the time goes in v19:
time: 30.8 us; the launch traced here: 30.6 us
  starting transfers between devices  22.3 us (72%)
  Pallas kernels  4.35 us (14%)
  waiting for transfers between devices  3.74 us (12%)
    ppermute x14, starting transfers between devices, hop(): return lax.ppermute(block, 'samp', ring)  15.4 us
    ppermute x5, starting transfers between devices, hand_over(): return lax.ppermute(block, 'samp', twins)  6.88 us
    pallas_call x2, Pallas kernels, call(): pl.pallas_call(functools.partial(kernel, spans), out_shape=out_shape, in_...  3.99 us
    ppermute x14, waiting for transfers between devices, hop(): return lax.ppermute(block, 'samp', ring)  3.72 us
  transfers between devices with their start and end apart: 19, of which 7 were waited for; matrix products, arithmetic and copies ran while one was open for 0% of the time, Pallas kernels for 7%

profile of v19, /device:TPU:1, one launch (start us, length us, event | category | flops | bytes accessed | tf_op | source)
XLA Modules:
  0.0 30.6 jit_solution(6552837289217194559)
XLA Ops:
  0.0 0.0 copy-start
  0.0 0.1 collective-permute-start
  0.1 2.7 %collective-permute-start.3 = (bf16[16,4096]{1,0:T(8,128)(2,1)}, bf16[16,4096]{1,0:T(8,128)(2,1)S(1)}, u32[]{:S(2)}, u32[]{:S(2)}) collective-permute-start(bf16[16,4096]{1,0:T(8,128)(2,1)} %param.5), channel_id=1, source_target_pairs={{0,4},{1,3},{4,8},{5,1},{8,12},{9,5},{12,14},{13,9},{14,10},{15,13... | collective-permute-start | bytes 393224 | tf_op jit(solution)/shard_map/ppermute | solution.py:42
  2.7 0.4 %collective-permute-start.8 = (bf16[16,4096]{1,0:T(8,128)(2,1)}, bf16[16,4096]{1,0:T(8,128)(2,1)S(1)}, u32[]{:S(2)}, u32[]{:S(2)}) collective-permute-start(bf16[16,4096]{1,0:T(8,128)(2,1)} %param.4), channel_id=1, source_target_pairs={{0,1},{1,0},{2,3},{3,2},{4,5},{5,4},{6,7},{7,6},{8,9},{9,8},{10,11... | collective-permute-start | bytes 393224 | tf_op jit(solution)/shard_map/ppermute | solution.py:45
  3.1 0.9 %collective-permute-start.9 = (bf16[16,4096]{1,0:T(8,128)(2,1)}, bf16[16,4096]{1,0:T(8,128)(2,1)S(1)}, u32[]{:S(2)}, u32[]{:S(2)}) collective-permute-start(bf16[16,4096]{1,0:T(8,128)(2,1)} %param.4), channel_id=1, source_target_pairs={{0,4},{1,3},{4,8},{5,1},{8,12},{9,5},{12,14},{13,9},{14,10},{15,13... | collective-permute-start | bytes 393224 | tf_op jit(solution)/shard_map/ppermute | solution.py:42
  4.0 0.0 collective-permute-done.refs_0_.refs_2_
  4.1 1.3 %collective-permute-start.1 = (bf16[16,4096]{1,0:T(8,128)(2,1)S(1)}, bf16[16,4096]{1,0:T(8,128)(2,1)S(1)}, u32[]{:S(2)}, u32[]{:S(2)}) collective-permute-start(bf16[16,4096]{1,0:T(8,128)(2,1)S(1)} %collective-permute-done.refs_0_.refs_2_), channel_id=1, source_target_pairs={{0,4},{1,3},{4,8},{5,1},{8,12},{9,5},{12,14},{13,9},{14,10},{15,13... | collective-permute-start | bytes 393224 | tf_op jit(solution)/shard_map/ppermute | solution.py:42
  5.4 0.3 collective-permute-done.3.refs_0_.refs_3_
  5.7 1.4 %collective-permute-start.4 = (bf16[16,4096]{1,0:T(8,128)(2,1)S(1)}, bf16[16,4096]{1,0:T(8,128)(2,1)S(1)}, u32[]{:S(2)}, u32[]{:S(2)}) collective-permute-start(bf16[16,4096]{1,0:T(8,128)(2,1)S(1)} %collective-permute-done.3.refs_0_.refs_3_), channel_id=1, source_target_pairs={{0,4},{1,3},{4,8},{5,1},{8,12},{9,5},{12,14},{13,9},{14,10},{15,13... | collective-permute-start | bytes 393224 | tf_op jit(solution)/shard_map/ppermute | solution.py:42
  7.1 0.1 shard_map.37.refs_0_
  7.1 0.0 collective-permute-done.8.refs_0_
  7.2 1.3 %collective-permute-start.10 = (bf16[16,4096]{1,0:T(8,128)(2,1)S(1)}, bf16[16,4096]{1,0:T(8,128)(2,1)S(1)}, u32[]{:S(2)}, u32[]{:S(2)}) collective-permute-start(bf16[16,4096]{1,0:T(8,128)(2,1)S(1)} %collective-permute-done.8.refs_0_), channel_id=1, source_target_pairs={{0,4},{1,3},{4,8},{5,1},{8,12},{9,5},{12,14},{13,9},{14,10},{15,13... | collective-permute-start | bytes 393224 | tf_op jit(solution)/shard_map/ppermute | solution.py:42
  8.5 0.0 collective-permute-done.9.refs_1_
  8.5 1.3 %collective-permute-start.11 = (bf16[16,4096]{1,0:T(8,128)(2,1)S(1)}, bf16[16,4096]{1,0:T(8,128)(2,1)S(1)}, u32[]{:S(2)}, u32[]{:S(2)}) collective-permute-start(bf16[16,4096]{1,0:T(8,128)(2,1)S(1)} %collective-permute-done.9.refs_1_), channel_id=1, source_target_pairs={{0,4},{1,3},{4,8},{5,1},{8,12},{9,5},{12,14},{13,9},{14,10},{15,13... | collective-permute-start | bytes 393224 | tf_op jit(solution)/shard_map/ppermute | solution.py:42
  9.8 0.0 collective-permute-done.1.refs_1_.refs_4_
  9.8 1.3 %collective-permute-start.2 = (bf16[16,4096]{1,0:T(8,128)(2,1)S(1)}, bf16[16,4096]{1,0:T(8,128)(2,1)S(1)}, u32[]{:S(2)}, u32[]{:S(2)}) collective-permute-start(bf16[16,4096]{1,0:T(8,128)(2,1)S(1)} %collective-permute-done.1.refs_1_.refs_4_), channel_id=1, source_target_pairs={{0,4},{1,3},{4,8},{5,1},{8,12},{9,5},{12,14},{13,9},{14,10},{15,13... | collective-permute-start | bytes 393224 | tf_op jit(solution)/shard_map/ppermute | solution.py:42
  11.1 0.0 collective-permute-done.4.refs_2_.refs_5_
  11.1 0.2 collective-permute-start.5
  11.4 0.3 collective-permute-done.10.refs_2_
  11.7 1.0 %collective-permute-start.14 = (bf16[16,4096]{1,0:T(8,128)(2,1)S(1)}, bf16[16,4096]{1,0:T(8,128)(2,1)S(1)}, u32[]{:S(2)}, u32[]{:S(2)}) collective-permute-start(bf16[16,4096]{1,0:T(8,128)(2,1)S(1)} %collective-permute-done.10.refs_2_), channel_id=1, source_target_pairs={{0,4},{1,3},{4,8},{5,1},{8,12},{9,5},{12,14},{13,9},{14,10},{15,13... | collective-permute-start | bytes 393224 | tf_op jit(solution)/shard_map/ppermute | solution.py:42
  12.7 0.3 collective-permute-done.11.refs_3_
  13.0 1.1 %collective-permute-start.15 = (bf16[16,4096]{1,0:T(8,128)(2,1)S(1)}, bf16[16,4096]{1,0:T(8,128)(2,1)S(1)}, u32[]{:S(2)}, u32[]{:S(2)}) collective-permute-start(bf16[16,4096]{1,0:T(8,128)(2,1)S(1)} %collective-permute-done.11.refs_3_), channel_id=1, source_target_pairs={{0,4},{1,3},{4,8},{5,1},{8,12},{9,5},{12,14},{13,9},{14,10},{15,13... | collective-permute-start | bytes 393224 | tf_op jit(solution)/shard_map/ppermute | solution.py:42
  14.1 0.4 %collective-permute-done.2.refs_3_.refs_7_ = bf16[16,4096]{1,0:T(8,128)(2,1)S(1)} collective-permute-done((bf16[16,4096]{1,0:T(8,128)(2,1)S(1)}, bf16[16,4096]{1,0:T(8,128)(2,1)S(1)}, u32[]{:S(2)}, u32[]{:S(2)}) %collective-permute-start.2) | collective-permute-done | bytes 131104 | tf_op jit(solution)/shard_map/ppermute | solution.py:42
  14.5 1.0 %collective-permute-start.6 = (bf16[16,4096]{1,0:T(8,128)(2,1)S(1)}, bf16[16,4096]{1,0:T(8,128)(2,1)S(1)}, u32[]{:S(2)}, u32[]{:S(2)}) collective-permute-start(bf16[16,4096]{1,0:T(8,128)(2,1)S(1)} %collective-permute-done.2.refs_3_.refs_7_), channel_id=1, source_target_pairs={{0,4},{1,3},{4,8},{5,1},{8,12},{9,5},{12,14},{13,9},{14,10},{15,13... | collective-permute-start | bytes 393224 | tf_op jit(solution)/shard_map/ppermute | solution.py:42
  15.5 0.4 %collective-permute-done.5.refs_4_.refs_8_ = bf16[16,4096]{1,0:T(8,128)(2,1)S(1)} collective-permute-done((bf16[16,4096]{1,0:T(8,128)(2,1)S(1)}, bf16[16,4096]{1,0:T(8,128)(2,1)S(1)}, u32[]{:S(2)}, u32[]{:S(2)}) %collective-permute-start.5) | collective-permute-done | bytes 131104 | tf_op jit(solution)/shard_map/ppermute | solution.py:42
  15.9 1.0 %collective-permute-start.7 = (bf16[16,4096]{1,0:T(8,128)(2,1)S(1)}, bf16[16,4096]{1,0:T(8,128)(2,1)S(1)}, u32[]{:S(2)}, u32[]{:S(2)}) collective-permute-start(bf16[16,4096]{1,0:T(8,128)(2,1)S(1)} %collective-permute-done.5.refs_4_.refs_8_), channel_id=1, source_target_pairs={{0,4},{1,3},{4,8},{5,1},{8,12},{9,5},{12,14},{13,9},{14,10},{15,13... | collective-permute-start | bytes 393224 | tf_op jit(solution)/shard_map/ppermute | solution.py:42
  16.9 2.7 %collective-permute-start.12 = (bf16[128,4096]{1,0:T(8,128)(2,1)S(1)}, bf16[128,4096]{1,0:T(8,128)(2,1)S(1)}, u32[]{:S(2)}, u32[]{:S(2)}) collective-permute-start(bf16[128,4096]{1,0:T(8,128)(2,1)S(1)} %constant_dynamic-update-slice_fusion), channel_id=1, source_target_pairs={{0,1},{1,0},{2,3},{3,2},{4,5},{5,4},{6,7},{7,6},{8,9},{9,8},{10,11... | collective-permute-start | bytes 3145736 | tf_op jit(solution)/shard_map/ppermute | solution.py:45
  19.6 0.0 collective-permute-done.14.refs_5_
  19.6 0.4 %collective-permute-start.16 = (bf16[16,4096]{1,0:T(8,128)(2,1)S(1)}, bf16[16,4096]{1,0:T(8,128)(2,1)S(1)}, u32[]{:S(2)}, u32[]{:S(2)}) collective-permute-start(bf16[16,4096]{1,0:T(8,128)(2,1)S(1)} %collective-permute-done.14.refs_5_), channel_id=1, source_target_pairs={{0,4},{1,3},{4,8},{5,1},{8,12},{9,5},{12,14},{13,9},{14,10},{15,13... | collective-permute-start | bytes 393224 | tf_op jit(solution)/shard_map/ppermute | solution.py:42
  20.0 0.0 collective-permute-done.15.refs_6_
  20.0 0.4 %collective-permute-start.17 = (bf16[16,4096]{1,0:T(8,128)(2,1)S(1)}, bf16[16,4096]{1,0:T(8,128)(2,1)S(1)}, u32[]{:S(2)}, u32[]{:S(2)}) collective-permute-start(bf16[16,4096]{1,0:T(8,128)(2,1)S(1)} %collective-permute-done.15.refs_6_), channel_id=1, source_target_pairs={{0,4},{1,3},{4,8},{5,1},{8,12},{9,5},{12,14},{13,9},{14,10},{15,13... | collective-permute-start | bytes 393224 | tf_op jit(solution)/shard_map/ppermute | solution.py:42
  20.4 0.0 collective-permute-done.6.refs_5_.refs_9_
  20.4 1.1 %collective-permute-done.7.refs_6_.refs_10_ = bf16[16,4096]{1,0:T(8,128)(2,1)S(1)} collective-permute-done((bf16[16,4096]{1,0:T(8,128)(2,1)S(1)}, bf16[16,4096]{1,0:T(8,128)(2,1)S(1)}, u32[]{:S(2)}, u32[]{:S(2)}) %collective-permute-start.7) | collective-permute-done | bytes 131104 | tf_op jit(solution)/shard_map/ppermute | solution.py:42
  21.5 0.3 %shard_map.38.refs_1_ = f32[1,4096]{1,0:T(1,128)S(1)} custom-call(bf16[16,4096]{1,0:T(8,128)(2,1)S(1)} %collective-permute-done.3.refs_0_.refs_3_, bf16[16,4096]{1,0:T(8,128)(2,1)S(1)} %collective-permute-done.1.refs_1_.refs_4_, bf16[16,4096]{1,0:T(8,128)(2,1)S(1)} %collective-permute-done.4.refs_2_.refs_5_, ...), custom_call_target="tpu_custom_call" | custom-call | tf_op jit(solution)/shard_map/pallas_call | solution.py:163
  21.9 2.3 %collective-permute-start.13 = (bf16[64,4096]{1,0:T(8,128)(2,1)S(1)}, bf16[64,4096]{1,0:T(8,128)(2,1)S(1)}, u32[]{:S(2)}, u32[]{:S(2)}) collective-permute-start(bf16[64,4096]{1,0:T(8,128)(2,1)S(1)} %pad_maximum_fusion), channel_id=1, source_target_pairs={{0,1},{1,0},{2,3},{3,2},{4,5},{5,4},{6,7},{7,6},{8,9},{9,8},{10,11... | collective-permute-start | bytes 1572872 | tf_op jit(solution)/shard_map/ppermute | solution.py:45
  24.1 0.0 collective-permute-done.16.refs_7_
  24.1 1.0 %collective-permute-done.17.refs_8_ = bf16[16,4096]{1,0:T(8,128)(2,1)S(1)} collective-permute-done((bf16[16,4096]{1,0:T(8,128)(2,1)S(1)}, bf16[16,4096]{1,0:T(8,128)(2,1)S(1)}, u32[]{:S(2)}, u32[]{:S(2)}) %collective-permute-start.17) | collective-permute-done | bytes 131104 | tf_op jit(solution)/shard_map/ppermute | solution.py:42
  25.1 1.5 %collective-permute-start.18 = (bf16[64,4096]{1,0:T(8,128)(2,1)S(1)}, bf16[64,4096]{1,0:T(8,128)(2,1)S(1)}, u32[]{:S(2)}, u32[]{:S(2)}) collective-permute-start(bf16[64,4096]{1,0:T(8,128)(2,1)S(1)} %pad_maximum_fusion.1), channel_id=1, source_target_pairs={{0,1},{1,0},{2,3},{3,2},{4,5},{5,4},{6,7},{7,6},{8,9},{9,8},{10,11... | collective-permute-start | bytes 1572872 | tf_op jit(solution)/shard_map/ppermute | solution.py:45
  26.6 0.0 collective-permute-done.13.refs_11_
  26.6 0.0 collective-permute-done.12.refs_6_.refs_4_
  26.6 0.0 copy-done
  26.6 1.9 %shard_map.39 = (bf16[512,4096]{1,0:T(8,128)(2,1)S(1)}, f32[1,4096]{1,0:T(1,128)S(1)}, f32[1,512]{1,0:T(1,128)S(1)}) custom-call(bf16[512,4096]{1,0:T(8,128)(2,1)S(1)} %copy-done, f32[1,4096]{1,0:T(1,128)S(1)} %shard_map.37.refs_0_, f32[1,4096]{1,0:T(1,128)S(1)} %shard_map.38.refs_1_, bf16[16,4096]{1,0:T(8,128)(2,1)S(1)} %collective-permute-done.refs_0_.refs_2_, ...), custom_call_target="tpu_custom_call" | custom-call | flops 1073741824 | bytes 6291456 | tf_op jit(solution)/shard_map/pallas_call | solution.py:222
  28.6 0.0 collective-permute-done.18.refs_9_
  28.6 2.1 %shard_map.40 = f32[1,512]{1,0:T(1,128)} custom-call(f32[1,512]{1,0:T(1,128)S(1)} %get-tuple-element.16.ref_log, bf16[512,4096]{1,0:T(8,128)(2,1)S(1)} %get-tuple-element.17.probes, f32[1,4096]{1,0:T(1,128)S(1)} %get-tuple-element.18.mean, bf16[16,4096]{1,0:T(8,128)(2,1)S(1)} %collective-permute-done.8.refs_0_, ...), custom_call_target="tpu_custom_call" | custom-call | flops 1073741824 | bytes 6291456 | tf_op jit(solution)/shard_map/pallas_call | solution.py:222
  (10 shorter events, 0.1 us)
Async XLA Ops:
  0.0 26.6 %copy-start = (bf16[512,4096]{1,0:T(8,128)(2,1)S(1)}, bf16[512,4096]{1,0:T(8,128)(2,1)}, u32[]{:S(2)}) copy-start(bf16[512,4096]{1,0:T(8,128)(2,1)} %queries.1) | copy-start | bytes 12582916
  0.0 4.0 %collective-permute-start = (bf16[16,4096]{1,0:T(8,128)(2,1)}, bf16[16,4096]{1,0:T(8,128)(2,1)S(1)}, u32[]{:S(2)}, u32[]{:S(2)}) collective-permute-start(bf16[16,4096]{1,0:T(8,128)(2,1)} %param.5), channel_id=1, source_target_pairs={{0,1},{1,0},{2,3},{3,2},{4,5},{5,4},{6,7},{7,6},{8,9},{9,8},{10,11... | collective-permute-start | bytes 393224 | tf_op jit(solution)/shard_map/ppermute | solution.py:45
  0.1 5.6 %collective-permute-start.3 = (bf16[16,4096]{1,0:T(8,128)(2,1)}, bf16[16,4096]{1,0:T(8,128)(2,1)S(1)}, u32[]{:S(2)}, u32[]{:S(2)}) collective-permute-start(bf16[16,4096]{1,0:T(8,128)(2,1)} %param.5), channel_id=1, source_target_pairs={{0,4},{1,3},{4,8},{5,1},{8,12},{9,5},{12,14},{13,9},{14,10},{15,13... | collective-permute-start | bytes 393224 | tf_op jit(solution)/shard_map/ppermute | solution.py:42
  2.7 4.4 %collective-permute-start.8 = (bf16[16,4096]{1,0:T(8,128)(2,1)}, bf16[16,4096]{1,0:T(8,128)(2,1)S(1)}, u32[]{:S(2)}, u32[]{:S(2)}) collective-permute-start(bf16[16,4096]{1,0:T(8,128)(2,1)} %param.4), channel_id=1, source_target_pairs={{0,1},{1,0},{2,3},{3,2},{4,5},{5,4},{6,7},{7,6},{8,9},{9,8},{10,11... | collective-permute-start | bytes 393224 | tf_op jit(solution)/shard_map/ppermute | solution.py:45
  3.1 5.4 %collective-permute-start.9 = (bf16[16,4096]{1,0:T(8,128)(2,1)}, bf16[16,4096]{1,0:T(8,128)(2,1)S(1)}, u32[]{:S(2)}, u32[]{:S(2)}) collective-permute-start(bf16[16,4096]{1,0:T(8,128)(2,1)} %param.4), channel_id=1, source_target_pairs={{0,4},{1,3},{4,8},{5,1},{8,12},{9,5},{12,14},{13,9},{14,10},{15,13... | collective-permute-start | bytes 393224 | tf_op jit(solution)/shard_map/ppermute | solution.py:42
  4.1 5.8 %collective-permute-start.1 = (bf16[16,4096]{1,0:T(8,128)(2,1)S(1)}, bf16[16,4096]{1,0:T(8,128)(2,1)S(1)}, u32[]{:S(2)}, u32[]{:S(2)}) collective-permute-start(bf16[16,4096]{1,0:T(8,128)(2,1)S(1)} %collective-permute-done.refs_0_.refs_2_), channel_id=1, source_target_pairs={{0,4},{1,3},{4,8},{5,1},{8,12},{9,5},{12,14},{13,9},{14,10},{15,13... | collective-permute-start | bytes 393224 | tf_op jit(solution)/shard_map/ppermute | solution.py:42
  5.7 5.4 %collective-permute-start.4 = (bf16[16,4096]{1,0:T(8,128)(2,1)S(1)}, bf16[16,4096]{1,0:T(8,128)(2,1)S(1)}, u32[]{:S(2)}, u32[]{:S(2)}) collective-permute-start(bf16[16,4096]{1,0:T(8,128)(2,1)S(1)} %collective-permute-done.3.refs_0_.refs_3_), channel_id=1, source_target_pairs={{0,4},{1,3},{4,8},{5,1},{8,12},{9,5},{12,14},{13,9},{14,10},{15,13... | collective-permute-start | bytes 393224 | tf_op jit(solution)/shard_map/ppermute | solution.py:42
  7.2 4.5 %collective-permute-start.10 = (bf16[16,4096]{1,0:T(8,128)(2,1)S(1)}, bf16[16,4096]{1,0:T(8,128)(2,1)S(1)}, u32[]{:S(2)}, u32[]{:S(2)}) collective-permute-start(bf16[16,4096]{1,0:T(8,128)(2,1)S(1)} %collective-permute-done.8.refs_0_), channel_id=1, source_target_pairs={{0,4},{1,3},{4,8},{5,1},{8,12},{9,5},{12,14},{13,9},{14,10},{15,13... | collective-permute-start | bytes 393224 | tf_op jit(solution)/shard_map/ppermute | solution.py:42
  8.5 4.5 %collective-permute-start.11 = (bf16[16,4096]{1,0:T(8,128)(2,1)S(1)}, bf16[16,4096]{1,0:T(8,128)(2,1)S(1)}, u32[]{:S(2)}, u32[]{:S(2)}) collective-permute-start(bf16[16,4096]{1,0:T(8,128)(2,1)S(1)} %collective-permute-done.9.refs_1_), channel_id=1, source_target_pairs={{0,4},{1,3},{4,8},{5,1},{8,12},{9,5},{12,14},{13,9},{14,10},{15,13... | collective-permute-start | bytes 393224 | tf_op jit(solution)/shard_map/ppermute | solution.py:42
  9.8 4.7 %collective-permute-start.2 = (bf16[16,4096]{1,0:T(8,128)(2,1)S(1)}, bf16[16,4096]{1,0:T(8,128)(2,1)S(1)}, u32[]{:S(2)}, u32[]{:S(2)}) collective-permute-start(bf16[16,4096]{1,0:T(8,128)(2,1)S(1)} %collective-permute-done.1.refs_1_.refs_4_), channel_id=1, source_target_pairs={{0,4},{1,3},{4,8},{5,1},{8,12},{9,5},{12,14},{13,9},{14,10},{15,13... | collective-permute-start | bytes 393224 | tf_op jit(solution)/shard_map/ppermute | solution.py:42
  11.1 4.8 %collective-permute-start.5 = (bf16[16,4096]{1,0:T(8,128)(2,1)S(1)}, bf16[16,4096]{1,0:T(8,128)(2,1)S(1)}, u32[]{:S(2)}, u32[]{:S(2)}) collective-permute-start(bf16[16,4096]{1,0:T(8,128)(2,1)S(1)} %collective-permute-done.4.refs_2_.refs_5_), channel_id=1, source_target_pairs={{0,4},{1,3},{4,8},{5,1},{8,12},{9,5},{12,14},{13,9},{14,10},{15,13... | collective-permute-start | bytes 393224 | tf_op jit(solution)/shard_map/ppermute | solution.py:42
  11.7 7.9 %collective-permute-start.14 = (bf16[16,4096]{1,0:T(8,128)(2,1)S(1)}, bf16[16,4096]{1,0:T(8,128)(2,1)S(1)}, u32[]{:S(2)}, u32[]{:S(2)}) collective-permute-start(bf16[16,4096]{1,0:T(8,128)(2,1)S(1)} %collective-permute-done.10.refs_2_), channel_id=1, source_target_pairs={{0,4},{1,3},{4,8},{5,1},{8,12},{9,5},{12,14},{13,9},{14,10},{15,13... | collective-permute-start | bytes 393224 | tf_op jit(solution)/shard_map/ppermute | solution.py:42
  13.0 7.0 %collective-permute-start.15 = (bf16[16,4096]{1,0:T(8,128)(2,1)S(1)}, bf16[16,4096]{1,0:T(8,128)(2,1)S(1)}, u32[]{:S(2)}, u32[]{:S(2)}) collective-permute-start(bf16[16,4096]{1,0:T(8,128)(2,1)S(1)} %collective-permute-done.11.refs_3_), channel_id=1, source_target_pairs={{0,4},{1,3},{4,8},{5,1},{8,12},{9,5},{12,14},{13,9},{14,10},{15,13... | collective-permute-start | bytes 393224 | tf_op jit(solution)/shard_map/ppermute | solution.py:42
  14.5 5.9 %collective-permute-start.6 = (bf16[16,4096]{1,0:T(8,128)(2,1)S(1)}, bf16[16,4096]{1,0:T(8,128)(2,1)S(1)}, u32[]{:S(2)}, u32[]{:S(2)}) collective-permute-start(bf16[16,4096]{1,0:T(8,128)(2,1)S(1)} %collective-permute-done.2.refs_3_.refs_7_), channel_id=1, source_target_pairs={{0,4},{1,3},{4,8},{5,1},{8,12},{9,5},{12,14},{13,9},{14,10},{15,13... | collective-permute-start | bytes 393224 | tf_op jit(solution)/shard_map/ppermute | solution.py:42
  15.9 5.6 %collective-permute-start.7 = (bf16[16,4096]{1,0:T(8,128)(2,1)S(1)}, bf16[16,4096]{1,0:T(8,128)(2,1)S(1)}, u32[]{:S(2)}, u32[]{:S(2)}) collective-permute-start(bf16[16,4096]{1,0:T(8,128)(2,1)S(1)} %collective-permute-done.5.refs_4_.refs_8_), channel_id=1, source_target_pairs={{0,4},{1,3},{4,8},{5,1},{8,12},{9,5},{12,14},{13,9},{14,10},{15,13... | collective-permute-start | bytes 393224 | tf_op jit(solution)/shard_map/ppermute | solution.py:42
  16.9 9.7 %collective-permute-start.12 = (bf16[128,4096]{1,0:T(8,128)(2,1)S(1)}, bf16[128,4096]{1,0:T(8,128)(2,1)S(1)}, u32[]{:S(2)}, u32[]{:S(2)}) collective-permute-start(bf16[128,4096]{1,0:T(8,128)(2,1)S(1)} %constant_dynamic-update-slice_fusion), channel_id=1, source_target_pairs={{0,1},{1,0},{2,3},{3,2},{4,5},{5,4},{6,7},{7,6},{8,9},{9,8},{10,11... | collective-permute-start | bytes 3145736 | tf_op jit(solution)/shard_map/ppermute | solution.py:45
  19.6 4.6 %collective-permute-start.16 = (bf16[16,4096]{1,0:T(8,128)(2,1)S(1)}, bf16[16,4096]{1,0:T(8,128)(2,1)S(1)}, u32[]{:S(2)}, u32[]{:S(2)}) collective-permute-start(bf16[16,4096]{1,0:T(8,128)(2,1)S(1)} %collective-permute-done.14.refs_5_), channel_id=1, source_target_pairs={{0,4},{1,3},{4,8},{5,1},{8,12},{9,5},{12,14},{13,9},{14,10},{15,13... | collective-permute-start | bytes 393224 | tf_op jit(solution)/shard_map/ppermute | solution.py:42
  20.0 5.1 %collective-permute-start.17 = (bf16[16,4096]{1,0:T(8,128)(2,1)S(1)}, bf16[16,4096]{1,0:T(8,128)(2,1)S(1)}, u32[]{:S(2)}, u32[]{:S(2)}) collective-permute-start(bf16[16,4096]{1,0:T(8,128)(2,1)S(1)} %collective-permute-done.15.refs_6_), channel_id=1, source_target_pairs={{0,4},{1,3},{4,8},{5,1},{8,12},{9,5},{12,14},{13,9},{14,10},{15,13... | collective-permute-start | bytes 393224 | tf_op jit(solution)/shard_map/ppermute | solution.py:42
  21.9 4.8 %collective-permute-start.13 = (bf16[64,4096]{1,0:T(8,128)(2,1)S(1)}, bf16[64,4096]{1,0:T(8,128)(2,1)S(1)}, u32[]{:S(2)}, u32[]{:S(2)}) collective-permute-start(bf16[64,4096]{1,0:T(8,128)(2,1)S(1)} %pad_maximum_fusion), channel_id=1, source_target_pairs={{0,1},{1,0},{2,3},{3,2},{4,5},{5,4},{6,7},{7,6},{8,9},{9,8},{10,11... | collective-permute-start | bytes 1572872 | tf_op jit(solution)/shard_map/ppermute | solution.py:45
  25.1 3.4 %collective-permute-start.18 = (bf16[64,4096]{1,0:T(8,128)(2,1)S(1)}, bf16[64,4096]{1,0:T(8,128)(2,1)S(1)}, u32[]{:S(2)}, u32[]{:S(2)}) collective-permute-start(bf16[64,4096]{1,0:T(8,128)(2,1)S(1)} %pad_maximum_fusion.1), channel_id=1, source_target_pairs={{0,1},{1,0},{2,3},{3,2},{4,5},{5,4},{6,7},{7,6},{8,9},{9,8},{10,11... | collective-permute-start | bytes 1572872 | tf_op jit(solution)/shard_map/ppermute | solution.py:45

commit v20 on v19

--- a/solution.py
+++ b/solution.py
@@ -10,7 +10,7 @@
 TEMP = 64
 LANES = 128
 CHUNK = 1024
-GROUP = 32
+GROUP = 64
 BLOCK = 256
 LIMIT = 40 * 2**20
 

time: 30.8 us -> 30.8 us (level)
  no operation moved by 1% of the time
where the time goes in v20:
time: 30.8 us; the launch traced here: 30.7 us
  starting transfers between devices  22.3 us (72%)
  Pallas kernels  4.36 us (14%)
  waiting for transfers between devices  3.74 us (12%)
    ppermute x14, starting transfers between devices, hop(): return lax.ppermute(block, 'samp', ring)  15.4 us
    ppermute x5, starting transfers between devices, hand_over(): return lax.ppermute(block, 'samp', twins)  6.88 us
    pallas_call x2, Pallas kernels, call(): pl.pallas_call(functools.partial(kernel, spans), out_shape=out_shape, in_...  4 us
    ppermute x14, waiting for transfers between devices, hop(): return lax.ppermute(block, 'samp', ring)  3.72 us
  transfers between devices with their start and end apart: 19, of which 7 were waited for; matrix products, arithmetic and copies ran while one was open for 0% of the time, Pallas kernels for 7%

profile of v20, /device:TPU:1, one launch (start us, length us, event | category | flops | bytes accessed | tf_op | source)
XLA Modules:
  0.0 30.7 jit_solution(8999462651488282450)
XLA Ops:
  0.0 0.0 copy-start
  0.0 0.1 collective-permute-start
  0.1 2.7 %collective-permute-start.3 = (bf16[16,4096]{1,0:T(8,128)(2,1)}, bf16[16,4096]{1,0:T(8,128)(2,1)S(1)}, u32[]{:S(2)}, u32[]{:S(2)}) collective-permute-start(bf16[16,4096]{1,0:T(8,128)(2,1)} %param.5), channel_id=1, source_target_pairs={{0,4},{1,3},{4,8},{5,1},{8,12},{9,5},{12,14},{13,9},{14,10},{15,13... | collective-permute-start | bytes 393224 | tf_op jit(solution)/shard_map/ppermute | solution.py:42
  2.7 0.4 %collective-permute-start.8 = (bf16[16,4096]{1,0:T(8,128)(2,1)}, bf16[16,4096]{1,0:T(8,128)(2,1)S(1)}, u32[]{:S(2)}, u32[]{:S(2)}) collective-permute-start(bf16[16,4096]{1,0:T(8,128)(2,1)} %param.4), channel_id=1, source_target_pairs={{0,1},{1,0},{2,3},{3,2},{4,5},{5,4},{6,7},{7,6},{8,9},{9,8},{10,11... | collective-permute-start | bytes 393224 | tf_op jit(solution)/shard_map/ppermute | solution.py:45
  3.1 0.9 %collective-permute-start.9 = (bf16[16,4096]{1,0:T(8,128)(2,1)}, bf16[16,4096]{1,0:T(8,128)(2,1)S(1)}, u32[]{:S(2)}, u32[]{:S(2)}) collective-permute-start(bf16[16,4096]{1,0:T(8,128)(2,1)} %param.4), channel_id=1, source_target_pairs={{0,4},{1,3},{4,8},{5,1},{8,12},{9,5},{12,14},{13,9},{14,10},{15,13... | collective-permute-start | bytes 393224 | tf_op jit(solution)/shard_map/ppermute | solution.py:42
  4.0 0.0 collective-permute-done.refs_0_.refs_2_
  4.1 1.3 %collective-permute-start.1 = (bf16[16,4096]{1,0:T(8,128)(2,1)S(1)}, bf16[16,4096]{1,0:T(8,128)(2,1)S(1)}, u32[]{:S(2)}, u32[]{:S(2)}) collective-permute-start(bf16[16,4096]{1,0:T(8,128)(2,1)S(1)} %collective-permute-done.refs_0_.refs_2_), channel_id=1, source_target_pairs={{0,4},{1,3},{4,8},{5,1},{8,12},{9,5},{12,14},{13,9},{14,10},{15,13... | collective-permute-start | bytes 393224 | tf_op jit(solution)/shard_map/ppermute | solution.py:42
  5.4 0.3 collective-permute-done.3.refs_0_.refs_3_
  5.7 1.4 %collective-permute-start.4 = (bf16[16,4096]{1,0:T(8,128)(2,1)S(1)}, bf16[16,4096]{1,0:T(8,128)(2,1)S(1)}, u32[]{:S(2)}, u32[]{:S(2)}) collective-permute-start(bf16[16,4096]{1,0:T(8,128)(2,1)S(1)} %collective-permute-done.3.refs_0_.refs_3_), channel_id=1, source_target_pairs={{0,4},{1,3},{4,8},{5,1},{8,12},{9,5},{12,14},{13,9},{14,10},{15,13... | collective-permute-start | bytes 393224 | tf_op jit(solution)/shard_map/ppermute | solution.py:42
  7.1 0.1 shard_map.37.refs_0_
  7.1 0.0 collective-permute-done.8.refs_0_
  7.2 1.3 %collective-permute-start.10 = (bf16[16,4096]{1,0:T(8,128)(2,1)S(1)}, bf16[16,4096]{1,0:T(8,128)(2,1)S(1)}, u32[]{:S(2)}, u32[]{:S(2)}) collective-permute-start(bf16[16,4096]{1,0:T(8,128)(2,1)S(1)} %collective-permute-done.8.refs_0_), channel_id=1, source_target_pairs={{0,4},{1,3},{4,8},{5,1},{8,12},{9,5},{12,14},{13,9},{14,10},{15,13... | collective-permute-start | bytes 393224 | tf_op jit(solution)/shard_map/ppermute | solution.py:42
  8.5 0.0 collective-permute-done.9.refs_1_
  8.5 1.3 %collective-permute-start.11 = (bf16[16,4096]{1,0:T(8,128)(2,1)S(1)}, bf16[16,4096]{1,0:T(8,128)(2,1)S(1)}, u32[]{:S(2)}, u32[]{:S(2)}) collective-permute-start(bf16[16,4096]{1,0:T(8,128)(2,1)S(1)} %collective-permute-done.9.refs_1_), channel_id=1, source_target_pairs={{0,4},{1,3},{4,8},{5,1},{8,12},{9,5},{12,14},{13,9},{14,10},{15,13... | collective-permute-start | bytes 393224 | tf_op jit(solution)/shard_map/ppermute | solution.py:42
  9.8 0.0 collective-permute-done.1.refs_1_.refs_4_
  9.8 1.3 %collective-permute-start.2 = (bf16[16,4096]{1,0:T(8,128)(2,1)S(1)}, bf16[16,4096]{1,0:T(8,128)(2,1)S(1)}, u32[]{:S(2)}, u32[]{:S(2)}) collective-permute-start(bf16[16,4096]{1,0:T(8,128)(2,1)S(1)} %collective-permute-done.1.refs_1_.refs_4_), channel_id=1, source_target_pairs={{0,4},{1,3},{4,8},{5,1},{8,12},{9,5},{12,14},{13,9},{14,10},{15,13... | collective-permute-start | bytes 393224 | tf_op jit(solution)/shard_map/ppermute | solution.py:42
  11.1 0.0 collective-permute-done.4.refs_2_.refs_5_
  11.1 0.2 collective-permute-start.5
  11.4 0.3 collective-permute-done.10.refs_2_
  11.7 1.0 %collective-permute-start.14 = (bf16[16,4096]{1,0:T(8,128)(2,1)S(1)}, bf16[16,4096]{1,0:T(8,128)(2,1)S(1)}, u32[]{:S(2)}, u32[]{:S(2)}) collective-permute-start(bf16[16,4096]{1,0:T(8,128)(2,1)S(1)} %collective-permute-done.10.refs_2_), channel_id=1, source_target_pairs={{0,4},{1,3},{4,8},{5,1},{8,12},{9,5},{12,14},{13,9},{14,10},{15,13... | collective-permute-start | bytes 393224 | tf_op jit(solution)/shard_map/ppermute | solution.py:42
  12.7 0.3 collective-permute-done.11.refs_3_
  13.0 1.1 %collective-permute-start.15 = (bf16[16,4096]{1,0:T(8,128)(2,1)S(1)}, bf16[16,4096]{1,0:T(8,128)(2,1)S(1)}, u32[]{:S(2)}, u32[]{:S(2)}) collective-permute-start(bf16[16,4096]{1,0:T(8,128)(2,1)S(1)} %collective-permute-done.11.refs_3_), channel_id=1, source_target_pairs={{0,4},{1,3},{4,8},{5,1},{8,12},{9,5},{12,14},{13,9},{14,10},{15,13... | collective-permute-start | bytes 393224 | tf_op jit(solution)/shard_map/ppermute | solution.py:42
  14.1 0.4 %collective-permute-done.2.refs_3_.refs_7_ = bf16[16,4096]{1,0:T(8,128)(2,1)S(1)} collective-permute-done((bf16[16,4096]{1,0:T(8,128)(2,1)S(1)}, bf16[16,4096]{1,0:T(8,128)(2,1)S(1)}, u32[]{:S(2)}, u32[]{:S(2)}) %collective-permute-start.2) | collective-permute-done | bytes 131104 | tf_op jit(solution)/shard_map/ppermute | solution.py:42
  14.5 1.0 %collective-permute-start.6 = (bf16[16,4096]{1,0:T(8,128)(2,1)S(1)}, bf16[16,4096]{1,0:T(8,128)(2,1)S(1)}, u32[]{:S(2)}, u32[]{:S(2)}) collective-permute-start(bf16[16,4096]{1,0:T(8,128)(2,1)S(1)} %collective-permute-done.2.refs_3_.refs_7_), channel_id=1, source_target_pairs={{0,4},{1,3},{4,8},{5,1},{8,12},{9,5},{12,14},{13,9},{14,10},{15,13... | collective-permute-start | bytes 393224 | tf_op jit(solution)/shard_map/ppermute | solution.py:42
  15.5 0.4 %collective-permute-done.5.refs_4_.refs_8_ = bf16[16,4096]{1,0:T(8,128)(2,1)S(1)} collective-permute-done((bf16[16,4096]{1,0:T(8,128)(2,1)S(1)}, bf16[16,4096]{1,0:T(8,128)(2,1)S(1)}, u32[]{:S(2)}, u32[]{:S(2)}) %collective-permute-start.5) | collective-permute-done | bytes 131104 | tf_op jit(solution)/shard_map/ppermute | solution.py:42
  15.9 1.0 %collective-permute-start.7 = (bf16[16,4096]{1,0:T(8,128)(2,1)S(1)}, bf16[16,4096]{1,0:T(8,128)(2,1)S(1)}, u32[]{:S(2)}, u32[]{:S(2)}) collective-permute-start(bf16[16,4096]{1,0:T(8,128)(2,1)S(1)} %collective-permute-done.5.refs_4_.refs_8_), channel_id=1, source_target_pairs={{0,4},{1,3},{4,8},{5,1},{8,12},{9,5},{12,14},{13,9},{14,10},{15,13... | collective-permute-start | bytes 393224 | tf_op jit(solution)/shard_map/ppermute | solution.py:42
  16.9 2.7 %collective-permute-start.12 = (bf16[128,4096]{1,0:T(8,128)(2,1)S(1)}, bf16[128,4096]{1,0:T(8,128)(2,1)S(1)}, u32[]{:S(2)}, u32[]{:S(2)}) collective-permute-start(bf16[128,4096]{1,0:T(8,128)(2,1)S(1)} %constant_dynamic-update-slice_fusion), channel_id=1, source_target_pairs={{0,1},{1,0},{2,3},{3,2},{4,5},{5,4},{6,7},{7,6},{8,9},{9,8},{10,11... | collective-permute-start | bytes 3145736 | tf_op jit(solution)/shard_map/ppermute | solution.py:45
  19.6 0.0 collective-permute-done.14.refs_5_
  19.6 0.4 %collective-permute-start.16 = (bf16[16,4096]{1,0:T(8,128)(2,1)S(1)}, bf16[16,4096]{1,0:T(8,128)(2,1)S(1)}, u32[]{:S(2)}, u32[]{:S(2)}) collective-permute-start(bf16[16,4096]{1,0:T(8,128)(2,1)S(1)} %collective-permute-done.14.refs_5_), channel_id=1, source_target_pairs={{0,4},{1,3},{4,8},{5,1},{8,12},{9,5},{12,14},{13,9},{14,10},{15,13... | collective-permute-start | bytes 393224 | tf_op jit(solution)/shard_map/ppermute | solution.py:42
  20.0 0.0 collective-permute-done.15.refs_6_
  20.0 0.4 %collective-permute-start.17 = (bf16[16,4096]{1,0:T(8,128)(2,1)S(1)}, bf16[16,4096]{1,0:T(8,128)(2,1)S(1)}, u32[]{:S(2)}, u32[]{:S(2)}) collective-permute-start(bf16[16,4096]{1,0:T(8,128)(2,1)S(1)} %collective-permute-done.15.refs_6_), channel_id=1, source_target_pairs={{0,4},{1,3},{4,8},{5,1},{8,12},{9,5},{12,14},{13,9},{14,10},{15,13... | collective-permute-start | bytes 393224 | tf_op jit(solution)/shard_map/ppermute | solution.py:42
  20.4 0.0 collective-permute-done.6.refs_5_.refs_9_
  20.4 1.1 %collective-permute-done.7.refs_6_.refs_10_ = bf16[16,4096]{1,0:T(8,128)(2,1)S(1)} collective-permute-done((bf16[16,4096]{1,0:T(8,128)(2,1)S(1)}, bf16[16,4096]{1,0:T(8,128)(2,1)S(1)}, u32[]{:S(2)}, u32[]{:S(2)}) %collective-permute-start.7) | collective-permute-done | bytes 131104 | tf_op jit(solution)/shard_map/ppermute | solution.py:42
  21.5 0.3 %shard_map.38.refs_1_ = f32[1,4096]{1,0:T(1,128)S(1)} custom-call(bf16[16,4096]{1,0:T(8,128)(2,1)S(1)} %collective-permute-done.3.refs_0_.refs_3_, bf16[16,4096]{1,0:T(8,128)(2,1)S(1)} %collective-permute-done.1.refs_1_.refs_4_, bf16[16,4096]{1,0:T(8,128)(2,1)S(1)} %collective-permute-done.4.refs_2_.refs_5_, ...), custom_call_target="tpu_custom_call" | custom-call | tf_op jit(solution)/shard_map/pallas_call | solution.py:163
  21.9 2.3 %collective-permute-start.13 = (bf16[64,4096]{1,0:T(8,128)(2,1)S(1)}, bf16[64,4096]{1,0:T(8,128)(2,1)S(1)}, u32[]{:S(2)}, u32[]{:S(2)}) collective-permute-start(bf16[64,4096]{1,0:T(8,128)(2,1)S(1)} %pad_maximum_fusion), channel_id=1, source_target_pairs={{0,1},{1,0},{2,3},{3,2},{4,5},{5,4},{6,7},{7,6},{8,9},{9,8},{10,11... | collective-permute-start | bytes 1572872 | tf_op jit(solution)/shard_map/ppermute | solution.py:45
  24.1 0.0 collective-permute-done.16.refs_7_
  24.1 1.0 %collective-permute-done.17.refs_8_ = bf16[16,4096]{1,0:T(8,128)(2,1)S(1)} collective-permute-done((bf16[16,4096]{1,0:T(8,128)(2,1)S(1)}, bf16[16,4096]{1,0:T(8,128)(2,1)S(1)}, u32[]{:S(2)}, u32[]{:S(2)}) %collective-permute-start.17) | collective-permute-done | bytes 131104 | tf_op jit(solution)/shard_map/ppermute | solution.py:42
  25.1 1.5 %collective-permute-start.18 = (bf16[64,4096]{1,0:T(8,128)(2,1)S(1)}, bf16[64,4096]{1,0:T(8,128)(2,1)S(1)}, u32[]{:S(2)}, u32[]{:S(2)}) collective-permute-start(bf16[64,4096]{1,0:T(8,128)(2,1)S(1)} %pad_maximum_fusion.1), channel_id=1, source_target_pairs={{0,1},{1,0},{2,3},{3,2},{4,5},{5,4},{6,7},{7,6},{8,9},{9,8},{10,11... | collective-permute-start | bytes 1572872 | tf_op jit(solution)/shard_map/ppermute | solution.py:45
  26.6 0.0 collective-permute-done.13.refs_11_
  26.6 0.0 collective-permute-done.12.refs_6_.refs_4_
  26.6 0.0 copy-done
  26.6 1.9 %shard_map.39 = (bf16[512,4096]{1,0:T(8,128)(2,1)S(1)}, f32[1,4096]{1,0:T(1,128)S(1)}, f32[1,512]{1,0:T(1,128)S(1)}) custom-call(bf16[512,4096]{1,0:T(8,128)(2,1)S(1)} %copy-done, f32[1,4096]{1,0:T(1,128)S(1)} %shard_map.37.refs_0_, f32[1,4096]{1,0:T(1,128)S(1)} %shard_map.38.refs_1_, bf16[16,4096]{1,0:T(8,128)(2,1)S(1)} %collective-permute-done.refs_0_.refs_2_, ...), custom_call_target="tpu_custom_call" | custom-call | flops 1073741824 | bytes 6291456 | tf_op jit(solution)/shard_map/pallas_call | solution.py:222
  28.6 0.0 collective-permute-done.18.refs_9_
  28.6 2.1 %shard_map.40 = f32[1,512]{1,0:T(1,128)} custom-call(f32[1,512]{1,0:T(1,128)S(1)} %get-tuple-element.16.ref_log, bf16[512,4096]{1,0:T(8,128)(2,1)S(1)} %get-tuple-element.17.probes, f32[1,4096]{1,0:T(1,128)S(1)} %get-tuple-element.18.mean, bf16[16,4096]{1,0:T(8,128)(2,1)S(1)} %collective-permute-done.8.refs_0_, ...), custom_call_target="tpu_custom_call" | custom-call | flops 1073741824 | bytes 6291456 | tf_op jit(solution)/shard_map/pallas_call | solution.py:222
  (10 shorter events, 0.1 us)
Async XLA Ops:
  0.0 26.6 %copy-start = (bf16[512,4096]{1,0:T(8,128)(2,1)S(1)}, bf16[512,4096]{1,0:T(8,128)(2,1)}, u32[]{:S(2)}) copy-start(bf16[512,4096]{1,0:T(8,128)(2,1)} %queries.1) | copy-start | bytes 12582916
  0.0 4.0 %collective-permute-start = (bf16[16,4096]{1,0:T(8,128)(2,1)}, bf16[16,4096]{1,0:T(8,128)(2,1)S(1)}, u32[]{:S(2)}, u32[]{:S(2)}) collective-permute-start(bf16[16,4096]{1,0:T(8,128)(2,1)} %param.5), channel_id=1, source_target_pairs={{0,1},{1,0},{2,3},{3,2},{4,5},{5,4},{6,7},{7,6},{8,9},{9,8},{10,11... | collective-permute-start | bytes 393224 | tf_op jit(solution)/shard_map/ppermute | solution.py:45
  0.1 5.6 %collective-permute-start.3 = (bf16[16,4096]{1,0:T(8,128)(2,1)}, bf16[16,4096]{1,0:T(8,128)(2,1)S(1)}, u32[]{:S(2)}, u32[]{:S(2)}) collective-permute-start(bf16[16,4096]{1,0:T(8,128)(2,1)} %param.5), channel_id=1, source_target_pairs={{0,4},{1,3},{4,8},{5,1},{8,12},{9,5},{12,14},{13,9},{14,10},{15,13... | collective-permute-start | bytes 393224 | tf_op jit(solution)/shard_map/ppermute | solution.py:42
  2.7 4.4 %collective-permute-start.8 = (bf16[16,4096]{1,0:T(8,128)(2,1)}, bf16[16,4096]{1,0:T(8,128)(2,1)S(1)}, u32[]{:S(2)}, u32[]{:S(2)}) collective-permute-start(bf16[16,4096]{1,0:T(8,128)(2,1)} %param.4), channel_id=1, source_target_pairs={{0,1},{1,0},{2,3},{3,2},{4,5},{5,4},{6,7},{7,6},{8,9},{9,8},{10,11... | collective-permute-start | bytes 393224 | tf_op jit(solution)/shard_map/ppermute | solution.py:45
  3.1 5.4 %collective-permute-start.9 = (bf16[16,4096]{1,0:T(8,128)(2,1)}, bf16[16,4096]{1,0:T(8,128)(2,1)S(1)}, u32[]{:S(2)}, u32[]{:S(2)}) collective-permute-start(bf16[16,4096]{1,0:T(8,128)(2,1)} %param.4), channel_id=1, source_target_pairs={{0,4},{1,3},{4,8},{5,1},{8,12},{9,5},{12,14},{13,9},{14,10},{15,13... | collective-permute-start | bytes 393224 | tf_op jit(solution)/shard_map/ppermute | solution.py:42
  4.1 5.8 %collective-permute-start.1 = (bf16[16,4096]{1,0:T(8,128)(2,1)S(1)}, bf16[16,4096]{1,0:T(8,128)(2,1)S(1)}, u32[]{:S(2)}, u32[]{:S(2)}) collective-permute-start(bf16[16,4096]{1,0:T(8,128)(2,1)S(1)} %collective-permute-done.refs_0_.refs_2_), channel_id=1, source_target_pairs={{0,4},{1,3},{4,8},{5,1},{8,12},{9,5},{12,14},{13,9},{14,10},{15,13... | collective-permute-start | bytes 393224 | tf_op jit(solution)/shard_map/ppermute | solution.py:42
  5.7 5.4 %collective-permute-start.4 = (bf16[16,4096]{1,0:T(8,128)(2,1)S(1)}, bf16[16,4096]{1,0:T(8,128)(2,1)S(1)}, u32[]{:S(2)}, u32[]{:S(2)}) collective-permute-start(bf16[16,4096]{1,0:T(8,128)(2,1)S(1)} %collective-permute-done.3.refs_0_.refs_3_), channel_id=1, source_target_pairs={{0,4},{1,3},{4,8},{5,1},{8,12},{9,5},{12,14},{13,9},{14,10},{15,13... | collective-permute-start | bytes 393224 | tf_op jit(solution)/shard_map/ppermute | solution.py:42
  7.2 4.5 %collective-permute-start.10 = (bf16[16,4096]{1,0:T(8,128)(2,1)S(1)}, bf16[16,4096]{1,0:T(8,128)(2,1)S(1)}, u32[]{:S(2)}, u32[]{:S(2)}) collective-permute-start(bf16[16,4096]{1,0:T(8,128)(2,1)S(1)} %collective-permute-done.8.refs_0_), channel_id=1, source_target_pairs={{0,4},{1,3},{4,8},{5,1},{8,12},{9,5},{12,14},{13,9},{14,10},{15,13... | collective-permute-start | bytes 393224 | tf_op jit(solution)/shard_map/ppermute | solution.py:42
  8.5 4.5 %collective-permute-start.11 = (bf16[16,4096]{1,0:T(8,128)(2,1)S(1)}, bf16[16,4096]{1,0:T(8,128)(2,1)S(1)}, u32[]{:S(2)}, u32[]{:S(2)}) collective-permute-start(bf16[16,4096]{1,0:T(8,128)(2,1)S(1)} %collective-permute-done.9.refs_1_), channel_id=1, source_target_pairs={{0,4},{1,3},{4,8},{5,1},{8,12},{9,5},{12,14},{13,9},{14,10},{15,13... | collective-permute-start | bytes 393224 | tf_op jit(solution)/shard_map/ppermute | solution.py:42
  9.8 4.7 %collective-permute-start.2 = (bf16[16,4096]{1,0:T(8,128)(2,1)S(1)}, bf16[16,4096]{1,0:T(8,128)(2,1)S(1)}, u32[]{:S(2)}, u32[]{:S(2)}) collective-permute-start(bf16[16,4096]{1,0:T(8,128)(2,1)S(1)} %collective-permute-done.1.refs_1_.refs_4_), channel_id=1, source_target_pairs={{0,4},{1,3},{4,8},{5,1},{8,12},{9,5},{12,14},{13,9},{14,10},{15,13... | collective-permute-start | bytes 393224 | tf_op jit(solution)/shard_map/ppermute | solution.py:42
  11.1 4.8 %collective-permute-start.5 = (bf16[16,4096]{1,0:T(8,128)(2,1)S(1)}, bf16[16,4096]{1,0:T(8,128)(2,1)S(1)}, u32[]{:S(2)}, u32[]{:S(2)}) collective-permute-start(bf16[16,4096]{1,0:T(8,128)(2,1)S(1)} %collective-permute-done.4.refs_2_.refs_5_), channel_id=1, source_target_pairs={{0,4},{1,3},{4,8},{5,1},{8,12},{9,5},{12,14},{13,9},{14,10},{15,13... | collective-permute-start | bytes 393224 | tf_op jit(solution)/shard_map/ppermute | solution.py:42
  11.7 7.9 %collective-permute-start.14 = (bf16[16,4096]{1,0:T(8,128)(2,1)S(1)}, bf16[16,4096]{1,0:T(8,128)(2,1)S(1)}, u32[]{:S(2)}, u32[]{:S(2)}) collective-permute-start(bf16[16,4096]{1,0:T(8,128)(2,1)S(1)} %collective-permute-done.10.refs_2_), channel_id=1, source_target_pairs={{0,4},{1,3},{4,8},{5,1},{8,12},{9,5},{12,14},{13,9},{14,10},{15,13... | collective-permute-start | bytes 393224 | tf_op jit(solution)/shard_map/ppermute | solution.py:42
  13.0 7.0 %collective-permute-start.15 = (bf16[16,4096]{1,0:T(8,128)(2,1)S(1)}, bf16[16,4096]{1,0:T(8,128)(2,1)S(1)}, u32[]{:S(2)}, u32[]{:S(2)}) collective-permute-start(bf16[16,4096]{1,0:T(8,128)(2,1)S(1)} %collective-permute-done.11.refs_3_), channel_id=1, source_target_pairs={{0,4},{1,3},{4,8},{5,1},{8,12},{9,5},{12,14},{13,9},{14,10},{15,13... | collective-permute-start | bytes 393224 | tf_op jit(solution)/shard_map/ppermute | solution.py:42
  14.5 5.9 %collective-permute-start.6 = (bf16[16,4096]{1,0:T(8,128)(2,1)S(1)}, bf16[16,4096]{1,0:T(8,128)(2,1)S(1)}, u32[]{:S(2)}, u32[]{:S(2)}) collective-permute-start(bf16[16,4096]{1,0:T(8,128)(2,1)S(1)} %collective-permute-done.2.refs_3_.refs_7_), channel_id=1, source_target_pairs={{0,4},{1,3},{4,8},{5,1},{8,12},{9,5},{12,14},{13,9},{14,10},{15,13... | collective-permute-start | bytes 393224 | tf_op jit(solution)/shard_map/ppermute | solution.py:42
  15.9 5.6 %collective-permute-start.7 = (bf16[16,4096]{1,0:T(8,128)(2,1)S(1)}, bf16[16,4096]{1,0:T(8,128)(2,1)S(1)}, u32[]{:S(2)}, u32[]{:S(2)}) collective-permute-start(bf16[16,4096]{1,0:T(8,128)(2,1)S(1)} %collective-permute-done.5.refs_4_.refs_8_), channel_id=1, source_target_pairs={{0,4},{1,3},{4,8},{5,1},{8,12},{9,5},{12,14},{13,9},{14,10},{15,13... | collective-permute-start | bytes 393224 | tf_op jit(solution)/shard_map/ppermute | solution.py:42
  16.9 9.7 %collective-permute-start.12 = (bf16[128,4096]{1,0:T(8,128)(2,1)S(1)}, bf16[128,4096]{1,0:T(8,128)(2,1)S(1)}, u32[]{:S(2)}, u32[]{:S(2)}) collective-permute-start(bf16[128,4096]{1,0:T(8,128)(2,1)S(1)} %constant_dynamic-update-slice_fusion), channel_id=1, source_target_pairs={{0,1},{1,0},{2,3},{3,2},{4,5},{5,4},{6,7},{7,6},{8,9},{9,8},{10,11... | collective-permute-start | bytes 3145736 | tf_op jit(solution)/shard_map/ppermute | solution.py:45
  19.6 4.6 %collective-permute-start.16 = (bf16[16,4096]{1,0:T(8,128)(2,1)S(1)}, bf16[16,4096]{1,0:T(8,128)(2,1)S(1)}, u32[]{:S(2)}, u32[]{:S(2)}) collective-permute-start(bf16[16,4096]{1,0:T(8,128)(2,1)S(1)} %collective-permute-done.14.refs_5_), channel_id=1, source_target_pairs={{0,4},{1,3},{4,8},{5,1},{8,12},{9,5},{12,14},{13,9},{14,10},{15,13... | collective-permute-start | bytes 393224 | tf_op jit(solution)/shard_map/ppermute | solution.py:42
  20.0 5.1 %collective-permute-start.17 = (bf16[16,4096]{1,0:T(8,128)(2,1)S(1)}, bf16[16,4096]{1,0:T(8,128)(2,1)S(1)}, u32[]{:S(2)}, u32[]{:S(2)}) collective-permute-start(bf16[16,4096]{1,0:T(8,128)(2,1)S(1)} %collective-permute-done.15.refs_6_), channel_id=1, source_target_pairs={{0,4},{1,3},{4,8},{5,1},{8,12},{9,5},{12,14},{13,9},{14,10},{15,13... | collective-permute-start | bytes 393224 | tf_op jit(solution)/shard_map/ppermute | solution.py:42
  21.9 4.8 %collective-permute-start.13 = (bf16[64,4096]{1,0:T(8,128)(2,1)S(1)}, bf16[64,4096]{1,0:T(8,128)(2,1)S(1)}, u32[]{:S(2)}, u32[]{:S(2)}) collective-permute-start(bf16[64,4096]{1,0:T(8,128)(2,1)S(1)} %pad_maximum_fusion), channel_id=1, source_target_pairs={{0,1},{1,0},{2,3},{3,2},{4,5},{5,4},{6,7},{7,6},{8,9},{9,8},{10,11... | collective-permute-start | bytes 1572872 | tf_op jit(solution)/shard_map/ppermute | solution.py:45
  25.1 3.4 %collective-permute-start.18 = (bf16[64,4096]{1,0:T(8,128)(2,1)S(1)}, bf16[64,4096]{1,0:T(8,128)(2,1)S(1)}, u32[]{:S(2)}, u32[]{:S(2)}) collective-permute-start(bf16[64,4096]{1,0:T(8,128)(2,1)S(1)} %pad_maximum_fusion.1), channel_id=1, source_target_pairs={{0,1},{1,0},{2,3},{3,2},{4,5},{5,4},{6,7},{7,6},{8,9},{9,8},{10,11... | collective-permute-start | bytes 1572872 | tf_op jit(solution)/shard_map/ppermute | solution.py:45

commit v21 on v19

--- a/solution.py
+++ b/solution.py
@@ -12,6 +12,7 @@
 CHUNK = 1024
 GROUP = 32
 BLOCK = 256
+TURN = 256
 LIMIT = 40 * 2**20
 
 
@@ -113,7 +114,7 @@
 
 def add_products(cols, queries, probes, centered, scores, first):
     products = lax.dot_general(
-        centered[:, cols], probes[queries, cols], (((1,), (1,)), ((), ())),
+        centered[:, cols], probes[cols, queries], (((1,), (0,)), ((), ())),
         preferred_element_type=jnp.float32,
     )
     scores[:, queries] = products if first else scores[:, queries] + products
@@ -132,7 +133,7 @@
                 step()
         waiting += [
             functools.partial(add_products, cols, queries, probes, centered, scores, first)
-            for queries in row_groups(probes.shape[0], BLOCK)
+            for queries in row_groups(probes.shape[1], BLOCK)
         ]
     for step in waiting:
         step()
@@ -184,18 +185,20 @@
         mean[:, cols] = total / count
 
     def center_queries(rows, cols):
-        probes[rows, cols] = center(queries[rows, cols], mean[:, cols])
+        probes[cols, rows] = center(queries[rows, cols], mean[:, cols]).T
 
     def prepare(cols, first):
         work = []
         for group in groups:
             work.append(functools.partial(center_group, group, cols, mean, centered, squares, first))
-        for rows in row_groups(probes.shape[0], GROUP):
-            work.append(functools.partial(center_queries, rows, cols))
+        for rows in row_groups(probes.shape[1], LANES):
+            for part in row_groups(CHUNK, TURN):
+                part = slice(cols.start + part.start, cols.start + part.stop)
+                work.append(functools.partial(center_queries, rows, part))
         return work
 
     interleave(features, prepare, probes, centered, scores)
-    for block in row_groups(probes.shape[0], BLOCK):
+    for block in row_groups(probes.shape[1], BLOCK):
         ref_log[:, block] = log_sum(squares, scores, block)
 
 
@@ -210,7 +213,7 @@
         ]
 
     interleave(centered.shape[1], prepare, probes, centered, scores)
-    for block in row_groups(probes.shape[0], BLOCK):
+    for block in row_groups(probes.shape[1], BLOCK):
         proof[:, block] = log_sum(squares, scores, block) - ref_log[:, block]
 
 
@@ -254,7 +257,7 @@
         ref_pieces,
         count,
         (
-            jax.ShapeDtypeStruct((count, features), jnp.bfloat16),
+            jax.ShapeDtypeStruct((features, count), jnp.bfloat16),
             jax.ShapeDtypeStruct((1, features), jnp.float32),
             logs,
         ),

time: 30.8 us -> 31.3 us (1.016)
  Pallas kernels: 4.35 us -> 4.83 us
    pallas_call x2, Pallas kernels: 3.99 us -> 4.47 us  [call(): pl.pallas_call(functools.partial(kernel, spans), out_shape=out_shape, in_...]
  transfers between devices with their start and end apart: 19 -> 19, of which waited for: 7 -> 7; matrix products, arithmetic and copies ran while one was open for 0% -> 0% of each run, Pallas kernels for 7% -> 9%
where the time goes in v21:
time: 31.3 us; the launch traced here: 31.1 us
  starting transfers between devices  22.3 us (71%)
  Pallas kernels  4.83 us (15%)
  waiting for transfers between devices  3.74 us (12%)
    ppermute x14, starting transfers between devices, hop(): return lax.ppermute(block, 'samp', ring)  15.4 us
    ppermute x5, starting transfers between devices, hand_over(): return lax.ppermute(block, 'samp', twins)  6.88 us
    pallas_call x2, Pallas kernels, call(): pl.pallas_call(functools.partial(kernel, spans), out_shape=out_shape, in_...  4.47 us
    ppermute x14, waiting for transfers between devices, hop(): return lax.ppermute(block, 'samp', ring)  3.72 us
  transfers between devices with their start and end apart: 19, of which 7 were waited for; matrix products, arithmetic and copies ran while one was open for 0% of the time, Pallas kernels for 9%

profile of v21, /device:TPU:1, one launch (start us, length us, event | category | flops | bytes accessed | tf_op | source)
XLA Modules:
  0.0 31.1 jit_solution(7608653676993442124)
XLA Ops:
  0.0 0.0 copy-start
  0.0 0.1 collective-permute-start
  0.1 2.7 %collective-permute-start.3 = (bf16[16,4096]{1,0:T(8,128)(2,1)}, bf16[16,4096]{1,0:T(8,128)(2,1)S(1)}, u32[]{:S(2)}, u32[]{:S(2)}) collective-permute-start(bf16[16,4096]{1,0:T(8,128)(2,1)} %param.5), channel_id=1, source_target_pairs={{0,4},{1,3},{4,8},{5,1},{8,12},{9,5},{12,14},{13,9},{14,10},{15,13... | collective-permute-start | bytes 393224 | tf_op jit(solution)/shard_map/ppermute | solution.py:43
  2.7 0.4 %collective-permute-start.8 = (bf16[16,4096]{1,0:T(8,128)(2,1)}, bf16[16,4096]{1,0:T(8,128)(2,1)S(1)}, u32[]{:S(2)}, u32[]{:S(2)}) collective-permute-start(bf16[16,4096]{1,0:T(8,128)(2,1)} %param.4), channel_id=1, source_target_pairs={{0,1},{1,0},{2,3},{3,2},{4,5},{5,4},{6,7},{7,6},{8,9},{9,8},{10,11... | collective-permute-start | bytes 393224 | tf_op jit(solution)/shard_map/ppermute | solution.py:46
  3.1 0.9 %collective-permute-start.9 = (bf16[16,4096]{1,0:T(8,128)(2,1)}, bf16[16,4096]{1,0:T(8,128)(2,1)S(1)}, u32[]{:S(2)}, u32[]{:S(2)}) collective-permute-start(bf16[16,4096]{1,0:T(8,128)(2,1)} %param.4), channel_id=1, source_target_pairs={{0,4},{1,3},{4,8},{5,1},{8,12},{9,5},{12,14},{13,9},{14,10},{15,13... | collective-permute-start | bytes 393224 | tf_op jit(solution)/shard_map/ppermute | solution.py:43
  4.0 0.0 collective-permute-done.refs_0_.refs_2_
  4.1 1.3 %collective-permute-start.1 = (bf16[16,4096]{1,0:T(8,128)(2,1)S(1)}, bf16[16,4096]{1,0:T(8,128)(2,1)S(1)}, u32[]{:S(2)}, u32[]{:S(2)}) collective-permute-start(bf16[16,4096]{1,0:T(8,128)(2,1)S(1)} %collective-permute-done.refs_0_.refs_2_), channel_id=1, source_target_pairs={{0,4},{1,3},{4,8},{5,1},{8,12},{9,5},{12,14},{13,9},{14,10},{15,13... | collective-permute-start | bytes 393224 | tf_op jit(solution)/shard_map/ppermute | solution.py:43
  5.4 0.3 collective-permute-done.3.refs_0_.refs_3_
  5.7 1.4 %collective-permute-start.4 = (bf16[16,4096]{1,0:T(8,128)(2,1)S(1)}, bf16[16,4096]{1,0:T(8,128)(2,1)S(1)}, u32[]{:S(2)}, u32[]{:S(2)}) collective-permute-start(bf16[16,4096]{1,0:T(8,128)(2,1)S(1)} %collective-permute-done.3.refs_0_.refs_3_), channel_id=1, source_target_pairs={{0,4},{1,3},{4,8},{5,1},{8,12},{9,5},{12,14},{13,9},{14,10},{15,13... | collective-permute-start | bytes 393224 | tf_op jit(solution)/shard_map/ppermute | solution.py:43
  7.1 0.1 shard_map.37.refs_0_
  7.1 0.0 collective-permute-done.8.refs_0_
  7.2 1.3 %collective-permute-start.10 = (bf16[16,4096]{1,0:T(8,128)(2,1)S(1)}, bf16[16,4096]{1,0:T(8,128)(2,1)S(1)}, u32[]{:S(2)}, u32[]{:S(2)}) collective-permute-start(bf16[16,4096]{1,0:T(8,128)(2,1)S(1)} %collective-permute-done.8.refs_0_), channel_id=1, source_target_pairs={{0,4},{1,3},{4,8},{5,1},{8,12},{9,5},{12,14},{13,9},{14,10},{15,13... | collective-permute-start | bytes 393224 | tf_op jit(solution)/shard_map/ppermute | solution.py:43
  8.5 0.0 collective-permute-done.9.refs_1_
  8.5 1.3 %collective-permute-start.11 = (bf16[16,4096]{1,0:T(8,128)(2,1)S(1)}, bf16[16,4096]{1,0:T(8,128)(2,1)S(1)}, u32[]{:S(2)}, u32[]{:S(2)}) collective-permute-start(bf16[16,4096]{1,0:T(8,128)(2,1)S(1)} %collective-permute-done.9.refs_1_), channel_id=1, source_target_pairs={{0,4},{1,3},{4,8},{5,1},{8,12},{9,5},{12,14},{13,9},{14,10},{15,13... | collective-permute-start | bytes 393224 | tf_op jit(solution)/shard_map/ppermute | solution.py:43
  9.8 0.0 collective-permute-done.1.refs_1_.refs_4_
  9.8 1.3 %collective-permute-start.2 = (bf16[16,4096]{1,0:T(8,128)(2,1)S(1)}, bf16[16,4096]{1,0:T(8,128)(2,1)S(1)}, u32[]{:S(2)}, u32[]{:S(2)}) collective-permute-start(bf16[16,4096]{1,0:T(8,128)(2,1)S(1)} %collective-permute-done.1.refs_1_.refs_4_), channel_id=1, source_target_pairs={{0,4},{1,3},{4,8},{5,1},{8,12},{9,5},{12,14},{13,9},{14,10},{15,13... | collective-permute-start | bytes 393224 | tf_op jit(solution)/shard_map/ppermute | solution.py:43
  11.1 0.0 collective-permute-done.4.refs_2_.refs_5_
  11.1 0.2 collective-permute-start.5
  11.4 0.3 collective-permute-done.10.refs_2_
  11.7 1.0 %collective-permute-start.14 = (bf16[16,4096]{1,0:T(8,128)(2,1)S(1)}, bf16[16,4096]{1,0:T(8,128)(2,1)S(1)}, u32[]{:S(2)}, u32[]{:S(2)}) collective-permute-start(bf16[16,4096]{1,0:T(8,128)(2,1)S(1)} %collective-permute-done.10.refs_2_), channel_id=1, source_target_pairs={{0,4},{1,3},{4,8},{5,1},{8,12},{9,5},{12,14},{13,9},{14,10},{15,13... | collective-permute-start | bytes 393224 | tf_op jit(solution)/shard_map/ppermute | solution.py:43
  12.7 0.3 collective-permute-done.11.refs_3_
  13.0 1.1 %collective-permute-start.15 = (bf16[16,4096]{1,0:T(8,128)(2,1)S(1)}, bf16[16,4096]{1,0:T(8,128)(2,1)S(1)}, u32[]{:S(2)}, u32[]{:S(2)}) collective-permute-start(bf16[16,4096]{1,0:T(8,128)(2,1)S(1)} %collective-permute-done.11.refs_3_), channel_id=1, source_target_pairs={{0,4},{1,3},{4,8},{5,1},{8,12},{9,5},{12,14},{13,9},{14,10},{15,13... | collective-permute-start | bytes 393224 | tf_op jit(solution)/shard_map/ppermute | solution.py:43
  14.1 0.4 %collective-permute-done.2.refs_3_.refs_7_ = bf16[16,4096]{1,0:T(8,128)(2,1)S(1)} collective-permute-done((bf16[16,4096]{1,0:T(8,128)(2,1)S(1)}, bf16[16,4096]{1,0:T(8,128)(2,1)S(1)}, u32[]{:S(2)}, u32[]{:S(2)}) %collective-permute-start.2) | collective-permute-done | bytes 131104 | tf_op jit(solution)/shard_map/ppermute | solution.py:43
  14.5 1.0 %collective-permute-start.6 = (bf16[16,4096]{1,0:T(8,128)(2,1)S(1)}, bf16[16,4096]{1,0:T(8,128)(2,1)S(1)}, u32[]{:S(2)}, u32[]{:S(2)}) collective-permute-start(bf16[16,4096]{1,0:T(8,128)(2,1)S(1)} %collective-permute-done.2.refs_3_.refs_7_), channel_id=1, source_target_pairs={{0,4},{1,3},{4,8},{5,1},{8,12},{9,5},{12,14},{13,9},{14,10},{15,13... | collective-permute-start | bytes 393224 | tf_op jit(solution)/shard_map/ppermute | solution.py:43
  15.5 0.4 %collective-permute-done.5.refs_4_.refs_8_ = bf16[16,4096]{1,0:T(8,128)(2,1)S(1)} collective-permute-done((bf16[16,4096]{1,0:T(8,128)(2,1)S(1)}, bf16[16,4096]{1,0:T(8,128)(2,1)S(1)}, u32[]{:S(2)}, u32[]{:S(2)}) %collective-permute-start.5) | collective-permute-done | bytes 131104 | tf_op jit(solution)/shard_map/ppermute | solution.py:43
  15.9 1.0 %collective-permute-start.7 = (bf16[16,4096]{1,0:T(8,128)(2,1)S(1)}, bf16[16,4096]{1,0:T(8,128)(2,1)S(1)}, u32[]{:S(2)}, u32[]{:S(2)}) collective-permute-start(bf16[16,4096]{1,0:T(8,128)(2,1)S(1)} %collective-permute-done.5.refs_4_.refs_8_), channel_id=1, source_target_pairs={{0,4},{1,3},{4,8},{5,1},{8,12},{9,5},{12,14},{13,9},{14,10},{15,13... | collective-permute-start | bytes 393224 | tf_op jit(solution)/shard_map/ppermute | solution.py:43
  16.9 2.7 %collective-permute-start.12 = (bf16[128,4096]{1,0:T(8,128)(2,1)S(1)}, bf16[128,4096]{1,0:T(8,128)(2,1)S(1)}, u32[]{:S(2)}, u32[]{:S(2)}) collective-permute-start(bf16[128,4096]{1,0:T(8,128)(2,1)S(1)} %constant_dynamic-update-slice_fusion), channel_id=1, source_target_pairs={{0,1},{1,0},{2,3},{3,2},{4,5},{5,4},{6,7},{7,6},{8,9},{9,8},{10,11... | collective-permute-start | bytes 3145736 | tf_op jit(solution)/shard_map/ppermute | solution.py:46
  19.6 0.0 collective-permute-done.14.refs_5_
  19.6 0.4 %collective-permute-start.16 = (bf16[16,4096]{1,0:T(8,128)(2,1)S(1)}, bf16[16,4096]{1,0:T(8,128)(2,1)S(1)}, u32[]{:S(2)}, u32[]{:S(2)}) collective-permute-start(bf16[16,4096]{1,0:T(8,128)(2,1)S(1)} %collective-permute-done.14.refs_5_), channel_id=1, source_target_pairs={{0,4},{1,3},{4,8},{5,1},{8,12},{9,5},{12,14},{13,9},{14,10},{15,13... | collective-permute-start | bytes 393224 | tf_op jit(solution)/shard_map/ppermute | solution.py:43
  20.0 0.0 collective-permute-done.15.refs_6_
  20.0 0.4 %collective-permute-start.17 = (bf16[16,4096]{1,0:T(8,128)(2,1)S(1)}, bf16[16,4096]{1,0:T(8,128)(2,1)S(1)}, u32[]{:S(2)}, u32[]{:S(2)}) collective-permute-start(bf16[16,4096]{1,0:T(8,128)(2,1)S(1)} %collective-permute-done.15.refs_6_), channel_id=1, source_target_pairs={{0,4},{1,3},{4,8},{5,1},{8,12},{9,5},{12,14},{13,9},{14,10},{15,13... | collective-permute-start | bytes 393224 | tf_op jit(solution)/shard_map/ppermute | solution.py:43
  20.4 0.0 collective-permute-done.6.refs_5_.refs_9_
  20.4 1.1 %collective-permute-done.7.refs_6_.refs_10_ = bf16[16,4096]{1,0:T(8,128)(2,1)S(1)} collective-permute-done((bf16[16,4096]{1,0:T(8,128)(2,1)S(1)}, bf16[16,4096]{1,0:T(8,128)(2,1)S(1)}, u32[]{:S(2)}, u32[]{:S(2)}) %collective-permute-start.7) | collective-permute-done | bytes 131104 | tf_op jit(solution)/shard_map/ppermute | solution.py:43
  21.5 0.3 shard_map.38.refs_1_
  21.9 2.3 %collective-permute-start.13 = (bf16[64,4096]{1,0:T(8,128)(2,1)S(1)}, bf16[64,4096]{1,0:T(8,128)(2,1)S(1)}, u32[]{:S(2)}, u32[]{:S(2)}) collective-permute-start(bf16[64,4096]{1,0:T(8,128)(2,1)S(1)} %pad_maximum_fusion), channel_id=1, source_target_pairs={{0,1},{1,0},{2,3},{3,2},{4,5},{5,4},{6,7},{7,6},{8,9},{9,8},{10,11... | collective-permute-start | bytes 1572872 | tf_op jit(solution)/shard_map/ppermute | solution.py:46
  24.1 0.0 collective-permute-done.16.refs_7_
  24.1 1.0 %collective-permute-done.17.refs_8_ = bf16[16,4096]{1,0:T(8,128)(2,1)S(1)} collective-permute-done((bf16[16,4096]{1,0:T(8,128)(2,1)S(1)}, bf16[16,4096]{1,0:T(8,128)(2,1)S(1)}, u32[]{:S(2)}, u32[]{:S(2)}) %collective-permute-start.17) | collective-permute-done | bytes 131104 | tf_op jit(solution)/shard_map/ppermute | solution.py:43
  25.1 1.5 %collective-permute-start.18 = (bf16[64,4096]{1,0:T(8,128)(2,1)S(1)}, bf16[64,4096]{1,0:T(8,128)(2,1)S(1)}, u32[]{:S(2)}, u32[]{:S(2)}) collective-permute-start(bf16[64,4096]{1,0:T(8,128)(2,1)S(1)} %pad_maximum_fusion.1), channel_id=1, source_target_pairs={{0,1},{1,0},{2,3},{3,2},{4,5},{5,4},{6,7},{7,6},{8,9},{9,8},{10,11... | collective-permute-start | bytes 1572872 | tf_op jit(solution)/shard_map/ppermute | solution.py:46
  26.6 0.0 collective-permute-done.13.refs_11_
  26.6 0.0 collective-permute-done.12.refs_6_.refs_4_
  26.6 0.0 copy-done
  26.6 2.5 %shard_map.39 = (bf16[4096,512]{1,0:T(8,128)(2,1)S(1)}, f32[1,4096]{1,0:T(1,128)S(1)}, f32[1,512]{1,0:T(1,128)S(1)}) custom-call(bf16[512,4096]{1,0:T(8,128)(2,1)S(1)} %copy-done, f32[1,4096]{1,0:T(1,128)S(1)} %shard_map.37.refs_0_, f32[1,4096]{1,0:T(1,128)S(1)} %shard_map.38.refs_1_, bf16[16,4096]{1,0:T(8,128)(2,1)S(1)} %collective-permute-done.refs_0_.refs_2_, ...), custom_call_target="tpu_custom_call" | custom-call | flops 1073741824 | bytes 6291456 | tf_op jit(solution)/shard_map/pallas_call | solution.py:225
  29.1 0.0 collective-permute-done.18.refs_9_
  29.1 2.0 %shard_map.40 = f32[1,512]{1,0:T(1,128)} custom-call(f32[1,512]{1,0:T(1,128)S(1)} %get-tuple-element.16.ref_log, bf16[4096,512]{1,0:T(8,128)(2,1)S(1)} %get-tuple-element.17.probes, f32[1,4096]{1,0:T(1,128)S(1)} %get-tuple-element.18.mean, bf16[16,4096]{1,0:T(8,128)(2,1)S(1)} %collective-permute-done.8.refs_0_, ...), custom_call_target="tpu_custom_call" | custom-call | flops 1073741824 | bytes 6291456 | tf_op jit(solution)/shard_map/pallas_call | solution.py:225
  (10 shorter events, 0.2 us)
Async XLA Ops:
  0.0 26.6 %copy-start = (bf16[512,4096]{1,0:T(8,128)(2,1)S(1)}, bf16[512,4096]{1,0:T(8,128)(2,1)}, u32[]{:S(2)}) copy-start(bf16[512,4096]{1,0:T(8,128)(2,1)} %queries.1) | copy-start | bytes 12582916
  0.0 4.0 %collective-permute-start = (bf16[16,4096]{1,0:T(8,128)(2,1)}, bf16[16,4096]{1,0:T(8,128)(2,1)S(1)}, u32[]{:S(2)}, u32[]{:S(2)}) collective-permute-start(bf16[16,4096]{1,0:T(8,128)(2,1)} %param.5), channel_id=1, source_target_pairs={{0,1},{1,0},{2,3},{3,2},{4,5},{5,4},{6,7},{7,6},{8,9},{9,8},{10,11... | collective-permute-start | bytes 393224 | tf_op jit(solution)/shard_map/ppermute | solution.py:46
  0.1 5.6 %collective-permute-start.3 = (bf16[16,4096]{1,0:T(8,128)(2,1)}, bf16[16,4096]{1,0:T(8,128)(2,1)S(1)}, u32[]{:S(2)}, u32[]{:S(2)}) collective-permute-start(bf16[16,4096]{1,0:T(8,128)(2,1)} %param.5), channel_id=1, source_target_pairs={{0,4},{1,3},{4,8},{5,1},{8,12},{9,5},{12,14},{13,9},{14,10},{15,13... | collective-permute-start | bytes 393224 | tf_op jit(solution)/shard_map/ppermute | solution.py:43
  2.7 4.4 %collective-permute-start.8 = (bf16[16,4096]{1,0:T(8,128)(2,1)}, bf16[16,4096]{1,0:T(8,128)(2,1)S(1)}, u32[]{:S(2)}, u32[]{:S(2)}) collective-permute-start(bf16[16,4096]{1,0:T(8,128)(2,1)} %param.4), channel_id=1, source_target_pairs={{0,1},{1,0},{2,3},{3,2},{4,5},{5,4},{6,7},{7,6},{8,9},{9,8},{10,11... | collective-permute-start | bytes 393224 | tf_op jit(solution)/shard_map/ppermute | solution.py:46
  3.1 5.4 %collective-permute-start.9 = (bf16[16,4096]{1,0:T(8,128)(2,1)}, bf16[16,4096]{1,0:T(8,128)(2,1)S(1)}, u32[]{:S(2)}, u32[]{:S(2)}) collective-permute-start(bf16[16,4096]{1,0:T(8,128)(2,1)} %param.4), channel_id=1, source_target_pairs={{0,4},{1,3},{4,8},{5,1},{8,12},{9,5},{12,14},{13,9},{14,10},{15,13... | collective-permute-start | bytes 393224 | tf_op jit(solution)/shard_map/ppermute | solution.py:43
  4.1 5.8 %collective-permute-start.1 = (bf16[16,4096]{1,0:T(8,128)(2,1)S(1)}, bf16[16,4096]{1,0:T(8,128)(2,1)S(1)}, u32[]{:S(2)}, u32[]{:S(2)}) collective-permute-start(bf16[16,4096]{1,0:T(8,128)(2,1)S(1)} %collective-permute-done.refs_0_.refs_2_), channel_id=1, source_target_pairs={{0,4},{1,3},{4,8},{5,1},{8,12},{9,5},{12,14},{13,9},{14,10},{15,13... | collective-permute-start | bytes 393224 | tf_op jit(solution)/shard_map/ppermute | solution.py:43
  5.7 5.4 %collective-permute-start.4 = (bf16[16,4096]{1,0:T(8,128)(2,1)S(1)}, bf16[16,4096]{1,0:T(8,128)(2,1)S(1)}, u32[]{:S(2)}, u32[]{:S(2)}) collective-permute-start(bf16[16,4096]{1,0:T(8,128)(2,1)S(1)} %collective-permute-done.3.refs_0_.refs_3_), channel_id=1, source_target_pairs={{0,4},{1,3},{4,8},{5,1},{8,12},{9,5},{12,14},{13,9},{14,10},{15,13... | collective-permute-start | bytes 393224 | tf_op jit(solution)/shard_map/ppermute | solution.py:43
  7.2 4.5 %collective-permute-start.10 = (bf16[16,4096]{1,0:T(8,128)(2,1)S(1)}, bf16[16,4096]{1,0:T(8,128)(2,1)S(1)}, u32[]{:S(2)}, u32[]{:S(2)}) collective-permute-start(bf16[16,4096]{1,0:T(8,128)(2,1)S(1)} %collective-permute-done.8.refs_0_), channel_id=1, source_target_pairs={{0,4},{1,3},{4,8},{5,1},{8,12},{9,5},{12,14},{13,9},{14,10},{15,13... | collective-permute-start | bytes 393224 | tf_op jit(solution)/shard_map/ppermute | solution.py:43
  8.5 4.5 %collective-permute-start.11 = (bf16[16,4096]{1,0:T(8,128)(2,1)S(1)}, bf16[16,4096]{1,0:T(8,128)(2,1)S(1)}, u32[]{:S(2)}, u32[]{:S(2)}) collective-permute-start(bf16[16,4096]{1,0:T(8,128)(2,1)S(1)} %collective-permute-done.9.refs_1_), channel_id=1, source_target_pairs={{0,4},{1,3},{4,8},{5,1},{8,12},{9,5},{12,14},{13,9},{14,10},{15,13... | collective-permute-start | bytes 393224 | tf_op jit(solution)/shard_map/ppermute | solution.py:43
  9.8 4.7 %collective-permute-start.2 = (bf16[16,4096]{1,0:T(8,128)(2,1)S(1)}, bf16[16,4096]{1,0:T(8,128)(2,1)S(1)}, u32[]{:S(2)}, u32[]{:S(2)}) collective-permute-start(bf16[16,4096]{1,0:T(8,128)(2,1)S(1)} %collective-permute-done.1.refs_1_.refs_4_), channel_id=1, source_target_pairs={{0,4},{1,3},{4,8},{5,1},{8,12},{9,5},{12,14},{13,9},{14,10},{15,13... | collective-permute-start | bytes 393224 | tf_op jit(solution)/shard_map/ppermute | solution.py:43
  11.1 4.8 %collective-permute-start.5 = (bf16[16,4096]{1,0:T(8,128)(2,1)S(1)}, bf16[16,4096]{1,0:T(8,128)(2,1)S(1)}, u32[]{:S(2)}, u32[]{:S(2)}) collective-permute-start(bf16[16,4096]{1,0:T(8,128)(2,1)S(1)} %collective-permute-done.4.refs_2_.refs_5_), channel_id=1, source_target_pairs={{0,4},{1,3},{4,8},{5,1},{8,12},{9,5},{12,14},{13,9},{14,10},{15,13... | collective-permute-start | bytes 393224 | tf_op jit(solution)/shard_map/ppermute | solution.py:43
  11.7 7.9 %collective-permute-start.14 = (bf16[16,4096]{1,0:T(8,128)(2,1)S(1)}, bf16[16,4096]{1,0:T(8,128)(2,1)S(1)}, u32[]{:S(2)}, u32[]{:S(2)}) collective-permute-start(bf16[16,4096]{1,0:T(8,128)(2,1)S(1)} %collective-permute-done.10.refs_2_), channel_id=1, source_target_pairs={{0,4},{1,3},{4,8},{5,1},{8,12},{9,5},{12,14},{13,9},{14,10},{15,13... | collective-permute-start | bytes 393224 | tf_op jit(solution)/shard_map/ppermute | solution.py:43
  13.0 7.0 %collective-permute-start.15 = (bf16[16,4096]{1,0:T(8,128)(2,1)S(1)}, bf16[16,4096]{1,0:T(8,128)(2,1)S(1)}, u32[]{:S(2)}, u32[]{:S(2)}) collective-permute-start(bf16[16,4096]{1,0:T(8,128)(2,1)S(1)} %collective-permute-done.11.refs_3_), channel_id=1, source_target_pairs={{0,4},{1,3},{4,8},{5,1},{8,12},{9,5},{12,14},{13,9},{14,10},{15,13... | collective-permute-start | bytes 393224 | tf_op jit(solution)/shard_map/ppermute | solution.py:43
  14.5 5.9 %collective-permute-start.6 = (bf16[16,4096]{1,0:T(8,128)(2,1)S(1)}, bf16[16,4096]{1,0:T(8,128)(2,1)S(1)}, u32[]{:S(2)}, u32[]{:S(2)}) collective-permute-start(bf16[16,4096]{1,0:T(8,128)(2,1)S(1)} %collective-permute-done.2.refs_3_.refs_7_), channel_id=1, source_target_pairs={{0,4},{1,3},{4,8},{5,1},{8,12},{9,5},{12,14},{13,9},{14,10},{15,13... | collective-permute-start | bytes 393224 | tf_op jit(solution)/shard_map/ppermute | solution.py:43
  15.9 5.6 %collective-permute-start.7 = (bf16[16,4096]{1,0:T(8,128)(2,1)S(1)}, bf16[16,4096]{1,0:T(8,128)(2,1)S(1)}, u32[]{:S(2)}, u32[]{:S(2)}) collective-permute-start(bf16[16,4096]{1,0:T(8,128)(2,1)S(1)} %collective-permute-done.5.refs_4_.refs_8_), channel_id=1, source_target_pairs={{0,4},{1,3},{4,8},{5,1},{8,12},{9,5},{12,14},{13,9},{14,10},{15,13... | collective-permute-start | bytes 393224 | tf_op jit(solution)/shard_map/ppermute | solution.py:43
  16.9 9.7 %collective-permute-start.12 = (bf16[128,4096]{1,0:T(8,128)(2,1)S(1)}, bf16[128,4096]{1,0:T(8,128)(2,1)S(1)}, u32[]{:S(2)}, u32[]{:S(2)}) collective-permute-start(bf16[128,4096]{1,0:T(8,128)(2,1)S(1)} %constant_dynamic-update-slice_fusion), channel_id=1, source_target_pairs={{0,1},{1,0},{2,3},{3,2},{4,5},{5,4},{6,7},{7,6},{8,9},{9,8},{10,11... | collective-permute-start | bytes 3145736 | tf_op jit(solution)/shard_map/ppermute | solution.py:46
  19.6 4.6 %collective-permute-start.16 = (bf16[16,4096]{1,0:T(8,128)(2,1)S(1)}, bf16[16,4096]{1,0:T(8,128)(2,1)S(1)}, u32[]{:S(2)}, u32[]{:S(2)}) collective-permute-start(bf16[16,4096]{1,0:T(8,128)(2,1)S(1)} %collective-permute-done.14.refs_5_), channel_id=1, source_target_pairs={{0,4},{1,3},{4,8},{5,1},{8,12},{9,5},{12,14},{13,9},{14,10},{15,13... | collective-permute-start | bytes 393224 | tf_op jit(solution)/shard_map/ppermute | solution.py:43
  20.0 5.1 %collective-permute-start.17 = (bf16[16,4096]{1,0:T(8,128)(2,1)S(1)}, bf16[16,4096]{1,0:T(8,128)(2,1)S(1)}, u32[]{:S(2)}, u32[]{:S(2)}) collective-permute-start(bf16[16,4096]{1,0:T(8,128)(2,1)S(1)} %collective-permute-done.15.refs_6_), channel_id=1, source_target_pairs={{0,4},{1,3},{4,8},{5,1},{8,12},{9,5},{12,14},{13,9},{14,10},{15,13... | collective-permute-start | bytes 393224 | tf_op jit(solution)/shard_map/ppermute | solution.py:43
  21.9 4.8 %collective-permute-start.13 = (bf16[64,4096]{1,0:T(8,128)(2,1)S(1)}, bf16[64,4096]{1,0:T(8,128)(2,1)S(1)}, u32[]{:S(2)}, u32[]{:S(2)}) collective-permute-start(bf16[64,4096]{1,0:T(8,128)(2,1)S(1)} %pad_maximum_fusion), channel_id=1, source_target_pairs={{0,1},{1,0},{2,3},{3,2},{4,5},{5,4},{6,7},{7,6},{8,9},{9,8},{10,11... | collective-permute-start | bytes 1572872 | tf_op jit(solution)/shard_map/ppermute | solution.py:46
  25.1 4.0 %collective-permute-start.18 = (bf16[64,4096]{1,0:T(8,128)(2,1)S(1)}, bf16[64,4096]{1,0:T(8,128)(2,1)S(1)}, u32[]{:S(2)}, u32[]{:S(2)}) collective-permute-start(bf16[64,4096]{1,0:T(8,128)(2,1)S(1)} %pad_maximum_fusion.1), channel_id=1, source_target_pairs={{0,1},{1,0},{2,3},{3,2},{4,5},{5,4},{6,7},{7,6},{8,9},{9,8},{10,11... | collective-permute-start | bytes 1572872 | tf_op jit(solution)/shard_map/ppermute | solution.py:46

commit v22 on v19

--- a/solution.py
+++ b/solution.py
@@ -9,7 +9,7 @@
 
 TEMP = 64
 LANES = 128
-CHUNK = 1024
+CHUNK = 2048
 GROUP = 32
 BLOCK = 256
 LIMIT = 40 * 2**20

time: 30.8 us -> 30.8 us (level)
  no operation moved by 1% of the time
where the time goes in v22:
time: 30.8 us; the launch traced here: 30.6 us
  starting transfers between devices  22.3 us (72%)
  Pallas kernels  4.34 us (14%)
  waiting for transfers between devices  3.74 us (12%)
    ppermute x14, starting transfers between devices, hop(): return lax.ppermute(block, 'samp', ring)  15.4 us
    ppermute x5, starting transfers between devices, hand_over(): return lax.ppermute(block, 'samp', twins)  6.88 us
    pallas_call x2, Pallas kernels, call(): pl.pallas_call(functools.partial(kernel, spans), out_shape=out_shape, in_...  3.97 us
    ppermute x14, waiting for transfers between devices, hop(): return lax.ppermute(block, 'samp', ring)  3.72 us
  transfers between devices with their start and end apart: 19, of which 7 were waited for; matrix products, arithmetic and copies ran while one was open for 0% of the time, Pallas kernels for 7%

profile of v22, /device:TPU:1, one launch (start us, length us, event | category | flops | bytes accessed | tf_op | source)
XLA Modules:
  0.0 30.6 jit_solution(2375307432586926506)
XLA Ops:
  0.0 0.0 copy-start
  0.0 0.1 collective-permute-start
  0.1 2.7 %collective-permute-start.3 = (bf16[16,4096]{1,0:T(8,128)(2,1)}, bf16[16,4096]{1,0:T(8,128)(2,1)S(1)}, u32[]{:S(2)}, u32[]{:S(2)}) collective-permute-start(bf16[16,4096]{1,0:T(8,128)(2,1)} %param.5), channel_id=1, source_target_pairs={{0,4},{1,3},{4,8},{5,1},{8,12},{9,5},{12,14},{13,9},{14,10},{15,13... | collective-permute-start | bytes 393224 | tf_op jit(solution)/shard_map/ppermute | solution.py:42
  2.7 0.4 %collective-permute-start.8 = (bf16[16,4096]{1,0:T(8,128)(2,1)}, bf16[16,4096]{1,0:T(8,128)(2,1)S(1)}, u32[]{:S(2)}, u32[]{:S(2)}) collective-permute-start(bf16[16,4096]{1,0:T(8,128)(2,1)} %param.4), channel_id=1, source_target_pairs={{0,1},{1,0},{2,3},{3,2},{4,5},{5,4},{6,7},{7,6},{8,9},{9,8},{10,11... | collective-permute-start | bytes 393224 | tf_op jit(solution)/shard_map/ppermute | solution.py:45
  3.1 0.9 %collective-permute-start.9 = (bf16[16,4096]{1,0:T(8,128)(2,1)}, bf16[16,4096]{1,0:T(8,128)(2,1)S(1)}, u32[]{:S(2)}, u32[]{:S(2)}) collective-permute-start(bf16[16,4096]{1,0:T(8,128)(2,1)} %param.4), channel_id=1, source_target_pairs={{0,4},{1,3},{4,8},{5,1},{8,12},{9,5},{12,14},{13,9},{14,10},{15,13... | collective-permute-start | bytes 393224 | tf_op jit(solution)/shard_map/ppermute | solution.py:42
  4.0 0.0 collective-permute-done.refs_0_.refs_2_
  4.1 1.3 %collective-permute-start.1 = (bf16[16,4096]{1,0:T(8,128)(2,1)S(1)}, bf16[16,4096]{1,0:T(8,128)(2,1)S(1)}, u32[]{:S(2)}, u32[]{:S(2)}) collective-permute-start(bf16[16,4096]{1,0:T(8,128)(2,1)S(1)} %collective-permute-done.refs_0_.refs_2_), channel_id=1, source_target_pairs={{0,4},{1,3},{4,8},{5,1},{8,12},{9,5},{12,14},{13,9},{14,10},{15,13... | collective-permute-start | bytes 393224 | tf_op jit(solution)/shard_map/ppermute | solution.py:42
  5.4 0.3 collective-permute-done.3.refs_0_.refs_3_
  5.7 1.4 %collective-permute-start.4 = (bf16[16,4096]{1,0:T(8,128)(2,1)S(1)}, bf16[16,4096]{1,0:T(8,128)(2,1)S(1)}, u32[]{:S(2)}, u32[]{:S(2)}) collective-permute-start(bf16[16,4096]{1,0:T(8,128)(2,1)S(1)} %collective-permute-done.3.refs_0_.refs_3_), channel_id=1, source_target_pairs={{0,4},{1,3},{4,8},{5,1},{8,12},{9,5},{12,14},{13,9},{14,10},{15,13... | collective-permute-start | bytes 393224 | tf_op jit(solution)/shard_map/ppermute | solution.py:42
  7.1 0.1 shard_map.37.refs_0_
  7.1 0.0 collective-permute-done.8.refs_0_
  7.2 1.3 %collective-permute-start.10 = (bf16[16,4096]{1,0:T(8,128)(2,1)S(1)}, bf16[16,4096]{1,0:T(8,128)(2,1)S(1)}, u32[]{:S(2)}, u32[]{:S(2)}) collective-permute-start(bf16[16,4096]{1,0:T(8,128)(2,1)S(1)} %collective-permute-done.8.refs_0_), channel_id=1, source_target_pairs={{0,4},{1,3},{4,8},{5,1},{8,12},{9,5},{12,14},{13,9},{14,10},{15,13... | collective-permute-start | bytes 393224 | tf_op jit(solution)/shard_map/ppermute | solution.py:42
  8.5 0.0 collective-permute-done.9.refs_1_
  8.5 1.3 %collective-permute-start.11 = (bf16[16,4096]{1,0:T(8,128)(2,1)S(1)}, bf16[16,4096]{1,0:T(8,128)(2,1)S(1)}, u32[]{:S(2)}, u32[]{:S(2)}) collective-permute-start(bf16[16,4096]{1,0:T(8,128)(2,1)S(1)} %collective-permute-done.9.refs_1_), channel_id=1, source_target_pairs={{0,4},{1,3},{4,8},{5,1},{8,12},{9,5},{12,14},{13,9},{14,10},{15,13... | collective-permute-start | bytes 393224 | tf_op jit(solution)/shard_map/ppermute | solution.py:42
  9.8 0.0 collective-permute-done.1.refs_1_.refs_4_
  9.8 1.3 %collective-permute-start.2 = (bf16[16,4096]{1,0:T(8,128)(2,1)S(1)}, bf16[16,4096]{1,0:T(8,128)(2,1)S(1)}, u32[]{:S(2)}, u32[]{:S(2)}) collective-permute-start(bf16[16,4096]{1,0:T(8,128)(2,1)S(1)} %collective-permute-done.1.refs_1_.refs_4_), channel_id=1, source_target_pairs={{0,4},{1,3},{4,8},{5,1},{8,12},{9,5},{12,14},{13,9},{14,10},{15,13... | collective-permute-start | bytes 393224 | tf_op jit(solution)/shard_map/ppermute | solution.py:42
  11.1 0.0 collective-permute-done.4.refs_2_.refs_5_
  11.1 0.2 collective-permute-start.5
  11.4 0.3 collective-permute-done.10.refs_2_
  11.7 1.0 %collective-permute-start.14 = (bf16[16,4096]{1,0:T(8,128)(2,1)S(1)}, bf16[16,4096]{1,0:T(8,128)(2,1)S(1)}, u32[]{:S(2)}, u32[]{:S(2)}) collective-permute-start(bf16[16,4096]{1,0:T(8,128)(2,1)S(1)} %collective-permute-done.10.refs_2_), channel_id=1, source_target_pairs={{0,4},{1,3},{4,8},{5,1},{8,12},{9,5},{12,14},{13,9},{14,10},{15,13... | collective-permute-start | bytes 393224 | tf_op jit(solution)/shard_map/ppermute | solution.py:42
  12.7 0.3 collective-permute-done.11.refs_3_
  13.0 1.1 %collective-permute-start.15 = (bf16[16,4096]{1,0:T(8,128)(2,1)S(1)}, bf16[16,4096]{1,0:T(8,128)(2,1)S(1)}, u32[]{:S(2)}, u32[]{:S(2)}) collective-permute-start(bf16[16,4096]{1,0:T(8,128)(2,1)S(1)} %collective-permute-done.11.refs_3_), channel_id=1, source_target_pairs={{0,4},{1,3},{4,8},{5,1},{8,12},{9,5},{12,14},{13,9},{14,10},{15,13... | collective-permute-start | bytes 393224 | tf_op jit(solution)/shard_map/ppermute | solution.py:42
  14.1 0.4 %collective-permute-done.2.refs_3_.refs_7_ = bf16[16,4096]{1,0:T(8,128)(2,1)S(1)} collective-permute-done((bf16[16,4096]{1,0:T(8,128)(2,1)S(1)}, bf16[16,4096]{1,0:T(8,128)(2,1)S(1)}, u32[]{:S(2)}, u32[]{:S(2)}) %collective-permute-start.2) | collective-permute-done | bytes 131104 | tf_op jit(solution)/shard_map/ppermute | solution.py:42
  14.5 1.0 %collective-permute-start.6 = (bf16[16,4096]{1,0:T(8,128)(2,1)S(1)}, bf16[16,4096]{1,0:T(8,128)(2,1)S(1)}, u32[]{:S(2)}, u32[]{:S(2)}) collective-permute-start(bf16[16,4096]{1,0:T(8,128)(2,1)S(1)} %collective-permute-done.2.refs_3_.refs_7_), channel_id=1, source_target_pairs={{0,4},{1,3},{4,8},{5,1},{8,12},{9,5},{12,14},{13,9},{14,10},{15,13... | collective-permute-start | bytes 393224 | tf_op jit(solution)/shard_map/ppermute | solution.py:42
  15.5 0.4 %collective-permute-done.5.refs_4_.refs_8_ = bf16[16,4096]{1,0:T(8,128)(2,1)S(1)} collective-permute-done((bf16[16,4096]{1,0:T(8,128)(2,1)S(1)}, bf16[16,4096]{1,0:T(8,128)(2,1)S(1)}, u32[]{:S(2)}, u32[]{:S(2)}) %collective-permute-start.5) | collective-permute-done | bytes 131104 | tf_op jit(solution)/shard_map/ppermute | solution.py:42
  15.9 1.0 %collective-permute-start.7 = (bf16[16,4096]{1,0:T(8,128)(2,1)S(1)}, bf16[16,4096]{1,0:T(8,128)(2,1)S(1)}, u32[]{:S(2)}, u32[]{:S(2)}) collective-permute-start(bf16[16,4096]{1,0:T(8,128)(2,1)S(1)} %collective-permute-done.5.refs_4_.refs_8_), channel_id=1, source_target_pairs={{0,4},{1,3},{4,8},{5,1},{8,12},{9,5},{12,14},{13,9},{14,10},{15,13... | collective-permute-start | bytes 393224 | tf_op jit(solution)/shard_map/ppermute | solution.py:42
  16.9 2.7 %collective-permute-start.12 = (bf16[128,4096]{1,0:T(8,128)(2,1)S(1)}, bf16[128,4096]{1,0:T(8,128)(2,1)S(1)}, u32[]{:S(2)}, u32[]{:S(2)}) collective-permute-start(bf16[128,4096]{1,0:T(8,128)(2,1)S(1)} %constant_dynamic-update-slice_fusion), channel_id=1, source_target_pairs={{0,1},{1,0},{2,3},{3,2},{4,5},{5,4},{6,7},{7,6},{8,9},{9,8},{10,11... | collective-permute-start | bytes 3145736 | tf_op jit(solution)/shard_map/ppermute | solution.py:45
  19.6 0.0 collective-permute-done.14.refs_5_
  19.6 0.4 %collective-permute-start.16 = (bf16[16,4096]{1,0:T(8,128)(2,1)S(1)}, bf16[16,4096]{1,0:T(8,128)(2,1)S(1)}, u32[]{:S(2)}, u32[]{:S(2)}) collective-permute-start(bf16[16,4096]{1,0:T(8,128)(2,1)S(1)} %collective-permute-done.14.refs_5_), channel_id=1, source_target_pairs={{0,4},{1,3},{4,8},{5,1},{8,12},{9,5},{12,14},{13,9},{14,10},{15,13... | collective-permute-start | bytes 393224 | tf_op jit(solution)/shard_map/ppermute | solution.py:42
  20.0 0.0 collective-permute-done.15.refs_6_
  20.0 0.4 %collective-permute-start.17 = (bf16[16,4096]{1,0:T(8,128)(2,1)S(1)}, bf16[16,4096]{1,0:T(8,128)(2,1)S(1)}, u32[]{:S(2)}, u32[]{:S(2)}) collective-permute-start(bf16[16,4096]{1,0:T(8,128)(2,1)S(1)} %collective-permute-done.15.refs_6_), channel_id=1, source_target_pairs={{0,4},{1,3},{4,8},{5,1},{8,12},{9,5},{12,14},{13,9},{14,10},{15,13... | collective-permute-start | bytes 393224 | tf_op jit(solution)/shard_map/ppermute | solution.py:42
  20.4 0.0 collective-permute-done.6.refs_5_.refs_9_
  20.4 1.1 %collective-permute-done.7.refs_6_.refs_10_ = bf16[16,4096]{1,0:T(8,128)(2,1)S(1)} collective-permute-done((bf16[16,4096]{1,0:T(8,128)(2,1)S(1)}, bf16[16,4096]{1,0:T(8,128)(2,1)S(1)}, u32[]{:S(2)}, u32[]{:S(2)}) %collective-permute-start.7) | collective-permute-done | bytes 131104 | tf_op jit(solution)/shard_map/ppermute | solution.py:42
  21.5 0.3 %shard_map.38.refs_1_ = f32[1,4096]{1,0:T(1,128)S(1)} custom-call(bf16[16,4096]{1,0:T(8,128)(2,1)S(1)} %collective-permute-done.3.refs_0_.refs_3_, bf16[16,4096]{1,0:T(8,128)(2,1)S(1)} %collective-permute-done.1.refs_1_.refs_4_, bf16[16,4096]{1,0:T(8,128)(2,1)S(1)} %collective-permute-done.4.refs_2_.refs_5_, ...), custom_call_target="tpu_custom_call" | custom-call | tf_op jit(solution)/shard_map/pallas_call | solution.py:163
  21.9 2.3 %collective-permute-start.13 = (bf16[64,4096]{1,0:T(8,128)(2,1)S(1)}, bf16[64,4096]{1,0:T(8,128)(2,1)S(1)}, u32[]{:S(2)}, u32[]{:S(2)}) collective-permute-start(bf16[64,4096]{1,0:T(8,128)(2,1)S(1)} %pad_maximum_fusion), channel_id=1, source_target_pairs={{0,1},{1,0},{2,3},{3,2},{4,5},{5,4},{6,7},{7,6},{8,9},{9,8},{10,11... | collective-permute-start | bytes 1572872 | tf_op jit(solution)/shard_map/ppermute | solution.py:45
  24.1 0.0 collective-permute-done.16.refs_7_
  24.1 1.0 %collective-permute-done.17.refs_8_ = bf16[16,4096]{1,0:T(8,128)(2,1)S(1)} collective-permute-done((bf16[16,4096]{1,0:T(8,128)(2,1)S(1)}, bf16[16,4096]{1,0:T(8,128)(2,1)S(1)}, u32[]{:S(2)}, u32[]{:S(2)}) %collective-permute-start.17) | collective-permute-done | bytes 131104 | tf_op jit(solution)/shard_map/ppermute | solution.py:42
  25.1 1.5 %collective-permute-start.18 = (bf16[64,4096]{1,0:T(8,128)(2,1)S(1)}, bf16[64,4096]{1,0:T(8,128)(2,1)S(1)}, u32[]{:S(2)}, u32[]{:S(2)}) collective-permute-start(bf16[64,4096]{1,0:T(8,128)(2,1)S(1)} %pad_maximum_fusion.1), channel_id=1, source_target_pairs={{0,1},{1,0},{2,3},{3,2},{4,5},{5,4},{6,7},{7,6},{8,9},{9,8},{10,11... | collective-permute-start | bytes 1572872 | tf_op jit(solution)/shard_map/ppermute | solution.py:45
  26.6 0.0 collective-permute-done.13.refs_11_
  26.6 0.0 collective-permute-done.12.refs_6_.refs_4_
  26.6 0.0 copy-done
  26.6 1.9 %shard_map.39 = (bf16[512,4096]{1,0:T(8,128)(2,1)S(1)}, f32[1,4096]{1,0:T(1,128)S(1)}, f32[1,512]{1,0:T(1,128)S(1)}) custom-call(bf16[512,4096]{1,0:T(8,128)(2,1)S(1)} %copy-done, f32[1,4096]{1,0:T(1,128)S(1)} %shard_map.37.refs_0_, f32[1,4096]{1,0:T(1,128)S(1)} %shard_map.38.refs_1_, bf16[16,4096]{1,0:T(8,128)(2,1)S(1)} %collective-permute-done.refs_0_.refs_2_, ...), custom_call_target="tpu_custom_call" | custom-call | flops 1073741824 | bytes 6291456 | tf_op jit(solution)/shard_map/pallas_call | solution.py:222
  28.5 0.0 collective-permute-done.18.refs_9_
  28.6 2.1 %shard_map.40 = f32[1,512]{1,0:T(1,128)} custom-call(f32[1,512]{1,0:T(1,128)S(1)} %get-tuple-element.16.ref_log, bf16[512,4096]{1,0:T(8,128)(2,1)S(1)} %get-tuple-element.17.probes, f32[1,4096]{1,0:T(1,128)S(1)} %get-tuple-element.18.mean, bf16[16,4096]{1,0:T(8,128)(2,1)S(1)} %collective-permute-done.8.refs_0_, ...), custom_call_target="tpu_custom_call" | custom-call | flops 1073741824 | bytes 6291456 | tf_op jit(solution)/shard_map/pallas_call | solution.py:222
  (10 shorter events, 0.1 us)
Async XLA Ops:
  0.0 26.6 %copy-start = (bf16[512,4096]{1,0:T(8,128)(2,1)S(1)}, bf16[512,4096]{1,0:T(8,128)(2,1)}, u32[]{:S(2)}) copy-start(bf16[512,4096]{1,0:T(8,128)(2,1)} %queries.1) | copy-start | bytes 12582916
  0.0 4.0 %collective-permute-start = (bf16[16,4096]{1,0:T(8,128)(2,1)}, bf16[16,4096]{1,0:T(8,128)(2,1)S(1)}, u32[]{:S(2)}, u32[]{:S(2)}) collective-permute-start(bf16[16,4096]{1,0:T(8,128)(2,1)} %param.5), channel_id=1, source_target_pairs={{0,1},{1,0},{2,3},{3,2},{4,5},{5,4},{6,7},{7,6},{8,9},{9,8},{10,11... | collective-permute-start | bytes 393224 | tf_op jit(solution)/shard_map/ppermute | solution.py:45
  0.1 5.6 %collective-permute-start.3 = (bf16[16,4096]{1,0:T(8,128)(2,1)}, bf16[16,4096]{1,0:T(8,128)(2,1)S(1)}, u32[]{:S(2)}, u32[]{:S(2)}) collective-permute-start(bf16[16,4096]{1,0:T(8,128)(2,1)} %param.5), channel_id=1, source_target_pairs={{0,4},{1,3},{4,8},{5,1},{8,12},{9,5},{12,14},{13,9},{14,10},{15,13... | collective-permute-start | bytes 393224 | tf_op jit(solution)/shard_map/ppermute | solution.py:42
  2.7 4.4 %collective-permute-start.8 = (bf16[16,4096]{1,0:T(8,128)(2,1)}, bf16[16,4096]{1,0:T(8,128)(2,1)S(1)}, u32[]{:S(2)}, u32[]{:S(2)}) collective-permute-start(bf16[16,4096]{1,0:T(8,128)(2,1)} %param.4), channel_id=1, source_target_pairs={{0,1},{1,0},{2,3},{3,2},{4,5},{5,4},{6,7},{7,6},{8,9},{9,8},{10,11... | collective-permute-start | bytes 393224 | tf_op jit(solution)/shard_map/ppermute | solution.py:45
  3.1 5.4 %collective-permute-start.9 = (bf16[16,4096]{1,0:T(8,128)(2,1)}, bf16[16,4096]{1,0:T(8,128)(2,1)S(1)}, u32[]{:S(2)}, u32[]{:S(2)}) collective-permute-start(bf16[16,4096]{1,0:T(8,128)(2,1)} %param.4), channel_id=1, source_target_pairs={{0,4},{1,3},{4,8},{5,1},{8,12},{9,5},{12,14},{13,9},{14,10},{15,13... | collective-permute-start | bytes 393224 | tf_op jit(solution)/shard_map/ppermute | solution.py:42
  4.1 5.8 %collective-permute-start.1 = (bf16[16,4096]{1,0:T(8,128)(2,1)S(1)}, bf16[16,4096]{1,0:T(8,128)(2,1)S(1)}, u32[]{:S(2)}, u32[]{:S(2)}) collective-permute-start(bf16[16,4096]{1,0:T(8,128)(2,1)S(1)} %collective-permute-done.refs_0_.refs_2_), channel_id=1, source_target_pairs={{0,4},{1,3},{4,8},{5,1},{8,12},{9,5},{12,14},{13,9},{14,10},{15,13... | collective-permute-start | bytes 393224 | tf_op jit(solution)/shard_map/ppermute | solution.py:42
  5.7 5.4 %collective-permute-start.4 = (bf16[16,4096]{1,0:T(8,128)(2,1)S(1)}, bf16[16,4096]{1,0:T(8,128)(2,1)S(1)}, u32[]{:S(2)}, u32[]{:S(2)}) collective-permute-start(bf16[16,4096]{1,0:T(8,128)(2,1)S(1)} %collective-permute-done.3.refs_0_.refs_3_), channel_id=1, source_target_pairs={{0,4},{1,3},{4,8},{5,1},{8,12},{9,5},{12,14},{13,9},{14,10},{15,13... | collective-permute-start | bytes 393224 | tf_op jit(solution)/shard_map/ppermute | solution.py:42
  7.2 4.5 %collective-permute-start.10 = (bf16[16,4096]{1,0:T(8,128)(2,1)S(1)}, bf16[16,4096]{1,0:T(8,128)(2,1)S(1)}, u32[]{:S(2)}, u32[]{:S(2)}) collective-permute-start(bf16[16,4096]{1,0:T(8,128)(2,1)S(1)} %collective-permute-done.8.refs_0_), channel_id=1, source_target_pairs={{0,4},{1,3},{4,8},{5,1},{8,12},{9,5},{12,14},{13,9},{14,10},{15,13... | collective-permute-start | bytes 393224 | tf_op jit(solution)/shard_map/ppermute | solution.py:42
  8.5 4.5 %collective-permute-start.11 = (bf16[16,4096]{1,0:T(8,128)(2,1)S(1)}, bf16[16,4096]{1,0:T(8,128)(2,1)S(1)}, u32[]{:S(2)}, u32[]{:S(2)}) collective-permute-start(bf16[16,4096]{1,0:T(8,128)(2,1)S(1)} %collective-permute-done.9.refs_1_), channel_id=1, source_target_pairs={{0,4},{1,3},{4,8},{5,1},{8,12},{9,5},{12,14},{13,9},{14,10},{15,13... | collective-permute-start | bytes 393224 | tf_op jit(solution)/shard_map/ppermute | solution.py:42
  9.8 4.7 %collective-permute-start.2 = (bf16[16,4096]{1,0:T(8,128)(2,1)S(1)}, bf16[16,4096]{1,0:T(8,128)(2,1)S(1)}, u32[]{:S(2)}, u32[]{:S(2)}) collective-permute-start(bf16[16,4096]{1,0:T(8,128)(2,1)S(1)} %collective-permute-done.1.refs_1_.refs_4_), channel_id=1, source_target_pairs={{0,4},{1,3},{4,8},{5,1},{8,12},{9,5},{12,14},{13,9},{14,10},{15,13... | collective-permute-start | bytes 393224 | tf_op jit(solution)/shard_map/ppermute | solution.py:42
  11.1 4.8 %collective-permute-start.5 = (bf16[16,4096]{1,0:T(8,128)(2,1)S(1)}, bf16[16,4096]{1,0:T(8,128)(2,1)S(1)}, u32[]{:S(2)}, u32[]{:S(2)}) collective-permute-start(bf16[16,4096]{1,0:T(8,128)(2,1)S(1)} %collective-permute-done.4.refs_2_.refs_5_), channel_id=1, source_target_pairs={{0,4},{1,3},{4,8},{5,1},{8,12},{9,5},{12,14},{13,9},{14,10},{15,13... | collective-permute-start | bytes 393224 | tf_op jit(solution)/shard_map/ppermute | solution.py:42
  11.7 7.9 %collective-permute-start.14 = (bf16[16,4096]{1,0:T(8,128)(2,1)S(1)}, bf16[16,4096]{1,0:T(8,128)(2,1)S(1)}, u32[]{:S(2)}, u32[]{:S(2)}) collective-permute-start(bf16[16,4096]{1,0:T(8,128)(2,1)S(1)} %collective-permute-done.10.refs_2_), channel_id=1, source_target_pairs={{0,4},{1,3},{4,8},{5,1},{8,12},{9,5},{12,14},{13,9},{14,10},{15,13... | collective-permute-start | bytes 393224 | tf_op jit(solution)/shard_map/ppermute | solution.py:42
  13.0 7.0 %collective-permute-start.15 = (bf16[16,4096]{1,0:T(8,128)(2,1)S(1)}, bf16[16,4096]{1,0:T(8,128)(2,1)S(1)}, u32[]{:S(2)}, u32[]{:S(2)}) collective-permute-start(bf16[16,4096]{1,0:T(8,128)(2,1)S(1)} %collective-permute-done.11.refs_3_), channel_id=1, source_target_pairs={{0,4},{1,3},{4,8},{5,1},{8,12},{9,5},{12,14},{13,9},{14,10},{15,13... | collective-permute-start | bytes 393224 | tf_op jit(solution)/shard_map/ppermute | solution.py:42
  14.5 5.9 %collective-permute-start.6 = (bf16[16,4096]{1,0:T(8,128)(2,1)S(1)}, bf16[16,4096]{1,0:T(8,128)(2,1)S(1)}, u32[]{:S(2)}, u32[]{:S(2)}) collective-permute-start(bf16[16,4096]{1,0:T(8,128)(2,1)S(1)} %collective-permute-done.2.refs_3_.refs_7_), channel_id=1, source_target_pairs={{0,4},{1,3},{4,8},{5,1},{8,12},{9,5},{12,14},{13,9},{14,10},{15,13... | collective-permute-start | bytes 393224 | tf_op jit(solution)/shard_map/ppermute | solution.py:42
  15.9 5.6 %collective-permute-start.7 = (bf16[16,4096]{1,0:T(8,128)(2,1)S(1)}, bf16[16,4096]{1,0:T(8,128)(2,1)S(1)}, u32[]{:S(2)}, u32[]{:S(2)}) collective-permute-start(bf16[16,4096]{1,0:T(8,128)(2,1)S(1)} %collective-permute-done.5.refs_4_.refs_8_), channel_id=1, source_target_pairs={{0,4},{1,3},{4,8},{5,1},{8,12},{9,5},{12,14},{13,9},{14,10},{15,13... | collective-permute-start | bytes 393224 | tf_op jit(solution)/shard_map/ppermute | solution.py:42
  16.9 9.7 %collective-permute-start.12 = (bf16[128,4096]{1,0:T(8,128)(2,1)S(1)}, bf16[128,4096]{1,0:T(8,128)(2,1)S(1)}, u32[]{:S(2)}, u32[]{:S(2)}) collective-permute-start(bf16[128,4096]{1,0:T(8,128)(2,1)S(1)} %constant_dynamic-update-slice_fusion), channel_id=1, source_target_pairs={{0,1},{1,0},{2,3},{3,2},{4,5},{5,4},{6,7},{7,6},{8,9},{9,8},{10,11... | collective-permute-start | bytes 3145736 | tf_op jit(solution)/shard_map/ppermute | solution.py:45
  19.6 4.6 %collective-permute-start.16 = (bf16[16,4096]{1,0:T(8,128)(2,1)S(1)}, bf16[16,4096]{1,0:T(8,128)(2,1)S(1)}, u32[]{:S(2)}, u32[]{:S(2)}) collective-permute-start(bf16[16,4096]{1,0:T(8,128)(2,1)S(1)} %collective-permute-done.14.refs_5_), channel_id=1, source_target_pairs={{0,4},{1,3},{4,8},{5,1},{8,12},{9,5},{12,14},{13,9},{14,10},{15,13... | collective-permute-start | bytes 393224 | tf_op jit(solution)/shard_map/ppermute | solution.py:42
  20.0 5.1 %collective-permute-start.17 = (bf16[16,4096]{1,0:T(8,128)(2,1)S(1)}, bf16[16,4096]{1,0:T(8,128)(2,1)S(1)}, u32[]{:S(2)}, u32[]{:S(2)}) collective-permute-start(bf16[16,4096]{1,0:T(8,128)(2,1)S(1)} %collective-permute-done.15.refs_6_), channel_id=1, source_target_pairs={{0,4},{1,3},{4,8},{5,1},{8,12},{9,5},{12,14},{13,9},{14,10},{15,13... | collective-permute-start | bytes 393224 | tf_op jit(solution)/shard_map/ppermute | solution.py:42
  21.9 4.8 %collective-permute-start.13 = (bf16[64,4096]{1,0:T(8,128)(2,1)S(1)}, bf16[64,4096]{1,0:T(8,128)(2,1)S(1)}, u32[]{:S(2)}, u32[]{:S(2)}) collective-permute-start(bf16[64,4096]{1,0:T(8,128)(2,1)S(1)} %pad_maximum_fusion), channel_id=1, source_target_pairs={{0,1},{1,0},{2,3},{3,2},{4,5},{5,4},{6,7},{7,6},{8,9},{9,8},{10,11... | collective-permute-start | bytes 1572872 | tf_op jit(solution)/shard_map/ppermute | solution.py:45
  25.1 3.4 %collective-permute-start.18 = (bf16[64,4096]{1,0:T(8,128)(2,1)S(1)}, bf16[64,4096]{1,0:T(8,128)(2,1)S(1)}, u32[]{:S(2)}, u32[]{:S(2)}) collective-permute-start(bf16[64,4096]{1,0:T(8,128)(2,1)S(1)} %pad_maximum_fusion.1), channel_id=1, source_target_pairs={{0,1},{1,0},{2,3},{3,2},{4,5},{5,4},{6,7},{7,6},{8,9},{9,8},{10,11... | collective-permute-start | bytes 1572872 | tf_op jit(solution)/shard_map/ppermute | solution.py:45

commit v23 on v19

--- a/solution.py
+++ b/solution.py
@@ -175,8 +175,7 @@
     panel, (probes, mean, ref_log, centered, squares, scores) = refs[: len(spans)], refs[len(spans) :]
     groups = panel_groups(panel, spans)
     count, features = centered.shape
-    for start in range(0, features, CHUNK):
-        cols = slice(start, start + CHUNK)
+    def take_mean(cols):
         total = totals[0][:, cols] + totals[1][:, cols]
         for k in late:
             low, high = spans[k]
@@ -187,7 +186,7 @@
         probes[rows, cols] = center(queries[rows, cols], mean[:, cols])
 
     def prepare(cols, first):
-        work = []
+        work = [functools.partial(take_mean, cols)]
         for group in groups:
             work.append(functools.partial(center_group, group, cols, mean, centered, squares, first))
         for rows in row_groups(probes.shape[0], GROUP):

time: 30.8 us -> 30.8 us (level)
  no operation moved by 1% of the time
where the time goes in v23:
time: 30.8 us; the launch traced here: 30.6 us
  starting transfers between devices  22.3 us (72%)
  Pallas kernels  4.35 us (14%)
  waiting for transfers between devices  3.74 us (12%)
    ppermute x14, starting transfers between devices, hop(): return lax.ppermute(block, 'samp', ring)  15.4 us
    ppermute x5, starting transfers between devices, hand_over(): return lax.ppermute(block, 'samp', twins)  6.88 us
    pallas_call x2, Pallas kernels, call(): pl.pallas_call(functools.partial(kernel, spans), out_shape=out_shape, in_...  3.99 us
    ppermute x14, waiting for transfers between devices, hop(): return lax.ppermute(block, 'samp', ring)  3.72 us
  transfers between devices with their start and end apart: 19, of which 7 were waited for; matrix products, arithmetic and copies ran while one was open for 0% of the time, Pallas kernels for 7%

profile of v23, /device:TPU:1, one launch (start us, length us, event | category | flops | bytes accessed | tf_op | source)
XLA Modules:
  0.0 30.6 jit_solution(6552837289217194559)
XLA Ops:
  0.0 0.0 copy-start
  0.0 0.1 collective-permute-start
  0.1 2.7 %collective-permute-start.3 = (bf16[16,4096]{1,0:T(8,128)(2,1)}, bf16[16,4096]{1,0:T(8,128)(2,1)S(1)}, u32[]{:S(2)}, u32[]{:S(2)}) collective-permute-start(bf16[16,4096]{1,0:T(8,128)(2,1)} %param.5), channel_id=1, source_target_pairs={{0,4},{1,3},{4,8},{5,1},{8,12},{9,5},{12,14},{13,9},{14,10},{15,13... | collective-permute-start | bytes 393224 | tf_op jit(solution)/shard_map/ppermute | solution.py:42
  2.7 0.4 %collective-permute-start.8 = (bf16[16,4096]{1,0:T(8,128)(2,1)}, bf16[16,4096]{1,0:T(8,128)(2,1)S(1)}, u32[]{:S(2)}, u32[]{:S(2)}) collective-permute-start(bf16[16,4096]{1,0:T(8,128)(2,1)} %param.4), channel_id=1, source_target_pairs={{0,1},{1,0},{2,3},{3,2},{4,5},{5,4},{6,7},{7,6},{8,9},{9,8},{10,11... | collective-permute-start | bytes 393224 | tf_op jit(solution)/shard_map/ppermute | solution.py:45
  3.1 0.9 %collective-permute-start.9 = (bf16[16,4096]{1,0:T(8,128)(2,1)}, bf16[16,4096]{1,0:T(8,128)(2,1)S(1)}, u32[]{:S(2)}, u32[]{:S(2)}) collective-permute-start(bf16[16,4096]{1,0:T(8,128)(2,1)} %param.4), channel_id=1, source_target_pairs={{0,4},{1,3},{4,8},{5,1},{8,12},{9,5},{12,14},{13,9},{14,10},{15,13... | collective-permute-start | bytes 393224 | tf_op jit(solution)/shard_map/ppermute | solution.py:42
  4.0 0.0 collective-permute-done.refs_0_.refs_2_
  4.1 1.3 %collective-permute-start.1 = (bf16[16,4096]{1,0:T(8,128)(2,1)S(1)}, bf16[16,4096]{1,0:T(8,128)(2,1)S(1)}, u32[]{:S(2)}, u32[]{:S(2)}) collective-permute-start(bf16[16,4096]{1,0:T(8,128)(2,1)S(1)} %collective-permute-done.refs_0_.refs_2_), channel_id=1, source_target_pairs={{0,4},{1,3},{4,8},{5,1},{8,12},{9,5},{12,14},{13,9},{14,10},{15,13... | collective-permute-start | bytes 393224 | tf_op jit(solution)/shard_map/ppermute | solution.py:42
  5.4 0.3 collective-permute-done.3.refs_0_.refs_3_
  5.7 1.4 %collective-permute-start.4 = (bf16[16,4096]{1,0:T(8,128)(2,1)S(1)}, bf16[16,4096]{1,0:T(8,128)(2,1)S(1)}, u32[]{:S(2)}, u32[]{:S(2)}) collective-permute-start(bf16[16,4096]{1,0:T(8,128)(2,1)S(1)} %collective-permute-done.3.refs_0_.refs_3_), channel_id=1, source_target_pairs={{0,4},{1,3},{4,8},{5,1},{8,12},{9,5},{12,14},{13,9},{14,10},{15,13... | collective-permute-start | bytes 393224 | tf_op jit(solution)/shard_map/ppermute | solution.py:42
  7.1 0.1 shard_map.37.refs_0_
  7.1 0.0 collective-permute-done.8.refs_0_
  7.2 1.3 %collective-permute-start.10 = (bf16[16,4096]{1,0:T(8,128)(2,1)S(1)}, bf16[16,4096]{1,0:T(8,128)(2,1)S(1)}, u32[]{:S(2)}, u32[]{:S(2)}) collective-permute-start(bf16[16,4096]{1,0:T(8,128)(2,1)S(1)} %collective-permute-done.8.refs_0_), channel_id=1, source_target_pairs={{0,4},{1,3},{4,8},{5,1},{8,12},{9,5},{12,14},{13,9},{14,10},{15,13... | collective-permute-start | bytes 393224 | tf_op jit(solution)/shard_map/ppermute | solution.py:42
  8.5 0.0 collective-permute-done.9.refs_1_
  8.5 1.3 %collective-permute-start.11 = (bf16[16,4096]{1,0:T(8,128)(2,1)S(1)}, bf16[16,4096]{1,0:T(8,128)(2,1)S(1)}, u32[]{:S(2)}, u32[]{:S(2)}) collective-permute-start(bf16[16,4096]{1,0:T(8,128)(2,1)S(1)} %collective-permute-done.9.refs_1_), channel_id=1, source_target_pairs={{0,4},{1,3},{4,8},{5,1},{8,12},{9,5},{12,14},{13,9},{14,10},{15,13... | collective-permute-start | bytes 393224 | tf_op jit(solution)/shard_map/ppermute | solution.py:42
  9.8 0.0 collective-permute-done.1.refs_1_.refs_4_
  9.8 1.3 %collective-permute-start.2 = (bf16[16,4096]{1,0:T(8,128)(2,1)S(1)}, bf16[16,4096]{1,0:T(8,128)(2,1)S(1)}, u32[]{:S(2)}, u32[]{:S(2)}) collective-permute-start(bf16[16,4096]{1,0:T(8,128)(2,1)S(1)} %collective-permute-done.1.refs_1_.refs_4_), channel_id=1, source_target_pairs={{0,4},{1,3},{4,8},{5,1},{8,12},{9,5},{12,14},{13,9},{14,10},{15,13... | collective-permute-start | bytes 393224 | tf_op jit(solution)/shard_map/ppermute | solution.py:42
  11.1 0.0 collective-permute-done.4.refs_2_.refs_5_
  11.1 0.2 collective-permute-start.5
  11.4 0.3 collective-permute-done.10.refs_2_
  11.7 1.0 %collective-permute-start.14 = (bf16[16,4096]{1,0:T(8,128)(2,1)S(1)}, bf16[16,4096]{1,0:T(8,128)(2,1)S(1)}, u32[]{:S(2)}, u32[]{:S(2)}) collective-permute-start(bf16[16,4096]{1,0:T(8,128)(2,1)S(1)} %collective-permute-done.10.refs_2_), channel_id=1, source_target_pairs={{0,4},{1,3},{4,8},{5,1},{8,12},{9,5},{12,14},{13,9},{14,10},{15,13... | collective-permute-start | bytes 393224 | tf_op jit(solution)/shard_map/ppermute | solution.py:42
  12.7 0.3 collective-permute-done.11.refs_3_
  13.0 1.1 %collective-permute-start.15 = (bf16[16,4096]{1,0:T(8,128)(2,1)S(1)}, bf16[16,4096]{1,0:T(8,128)(2,1)S(1)}, u32[]{:S(2)}, u32[]{:S(2)}) collective-permute-start(bf16[16,4096]{1,0:T(8,128)(2,1)S(1)} %collective-permute-done.11.refs_3_), channel_id=1, source_target_pairs={{0,4},{1,3},{4,8},{5,1},{8,12},{9,5},{12,14},{13,9},{14,10},{15,13... | collective-permute-start | bytes 393224 | tf_op jit(solution)/shard_map/ppermute | solution.py:42
  14.1 0.4 %collective-permute-done.2.refs_3_.refs_7_ = bf16[16,4096]{1,0:T(8,128)(2,1)S(1)} collective-permute-done((bf16[16,4096]{1,0:T(8,128)(2,1)S(1)}, bf16[16,4096]{1,0:T(8,128)(2,1)S(1)}, u32[]{:S(2)}, u32[]{:S(2)}) %collective-permute-start.2) | collective-permute-done | bytes 131104 | tf_op jit(solution)/shard_map/ppermute | solution.py:42
  14.5 1.0 %collective-permute-start.6 = (bf16[16,4096]{1,0:T(8,128)(2,1)S(1)}, bf16[16,4096]{1,0:T(8,128)(2,1)S(1)}, u32[]{:S(2)}, u32[]{:S(2)}) collective-permute-start(bf16[16,4096]{1,0:T(8,128)(2,1)S(1)} %collective-permute-done.2.refs_3_.refs_7_), channel_id=1, source_target_pairs={{0,4},{1,3},{4,8},{5,1},{8,12},{9,5},{12,14},{13,9},{14,10},{15,13... | collective-permute-start | bytes 393224 | tf_op jit(solution)/shard_map/ppermute | solution.py:42
  15.5 0.4 %collective-permute-done.5.refs_4_.refs_8_ = bf16[16,4096]{1,0:T(8,128)(2,1)S(1)} collective-permute-done((bf16[16,4096]{1,0:T(8,128)(2,1)S(1)}, bf16[16,4096]{1,0:T(8,128)(2,1)S(1)}, u32[]{:S(2)}, u32[]{:S(2)}) %collective-permute-start.5) | collective-permute-done | bytes 131104 | tf_op jit(solution)/shard_map/ppermute | solution.py:42
  15.9 1.0 %collective-permute-start.7 = (bf16[16,4096]{1,0:T(8,128)(2,1)S(1)}, bf16[16,4096]{1,0:T(8,128)(2,1)S(1)}, u32[]{:S(2)}, u32[]{:S(2)}) collective-permute-start(bf16[16,4096]{1,0:T(8,128)(2,1)S(1)} %collective-permute-done.5.refs_4_.refs_8_), channel_id=1, source_target_pairs={{0,4},{1,3},{4,8},{5,1},{8,12},{9,5},{12,14},{13,9},{14,10},{15,13... | collective-permute-start | bytes 393224 | tf_op jit(solution)/shard_map/ppermute | solution.py:42
  16.9 2.7 %collective-permute-start.12 = (bf16[128,4096]{1,0:T(8,128)(2,1)S(1)}, bf16[128,4096]{1,0:T(8,128)(2,1)S(1)}, u32[]{:S(2)}, u32[]{:S(2)}) collective-permute-start(bf16[128,4096]{1,0:T(8,128)(2,1)S(1)} %constant_dynamic-update-slice_fusion), channel_id=1, source_target_pairs={{0,1},{1,0},{2,3},{3,2},{4,5},{5,4},{6,7},{7,6},{8,9},{9,8},{10,11... | collective-permute-start | bytes 3145736 | tf_op jit(solution)/shard_map/ppermute | solution.py:45
  19.6 0.0 collective-permute-done.14.refs_5_
  19.6 0.4 %collective-permute-start.16 = (bf16[16,4096]{1,0:T(8,128)(2,1)S(1)}, bf16[16,4096]{1,0:T(8,128)(2,1)S(1)}, u32[]{:S(2)}, u32[]{:S(2)}) collective-permute-start(bf16[16,4096]{1,0:T(8,128)(2,1)S(1)} %collective-permute-done.14.refs_5_), channel_id=1, source_target_pairs={{0,4},{1,3},{4,8},{5,1},{8,12},{9,5},{12,14},{13,9},{14,10},{15,13... | collective-permute-start | bytes 393224 | tf_op jit(solution)/shard_map/ppermute | solution.py:42
  20.0 0.0 collective-permute-done.15.refs_6_
  20.0 0.4 %collective-permute-start.17 = (bf16[16,4096]{1,0:T(8,128)(2,1)S(1)}, bf16[16,4096]{1,0:T(8,128)(2,1)S(1)}, u32[]{:S(2)}, u32[]{:S(2)}) collective-permute-start(bf16[16,4096]{1,0:T(8,128)(2,1)S(1)} %collective-permute-done.15.refs_6_), channel_id=1, source_target_pairs={{0,4},{1,3},{4,8},{5,1},{8,12},{9,5},{12,14},{13,9},{14,10},{15,13... | collective-permute-start | bytes 393224 | tf_op jit(solution)/shard_map/ppermute | solution.py:42
  20.4 0.0 collective-permute-done.6.refs_5_.refs_9_
  20.4 1.1 %collective-permute-done.7.refs_6_.refs_10_ = bf16[16,4096]{1,0:T(8,128)(2,1)S(1)} collective-permute-done((bf16[16,4096]{1,0:T(8,128)(2,1)S(1)}, bf16[16,4096]{1,0:T(8,128)(2,1)S(1)}, u32[]{:S(2)}, u32[]{:S(2)}) %collective-permute-start.7) | collective-permute-done | bytes 131104 | tf_op jit(solution)/shard_map/ppermute | solution.py:42
  21.5 0.3 %shard_map.38.refs_1_ = f32[1,4096]{1,0:T(1,128)S(1)} custom-call(bf16[16,4096]{1,0:T(8,128)(2,1)S(1)} %collective-permute-done.3.refs_0_.refs_3_, bf16[16,4096]{1,0:T(8,128)(2,1)S(1)} %collective-permute-done.1.refs_1_.refs_4_, bf16[16,4096]{1,0:T(8,128)(2,1)S(1)} %collective-permute-done.4.refs_2_.refs_5_, ...), custom_call_target="tpu_custom_call" | custom-call | tf_op jit(solution)/shard_map/pallas_call | solution.py:163
  21.9 2.3 %collective-permute-start.13 = (bf16[64,4096]{1,0:T(8,128)(2,1)S(1)}, bf16[64,4096]{1,0:T(8,128)(2,1)S(1)}, u32[]{:S(2)}, u32[]{:S(2)}) collective-permute-start(bf16[64,4096]{1,0:T(8,128)(2,1)S(1)} %pad_maximum_fusion), channel_id=1, source_target_pairs={{0,1},{1,0},{2,3},{3,2},{4,5},{5,4},{6,7},{7,6},{8,9},{9,8},{10,11... | collective-permute-start | bytes 1572872 | tf_op jit(solution)/shard_map/ppermute | solution.py:45
  24.1 0.0 collective-permute-done.16.refs_7_
  24.1 1.0 %collective-permute-done.17.refs_8_ = bf16[16,4096]{1,0:T(8,128)(2,1)S(1)} collective-permute-done((bf16[16,4096]{1,0:T(8,128)(2,1)S(1)}, bf16[16,4096]{1,0:T(8,128)(2,1)S(1)}, u32[]{:S(2)}, u32[]{:S(2)}) %collective-permute-start.17) | collective-permute-done | bytes 131104 | tf_op jit(solution)/shard_map/ppermute | solution.py:42
  25.1 1.5 %collective-permute-start.18 = (bf16[64,4096]{1,0:T(8,128)(2,1)S(1)}, bf16[64,4096]{1,0:T(8,128)(2,1)S(1)}, u32[]{:S(2)}, u32[]{:S(2)}) collective-permute-start(bf16[64,4096]{1,0:T(8,128)(2,1)S(1)} %pad_maximum_fusion.1), channel_id=1, source_target_pairs={{0,1},{1,0},{2,3},{3,2},{4,5},{5,4},{6,7},{7,6},{8,9},{9,8},{10,11... | collective-permute-start | bytes 1572872 | tf_op jit(solution)/shard_map/ppermute | solution.py:45
  26.6 0.0 collective-permute-done.13.refs_11_
  26.6 0.0 collective-permute-done.12.refs_6_.refs_4_
  26.6 0.0 copy-done
  26.6 1.9 %shard_map.39 = (bf16[512,4096]{1,0:T(8,128)(2,1)S(1)}, f32[1,4096]{1,0:T(1,128)S(1)}, f32[1,512]{1,0:T(1,128)S(1)}) custom-call(bf16[512,4096]{1,0:T(8,128)(2,1)S(1)} %copy-done, f32[1,4096]{1,0:T(1,128)S(1)} %shard_map.37.refs_0_, f32[1,4096]{1,0:T(1,128)S(1)} %shard_map.38.refs_1_, bf16[16,4096]{1,0:T(8,128)(2,1)S(1)} %collective-permute-done.refs_0_.refs_2_, ...), custom_call_target="tpu_custom_call" | custom-call | flops 1073741824 | bytes 6291456 | tf_op jit(solution)/shard_map/pallas_call | solution.py:221
  28.6 0.0 collective-permute-done.18.refs_9_
  28.6 2.1 %shard_map.40 = f32[1,512]{1,0:T(1,128)} custom-call(f32[1,512]{1,0:T(1,128)S(1)} %get-tuple-element.16.ref_log, bf16[512,4096]{1,0:T(8,128)(2,1)S(1)} %get-tuple-element.17.probes, f32[1,4096]{1,0:T(1,128)S(1)} %get-tuple-element.18.mean, bf16[16,4096]{1,0:T(8,128)(2,1)S(1)} %collective-permute-done.8.refs_0_, ...), custom_call_target="tpu_custom_call" | custom-call | flops 1073741824 | bytes 6291456 | tf_op jit(solution)/shard_map/pallas_call | solution.py:221
  (10 shorter events, 0.1 us)
Async XLA Ops:
  0.0 26.6 %copy-start = (bf16[512,4096]{1,0:T(8,128)(2,1)S(1)}, bf16[512,4096]{1,0:T(8,128)(2,1)}, u32[]{:S(2)}) copy-start(bf16[512,4096]{1,0:T(8,128)(2,1)} %queries.1) | copy-start | bytes 12582916
  0.0 4.0 %collective-permute-start = (bf16[16,4096]{1,0:T(8,128)(2,1)}, bf16[16,4096]{1,0:T(8,128)(2,1)S(1)}, u32[]{:S(2)}, u32[]{:S(2)}) collective-permute-start(bf16[16,4096]{1,0:T(8,128)(2,1)} %param.5), channel_id=1, source_target_pairs={{0,1},{1,0},{2,3},{3,2},{4,5},{5,4},{6,7},{7,6},{8,9},{9,8},{10,11... | collective-permute-start | bytes 393224 | tf_op jit(solution)/shard_map/ppermute | solution.py:45
  0.1 5.6 %collective-permute-start.3 = (bf16[16,4096]{1,0:T(8,128)(2,1)}, bf16[16,4096]{1,0:T(8,128)(2,1)S(1)}, u32[]{:S(2)}, u32[]{:S(2)}) collective-permute-start(bf16[16,4096]{1,0:T(8,128)(2,1)} %param.5), channel_id=1, source_target_pairs={{0,4},{1,3},{4,8},{5,1},{8,12},{9,5},{12,14},{13,9},{14,10},{15,13... | collective-permute-start | bytes 393224 | tf_op jit(solution)/shard_map/ppermute | solution.py:42
  2.7 4.4 %collective-permute-start.8 = (bf16[16,4096]{1,0:T(8,128)(2,1)}, bf16[16,4096]{1,0:T(8,128)(2,1)S(1)}, u32[]{:S(2)}, u32[]{:S(2)}) collective-permute-start(bf16[16,4096]{1,0:T(8,128)(2,1)} %param.4), channel_id=1, source_target_pairs={{0,1},{1,0},{2,3},{3,2},{4,5},{5,4},{6,7},{7,6},{8,9},{9,8},{10,11... | collective-permute-start | bytes 393224 | tf_op jit(solution)/shard_map/ppermute | solution.py:45
  3.1 5.4 %collective-permute-start.9 = (bf16[16,4096]{1,0:T(8,128)(2,1)}, bf16[16,4096]{1,0:T(8,128)(2,1)S(1)}, u32[]{:S(2)}, u32[]{:S(2)}) collective-permute-start(bf16[16,4096]{1,0:T(8,128)(2,1)} %param.4), channel_id=1, source_target_pairs={{0,4},{1,3},{4,8},{5,1},{8,12},{9,5},{12,14},{13,9},{14,10},{15,13... | collective-permute-start | bytes 393224 | tf_op jit(solution)/shard_map/ppermute | solution.py:42
  4.1 5.8 %collective-permute-start.1 = (bf16[16,4096]{1,0:T(8,128)(2,1)S(1)}, bf16[16,4096]{1,0:T(8,128)(2,1)S(1)}, u32[]{:S(2)}, u32[]{:S(2)}) collective-permute-start(bf16[16,4096]{1,0:T(8,128)(2,1)S(1)} %collective-permute-done.refs_0_.refs_2_), channel_id=1, source_target_pairs={{0,4},{1,3},{4,8},{5,1},{8,12},{9,5},{12,14},{13,9},{14,10},{15,13... | collective-permute-start | bytes 393224 | tf_op jit(solution)/shard_map/ppermute | solution.py:42
  5.7 5.4 %collective-permute-start.4 = (bf16[16,4096]{1,0:T(8,128)(2,1)S(1)}, bf16[16,4096]{1,0:T(8,128)(2,1)S(1)}, u32[]{:S(2)}, u32[]{:S(2)}) collective-permute-start(bf16[16,4096]{1,0:T(8,128)(2,1)S(1)} %collective-permute-done.3.refs_0_.refs_3_), channel_id=1, source_target_pairs={{0,4},{1,3},{4,8},{5,1},{8,12},{9,5},{12,14},{13,9},{14,10},{15,13... | collective-permute-start | bytes 393224 | tf_op jit(solution)/shard_map/ppermute | solution.py:42
  7.2 4.5 %collective-permute-start.10 = (bf16[16,4096]{1,0:T(8,128)(2,1)S(1)}, bf16[16,4096]{1,0:T(8,128)(2,1)S(1)}, u32[]{:S(2)}, u32[]{:S(2)}) collective-permute-start(bf16[16,4096]{1,0:T(8,128)(2,1)S(1)} %collective-permute-done.8.refs_0_), channel_id=1, source_target_pairs={{0,4},{1,3},{4,8},{5,1},{8,12},{9,5},{12,14},{13,9},{14,10},{15,13... | collective-permute-start | bytes 393224 | tf_op jit(solution)/shard_map/ppermute | solution.py:42
  8.5 4.5 %collective-permute-start.11 = (bf16[16,4096]{1,0:T(8,128)(2,1)S(1)}, bf16[16,4096]{1,0:T(8,128)(2,1)S(1)}, u32[]{:S(2)}, u32[]{:S(2)}) collective-permute-start(bf16[16,4096]{1,0:T(8,128)(2,1)S(1)} %collective-permute-done.9.refs_1_), channel_id=1, source_target_pairs={{0,4},{1,3},{4,8},{5,1},{8,12},{9,5},{12,14},{13,9},{14,10},{15,13... | collective-permute-start | bytes 393224 | tf_op jit(solution)/shard_map/ppermute | solution.py:42
  9.8 4.7 %collective-permute-start.2 = (bf16[16,4096]{1,0:T(8,128)(2,1)S(1)}, bf16[16,4096]{1,0:T(8,128)(2,1)S(1)}, u32[]{:S(2)}, u32[]{:S(2)}) collective-permute-start(bf16[16,4096]{1,0:T(8,128)(2,1)S(1)} %collective-permute-done.1.refs_1_.refs_4_), channel_id=1, source_target_pairs={{0,4},{1,3},{4,8},{5,1},{8,12},{9,5},{12,14},{13,9},{14,10},{15,13... | collective-permute-start | bytes 393224 | tf_op jit(solution)/shard_map/ppermute | solution.py:42
  11.1 4.8 %collective-permute-start.5 = (bf16[16,4096]{1,0:T(8,128)(2,1)S(1)}, bf16[16,4096]{1,0:T(8,128)(2,1)S(1)}, u32[]{:S(2)}, u32[]{:S(2)}) collective-permute-start(bf16[16,4096]{1,0:T(8,128)(2,1)S(1)} %collective-permute-done.4.refs_2_.refs_5_), channel_id=1, source_target_pairs={{0,4},{1,3},{4,8},{5,1},{8,12},{9,5},{12,14},{13,9},{14,10},{15,13... | collective-permute-start | bytes 393224 | tf_op jit(solution)/shard_map/ppermute | solution.py:42
  11.7 7.9 %collective-permute-start.14 = (bf16[16,4096]{1,0:T(8,128)(2,1)S(1)}, bf16[16,4096]{1,0:T(8,128)(2,1)S(1)}, u32[]{:S(2)}, u32[]{:S(2)}) collective-permute-start(bf16[16,4096]{1,0:T(8,128)(2,1)S(1)} %collective-permute-done.10.refs_2_), channel_id=1, source_target_pairs={{0,4},{1,3},{4,8},{5,1},{8,12},{9,5},{12,14},{13,9},{14,10},{15,13... | collective-permute-start | bytes 393224 | tf_op jit(solution)/shard_map/ppermute | solution.py:42
  13.0 7.0 %collective-permute-start.15 = (bf16[16,4096]{1,0:T(8,128)(2,1)S(1)}, bf16[16,4096]{1,0:T(8,128)(2,1)S(1)}, u32[]{:S(2)}, u32[]{:S(2)}) collective-permute-start(bf16[16,4096]{1,0:T(8,128)(2,1)S(1)} %collective-permute-done.11.refs_3_), channel_id=1, source_target_pairs={{0,4},{1,3},{4,8},{5,1},{8,12},{9,5},{12,14},{13,9},{14,10},{15,13... | collective-permute-start | bytes 393224 | tf_op jit(solution)/shard_map/ppermute | solution.py:42
  14.5 5.9 %collective-permute-start.6 = (bf16[16,4096]{1,0:T(8,128)(2,1)S(1)}, bf16[16,4096]{1,0:T(8,128)(2,1)S(1)}, u32[]{:S(2)}, u32[]{:S(2)}) collective-permute-start(bf16[16,4096]{1,0:T(8,128)(2,1)S(1)} %collective-permute-done.2.refs_3_.refs_7_), channel_id=1, source_target_pairs={{0,4},{1,3},{4,8},{5,1},{8,12},{9,5},{12,14},{13,9},{14,10},{15,13... | collective-permute-start | bytes 393224 | tf_op jit(solution)/shard_map/ppermute | solution.py:42
  15.9 5.6 %collective-permute-start.7 = (bf16[16,4096]{1,0:T(8,128)(2,1)S(1)}, bf16[16,4096]{1,0:T(8,128)(2,1)S(1)}, u32[]{:S(2)}, u32[]{:S(2)}) collective-permute-start(bf16[16,4096]{1,0:T(8,128)(2,1)S(1)} %collective-permute-done.5.refs_4_.refs_8_), channel_id=1, source_target_pairs={{0,4},{1,3},{4,8},{5,1},{8,12},{9,5},{12,14},{13,9},{14,10},{15,13... | collective-permute-start | bytes 393224 | tf_op jit(solution)/shard_map/ppermute | solution.py:42
  16.9 9.7 %collective-permute-start.12 = (bf16[128,4096]{1,0:T(8,128)(2,1)S(1)}, bf16[128,4096]{1,0:T(8,128)(2,1)S(1)}, u32[]{:S(2)}, u32[]{:S(2)}) collective-permute-start(bf16[128,4096]{1,0:T(8,128)(2,1)S(1)} %constant_dynamic-update-slice_fusion), channel_id=1, source_target_pairs={{0,1},{1,0},{2,3},{3,2},{4,5},{5,4},{6,7},{7,6},{8,9},{9,8},{10,11... | collective-permute-start | bytes 3145736 | tf_op jit(solution)/shard_map/ppermute | solution.py:45
  19.6 4.6 %collective-permute-start.16 = (bf16[16,4096]{1,0:T(8,128)(2,1)S(1)}, bf16[16,4096]{1,0:T(8,128)(2,1)S(1)}, u32[]{:S(2)}, u32[]{:S(2)}) collective-permute-start(bf16[16,4096]{1,0:T(8,128)(2,1)S(1)} %collective-permute-done.14.refs_5_), channel_id=1, source_target_pairs={{0,4},{1,3},{4,8},{5,1},{8,12},{9,5},{12,14},{13,9},{14,10},{15,13... | collective-permute-start | bytes 393224 | tf_op jit(solution)/shard_map/ppermute | solution.py:42
  20.0 5.1 %collective-permute-start.17 = (bf16[16,4096]{1,0:T(8,128)(2,1)S(1)}, bf16[16,4096]{1,0:T(8,128)(2,1)S(1)}, u32[]{:S(2)}, u32[]{:S(2)}) collective-permute-start(bf16[16,4096]{1,0:T(8,128)(2,1)S(1)} %collective-permute-done.15.refs_6_), channel_id=1, source_target_pairs={{0,4},{1,3},{4,8},{5,1},{8,12},{9,5},{12,14},{13,9},{14,10},{15,13... | collective-permute-start | bytes 393224 | tf_op jit(solution)/shard_map/ppermute | solution.py:42
  21.9 4.8 %collective-permute-start.13 = (bf16[64,4096]{1,0:T(8,128)(2,1)S(1)}, bf16[64,4096]{1,0:T(8,128)(2,1)S(1)}, u32[]{:S(2)}, u32[]{:S(2)}) collective-permute-start(bf16[64,4096]{1,0:T(8,128)(2,1)S(1)} %pad_maximum_fusion), channel_id=1, source_target_pairs={{0,1},{1,0},{2,3},{3,2},{4,5},{5,4},{6,7},{7,6},{8,9},{9,8},{10,11... | collective-permute-start | bytes 1572872 | tf_op jit(solution)/shard_map/ppermute | solution.py:45
  25.1 3.4 %collective-permute-start.18 = (bf16[64,4096]{1,0:T(8,128)(2,1)S(1)}, bf16[64,4096]{1,0:T(8,128)(2,1)S(1)}, u32[]{:S(2)}, u32[]{:S(2)}) collective-permute-start(bf16[64,4096]{1,0:T(8,128)(2,1)S(1)} %pad_maximum_fusion.1), channel_id=1, source_target_pairs={{0,1},{1,0},{2,3},{3,2},{4,5},{5,4},{6,7},{7,6},{8,9},{9,8},{10,11... | collective-permute-start | bytes 1572872 | tf_op jit(solution)/shard_map/ppermute | solution.py:45

commit v24 on v19

--- a/solution.py
+++ b/solution.py
@@ -11,7 +11,7 @@
 LANES = 128
 CHUNK = 1024
 GROUP = 32
-BLOCK = 256
+BLOCK = 512
 LIMIT = 40 * 2**20
 
 

time: 30.8 us -> 30.8 us (level)
  no operation moved by 1% of the time
where the time goes in v24:
time: 30.8 us; the launch traced here: 30.6 us
  starting transfers between devices  22.3 us (72%)
  Pallas kernels  4.34 us (14%)
  waiting for transfers between devices  3.74 us (12%)
    ppermute x14, starting transfers between devices, hop(): return lax.ppermute(block, 'samp', ring)  15.4 us
    ppermute x5, starting transfers between devices, hand_over(): return lax.ppermute(block, 'samp', twins)  6.88 us
    pallas_call x2, Pallas kernels, call(): pl.pallas_call(functools.partial(kernel, spans), out_shape=out_shape, in_...  3.98 us
    ppermute x14, waiting for transfers between devices, hop(): return lax.ppermute(block, 'samp', ring)  3.72 us
  transfers between devices with their start and end apart: 19, of which 7 were waited for; matrix products, arithmetic and copies ran while one was open for 0% of the time, Pallas kernels for 7%

profile of v24, /device:TPU:1, one launch (start us, length us, event | category | flops | bytes accessed | tf_op | source)
XLA Modules:
  0.0 30.6 jit_solution(12106977386093073522)
XLA Ops:
  0.0 0.0 copy-start
  0.0 0.1 collective-permute-start
  0.1 2.7 %collective-permute-start.3 = (bf16[16,4096]{1,0:T(8,128)(2,1)}, bf16[16,4096]{1,0:T(8,128)(2,1)S(1)}, u32[]{:S(2)}, u32[]{:S(2)}) collective-permute-start(bf16[16,4096]{1,0:T(8,128)(2,1)} %param.5), channel_id=1, source_target_pairs={{0,4},{1,3},{4,8},{5,1},{8,12},{9,5},{12,14},{13,9},{14,10},{15,13... | collective-permute-start | bytes 393224 | tf_op jit(solution)/shard_map/ppermute | solution.py:42
  2.7 0.4 %collective-permute-start.8 = (bf16[16,4096]{1,0:T(8,128)(2,1)}, bf16[16,4096]{1,0:T(8,128)(2,1)S(1)}, u32[]{:S(2)}, u32[]{:S(2)}) collective-permute-start(bf16[16,4096]{1,0:T(8,128)(2,1)} %param.4), channel_id=1, source_target_pairs={{0,1},{1,0},{2,3},{3,2},{4,5},{5,4},{6,7},{7,6},{8,9},{9,8},{10,11... | collective-permute-start | bytes 393224 | tf_op jit(solution)/shard_map/ppermute | solution.py:45
  3.1 0.9 %collective-permute-start.9 = (bf16[16,4096]{1,0:T(8,128)(2,1)}, bf16[16,4096]{1,0:T(8,128)(2,1)S(1)}, u32[]{:S(2)}, u32[]{:S(2)}) collective-permute-start(bf16[16,4096]{1,0:T(8,128)(2,1)} %param.4), channel_id=1, source_target_pairs={{0,4},{1,3},{4,8},{5,1},{8,12},{9,5},{12,14},{13,9},{14,10},{15,13... | collective-permute-start | bytes 393224 | tf_op jit(solution)/shard_map/ppermute | solution.py:42
  4.0 0.0 collective-permute-done.refs_0_.refs_2_
  4.1 1.3 %collective-permute-start.1 = (bf16[16,4096]{1,0:T(8,128)(2,1)S(1)}, bf16[16,4096]{1,0:T(8,128)(2,1)S(1)}, u32[]{:S(2)}, u32[]{:S(2)}) collective-permute-start(bf16[16,4096]{1,0:T(8,128)(2,1)S(1)} %collective-permute-done.refs_0_.refs_2_), channel_id=1, source_target_pairs={{0,4},{1,3},{4,8},{5,1},{8,12},{9,5},{12,14},{13,9},{14,10},{15,13... | collective-permute-start | bytes 393224 | tf_op jit(solution)/shard_map/ppermute | solution.py:42
  5.4 0.3 collective-permute-done.3.refs_0_.refs_3_
  5.7 1.4 %collective-permute-start.4 = (bf16[16,4096]{1,0:T(8,128)(2,1)S(1)}, bf16[16,4096]{1,0:T(8,128)(2,1)S(1)}, u32[]{:S(2)}, u32[]{:S(2)}) collective-permute-start(bf16[16,4096]{1,0:T(8,128)(2,1)S(1)} %collective-permute-done.3.refs_0_.refs_3_), channel_id=1, source_target_pairs={{0,4},{1,3},{4,8},{5,1},{8,12},{9,5},{12,14},{13,9},{14,10},{15,13... | collective-permute-start | bytes 393224 | tf_op jit(solution)/shard_map/ppermute | solution.py:42
  7.1 0.1 shard_map.37.refs_0_
  7.1 0.0 collective-permute-done.8.refs_0_
  7.2 1.3 %collective-permute-start.10 = (bf16[16,4096]{1,0:T(8,128)(2,1)S(1)}, bf16[16,4096]{1,0:T(8,128)(2,1)S(1)}, u32[]{:S(2)}, u32[]{:S(2)}) collective-permute-start(bf16[16,4096]{1,0:T(8,128)(2,1)S(1)} %collective-permute-done.8.refs_0_), channel_id=1, source_target_pairs={{0,4},{1,3},{4,8},{5,1},{8,12},{9,5},{12,14},{13,9},{14,10},{15,13... | collective-permute-start | bytes 393224 | tf_op jit(solution)/shard_map/ppermute | solution.py:42
  8.5 0.0 collective-permute-done.9.refs_1_
  8.5 1.3 %collective-permute-start.11 = (bf16[16,4096]{1,0:T(8,128)(2,1)S(1)}, bf16[16,4096]{1,0:T(8,128)(2,1)S(1)}, u32[]{:S(2)}, u32[]{:S(2)}) collective-permute-start(bf16[16,4096]{1,0:T(8,128)(2,1)S(1)} %collective-permute-done.9.refs_1_), channel_id=1, source_target_pairs={{0,4},{1,3},{4,8},{5,1},{8,12},{9,5},{12,14},{13,9},{14,10},{15,13... | collective-permute-start | bytes 393224 | tf_op jit(solution)/shard_map/ppermute | solution.py:42
  9.8 0.0 collective-permute-done.1.refs_1_.refs_4_
  9.8 1.3 %collective-permute-start.2 = (bf16[16,4096]{1,0:T(8,128)(2,1)S(1)}, bf16[16,4096]{1,0:T(8,128)(2,1)S(1)}, u32[]{:S(2)}, u32[]{:S(2)}) collective-permute-start(bf16[16,4096]{1,0:T(8,128)(2,1)S(1)} %collective-permute-done.1.refs_1_.refs_4_), channel_id=1, source_target_pairs={{0,4},{1,3},{4,8},{5,1},{8,12},{9,5},{12,14},{13,9},{14,10},{15,13... | collective-permute-start | bytes 393224 | tf_op jit(solution)/shard_map/ppermute | solution.py:42
  11.1 0.0 collective-permute-done.4.refs_2_.refs_5_
  11.1 0.2 collective-permute-start.5
  11.4 0.3 collective-permute-done.10.refs_2_
  11.7 1.0 %collective-permute-start.14 = (bf16[16,4096]{1,0:T(8,128)(2,1)S(1)}, bf16[16,4096]{1,0:T(8,128)(2,1)S(1)}, u32[]{:S(2)}, u32[]{:S(2)}) collective-permute-start(bf16[16,4096]{1,0:T(8,128)(2,1)S(1)} %collective-permute-done.10.refs_2_), channel_id=1, source_target_pairs={{0,4},{1,3},{4,8},{5,1},{8,12},{9,5},{12,14},{13,9},{14,10},{15,13... | collective-permute-start | bytes 393224 | tf_op jit(solution)/shard_map/ppermute | solution.py:42
  12.7 0.3 collective-permute-done.11.refs_3_
  13.0 1.1 %collective-permute-start.15 = (bf16[16,4096]{1,0:T(8,128)(2,1)S(1)}, bf16[16,4096]{1,0:T(8,128)(2,1)S(1)}, u32[]{:S(2)}, u32[]{:S(2)}) collective-permute-start(bf16[16,4096]{1,0:T(8,128)(2,1)S(1)} %collective-permute-done.11.refs_3_), channel_id=1, source_target_pairs={{0,4},{1,3},{4,8},{5,1},{8,12},{9,5},{12,14},{13,9},{14,10},{15,13... | collective-permute-start | bytes 393224 | tf_op jit(solution)/shard_map/ppermute | solution.py:42
  14.1 0.4 %collective-permute-done.2.refs_3_.refs_7_ = bf16[16,4096]{1,0:T(8,128)(2,1)S(1)} collective-permute-done((bf16[16,4096]{1,0:T(8,128)(2,1)S(1)}, bf16[16,4096]{1,0:T(8,128)(2,1)S(1)}, u32[]{:S(2)}, u32[]{:S(2)}) %collective-permute-start.2) | collective-permute-done | bytes 131104 | tf_op jit(solution)/shard_map/ppermute | solution.py:42
  14.5 1.0 %collective-permute-start.6 = (bf16[16,4096]{1,0:T(8,128)(2,1)S(1)}, bf16[16,4096]{1,0:T(8,128)(2,1)S(1)}, u32[]{:S(2)}, u32[]{:S(2)}) collective-permute-start(bf16[16,4096]{1,0:T(8,128)(2,1)S(1)} %collective-permute-done.2.refs_3_.refs_7_), channel_id=1, source_target_pairs={{0,4},{1,3},{4,8},{5,1},{8,12},{9,5},{12,14},{13,9},{14,10},{15,13... | collective-permute-start | bytes 393224 | tf_op jit(solution)/shard_map/ppermute | solution.py:42
  15.5 0.4 %collective-permute-done.5.refs_4_.refs_8_ = bf16[16,4096]{1,0:T(8,128)(2,1)S(1)} collective-permute-done((bf16[16,4096]{1,0:T(8,128)(2,1)S(1)}, bf16[16,4096]{1,0:T(8,128)(2,1)S(1)}, u32[]{:S(2)}, u32[]{:S(2)}) %collective-permute-start.5) | collective-permute-done | bytes 131104 | tf_op jit(solution)/shard_map/ppermute | solution.py:42
  15.9 1.0 %collective-permute-start.7 = (bf16[16,4096]{1,0:T(8,128)(2,1)S(1)}, bf16[16,4096]{1,0:T(8,128)(2,1)S(1)}, u32[]{:S(2)}, u32[]{:S(2)}) collective-permute-start(bf16[16,4096]{1,0:T(8,128)(2,1)S(1)} %collective-permute-done.5.refs_4_.refs_8_), channel_id=1, source_target_pairs={{0,4},{1,3},{4,8},{5,1},{8,12},{9,5},{12,14},{13,9},{14,10},{15,13... | collective-permute-start | bytes 393224 | tf_op jit(solution)/shard_map/ppermute | solution.py:42
  16.9 2.7 %collective-permute-start.12 = (bf16[128,4096]{1,0:T(8,128)(2,1)S(1)}, bf16[128,4096]{1,0:T(8,128)(2,1)S(1)}, u32[]{:S(2)}, u32[]{:S(2)}) collective-permute-start(bf16[128,4096]{1,0:T(8,128)(2,1)S(1)} %constant_dynamic-update-slice_fusion), channel_id=1, source_target_pairs={{0,1},{1,0},{2,3},{3,2},{4,5},{5,4},{6,7},{7,6},{8,9},{9,8},{10,11... | collective-permute-start | bytes 3145736 | tf_op jit(solution)/shard_map/ppermute | solution.py:45
  19.6 0.0 collective-permute-done.14.refs_5_
  19.6 0.4 %collective-permute-start.16 = (bf16[16,4096]{1,0:T(8,128)(2,1)S(1)}, bf16[16,4096]{1,0:T(8,128)(2,1)S(1)}, u32[]{:S(2)}, u32[]{:S(2)}) collective-permute-start(bf16[16,4096]{1,0:T(8,128)(2,1)S(1)} %collective-permute-done.14.refs_5_), channel_id=1, source_target_pairs={{0,4},{1,3},{4,8},{5,1},{8,12},{9,5},{12,14},{13,9},{14,10},{15,13... | collective-permute-start | bytes 393224 | tf_op jit(solution)/shard_map/ppermute | solution.py:42
  20.0 0.0 collective-permute-done.15.refs_6_
  20.0 0.4 %collective-permute-start.17 = (bf16[16,4096]{1,0:T(8,128)(2,1)S(1)}, bf16[16,4096]{1,0:T(8,128)(2,1)S(1)}, u32[]{:S(2)}, u32[]{:S(2)}) collective-permute-start(bf16[16,4096]{1,0:T(8,128)(2,1)S(1)} %collective-permute-done.15.refs_6_), channel_id=1, source_target_pairs={{0,4},{1,3},{4,8},{5,1},{8,12},{9,5},{12,14},{13,9},{14,10},{15,13... | collective-permute-start | bytes 393224 | tf_op jit(solution)/shard_map/ppermute | solution.py:42
  20.4 0.0 collective-permute-done.6.refs_5_.refs_9_
  20.4 1.1 %collective-permute-done.7.refs_6_.refs_10_ = bf16[16,4096]{1,0:T(8,128)(2,1)S(1)} collective-permute-done((bf16[16,4096]{1,0:T(8,128)(2,1)S(1)}, bf16[16,4096]{1,0:T(8,128)(2,1)S(1)}, u32[]{:S(2)}, u32[]{:S(2)}) %collective-permute-start.7) | collective-permute-done | bytes 131104 | tf_op jit(solution)/shard_map/ppermute | solution.py:42
  21.5 0.3 %shard_map.38.refs_1_ = f32[1,4096]{1,0:T(1,128)S(1)} custom-call(bf16[16,4096]{1,0:T(8,128)(2,1)S(1)} %collective-permute-done.3.refs_0_.refs_3_, bf16[16,4096]{1,0:T(8,128)(2,1)S(1)} %collective-permute-done.1.refs_1_.refs_4_, bf16[16,4096]{1,0:T(8,128)(2,1)S(1)} %collective-permute-done.4.refs_2_.refs_5_, ...), custom_call_target="tpu_custom_call" | custom-call | tf_op jit(solution)/shard_map/pallas_call | solution.py:163
  21.9 2.3 %collective-permute-start.13 = (bf16[64,4096]{1,0:T(8,128)(2,1)S(1)}, bf16[64,4096]{1,0:T(8,128)(2,1)S(1)}, u32[]{:S(2)}, u32[]{:S(2)}) collective-permute-start(bf16[64,4096]{1,0:T(8,128)(2,1)S(1)} %pad_maximum_fusion), channel_id=1, source_target_pairs={{0,1},{1,0},{2,3},{3,2},{4,5},{5,4},{6,7},{7,6},{8,9},{9,8},{10,11... | collective-permute-start | bytes 1572872 | tf_op jit(solution)/shard_map/ppermute | solution.py:45
  24.1 0.0 collective-permute-done.16.refs_7_
  24.1 1.0 %collective-permute-done.17.refs_8_ = bf16[16,4096]{1,0:T(8,128)(2,1)S(1)} collective-permute-done((bf16[16,4096]{1,0:T(8,128)(2,1)S(1)}, bf16[16,4096]{1,0:T(8,128)(2,1)S(1)}, u32[]{:S(2)}, u32[]{:S(2)}) %collective-permute-start.17) | collective-permute-done | bytes 131104 | tf_op jit(solution)/shard_map/ppermute | solution.py:42
  25.1 1.5 %collective-permute-start.18 = (bf16[64,4096]{1,0:T(8,128)(2,1)S(1)}, bf16[64,4096]{1,0:T(8,128)(2,1)S(1)}, u32[]{:S(2)}, u32[]{:S(2)}) collective-permute-start(bf16[64,4096]{1,0:T(8,128)(2,1)S(1)} %pad_maximum_fusion.1), channel_id=1, source_target_pairs={{0,1},{1,0},{2,3},{3,2},{4,5},{5,4},{6,7},{7,6},{8,9},{9,8},{10,11... | collective-permute-start | bytes 1572872 | tf_op jit(solution)/shard_map/ppermute | solution.py:45
  26.6 0.0 collective-permute-done.13.refs_11_
  26.6 0.0 collective-permute-done.12.refs_6_.refs_4_
  26.6 0.0 copy-done
  26.6 1.9 %shard_map.39 = (bf16[512,4096]{1,0:T(8,128)(2,1)S(1)}, f32[1,4096]{1,0:T(1,128)S(1)}, f32[1,512]{1,0:T(1,128)S(1)}) custom-call(bf16[512,4096]{1,0:T(8,128)(2,1)S(1)} %copy-done, f32[1,4096]{1,0:T(1,128)S(1)} %shard_map.37.refs_0_, f32[1,4096]{1,0:T(1,128)S(1)} %shard_map.38.refs_1_, bf16[16,4096]{1,0:T(8,128)(2,1)S(1)} %collective-permute-done.refs_0_.refs_2_, ...), custom_call_target="tpu_custom_call" | custom-call | flops 1073741824 | bytes 6291456 | tf_op jit(solution)/shard_map/pallas_call | solution.py:222
  28.6 0.0 collective-permute-done.18.refs_9_
  28.6 2.1 %shard_map.40 = f32[1,512]{1,0:T(1,128)} custom-call(f32[1,512]{1,0:T(1,128)S(1)} %get-tuple-element.16.ref_log, bf16[512,4096]{1,0:T(8,128)(2,1)S(1)} %get-tuple-element.17.probes, f32[1,4096]{1,0:T(1,128)S(1)} %get-tuple-element.18.mean, bf16[16,4096]{1,0:T(8,128)(2,1)S(1)} %collective-permute-done.8.refs_0_, ...), custom_call_target="tpu_custom_call" | custom-call | flops 1073741824 | bytes 6291456 | tf_op jit(solution)/shard_map/pallas_call | solution.py:222
  (10 shorter events, 0.1 us)
Async XLA Ops:
  0.0 26.6 %copy-start = (bf16[512,4096]{1,0:T(8,128)(2,1)S(1)}, bf16[512,4096]{1,0:T(8,128)(2,1)}, u32[]{:S(2)}) copy-start(bf16[512,4096]{1,0:T(8,128)(2,1)} %queries.1) | copy-start | bytes 12582916
  0.0 4.0 %collective-permute-start = (bf16[16,4096]{1,0:T(8,128)(2,1)}, bf16[16,4096]{1,0:T(8,128)(2,1)S(1)}, u32[]{:S(2)}, u32[]{:S(2)}) collective-permute-start(bf16[16,4096]{1,0:T(8,128)(2,1)} %param.5), channel_id=1, source_target_pairs={{0,1},{1,0},{2,3},{3,2},{4,5},{5,4},{6,7},{7,6},{8,9},{9,8},{10,11... | collective-permute-start | bytes 393224 | tf_op jit(solution)/shard_map/ppermute | solution.py:45
  0.1 5.6 %collective-permute-start.3 = (bf16[16,4096]{1,0:T(8,128)(2,1)}, bf16[16,4096]{1,0:T(8,128)(2,1)S(1)}, u32[]{:S(2)}, u32[]{:S(2)}) collective-permute-start(bf16[16,4096]{1,0:T(8,128)(2,1)} %param.5), channel_id=1, source_target_pairs={{0,4},{1,3},{4,8},{5,1},{8,12},{9,5},{12,14},{13,9},{14,10},{15,13... | collective-permute-start | bytes 393224 | tf_op jit(solution)/shard_map/ppermute | solution.py:42
  2.7 4.4 %collective-permute-start.8 = (bf16[16,4096]{1,0:T(8,128)(2,1)}, bf16[16,4096]{1,0:T(8,128)(2,1)S(1)}, u32[]{:S(2)}, u32[]{:S(2)}) collective-permute-start(bf16[16,4096]{1,0:T(8,128)(2,1)} %param.4), channel_id=1, source_target_pairs={{0,1},{1,0},{2,3},{3,2},{4,5},{5,4},{6,7},{7,6},{8,9},{9,8},{10,11... | collective-permute-start | bytes 393224 | tf_op jit(solution)/shard_map/ppermute | solution.py:45
  3.1 5.4 %collective-permute-start.9 = (bf16[16,4096]{1,0:T(8,128)(2,1)}, bf16[16,4096]{1,0:T(8,128)(2,1)S(1)}, u32[]{:S(2)}, u32[]{:S(2)}) collective-permute-start(bf16[16,4096]{1,0:T(8,128)(2,1)} %param.4), channel_id=1, source_target_pairs={{0,4},{1,3},{4,8},{5,1},{8,12},{9,5},{12,14},{13,9},{14,10},{15,13... | collective-permute-start | bytes 393224 | tf_op jit(solution)/shard_map/ppermute | solution.py:42
  4.1 5.8 %collective-permute-start.1 = (bf16[16,4096]{1,0:T(8,128)(2,1)S(1)}, bf16[16,4096]{1,0:T(8,128)(2,1)S(1)}, u32[]{:S(2)}, u32[]{:S(2)}) collective-permute-start(bf16[16,4096]{1,0:T(8,128)(2,1)S(1)} %collective-permute-done.refs_0_.refs_2_), channel_id=1, source_target_pairs={{0,4},{1,3},{4,8},{5,1},{8,12},{9,5},{12,14},{13,9},{14,10},{15,13... | collective-permute-start | bytes 393224 | tf_op jit(solution)/shard_map/ppermute | solution.py:42
  5.7 5.4 %collective-permute-start.4 = (bf16[16,4096]{1,0:T(8,128)(2,1)S(1)}, bf16[16,4096]{1,0:T(8,128)(2,1)S(1)}, u32[]{:S(2)}, u32[]{:S(2)}) collective-permute-start(bf16[16,4096]{1,0:T(8,128)(2,1)S(1)} %collective-permute-done.3.refs_0_.refs_3_), channel_id=1, source_target_pairs={{0,4},{1,3},{4,8},{5,1},{8,12},{9,5},{12,14},{13,9},{14,10},{15,13... | collective-permute-start | bytes 393224 | tf_op jit(solution)/shard_map/ppermute | solution.py:42
  7.2 4.5 %collective-permute-start.10 = (bf16[16,4096]{1,0:T(8,128)(2,1)S(1)}, bf16[16,4096]{1,0:T(8,128)(2,1)S(1)}, u32[]{:S(2)}, u32[]{:S(2)}) collective-permute-start(bf16[16,4096]{1,0:T(8,128)(2,1)S(1)} %collective-permute-done.8.refs_0_), channel_id=1, source_target_pairs={{0,4},{1,3},{4,8},{5,1},{8,12},{9,5},{12,14},{13,9},{14,10},{15,13... | collective-permute-start | bytes 393224 | tf_op jit(solution)/shard_map/ppermute | solution.py:42
  8.5 4.5 %collective-permute-start.11 = (bf16[16,4096]{1,0:T(8,128)(2,1)S(1)}, bf16[16,4096]{1,0:T(8,128)(2,1)S(1)}, u32[]{:S(2)}, u32[]{:S(2)}) collective-permute-start(bf16[16,4096]{1,0:T(8,128)(2,1)S(1)} %collective-permute-done.9.refs_1_), channel_id=1, source_target_pairs={{0,4},{1,3},{4,8},{5,1},{8,12},{9,5},{12,14},{13,9},{14,10},{15,13... | collective-permute-start | bytes 393224 | tf_op jit(solution)/shard_map/ppermute | solution.py:42
  9.8 4.7 %collective-permute-start.2 = (bf16[16,4096]{1,0:T(8,128)(2,1)S(1)}, bf16[16,4096]{1,0:T(8,128)(2,1)S(1)}, u32[]{:S(2)}, u32[]{:S(2)}) collective-permute-start(bf16[16,4096]{1,0:T(8,128)(2,1)S(1)} %collective-permute-done.1.refs_1_.refs_4_), channel_id=1, source_target_pairs={{0,4},{1,3},{4,8},{5,1},{8,12},{9,5},{12,14},{13,9},{14,10},{15,13... | collective-permute-start | bytes 393224 | tf_op jit(solution)/shard_map/ppermute | solution.py:42
  11.1 4.8 %collective-permute-start.5 = (bf16[16,4096]{1,0:T(8,128)(2,1)S(1)}, bf16[16,4096]{1,0:T(8,128)(2,1)S(1)}, u32[]{:S(2)}, u32[]{:S(2)}) collective-permute-start(bf16[16,4096]{1,0:T(8,128)(2,1)S(1)} %collective-permute-done.4.refs_2_.refs_5_), channel_id=1, source_target_pairs={{0,4},{1,3},{4,8},{5,1},{8,12},{9,5},{12,14},{13,9},{14,10},{15,13... | collective-permute-start | bytes 393224 | tf_op jit(solution)/shard_map/ppermute | solution.py:42
  11.7 7.9 %collective-permute-start.14 = (bf16[16,4096]{1,0:T(8,128)(2,1)S(1)}, bf16[16,4096]{1,0:T(8,128)(2,1)S(1)}, u32[]{:S(2)}, u32[]{:S(2)}) collective-permute-start(bf16[16,4096]{1,0:T(8,128)(2,1)S(1)} %collective-permute-done.10.refs_2_), channel_id=1, source_target_pairs={{0,4},{1,3},{4,8},{5,1},{8,12},{9,5},{12,14},{13,9},{14,10},{15,13... | collective-permute-start | bytes 393224 | tf_op jit(solution)/shard_map/ppermute | solution.py:42
  13.0 7.0 %collective-permute-start.15 = (bf16[16,4096]{1,0:T(8,128)(2,1)S(1)}, bf16[16,4096]{1,0:T(8,128)(2,1)S(1)}, u32[]{:S(2)}, u32[]{:S(2)}) collective-permute-start(bf16[16,4096]{1,0:T(8,128)(2,1)S(1)} %collective-permute-done.11.refs_3_), channel_id=1, source_target_pairs={{0,4},{1,3},{4,8},{5,1},{8,12},{9,5},{12,14},{13,9},{14,10},{15,13... | collective-permute-start | bytes 393224 | tf_op jit(solution)/shard_map/ppermute | solution.py:42
  14.5 5.9 %collective-permute-start.6 = (bf16[16,4096]{1,0:T(8,128)(2,1)S(1)}, bf16[16,4096]{1,0:T(8,128)(2,1)S(1)}, u32[]{:S(2)}, u32[]{:S(2)}) collective-permute-start(bf16[16,4096]{1,0:T(8,128)(2,1)S(1)} %collective-permute-done.2.refs_3_.refs_7_), channel_id=1, source_target_pairs={{0,4},{1,3},{4,8},{5,1},{8,12},{9,5},{12,14},{13,9},{14,10},{15,13... | collective-permute-start | bytes 393224 | tf_op jit(solution)/shard_map/ppermute | solution.py:42
  15.9 5.6 %collective-permute-start.7 = (bf16[16,4096]{1,0:T(8,128)(2,1)S(1)}, bf16[16,4096]{1,0:T(8,128)(2,1)S(1)}, u32[]{:S(2)}, u32[]{:S(2)}) collective-permute-start(bf16[16,4096]{1,0:T(8,128)(2,1)S(1)} %collective-permute-done.5.refs_4_.refs_8_), channel_id=1, source_target_pairs={{0,4},{1,3},{4,8},{5,1},{8,12},{9,5},{12,14},{13,9},{14,10},{15,13... | collective-permute-start | bytes 393224 | tf_op jit(solution)/shard_map/ppermute | solution.py:42
  16.9 9.7 %collective-permute-start.12 = (bf16[128,4096]{1,0:T(8,128)(2,1)S(1)}, bf16[128,4096]{1,0:T(8,128)(2,1)S(1)}, u32[]{:S(2)}, u32[]{:S(2)}) collective-permute-start(bf16[128,4096]{1,0:T(8,128)(2,1)S(1)} %constant_dynamic-update-slice_fusion), channel_id=1, source_target_pairs={{0,1},{1,0},{2,3},{3,2},{4,5},{5,4},{6,7},{7,6},{8,9},{9,8},{10,11... | collective-permute-start | bytes 3145736 | tf_op jit(solution)/shard_map/ppermute | solution.py:45
  19.6 4.6 %collective-permute-start.16 = (bf16[16,4096]{1,0:T(8,128)(2,1)S(1)}, bf16[16,4096]{1,0:T(8,128)(2,1)S(1)}, u32[]{:S(2)}, u32[]{:S(2)}) collective-permute-start(bf16[16,4096]{1,0:T(8,128)(2,1)S(1)} %collective-permute-done.14.refs_5_), channel_id=1, source_target_pairs={{0,4},{1,3},{4,8},{5,1},{8,12},{9,5},{12,14},{13,9},{14,10},{15,13... | collective-permute-start | bytes 393224 | tf_op jit(solution)/shard_map/ppermute | solution.py:42
  20.0 5.1 %collective-permute-start.17 = (bf16[16,4096]{1,0:T(8,128)(2,1)S(1)}, bf16[16,4096]{1,0:T(8,128)(2,1)S(1)}, u32[]{:S(2)}, u32[]{:S(2)}) collective-permute-start(bf16[16,4096]{1,0:T(8,128)(2,1)S(1)} %collective-permute-done.15.refs_6_), channel_id=1, source_target_pairs={{0,4},{1,3},{4,8},{5,1},{8,12},{9,5},{12,14},{13,9},{14,10},{15,13... | collective-permute-start | bytes 393224 | tf_op jit(solution)/shard_map/ppermute | solution.py:42
  21.9 4.8 %collective-permute-start.13 = (bf16[64,4096]{1,0:T(8,128)(2,1)S(1)}, bf16[64,4096]{1,0:T(8,128)(2,1)S(1)}, u32[]{:S(2)}, u32[]{:S(2)}) collective-permute-start(bf16[64,4096]{1,0:T(8,128)(2,1)S(1)} %pad_maximum_fusion), channel_id=1, source_target_pairs={{0,1},{1,0},{2,3},{3,2},{4,5},{5,4},{6,7},{7,6},{8,9},{9,8},{10,11... | collective-permute-start | bytes 1572872 | tf_op jit(solution)/shard_map/ppermute | solution.py:45
  25.1 3.4 %collective-permute-start.18 = (bf16[64,4096]{1,0:T(8,128)(2,1)S(1)}, bf16[64,4096]{1,0:T(8,128)(2,1)S(1)}, u32[]{:S(2)}, u32[]{:S(2)}) collective-permute-start(bf16[64,4096]{1,0:T(8,128)(2,1)S(1)} %pad_maximum_fusion.1), channel_id=1, source_target_pairs={{0,1},{1,0},{2,3},{3,2},{4,5},{5,4},{6,7},{7,6},{8,9},{9,8},{10,11... | collective-permute-start | bytes 1572872 | tf_op jit(solution)/shard_map/ppermute | solution.py:45

commit v25 on v19

--- a/solution.py
+++ b/solution.py
@@ -25,8 +25,8 @@
     for place, chip in enumerate(order):
         after = order[(place + 1) % len(order)]
         before = order[place - 1]
-        pairs.append((2 * chip, 2 * after))
-        pairs.append((2 * chip + 1, 2 * before + 1))
+        pairs.append((2 * chip, 2 * before))
+        pairs.append((2 * chip + 1, 2 * after + 1))
     return pairs
 
 

time: 30.8 us -> 30.8 us (level)
  waiting for transfers between devices: 3.74 us -> 3.11 us
  starting transfers between devices: 22.3 us -> 22.9 us
    ppermute x14, starting transfers between devices: 15.4 us -> 16.2 us  [hop(): return lax.ppermute(block, 'samp', ring)]
    ppermute x14, waiting for transfers between devices: 3.72 us -> 3.09 us  [hop(): return lax.ppermute(block, 'samp', ring)]
where the time goes in v25:
time: 30.8 us; the launch traced here: 30.6 us
  starting transfers between devices  22.9 us (74%)
  Pallas kernels  4.35 us (14%)
  waiting for transfers between devices  3.11 us (10%)
    ppermute x14, starting transfers between devices, hop(): return lax.ppermute(block, 'samp', ring)  16.2 us
    ppermute x5, starting transfers between devices, hand_over(): return lax.ppermute(block, 'samp', twins)  6.77 us
    pallas_call x2, Pallas kernels, call(): pl.pallas_call(functools.partial(kernel, spans), out_shape=out_shape, in_...  3.99 us
    ppermute x14, waiting for transfers between devices, hop(): return lax.ppermute(block, 'samp', ring)  3.09 us
  transfers between devices with their start and end apart: 19, of which 7 were waited for; matrix products, arithmetic and copies ran while one was open for 0% of the time, Pallas kernels for 7%

profile of v25, /device:TPU:1, one launch (start us, length us, event | category | flops | bytes accessed | tf_op | source)
XLA Modules:
  0.0 30.6 jit_solution(9507888333203245057)
XLA Ops:
  0.0 0.0 copy-start
  0.0 0.1 collective-permute-start
  0.1 2.7 %collective-permute-start.3 = (bf16[16,4096]{1,0:T(8,128)(2,1)}, bf16[16,4096]{1,0:T(8,128)(2,1)S(1)}, u32[]{:S(2)}, u32[]{:S(2)}) collective-permute-start(bf16[16,4096]{1,0:T(8,128)(2,1)} %param.5), channel_id=1, source_target_pairs={{0,2},{1,5},{4,0},{5,9},{8,4},{9,13},{12,8},{13,15},{14,12},{15,11... | collective-permute-start | bytes 393224 | tf_op jit(solution)/shard_map/ppermute | solution.py:42
  2.8 0.3 collective-permute-start.8
  3.1 1.0 %collective-permute-start.9 = (bf16[16,4096]{1,0:T(8,128)(2,1)}, bf16[16,4096]{1,0:T(8,128)(2,1)S(1)}, u32[]{:S(2)}, u32[]{:S(2)}) collective-permute-start(bf16[16,4096]{1,0:T(8,128)(2,1)} %param.4), channel_id=1, source_target_pairs={{0,2},{1,5},{4,0},{5,9},{8,4},{9,13},{12,8},{13,15},{14,12},{15,11... | collective-permute-start | bytes 393224 | tf_op jit(solution)/shard_map/ppermute | solution.py:42
  4.1 0.0 collective-permute-done.refs_0_.refs_2_
  4.1 1.3 %collective-permute-start.1 = (bf16[16,4096]{1,0:T(8,128)(2,1)S(1)}, bf16[16,4096]{1,0:T(8,128)(2,1)S(1)}, u32[]{:S(2)}, u32[]{:S(2)}) collective-permute-start(bf16[16,4096]{1,0:T(8,128)(2,1)S(1)} %collective-permute-done.refs_0_.refs_2_), channel_id=1, source_target_pairs={{0,2},{1,5},{4,0},{5,9},{8,4},{9,13},{12,8},{13,15},{14,12},{15,11... | collective-permute-start | bytes 393224 | tf_op jit(solution)/shard_map/ppermute | solution.py:42
  5.4 0.2 collective-permute-done.3.refs_0_.refs_3_
  5.6 1.5 %collective-permute-start.4 = (bf16[16,4096]{1,0:T(8,128)(2,1)S(1)}, bf16[16,4096]{1,0:T(8,128)(2,1)S(1)}, u32[]{:S(2)}, u32[]{:S(2)}) collective-permute-start(bf16[16,4096]{1,0:T(8,128)(2,1)S(1)} %collective-permute-done.3.refs_0_.refs_3_), channel_id=1, source_target_pairs={{0,2},{1,5},{4,0},{5,9},{8,4},{9,13},{12,8},{13,15},{14,12},{15,11... | collective-permute-start | bytes 393224 | tf_op jit(solution)/shard_map/ppermute | solution.py:42
  7.1 0.1 shard_map.37.refs_0_
  7.2 0.0 collective-permute-done.8.refs_0_
  7.2 1.3 %collective-permute-start.10 = (bf16[16,4096]{1,0:T(8,128)(2,1)S(1)}, bf16[16,4096]{1,0:T(8,128)(2,1)S(1)}, u32[]{:S(2)}, u32[]{:S(2)}) collective-permute-start(bf16[16,4096]{1,0:T(8,128)(2,1)S(1)} %collective-permute-done.8.refs_0_), channel_id=1, source_target_pairs={{0,2},{1,5},{4,0},{5,9},{8,4},{9,13},{12,8},{13,15},{14,12},{15,11... | collective-permute-start | bytes 393224 | tf_op jit(solution)/shard_map/ppermute | solution.py:42
  8.6 0.0 collective-permute-done.9.refs_1_
  8.6 1.3 %collective-permute-start.11 = (bf16[16,4096]{1,0:T(8,128)(2,1)S(1)}, bf16[16,4096]{1,0:T(8,128)(2,1)S(1)}, u32[]{:S(2)}, u32[]{:S(2)}) collective-permute-start(bf16[16,4096]{1,0:T(8,128)(2,1)S(1)} %collective-permute-done.9.refs_1_), channel_id=1, source_target_pairs={{0,2},{1,5},{4,0},{5,9},{8,4},{9,13},{12,8},{13,15},{14,12},{15,11... | collective-permute-start | bytes 393224 | tf_op jit(solution)/shard_map/ppermute | solution.py:42
  9.9 0.0 collective-permute-done.1.refs_1_.refs_4_
  9.9 1.2 %collective-permute-start.2 = (bf16[16,4096]{1,0:T(8,128)(2,1)S(1)}, bf16[16,4096]{1,0:T(8,128)(2,1)S(1)}, u32[]{:S(2)}, u32[]{:S(2)}) collective-permute-start(bf16[16,4096]{1,0:T(8,128)(2,1)S(1)} %collective-permute-done.1.refs_1_.refs_4_), channel_id=1, source_target_pairs={{0,2},{1,5},{4,0},{5,9},{8,4},{9,13},{12,8},{13,15},{14,12},{15,11... | collective-permute-start | bytes 393224 | tf_op jit(solution)/shard_map/ppermute | solution.py:42
  11.1 0.0 collective-permute-done.4.refs_2_.refs_5_
  11.1 0.2 collective-permute-start.5
  11.4 0.2 collective-permute-done.10.refs_2_
  11.6 1.2 %collective-permute-start.14 = (bf16[16,4096]{1,0:T(8,128)(2,1)S(1)}, bf16[16,4096]{1,0:T(8,128)(2,1)S(1)}, u32[]{:S(2)}, u32[]{:S(2)}) collective-permute-start(bf16[16,4096]{1,0:T(8,128)(2,1)S(1)} %collective-permute-done.10.refs_2_), channel_id=1, source_target_pairs={{0,2},{1,5},{4,0},{5,9},{8,4},{9,13},{12,8},{13,15},{14,12},{15,11... | collective-permute-start | bytes 393224 | tf_op jit(solution)/shard_map/ppermute | solution.py:42
  12.8 0.2 collective-permute-done.11.refs_3_
  13.0 1.2 %collective-permute-start.15 = (bf16[16,4096]{1,0:T(8,128)(2,1)S(1)}, bf16[16,4096]{1,0:T(8,128)(2,1)S(1)}, u32[]{:S(2)}, u32[]{:S(2)}) collective-permute-start(bf16[16,4096]{1,0:T(8,128)(2,1)S(1)} %collective-permute-done.11.refs_3_), channel_id=1, source_target_pairs={{0,2},{1,5},{4,0},{5,9},{8,4},{9,13},{12,8},{13,15},{14,12},{15,11... | collective-permute-start | bytes 393224 | tf_op jit(solution)/shard_map/ppermute | solution.py:42
  14.2 0.3 collective-permute-done.2.refs_3_.refs_7_
  14.4 1.1 %collective-permute-start.6 = (bf16[16,4096]{1,0:T(8,128)(2,1)S(1)}, bf16[16,4096]{1,0:T(8,128)(2,1)S(1)}, u32[]{:S(2)}, u32[]{:S(2)}) collective-permute-start(bf16[16,4096]{1,0:T(8,128)(2,1)S(1)} %collective-permute-done.2.refs_3_.refs_7_), channel_id=1, source_target_pairs={{0,2},{1,5},{4,0},{5,9},{8,4},{9,13},{12,8},{13,15},{14,12},{15,11... | collective-permute-start | bytes 393224 | tf_op jit(solution)/shard_map/ppermute | solution.py:42
  15.6 0.3 collective-permute-done.5.refs_4_.refs_8_
  15.8 1.1 %collective-permute-start.7 = (bf16[16,4096]{1,0:T(8,128)(2,1)S(1)}, bf16[16,4096]{1,0:T(8,128)(2,1)S(1)}, u32[]{:S(2)}, u32[]{:S(2)}) collective-permute-start(bf16[16,4096]{1,0:T(8,128)(2,1)S(1)} %collective-permute-done.5.refs_4_.refs_8_), channel_id=1, source_target_pairs={{0,2},{1,5},{4,0},{5,9},{8,4},{9,13},{12,8},{13,15},{14,12},{15,11... | collective-permute-start | bytes 393224 | tf_op jit(solution)/shard_map/ppermute | solution.py:42
  17.0 2.6 %collective-permute-start.12 = (bf16[128,4096]{1,0:T(8,128)(2,1)S(1)}, bf16[128,4096]{1,0:T(8,128)(2,1)S(1)}, u32[]{:S(2)}, u32[]{:S(2)}) collective-permute-start(bf16[128,4096]{1,0:T(8,128)(2,1)S(1)} %constant_dynamic-update-slice_fusion), channel_id=1, source_target_pairs={{0,1},{1,0},{2,3},{3,2},{4,5},{5,4},{6,7},{7,6},{8,9},{9,8},{10,11... | collective-permute-start | bytes 3145736 | tf_op jit(solution)/shard_map/ppermute | solution.py:45
  19.6 0.0 collective-permute-done.14.refs_5_
  19.6 0.4 %collective-permute-start.16 = (bf16[16,4096]{1,0:T(8,128)(2,1)S(1)}, bf16[16,4096]{1,0:T(8,128)(2,1)S(1)}, u32[]{:S(2)}, u32[]{:S(2)}) collective-permute-start(bf16[16,4096]{1,0:T(8,128)(2,1)S(1)} %collective-permute-done.14.refs_5_), channel_id=1, source_target_pairs={{0,2},{1,5},{4,0},{5,9},{8,4},{9,13},{12,8},{13,15},{14,12},{15,11... | collective-permute-start | bytes 393224 | tf_op jit(solution)/shard_map/ppermute | solution.py:42
  20.0 0.0 collective-permute-done.15.refs_6_
  20.0 0.4 %collective-permute-start.17 = (bf16[16,4096]{1,0:T(8,128)(2,1)S(1)}, bf16[16,4096]{1,0:T(8,128)(2,1)S(1)}, u32[]{:S(2)}, u32[]{:S(2)}) collective-permute-start(bf16[16,4096]{1,0:T(8,128)(2,1)S(1)} %collective-permute-done.15.refs_6_), channel_id=1, source_target_pairs={{0,2},{1,5},{4,0},{5,9},{8,4},{9,13},{12,8},{13,15},{14,12},{15,11... | collective-permute-start | bytes 393224 | tf_op jit(solution)/shard_map/ppermute | solution.py:42
  20.5 0.0 collective-permute-done.6.refs_5_.refs_9_
  20.5 1.0 %collective-permute-done.7.refs_6_.refs_10_ = bf16[16,4096]{1,0:T(8,128)(2,1)S(1)} collective-permute-done((bf16[16,4096]{1,0:T(8,128)(2,1)S(1)}, bf16[16,4096]{1,0:T(8,128)(2,1)S(1)}, u32[]{:S(2)}, u32[]{:S(2)}) %collective-permute-start.7) | collective-permute-done | bytes 131104 | tf_op jit(solution)/shard_map/ppermute | solution.py:42
  21.5 0.3 %shard_map.38.refs_1_ = f32[1,4096]{1,0:T(1,128)S(1)} custom-call(bf16[16,4096]{1,0:T(8,128)(2,1)S(1)} %collective-permute-done.3.refs_0_.refs_3_, bf16[16,4096]{1,0:T(8,128)(2,1)S(1)} %collective-permute-done.1.refs_1_.refs_4_, bf16[16,4096]{1,0:T(8,128)(2,1)S(1)} %collective-permute-done.4.refs_2_.refs_5_, ...), custom_call_target="tpu_custom_call" | custom-call | tf_op jit(solution)/shard_map/pallas_call | solution.py:163
  21.8 2.3 %collective-permute-start.13 = (bf16[64,4096]{1,0:T(8,128)(2,1)S(1)}, bf16[64,4096]{1,0:T(8,128)(2,1)S(1)}, u32[]{:S(2)}, u32[]{:S(2)}) collective-permute-start(bf16[64,4096]{1,0:T(8,128)(2,1)S(1)} %pad_maximum_fusion), channel_id=1, source_target_pairs={{0,1},{1,0},{2,3},{3,2},{4,5},{5,4},{6,7},{7,6},{8,9},{9,8},{10,11... | collective-permute-start | bytes 1572872 | tf_op jit(solution)/shard_map/ppermute | solution.py:45
  24.1 0.0 collective-permute-done.16.refs_7_
  24.1 1.0 %collective-permute-done.17.refs_8_ = bf16[16,4096]{1,0:T(8,128)(2,1)S(1)} collective-permute-done((bf16[16,4096]{1,0:T(8,128)(2,1)S(1)}, bf16[16,4096]{1,0:T(8,128)(2,1)S(1)}, u32[]{:S(2)}, u32[]{:S(2)}) %collective-permute-start.17) | collective-permute-done | bytes 131104 | tf_op jit(solution)/shard_map/ppermute | solution.py:42
  25.1 1.5 %collective-permute-start.18 = (bf16[64,4096]{1,0:T(8,128)(2,1)S(1)}, bf16[64,4096]{1,0:T(8,128)(2,1)S(1)}, u32[]{:S(2)}, u32[]{:S(2)}) collective-permute-start(bf16[64,4096]{1,0:T(8,128)(2,1)S(1)} %pad_maximum_fusion.1), channel_id=1, source_target_pairs={{0,1},{1,0},{2,3},{3,2},{4,5},{5,4},{6,7},{7,6},{8,9},{9,8},{10,11... | collective-permute-start | bytes 1572872 | tf_op jit(solution)/shard_map/ppermute | solution.py:45
  26.6 0.0 collective-permute-done.13.refs_11_
  26.6 0.0 collective-permute-done.12.refs_6_.refs_4_
  26.6 0.0 copy-done
  26.6 1.9 %shard_map.39 = (bf16[512,4096]{1,0:T(8,128)(2,1)S(1)}, f32[1,4096]{1,0:T(1,128)S(1)}, f32[1,512]{1,0:T(1,128)S(1)}) custom-call(bf16[512,4096]{1,0:T(8,128)(2,1)S(1)} %copy-done, f32[1,4096]{1,0:T(1,128)S(1)} %shard_map.37.refs_0_, f32[1,4096]{1,0:T(1,128)S(1)} %shard_map.38.refs_1_, bf16[16,4096]{1,0:T(8,128)(2,1)S(1)} %collective-permute-done.refs_0_.refs_2_, ...), custom_call_target="tpu_custom_call" | custom-call | flops 1073741824 | bytes 6291456 | tf_op jit(solution)/shard_map/pallas_call | solution.py:222
  28.6 0.0 collective-permute-done.18.refs_9_
  28.6 2.1 %shard_map.40 = f32[1,512]{1,0:T(1,128)} custom-call(f32[1,512]{1,0:T(1,128)S(1)} %get-tuple-element.16.ref_log, bf16[512,4096]{1,0:T(8,128)(2,1)S(1)} %get-tuple-element.17.probes, f32[1,4096]{1,0:T(1,128)S(1)} %get-tuple-element.18.mean, bf16[16,4096]{1,0:T(8,128)(2,1)S(1)} %collective-permute-done.8.refs_0_, ...), custom_call_target="tpu_custom_call" | custom-call | flops 1073741824 | bytes 6291456 | tf_op jit(solution)/shard_map/pallas_call | solution.py:222
  (10 shorter events, 0.1 us)
Async XLA Ops:
  0.0 26.6 %copy-start = (bf16[512,4096]{1,0:T(8,128)(2,1)S(1)}, bf16[512,4096]{1,0:T(8,128)(2,1)}, u32[]{:S(2)}) copy-start(bf16[512,4096]{1,0:T(8,128)(2,1)} %queries.1) | copy-start | bytes 12582916
  0.0 4.1 %collective-permute-start = (bf16[16,4096]{1,0:T(8,128)(2,1)}, bf16[16,4096]{1,0:T(8,128)(2,1)S(1)}, u32[]{:S(2)}, u32[]{:S(2)}) collective-permute-start(bf16[16,4096]{1,0:T(8,128)(2,1)} %param.5), channel_id=1, source_target_pairs={{0,1},{1,0},{2,3},{3,2},{4,5},{5,4},{6,7},{7,6},{8,9},{9,8},{10,11... | collective-permute-start | bytes 393224 | tf_op jit(solution)/shard_map/ppermute | solution.py:45
  0.1 5.5 %collective-permute-start.3 = (bf16[16,4096]{1,0:T(8,128)(2,1)}, bf16[16,4096]{1,0:T(8,128)(2,1)S(1)}, u32[]{:S(2)}, u32[]{:S(2)}) collective-permute-start(bf16[16,4096]{1,0:T(8,128)(2,1)} %param.5), channel_id=1, source_target_pairs={{0,2},{1,5},{4,0},{5,9},{8,4},{9,13},{12,8},{13,15},{14,12},{15,11... | collective-permute-start | bytes 393224 | tf_op jit(solution)/shard_map/ppermute | solution.py:42
  2.8 4.4 %collective-permute-start.8 = (bf16[16,4096]{1,0:T(8,128)(2,1)}, bf16[16,4096]{1,0:T(8,128)(2,1)S(1)}, u32[]{:S(2)}, u32[]{:S(2)}) collective-permute-start(bf16[16,4096]{1,0:T(8,128)(2,1)} %param.4), channel_id=1, source_target_pairs={{0,1},{1,0},{2,3},{3,2},{4,5},{5,4},{6,7},{7,6},{8,9},{9,8},{10,11... | collective-permute-start | bytes 393224 | tf_op jit(solution)/shard_map/ppermute | solution.py:45
  3.1 5.5 %collective-permute-start.9 = (bf16[16,4096]{1,0:T(8,128)(2,1)}, bf16[16,4096]{1,0:T(8,128)(2,1)S(1)}, u32[]{:S(2)}, u32[]{:S(2)}) collective-permute-start(bf16[16,4096]{1,0:T(8,128)(2,1)} %param.4), channel_id=1, source_target_pairs={{0,2},{1,5},{4,0},{5,9},{8,4},{9,13},{12,8},{13,15},{14,12},{15,11... | collective-permute-start | bytes 393224 | tf_op jit(solution)/shard_map/ppermute | solution.py:42
  4.1 5.8 %collective-permute-start.1 = (bf16[16,4096]{1,0:T(8,128)(2,1)S(1)}, bf16[16,4096]{1,0:T(8,128)(2,1)S(1)}, u32[]{:S(2)}, u32[]{:S(2)}) collective-permute-start(bf16[16,4096]{1,0:T(8,128)(2,1)S(1)} %collective-permute-done.refs_0_.refs_2_), channel_id=1, source_target_pairs={{0,2},{1,5},{4,0},{5,9},{8,4},{9,13},{12,8},{13,15},{14,12},{15,11... | collective-permute-start | bytes 393224 | tf_op jit(solution)/shard_map/ppermute | solution.py:42
  5.6 5.5 %collective-permute-start.4 = (bf16[16,4096]{1,0:T(8,128)(2,1)S(1)}, bf16[16,4096]{1,0:T(8,128)(2,1)S(1)}, u32[]{:S(2)}, u32[]{:S(2)}) collective-permute-start(bf16[16,4096]{1,0:T(8,128)(2,1)S(1)} %collective-permute-done.3.refs_0_.refs_3_), channel_id=1, source_target_pairs={{0,2},{1,5},{4,0},{5,9},{8,4},{9,13},{12,8},{13,15},{14,12},{15,11... | collective-permute-start | bytes 393224 | tf_op jit(solution)/shard_map/ppermute | solution.py:42
  7.2 4.4 %collective-permute-start.10 = (bf16[16,4096]{1,0:T(8,128)(2,1)S(1)}, bf16[16,4096]{1,0:T(8,128)(2,1)S(1)}, u32[]{:S(2)}, u32[]{:S(2)}) collective-permute-start(bf16[16,4096]{1,0:T(8,128)(2,1)S(1)} %collective-permute-done.8.refs_0_), channel_id=1, source_target_pairs={{0,2},{1,5},{4,0},{5,9},{8,4},{9,13},{12,8},{13,15},{14,12},{15,11... | collective-permute-start | bytes 393224 | tf_op jit(solution)/shard_map/ppermute | solution.py:42
  8.6 4.4 %collective-permute-start.11 = (bf16[16,4096]{1,0:T(8,128)(2,1)S(1)}, bf16[16,4096]{1,0:T(8,128)(2,1)S(1)}, u32[]{:S(2)}, u32[]{:S(2)}) collective-permute-start(bf16[16,4096]{1,0:T(8,128)(2,1)S(1)} %collective-permute-done.9.refs_1_), channel_id=1, source_target_pairs={{0,2},{1,5},{4,0},{5,9},{8,4},{9,13},{12,8},{13,15},{14,12},{15,11... | collective-permute-start | bytes 393224 | tf_op jit(solution)/shard_map/ppermute | solution.py:42
  9.9 4.6 %collective-permute-start.2 = (bf16[16,4096]{1,0:T(8,128)(2,1)S(1)}, bf16[16,4096]{1,0:T(8,128)(2,1)S(1)}, u32[]{:S(2)}, u32[]{:S(2)}) collective-permute-start(bf16[16,4096]{1,0:T(8,128)(2,1)S(1)} %collective-permute-done.1.refs_1_.refs_4_), channel_id=1, source_target_pairs={{0,2},{1,5},{4,0},{5,9},{8,4},{9,13},{12,8},{13,15},{14,12},{15,11... | collective-permute-start | bytes 393224 | tf_op jit(solution)/shard_map/ppermute | solution.py:42
  11.1 4.7 %collective-permute-start.5 = (bf16[16,4096]{1,0:T(8,128)(2,1)S(1)}, bf16[16,4096]{1,0:T(8,128)(2,1)S(1)}, u32[]{:S(2)}, u32[]{:S(2)}) collective-permute-start(bf16[16,4096]{1,0:T(8,128)(2,1)S(1)} %collective-permute-done.4.refs_2_.refs_5_), channel_id=1, source_target_pairs={{0,2},{1,5},{4,0},{5,9},{8,4},{9,13},{12,8},{13,15},{14,12},{15,11... | collective-permute-start | bytes 393224 | tf_op jit(solution)/shard_map/ppermute | solution.py:42
  11.6 8.0 %collective-permute-start.14 = (bf16[16,4096]{1,0:T(8,128)(2,1)S(1)}, bf16[16,4096]{1,0:T(8,128)(2,1)S(1)}, u32[]{:S(2)}, u32[]{:S(2)}) collective-permute-start(bf16[16,4096]{1,0:T(8,128)(2,1)S(1)} %collective-permute-done.10.refs_2_), channel_id=1, source_target_pairs={{0,2},{1,5},{4,0},{5,9},{8,4},{9,13},{12,8},{13,15},{14,12},{15,11... | collective-permute-start | bytes 393224 | tf_op jit(solution)/shard_map/ppermute | solution.py:42
  13.0 7.0 %collective-permute-start.15 = (bf16[16,4096]{1,0:T(8,128)(2,1)S(1)}, bf16[16,4096]{1,0:T(8,128)(2,1)S(1)}, u32[]{:S(2)}, u32[]{:S(2)}) collective-permute-start(bf16[16,4096]{1,0:T(8,128)(2,1)S(1)} %collective-permute-done.11.refs_3_), channel_id=1, source_target_pairs={{0,2},{1,5},{4,0},{5,9},{8,4},{9,13},{12,8},{13,15},{14,12},{15,11... | collective-permute-start | bytes 393224 | tf_op jit(solution)/shard_map/ppermute | solution.py:42
  14.4 6.0 %collective-permute-start.6 = (bf16[16,4096]{1,0:T(8,128)(2,1)S(1)}, bf16[16,4096]{1,0:T(8,128)(2,1)S(1)}, u32[]{:S(2)}, u32[]{:S(2)}) collective-permute-start(bf16[16,4096]{1,0:T(8,128)(2,1)S(1)} %collective-permute-done.2.refs_3_.refs_7_), channel_id=1, source_target_pairs={{0,2},{1,5},{4,0},{5,9},{8,4},{9,13},{12,8},{13,15},{14,12},{15,11... | collective-permute-start | bytes 393224 | tf_op jit(solution)/shard_map/ppermute | solution.py:42
  15.8 5.6 %collective-permute-start.7 = (bf16[16,4096]{1,0:T(8,128)(2,1)S(1)}, bf16[16,4096]{1,0:T(8,128)(2,1)S(1)}, u32[]{:S(2)}, u32[]{:S(2)}) collective-permute-start(bf16[16,4096]{1,0:T(8,128)(2,1)S(1)} %collective-permute-done.5.refs_4_.refs_8_), channel_id=1, source_target_pairs={{0,2},{1,5},{4,0},{5,9},{8,4},{9,13},{12,8},{13,15},{14,12},{15,11... | collective-permute-start | bytes 393224 | tf_op jit(solution)/shard_map/ppermute | solution.py:42
  17.0 9.7 %collective-permute-start.12 = (bf16[128,4096]{1,0:T(8,128)(2,1)S(1)}, bf16[128,4096]{1,0:T(8,128)(2,1)S(1)}, u32[]{:S(2)}, u32[]{:S(2)}) collective-permute-start(bf16[128,4096]{1,0:T(8,128)(2,1)S(1)} %constant_dynamic-update-slice_fusion), channel_id=1, source_target_pairs={{0,1},{1,0},{2,3},{3,2},{4,5},{5,4},{6,7},{7,6},{8,9},{9,8},{10,11... | collective-permute-start | bytes 3145736 | tf_op jit(solution)/shard_map/ppermute | solution.py:45
  19.6 4.6 %collective-permute-start.16 = (bf16[16,4096]{1,0:T(8,128)(2,1)S(1)}, bf16[16,4096]{1,0:T(8,128)(2,1)S(1)}, u32[]{:S(2)}, u32[]{:S(2)}) collective-permute-start(bf16[16,4096]{1,0:T(8,128)(2,1)S(1)} %collective-permute-done.14.refs_5_), channel_id=1, source_target_pairs={{0,2},{1,5},{4,0},{5,9},{8,4},{9,13},{12,8},{13,15},{14,12},{15,11... | collective-permute-start | bytes 393224 | tf_op jit(solution)/shard_map/ppermute | solution.py:42
  20.0 5.1 %collective-permute-start.17 = (bf16[16,4096]{1,0:T(8,128)(2,1)S(1)}, bf16[16,4096]{1,0:T(8,128)(2,1)S(1)}, u32[]{:S(2)}, u32[]{:S(2)}) collective-permute-start(bf16[16,4096]{1,0:T(8,128)(2,1)S(1)} %collective-permute-done.15.refs_6_), channel_id=1, source_target_pairs={{0,2},{1,5},{4,0},{5,9},{8,4},{9,13},{12,8},{13,15},{14,12},{15,11... | collective-permute-start | bytes 393224 | tf_op jit(solution)/shard_map/ppermute | solution.py:42
  21.8 4.8 %collective-permute-start.13 = (bf16[64,4096]{1,0:T(8,128)(2,1)S(1)}, bf16[64,4096]{1,0:T(8,128)(2,1)S(1)}, u32[]{:S(2)}, u32[]{:S(2)}) collective-permute-start(bf16[64,4096]{1,0:T(8,128)(2,1)S(1)} %pad_maximum_fusion), channel_id=1, source_target_pairs={{0,1},{1,0},{2,3},{3,2},{4,5},{5,4},{6,7},{7,6},{8,9},{9,8},{10,11... | collective-permute-start | bytes 1572872 | tf_op jit(solution)/shard_map/ppermute | solution.py:45
  25.1 3.4 %collective-permute-start.18 = (bf16[64,4096]{1,0:T(8,128)(2,1)S(1)}, bf16[64,4096]{1,0:T(8,128)(2,1)S(1)}, u32[]{:S(2)}, u32[]{:S(2)}) collective-permute-start(bf16[64,4096]{1,0:T(8,128)(2,1)S(1)} %pad_maximum_fusion.1), channel_id=1, source_target_pairs={{0,1},{1,0},{2,3},{3,2},{4,5},{5,4},{6,7},{7,6},{8,9},{9,8},{10,11... | collective-permute-start | bytes 1572872 | tf_op jit(solution)/shard_map/ppermute | solution.py:45
